TPU v7x, 32 devices: a whole 2x2x4 slice. The times are simulated.
32 devices in a mesh: row: 8 (over y, x, core), rep: 4 (over z).
Axes of the slice: x: 2, y: 2, z: 4, core: 2. Of those that a mesh axis runs over, the one named last changes fastest.
Arguments:
- features: bfloat16 [32768, 1024], P('row', 'rep'), may hold values from -6 to 6
- tiles: bfloat16 [256, 16, 128, 128], P('row'), may hold values from -0.1875 to 0.1875
- columns: int32 [256, 16], P('row'), may hold values from 0 to 255
- counts: int32 [256], P('row'), may hold values from 1 to 16, as said below
- weight: bfloat16 [1024, 1024], P(None, 'rep'), may hold values from -0.1875 to 0.1875
- cotangent: bfloat16 [32768, 1024], P('row', 'rep'), may hold values from -6 to 6
Outputs:
- activations: bfloat16 [32768, 1024], P('row', 'rep')
- feature_grad: bfloat16 [32768, 1024], P('row', 'rep')
- weight_grad: float32 [1024, 1024], P('rep', 'row')
Inputs may be any that keep to these rules, and one draw needn't show every extreme that they name: `counts`: in every draw some row block has all 16 slots in use.
All inputs are finite; a program needn't handle non-finite values.
Results may differ from a plain program's by a relative error of at most 0.014.
Values may be sent and summed in bfloat16 or wider, within the bound.
No kernel may reach another device: no remote copies, remote signals or barrier semaphores. Data moves between devices by JAX's collectives and lax.ppermute only.
A program may use at most 192 MiB of HBM per device.

v0:
```python
import jax
import jax.numpy as jnp
from jax import lax
from jax.sharding import PartitionSpec as P


def local(features, tiles, columns, counts, weight, cotangent):
    rows_here, feat_local = features.shape
    blocks_here, slots = columns.shape
    tile_size = tiles.shape[2]
    total_blocks = blocks_here * lax.axis_size("row")
    gathered = lax.all_gather(features, "row", axis=0, tiled=True)
    source_blocks = gathered.reshape(total_blocks, tile_size, feat_local)
    alive_mask = jnp.arange(slots)[None, :] < counts[:, None]
    masked_tiles = jnp.where(alive_mask[:, :, None, None], tiles, jnp.zeros((), tiles.dtype))
    operand = jnp.take(source_blocks, columns, axis=0)
    summed = jnp.einsum("bkij,bkjf->bif", masked_tiles, operand, preferred_element_type=jnp.float32)
    mixed = summed.reshape(rows_here, feat_local).astype(jnp.bfloat16)
    preact = jnp.dot(
        lax.all_gather(mixed, "rep", axis=1, tiled=True), weight, preferred_element_type=jnp.float32
    )
    sigmoid_pre = jax.nn.sigmoid(preact)
    activations = (preact * sigmoid_pre).astype(jnp.bfloat16)
    grad_out = (
        cotangent.astype(jnp.float32) * sigmoid_pre * (1.0 + preact * (1.0 - sigmoid_pre))
    ).astype(jnp.bfloat16)
    grad_cols = lax.all_gather(grad_out, "rep", axis=1, tiled=True)
    weight_terms = jnp.einsum("nf,nh->fh", mixed, grad_cols, preferred_element_type=jnp.float32)
    weight_grad = lax.psum_scatter(
        weight_terms.astype(jnp.bfloat16), "row", scatter_dimension=1, tiled=True
    ).astype(jnp.float32)
    full_weight = lax.all_gather(weight, "rep", axis=1, tiled=True)
    row_offset = lax.axis_index("rep") * feat_local
    own_rows = lax.dynamic_slice_in_dim(full_weight, row_offset, feat_local, 0)
    mixed_grad = jnp.einsum(
        "nh,fh->nf", grad_cols, own_rows, preferred_element_type=jnp.float32
    ).astype(jnp.bfloat16)
    grad_blocks = mixed_grad.reshape(blocks_here, tile_size, feat_local)
    contrib = jnp.einsum(
        "bkij,bif->bkjf", masked_tiles, grad_blocks, preferred_element_type=jnp.float32
    )
    scattered = jax.ops.segment_sum(
        contrib.reshape(blocks_here * slots, tile_size, feat_local),
        columns.reshape(-1),
        num_segments=total_blocks,
    )
    scattered = scattered.reshape(total_blocks * tile_size, feat_local)
    feature_grad = lax.psum_scatter(
        scattered.astype(jnp.bfloat16), "row", scatter_dimension=0, tiled=True
    )
    return (activations, feature_grad, weight_grad)


def solution(mesh):
    in_specs = (
        P("row", "rep"),
        P("row", None, None, None),
        P("row", None),
        P("row"),
        P(None, "rep"),
        P("row", "rep"),
    )
    out_specs = (P("row", "rep"), P("row", "rep"), P("rep", "row"))
    return jax.shard_map(local, mesh=mesh, in_specs=in_specs, out_specs=out_specs, check_vma=False)
```

profile of v0, /device:TPU:0, one launch (start us, length us, event | category | flops | bytes accessed | tf_op | source)
XLA Modules:
  0.0 829.6 jit_solution(7041006375168055827)
XLA Ops:
  7.2 0.0 all-gather.5.cloned.1.call-start
  7.2 0.7 all-gather.5.cloned.1.call-update
  7.9 0.0 all-gather.7.cloned.1.call-start
  7.9 0.7 compare_and_fusion
  8.7 0.1 copy.15
  8.7 0.7 compare_select_fusion
  9.4 0.1 copy.16
  9.5 0.1 reshape.50
  9.6 0.7 iota_compare_fusion
  10.3 92.1 %all-gather.5.cloned.1.call-done = bf16[32768,256]{1,0:T(8,128)(2,1)} async-done(((bf16[4096,256]{1,0:T(8,128)(2,1)}), bf16[32768,256]{1,0:T(8,128)(2,1)}) %all-gather.5.cloned.1.call-update) | async-done | bytes 16777232 | tf_op jit(solution)/shard_map/all_gather | solution.py:12
  102.5 21.8 %gather_fusion = bf16[512,128,256]{2,1,0:T(8,128)(2,1)} fusion(bf16[256,128,256]{2,1,0:T(8,128)(2,1)} %bitcast.21, s32[1024]{0:T(1024)S(1)} %pad_clamp_fusion), kind=kCustom, calls=%fused_computation | custom fusion | bytes 67110912 | tf_op jit(solution)/shard_map/jit(_take)/gather | solution.py:16
  124.3 0.0 copy-start.1
  124.3 19.1 %bitcast_convert_fusion = bf16[32,128,256]{2,1,0:T(8,128)(2,1)} fusion(bf16[32,16,128,256]{3,2,1,0:T(8,128)(2,1)} %bitcast.23, pred[32,16]{1,0:T(8,128)(4,1)S(1)} %copy.15, bf16[32,16,128,128]{3,2,1,0:T(8,128)(2,1)} %param.7, pred[32,16]{1,0:T(8,128)(4,1)S(1)} %iota_compare_fusion), kind=kOutput, calls=%fused_computation.11 | convolution fusion | flops 4321181696 | bytes 52429824 | tf_op jit(solution)/shard_map/bkij,bkjf->bif/dot_general | solution.py:17
  143.4 0.0 all-gather.7.cloned.1.call-update
  143.4 0.0 copy-start.2
  143.4 0.0 copy-start
  143.4 0.0 all-gather.9.cloned.1.call-start
  143.5 149.2 %all-gather.7.cloned.1.call-done = bf16[4096,1024]{1,0:T(8,128)(2,1)} async-done(((bf16[4096,256]{1,0:T(8,128)(2,1)}), bf16[4096,1024]{1,0:T(8,128)(2,1)}) %all-gather.7.cloned.1.call-update) | async-done | bytes 8388624 | tf_op jit(solution)/shard_map/all_gather | solution.py:20
  292.7 0.0 copy-done.1
  292.7 9.4 %multiply_convert_fusion = (bf16[4096,256]{1,0:T(8,128)(2,1)}, bf16[4096,256]{1,0:T(8,128)(2,1)}) fusion(bf16[4096,256]{1,0:T(8,128)(2,1)} %param.11, bf16[4096,1024]{1,0:T(8,128)(2,1)} %all-gather.7.cloned.1.call-done, bf16[1024,256]{1,0:T(8,128)(2,1)S(1)} %copy-done.1), kind=kOutput, calls=%fused_computation.12 | convolution fusion | flops 2160066560 | bytes 15204352 | tf_op jit(solution)/shard_map/dot_general | solution.py:19
  302.1 0.0 all-gather.9.cloned.1.call-update
  302.2 0.0 all-gather.11.cloned.1.call-start
  302.2 0.5 all-gather.11.cloned.1.call-update
  302.7 0.0 reduce-scatter.7.cloned.1.call-start
  302.8 0.0 copy-done.2
  302.8 0.1 copy.17
  302.9 0.1 reshape.58
  303.0 146.7 %all-gather.9.cloned.1.call-done = bf16[4096,1024]{1,0:T(8,128)(2,1)} async-done(((bf16[4096,256]{1,0:T(8,128)(2,1)}), bf16[4096,1024]{1,0:T(8,128)(2,1)}) %all-gather.9.cloned.1.call-update) | async-done | bytes 8388624 | tf_op jit(solution)/shard_map/all_gather | solution.py:27
  449.6 0.0 copy-done
  449.6 5.7 convolution_convert_fusion.1
  455.4 1.0 copy.22
  456.4 0.0 reduce-scatter.7.cloned.1.call-update
  456.4 0.2 reduce-scatter.5.cloned.1.call-start
  456.6 38.9 %all-gather.11.cloned.1.call-done = bf16[1024,1024]{1,0:T(8,128)(2,1)} async-done(((bf16[1024,256]{1,0:T(8,128)(2,1)}), bf16[1024,1024]{1,0:T(8,128)(2,1)}) %all-gather.11.cloned.1.call-update) | async-done | bytes 2097168 | tf_op jit(solution)/shard_map/all_gather | solution.py:32
  495.5 5.8 convolution_convert_fusion
  501.3 30.1 %fusion.4 = f32[32,16,128,256]{3,2,1,0:T(8,128)} fusion(bf16[32,128,256,1]{2,1,3,0:T(8,128)(2,1)S(1)} %bitcast.26, bf16[32,16,128,128]{3,2,1,0:T(8,128)(2,1)} %param.7, pred[32,16]{1,0:T(8,128)(4,1)S(1)} %iota_compare_fusion), kind=kOutput, calls=%fused_computation.7 | convolution fusion | flops 4303355904 | bytes 85983744 | tf_op jit(solution)/shard_map/bkij,bif->bkjf/dot_general | solution.py:39
  531.5 11.3 %broadcast_in_dim.35 = f32[256,128,256]{2,1,0:T(8,128)} broadcast(f32[]{:T(128)} %constant.8.clone.1), dimensions={} | broadcast | bytes 33554436 | tf_op jit(solution)/shard_map/broadcast_in_dim | solution.py:42
  542.8 148.3 %scatter_fusion = f32[256,128,256]{2,1,0:T(8,128)} fusion(f32[256,128,256]{2,1,0:T(8,128)} %broadcast_in_dim.35, s32[512]{0:T(512)S(1)} %reshape.58, f32[512,128,256]{2,1,0:T(8,128)} %bitcast.8), kind=kCustom, calls=%fused_computation.1 | custom fusion | flops 16777216 | bytes 201328640 | tf_op jit(solution)/shard_map/scatter-add | solution.py:42
  691.1 17.4 %convert_element_type.36 = bf16[256,128,256]{2,1,0:T(8,128)(2,1)} convert(f32[256,128,256]{2,1,0:T(8,128)} %scatter_fusion) | non-fusion elementwise | flops 8388608 | bytes 50331648 | tf_op jit(solution)/shard_map/convert_element_type | solution.py:49
  708.5 0.0 reduce-scatter.5.cloned.1.call-update
  708.5 0.0 reduce-scatter.7.cloned.1.call-done
  708.5 0.9 copy.23
  709.5 0.7 convert_element_type.39
  710.2 112.6 %reduce-scatter.5.cloned.1.call-done = bf16[4096,256]{1,0:T(8,128)(2,1)} async-done(((bf16[32768,256]{1,0:T(8,128)(2,1)}), bf16[4096,256]{1,0:T(8,128)(2,1)}) %reduce-scatter.5.cloned.1.call-update) | async-done | bytes 2097168 | tf_op jit(solution)/shard_map/reduce_scatter | solution.py:48
  (1 shorter events, 0.0 us)
Async XLA Ops:
  7.2 95.3 %all-gather.5.cloned.1.call-start = ((), (), s32[]{:S(2)}) async-start(), calls=%async_computation.2 | async-start | bytes 18874368 | tf_op jit(solution)/shard_map/all_gather | solution.py:12
  7.9 284.8 %all-gather.7.cloned.1.call-start = ((), (), s32[]{:S(2)}) async-start(), calls=%async_computation.3 | async-start | bytes 10485760 | tf_op jit(solution)/shard_map/all_gather | solution.py:20
  124.3 168.4 %copy-start.1 = (bf16[1024,256]{1,0:T(8,128)(2,1)S(1)}, bf16[1024,256]{1,0:T(8,128)(2,1)}, u32[]{:S(2)}) copy-start(bf16[1024,256]{1,0:T(8,128)(2,1)} %param.10) | copy-start | bytes 1572868
  143.4 159.4 %copy-start.2 = (s32[32,16]{0,1:T(8,128)S(1)}, s32[32,16]{0,1:T(8,128)}, u32[]{:S(2)}) copy-start(s32[32,16]{0,1:T(8,128)} %param.8) | copy-start | bytes 6148
  143.4 306.2 %copy-start = (bf16[32,128,256]{2,1,0:T(8,128)(2,1)S(1)}, bf16[32,128,256]{2,1,0:T(8,128)(2,1)}, u32[]{:S(2)}) copy-start(bf16[32,128,256]{2,1,0:T(8,128)(2,1)} %bitcast_convert_fusion) | copy-start | bytes 6291460
  143.4 306.2 %all-gather.9.cloned.1.call-start = ((), (), s32[]{:S(2)}) async-start(), calls=%async_computation.4 | async-start | bytes 10485760 | tf_op jit(solution)/shard_map/all_gather | solution.py:27
  302.2 193.4 %all-gather.11.cloned.1.call-start = ((), (), s32[]{:S(2)}) async-start(), calls=%async_computation.5 | async-start | bytes 2621440 | tf_op jit(solution)/shard_map/all_gather | solution.py:32
  302.7 405.8 %reduce-scatter.7.cloned.1.call-start = ((), (), s32[]{:S(2)}) async-start(), calls=%async_computation.7 | async-start | bytes 589824
  456.4 366.4 %reduce-scatter.5.cloned.1.call-start = ((), (), s32[]{:S(2)}) async-start(), calls=%async_computation.6 | async-start | bytes 18874368 | tf_op jit(solution)/shard_map/reduce_scatter | solution.py:48
Sparse Core Ops, SparseCore 0:
  9.9 92.5 all-gather.4
  143.5 149.1 all-gather.6
  302.3 147.3 all-gather.8
  451.1 44.4 all-gather.10
  498.4 32.3 reduce-scatter.6
  708.6 114.1 reduce-scatter.4
where the time goes:
time: 830 us
  waiting for transfers between devices  541 us (65%)
  other arithmetic  169 us (20%)
  matrix products  70.2 us (8%)
  local copies, waits for them, and re-layouts  35.5 us (4%)
  between operations  14.2 us (2%)
    all_gather x1, waiting for transfers between devices, local(): lax.all_gather(mixed, 'rep', axis=1, tiled=True)  149 us
    scatter-add x1, other arithmetic, local(): jax.ops.segment_sum(contrib.reshape(blocks_here * slots, tile_size, feat_...  148 us
    all_gather x1, waiting for transfers between devices, local(): grad_cols = lax.all_gather(grad_out, 'rep', axis=1, tiled=True)  147 us
    reduce_scatter x1, waiting for transfers between devices, local(): lax.psum_scatter(scattered.astype(jnp.bfloat16), 'row', scatter_dimension...  113 us
    all_gather x1, waiting for transfers between devices, local(): gathered = lax.all_gather(features, 'row', axis=0, tiled=True)  92.1 us
    all_gather x1, waiting for transfers between devices, local(): full_weight = lax.all_gather(weight, 'rep', axis=1, tiled=True)  38.9 us
    dot_general x1, matrix products, local(): jnp.einsum('bkij,bif->bkjf', masked_tiles, grad_blocks, preferred_element...  30.1 us
    gather x1, local copies, waits for them, and re-layouts, local(): operand = jnp.take(source_blocks, columns, axis=0)  21.8 us
  transfers between devices with their start and end apart: 6, of which 5 were waited for; matrix products, arithmetic and copies ran while one was open for 27% of the time, Pallas kernels for 0%

commit v1 on v0

v1 whole, which is shorter than its diff:
```python
import functools
import jax
import jax.numpy as jnp
from jax import lax
from jax.experimental import pallas as pl
from jax.experimental.pallas import tpu as pltpu
from jax.sharding import PartitionSpec as P

BF16, F32 = jnp.bfloat16, jnp.float32
VMEM_LIMIT = 56 * 1024 * 1024
LANES = 128
CORES = 2


def params():
    return pltpu.CompilerParams(vmem_limit_bytes=VMEM_LIMIT)


def any_spec():
    return pl.BlockSpec(memory_space=pl.ANY)


class Ring:
    def __init__(self, devices):
        self.chips = devices // CORES
        half = self.chips // 2
        self.order = list(range(half)) + list(range(self.chips - 1, half - 1, -1))
        self.devices = devices

    def perm(self, step):
        pairs = []
        for place, chip in enumerate(self.order):
            to = self.order[(place + step) % self.chips]
            pairs += [(chip * CORES + core, to * CORES + core) for core in range(CORES)]
        return pairs

    def hop(self, value, step):
        return lax.ppermute(value, "row", self.perm(step))

    def sibling(self, value):
        return lax.ppermute(value, "row", [(d, d ^ 1) for d in range(self.devices)])

    def device_at(self, offset, other_core):
        me = lax.axis_index("row")
        order = jnp.array(self.order, jnp.int32)
        place_of = jnp.array([self.order.index(c) for c in range(self.chips)], jnp.int32)
        chip = order[(place_of[me // CORES] + offset) % self.chips]
        core = me % CORES
        return chip * CORES + (1 - core if other_core else core)


def gather_pieces(ring, x):
    rows = x.shape[0]
    half = rows // 2
    middle = ring.chips // 2
    got = [(0, 0, x)]
    up = down = x
    for step in range(1, middle):
        up, down = ring.hop(up, 1), ring.hop(down, -1)
        got += [(-step, 0, up), (step, 0, down)]
    got += [(middle, 0, ring.hop(up[:half], 1)), (middle, half, ring.hop(down[half:], -1))]
    pieces = []
    for offset, start, value in got:
        pieces.append((ring.device_at(offset, False) * rows + start, value))
        pieces.append((ring.device_at(offset, True) * rows + start, ring.sibling(value)))
    return pieces


def add(*values):
    return functools.reduce(lambda a, b: a + b, [v.astype(F32) for v in values])


def reduce_pieces(ring, own, other):
    half = own[0].shape[0] // 2
    middle = ring.chips // 2
    total = [add(own[o], ring.sibling(other[o])) for o in range(ring.chips)]
    up = ring.hop(total[middle][:half].astype(BF16), 1)
    down = ring.hop(total[middle][half:].astype(BF16), -1)
    for step in range(middle - 1, 0, -1):
        to_up, to_down = total[step], total[ring.chips - step]
        if step == middle - 1:
            to_up = jnp.concatenate([to_up[:half] + up.astype(F32), to_up[half:]])
            to_down = jnp.concatenate([to_down[:half], to_down[half:] + down.astype(F32)])
        else:
            to_up, to_down = add(to_up, up), add(to_down, down)
        up, down = ring.hop(to_up.astype(BF16), 1), ring.hop(to_down.astype(BF16), -1)
    if middle == 1:
        return (total[0] + jnp.concatenate([up, down]).astype(F32)).astype(BF16)
    return add(total[0], up, down).astype(BF16)


def exchange(blocks):
    size = len(blocks)
    got = [blocks[0]] + [None] * (size - 1)
    for u in range(1, size):
        got[(size - u) % size] = lax.ppermute(blocks[u], "rep", [(i, (i + u) % size) for i in range(size)])
    return got


def row_block(t, me, per_part, parts):
    return lax.rem(me + t // per_part, parts) * per_part + lax.rem(t, per_part)


def spmm_kernel(n_pieces, parts, group, cols, counts, meta, tiles, *refs):
    pieces, outs = refs[:n_pieces], refs[n_pieces : n_pieces + parts]
    source, acc, sems = refs[n_pieces + parts :]
    t = pl.program_id(0)
    tile_size = tiles.shape[2]
    slots = tiles.shape[1]
    per_part = pl.num_programs(0) // parts

    @pl.when(t == 0)
    def _():
        copies = []
        for p, piece in enumerate(pieces):
            start = pl.multiple_of(meta[1 + p], tile_size)
            copies.append(pltpu.make_async_copy(piece, source.at[pl.ds(start, piece.shape[0])], sems.at[p]))
            copies[-1].start()
        for copy in copies:
            copy.wait()

    b = row_block(t, meta[0], per_part, parts)
    count = counts[b]
    for first in range(0, slots, group):

        @pl.when(count > first)
        def _():
            left, right = [], []
            for k in range(first, first + group):
                tile = tiles[0, k]
                left.append(jnp.where(k < count, tile, jnp.zeros_like(tile)))
                right.append(source[pl.ds(pl.multiple_of(cols[b, k] * tile_size, tile_size), tile_size), :])
            part = jnp.dot(
                jnp.concatenate(left, axis=1), jnp.concatenate(right, axis=0), preferred_element_type=F32
            )
            if first:
                acc[...] += part
            else:
                acc[...] = part

    for u in range(parts):

        @pl.when(t // per_part == u)
        def _():
            outs[u][...] = acc[...].astype(BF16)


def spmm(tiles, columns, counts, me, pieces, parts):
    blocks, slots, tile_size, _ = tiles.shape
    width = pieces[0][1].shape[1]
    total_rows = sum(v.shape[0] for _, v in pieces)
    per_part = blocks // parts
    meta = jnp.stack([me] + [start for start, _ in pieces]).astype(jnp.int32)

    def out_spec(u):
        return pl.BlockSpec(
            (tile_size, width), lambda t, cols, cnt, meta: (jnp.clip(t - u * per_part, 0, per_part - 1), 0)
        )

    return pl.pallas_call(
        functools.partial(spmm_kernel, len(pieces), parts, min(slots, 8)),
        grid_spec=pltpu.PrefetchScalarGridSpec(
            num_scalar_prefetch=3,
            grid=(blocks,),
            in_specs=[
                pl.BlockSpec(
                    (1, slots, tile_size, tile_size),
                    lambda t, cols, cnt, meta: (row_block(t, meta[0], per_part, parts), 0, 0, 0),
                )
            ]
            + [any_spec()] * len(pieces),
            out_specs=[out_spec(u) for u in range(parts)],
            scratch_shapes=[
                pltpu.VMEM((total_rows, width), BF16),
                pltpu.VMEM((tile_size, width), F32),
                pltpu.SemaphoreType.DMA((len(pieces),)),
            ],
        ),
        out_shape=[jax.ShapeDtypeStruct((per_part * tile_size, width), BF16) for _ in range(parts)],
        compiler_params=params(),
        cost_estimate=pl.CostEstimate(
            flops=2 * blocks * slots * tile_size * tile_size * width,
            bytes_accessed=2 * (tiles.size + total_rows * width),
            transcendentals=0,
        ),
        name="spmm",
    )(columns, counts, meta, tiles, *[v for _, v in pieces])


def spmm_t_kernel(parts, n_outs, group, cols, counts, meta, tiles, *refs):
    grads, outs = refs[:parts], refs[parts : parts + n_outs]
    total, grad, stage, in_sems, out_sems = refs[parts + n_outs :]
    t = pl.program_id(0)
    slots, tile_size = tiles.shape[1], tiles.shape[2]
    per_part = pl.num_programs(0) // parts
    part_rows = per_part * tile_size
    width = grad.shape[1]

    @pl.when(t == 0)
    def _():
        copies = []
        for u in range(parts):
            copies.append(pltpu.make_async_copy(grads[u], grad.at[pl.ds(u * part_rows, part_rows)], in_sems.at[u]))
            copies[-1].start()

        @pl.loop(0, total.shape[0] // tile_size)
        def _(i):
            total[pl.ds(pl.multiple_of(i * tile_size, tile_size), tile_size), :] = jnp.zeros((tile_size, width), F32)

        for copy in copies:
            copy.wait()

    b = row_block(t, meta[0], per_part, parts)
    count = counts[b]
    block_grad = grad[pl.ds(pl.multiple_of(t * tile_size, tile_size), tile_size), :]
    for first in range(0, slots, group):

        @pl.when(count > first)
        def _():
            left = tiles[0, first : first + group].reshape(group * tile_size, tile_size)
            part = jnp.dot(left, block_grad, preferred_element_type=F32)
            for k in range(group):
                at = pl.ds(pl.multiple_of(cols[b, first + k] * tile_size, tile_size), tile_size)
                total[at, :] += part[k * tile_size : (k + 1) * tile_size]

    @pl.when(t == pl.num_programs(0) - 1)
    def _():
        copies = []
        for o in range(n_outs):
            slot = o % 2
            rows = outs[o].shape[0]
            if o >= 2:
                copies[o - 2].wait()

            @pl.loop(0, rows // tile_size)
            def _(i):
                start = pl.multiple_of(meta[1 + o] + i * tile_size, tile_size)
                to = pl.multiple_of(i * tile_size, tile_size)
                stage[slot, pl.ds(to, tile_size), :] = total[pl.ds(start, tile_size), :].astype(BF16)

            copies.append(pltpu.make_async_copy(stage.at[slot, pl.ds(0, rows)], outs[o], out_sems.at[o]))
            copies[o].start()
        for copy in copies[-2:]:
            copy.wait()


def spmm_t(tiles_t, columns, counts, me, grads, starts, rows, total_rows):
    blocks, slots, tile_size, _ = tiles_t.shape
    parts = len(grads)
    part_rows, width = grads[0].shape
    per_part = blocks // parts
    meta = jnp.stack([me] + starts).astype(jnp.int32)
    return pl.pallas_call(
        functools.partial(spmm_t_kernel, parts, len(starts), min(slots, 4)),
        grid_spec=pltpu.PrefetchScalarGridSpec(
            num_scalar_prefetch=3,
            grid=(blocks,),
            in_specs=[
                pl.BlockSpec(
                    (1, slots, tile_size, tile_size),
                    lambda t, cols, cnt, meta: (row_block(t, meta[0], per_part, parts), 0, 0, 0),
                )
            ]
            + [any_spec()] * parts,
            out_specs=[any_spec()] * len(starts),
            scratch_shapes=[
                pltpu.VMEM((total_rows, width), F32),
                pltpu.VMEM((parts * part_rows, width), BF16),
                pltpu.VMEM((2, rows, width), BF16),
                pltpu.SemaphoreType.DMA((parts,)),
                pltpu.SemaphoreType.DMA((len(starts),)),
            ],
        ),
        out_shape=[jax.ShapeDtypeStruct((rows, width), BF16) for _ in starts],
        compiler_params=params(),
        cost_estimate=pl.CostEstimate(
            flops=2 * blocks * slots * tile_size * tile_size * width,
            bytes_accessed=2 * (tiles_t.size + total_rows * width),
            transcendentals=0,
        ),
        name="spmm_t",
    )(columns, counts, meta, tiles_t, *grads)


def dense_kernel(parts, chunks, meta, *refs):
    n_mixed = parts * chunks
    mixed_refs, cot_refs, w_hbm = refs[:n_mixed], refs[n_mixed : n_mixed + parts], refs[n_mixed + parts]
    outs = refs[n_mixed + parts + 1 :]
    act_outs, mg_outs = outs[:parts], outs[parts : parts + n_mixed]
    mixed_out, grad_out, weight, sems = outs[parts + n_mixed :]
    f_wide, h_wide = weight.shape[0] // parts, weight.shape[1] // parts
    width = f_wide // chunks
    me = meta[0]

    def place(u):
        return lax.rem(me + u, parts)

    @pl.when(pl.program_id(0) == 0)
    def _():
        copies = []
        for i in range(parts):
            for j in range(parts):
                src = w_hbm.at[
                    pl.ds(pl.multiple_of(place(i) * f_wide, f_wide), f_wide),
                    pl.ds(pl.multiple_of(place(j) * h_wide, h_wide), h_wide),
                ]
                dst = weight.at[pl.ds(i * f_wide, f_wide), pl.ds(j * h_wide, h_wide)]
                copies.append(pltpu.make_async_copy(src, dst, sems.at[i * parts + j]))
                copies[-1].start()
        for copy in copies:
            copy.wait()

    mixed = jnp.concatenate([ref[...] for ref in mixed_refs], axis=1)
    for u in range(parts):
        at = pl.ds(pl.multiple_of(place(u) * f_wide, f_wide), f_wide)
        mixed_out[:, at] = mixed[:, u * f_wide : (u + 1) * f_wide]
    grads = []
    for u in range(parts):
        preact = jnp.dot(mixed, weight[:, u * h_wide : (u + 1) * h_wide], preferred_element_type=F32)
        sig = jax.nn.sigmoid(preact)
        act_outs[u][...] = (preact * sig).astype(BF16)
        grads.append((cot_refs[u][...].astype(F32) * sig * (1.0 + preact * (1.0 - sig))).astype(BF16))
        at = pl.ds(pl.multiple_of(place(u) * h_wide, h_wide), h_wide)
        grad_out[:, at] = grads[u]
    grad = jnp.concatenate(grads, axis=1)
    back = lax.dot_general(grad, weight[...], (((1,), (1,)), ((), ())), preferred_element_type=F32).astype(BF16)
    for i in range(n_mixed):
        mg_outs[i][...] = back[:, i * width : (i + 1) * width]


def dense(me, mixed, cot, weight):
    parts, chunks = len(mixed), len(mixed[0])
    rows, width = mixed[0][0].shape
    features, hidden = weight.shape
    h_wide = hidden // parts
    step = min(rows, 256)

    def spec(w):
        return pl.BlockSpec((step, w), lambda t, meta: (t, 0))

    outs = pl.pallas_call(
        functools.partial(dense_kernel, parts, chunks),
        grid_spec=pltpu.PrefetchScalarGridSpec(
            num_scalar_prefetch=1,
            grid=(rows // step,),
            in_specs=[spec(width)] * (parts * chunks) + [spec(h_wide)] * parts + [any_spec()],
            out_specs=[spec(h_wide)] * parts + [spec(width)] * (parts * chunks) + [spec(features), spec(hidden)],
            scratch_shapes=[pltpu.VMEM((features, hidden), BF16), pltpu.SemaphoreType.DMA((parts * parts,))],
        ),
        out_shape=[jax.ShapeDtypeStruct((rows, h_wide), BF16)] * parts
        + [jax.ShapeDtypeStruct((rows, width), BF16)] * (parts * chunks)
        + [jax.ShapeDtypeStruct((rows, features), BF16), jax.ShapeDtypeStruct((rows, hidden), BF16)],
        compiler_params=params(),
        cost_estimate=pl.CostEstimate(
            flops=4 * rows * features * hidden,
            bytes_accessed=2 * (features * hidden + 6 * rows * hidden),
            transcendentals=rows * hidden,
        ),
        name="dense",
    )(me[None].astype(jnp.int32), *[m for row in mixed for m in row], *cot, weight)
    n = parts * chunks
    act, back = outs[:parts], outs[parts : parts + n]
    return act, [back[u * chunks : (u + 1) * chunks] for u in range(parts)], outs[-2], outs[-1]


def local(features, tiles, columns, counts, weight, cotangent):
    rows, f_wide = features.shape
    blocks, slots, tile_size, _ = tiles.shape
    row_size, parts = lax.axis_size("row"), lax.axis_size("rep")
    ring = Ring(row_size)
    rep = lax.axis_index("rep")
    chunks = f_wide // LANES if f_wide % LANES == 0 else 1
    width = f_wide // chunks
    part_rows = rows // parts

    def part_of(x, u):
        return lax.dynamic_slice_in_dim(x, lax.rem(rep + u, parts) * part_rows, part_rows, 0)

    share = weight.shape[0] // row_size
    w_share = lax.dynamic_slice_in_dim(weight, lax.axis_index("row") * share, share, 0)
    w_full = lax.all_gather(lax.all_gather(w_share, "rep", axis=1, tiled=True), "row", axis=0, tiled=True)

    cot = exchange([part_of(cotangent, u) for u in range(parts)])

    alive = jnp.arange(slots)[None, :] < counts[:, None]
    tiles_t = jnp.swapaxes(jnp.where(alive[:, :, None, None], tiles, jnp.zeros((), tiles.dtype)), 2, 3)

    mixed = []
    for c in range(chunks):
        x = features[:, c * width : (c + 1) * width]
        if c:
            x, *_ = lax.optimization_barrier((x, *[v for _, v in pieces]))
        pieces = gather_pieces(ring, x)
        mixed.append(exchange(spmm(tiles, columns, counts, rep, pieces, parts)))
    mixed = [[mixed[c][u] for c in range(chunks)] for u in range(parts)]

    act, back, mixed_rows, grad_rows = dense(rep, mixed, cot, w_full)

    weight_terms = lax.dot_general(mixed_rows, grad_rows, (((0,), (0,)), ((), ())), preferred_element_type=F32)
    weight_terms = lax.psum_scatter(weight_terms.astype(BF16), "row", scatter_dimension=1, tiled=True)
    weight_grad = lax.psum_scatter(weight_terms, "rep", scatter_dimension=0, tiled=True).astype(F32)

    starts = [ring.device_at(o, other) * rows for other in (False, True) for o in range(ring.chips)]
    feature_grad = []
    for c in range(chunks):
        grads = exchange([back[u][c] for u in range(parts)])
        terms = spmm_t(tiles_t, columns, counts, rep, grads, starts, rows, rows * row_size)
        feature_grad.append(reduce_pieces(ring, terms[: ring.chips], terms[ring.chips :]))
    feature_grad = jnp.concatenate(feature_grad, axis=1)

    act, _ = lax.optimization_barrier((act, grads))
    act = exchange(act)
    activations = jnp.zeros((rows, cotangent.shape[1]), BF16)
    for u in range(parts):
        activations = lax.dynamic_update_slice_in_dim(activations, act[u], lax.rem(rep + u, parts) * part_rows, 0)
    return (activations, feature_grad, weight_grad)


def solution(mesh):
    in_specs = (
        P("row", "rep"),
        P("row", None, None, None),
        P("row", None),
        P("row"),
        P(None, "rep"),
        P("row", "rep"),
    )
    out_specs = (P("row", "rep"), P("row", "rep"), P("rep", "row"))
    return jax.shard_map(local, mesh=mesh, in_specs=in_specs, out_specs=out_specs, check_vma=False)
```

time: 830 us -> 454 us (0.55)
  waiting for transfers between devices: 541 us -> 150 us
  other arithmetic: 169 us -> 25.7 us
  Pallas kernels: 0 us -> 140 us
  matrix products: 70.2 us -> 2.39 us
  starting transfers between devices: 0.42 us -> 48.4 us
  blocking collectives: 0 us -> 15.1 us
  local copies, waits for them, and re-layouts: 35.5 us -> 45 us
    all_gather x4 -> x1, waiting for transfers between devices: 427 us -> 0.02 us  [local(): lax.all_gather(lax.all_gather(w_share, 'rep', axis=1, tiled=True), 'row',...]
    ppermute x0 -> x52, waiting for transfers between devices: none -> 150 us  [the longest x16 127 us: hop(): return lax.ppermute(value, 'row', self.perm(step))]
    scatter-add x1 -> x0, other arithmetic: 148 us -> none  [local(): jax.ops.segment_sum(contrib.reshape(blocks_here * slots, tile_size, feat_...]
    pallas_call x0 -> x5, Pallas kernels: none -> 140 us  [the longest x2 69.4 us: spmm_t(): pl.pallas_call(functools.partial(spmm_t_kernel, parts, len(starts), min(s...]
    reduce_scatter x1, waiting for transfers between devices: 113 us -> 0.01 us  [local(): lax.psum_scatter(weight_terms, 'rep', scatter_dimension=0, tiled=True)]
    dot_general x5 -> x1, matrix products: 70.2 us -> 2.39 us  [local(): lax.dot_general(mixed_rows, grad_rows, (((0,), (0,)), ((), ())), preferre...]
    ppermute x0 -> x52, starting transfers between devices: none -> 48.2 us  [the longest x18 25.9 us: exchange(): lax.ppermute(blocks[u], 'rep', [(i, (i + u) % size) for i in range(size)])]
    unnamed x9 -> x86, local copies, waits for them, and re-layouts: 2.04 us -> 30.1 us
  transfers between devices with their start and end apart: 6 -> 55, of which waited for: 5 -> 16; matrix products, arithmetic and copies ran while one was open for 27% -> 15% of each run, Pallas kernels for 0% -> 29%
where the time goes in v1:
time: 454 us; the launch traced here: 449 us
  waiting for transfers between devices  150 us (33%)
  Pallas kernels  140 us (31%)
  starting transfers between devices  48.4 us (11%)
  local copies, waits for them, and re-layouts  45 us (10%)
  other arithmetic  25.7 us (6%)
  between operations  22.3 us (5%)
  blocking collectives  15.1 us (3%)
    ppermute x16, waiting for transfers between devices, hop(): return lax.ppermute(value, 'row', self.perm(step))  127 us
    pallas_call x2, Pallas kernels, spmm_t(): pl.pallas_call(functools.partial(spmm_t_kernel, parts, len(starts), min(s...  69.4 us
    pallas_call x2, Pallas kernels, spmm(): pl.pallas_call(functools.partial(spmm_kernel, len(pieces), parts, min(slo...  60.5 us
    unnamed x86, local copies, waits for them, and re-layouts  30.1 us
    ppermute x18, starting transfers between devices, exchange(): lax.ppermute(blocks[u], 'rep', [(i, (i + u) % size) for i in range(size)])  25.9 us
    ppermute x16, starting transfers between devices, hop(): return lax.ppermute(value, 'row', self.perm(step))  18.6 us
    ppermute x18, waiting for transfers between devices, exchange(): lax.ppermute(blocks[u], 'rep', [(i, (i + u) % size) for i in range(size)])  18.1 us
    all_gather x1, blocking collectives, local(): lax.all_gather(w_share, 'rep', axis=1, tiled=True)  15.1 us
  transfers between devices with their start and end apart: 55, of which 16 were waited for; matrix products, arithmetic and copies ran while one was open for 15% of the time, Pallas kernels for 29%

profile of v1, /device:TPU:0, one launch (start us, length us, event | category | flops | bytes accessed | tf_op | source)
XLA Modules:
  0.0 449.3 jit_solution(7881928742935967586)
XLA Ops:
  7.2 1.7 fusion.4
  9.0 3.0 collective-permute-start.1
  12.1 23.2 %collective-permute-done.1.refs_2_ = bf16[4096,128]{1,0:T(8,128)(2,1)} collective-permute-done((bf16[4096,128]{1,0:T(8,128)(2,1)S(1)}, bf16[4096,128]{1,0:T(8,128)(2,1)}, u32[]{:S(2)}, u32[]{:S(2)}) %collective-permute-start.1) | collective-permute-done | bytes 1048608 | tf_op jit(solution)/shard_map/ppermute | solution.py:38
  35.3 1.9 slice.80
  37.1 1.7 collective-permute-start.5
  39.4 1.9 slice.81
  41.6 15.1 %all_gather.6 = bf16[128,1024]{1,0:T(8,128)(2,1)} all-gather(bf16[128,256]{1,0:T(8,128)(2,1)S(1)} %constant_dynamic-slice_fusion.1), channel_id=1, replica_groups=mesh['row'=8,'rep'=4] {'rep'}, dimensions={1}, use_global_device_ids=true | all-gather | bytes 327680 | tf_op jit(solution)/shard_map/all_gather | solution.py:381
  57.4 1.4 collective-permute-done.6.refs_7_
  59.7 1.5 collective-permute-start.10
  62.0 31.4 %collective-permute-done.10.refs_2_ = bf16[4096,128]{1,0:T(8,128)(2,1)} collective-permute-done((bf16[4096,128]{1,0:T(8,128)(2,1)S(1)}, bf16[4096,128]{1,0:T(8,128)(2,1)}, u32[]{:S(2)}, u32[]{:S(2)}) %collective-permute-start.10) | collective-permute-done | bytes 1048608 | tf_op jit(solution)/shard_map/ppermute | solution.py:38
  94.5 1.5 collective-permute-start.14
  98.3 8.8 %collective-permute-done.14.refs_6_ = bf16[2048,128]{1,0:T(8,128)(2,1)} collective-permute-done((bf16[2048,128]{1,0:T(8,128)(2,1)S(1)}, bf16[2048,128]{1,0:T(8,128)(2,1)}, u32[]{:S(2)}, u32[]{:S(2)}) %collective-permute-start.14) | collective-permute-done | bytes 524320 | tf_op jit(solution)/shard_map/ppermute | solution.py:38
  107.1 3.1 collective-permute-done.16.refs_8_
  110.2 2.9 constant_dynamic-slice_fusion
  113.1 3.9 collective-permute-start.24
  127.4 30.3 %spmm.2 = (bf16[1024,128]{1,0:T(8,128)(2,1)}, bf16[1024,128]{1,0:T(8,128)(2,1)}, bf16[1024,128]{1,0:T(8,128)(2,1)}, bf16[1024,128]{1,0:T(8,128)(2,1)}) custom-call(s32[32,16]{1,0:T(8,128)} %copy.70.cols, s32[32]{0:T(128)} %counts.7, s32[11]{0:T(128)} %stack.116.meta, bf16[32,16,128,128]{3,2,1,0:T(8,128)(2,1)} %tiles.3, bf16[4096,128]{1,0:T(8,128)(2,1)} %copy-done.3, ...), custom_call_target="tpu_custom_call" | custom-call | flops 2147483648 | bytes 25165824 | tf_op jit(solution)/shard_map/spmm/pallas_call | solution.py:160
  157.7 3.5 collective-permute-start.18
  162.2 30.3 %spmm.3 = (bf16[1024,128]{1,0:T(8,128)(2,1)}, bf16[1024,128]{1,0:T(8,128)(2,1)}, bf16[1024,128]{1,0:T(8,128)(2,1)}, bf16[1024,128]{1,0:T(8,128)(2,1)}) custom-call(s32[32,16]{1,0:T(8,128)} %copy.70.cols, s32[32]{0:T(128)} %counts.7, s32[11]{0:T(128)} %stack.116.meta, bf16[32,16,128,128]{3,2,1,0:T(8,128)(2,1)} %tiles.3, bf16[4096,128]{1,0:T(8,128)(2,1)} %copy-done.2, ...), custom_call_target="tpu_custom_call" | custom-call | flops 2147483648 | bytes 25165824 | tf_op jit(solution)/shard_map/spmm/pallas_call | solution.py:160
  192.9 3.6 collective-permute-start.19
  197.1 22.5 %copy.72 = bf16[32,16,128,128]{2,3,1,0:T(8,128)(2,1)} copy(bf16[32,16,128,128]{3,2,1,0:T(8,128)(2,1)} %tiles.3) | data formatting | bytes 33554432 | tf_op args[1]
  219.8 4.6 %collective-permute-done.21.refs_5_ = bf16[1024,128]{1,0:T(8,128)(2,1)S(1)} collective-permute-done((bf16[1024,128]{1,0:T(8,128)(2,1)}, bf16[1024,128]{1,0:T(8,128)(2,1)S(1)}, u32[]{:S(2)}, u32[]{:S(2)}) %collective-permute-start.21) | collective-permute-done | bytes 262176 | tf_op jit(solution)/shard_map/ppermute | solution.py:96
  225.3 10.3 %dense.1 = (bf16[1024,256]{1,0:T(8,128)(2,1)}, bf16[1024,256]{1,0:T(8,128)(2,1)}, bf16[1024,256]{1,0:T(8,128)(2,1)}, bf16[1024,256]{1,0:T(8,128)(2,1)}, bf16[102...) custom-call(s32[1]{0:T(128)} %bitcast.meta, ...), custom_call_target="tpu_custom_call" | custom-call | flops 4294967296 | bytes 14680064 | tf_op jit(solution)/shard_map/dense/pallas_call | solution.py:341
  235.9 1.9 collective-permute-start.29
  237.8 2.2 collective-permute-start.33
  240.0 14.0 %select_bitcast_fusion.tiles = bf16[32,16,128,128]{3,2,1,0:T(8,128)(2,1)} fusion(bf16[32,16,128,128]{2,3,1,0:T(8,128)(2,1)} %copy.72, pred[32,16]{1,0:T(8,128)(4,1)S(1)} %iota_compare_fusion), kind=kLoop, calls=%fused_computation | loop fusion | flops 8388608 | bytes 33554944 | tf_op jit(solution)/shard_map/transpose | solution.py:386
  256.0 1.9 collective-permute-start.35
  257.9 13.4 %collective-permute-done.28.refs_2_ = bf16[1024,128]{1,0:T(8,128)(2,1)S(1)} collective-permute-done((bf16[1024,128]{1,0:T(8,128)(2,1)}, bf16[1024,128]{1,0:T(8,128)(2,1)S(1)}, u32[]{:S(2)}, u32[]{:S(2)}) %collective-permute-start.28) | collective-permute-done | bytes 262176 | tf_op jit(solution)/shard_map/ppermute | solution.py:96
  271.4 2.8 collective-permute-start.31
  274.2 34.7 %spmm_t.3 = (bf16[4096,128]{1,0:T(8,128)(2,1)}, bf16[4096,128]{1,0:T(8,128)(2,1)}, bf16[4096,128]{1,0:T(8,128)(2,1)}, bf16[4096,128]{1,0:T(8,128)(2,1)}, bf16[40...) custom-call(s32[32,16]{1,0:T(8,128)} %copy.70.cols, ...), custom_call_target="tpu_custom_call" | custom-call | flops 2147483648 | bytes 25165824 | tf_op jit(solution)/shard_map/spmm_t/pallas_call | solution.py:253
  309.0 2.4 convolution_convert_fusion
  311.4 2.6 copy.75
  315.0 2.5 collective-permute-start.32
  317.7 34.8 %spmm_t.2 = (bf16[4096,128]{1,0:T(8,128)(2,1)}, bf16[4096,128]{1,0:T(8,128)(2,1)}, bf16[4096,128]{1,0:T(8,128)(2,1)}, bf16[4096,128]{1,0:T(8,128)(2,1)}, bf16[40...) custom-call(s32[32,16]{1,0:T(8,128)} %copy.70.cols, ...), custom_call_target="tpu_custom_call" | custom-call | flops 2147483648 | bytes 25165824 | tf_op jit(solution)/shard_map/spmm_t/pallas_call | solution.py:253
  352.7 1.2 constant_dynamic-update-slice_fusion.1
  354.6 1.7 convert_add_fusion
  357.0 1.3 collective-permute-done.41
  361.5 2.9 collective-permute-start.47
  365.0 11.5 %collective-permute-done.50 = bf16[2048,128]{1,0:T(8,128)(2,1)S(1)} collective-permute-done((bf16[2048,128]{1,0:T(8,128)(2,1)S(1)}, bf16[2048,128]{1,0:T(8,128)(2,1)S(1)}, u32[]{:S(2)}, u32[]{:S(2)}) %collective-permute-start.50) | collective-permute-done | bytes 524320 | tf_op jit(solution)/shard_map/ppermute | solution.py:38
  376.6 2.1 collective-permute-start.39
  378.9 11.2 %collective-permute-done.42 = bf16[2048,128]{1,0:T(8,128)(2,1)S(1)} collective-permute-done((bf16[2048,128]{1,0:T(8,128)(2,1)S(1)}, bf16[2048,128]{1,0:T(8,128)(2,1)S(1)}, u32[]{:S(2)}, u32[]{:S(2)}) %collective-permute-start.42) | collective-permute-done | bytes 524320 | tf_op jit(solution)/shard_map/ppermute | solution.py:38
  390.5 1.8 collective-permute-start.48
  394.9 1.7 collective-permute-start.40
  396.7 19.6 %collective-permute-done.51 = bf16[4096,128]{1,0:T(8,128)(2,1)S(1)} collective-permute-done((bf16[4096,128]{1,0:T(8,128)(2,1)S(1)}, bf16[4096,128]{1,0:T(8,128)(2,1)S(1)}, u32[]{:S(2)}, u32[]{:S(2)}) %collective-permute-start.51) | collective-permute-done | bytes 1048608 | tf_op jit(solution)/shard_map/ppermute | solution.py:38
  417.3 1.8 copy.76
  419.2 17.6 %collective-permute-done.43 = bf16[4096,128]{1,0:T(8,128)(2,1)} collective-permute-done((bf16[4096,128]{1,0:T(8,128)(2,1)}, bf16[4096,128]{1,0:T(8,128)(2,1)}, u32[]{:S(2)}, u32[]{:S(2)}) %collective-permute-start.43) | collective-permute-done | bytes 1048608 | tf_op jit(solution)/shard_map/ppermute | solution.py:38
  437.3 2.5 add_convert_fusion.2
  439.7 1.5 pad_maximum_fusion
  441.3 1.5 convert_element_type.119
  (200 shorter events, 26.1 us)
Async XLA Ops:
  7.2 212.6 %all-gather.2.cloned.1.call-start = ((), (), s32[]{:S(2)}) async-start(), calls=%async_computation.2 | async-start | bytes 2359296 | tf_op jit(solution)/shard_map/all_gather | solution.py:381
  9.0 26.3 %collective-permute-start.1 = (bf16[4096,128]{1,0:T(8,128)(2,1)S(1)}, bf16[4096,128]{1,0:T(8,128)(2,1)}, u32[]{:S(2)}, u32[]{:S(2)}) collective-permute-start(bf16[4096,128]{1,0:T(8,128)(2,1)S(1)} %get-tuple-element.94.refs_0_), channel_id=1, source_target_pairs={{0,8},{4,12},{8,24},{12,28},{24,16},{28,20},{16,0},{20,4},{1,9},{5... | collective-permute-start | bytes 3145736 | tf_op jit(solution)/shard_map/ppermute | solution.py:38
  12.0 26.9 %collective-permute-start.3 = (bf16[4096,128]{1,0:T(8,128)(2,1)S(1)}, bf16[4096,128]{1,0:T(8,128)(2,1)}, u32[]{:S(2)}, u32[]{:S(2)}) collective-permute-start(bf16[4096,128]{1,0:T(8,128)(2,1)S(1)} %get-tuple-element.94.refs_0_), channel_id=1, source_target_pairs={{0,16},{4,20},{8,0},{12,4},{24,8},{28,12},{16,24},{20,28},{1,17},{... | collective-permute-start | bytes 3145736 | tf_op jit(solution)/shard_map/ppermute | solution.py:38
  12.1 45.3 %collective-permute-start = (bf16[4096,128]{1,0:T(8,128)(2,1)S(1)}, bf16[4096,128]{1,0:T(8,128)(2,1)}, u32[]{:S(2)}, u32[]{:S(2)}) collective-permute-start(bf16[4096,128]{1,0:T(8,128)(2,1)S(1)} %get-tuple-element.94.refs_0_), channel_id=1, source_target_pairs={{0,4},{4,0},{8,12},{12,8},{16,20},{20,16},{24,28},{28,24},{1,5},{5... | collective-permute-start | bytes 3145736 | tf_op jit(solution)/shard_map/ppermute | solution.py:41
  37.1 19.6 %collective-permute-start.5 = (bf16[2048,128]{1,0:T(8,128)(2,1)}, bf16[2048,128]{1,0:T(8,128)(2,1)S(1)}, u32[]{:S(2)}, u32[]{:S(2)}) collective-permute-start(bf16[2048,128]{1,0:T(8,128)(2,1)} %slice.80), channel_id=1, source_target_pairs={{0,8},{4,12},{8,24},{12,28},{24,16},{28,20},{16,0},{20,4},{1,9},{5... | collective-permute-start | bytes 1572872 | tf_op jit(solution)/shard_map/ppermute | solution.py:38
  38.9 18.5 %collective-permute-start.2 = (bf16[4096,128]{1,0:T(8,128)(2,1)}, bf16[4096,128]{1,0:T(8,128)(2,1)}, u32[]{:S(2)}, u32[]{:S(2)}) collective-permute-start(bf16[4096,128]{1,0:T(8,128)(2,1)} %collective-permute-done.1.refs_2_), channel_id=1, source_target_pairs={{0,4},{4,0},{8,12},{12,8},{16,20},{20,16},{24,28},{28,24},{1,5},{5... | collective-permute-start | bytes 3145736 | tf_op jit(solution)/shard_map/ppermute | solution.py:41
  38.9 18.5 %collective-permute-start.4 = (bf16[4096,128]{1,0:T(8,128)(2,1)}, bf16[4096,128]{1,0:T(8,128)(2,1)}, u32[]{:S(2)}, u32[]{:S(2)}) collective-permute-start(bf16[4096,128]{1,0:T(8,128)(2,1)} %collective-permute-done.3.refs_4_), channel_id=1, source_target_pairs={{0,4},{4,0},{8,12},{12,8},{16,20},{20,16},{24,28},{28,24},{1,5},{5... | collective-permute-start | bytes 3145736 | tf_op jit(solution)/shard_map/ppermute | solution.py:41
  41.3 15.6 %collective-permute-start.7 = (bf16[2048,128]{1,0:T(8,128)(2,1)}, bf16[2048,128]{1,0:T(8,128)(2,1)}, u32[]{:S(2)}, u32[]{:S(2)}) collective-permute-start(bf16[2048,128]{1,0:T(8,128)(2,1)} %slice.81), channel_id=1, source_target_pairs={{0,16},{4,20},{8,0},{12,4},{24,8},{28,12},{16,24},{20,28},{1,17},{... | collective-permute-start | bytes 1572872 | tf_op jit(solution)/shard_map/ppermute | solution.py:38
  56.7 360.6 %reduce-scatter.7.cloned.1.call-start = ((), (), s32[]{:S(2)}) async-start(), calls=%async_computation.4 | async-start | bytes 2359296
  59.7 33.7 %collective-permute-start.10 = (bf16[4096,128]{1,0:T(8,128)(2,1)S(1)}, bf16[4096,128]{1,0:T(8,128)(2,1)}, u32[]{:S(2)}, u32[]{:S(2)}) collective-permute-start(bf16[4096,128]{1,0:T(8,128)(2,1)S(1)} %get-tuple-element.47.refs_0_), channel_id=1, source_target_pairs={{0,8},{4,12},{8,24},{12,28},{24,16},{28,20},{16,0},{20,4},{1,9},{5... | collective-permute-start | bytes 3145736 | tf_op jit(solution)/shard_map/ppermute | solution.py:38
  61.2 34.9 %collective-permute-start.12 = (bf16[4096,128]{1,0:T(8,128)(2,1)S(1)}, bf16[4096,128]{1,0:T(8,128)(2,1)}, u32[]{:S(2)}, u32[]{:S(2)}) collective-permute-start(bf16[4096,128]{1,0:T(8,128)(2,1)S(1)} %get-tuple-element.47.refs_0_), channel_id=1, source_target_pairs={{0,16},{4,20},{8,0},{12,4},{24,8},{28,12},{16,24},{20,28},{1,17},{... | collective-permute-start | bytes 3145736 | tf_op jit(solution)/shard_map/ppermute | solution.py:38
  62.0 51.1 %collective-permute-start.9 = (bf16[4096,128]{1,0:T(8,128)(2,1)S(1)}, bf16[4096,128]{1,0:T(8,128)(2,1)}, u32[]{:S(2)}, u32[]{:S(2)}) collective-permute-start(bf16[4096,128]{1,0:T(8,128)(2,1)S(1)} %get-tuple-element.47.refs_0_), channel_id=1, source_target_pairs={{0,4},{4,0},{8,12},{12,8},{16,20},{20,16},{24,28},{28,24},{1,5},{5... | collective-permute-start | bytes 3145736 | tf_op jit(solution)/shard_map/ppermute | solution.py:41
  94.5 12.5 %collective-permute-start.14 = (bf16[2048,128]{1,0:T(8,128)(2,1)S(1)}, bf16[2048,128]{1,0:T(8,128)(2,1)}, u32[]{:S(2)}, u32[]{:S(2)}) collective-permute-start(bf16[2048,128]{1,0:T(8,128)(2,1)S(1)} %slice.82), channel_id=1, source_target_pairs={{0,8},{4,12},{8,24},{12,28},{24,16},{28,20},{16,0},{20,4},{1,9},{5... | collective-permute-start | bytes 1572872 | tf_op jit(solution)/shard_map/ppermute | solution.py:38
  97.2 13.0 %collective-permute-start.16 = (bf16[2048,128]{1,0:T(8,128)(2,1)S(1)}, bf16[2048,128]{1,0:T(8,128)(2,1)}, u32[]{:S(2)}, u32[]{:S(2)}) collective-permute-start(bf16[2048,128]{1,0:T(8,128)(2,1)S(1)} %slice.83), channel_id=1, source_target_pairs={{0,16},{4,20},{8,0},{12,4},{24,8},{28,12},{16,24},{20,28},{1,17},{... | collective-permute-start | bytes 1572872 | tf_op jit(solution)/shard_map/ppermute | solution.py:38
  97.7 59.9 %collective-permute-start.11 = (bf16[4096,128]{1,0:T(8,128)(2,1)}, bf16[4096,128]{1,0:T(8,128)(2,1)S(1)}, u32[]{:S(2)}, u32[]{:S(2)}) collective-permute-start(bf16[4096,128]{1,0:T(8,128)(2,1)} %collective-permute-done.10.refs_2_), channel_id=1, source_target_pairs={{0,4},{4,0},{8,12},{12,8},{16,20},{20,16},{24,28},{28,24},{1,5},{5... | collective-permute-start | bytes 3145736 | tf_op jit(solution)/shard_map/ppermute | solution.py:41
  97.8 63.4 %collective-permute-start.13 = (bf16[4096,128]{1,0:T(8,128)(2,1)}, bf16[4096,128]{1,0:T(8,128)(2,1)}, u32[]{:S(2)}, u32[]{:S(2)}) collective-permute-start(bf16[4096,128]{1,0:T(8,128)(2,1)} %collective-permute-done.12.refs_4_), channel_id=1, source_target_pairs={{0,4},{4,0},{8,12},{12,8},{16,20},{20,16},{24,28},{28,24},{1,5},{5... | collective-permute-start | bytes 3145736 | tf_op jit(solution)/shard_map/ppermute | solution.py:41
  107.1 9.9 %collective-permute-start.15 = (bf16[2048,128]{1,0:T(8,128)(2,1)}, bf16[2048,128]{1,0:T(8,128)(2,1)}, u32[]{:S(2)}, u32[]{:S(2)}) collective-permute-start(bf16[2048,128]{1,0:T(8,128)(2,1)} %collective-permute-done.14.refs_6_), channel_id=1, source_target_pairs={{0,4},{4,0},{8,12},{12,8},{16,20},{20,16},{24,28},{28,24},{1,5},{5... | collective-permute-start | bytes 1572872 | tf_op jit(solution)/shard_map/ppermute | solution.py:41
  113.1 79.4 %collective-permute-start.24 = (bf16[1024,256]{1,0:T(8,128)(2,1)}, bf16[1024,256]{1,0:T(8,128)(2,1)S(1)}, u32[]{:S(2)}, u32[]{:S(2)}) collective-permute-start(bf16[1024,256]{1,0:T(8,128)(2,1)} %get-tuple-element.90), channel_id=1, source_target_pairs={{0,3},{1,0},{2,1},{3,2},{4,7},{5,4},{6,5},{7,6},{8,11},{9,8},{10,9... | collective-permute-start | bytes 1572872 | tf_op jit(solution)/shard_map/ppermute | solution.py:96
  117.0 75.9 %collective-permute-start.25 = (bf16[1024,256]{1,0:T(8,128)(2,1)}, bf16[1024,256]{1,0:T(8,128)(2,1)S(1)}, u32[]{:S(2)}, u32[]{:S(2)}) collective-permute-start(bf16[1024,256]{1,0:T(8,128)(2,1)} %get-tuple-element.92), channel_id=1, source_target_pairs={{0,2},{1,3},{2,0},{3,1},{4,6},{5,7},{6,4},{7,5},{8,10},{9,11},{10,... | collective-permute-start | bytes 1572872 | tf_op jit(solution)/shard_map/ppermute | solution.py:96
  117.0 79.4 %collective-permute-start.26 = (bf16[1024,256]{1,0:T(8,128)(2,1)}, bf16[1024,256]{1,0:T(8,128)(2,1)S(1)}, u32[]{:S(2)}, u32[]{:S(2)}) collective-permute-start(bf16[1024,256]{1,0:T(8,128)(2,1)} %get-tuple-element.89), channel_id=1, source_target_pairs={{0,1},{1,2},{2,3},{3,0},{4,5},{5,6},{6,7},{7,4},{8,9},{9,10},{10,1... | collective-permute-start | bytes 1572872 | tf_op jit(solution)/shard_map/ppermute | solution.py:96
  157.7 39.1 %collective-permute-start.18 = (bf16[1024,128]{1,0:T(8,128)(2,1)}, bf16[1024,128]{1,0:T(8,128)(2,1)S(1)}, u32[]{:S(2)}, u32[]{:S(2)}) collective-permute-start(bf16[1024,128]{1,0:T(8,128)(2,1)} %get-tuple-element.49), channel_id=1, source_target_pairs={{0,3},{1,0},{2,1},{3,2},{4,7},{5,4},{6,5},{7,6},{8,11},{9,8},{10,9... | collective-permute-start | bytes 786440 | tf_op jit(solution)/shard_map/ppermute | solution.py:96
  161.2 58.6 %collective-permute-start.20 = (bf16[1024,128]{1,0:T(8,128)(2,1)}, bf16[1024,128]{1,0:T(8,128)(2,1)S(1)}, u32[]{:S(2)}, u32[]{:S(2)}) collective-permute-start(bf16[1024,128]{1,0:T(8,128)(2,1)} %get-tuple-element.51), channel_id=1, source_target_pairs={{0,2},{1,3},{2,0},{3,1},{4,6},{5,7},{6,4},{7,5},{8,10},{9,11},{10,... | collective-permute-start | bytes 786440 | tf_op jit(solution)/shard_map/ppermute | solution.py:96
  192.5 27.2 %collective-permute-start.22 = (bf16[1024,128]{1,0:T(8,128)(2,1)}, bf16[1024,128]{1,0:T(8,128)(2,1)S(1)}, u32[]{:S(2)}, u32[]{:S(2)}) collective-permute-start(bf16[1024,128]{1,0:T(8,128)(2,1)} %get-tuple-element.53), channel_id=1, source_target_pairs={{0,1},{1,2},{2,3},{3,0},{4,5},{5,6},{6,7},{7,4},{8,9},{9,10},{10,1... | collective-permute-start | bytes 786440 | tf_op jit(solution)/shard_map/ppermute | solution.py:96
  192.9 26.9 %collective-permute-start.19 = (bf16[1024,128]{1,0:T(8,128)(2,1)}, bf16[1024,128]{1,0:T(8,128)(2,1)S(1)}, u32[]{:S(2)}, u32[]{:S(2)}) collective-permute-start(bf16[1024,128]{1,0:T(8,128)(2,1)} %get-tuple-element.50), channel_id=1, source_target_pairs={{0,3},{1,0},{2,1},{3,2},{4,7},{5,4},{6,5},{7,6},{8,11},{9,8},{10,9... | collective-permute-start | bytes 786440 | tf_op jit(solution)/shard_map/ppermute | solution.py:96
  196.4 28.0 %collective-permute-start.21 = (bf16[1024,128]{1,0:T(8,128)(2,1)}, bf16[1024,128]{1,0:T(8,128)(2,1)S(1)}, u32[]{:S(2)}, u32[]{:S(2)}) collective-permute-start(bf16[1024,128]{1,0:T(8,128)(2,1)} %get-tuple-element.52), channel_id=1, source_target_pairs={{0,2},{1,3},{2,0},{3,1},{4,6},{5,7},{6,4},{7,5},{8,10},{9,11},{10,... | collective-permute-start | bytes 786440 | tf_op jit(solution)/shard_map/ppermute | solution.py:96
  196.8 27.7 %collective-permute-start.23 = (bf16[1024,128]{1,0:T(8,128)(2,1)}, bf16[1024,128]{1,0:T(8,128)(2,1)S(1)}, u32[]{:S(2)}, u32[]{:S(2)}) collective-permute-start(bf16[1024,128]{1,0:T(8,128)(2,1)} %get-tuple-element.54), channel_id=1, source_target_pairs={{0,1},{1,2},{2,3},{3,0},{4,5},{5,6},{6,7},{7,4},{8,9},{9,10},{10,1... | collective-permute-start | bytes 786440 | tf_op jit(solution)/shard_map/ppermute | solution.py:96
  235.6 20.4 %collective-permute-start.27 = (bf16[1024,128]{1,0:T(8,128)(2,1)}, bf16[1024,128]{1,0:T(8,128)(2,1)S(1)}, u32[]{:S(2)}, u32[]{:S(2)}) collective-permute-start(bf16[1024,128]{1,0:T(8,128)(2,1)} %get-tuple-element.60), channel_id=1, source_target_pairs={{0,3},{1,0},{2,1},{3,2},{4,7},{5,4},{6,5},{7,6},{8,11},{9,8},{10,9... | collective-permute-start | bytes 786440 | tf_op jit(solution)/shard_map/ppermute | solution.py:96
  235.7 35.7 %collective-permute-start.28 = (bf16[1024,128]{1,0:T(8,128)(2,1)}, bf16[1024,128]{1,0:T(8,128)(2,1)S(1)}, u32[]{:S(2)}, u32[]{:S(2)}) collective-permute-start(bf16[1024,128]{1,0:T(8,128)(2,1)} %get-tuple-element.61), channel_id=1, source_target_pairs={{0,2},{1,3},{2,0},{3,1},{4,6},{5,7},{6,4},{7,5},{8,10},{9,11},{10,... | collective-permute-start | bytes 786440 | tf_op jit(solution)/shard_map/ppermute | solution.py:96
  235.9 35.5 %collective-permute-start.29 = (bf16[1024,128]{1,0:T(8,128)(2,1)}, bf16[1024,128]{1,0:T(8,128)(2,1)S(1)}, u32[]{:S(2)}, u32[]{:S(2)}) collective-permute-start(bf16[1024,128]{1,0:T(8,128)(2,1)} %get-tuple-element.62), channel_id=1, source_target_pairs={{0,1},{1,2},{2,3},{3,0},{4,5},{5,6},{6,7},{7,4},{8,9},{9,10},{10,1... | collective-permute-start | bytes 786440 | tf_op jit(solution)/shard_map/ppermute | solution.py:96
  237.8 71.0 %collective-permute-start.33 = (bf16[1024,128]{1,0:T(8,128)(2,1)}, bf16[1024,128]{1,0:T(8,128)(2,1)S(1)}, u32[]{:S(2)}, u32[]{:S(2)}) collective-permute-start(bf16[1024,128]{1,0:T(8,128)(2,1)} %get-tuple-element.68), channel_id=1, source_target_pairs={{0,3},{1,0},{2,1},{3,2},{4,7},{5,4},{6,5},{7,6},{8,11},{9,8},{10,9... | collective-permute-start | bytes 786440 | tf_op jit(solution)/shard_map/ppermute | solution.py:96
  255.4 59.7 %collective-permute-start.34 = (bf16[1024,128]{1,0:T(8,128)(2,1)}, bf16[1024,128]{1,0:T(8,128)(2,1)}, u32[]{:S(2)}, u32[]{:S(2)}) collective-permute-start(bf16[1024,128]{1,0:T(8,128)(2,1)} %get-tuple-element.69), channel_id=1, source_target_pairs={{0,2},{1,3},{2,0},{3,1},{4,6},{5,7},{6,4},{7,5},{8,10},{9,11},{10,... | collective-permute-start | bytes 786440 | tf_op jit(solution)/shard_map/ppermute | solution.py:96
  256.0 61.5 %collective-permute-start.35 = (bf16[1024,128]{1,0:T(8,128)(2,1)}, bf16[1024,128]{1,0:T(8,128)(2,1)}, u32[]{:S(2)}, u32[]{:S(2)}) collective-permute-start(bf16[1024,128]{1,0:T(8,128)(2,1)} %get-tuple-element.70), channel_id=1, source_target_pairs={{0,1},{1,2},{2,3},{3,0},{4,5},{5,6},{6,7},{7,4},{8,9},{9,10},{10,1... | collective-permute-start | bytes 786440 | tf_op jit(solution)/shard_map/ppermute | solution.py:96
  271.4 81.2 %collective-permute-start.30 = (bf16[1024,256]{1,0:T(8,128)(2,1)}, bf16[1024,256]{1,0:T(8,128)(2,1)}, u32[]{:S(2)}, u32[]{:S(2)}) collective-permute-start(bf16[1024,256]{1,0:T(8,128)(2,1)} %get-tuple-element.64), channel_id=1, source_target_pairs={{0,3},{1,0},{2,1},{3,2},{4,7},{5,4},{6,5},{7,6},{8,11},{9,8},{10,9... | collective-permute-start | bytes 1572872 | tf_op jit(solution)/shard_map/ppermute | solution.py:96
  271.4 82.5 %collective-permute-start.31 = (bf16[1024,256]{1,0:T(8,128)(2,1)}, bf16[1024,256]{1,0:T(8,128)(2,1)S(1)}, u32[]{:S(2)}, u32[]{:S(2)}) collective-permute-start(bf16[1024,256]{1,0:T(8,128)(2,1)} %get-tuple-element.65), channel_id=1, source_target_pairs={{0,2},{1,3},{2,0},{3,1},{4,6},{5,7},{6,4},{7,5},{8,10},{9,11},{10,... | collective-permute-start | bytes 1572872 | tf_op jit(solution)/shard_map/ppermute | solution.py:96
  308.9 45.6 %collective-permute-start.49 = (bf16[4096,128]{1,0:T(8,128)(2,1)}, bf16[4096,128]{1,0:T(8,128)(2,1)}, u32[]{:S(2)}, u32[]{:S(2)}) collective-permute-start(bf16[4096,128]{1,0:T(8,128)(2,1)} %get-tuple-element.86), channel_id=1, source_target_pairs={{0,4},{4,0},{8,12},{12,8},{16,20},{20,16},{24,28},{28,24},{1,5},{5... | collective-permute-start | bytes 3145736 | tf_op jit(solution)/shard_map/ppermute | solution.py:41
  314.0 127.3 %reduce-scatter.5.cloned.1.call-start = ((), (), s32[]{:S(2)}) async-start(), calls=%async_computation.3 | async-start | bytes 327680 | tf_op jit(solution)/shard_map/reduce_scatter | solution.py:401
  315.0 79.6 %collective-permute-start.32 = (bf16[1024,256]{1,0:T(8,128)(2,1)}, bf16[1024,256]{1,0:T(8,128)(2,1)S(1)}, u32[]{:S(2)}, u32[]{:S(2)}) collective-permute-start(bf16[1024,256]{1,0:T(8,128)(2,1)} %get-tuple-element.66), channel_id=1, source_target_pairs={{0,1},{1,2},{2,3},{3,0},{4,5},{5,6},{6,7},{7,4},{8,9},{9,10},{10,1... | collective-permute-start | bytes 1572872 | tf_op jit(solution)/shard_map/ppermute | solution.py:96
  317.5 41.2 %collective-permute-start.46 = (bf16[4096,128]{1,0:T(8,128)(2,1)S(1)}, bf16[4096,128]{1,0:T(8,128)(2,1)S(1)}, u32[]{:S(2)}, u32[]{:S(2)}) collective-permute-start(bf16[4096,128]{1,0:T(8,128)(2,1)S(1)} %copy-done.26), channel_id=1, source_target_pairs={{0,4},{4,0},{8,12},{12,8},{16,20},{20,16},{24,28},{28,24},{1,5},{5... | collective-permute-start | bytes 3145736 | tf_op jit(solution)/shard_map/ppermute | solution.py:41
  353.9 41.0 %collective-permute-start.44 = (bf16[4096,128]{1,0:T(8,128)(2,1)S(1)}, bf16[4096,128]{1,0:T(8,128)(2,1)S(1)}, u32[]{:S(2)}, u32[]{:S(2)}) collective-permute-start(bf16[4096,128]{1,0:T(8,128)(2,1)S(1)} %copy-done.25), channel_id=1, source_target_pairs={{0,4},{4,0},{8,12},{12,8},{16,20},{20,16},{24,28},{28,24},{1,5},{5... | collective-permute-start | bytes 3145736 | tf_op jit(solution)/shard_map/ppermute | solution.py:41
  358.8 60.4 %collective-permute-start.36 = (bf16[4096,128]{1,0:T(8,128)(2,1)}, bf16[4096,128]{1,0:T(8,128)(2,1)}, u32[]{:S(2)}, u32[]{:S(2)}) collective-permute-start(bf16[4096,128]{1,0:T(8,128)(2,1)} %get-tuple-element.72), channel_id=1, source_target_pairs={{0,4},{4,0},{8,12},{12,8},{16,20},{20,16},{24,28},{28,24},{1,5},{5... | collective-permute-start | bytes 3145736 | tf_op jit(solution)/shard_map/ppermute | solution.py:41
  361.3 15.2 %collective-permute-start.50 = (bf16[2048,128]{1,0:T(8,128)(2,1)S(1)}, bf16[2048,128]{1,0:T(8,128)(2,1)S(1)}, u32[]{:S(2)}, u32[]{:S(2)}) collective-permute-start(bf16[2048,128]{1,0:T(8,128)(2,1)S(1)} %get-tuple-element.98), channel_id=1, source_target_pairs={{0,16},{4,20},{8,0},{12,4},{24,8},{28,12},{16,24},{20,28},{1,17},{... | collective-permute-start | bytes 1572872 | tf_op jit(solution)/shard_map/ppermute | solution.py:38
  361.5 15.1 %collective-permute-start.47 = (bf16[2048,128]{1,0:T(8,128)(2,1)S(1)}, bf16[2048,128]{1,0:T(8,128)(2,1)S(1)}, u32[]{:S(2)}, u32[]{:S(2)}) collective-permute-start(bf16[2048,128]{1,0:T(8,128)(2,1)S(1)} %get-tuple-element.97), channel_id=1, source_target_pairs={{0,8},{4,12},{8,24},{12,28},{24,16},{28,20},{16,0},{20,4},{1,9},{5... | collective-permute-start | bytes 1572872 | tf_op jit(solution)/shard_map/ppermute | solution.py:38
  376.5 13.7 %collective-permute-start.42 = (bf16[2048,128]{1,0:T(8,128)(2,1)S(1)}, bf16[2048,128]{1,0:T(8,128)(2,1)S(1)}, u32[]{:S(2)}, u32[]{:S(2)}) collective-permute-start(bf16[2048,128]{1,0:T(8,128)(2,1)S(1)} %get-tuple-element.96), channel_id=1, source_target_pairs={{0,16},{4,20},{8,0},{12,4},{24,8},{28,12},{16,24},{20,28},{1,17},{... | collective-permute-start | bytes 1572872 | tf_op jit(solution)/shard_map/ppermute | solution.py:38
  376.6 13.9 %collective-permute-start.39 = (bf16[2048,128]{1,0:T(8,128)(2,1)S(1)}, bf16[2048,128]{1,0:T(8,128)(2,1)S(1)}, u32[]{:S(2)}, u32[]{:S(2)}) collective-permute-start(bf16[2048,128]{1,0:T(8,128)(2,1)S(1)} %get-tuple-element.95), channel_id=1, source_target_pairs={{0,8},{4,12},{8,24},{12,28},{24,16},{28,20},{16,0},{20,4},{1,9},{5... | collective-permute-start | bytes 1572872 | tf_op jit(solution)/shard_map/ppermute | solution.py:38
  390.1 26.1 %collective-permute-start.51 = (bf16[4096,128]{1,0:T(8,128)(2,1)S(1)}, bf16[4096,128]{1,0:T(8,128)(2,1)S(1)}, u32[]{:S(2)}, u32[]{:S(2)}) collective-permute-start(bf16[4096,128]{1,0:T(8,128)(2,1)S(1)} %pad_maximum_fusion.4), channel_id=1, source_target_pairs={{0,16},{4,20},{8,0},{12,4},{24,8},{28,12},{16,24},{20,28},{1,17},{... | collective-permute-start | bytes 3145736 | tf_op jit(solution)/shard_map/ppermute | solution.py:38
  390.5 26.1 %collective-permute-start.48 = (bf16[4096,128]{1,0:T(8,128)(2,1)S(1)}, bf16[4096,128]{1,0:T(8,128)(2,1)S(1)}, u32[]{:S(2)}, u32[]{:S(2)}) collective-permute-start(bf16[4096,128]{1,0:T(8,128)(2,1)S(1)} %pad_maximum_fusion.3), channel_id=1, source_target_pairs={{0,8},{4,12},{8,24},{12,28},{24,16},{28,20},{16,0},{20,4},{1,9},{5... | collective-permute-start | bytes 3145736 | tf_op jit(solution)/shard_map/ppermute | solution.py:38
  394.6 42.2 %collective-permute-start.43 = (bf16[4096,128]{1,0:T(8,128)(2,1)}, bf16[4096,128]{1,0:T(8,128)(2,1)}, u32[]{:S(2)}, u32[]{:S(2)}) collective-permute-start(bf16[4096,128]{1,0:T(8,128)(2,1)} %pad_maximum_fusion.2), channel_id=1, source_target_pairs={{0,16},{4,20},{8,0},{12,4},{24,8},{28,12},{16,24},{20,28},{1,17},{... | collective-permute-start | bytes 3145736 | tf_op jit(solution)/shard_map/ppermute | solution.py:38
  394.9 42.4 %collective-permute-start.40 = (bf16[4096,128]{1,0:T(8,128)(2,1)}, bf16[4096,128]{1,0:T(8,128)(2,1)}, u32[]{:S(2)}, u32[]{:S(2)}) collective-permute-start(bf16[4096,128]{1,0:T(8,128)(2,1)} %pad_maximum_fusion.1), channel_id=1, source_target_pairs={{0,8},{4,12},{8,24},{12,28},{24,16},{28,20},{16,0},{20,4},{1,9},{5... | collective-permute-start | bytes 3145736 | tf_op jit(solution)/shard_map/ppermute | solution.py:38
  (48 other events, 745.4 us)
Sparse Core Ops, SparseCore 0:
  56.8 37.9 all-gather.1
  314.1 41.0 reduce-scatter.6
  419.3 19.3 reduce-scatter.4

commit v2 on v1

v2 whole, which is shorter than its diff:
```python
import functools
import jax
import jax.numpy as jnp
from jax import lax
from jax.experimental import pallas as pl
from jax.experimental.pallas import tpu as pltpu
from jax.sharding import PartitionSpec as P

BF16, F32 = jnp.bfloat16, jnp.float32
VMEM_LIMIT = 56 * 1024 * 1024
LANES = 128
CORES = 2


def params():
    return pltpu.CompilerParams(vmem_limit_bytes=VMEM_LIMIT)


def any_spec():
    return pl.BlockSpec(memory_space=pl.ANY)


class Ring:
    def __init__(self, devices):
        self.chips = devices // CORES
        half = self.chips // 2
        self.order = list(range(half)) + list(range(self.chips - 1, half - 1, -1))
        self.devices = devices

    def perm(self, step):
        pairs = []
        for place, chip in enumerate(self.order):
            to = self.order[(place + step) % self.chips]
            pairs += [(chip * CORES + core, to * CORES + core) for core in range(CORES)]
        return pairs

    def hop(self, value, step):
        return lax.ppermute(value, "row", self.perm(step))

    def sibling(self, value):
        return lax.ppermute(value, "row", [(d, d ^ 1) for d in range(self.devices)])

    def device_at(self, offset, other_core):
        me = lax.axis_index("row")
        order = jnp.array(self.order, jnp.int32)
        place_of = jnp.array([self.order.index(c) for c in range(self.chips)], jnp.int32)
        chip = order[(place_of[me // CORES] + offset) % self.chips]
        core = me % CORES
        return chip * CORES + (1 - core if other_core else core)


def after(value, *others):
    return lax.optimization_barrier((value, *others))[0]


def gather_chunks(ring, chunks):
    rows = chunks[0].shape[0]
    half = rows // 2
    middle = ring.chips // 2
    gate = ()
    pieces = []
    for x in chunks:
        low, high = after(x[:half], *gate), after(x[half:], *gate)
        got = [(0, 0, x)]
        up, down = (low, high), (high, low)
        for step in range(1, middle):
            up = tuple(ring.hop(v, 1) for v in up)
            down = tuple(ring.hop(v, -1) for v in down)
            got += [(-step, 0, up[0]), (step, half, down[0]), (-step, half, up[1]), (step, 0, down[1])]
        gate = (up[1], down[1]) if middle > 1 else ()
        got += [(middle, 0, ring.hop(up[0], 1)), (middle, half, ring.hop(down[0], -1))]
        pieces.append([])
        for offset, start, value in got:
            pieces[-1].append((ring.device_at(offset, False) * rows + start, value))
            pieces[-1].append((ring.device_at(offset, True) * rows + start, ring.sibling(value)))
    return pieces


def reduce_pieces(ring, own_far, own_near, other_far, other_near):
    rows = own_far.shape[0]
    half = rows // 2
    middle = ring.chips // 2
    got_far = ring.sibling(other_far)
    got_near = ring.sibling(other_near)

    def far(start):
        return own_far[start : start + half].astype(F32) + got_far[start : start + half].astype(F32)

    def near(offset):
        offset %= ring.chips
        at = offset - (offset > middle)
        return own_near[at].astype(F32) + got_near[at * rows : (at + 1) * rows].astype(F32)

    up = ring.hop(far(0).astype(BF16), 1)
    down = ring.hop(far(half).astype(BF16), -1)
    for step in range(middle - 1, 0, -1):
        to_up, to_down = near(step), near(-step)
        if step == middle - 1:
            to_up = jnp.concatenate([to_up[:half] + up.astype(F32), to_up[half:]])
            to_down = jnp.concatenate([to_down[:half], to_down[half:] + down.astype(F32)])
        else:
            to_up, to_down = to_up + up.astype(F32), to_down + down.astype(F32)
        up, down = ring.hop(to_up.astype(BF16), 1), ring.hop(to_down.astype(BF16), -1)
    if middle == 1:
        return (near(0) + jnp.concatenate([up, down]).astype(F32)).astype(BF16)
    return (near(0) + up.astype(F32) + down.astype(F32)).astype(BF16)


def exchange(blocks):
    size = len(blocks)
    got = [blocks[0]] + [None] * (size - 1)
    for u in range(1, size):
        got[(size - u) % size] = lax.ppermute(blocks[u], "rep", [(i, (i + u) % size) for i in range(size)])
    return got


def masked_tiles(tiles, i, count):
    found = []
    for k in range(tiles.shape[1]):
        tile = tiles[i, k]
        found.append(jnp.where(k < count, tile, jnp.zeros_like(tile)))
    return jnp.concatenate(found, axis=1)


def step_spec(blocks, slots, tile_size, parts, per_step, skip):
    def index(t, cols, cnt, meta):
        return (lax.rem(meta[0] + t, parts) * (blocks // parts // per_step) + skip, 0, 0, 0)

    return pl.BlockSpec((per_step, slots, tile_size, tile_size), index)


def aligned(start, size, unit):
    return pl.ds(pl.multiple_of(start, unit), size)


def spmm_kernel(n_pieces, per_part, skip, cols, counts, meta, tiles, *refs):
    parts = pl.num_programs(0)
    n_outs = len(refs) - n_pieces - 3
    pieces, outs = refs[:n_pieces], refs[n_pieces : n_pieces + n_outs]
    source, result, sems = refs[n_pieces + n_outs :]
    t = pl.program_id(0)
    per_step, slots, tile_size, _ = tiles.shape

    @pl.when(t == 0)
    def _():
        copies = []
        for p, piece in enumerate(pieces):
            copies.append(
                pltpu.make_async_copy(piece, source.at[aligned(meta[1 + p], piece.shape[0], tile_size)], sems.at[p])
            )
            copies[-1].start()
        for copy in copies:
            copy.wait()

    for i in range(per_step):
        b = lax.rem(meta[0] + t, parts) * per_part + skip * per_step + i
        right = [source[aligned(cols[b, k] * tile_size, tile_size, tile_size), :] for k in range(slots)]
        product = jnp.dot(
            masked_tiles(tiles, i, counts[b]), jnp.concatenate(right, axis=0), preferred_element_type=F32
        )
        result[i * tile_size : (i + 1) * tile_size, :] = product.astype(BF16)

    for u in range(n_outs):

        @pl.when(t == u)
        def _():
            outs[u][...] = result[...]


def spmm(tiles, columns, counts, me, pieces, parts, cut, skip):
    blocks, slots, tile_size, _ = tiles.shape
    width = pieces[0][1].shape[1]
    total_rows = sum(v.shape[0] for _, v in pieces)
    per_part = blocks // parts
    per_step = per_part // cut
    rows = per_step * tile_size
    meta = jnp.stack([me] + [start for start, _ in pieces]).astype(jnp.int32)
    return pl.pallas_call(
        functools.partial(spmm_kernel, len(pieces), per_part, skip),
        grid_spec=pltpu.PrefetchScalarGridSpec(
            num_scalar_prefetch=3,
            grid=(parts,),
            in_specs=[step_spec(blocks, slots, tile_size, parts, per_step, skip)] + [any_spec()] * len(pieces),
            out_specs=[pl.BlockSpec((rows, width), lambda t, cols, cnt, meta: (0, 0))] * parts,
            scratch_shapes=[
                pltpu.VMEM((total_rows, width), BF16),
                pltpu.VMEM((rows, width), BF16),
                pltpu.SemaphoreType.DMA((len(pieces),)),
            ],
        ),
        out_shape=[jax.ShapeDtypeStruct((rows, width), BF16)] * parts,
        compiler_params=params(),
        cost_estimate=pl.CostEstimate(
            flops=2 * parts * rows * slots * tile_size * width,
            bytes_accessed=2 * (tiles.size // cut + total_rows * width),
            transcendentals=0,
        ),
        name="spmm",
    )(columns, counts, meta, tiles, *[v for _, v in pieces])


def spmm_t_kernel(n_grads, per_part, n_outs, terms, cols, counts, meta, tiles, *refs):
    parts = pl.num_programs(0)
    grads, outs = refs[:n_grads], refs[n_grads : n_grads + n_outs]
    total, grad, stage, in_sems, out_sems = refs[n_grads + n_outs :]
    t = pl.program_id(0)
    per_step, slots, tile_size, _ = tiles.shape
    width = grad.shape[1]
    rows = stage.shape[1]

    @pl.when(t == 0)
    def _():
        copies, start = [], 0
        for g, ref in enumerate(grads):
            copies.append(pltpu.make_async_copy(ref, grad.at[pl.ds(start, ref.shape[0])], in_sems.at[g]))
            copies[-1].start()
            start += ref.shape[0]

        @pl.loop(0, total.shape[0] // tile_size, unroll=8)
        def _(i):
            total[aligned(i * tile_size, tile_size, tile_size), :] = jnp.zeros((tile_size, width), F32)

        for copy in copies:
            copy.wait()

    for i in range(per_step):
        b = lax.rem(meta[0] + t, parts) * per_part + i
        block = grad[aligned((t * per_step + i) * tile_size, tile_size, tile_size), :]
        part = lax.dot_general(
            masked_tiles(tiles, i, counts[b]), block, (((0,), (0,)), ((), ())), preferred_element_type=F32
        )
        for k in range(slots):
            total[aligned(cols[b, k] * tile_size, tile_size, tile_size), :] += part[k * tile_size : (k + 1) * tile_size]

    @pl.when(t == parts - 1)
    def _():
        copies = []
        for o, (out, at) in enumerate(terms):
            slot = o % 2
            if o >= 2:
                copies[o - 2].wait()

            @pl.loop(0, rows // tile_size, unroll=4)
            def _(i):
                start = aligned(meta[1 + o] + i * tile_size, tile_size, tile_size)
                stage[slot, aligned(i * tile_size, tile_size, tile_size), :] = total[start, :].astype(BF16)

            copies.append(
                pltpu.make_async_copy(stage.at[slot], outs[out].at[pl.ds(at * rows, rows)], out_sems.at[o])
            )
            copies[o].start()
        for copy in copies[-2:]:
            copy.wait()


def spmm_t(tiles, columns, counts, me, grads, parts, wanted, rows, total_rows):
    blocks, slots, tile_size, _ = tiles.shape
    width = grads[0].shape[1]
    per_part = blocks // parts
    flat = [(out, at) for out, starts in enumerate(wanted) for at in range(len(starts))]
    meta = jnp.stack([me] + [start for starts in wanted for start in starts]).astype(jnp.int32)
    return pl.pallas_call(
        functools.partial(spmm_t_kernel, len(grads), per_part, len(wanted), flat),
        grid_spec=pltpu.PrefetchScalarGridSpec(
            num_scalar_prefetch=3,
            grid=(parts,),
            in_specs=[step_spec(blocks, slots, tile_size, parts, per_part, 0)] + [any_spec()] * len(grads),
            out_specs=[any_spec()] * len(wanted),
            scratch_shapes=[
                pltpu.VMEM((total_rows, width), F32),
                pltpu.VMEM((rows, width), BF16),
                pltpu.VMEM((2, rows, width), BF16),
                pltpu.SemaphoreType.DMA((len(grads),)),
                pltpu.SemaphoreType.DMA((len(flat),)),
            ],
        ),
        out_shape=[jax.ShapeDtypeStruct((len(starts) * rows, width), BF16) for starts in wanted],
        compiler_params=params(),
        cost_estimate=pl.CostEstimate(
            flops=2 * blocks * slots * tile_size * tile_size * width,
            bytes_accessed=2 * (tiles.size + total_rows * width),
            transcendentals=0,
        ),
        name="spmm_t",
    )(columns, counts, meta, tiles, *grads)


def dense_kernel(parts, chunks, meta, *refs):
    n_mixed = parts * chunks
    mixed_refs, cot_refs, w_hbm = refs[:n_mixed], refs[n_mixed : n_mixed + parts], refs[n_mixed + parts]
    outs = refs[n_mixed + parts + 1 :]
    act_outs, mg_outs = outs[:parts], outs[parts : parts + n_mixed]
    mixed_out, grad_out, weight, sems = outs[parts + n_mixed :]
    f_wide, h_wide = weight.shape[0] // parts, weight.shape[1] // parts
    width = f_wide // chunks
    me = meta[0]

    def place(u):
        return lax.rem(me + u, parts)

    @pl.when(pl.program_id(0) == 0)
    def _():
        copies = []
        for i in range(parts):
            src = w_hbm.at[aligned(place(i) * f_wide, f_wide, f_wide)]
            copies.append(pltpu.make_async_copy(src, weight.at[pl.ds(i * f_wide, f_wide)], sems.at[i]))
            copies[-1].start()
        for copy in copies:
            copy.wait()

    mixed = jnp.concatenate([ref[...] for ref in mixed_refs], axis=1)
    for u in range(parts):
        at = pl.ds(pl.multiple_of(place(u) * f_wide, f_wide), f_wide)
        mixed_out[:, at] = mixed[:, u * f_wide : (u + 1) * f_wide]
    grads = []
    for u in range(parts):
        preact = jnp.dot(mixed, weight[:, u * h_wide : (u + 1) * h_wide], preferred_element_type=F32)
        sig = jax.nn.sigmoid(preact)
        act_outs[u][...] = (preact * sig).astype(BF16)
        grads.append((cot_refs[u][...].astype(F32) * sig * (1.0 + preact * (1.0 - sig))).astype(BF16))
        at = pl.ds(pl.multiple_of(place(u) * h_wide, h_wide), h_wide)
        grad_out[:, at] = grads[u]
    grad = jnp.concatenate(grads, axis=1)
    back = lax.dot_general(grad, weight[...], (((1,), (1,)), ((), ())), preferred_element_type=F32).astype(BF16)
    for i in range(n_mixed):
        mg_outs[i][...] = back[:, i * width : (i + 1) * width]


def dense(me, mixed, cot, weight, rows, first):
    parts, chunks = len(mixed), len(mixed[0])
    width = mixed[0][0][0].shape[1]
    features, hidden = weight.shape
    h_wide = hidden // parts
    step = min(rows, 256)

    def spec(w, start=0):
        return pl.BlockSpec((step, w), lambda t, meta: (t + start // step, 0))

    flat = [m for row in mixed for m in row]
    outs = pl.pallas_call(
        functools.partial(dense_kernel, parts, chunks),
        grid_spec=pltpu.PrefetchScalarGridSpec(
            num_scalar_prefetch=1,
            grid=(rows // step,),
            in_specs=[spec(width, at) for _, at in flat] + [spec(h_wide, first)] * parts + [any_spec()],
            out_specs=[spec(h_wide)] * parts + [spec(width)] * (parts * chunks) + [spec(features), spec(hidden)],
            scratch_shapes=[pltpu.VMEM((features, hidden), BF16), pltpu.SemaphoreType.DMA((parts,))],
        ),
        out_shape=[jax.ShapeDtypeStruct((rows, h_wide), BF16)] * parts
        + [jax.ShapeDtypeStruct((rows, width), BF16)] * (parts * chunks)
        + [jax.ShapeDtypeStruct((rows, features), BF16), jax.ShapeDtypeStruct((rows, hidden), BF16)],
        compiler_params=params(),
        cost_estimate=pl.CostEstimate(
            flops=4 * rows * features * hidden,
            bytes_accessed=2 * (features * hidden + 6 * rows * hidden),
            transcendentals=rows * hidden,
        ),
        name="dense",
    )(me[None].astype(jnp.int32), *[m for m, _ in flat], *cot, weight)
    n = parts * chunks
    act, back = outs[:parts], outs[parts : parts + n]
    return act, [back[u * chunks : (u + 1) * chunks] for u in range(parts)], outs[-2], outs[-1]


def local(features, tiles, columns, counts, weight, cotangent):
    rows, f_wide = features.shape
    h_wide = cotangent.shape[1]
    row_size, parts = lax.axis_size("row"), lax.axis_size("rep")
    ring = Ring(row_size)
    rep = lax.axis_index("rep")
    chunks = f_wide // LANES if f_wide % LANES == 0 else 1
    width = f_wide // chunks
    part_rows = rows // parts
    halves = 2
    half_rows = part_rows // halves

    def part_of(x, u):
        return lax.dynamic_slice_in_dim(x, lax.rem(rep + u, parts) * part_rows, part_rows, 0)

    share = weight.shape[0] // row_size
    w_share = lax.dynamic_slice_in_dim(weight, lax.axis_index("row") * share, share, 0)
    w_share = exchange([w_share] * parts)
    cot = exchange([after(part_of(cotangent, u), *w_share[1:2]) for u in range(parts)])

    pieces = gather_chunks(ring, [features[:, c * width : (c + 1) * width] for c in range(chunks)])
    w_share = after(jnp.concatenate(w_share, axis=1), pieces[-1][2][1])
    w_full = lax.all_gather(w_share, "row", axis=0, tiled=True)

    mixed = []
    for c in range(chunks):
        if c < chunks - 1:
            got = exchange(spmm(tiles, columns, counts, rep, pieces[c], parts, 1, 0))
            mixed.append([[(v, h * half_rows) for v in got] for h in range(halves)])
        else:
            got = [exchange(spmm(tiles, columns, counts, rep, pieces[c], parts, halves, h)) for h in range(halves)]
            mixed.append([[(v, 0) for v in got[h]] for h in range(halves)])

    act, back, weight_terms = [], [], 0.0
    for h in range(halves):
        blocks = [[mixed[c][h][u] for c in range(chunks)] for u in range(parts)]
        act_h, back_h, mixed_h, grad_h = dense(rep, blocks, cot, w_full, half_rows, h * half_rows)
        act.append(act_h)
        back.append(back_h)
        weight_terms += lax.dot_general(mixed_h, grad_h, (((0,), (0,)), ((), ())), preferred_element_type=F32)

    weight_terms = lax.psum_scatter(weight_terms.astype(BF16), "row", scatter_dimension=1, tiled=True)
    weight_grad = lax.psum_scatter(weight_terms, "rep", scatter_dimension=0, tiled=True).astype(F32)

    middle = ring.chips // 2
    near = [o for o in range(ring.chips) if o != middle]
    wanted = [
        [ring.device_at(o, other) * rows for o in offsets]
        for other in (False, True)
        for offsets in [[middle]] + ([[o] for o in near] if not other else [near])
    ]
    gate = ()
    feature_grad = []
    for c in range(chunks):
        got = []
        for h in range(halves):
            got.append(exchange([after(back[h][u][c], *gate) for u in range(parts)]))
        gate = got[0][1:]
        grads = [got[h][u] for u in range(parts) for h in range(halves)]
        terms = spmm_t(tiles, columns, counts, rep, grads, parts, wanted, rows, rows * row_size)
        feature_grad.append(reduce_pieces(ring, terms[0], terms[1 : 1 + len(near)], terms[-2], terms[-1]))
    feature_grad = jnp.concatenate(feature_grad, axis=1)

    activations = jnp.zeros((rows, h_wide), BF16)
    for h in range(halves):
        for u, value in enumerate(exchange([after(a, *gate) for a in act[h]])):
            start = lax.rem(rep + u, parts) * part_rows + h * half_rows
            activations = lax.dynamic_update_slice_in_dim(activations, value, start, 0)
    return (activations, feature_grad, weight_grad)


def solution(mesh):
    in_specs = (
        P("row", "rep"),
        P("row", None, None, None),
        P("row", None),
        P("row"),
        P(None, "rep"),
        P("row", "rep"),
    )
    out_specs = (P("row", "rep"), P("row", "rep"), P("rep", "row"))
    return jax.shard_map(local, mesh=mesh, in_specs=in_specs, out_specs=out_specs, check_vma=False)
```

time: 454 us -> 405 us (0.89)
  Pallas kernels: 140 us -> 85.8 us
  starting transfers between devices: 48.4 us -> 83.3 us
  local copies, waits for them, and re-layouts: 45 us -> 28.2 us
  blocking collectives: 15.1 us -> 0 us
  waiting for transfers between devices: 150 us -> 158 us
    pallas_call x4 -> x5, Pallas kernels: 130 us -> 71.6 us  [the longest x3 36.6 us: spmm(): pl.pallas_call(functools.partial(spmm_kernel, len(pieces), per_part, skip...]
    ppermute x18 -> x33, waiting for transfers between devices: 18.1 us -> 53.3 us  [exchange(): lax.ppermute(blocks[u], 'rep', [(i, (i + u) % size) for i in range(size)])]
    ppermute x18 -> x33, starting transfers between devices: 25.9 us -> 59.4 us  [exchange(): lax.ppermute(blocks[u], 'rep', [(i, (i + u) % size) for i in range(size)])]
    ppermute x16 -> x20, waiting for transfers between devices: 127 us -> 104 us  [hop(): return lax.ppermute(value, 'row', self.perm(step))]
    unnamed x86 -> x147, local copies, waits for them, and re-layouts: 30.1 us -> 11.3 us
    all_gather x1 -> x0, blocking collectives: 15.1 us -> none  [local(): lax.all_gather(w_share, 'rep', axis=1, tiled=True)]
    transpose x1 -> x0, other arithmetic: 14 us -> none  [local(): jnp.swapaxes(jnp.where(alive[:, :, None, None], tiles, jnp.zeros((), tile...]
    convert_element_type x2 -> x4, other arithmetic: 3.08 us -> 8.7 us  [the longest x2 4.95 us: reduce_pieces(): return (near(0) + up.astype(F32) + down.astype(F32)).astype(BF16)]
  transfers between devices with their start and end apart: 55 -> 74, of which waited for: 16 -> 25; matrix products, arithmetic and copies ran while one was open for 15% -> 10% of each run, Pallas kernels for 29% -> 21%
where the time goes in v2:
time: 405 us; the launch traced here: 404 us
  waiting for transfers between devices  158 us (39%)
  Pallas kernels  85.8 us (21%)
  starting transfers between devices  83.3 us (21%)
  local copies, waits for them, and re-layouts  28.2 us (7%)
  other arithmetic  23.1 us (6%)
  between operations  22.4 us (6%)
    ppermute x20, waiting for transfers between devices, hop(): return lax.ppermute(value, 'row', self.perm(step))  104 us
    ppermute x33, starting transfers between devices, exchange(): lax.ppermute(blocks[u], 'rep', [(i, (i + u) % size) for i in range(size)])  59.4 us
    ppermute x33, waiting for transfers between devices, exchange(): lax.ppermute(blocks[u], 'rep', [(i, (i + u) % size) for i in range(size)])  53.3 us
    pallas_call x3, Pallas kernels, spmm(): pl.pallas_call(functools.partial(spmm_kernel, len(pieces), per_part, skip...  36.6 us
    pallas_call x2, Pallas kernels, spmm_t(): pl.pallas_call(functools.partial(spmm_t_kernel, len(grads), per_part, len...  35.1 us
    ppermute x20, starting transfers between devices, hop(): return lax.ppermute(value, 'row', self.perm(step))  21.3 us
    pallas_call x2, Pallas kernels, dense(): pl.pallas_call(functools.partial(dense_kernel, parts, chunks), grid_spec=...  14.2 us
    unnamed x147, local copies, waits for them, and re-layouts  11.3 us
  transfers between devices with their start and end apart: 74, of which 25 were waited for; matrix products, arithmetic and copies ran while one was open for 10% of the time, Pallas kernels for 21%

profile of v2, /device:TPU:0, one launch (start us, length us, event | category | flops | bytes accessed | tf_op | source)
XLA Modules:
  0.0 404.0 jit_solution(2185895310267049552)
XLA Ops:
  7.2 2.8 fusion.4
  10.0 2.9 collective-permute-start.5
  13.0 11.9 %collective-permute-done.5.refs_6_ = bf16[2048,128]{1,0:T(8,128)(2,1)S(1)} collective-permute-done((bf16[2048,128]{1,0:T(8,128)(2,1)S(1)}, bf16[2048,128]{1,0:T(8,128)(2,1)S(1)}, u32[]{:S(2)}, u32[]{:S(2)}) %collective-permute-start.5) | collective-permute-done | bytes 524320 | tf_op jit(solution)/shard_map/ppermute | solution.py:38
  28.7 3.7 collective-permute-start.32
  35.4 2.1 collective-permute-done.36
  39.1 3.1 collective-permute-done.14.refs_2_
  44.2 3.1 constant_dynamic-slice_fusion.4
  47.4 3.6 collective-permute-start.33
  54.1 8.4 %collective-permute-done.33.refs_9_ = bf16[1024,256]{1,0:T(8,128)(2,1)S(1)} collective-permute-done((bf16[1024,256]{1,0:T(8,128)(2,1)S(1)}, bf16[1024,256]{1,0:T(8,128)(2,1)S(1)}, u32[]{:S(2)}, u32[]{:S(2)}) %collective-permute-start.33) | collective-permute-done | bytes 524320 | tf_op jit(solution)/shard_map/ppermute | solution.py:113
  64.1 4.2 %collective-permute-done.16.refs_4_ = bf16[2048,128]{1,0:T(8,128)(2,1)S(1)} collective-permute-done((bf16[2048,128]{1,0:T(8,128)(2,1)S(1)}, bf16[2048,128]{1,0:T(8,128)(2,1)S(1)}, u32[]{:S(2)}, u32[]{:S(2)}) %collective-permute-start.16) | collective-permute-done | bytes 524320 | tf_op jit(solution)/shard_map/ppermute | solution.py:38
  69.3 15.3 %collective-permute-done.20.refs_8_ = bf16[2048,128]{1,0:T(8,128)(2,1)} collective-permute-done((bf16[2048,128]{1,0:T(8,128)(2,1)}, bf16[2048,128]{1,0:T(8,128)(2,1)}, u32[]{:S(2)}, u32[]{:S(2)}) %collective-permute-start.20) | collective-permute-done | bytes 524320 | tf_op jit(solution)/shard_map/ppermute | solution.py:38
  85.3 10.2 %collective-permute-done.11.refs_12_ = bf16[2048,128]{1,0:T(8,128)(2,1)S(1)} collective-permute-done((bf16[2048,128]{1,0:T(8,128)(2,1)}, bf16[2048,128]{1,0:T(8,128)(2,1)S(1)}, u32[]{:S(2)}, u32[]{:S(2)}) %collective-permute-start.11) | collective-permute-done | bytes 524320 | tf_op jit(solution)/shard_map/ppermute | solution.py:38
  98.4 11.4 %collective-permute-done.22.refs_10_ = bf16[2048,128]{1,0:T(8,128)(2,1)S(1)} collective-permute-done((bf16[2048,128]{1,0:T(8,128)(2,1)S(1)}, bf16[2048,128]{1,0:T(8,128)(2,1)S(1)}, u32[]{:S(2)}, u32[]{:S(2)}) %collective-permute-start.22) | collective-permute-done | bytes 524320 | tf_op jit(solution)/shard_map/ppermute | solution.py:38
  124.3 14.5 %spmm.3 = (bf16[1024,128]{1,0:T(8,128)(2,1)}, bf16[1024,128]{1,0:T(8,128)(2,1)}, bf16[1024,128]{1,0:T(8,128)(2,1)}, bf16[1024,128]{1,0:T(8,128)(2,1)}) custom-call(s32[32,16]{1,0:T(8,128)} %copy.86.cols, s32[32]{0:T(128)} %counts.9, s32[15]{0:T(128)} %stack.160.meta, bf16[32,16,128,128]{3,2,1,0:T(8,128)(2,1)} %tiles.9, ...), custom_call_target="tpu_custom_call" | custom-call | flops 2147483648 | bytes 25165824 | tf_op jit(solution)/shard_map/spmm/pallas_call | solution.py:178
  138.9 3.4 collective-permute-start.26
  143.0 11.0 %spmm.5 = (bf16[512,128]{1,0:T(8,128)(2,1)}, bf16[512,128]{1,0:T(8,128)(2,1)}, bf16[512,128]{1,0:T(8,128)(2,1)}, bf16[512,128]{1,0:T(8,128)(2,1)}) custom-call(s32[32,16]{1,0:T(8,128)} %copy.86.cols, s32[32]{0:T(128)} %counts.9, s32[15]{0:T(128)} %stack.160.meta, bf16[32,16,128,128]{3,2,1,0:T(8,128)(2,1)} %tiles.9, bf16[4096,128]{1,0:T(8,128)(2,1)} %copy-done.2, ...), custom_call_target="tpu_custom_call" | custom-call | flops 1073741824 | bytes 16777216 | tf_op jit(solution)/shard_map/spmm/pallas_call | solution.py:178
  154.0 3.7 collective-permute-start.47
  157.7 4.2 %collective-permute-start.48 = (bf16[512,128]{1,0:T(8,128)(2,1)}, bf16[512,128]{1,0:T(8,128)(2,1)S(1)}, u32[]{:S(2)}, u32[]{:S(2)}) collective-permute-start(bf16[512,128]{1,0:T(8,128)(2,1)} %get-tuple-element.112), channel_id=1, source_target_pairs={{0,2},{1,3},{2,0},{3,1},{4,6},{5,7},{6,4},{7,5},{8,10},{9,11},{10,... | collective-permute-start | bytes 393224 | tf_op jit(solution)/shard_map/ppermute | solution.py:113
  161.9 9.4 %collective-permute-start.49 = (bf16[512,128]{1,0:T(8,128)(2,1)}, bf16[512,128]{1,0:T(8,128)(2,1)S(1)}, u32[]{:S(2)}, u32[]{:S(2)}) collective-permute-start(bf16[512,128]{1,0:T(8,128)(2,1)} %get-tuple-element.113), channel_id=1, source_target_pairs={{0,1},{1,2},{2,3},{3,0},{4,5},{5,6},{6,7},{7,4},{8,9},{9,10},{10,1... | collective-permute-start | bytes 393224 | tf_op jit(solution)/shard_map/ppermute | solution.py:113
  172.6 11.0 %spmm.4 = (bf16[512,128]{1,0:T(8,128)(2,1)}, bf16[512,128]{1,0:T(8,128)(2,1)}, bf16[512,128]{1,0:T(8,128)(2,1)}, bf16[512,128]{1,0:T(8,128)(2,1)}) custom-call(s32[32,16]{1,0:T(8,128)} %copy.86.cols, s32[32]{0:T(128)} %counts.9, s32[15]{0:T(128)} %stack.160.meta, bf16[32,16,128,128]{3,2,1,0:T(8,128)(2,1)} %tiles.9, bf16[4096,128]{1,0:T(8,128)(2,1)} %copy-done.2, ...), custom_call_target="tpu_custom_call" | custom-call | flops 1073741824 | bytes 16777216 | tf_op jit(solution)/shard_map/spmm/pallas_call | solution.py:178
  186.5 7.1 %dense.3 = (bf16[512,256]{1,0:T(8,128)(2,1)}, bf16[512,256]{1,0:T(8,128)(2,1)}, bf16[512,256]{1,0:T(8,128)(2,1)}, bf16[512,256]{1,0:T(8,128)(2,1)}, bf16[512,128...) custom-call(s32[1]{0:T(128)} %bitcast.meta, ...), custom_call_target="tpu_custom_call" | custom-call | flops 2147483648 | bytes 8388608 | tf_op jit(solution)/shard_map/dense/pallas_call | solution.py:340
  193.6 3.3 collective-permute-start.53
  199.3 7.1 %dense.2 = (bf16[512,256]{1,0:T(8,128)(2,1)}, bf16[512,256]{1,0:T(8,128)(2,1)}, bf16[512,256]{1,0:T(8,128)(2,1)}, bf16[512,256]{1,0:T(8,128)(2,1)}, bf16[512,128...) custom-call(s32[1]{0:T(128)} %bitcast.meta, ...), custom_call_target="tpu_custom_call" | custom-call | flops 2147483648 | bytes 8388608 | tf_op jit(solution)/shard_map/dense/pallas_call | solution.py:340
  206.4 2.4 collective-permute-start.38
  212.9 2.6 copy.91
  215.7 4.5 %collective-permute-done.39.refs_4_ = bf16[512,128]{1,0:T(8,128)(2,1)S(1)} collective-permute-done((bf16[512,128]{1,0:T(8,128)(2,1)}, bf16[512,128]{1,0:T(8,128)(2,1)S(1)}, u32[]{:S(2)}, u32[]{:S(2)}) %collective-permute-start.39) | collective-permute-done | bytes 131104 | tf_op jit(solution)/shard_map/ppermute | solution.py:113
  221.5 17.7 %spmm_t.2 = (bf16[4096,128]{1,0:T(8,128)(2,1)}, bf16[4096,128]{1,0:T(8,128)(2,1)}, bf16[4096,128]{1,0:T(8,128)(2,1)}, bf16[4096,128]{1,0:T(8,128)(2,1)}, bf16[40...) custom-call(s32[32,16]{1,0:T(8,128)} %copy.86.cols, s32[32]{0:T(128)} %counts.9, s32[9]{0:T(128)} %stack.184.meta, ...), custom_call_target="tpu_custom_call" | custom-call | flops 2147483648 | bytes 25165824 | tf_op jit(solution)/shard_map/spmm_t/pallas_call | solution.py:262
  240.4 2.8 collective-permute-start.41
  243.8 3.9 collective-permute-done.43.refs_6_
  247.6 4.8 %collective-permute-done.42.refs_4_ = bf16[512,128]{1,0:T(8,128)(2,1)S(1)} collective-permute-done((bf16[512,128]{1,0:T(8,128)(2,1)S(1)}, bf16[512,128]{1,0:T(8,128)(2,1)S(1)}, u32[]{:S(2)}, u32[]{:S(2)}) %collective-permute-start.42) | collective-permute-done | bytes 131104 | tf_op jit(solution)/shard_map/ppermute | solution.py:113
  252.4 3.7 collective-permute-start.62
  256.2 5.4 %collective-permute-start.46 = (bf16[512,256]{1,0:T(8,128)(2,1)}, bf16[512,256]{1,0:T(8,128)(2,1)S(1)}, u32[]{:S(2)}, u32[]{:S(2)}) collective-permute-start(bf16[512,256]{1,0:T(8,128)(2,1)} %get-tuple-element.109), channel_id=1, source_target_pairs={{0,1},{1,2},{2,3},{3,0},{4,5},{5,6},{6,7},{7,4},{8,9},{9,10},{10,1... | collective-permute-start | bytes 786440 | tf_op jit(solution)/shard_map/ppermute | solution.py:113
  261.6 13.3 %collective-permute-done.63.refs_5_ = bf16[512,128]{1,0:T(8,128)(2,1)} collective-permute-done((bf16[512,128]{1,0:T(8,128)(2,1)}, bf16[512,128]{1,0:T(8,128)(2,1)}, u32[]{:S(2)}, u32[]{:S(2)}) %collective-permute-start.63) | collective-permute-done | bytes 131104 | tf_op jit(solution)/shard_map/ppermute | solution.py:113
  275.0 17.3 %spmm_t.3 = (bf16[4096,128]{1,0:T(8,128)(2,1)}, bf16[4096,128]{1,0:T(8,128)(2,1)}, bf16[4096,128]{1,0:T(8,128)(2,1)}, bf16[4096,128]{1,0:T(8,128)(2,1)}, bf16[40...) custom-call(s32[32,16]{1,0:T(8,128)} %copy.86.cols, s32[32]{0:T(128)} %counts.9, s32[9]{0:T(128)} %stack.184.meta, ...), custom_call_target="tpu_custom_call" | custom-call | flops 2147483648 | bytes 25165824 | tf_op jit(solution)/shard_map/spmm_t/pallas_call | solution.py:262
  295.3 4.3 %collective-permute-start.50 = (bf16[512,256]{1,0:T(8,128)(2,1)S(1)}, bf16[512,256]{1,0:T(8,128)(2,1)S(1)}, u32[]{:S(2)}, u32[]{:S(2)}) collective-permute-start(bf16[512,256]{1,0:T(8,128)(2,1)S(1)} %copy-done.58), channel_id=1, source_target_pairs={{0,3},{1,0},{2,1},{3,2},{4,7},{5,4},{6,5},{7,6},{8,11},{9,8},{10,9... | collective-permute-start | bytes 786440 | tf_op jit(solution)/shard_map/ppermute | solution.py:113
  301.8 4.5 %collective-permute-done.50 = bf16[512,256]{1,0:T(8,128)(2,1)S(1)} collective-permute-done((bf16[512,256]{1,0:T(8,128)(2,1)S(1)}, bf16[512,256]{1,0:T(8,128)(2,1)S(1)}, u32[]{:S(2)}, u32[]{:S(2)}) %collective-permute-start.50) | collective-permute-done | bytes 262176 | tf_op jit(solution)/shard_map/ppermute | solution.py:113
  307.0 10.8 %collective-permute-done.51 = bf16[512,256]{1,0:T(8,128)(2,1)S(1)} collective-permute-done((bf16[512,256]{1,0:T(8,128)(2,1)S(1)}, bf16[512,256]{1,0:T(8,128)(2,1)S(1)}, u32[]{:S(2)}, u32[]{:S(2)}) %collective-permute-start.51) | collective-permute-done | bytes 262176 | tf_op jit(solution)/shard_map/ppermute | solution.py:113
  319.3 2.5 add_convert_fusion.6
  325.1 1.8 copy.92
  328.0 2.0 convert_add_fusion.3
  330.0 6.9 %collective-permute-done.58 = bf16[2048,128]{1,0:T(8,128)(2,1)} collective-permute-done((bf16[2048,128]{1,0:T(8,128)(2,1)}, bf16[2048,128]{1,0:T(8,128)(2,1)}, u32[]{:S(2)}, u32[]{:S(2)}) %collective-permute-start.58) | collective-permute-done | bytes 524320 | tf_op jit(solution)/shard_map/ppermute | solution.py:38
  343.9 1.9 convert_add_fusion.1
  345.9 2.1 collective-permute-done.67
  355.6 15.0 %collective-permute-done.59 = bf16[4096,128]{1,0:T(8,128)(2,1)} collective-permute-done((bf16[4096,128]{1,0:T(8,128)(2,1)}, bf16[4096,128]{1,0:T(8,128)(2,1)}, u32[]{:S(2)}, u32[]{:S(2)}) %collective-permute-start.59) | collective-permute-done | bytes 1048608 | tf_op jit(solution)/shard_map/ppermute | solution.py:38
  370.6 3.7 collective-permute-done.61
  374.3 2.5 add_convert_fusion.2
  376.8 15.0 %collective-permute-done.68 = bf16[4096,128]{1,0:T(8,128)(2,1)} collective-permute-done((bf16[4096,128]{1,0:T(8,128)(2,1)}, bf16[4096,128]{1,0:T(8,128)(2,1)}, u32[]{:S(2)}, u32[]{:S(2)}) %collective-permute-start.68) | collective-permute-done | bytes 1048608 | tf_op jit(solution)/shard_map/ppermute | solution.py:38
  393.4 2.5 add_convert_fusion.1
  (297 shorter events, 70.2 us)
Async XLA Ops:
  7.2 178.7 %all-gather.2.cloned.1.call-start = ((), (), s32[]{:S(2)}) async-start(), calls=%async_computation.2 | async-start | bytes 2359296 | tf_op jit(solution)/shard_map/all_gather | solution.py:387
  10.0 14.9 %collective-permute-start.5 = (bf16[2048,128]{1,0:T(8,128)(2,1)S(1)}, bf16[2048,128]{1,0:T(8,128)(2,1)S(1)}, u32[]{:S(2)}, u32[]{:S(2)}) collective-permute-start(bf16[2048,128]{1,0:T(8,128)(2,1)S(1)} %get-tuple-element.166), channel_id=1, source_target_pairs={{0,8},{4,12},{8,24},{12,28},{24,16},{28,20},{16,0},{20,4},{1,9},{5... | collective-permute-start | bytes 1572872 | tf_op jit(solution)/shard_map/ppermute | solution.py:38
  27.1 15.1 %collective-permute-start.14 = (bf16[2048,128]{1,0:T(8,128)(2,1)}, bf16[2048,128]{1,0:T(8,128)(2,1)S(1)}, u32[]{:S(2)}, u32[]{:S(2)}) collective-permute-start(bf16[2048,128]{1,0:T(8,128)(2,1)} %get-tuple-element.79), channel_id=1, source_target_pairs={{0,8},{4,12},{8,24},{12,28},{24,16},{28,20},{16,0},{20,4},{1,9},{5... | collective-permute-start | bytes 1572872 | tf_op jit(solution)/shard_map/ppermute | solution.py:38
  33.3 18.7 %collective-permute-start.1 = (bf16[2048,128]{1,0:T(8,128)(2,1)}, bf16[2048,128]{1,0:T(8,128)(2,1)}, u32[]{:S(2)}, u32[]{:S(2)}) collective-permute-start(bf16[2048,128]{1,0:T(8,128)(2,1)} %copy-done.41), channel_id=1, source_target_pairs={{0,8},{4,12},{8,24},{12,28},{24,16},{28,20},{16,0},{20,4},{1,9},{5... | collective-permute-start | bytes 1572872 | tf_op jit(solution)/shard_map/ppermute | solution.py:38
  34.4 18.6 %collective-permute-start.3 = (bf16[2048,128]{1,0:T(8,128)(2,1)}, bf16[2048,128]{1,0:T(8,128)(2,1)}, u32[]{:S(2)}, u32[]{:S(2)}) collective-permute-start(bf16[2048,128]{1,0:T(8,128)(2,1)} %copy-done.40), channel_id=1, source_target_pairs={{0,16},{4,20},{8,0},{12,4},{24,8},{28,12},{16,24},{20,28},{1,17},{... | collective-permute-start | bytes 1572872 | tf_op jit(solution)/shard_map/ppermute | solution.py:38
  43.1 282.0 %reduce-scatter.7.cloned.1.call-start = ((), (), s32[]{:S(2)}) async-start(), calls=%async_computation.4 | async-start | bytes 2359296
  44.2 40.4 %collective-permute-start.13 = (bf16[4096,128]{1,0:T(8,128)(2,1)S(1)}, bf16[4096,128]{1,0:T(8,128)(2,1)S(1)}, u32[]{:S(2)}, u32[]{:S(2)}) collective-permute-start(bf16[4096,128]{1,0:T(8,128)(2,1)S(1)} %get-tuple-element.169.refs_0_), channel_id=1, source_target_pairs={{0,4},{4,0},{8,12},{12,8},{16,20},{20,16},{24,28},{28,24},{1,5},{5... | collective-permute-start | bytes 3145736 | tf_op jit(solution)/shard_map/ppermute | solution.py:41
  47.4 15.2 %collective-permute-start.33 = (bf16[1024,256]{1,0:T(8,128)(2,1)S(1)}, bf16[1024,256]{1,0:T(8,128)(2,1)S(1)}, u32[]{:S(2)}, u32[]{:S(2)}) collective-permute-start(bf16[1024,256]{1,0:T(8,128)(2,1)S(1)} %get-tuple-element.89), channel_id=1, source_target_pairs={{0,3},{1,0},{2,1},{3,2},{4,7},{5,4},{6,5},{7,6},{8,11},{9,8},{10,9... | collective-permute-start | bytes 1572872 | tf_op jit(solution)/shard_map/ppermute | solution.py:113
  51.0 17.3 %collective-permute-start.16 = (bf16[2048,128]{1,0:T(8,128)(2,1)S(1)}, bf16[2048,128]{1,0:T(8,128)(2,1)S(1)}, u32[]{:S(2)}, u32[]{:S(2)}) collective-permute-start(bf16[2048,128]{1,0:T(8,128)(2,1)S(1)} %copy-done.39), channel_id=1, source_target_pairs={{0,16},{4,20},{8,0},{12,4},{24,8},{28,12},{16,24},{20,28},{1,17},{... | collective-permute-start | bytes 1572872 | tf_op jit(solution)/shard_map/ppermute | solution.py:38
  52.1 17.1 %collective-permute-start.18 = (bf16[2048,128]{1,0:T(8,128)(2,1)S(1)}, bf16[2048,128]{1,0:T(8,128)(2,1)S(1)}, u32[]{:S(2)}, u32[]{:S(2)}) collective-permute-start(bf16[2048,128]{1,0:T(8,128)(2,1)S(1)} %copy-done.39), channel_id=1, source_target_pairs={{0,8},{4,12},{8,24},{12,28},{24,16},{28,20},{16,0},{20,4},{1,9},{5... | collective-permute-start | bytes 1572872 | tf_op jit(solution)/shard_map/ppermute | solution.py:38
  53.0 31.6 %collective-permute-start.20 = (bf16[2048,128]{1,0:T(8,128)(2,1)}, bf16[2048,128]{1,0:T(8,128)(2,1)}, u32[]{:S(2)}, u32[]{:S(2)}) collective-permute-start(bf16[2048,128]{1,0:T(8,128)(2,1)} %get-tuple-element.79), channel_id=1, source_target_pairs={{0,16},{4,20},{8,0},{12,4},{24,8},{28,12},{16,24},{20,28},{1,17},{... | collective-permute-start | bytes 1572872 | tf_op jit(solution)/shard_map/ppermute | solution.py:38
  62.5 22.6 %collective-permute-start.9 = (bf16[2048,128]{1,0:T(8,128)(2,1)}, bf16[2048,128]{1,0:T(8,128)(2,1)S(1)}, u32[]{:S(2)}, u32[]{:S(2)}) collective-permute-start(bf16[2048,128]{1,0:T(8,128)(2,1)} %collective-permute-done.1.refs_2_), channel_id=1, source_target_pairs={{0,8},{4,12},{8,24},{12,28},{24,16},{28,20},{16,0},{20,4},{1,9},{5... | collective-permute-start | bytes 1572872 | tf_op jit(solution)/shard_map/ppermute | solution.py:38
  68.3 27.1 %collective-permute-start.11 = (bf16[2048,128]{1,0:T(8,128)(2,1)}, bf16[2048,128]{1,0:T(8,128)(2,1)S(1)}, u32[]{:S(2)}, u32[]{:S(2)}) collective-permute-start(bf16[2048,128]{1,0:T(8,128)(2,1)} %collective-permute-done.3.refs_4_), channel_id=1, source_target_pairs={{0,16},{4,20},{8,0},{12,4},{24,8},{28,12},{16,24},{20,28},{1,17},{... | collective-permute-start | bytes 1572872 | tf_op jit(solution)/shard_map/ppermute | solution.py:38
  69.2 29.0 %collective-permute-start = (bf16[4096,128]{1,0:T(8,128)(2,1)S(1)}, bf16[4096,128]{1,0:T(8,128)(2,1)S(1)}, u32[]{:S(2)}, u32[]{:S(2)}) collective-permute-start(bf16[4096,128]{1,0:T(8,128)(2,1)S(1)} %copy-done.5), channel_id=1, source_target_pairs={{0,4},{4,0},{8,12},{12,8},{16,20},{20,16},{24,28},{28,24},{1,5},{5... | collective-permute-start | bytes 3145736 | tf_op jit(solution)/shard_map/ppermute | solution.py:41
  111.2 27.7 %collective-permute-start.21 = (bf16[2048,128]{1,0:T(8,128)(2,1)}, bf16[2048,128]{1,0:T(8,128)(2,1)S(1)}, u32[]{:S(2)}, u32[]{:S(2)}) collective-permute-start(bf16[2048,128]{1,0:T(8,128)(2,1)} %collective-permute-done.20.refs_8_), channel_id=1, source_target_pairs={{0,4},{4,0},{8,12},{12,8},{16,20},{20,16},{24,28},{28,24},{1,5},{5... | collective-permute-start | bytes 1572872 | tf_op jit(solution)/shard_map/ppermute | solution.py:41
  111.7 30.6 %collective-permute-start.23 = (bf16[2048,128]{1,0:T(8,128)(2,1)S(1)}, bf16[2048,128]{1,0:T(8,128)(2,1)}, u32[]{:S(2)}, u32[]{:S(2)}) collective-permute-start(bf16[2048,128]{1,0:T(8,128)(2,1)S(1)} %collective-permute-done.22.refs_10_), channel_id=1, source_target_pairs={{0,4},{4,0},{8,12},{12,8},{16,20},{20,16},{24,28},{28,24},{1,5},{5... | collective-permute-start | bytes 1572872 | tf_op jit(solution)/shard_map/ppermute | solution.py:41
  112.0 30.7 %collective-permute-start.25 = (bf16[2048,128]{1,0:T(8,128)(2,1)S(1)}, bf16[2048,128]{1,0:T(8,128)(2,1)}, u32[]{:S(2)}, u32[]{:S(2)}) collective-permute-start(bf16[2048,128]{1,0:T(8,128)(2,1)S(1)} %collective-permute-done.24.refs_12_), channel_id=1, source_target_pairs={{0,4},{4,0},{8,12},{12,8},{16,20},{20,16},{24,28},{28,24},{1,5},{5... | collective-permute-start | bytes 1572872 | tf_op jit(solution)/shard_map/ppermute | solution.py:41
  112.5 41.5 %collective-permute-start.34 = (bf16[1024,256]{1,0:T(8,128)(2,1)}, bf16[1024,256]{1,0:T(8,128)(2,1)}, u32[]{:S(2)}, u32[]{:S(2)}) collective-permute-start(bf16[1024,256]{1,0:T(8,128)(2,1)} %get-tuple-element.90), channel_id=1, source_target_pairs={{0,2},{1,3},{2,0},{3,1},{4,6},{5,7},{6,4},{7,5},{8,10},{9,11},{10,... | collective-permute-start | bytes 1572872 | tf_op jit(solution)/shard_map/ppermute | solution.py:113
  114.1 43.6 %collective-permute-start.35 = (bf16[1024,256]{1,0:T(8,128)(2,1)}, bf16[1024,256]{1,0:T(8,128)(2,1)}, u32[]{:S(2)}, u32[]{:S(2)}) collective-permute-start(bf16[1024,256]{1,0:T(8,128)(2,1)} %get-tuple-element.91), channel_id=1, source_target_pairs={{0,1},{1,2},{2,3},{3,0},{4,5},{5,6},{6,7},{7,4},{8,9},{9,10},{10,1... | collective-permute-start | bytes 1572872 | tf_op jit(solution)/shard_map/ppermute | solution.py:113
  138.9 23.1 %collective-permute-start.26 = (bf16[1024,128]{1,0:T(8,128)(2,1)}, bf16[1024,128]{1,0:T(8,128)(2,1)S(1)}, u32[]{:S(2)}, u32[]{:S(2)}) collective-permute-start(bf16[1024,128]{1,0:T(8,128)(2,1)} %get-tuple-element.82), channel_id=1, source_target_pairs={{0,3},{1,0},{2,1},{3,2},{4,7},{5,4},{6,5},{7,6},{8,11},{9,8},{10,9... | collective-permute-start | bytes 786440 | tf_op jit(solution)/shard_map/ppermute | solution.py:113
  142.3 41.3 %collective-permute-start.28 = (bf16[1024,128]{1,0:T(8,128)(2,1)}, bf16[1024,128]{1,0:T(8,128)(2,1)S(1)}, u32[]{:S(2)}, u32[]{:S(2)}) collective-permute-start(bf16[1024,128]{1,0:T(8,128)(2,1)} %get-tuple-element.84), channel_id=1, source_target_pairs={{0,2},{1,3},{2,0},{3,1},{4,6},{5,7},{6,4},{7,5},{8,10},{9,11},{10,... | collective-permute-start | bytes 786440 | tf_op jit(solution)/shard_map/ppermute | solution.py:113
  142.7 41.0 %collective-permute-start.30 = (bf16[1024,128]{1,0:T(8,128)(2,1)}, bf16[1024,128]{1,0:T(8,128)(2,1)S(1)}, u32[]{:S(2)}, u32[]{:S(2)}) collective-permute-start(bf16[1024,128]{1,0:T(8,128)(2,1)} %get-tuple-element.86), channel_id=1, source_target_pairs={{0,1},{1,2},{2,3},{3,0},{4,5},{5,6},{6,7},{7,4},{8,9},{9,10},{10,1... | collective-permute-start | bytes 786440 | tf_op jit(solution)/shard_map/ppermute | solution.py:113
  154.0 31.1 %collective-permute-start.47 = (bf16[512,128]{1,0:T(8,128)(2,1)}, bf16[512,128]{1,0:T(8,128)(2,1)S(1)}, u32[]{:S(2)}, u32[]{:S(2)}) collective-permute-start(bf16[512,128]{1,0:T(8,128)(2,1)} %get-tuple-element.111), channel_id=1, source_target_pairs={{0,3},{1,0},{2,1},{3,2},{4,7},{5,4},{6,5},{7,6},{8,11},{9,8},{10,9... | collective-permute-start | bytes 393224 | tf_op jit(solution)/shard_map/ppermute | solution.py:113
  157.7 28.1 %collective-permute-start.48 = (bf16[512,128]{1,0:T(8,128)(2,1)}, bf16[512,128]{1,0:T(8,128)(2,1)S(1)}, u32[]{:S(2)}, u32[]{:S(2)}) collective-permute-start(bf16[512,128]{1,0:T(8,128)(2,1)} %get-tuple-element.112), channel_id=1, source_target_pairs={{0,2},{1,3},{2,0},{3,1},{4,6},{5,7},{6,4},{7,5},{8,10},{9,11},{10,... | collective-permute-start | bytes 393224 | tf_op jit(solution)/shard_map/ppermute | solution.py:113
  161.9 23.9 %collective-permute-start.49 = (bf16[512,128]{1,0:T(8,128)(2,1)}, bf16[512,128]{1,0:T(8,128)(2,1)S(1)}, u32[]{:S(2)}, u32[]{:S(2)}) collective-permute-start(bf16[512,128]{1,0:T(8,128)(2,1)} %get-tuple-element.113), channel_id=1, source_target_pairs={{0,1},{1,2},{2,3},{3,0},{4,5},{5,6},{6,7},{7,4},{8,9},{9,10},{10,1... | collective-permute-start | bytes 393224 | tf_op jit(solution)/shard_map/ppermute | solution.py:113
  193.6 17.6 %collective-permute-start.53 = (bf16[512,128]{1,0:T(8,128)(2,1)}, bf16[512,128]{1,0:T(8,128)(2,1)S(1)}, u32[]{:S(2)}, u32[]{:S(2)}) collective-permute-start(bf16[512,128]{1,0:T(8,128)(2,1)} %get-tuple-element.124), channel_id=1, source_target_pairs={{0,3},{1,0},{2,1},{3,2},{4,7},{5,4},{6,5},{7,6},{8,11},{9,8},{10,9... | collective-permute-start | bytes 393224 | tf_op jit(solution)/shard_map/ppermute | solution.py:113
  196.9 18.8 %collective-permute-start.54 = (bf16[512,128]{1,0:T(8,128)(2,1)}, bf16[512,128]{1,0:T(8,128)(2,1)S(1)}, u32[]{:S(2)}, u32[]{:S(2)}) collective-permute-start(bf16[512,128]{1,0:T(8,128)(2,1)} %get-tuple-element.125), channel_id=1, source_target_pairs={{0,2},{1,3},{2,0},{3,1},{4,6},{5,7},{6,4},{7,5},{8,10},{9,11},{10,... | collective-permute-start | bytes 393224 | tf_op jit(solution)/shard_map/ppermute | solution.py:113
  196.9 18.8 %collective-permute-start.55 = (bf16[512,128]{1,0:T(8,128)(2,1)}, bf16[512,128]{1,0:T(8,128)(2,1)S(1)}, u32[]{:S(2)}, u32[]{:S(2)}) collective-permute-start(bf16[512,128]{1,0:T(8,128)(2,1)} %get-tuple-element.126), channel_id=1, source_target_pairs={{0,1},{1,2},{2,3},{3,0},{4,5},{5,6},{6,7},{7,4},{8,9},{9,10},{10,1... | collective-permute-start | bytes 393224 | tf_op jit(solution)/shard_map/ppermute | solution.py:113
  215.5 138.5 %reduce-scatter.5.cloned.1.call-start = ((), (), s32[]{:S(2)}) async-start(), calls=%async_computation.3 | async-start | bytes 327680 | tf_op jit(solution)/shard_map/reduce_scatter | solution.py:407
  239.2 87.6 %collective-permute-start.56 = (bf16[12288,128]{1,0:T(8,128)(2,1)}, bf16[12288,128]{1,0:T(8,128)(2,1)S(1)}, u32[]{:S(2)}, u32[]{:S(2)}) collective-permute-start(bf16[12288,128]{1,0:T(8,128)(2,1)} %get-tuple-element.128), channel_id=1, source_target_pairs={{0,4},{4,0},{8,12},{12,8},{16,20},{20,16},{24,28},{28,24},{1,5},{5... | collective-permute-start | bytes 9437192 | tf_op jit(solution)/shard_map/ppermute | solution.py:41
  240.4 15.7 %collective-permute-start.41 = (bf16[512,128]{1,0:T(8,128)(2,1)S(1)}, bf16[512,128]{1,0:T(8,128)(2,1)S(1)}, u32[]{:S(2)}, u32[]{:S(2)}) collective-permute-start(bf16[512,128]{1,0:T(8,128)(2,1)S(1)} %copy-done.62), channel_id=1, source_target_pairs={{0,3},{1,0},{2,1},{3,2},{4,7},{5,4},{6,5},{7,6},{8,11},{9,8},{10,9... | collective-permute-start | bytes 393224 | tf_op jit(solution)/shard_map/ppermute | solution.py:113
  247.6 27.3 %collective-permute-start.63 = (bf16[512,128]{1,0:T(8,128)(2,1)}, bf16[512,128]{1,0:T(8,128)(2,1)}, u32[]{:S(2)}, u32[]{:S(2)}) collective-permute-start(bf16[512,128]{1,0:T(8,128)(2,1)} %get-tuple-element.140), channel_id=1, source_target_pairs={{0,2},{1,3},{2,0},{3,1},{4,6},{5,7},{6,4},{7,5},{8,10},{9,11},{10,... | collective-permute-start | bytes 393224 | tf_op jit(solution)/shard_map/ppermute | solution.py:113
  252.4 22.5 %collective-permute-start.62 = (bf16[512,128]{1,0:T(8,128)(2,1)}, bf16[512,128]{1,0:T(8,128)(2,1)}, u32[]{:S(2)}, u32[]{:S(2)}) collective-permute-start(bf16[512,128]{1,0:T(8,128)(2,1)} %get-tuple-element.138), channel_id=1, source_target_pairs={{0,3},{1,0},{2,1},{3,2},{4,7},{5,4},{6,5},{7,6},{8,11},{9,8},{10,9... | collective-permute-start | bytes 393224 | tf_op jit(solution)/shard_map/ppermute | solution.py:113
  256.1 63.1 %collective-permute-start.57 = (bf16[4096,128]{1,0:T(8,128)(2,1)}, bf16[4096,128]{1,0:T(8,128)(2,1)}, u32[]{:S(2)}, u32[]{:S(2)}) collective-permute-start(bf16[4096,128]{1,0:T(8,128)(2,1)} %get-tuple-element.131), channel_id=1, source_target_pairs={{0,4},{4,0},{8,12},{12,8},{16,20},{20,16},{24,28},{28,24},{1,5},{5... | collective-permute-start | bytes 3145736 | tf_op jit(solution)/shard_map/ppermute | solution.py:41
  256.2 44.1 %collective-permute-start.46 = (bf16[512,256]{1,0:T(8,128)(2,1)}, bf16[512,256]{1,0:T(8,128)(2,1)S(1)}, u32[]{:S(2)}, u32[]{:S(2)}) collective-permute-start(bf16[512,256]{1,0:T(8,128)(2,1)} %get-tuple-element.109), channel_id=1, source_target_pairs={{0,1},{1,2},{2,3},{3,0},{4,5},{5,6},{6,7},{7,4},{8,9},{9,10},{10,1... | collective-permute-start | bytes 786440 | tf_op jit(solution)/shard_map/ppermute | solution.py:113
  274.9 20.4 %collective-permute-start.45 = (bf16[512,256]{1,0:T(8,128)(2,1)}, bf16[512,256]{1,0:T(8,128)(2,1)S(1)}, u32[]{:S(2)}, u32[]{:S(2)}) collective-permute-start(bf16[512,256]{1,0:T(8,128)(2,1)} %get-tuple-element.107), channel_id=1, source_target_pairs={{0,2},{1,3},{2,0},{3,1},{4,6},{5,7},{6,4},{7,5},{8,10},{9,11},{10,... | collective-permute-start | bytes 786440 | tf_op jit(solution)/shard_map/ppermute | solution.py:113
  274.9 19.6 %collective-permute-start.44 = (bf16[512,256]{1,0:T(8,128)(2,1)}, bf16[512,256]{1,0:T(8,128)(2,1)S(1)}, u32[]{:S(2)}, u32[]{:S(2)}) collective-permute-start(bf16[512,256]{1,0:T(8,128)(2,1)} %get-tuple-element.105), channel_id=1, source_target_pairs={{0,3},{1,0},{2,1},{3,2},{4,7},{5,4},{6,5},{7,6},{8,11},{9,8},{10,9... | collective-permute-start | bytes 786440 | tf_op jit(solution)/shard_map/ppermute | solution.py:113
  294.5 28.3 %collective-permute-start.66 = (bf16[4096,128]{1,0:T(8,128)(2,1)S(1)}, bf16[4096,128]{1,0:T(8,128)(2,1)S(1)}, u32[]{:S(2)}, u32[]{:S(2)}) collective-permute-start(bf16[4096,128]{1,0:T(8,128)(2,1)S(1)} %copy-done.55), channel_id=1, source_target_pairs={{0,4},{4,0},{8,12},{12,8},{16,20},{20,16},{24,28},{28,24},{1,5},{5... | collective-permute-start | bytes 3145736 | tf_op jit(solution)/shard_map/ppermute | solution.py:41
  300.3 17.5 %collective-permute-start.51 = (bf16[512,256]{1,0:T(8,128)(2,1)S(1)}, bf16[512,256]{1,0:T(8,128)(2,1)S(1)}, u32[]{:S(2)}, u32[]{:S(2)}) collective-permute-start(bf16[512,256]{1,0:T(8,128)(2,1)S(1)} %copy-done.57), channel_id=1, source_target_pairs={{0,2},{1,3},{2,0},{3,1},{4,6},{5,7},{6,4},{7,5},{8,10},{9,11},{10,... | collective-permute-start | bytes 786440 | tf_op jit(solution)/shard_map/ppermute | solution.py:113
  306.3 37.2 %collective-permute-start.65 = (bf16[12288,128]{1,0:T(8,128)(2,1)}, bf16[12288,128]{1,0:T(8,128)(2,1)}, u32[]{:S(2)}, u32[]{:S(2)}) collective-permute-start(bf16[12288,128]{1,0:T(8,128)(2,1)} %get-tuple-element.144), channel_id=1, source_target_pairs={{0,4},{4,0},{8,12},{12,8},{16,20},{20,16},{24,28},{28,24},{1,5},{5... | collective-permute-start | bytes 9437192 | tf_op jit(solution)/shard_map/ppermute | solution.py:41
  317.8 35.5 %collective-permute-start.52 = (bf16[512,256]{1,0:T(8,128)(2,1)}, bf16[512,256]{1,0:T(8,128)(2,1)S(1)}, u32[]{:S(2)}, u32[]{:S(2)}) collective-permute-start(bf16[512,256]{1,0:T(8,128)(2,1)} %get-tuple-element.121), channel_id=1, source_target_pairs={{0,1},{1,2},{2,3},{3,0},{4,5},{5,6},{6,7},{7,4},{8,9},{9,10},{10,1... | collective-permute-start | bytes 786440 | tf_op jit(solution)/shard_map/ppermute | solution.py:113
  321.7 15.1 %collective-permute-start.58 = (bf16[2048,128]{1,0:T(8,128)(2,1)}, bf16[2048,128]{1,0:T(8,128)(2,1)}, u32[]{:S(2)}, u32[]{:S(2)}) collective-permute-start(bf16[2048,128]{1,0:T(8,128)(2,1)} %get-tuple-element.157), channel_id=1, source_target_pairs={{0,8},{4,12},{8,24},{12,28},{24,16},{28,20},{16,0},{20,4},{1,9},{5... | collective-permute-start | bytes 1572872 | tf_op jit(solution)/shard_map/ppermute | solution.py:38
  322.8 16.9 %collective-permute-start.60 = (bf16[2048,128]{1,0:T(8,128)(2,1)}, bf16[2048,128]{1,0:T(8,128)(2,1)}, u32[]{:S(2)}, u32[]{:S(2)}) collective-permute-start(bf16[2048,128]{1,0:T(8,128)(2,1)} %get-tuple-element.158), channel_id=1, source_target_pairs={{0,16},{4,20},{8,0},{12,4},{24,8},{28,12},{16,24},{20,28},{1,17},{... | collective-permute-start | bytes 1572872 | tf_op jit(solution)/shard_map/ppermute | solution.py:38
  326.9 21.1 %collective-permute-start.67 = (bf16[2048,128]{1,0:T(8,128)(2,1)}, bf16[2048,128]{1,0:T(8,128)(2,1)S(1)}, u32[]{:S(2)}, u32[]{:S(2)}) collective-permute-start(bf16[2048,128]{1,0:T(8,128)(2,1)} %get-tuple-element.159), channel_id=1, source_target_pairs={{0,8},{4,12},{8,24},{12,28},{24,16},{28,20},{16,0},{20,4},{1,9},{5... | collective-permute-start | bytes 1572872 | tf_op jit(solution)/shard_map/ppermute | solution.py:38
  339.7 30.9 %collective-permute-start.59 = (bf16[4096,128]{1,0:T(8,128)(2,1)}, bf16[4096,128]{1,0:T(8,128)(2,1)}, u32[]{:S(2)}, u32[]{:S(2)}) collective-permute-start(bf16[4096,128]{1,0:T(8,128)(2,1)} %pad_maximum_fusion.1), channel_id=1, source_target_pairs={{0,8},{4,12},{8,24},{12,28},{24,16},{28,20},{16,0},{20,4},{1,9},{5... | collective-permute-start | bytes 3145736 | tf_op jit(solution)/shard_map/ppermute | solution.py:38
  343.4 30.9 %collective-permute-start.61 = (bf16[4096,128]{1,0:T(8,128)(2,1)}, bf16[4096,128]{1,0:T(8,128)(2,1)}, u32[]{:S(2)}, u32[]{:S(2)}) collective-permute-start(bf16[4096,128]{1,0:T(8,128)(2,1)} %pad_maximum_fusion.2), channel_id=1, source_target_pairs={{0,16},{4,20},{8,0},{12,4},{24,8},{28,12},{16,24},{20,28},{1,17},{... | collective-permute-start | bytes 3145736 | tf_op jit(solution)/shard_map/ppermute | solution.py:38
  349.2 42.6 %collective-permute-start.68 = (bf16[4096,128]{1,0:T(8,128)(2,1)}, bf16[4096,128]{1,0:T(8,128)(2,1)}, u32[]{:S(2)}, u32[]{:S(2)}) collective-permute-start(bf16[4096,128]{1,0:T(8,128)(2,1)} %pad_maximum_fusion.3), channel_id=1, source_target_pairs={{0,8},{4,12},{8,24},{12,28},{24,16},{28,20},{16,0},{20,4},{1,9},{5... | collective-permute-start | bytes 3145736 | tf_op jit(solution)/shard_map/ppermute | solution.py:38
  352.9 40.5 %collective-permute-start.70 = (bf16[4096,128]{1,0:T(8,128)(2,1)}, bf16[4096,128]{1,0:T(8,128)(2,1)}, u32[]{:S(2)}, u32[]{:S(2)}) collective-permute-start(bf16[4096,128]{1,0:T(8,128)(2,1)} %pad_maximum_fusion.4), channel_id=1, source_target_pairs={{0,16},{4,20},{8,0},{12,4},{24,8},{28,12},{16,24},{20,28},{1,17},{... | collective-permute-start | bytes 3145736 | tf_op jit(solution)/shard_map/ppermute | solution.py:38
  (98 other events, 1338.8 us)
Sparse Core Ops, SparseCore 0:
  42.4 37.3 all-gather.1
  215.7 41.2 reduce-scatter.6
  327.0 19.5 reduce-scatter.4

commit v3 on v2

--- a/solution.py
+++ b/solution.py
@@ -49,69 +49,50 @@
         return chip * CORES + (1 - core if other_core else core)
 
 
-def after(value, *others):
-    return lax.optimization_barrier((value, *others))[0]
-
-
-def gather_chunks(ring, chunks):
-    rows = chunks[0].shape[0]
-    half = rows // 2
-    middle = ring.chips // 2
-    gate = ()
-    pieces = []
-    for x in chunks:
-        low, high = after(x[:half], *gate), after(x[half:], *gate)
-        got = [(0, 0, x)]
-        up, down = (low, high), (high, low)
-        for step in range(1, middle):
-            up = tuple(ring.hop(v, 1) for v in up)
-            down = tuple(ring.hop(v, -1) for v in down)
-            got += [(-step, 0, up[0]), (step, half, down[0]), (-step, half, up[1]), (step, 0, down[1])]
-        gate = (up[1], down[1]) if middle > 1 else ()
-        got += [(middle, 0, ring.hop(up[0], 1)), (middle, half, ring.hop(down[0], -1))]
-        pieces.append([])
-        for offset, start, value in got:
-            pieces[-1].append((ring.device_at(offset, False) * rows + start, value))
-            pieces[-1].append((ring.device_at(offset, True) * rows + start, ring.sibling(value)))
-    return pieces
-
-
-def reduce_pieces(ring, own_far, own_near, other_far, other_near):
-    rows = own_far.shape[0]
-    half = rows // 2
-    middle = ring.chips // 2
-    got_far = ring.sibling(other_far)
-    got_near = ring.sibling(other_near)
-
-    def far(start):
-        return own_far[start : start + half].astype(F32) + got_far[start : start + half].astype(F32)
-
-    def near(offset):
-        offset %= ring.chips
-        at = offset - (offset > middle)
-        return own_near[at].astype(F32) + got_near[at * rows : (at + 1) * rows].astype(F32)
-
-    up = ring.hop(far(0).astype(BF16), 1)
-    down = ring.hop(far(half).astype(BF16), -1)
-    for step in range(middle - 1, 0, -1):
-        to_up, to_down = near(step), near(-step)
-        if step == middle - 1:
-            to_up = jnp.concatenate([to_up[:half] + up.astype(F32), to_up[half:]])
-            to_down = jnp.concatenate([to_down[:half], to_down[half:] + down.astype(F32)])
-        else:
-            to_up, to_down = to_up + up.astype(F32), to_down + down.astype(F32)
-        up, down = ring.hop(to_up.astype(BF16), 1), ring.hop(to_down.astype(BF16), -1)
-    if middle == 1:
-        return (near(0) + jnp.concatenate([up, down]).astype(F32)).astype(BF16)
-    return (near(0) + up.astype(F32) + down.astype(F32)).astype(BF16)
-
-
-def exchange(blocks):
+class Waves:
+    def __init__(self):
+        self.pending = {}
+        self.done = {}
+        self.token = None
+
+    def go(self, **values):
+        assert not set(values) & (set(self.pending) | set(self.done))
+        self.pending.update(values)
+
+    def close(self):
+        names, values = list(self.pending), list(self.pending.values())
+        flat, tree = jax.tree.flatten(values)
+        flat = lax.optimization_barrier(flat)
+        self.token = flat[0]
+        self.done.update(zip(names, jax.tree.unflatten(tree, flat)))
+        self.pending = {}
+
+    def gate(self, value):
+        if self.token is None:
+            return value
+        return lax.optimization_barrier((value, self.token))[0]
+
+    def __getitem__(self, name):
+        return self.done[name]
+
+
+def shift_groups(size):
+    ends = sorted({1, size - 1})
+    return ends, [s for s in range(2, size - 1)]
+
+
+def send(blocks, shifts):
     size = len(blocks)
-    got = [blocks[0]] + [None] * (size - 1)
-    for u in range(1, size):
-        got[(size - u) % size] = lax.ppermute(blocks[u], "rep", [(i, (i + u) % size) for i in range(size)])
-    return got
+    return {
+        (size - s) % size: lax.ppermute(blocks[s], "rep", [(i, (i + s) % size) for i in range(size)]) for s in shifts
+    }
+
+
+def ordered(own, *groups):
+    got = {0: own}
+    for group in groups:
+        got.update(group)
+    return [got[u] for u in range(len(got))]
 
 
 def masked_tiles(tiles, i, count):
@@ -167,14 +148,13 @@
             outs[u][...] = result[...]
 
 
-def spmm(tiles, columns, counts, me, pieces, parts, cut, skip):
+def spmm(tiles, columns, counts, meta, pieces, parts, cut, skip):
     blocks, slots, tile_size, _ = tiles.shape
-    width = pieces[0][1].shape[1]
-    total_rows = sum(v.shape[0] for _, v in pieces)
+    width = pieces[0].shape[1]
+    total_rows = sum(v.shape[0] for v in pieces)
     per_part = blocks // parts
     per_step = per_part // cut
     rows = per_step * tile_size
-    meta = jnp.stack([me] + [start for start, _ in pieces]).astype(jnp.int32)
     return pl.pallas_call(
         functools.partial(spmm_kernel, len(pieces), per_part, skip),
         grid_spec=pltpu.PrefetchScalarGridSpec(
@@ -196,7 +176,7 @@
             transcendentals=0,
         ),
         name="spmm",
-    )(columns, counts, meta, tiles, *[v for _, v in pieces])
+    )(columns, counts, meta, tiles, *pieces)
 
 
 def spmm_t_kernel(n_grads, per_part, n_outs, terms, cols, counts, meta, tiles, *refs):
@@ -253,19 +233,18 @@
             copy.wait()
 
 
-def spmm_t(tiles, columns, counts, me, grads, parts, wanted, rows, total_rows):
+def spmm_t(tiles, columns, counts, meta, grads, parts, held, rows, total_rows):
     blocks, slots, tile_size, _ = tiles.shape
     width = grads[0].shape[1]
     per_part = blocks // parts
-    flat = [(out, at) for out, starts in enumerate(wanted) for at in range(len(starts))]
-    meta = jnp.stack([me] + [start for starts in wanted for start in starts]).astype(jnp.int32)
+    flat = [(out, at) for out, many in enumerate(held) for at in range(many)]
     return pl.pallas_call(
-        functools.partial(spmm_t_kernel, len(grads), per_part, len(wanted), flat),
+        functools.partial(spmm_t_kernel, len(grads), per_part, len(held), flat),
         grid_spec=pltpu.PrefetchScalarGridSpec(
             num_scalar_prefetch=3,
             grid=(parts,),
             in_specs=[step_spec(blocks, slots, tile_size, parts, per_part, 0)] + [any_spec()] * len(grads),
-            out_specs=[any_spec()] * len(wanted),
+            out_specs=[any_spec()] * len(held),
             scratch_shapes=[
                 pltpu.VMEM((total_rows, width), F32),
                 pltpu.VMEM((rows, width), BF16),
@@ -274,7 +253,7 @@
                 pltpu.SemaphoreType.DMA((len(flat),)),
             ],
         ),
-        out_shape=[jax.ShapeDtypeStruct((len(starts) * rows, width), BF16) for starts in wanted],
+        out_shape=[jax.ShapeDtypeStruct((many * rows, width), BF16) for many in held],
         compiler_params=params(),
         cost_estimate=pl.CostEstimate(
             flops=2 * blocks * slots * tile_size * tile_size * width,
@@ -302,9 +281,11 @@
     def _():
         copies = []
         for i in range(parts):
-            src = w_hbm.at[aligned(place(i) * f_wide, f_wide, f_wide)]
-            copies.append(pltpu.make_async_copy(src, weight.at[pl.ds(i * f_wide, f_wide)], sems.at[i]))
-            copies[-1].start()
+            for j in range(parts):
+                src = w_hbm.at[aligned(place(i) * f_wide, f_wide, f_wide), aligned(place(j) * h_wide, h_wide, h_wide)]
+                dst = weight.at[pl.ds(i * f_wide, f_wide), pl.ds(j * h_wide, h_wide)]
+                copies.append(pltpu.make_async_copy(src, dst, sems.at[i * parts + j]))
+                copies[-1].start()
         for copy in copies:
             copy.wait()
 
@@ -326,7 +307,7 @@
         mg_outs[i][...] = back[:, i * width : (i + 1) * width]
 
 
-def dense(me, mixed, cot, weight, rows, first):
+def dense(meta, mixed, cot, weight, rows, first):
     parts, chunks = len(mixed), len(mixed[0])
     width = mixed[0][0][0].shape[1]
     features, hidden = weight.shape
@@ -344,7 +325,7 @@
             grid=(rows // step,),
             in_specs=[spec(width, at) for _, at in flat] + [spec(h_wide, first)] * parts + [any_spec()],
             out_specs=[spec(h_wide)] * parts + [spec(width)] * (parts * chunks) + [spec(features), spec(hidden)],
-            scratch_shapes=[pltpu.VMEM((features, hidden), BF16), pltpu.SemaphoreType.DMA((parts,))],
+            scratch_shapes=[pltpu.VMEM((features, hidden), BF16), pltpu.SemaphoreType.DMA((parts * parts,))],
         ),
         out_shape=[jax.ShapeDtypeStruct((rows, h_wide), BF16)] * parts
         + [jax.ShapeDtypeStruct((rows, width), BF16)] * (parts * chunks)
@@ -356,7 +337,7 @@
             transcendentals=rows * hidden,
         ),
         name="dense",
-    )(me[None].astype(jnp.int32), *[m for m, _ in flat], *cot, weight)
+    )(meta, *[m for m, _ in flat], *cot, weight)
     n = parts * chunks
     act, back = outs[:parts], outs[parts : parts + n]
     return act, [back[u * chunks : (u + 1) * chunks] for u in range(parts)], outs[-2], outs[-1]
@@ -370,66 +351,164 @@
     rep = lax.axis_index("rep")
     chunks = f_wide // LANES if f_wide % LANES == 0 else 1
     width = f_wide // chunks
+    half = rows // 2
     part_rows = rows // parts
     halves = 2
     half_rows = part_rows // halves
+    middle = ring.chips // 2
+    near = [o for o in range(ring.chips) if o != middle]
+    ends, inner = shift_groups(parts)
+    last = chunks - 1
+    w = Waves()
+
+    offsets = [(0, 0)] + [(o, 0) for step in range(1, middle) for o in (-step, step)] + [(middle, 0), (middle, half)]
+    own_meta = [ring.device_at(o, False) * rows + at for o, at in offsets]
+    other_meta = [ring.device_at(o, True) * rows + at for o, at in offsets]
+    spmm_meta = jnp.stack([rep] + own_meta + other_meta).astype(jnp.int32)
+    held = [1] + [1] * len(near) + [1, len(near)]
+    order = [middle] + near
+    terms_at = [ring.device_at(o, other) * rows for other in (False, True) for o in order]
+    spmm_t_meta = jnp.stack([rep] + terms_at).astype(jnp.int32)
+    dense_meta = rep[None].astype(jnp.int32)
 
     def part_of(x, u):
         return lax.dynamic_slice_in_dim(x, lax.rem(rep + u, parts) * part_rows, part_rows, 0)
 
     share = weight.shape[0] // row_size
     w_share = lax.dynamic_slice_in_dim(weight, lax.axis_index("row") * share, share, 0)
-    w_share = exchange([w_share] * parts)
-    cot = exchange([after(part_of(cotangent, u), *w_share[1:2]) for u in range(parts)])
-
-    pieces = gather_chunks(ring, [features[:, c * width : (c + 1) * width] for c in range(chunks)])
-    w_share = after(jnp.concatenate(w_share, axis=1), pieces[-1][2][1])
-    w_full = lax.all_gather(w_share, "row", axis=0, tiled=True)
-
-    mixed = []
+    w_share = lax.all_gather(w_share, "rep", axis=1, tiled=True)
+
+    cot_blocks = [part_of(cotangent, u) for u in range(parts)]
+    xs = [features[:, c * width : (c + 1) * width] for c in range(chunks)]
+    up = down = xs[0]
+    got_own = {}
+    got_other = {}
+    mixed = {}
+
+    def run_spmm(c, cut, skip):
+        own = [got_own[c, i] for i in range(len(offsets))]
+        other = [got_other[c, i] for i in range(len(offsets))]
+        return spmm(tiles, columns, counts, spmm_meta, own + other, parts, cut, skip)
+
+    w.go(metas=(spmm_meta, spmm_t_meta, dense_meta))
     for c in range(chunks):
-        if c < chunks - 1:
-            got = exchange(spmm(tiles, columns, counts, rep, pieces[c], parts, 1, 0))
-            mixed.append([[(v, h * half_rows) for v in got] for h in range(halves)])
+        if c == 0:
+            w.go(own=ring.sibling(features), cot_ends=send(cot_blocks, ends))
+        got_own[c, 0] = xs[c]
+        for step in range(1, middle):
+            name = f"{c}_{step}"
+            w.go(**{"up" + name: ring.hop(up, 1), "down" + name: ring.hop(down, -1)})
+            if c and step == 1:
+                for i in (-2, -1):
+                    got_other[c - 1, len(offsets) + i] = ring.sibling(got_own[c - 1, len(offsets) + i])
+                w.go(**{f"mixed{c - 1}": run_spmm(c - 1, 1, 0)})
+            w.close()
+            up, down = w["up" + name], w["down" + name]
+            got_own[c, 2 * step - 1], got_own[c, 2 * step] = up, down
+            w.go(**{"other_up" + name: ring.sibling(up), "other_down" + name: ring.sibling(down)})
+        w.go(**{f"far_up{c}": ring.hop(up[:half], 1), f"far_down{c}": ring.hop(down[half:], -1)})
+        if c:
+            mixed[c - 1] = w[f"mixed{c - 1}"]
+            w.go(**{f"mixed_ends{c - 1}": send(mixed[c - 1], ends)})
+        w.close()
+        if c == 0:
+            spmm_meta, spmm_t_meta, dense_meta = w["metas"]
+        if c == 0:
+            w.go(cot_inner=send([w.gate(b) for b in cot_blocks], inner))
+            w_full = lax.all_gather(w.gate(w_share), "row", axis=0, tiled=True)
         else:
-            got = [exchange(spmm(tiles, columns, counts, rep, pieces[c], parts, halves, h)) for h in range(halves)]
-            mixed.append([[(v, 0) for v in got[h]] for h in range(halves)])
-
-    act, back, weight_terms = [], [], 0.0
+            w.go(**{f"mixed_inner{c - 1}": send(mixed[c - 1], inner)})
+        got_own[c, len(offsets) - 2], got_own[c, len(offsets) - 1] = w[f"far_up{c}"], w[f"far_down{c}"]
+        got_other[c, 0] = w["own"][:, c * width : (c + 1) * width]
+        for step in range(1, middle):
+            name = f"{c}_{step}"
+            got_other[c, 2 * step - 1], got_other[c, 2 * step] = w["other_up" + name], w["other_down" + name]
+        if c < last:
+            up = down = w.gate(xs[c + 1])
+    for i in (-2, -1):
+        got_other[last, len(offsets) + i] = ring.sibling(got_own[last, len(offsets) + i])
+
     for h in range(halves):
-        blocks = [[mixed[c][h][u] for c in range(chunks)] for u in range(parts)]
-        act_h, back_h, mixed_h, grad_h = dense(rep, blocks, cot, w_full, half_rows, h * half_rows)
-        act.append(act_h)
-        back.append(back_h)
-        weight_terms += lax.dot_general(mixed_h, grad_h, (((0,), (0,)), ((), ())), preferred_element_type=F32)
-
-    weight_terms = lax.psum_scatter(weight_terms.astype(BF16), "row", scatter_dimension=1, tiled=True)
+        w.go(**{f"half{h}": run_spmm(last, halves, h)})
+        w.close()
+        w.go(**{f"half_got{h}": send(w[f"half{h}"], ends + inner)})
+
+    cot = ordered(cot_blocks[0], w["cot_ends"], w["cot_inner"])
+    whole = [ordered(mixed[c][0], w[f"mixed_ends{c}"], w[f"mixed_inner{c}"]) for c in range(last)]
+    sums = 0.0
+    for h in range(halves):
+        part = ordered(w[f"half{h}"][0], w[f"half_got{h}"])
+        blocks = [[(whole[c][u], h * half_rows) for c in range(last)] + [(part[u], 0)] for u in range(parts)]
+        act, back, mixed_rows, grad_rows = dense(dense_meta, blocks, cot, w_full, half_rows, h * half_rows)
+        sums += lax.dot_general(mixed_rows, grad_rows, (((0,), (0,)), ((), ())), preferred_element_type=F32)
+        w.go(**{f"act{h}": act, f"back{h}": back})
+        w.close()
+        w.go(**{f"back_got0_{h}": send([b[0] for b in w[f"back{h}"]], ends + inner)})
+    w.close()
+
+    weight_terms = lax.psum_scatter(sums.astype(BF16), "row", scatter_dimension=1, tiled=True)
     weight_grad = lax.psum_scatter(weight_terms, "rep", scatter_dimension=0, tiled=True).astype(F32)
 
-    middle = ring.chips // 2
-    near = [o for o in range(ring.chips) if o != middle]
-    wanted = [
-        [ring.device_at(o, other) * rows for o in offsets]
-        for other in (False, True)
-        for offsets in [[middle]] + ([[o] for o in near] if not other else [near])
-    ]
-    gate = ()
+    act_blocks = [jnp.concatenate([w[f"act{h}"][u] for h in range(halves)]) for u in range(parts)]
     feature_grad = []
     for c in range(chunks):
-        got = []
-        for h in range(halves):
-            got.append(exchange([after(back[h][u][c], *gate) for u in range(parts)]))
-        gate = got[0][1:]
-        grads = [got[h][u] for u in range(parts) for h in range(halves)]
-        terms = spmm_t(tiles, columns, counts, rep, grads, parts, wanted, rows, rows * row_size)
-        feature_grad.append(reduce_pieces(ring, terms[0], terms[1 : 1 + len(near)], terms[-2], terms[-1]))
+        grads = [
+            ordered(w[f"back{h}"][0][c], w[f"back_got{c}_{h}"])[u] for u in range(parts) for h in range(halves)
+        ]
+        if c:
+            grads = [w.gate(g) for g in grads]
+        w.go(**{f"terms{c}": spmm_t(tiles, columns, counts, spmm_t_meta, grads, parts, held, rows, rows * row_size)})
+        if c < last:
+            for h in range(halves):
+                w.go(**{f"back_got{c + 1}_{h}": send([w.gate(b[c + 1]) for b in w[f"back{h}"]], ends + inner)})
+        w.close()
+        terms = w[f"terms{c}"]
+        own_far, own_near, other_far, other_near = terms[0], terms[1:-2], terms[-2], terms[-1]
+        got_far = ring.sibling(other_far)
+        w.go(**{f"got_near{c}": ring.sibling(other_near)})
+
+        def far(start):
+            return own_far[start : start + half].astype(F32) + got_far[start : start + half].astype(F32)
+
+        up = ring.hop(far(0).astype(BF16), 1)
+        down = ring.hop(far(half).astype(BF16), -1)
+        w.go(**{f"sum{c}_{middle}": (up, down)})
+        if c == last:
+            w.go(act_inner=send(act_blocks, inner))
+        w.close()
+        got_near = w[f"got_near{c}"]
+
+        def near_sum(offset):
+            at = near.index(offset % ring.chips)
+            return own_near[at].astype(F32) + got_near[at * rows : (at + 1) * rows].astype(F32)
+
+        for step in range(middle - 1, 0, -1):
+            up, down = w[f"sum{c}_{step + 1}"]
+            to_up, to_down = near_sum(step), near_sum(-step)
+            if step == middle - 1:
+                to_up = jnp.concatenate([to_up[:half] + up.astype(F32), to_up[half:]])
+                to_down = jnp.concatenate([to_down[:half], to_down[half:] + down.astype(F32)])
+            else:
+                to_up, to_down = to_up + up.astype(F32), to_down + down.astype(F32)
+            to_up, to_down = to_up.astype(BF16), to_down.astype(BF16)
+            w.go(**{f"sum{c}_{step}": (ring.hop(to_up, 1), ring.hop(to_down, -1))})
+            if c == 0 and step == middle - 1:
+                w.go(act_ends=send([w.gate(a) for a in act_blocks], ends))
+            if step > 1:
+                w.close()
+            elif c < last:
+                w.token = to_up[:8]
+        up, down = (w.pending if f"sum{c}_1" in w.pending else w.done)[f"sum{c}_1"]
+        if middle == 1:
+            feature_grad.append((near_sum(0) + jnp.concatenate([up, down]).astype(F32)).astype(BF16))
+        else:
+            feature_grad.append((near_sum(0) + up.astype(F32) + down.astype(F32)).astype(BF16))
+    act = {**w.pending, **w.done}
+    act = ordered(act_blocks[0], act["act_ends"], act["act_inner"])
     feature_grad = jnp.concatenate(feature_grad, axis=1)
-
     activations = jnp.zeros((rows, h_wide), BF16)
-    for h in range(halves):
-        for u, value in enumerate(exchange([after(a, *gate) for a in act[h]])):
-            start = lax.rem(rep + u, parts) * part_rows + h * half_rows
-            activations = lax.dynamic_update_slice_in_dim(activations, value, start, 0)
+    for u in range(parts):
+        activations = lax.dynamic_update_slice_in_dim(activations, act[u], lax.rem(rep + u, parts) * part_rows, 0)
     return (activations, feature_grad, weight_grad)
 
 

time: 405 us -> 352 us (0.87)
  waiting for transfers between devices: 158 us -> 121 us
  starting transfers between devices: 83.3 us -> 52.1 us
  blocking collectives: 0 us -> 15 us
    ppermute x20 -> x16, waiting for transfers between devices: 104 us -> 36.2 us  [hop(): return lax.ppermute(value, 'row', self.perm(step))]
    ppermute x33 -> x27, starting transfers between devices: 59.4 us -> 31.2 us  [send(): lax.ppermute(blocks[s], 'rep', [(i, (i + s) % size) for i in range(size)])]
    all_gather x0 -> x1, blocking collectives: none -> 15 us  [local(): w_share = lax.all_gather(w_share, 'rep', axis=1, tiled=True)]
    reduce_scatter x1, waiting for transfers between devices: 0.01 us -> 12.9 us  [local(): lax.psum_scatter(weight_terms, 'rep', scatter_dimension=0, tiled=True)]
    unnamed x4, waiting for transfers between devices: 0.05 us -> 11.1 us
    ppermute x18 -> x13, waiting for transfers between devices: 0.48 us -> 9.03 us  [sibling(): return lax.ppermute(value, 'row', [(d, d ^ 1) for d in range(self.devices)])]
    slice x6 -> x10, local copies, waits for them, and re-layouts: 4.1 us -> 8.76 us  [the longest x1 3.05 us: local(): got_other[c, 0] = w['own'][:, c * width:(c + 1) * width]]
    ppermute x20 -> x16, starting transfers between devices: 21.3 us -> 17 us  [hop(): return lax.ppermute(value, 'row', self.perm(step))]
  transfers between devices with their start and end apart: 74 -> 59, of which waited for: 25 -> 23; matrix products, arithmetic and copies ran while one was open for 10% -> 11% of each run, Pallas kernels for 21% -> 24%
where the time goes in v3:
time: 352 us; the launch traced here: 351 us
  waiting for transfers between devices  121 us (34%)
  Pallas kernels  85.6 us (24%)
  starting transfers between devices  52.1 us (15%)
  local copies, waits for them, and re-layouts  30.8 us (9%)
  between operations  22.4 us (6%)
  other arithmetic  21.2 us (6%)
  blocking collectives  15 us (4%)
    ppermute x27, waiting for transfers between devices, send(): lax.ppermute(blocks[s], 'rep', [(i, (i + s) % size) for i in range(size)])  52 us
    pallas_call x3, Pallas kernels, spmm(): pl.pallas_call(functools.partial(spmm_kernel, len(pieces), per_part, skip...  36.3 us
    ppermute x16, waiting for transfers between devices, hop(): return lax.ppermute(value, 'row', self.perm(step))  36.2 us
    pallas_call x2, Pallas kernels, spmm_t(): pl.pallas_call(functools.partial(spmm_t_kernel, len(grads), per_part, len...  34.9 us
    ppermute x27, starting transfers between devices, send(): lax.ppermute(blocks[s], 'rep', [(i, (i + s) % size) for i in range(size)])  31.2 us
    ppermute x16, starting transfers between devices, hop(): return lax.ppermute(value, 'row', self.perm(step))  17 us
    all_gather x1, blocking collectives, local(): w_share = lax.all_gather(w_share, 'rep', axis=1, tiled=True)  15 us
    pallas_call x2, Pallas kernels, dense(): pl.pallas_call(functools.partial(dense_kernel, parts, chunks), grid_spec=...  14.3 us
  transfers between devices with their start and end apart: 59, of which 23 were waited for; matrix products, arithmetic and copies ran while one was open for 11% of the time, Pallas kernels for 24%

profile of v3, /device:TPU:0, one launch (start us, length us, event | category | flops | bytes accessed | tf_op | source)
XLA Modules:
  0.0 350.9 jit_solution(14519742625584848422)
XLA Ops:
  7.7 1.7 fusion.5
  9.4 2.6 collective-permute-start.4
  12.1 2.7 constant_dynamic-slice_fusion.2
  14.8 4.1 %collective-permute-start.1 = (bf16[1024,256]{1,0:T(8,128)(2,1)}, bf16[1024,256]{1,0:T(8,128)(2,1)}, u32[]{:S(2)}, u32[]{:S(2)}) collective-permute-start(bf16[1024,256]{1,0:T(8,128)(2,1)} %get-tuple-element.348), channel_id=1, source_target_pairs={{0,3},{1,0},{2,1},{3,2},{4,7},{5,4},{6,5},{7,6},{8,11},{9,8},{10,9... | collective-permute-start | bytes 1572872 | tf_op jit(solution)/shard_map/ppermute | solution.py:87
  29.1 2.4 collective-permute-done.1.refs_9_
  31.5 11.1 %collective-permute-done.2.refs_11_ = bf16[1024,256]{1,0:T(8,128)(2,1)} collective-permute-done((bf16[1024,256]{1,0:T(8,128)(2,1)S(1)}, bf16[1024,256]{1,0:T(8,128)(2,1)}, u32[]{:S(2)}, u32[]{:S(2)}) %collective-permute-start.2) | collective-permute-done | bytes 524320 | tf_op jit(solution)/shard_map/ppermute | solution.py:87
  43.2 1.9 slice.99
  45.0 1.9 slice.100
  49.0 15.0 %all_gather.6 = bf16[128,1024]{1,0:T(8,128)(2,1)} all-gather(bf16[128,256]{1,0:T(8,128)(2,1)S(1)} %constant_dynamic-slice_fusion.3), channel_id=1, replica_groups=mesh['row'=8,'rep'=4] {'rep'}, dimensions={1}, use_global_device_ids=true | all-gather | bytes 327680 | tf_op jit(solution)/shard_map/all_gather | solution.py:379
  68.1 3.1 fusion.4
  72.2 14.4 %spmm.3 = (bf16[1024,128]{1,0:T(8,128)(2,1)}, bf16[1024,128]{1,0:T(8,128)(2,1)}, bf16[1024,128]{1,0:T(8,128)(2,1)}, bf16[1024,128]{1,0:T(8,128)(2,1)}) custom-call(s32[32,16]{1,0:T(8,128)} %copy.50.cols, s32[32]{0:T(128)} %counts.9, s32[11]{0:T(128)} %stack.75.meta, bf16[32,16,128,128]{3,2,1,0:T(8,128)(2,1)} %tiles.9, bf16[4096,128]{1,0:T(8,128)(2,1)} %copy-done.7, ...), custom_call_target="tpu_custom_call" | custom-call | flops 2147483648 | bytes 25165824 | tf_op jit(solution)/shard_map/spmm/pallas_call | solution.py:158
  86.6 3.3 collective-permute-done.9.refs_10_
  89.9 5.8 %collective-permute-done.11.refs_2_ = bf16[4096,128]{1,0:T(8,128)(2,1)S(1)} collective-permute-done((bf16[4096,128]{1,0:T(8,128)(2,1)S(1)}, bf16[4096,128]{1,0:T(8,128)(2,1)S(1)}, u32[]{:S(2)}, u32[]{:S(2)}) %collective-permute-start.11) | collective-permute-done | bytes 1048608 | tf_op jit(solution)/shard_map/ppermute | solution.py:38
  98.9 2.0 collective-permute-start.17
  101.0 5.0 %collective-permute-done.19.refs_2_ = bf16[1024,128]{1,0:T(8,128)(2,1)S(1)} collective-permute-done((bf16[1024,128]{1,0:T(8,128)(2,1)}, bf16[1024,128]{1,0:T(8,128)(2,1)S(1)}, u32[]{:S(2)}, u32[]{:S(2)}) %collective-permute-start.19) | collective-permute-done | bytes 262176 | tf_op jit(solution)/shard_map/ppermute | solution.py:87
  105.9 1.6 collective-permute-start.20
  107.6 7.6 %collective-permute-done.20.refs_6_ = bf16[1024,128]{1,0:T(8,128)(2,1)S(1)} collective-permute-done((bf16[1024,128]{1,0:T(8,128)(2,1)S(1)}, bf16[1024,128]{1,0:T(8,128)(2,1)S(1)}, u32[]{:S(2)}, u32[]{:S(2)}) %collective-permute-start.20) | collective-permute-done | bytes 262176 | tf_op jit(solution)/shard_map/ppermute | solution.py:87
  118.8 11.0 %spmm.4 = (bf16[512,128]{1,0:T(8,128)(2,1)}, bf16[512,128]{1,0:T(8,128)(2,1)}, bf16[512,128]{1,0:T(8,128)(2,1)}, bf16[512,128]{1,0:T(8,128)(2,1)}) custom-call(s32[32,16]{1,0:T(8,128)} %copy.50.cols, s32[32]{0:T(128)} %counts.9, s32[11]{0:T(128)} %stack.75.meta, bf16[32,16,128,128]{3,2,1,0:T(8,128)(2,1)} %tiles.9, bf16[4096,128]{1,0:T(8,128)(2,1)} %copy-done.2, ...), custom_call_target="tpu_custom_call" | custom-call | flops 1073741824 | bytes 16777216 | tf_op jit(solution)/shard_map/spmm/pallas_call | solution.py:158
  129.9 1.9 collective-permute-start.23
  132.8 11.0 %spmm.5 = (bf16[512,128]{1,0:T(8,128)(2,1)}, bf16[512,128]{1,0:T(8,128)(2,1)}, bf16[512,128]{1,0:T(8,128)(2,1)}, bf16[512,128]{1,0:T(8,128)(2,1)}) custom-call(s32[32,16]{1,0:T(8,128)} %copy.50.cols, s32[32]{0:T(128)} %counts.9, s32[11]{0:T(128)} %stack.75.meta, bf16[32,16,128,128]{3,2,1,0:T(8,128)(2,1)} %tiles.9, bf16[4096,128]{1,0:T(8,128)(2,1)} %copy-done.2, ...), custom_call_target="tpu_custom_call" | custom-call | flops 1073741824 | bytes 16777216 | tf_op jit(solution)/shard_map/spmm/pallas_call | solution.py:158
  143.9 2.9 collective-permute-start.26
  148.0 7.1 %dense.2 = (bf16[512,256]{1,0:T(8,128)(2,1)}, bf16[512,256]{1,0:T(8,128)(2,1)}, bf16[512,256]{1,0:T(8,128)(2,1)}, bf16[512,256]{1,0:T(8,128)(2,1)}, bf16[512,128...) custom-call(s32[1]{0:T(128)} %bitcast.meta, ...), custom_call_target="tpu_custom_call" | custom-call | flops 2147483648 | bytes 8388608 | tf_op jit(solution)/shard_map/dense/pallas_call | solution.py:321
  155.2 3.9 %collective-permute-done.27.refs_5_ = bf16[512,128]{1,0:T(8,128)(2,1)S(1)} collective-permute-done((bf16[512,128]{1,0:T(8,128)(2,1)}, bf16[512,128]{1,0:T(8,128)(2,1)S(1)}, u32[]{:S(2)}, u32[]{:S(2)}) %collective-permute-start.27) | collective-permute-done | bytes 131104 | tf_op jit(solution)/shard_map/ppermute | solution.py:87
  160.7 1.9 collective-permute-start.31
  162.7 7.1 %dense.3 = (bf16[512,256]{1,0:T(8,128)(2,1)}, bf16[512,256]{1,0:T(8,128)(2,1)}, bf16[512,256]{1,0:T(8,128)(2,1)}, bf16[512,256]{1,0:T(8,128)(2,1)}, bf16[512,128...) custom-call(s32[1]{0:T(128)} %bitcast.meta, ...), custom_call_target="tpu_custom_call" | custom-call | flops 2147483648 | bytes 8388608 | tf_op jit(solution)/shard_map/dense/pallas_call | solution.py:321
  169.8 2.4 collective-permute-done.30.refs_4_
  173.6 2.0 collective-permute-start.34
  175.6 2.4 collective-permute-done.32.refs_3_
  178.0 7.9 %collective-permute-done.33.refs_5_ = bf16[512,128]{1,0:T(8,128)(2,1)S(1)} collective-permute-done((bf16[512,128]{1,0:T(8,128)(2,1)}, bf16[512,128]{1,0:T(8,128)(2,1)S(1)}, u32[]{:S(2)}, u32[]{:S(2)}) %collective-permute-start.33) | collective-permute-done | bytes 131104 | tf_op jit(solution)/shard_map/ppermute | solution.py:87
  186.9 1.9 collective-permute-start.37
  188.8 1.9 collective-permute-start.38
  193.0 17.3 %spmm_t.2 = (bf16[4096,128]{1,0:T(8,128)(2,1)}, bf16[4096,128]{1,0:T(8,128)(2,1)}, bf16[4096,128]{1,0:T(8,128)(2,1)}, bf16[4096,128]{1,0:T(8,128)(2,1)}, bf16[40...) custom-call(s32[32,16]{1,0:T(8,128)} %copy.50.cols, s32[32]{0:T(128)} %counts.9, s32[9]{0:T(128)} %stack.84.meta, ...), custom_call_target="tpu_custom_call" | custom-call | flops 2147483648 | bytes 25165824 | tf_op jit(solution)/shard_map/spmm_t/pallas_call | solution.py:241
  211.0 6.9 %collective-permute-done.42 = bf16[4096,128]{1,0:T(8,128)(2,1)S(1)} collective-permute-done((bf16[4096,128]{1,0:T(8,128)(2,1)}, bf16[4096,128]{1,0:T(8,128)(2,1)S(1)}, u32[]{:S(2)}, u32[]{:S(2)}) %collective-permute-start.42) | collective-permute-done | bytes 1048608 | tf_op jit(solution)/shard_map/ppermute | solution.py:41
  222.7 10.6 %collective-permute-done.44 = bf16[2048,128]{1,0:T(8,128)(2,1)S(1)} collective-permute-done((bf16[2048,128]{1,0:T(8,128)(2,1)S(1)}, bf16[2048,128]{1,0:T(8,128)(2,1)S(1)}, u32[]{:S(2)}, u32[]{:S(2)}) %collective-permute-start.44) | collective-permute-done | bytes 524320 | tf_op jit(solution)/shard_map/ppermute | solution.py:38
  241.6 2.6 copy.55
  245.4 2.8 collective-permute-start.47
  248.2 17.7 %spmm_t.3 = (bf16[4096,128]{1,0:T(8,128)(2,1)}, bf16[4096,128]{1,0:T(8,128)(2,1)}, bf16[4096,128]{1,0:T(8,128)(2,1)}, bf16[4096,128]{1,0:T(8,128)(2,1)}, bf16[40...) custom-call(s32[32,16]{1,0:T(8,128)} %copy.50.cols, s32[32]{0:T(128)} %counts.9, s32[9]{0:T(128)} %stack.84.meta, ...), custom_call_target="tpu_custom_call" | custom-call | flops 2147483648 | bytes 25165824 | tf_op jit(solution)/shard_map/spmm_t/pallas_call | solution.py:241
  265.9 4.4 %collective-permute-done.48 = bf16[1024,256]{1,0:T(8,128)(2,1)S(1)} collective-permute-done((bf16[1024,256]{1,0:T(8,128)(2,1)S(1)}, bf16[1024,256]{1,0:T(8,128)(2,1)S(1)}, u32[]{:S(2)}, u32[]{:S(2)}) %collective-permute-start.48) | collective-permute-done | bytes 524320 | tf_op jit(solution)/shard_map/ppermute | solution.py:87
  274.1 11.0 %reduce-scatter.7.cloned.1.call-done = bf16[128,1024]{1,0:T(8,128)(2,1)} async-done(((bf16[1024,1024]{1,0:T(8,128)(2,1)}), bf16[128,1024]{1,0:T(8,128)(2,1)}) %reduce-scatter.7.cloned.1.call-update) | async-done | bytes 262160
  285.2 1.8 copy.56
  287.0 2.8 add_convert_fusion.3
  294.1 12.9 %reduce-scatter.5.cloned.1.call-done = bf16[256,128]{1,0:T(8,128)(2,1)} async-done(((bf16[1024,128]{1,0:T(8,128)(2,1)}), bf16[256,128]{1,0:T(8,128)(2,1)}) %reduce-scatter.5.cloned.1.call-update) | async-done | bytes 65552 | tf_op jit(solution)/shard_map/reduce_scatter | solution.py:450
  308.6 1.9 constant_dynamic-update-slice_fusion
  310.5 3.1 convert_add_fusion.1
  318.3 2.1 add_convert_fusion.2
  320.4 2.0 constant_dynamic-update-slice_fusion.1
  323.2 16.5 %collective-permute-done.55 = bf16[4096,128]{1,0:T(8,128)(2,1)S(1)} collective-permute-done((bf16[4096,128]{1,0:T(8,128)(2,1)S(1)}, bf16[4096,128]{1,0:T(8,128)(2,1)S(1)}, u32[]{:S(2)}, u32[]{:S(2)}) %collective-permute-start.55) | collective-permute-done | bytes 1048608 | tf_op jit(solution)/shard_map/ppermute | solution.py:38
  341.0 1.8 add_convert_fusion.1
  (261 shorter events, 59.0 us)
Async XLA Ops:
  7.2 140.8 %all-gather.2.cloned.1.call-start = ((), (), s32[]{:S(2)}) async-start(), calls=%async_computation.2 | async-start | bytes 2359296 | tf_op jit(solution)/shard_map/all_gather | solution.py:418
  7.2 35.4 %collective-permute-start = (bf16[4096,256]{1,0:T(8,128)(2,1)}, bf16[4096,256]{1,0:T(8,128)(2,1)}, u32[]{:S(2)}, u32[]{:S(2)}) collective-permute-start(bf16[4096,256]{1,0:T(8,128)(2,1)} %param.42), channel_id=1, source_target_pairs={{0,4},{4,0},{8,12},{12,8},{16,20},{20,16},{24,28},{28,24},{1,5},{5... | collective-permute-start | bytes 6291464 | tf_op jit(solution)/shard_map/ppermute | solution.py:41
  9.4 33.1 %collective-permute-start.4 = (bf16[4096,128]{1,0:T(8,128)(2,1)S(1)}, bf16[4096,128]{1,0:T(8,128)(2,1)}, u32[]{:S(2)}, u32[]{:S(2)}) collective-permute-start(bf16[4096,128]{1,0:T(8,128)(2,1)S(1)} %get-tuple-element.354.refs_0_), channel_id=1, source_target_pairs={{0,16},{4,20},{8,0},{12,4},{24,8},{28,12},{16,24},{20,28},{1,17},{... | collective-permute-start | bytes 3145736 | tf_op jit(solution)/shard_map/ppermute | solution.py:38
  12.1 30.5 %collective-permute-start.3 = (bf16[4096,128]{1,0:T(8,128)(2,1)S(1)}, bf16[4096,128]{1,0:T(8,128)(2,1)}, u32[]{:S(2)}, u32[]{:S(2)}) collective-permute-start(bf16[4096,128]{1,0:T(8,128)(2,1)S(1)} %get-tuple-element.354.refs_0_), channel_id=1, source_target_pairs={{0,8},{4,12},{8,24},{12,28},{24,16},{28,20},{16,0},{20,4},{1,9},{5... | collective-permute-start | bytes 3145736 | tf_op jit(solution)/shard_map/ppermute | solution.py:38
  14.8 16.7 %collective-permute-start.1 = (bf16[1024,256]{1,0:T(8,128)(2,1)}, bf16[1024,256]{1,0:T(8,128)(2,1)}, u32[]{:S(2)}, u32[]{:S(2)}) collective-permute-start(bf16[1024,256]{1,0:T(8,128)(2,1)} %get-tuple-element.348), channel_id=1, source_target_pairs={{0,3},{1,0},{2,1},{3,2},{4,7},{5,4},{6,5},{7,6},{8,11},{9,8},{10,9... | collective-permute-start | bytes 1572872 | tf_op jit(solution)/shard_map/ppermute | solution.py:87
  18.9 23.7 %collective-permute-start.2 = (bf16[1024,256]{1,0:T(8,128)(2,1)S(1)}, bf16[1024,256]{1,0:T(8,128)(2,1)}, u32[]{:S(2)}, u32[]{:S(2)}) collective-permute-start(bf16[1024,256]{1,0:T(8,128)(2,1)S(1)} %get-tuple-element.350), channel_id=1, source_target_pairs={{0,1},{1,2},{2,3},{3,0},{4,5},{5,6},{6,7},{7,4},{8,9},{9,10},{10,1... | collective-permute-start | bytes 1572872 | tf_op jit(solution)/shard_map/ppermute | solution.py:87
  42.6 21.4 %collective-permute-start.5 = (bf16[4096,128]{1,0:T(8,128)(2,1)}, bf16[4096,128]{1,0:T(8,128)(2,1)S(1)}, u32[]{:S(2)}, u32[]{:S(2)}) collective-permute-start(bf16[4096,128]{1,0:T(8,128)(2,1)} %collective-permute-done.3.refs_1_), channel_id=1, source_target_pairs={{0,4},{4,0},{8,12},{12,8},{16,20},{20,16},{24,28},{28,24},{1,5},{5... | collective-permute-start | bytes 3145736 | tf_op jit(solution)/shard_map/ppermute | solution.py:41
  42.7 21.3 %collective-permute-start.6 = (bf16[4096,128]{1,0:T(8,128)(2,1)}, bf16[4096,128]{1,0:T(8,128)(2,1)}, u32[]{:S(2)}, u32[]{:S(2)}) collective-permute-start(bf16[4096,128]{1,0:T(8,128)(2,1)} %collective-permute-done.4.refs_2_), channel_id=1, source_target_pairs={{0,4},{4,0},{8,12},{12,8},{16,20},{20,16},{24,28},{28,24},{1,5},{5... | collective-permute-start | bytes 3145736 | tf_op jit(solution)/shard_map/ppermute | solution.py:41
  46.9 17.0 %collective-permute-start.8 = (bf16[2048,128]{1,0:T(8,128)(2,1)}, bf16[2048,128]{1,0:T(8,128)(2,1)S(1)}, u32[]{:S(2)}, u32[]{:S(2)}) collective-permute-start(bf16[2048,128]{1,0:T(8,128)(2,1)} %slice.100), channel_id=1, source_target_pairs={{0,16},{4,20},{8,0},{12,4},{24,8},{28,12},{16,24},{20,28},{1,17},{... | collective-permute-start | bytes 1572872 | tf_op jit(solution)/shard_map/ppermute | solution.py:38
  48.4 15.5 %collective-permute-start.7 = (bf16[2048,128]{1,0:T(8,128)(2,1)}, bf16[2048,128]{1,0:T(8,128)(2,1)}, u32[]{:S(2)}, u32[]{:S(2)}) collective-permute-start(bf16[2048,128]{1,0:T(8,128)(2,1)} %slice.99), channel_id=1, source_target_pairs={{0,8},{4,12},{8,24},{12,28},{24,16},{28,20},{16,0},{20,4},{1,9},{5... | collective-permute-start | bytes 1572872 | tf_op jit(solution)/shard_map/ppermute | solution.py:38
  64.0 221.1 %reduce-scatter.7.cloned.1.call-start = ((), (), s32[]{:S(2)}) async-start(), calls=%async_computation.4 | async-start | bytes 2359296
  64.9 30.8 %collective-permute-start.11 = (bf16[4096,128]{1,0:T(8,128)(2,1)S(1)}, bf16[4096,128]{1,0:T(8,128)(2,1)S(1)}, u32[]{:S(2)}, u32[]{:S(2)}) collective-permute-start(bf16[4096,128]{1,0:T(8,128)(2,1)S(1)} %get-tuple-element.175.refs_0_), channel_id=1, source_target_pairs={{0,16},{4,20},{8,0},{12,4},{24,8},{28,12},{16,24},{20,28},{1,17},{... | collective-permute-start | bytes 3145736 | tf_op jit(solution)/shard_map/ppermute | solution.py:38
  66.5 30.5 %collective-permute-start.10 = (bf16[4096,128]{1,0:T(8,128)(2,1)S(1)}, bf16[4096,128]{1,0:T(8,128)(2,1)S(1)}, u32[]{:S(2)}, u32[]{:S(2)}) collective-permute-start(bf16[4096,128]{1,0:T(8,128)(2,1)S(1)} %get-tuple-element.175.refs_0_), channel_id=1, source_target_pairs={{0,8},{4,12},{8,24},{12,28},{24,16},{28,20},{16,0},{20,4},{1,9},{5... | collective-permute-start | bytes 3145736 | tf_op jit(solution)/shard_map/ppermute | solution.py:38
  67.0 22.9 %collective-permute-start.9 = (bf16[1024,256]{1,0:T(8,128)(2,1)}, bf16[1024,256]{1,0:T(8,128)(2,1)S(1)}, u32[]{:S(2)}, u32[]{:S(2)}) collective-permute-start(bf16[1024,256]{1,0:T(8,128)(2,1)} %get-tuple-element.174), channel_id=1, source_target_pairs={{0,2},{1,3},{2,0},{3,1},{4,6},{5,7},{6,4},{7,5},{8,10},{9,11},{10,... | collective-permute-start | bytes 1572872 | tf_op jit(solution)/shard_map/ppermute | solution.py:87
  96.9 18.3 %collective-permute-start.15 = (bf16[4096,128]{1,0:T(8,128)(2,1)S(1)}, bf16[4096,128]{1,0:T(8,128)(2,1)S(1)}, u32[]{:S(2)}, u32[]{:S(2)}) collective-permute-start(bf16[4096,128]{1,0:T(8,128)(2,1)S(1)} %collective-permute-done.10.refs_1_), channel_id=1, source_target_pairs={{0,4},{4,0},{8,12},{12,8},{16,20},{20,16},{24,28},{28,24},{1,5},{5... | collective-permute-start | bytes 3145736 | tf_op jit(solution)/shard_map/ppermute | solution.py:41
  96.9 18.3 %collective-permute-start.16 = (bf16[4096,128]{1,0:T(8,128)(2,1)S(1)}, bf16[4096,128]{1,0:T(8,128)(2,1)S(1)}, u32[]{:S(2)}, u32[]{:S(2)}) collective-permute-start(bf16[4096,128]{1,0:T(8,128)(2,1)S(1)} %collective-permute-done.11.refs_2_), channel_id=1, source_target_pairs={{0,4},{4,0},{8,12},{12,8},{16,20},{20,16},{24,28},{28,24},{1,5},{5... | collective-permute-start | bytes 3145736 | tf_op jit(solution)/shard_map/ppermute | solution.py:41
  98.9 16.3 %collective-permute-start.18 = (bf16[2048,128]{1,0:T(8,128)(2,1)S(1)}, bf16[2048,128]{1,0:T(8,128)(2,1)S(1)}, u32[]{:S(2)}, u32[]{:S(2)}) collective-permute-start(bf16[2048,128]{1,0:T(8,128)(2,1)S(1)} %slice.104), channel_id=1, source_target_pairs={{0,16},{4,20},{8,0},{12,4},{24,8},{28,12},{16,24},{20,28},{1,17},{... | collective-permute-start | bytes 1572872 | tf_op jit(solution)/shard_map/ppermute | solution.py:38
  98.9 16.3 %collective-permute-start.17 = (bf16[2048,128]{1,0:T(8,128)(2,1)S(1)}, bf16[2048,128]{1,0:T(8,128)(2,1)S(1)}, u32[]{:S(2)}, u32[]{:S(2)}) collective-permute-start(bf16[2048,128]{1,0:T(8,128)(2,1)S(1)} %slice.103), channel_id=1, source_target_pairs={{0,8},{4,12},{8,24},{12,28},{24,16},{28,20},{16,0},{20,4},{1,9},{5... | collective-permute-start | bytes 1572872 | tf_op jit(solution)/shard_map/ppermute | solution.py:38
  115.8 14.1 %collective-permute-start.14 = (bf16[1024,128]{1,0:T(8,128)(2,1)S(1)}, bf16[1024,128]{1,0:T(8,128)(2,1)S(1)}, u32[]{:S(2)}, u32[]{:S(2)}) collective-permute-start(bf16[1024,128]{1,0:T(8,128)(2,1)S(1)} %copy-done.57), channel_id=1, source_target_pairs={{0,2},{1,3},{2,0},{3,1},{4,6},{5,7},{6,4},{7,5},{8,10},{9,11},{10,... | collective-permute-start | bytes 786440 | tf_op jit(solution)/shard_map/ppermute | solution.py:87
  129.9 13.9 %collective-permute-start.23 = (bf16[512,128]{1,0:T(8,128)(2,1)}, bf16[512,128]{1,0:T(8,128)(2,1)S(1)}, u32[]{:S(2)}, u32[]{:S(2)}) collective-permute-start(bf16[512,128]{1,0:T(8,128)(2,1)} %get-tuple-element.198), channel_id=1, source_target_pairs={{0,3},{1,0},{2,1},{3,2},{4,7},{5,4},{6,5},{7,6},{8,11},{9,8},{10,9... | collective-permute-start | bytes 393224 | tf_op jit(solution)/shard_map/ppermute | solution.py:87
  131.8 12.0 %collective-permute-start.24 = (bf16[512,128]{1,0:T(8,128)(2,1)}, bf16[512,128]{1,0:T(8,128)(2,1)S(1)}, u32[]{:S(2)}, u32[]{:S(2)}) collective-permute-start(bf16[512,128]{1,0:T(8,128)(2,1)} %get-tuple-element.199), channel_id=1, source_target_pairs={{0,2},{1,3},{2,0},{3,1},{4,6},{5,7},{6,4},{7,5},{8,10},{9,11},{10,... | collective-permute-start | bytes 393224 | tf_op jit(solution)/shard_map/ppermute | solution.py:87
  131.8 12.0 %collective-permute-start.25 = (bf16[512,128]{1,0:T(8,128)(2,1)}, bf16[512,128]{1,0:T(8,128)(2,1)S(1)}, u32[]{:S(2)}, u32[]{:S(2)}) collective-permute-start(bf16[512,128]{1,0:T(8,128)(2,1)} %get-tuple-element.200), channel_id=1, source_target_pairs={{0,1},{1,2},{2,3},{3,0},{4,5},{5,6},{6,7},{7,4},{8,9},{9,10},{10,1... | collective-permute-start | bytes 393224 | tf_op jit(solution)/shard_map/ppermute | solution.py:87
  143.9 11.3 %collective-permute-start.26 = (bf16[512,128]{1,0:T(8,128)(2,1)}, bf16[512,128]{1,0:T(8,128)(2,1)S(1)}, u32[]{:S(2)}, u32[]{:S(2)}) collective-permute-start(bf16[512,128]{1,0:T(8,128)(2,1)} %get-tuple-element.205), channel_id=1, source_target_pairs={{0,3},{1,0},{2,1},{3,2},{4,7},{5,4},{6,5},{7,6},{8,11},{9,8},{10,9... | collective-permute-start | bytes 393224 | tf_op jit(solution)/shard_map/ppermute | solution.py:87
  146.8 12.3 %collective-permute-start.27 = (bf16[512,128]{1,0:T(8,128)(2,1)}, bf16[512,128]{1,0:T(8,128)(2,1)S(1)}, u32[]{:S(2)}, u32[]{:S(2)}) collective-permute-start(bf16[512,128]{1,0:T(8,128)(2,1)} %get-tuple-element.206), channel_id=1, source_target_pairs={{0,2},{1,3},{2,0},{3,1},{4,6},{5,7},{6,4},{7,5},{8,10},{9,11},{10,... | collective-permute-start | bytes 393224 | tf_op jit(solution)/shard_map/ppermute | solution.py:87
  159.5 12.7 %collective-permute-start.30 = (bf16[512,128]{1,0:T(8,128)(2,1)}, bf16[512,128]{1,0:T(8,128)(2,1)S(1)}, u32[]{:S(2)}, u32[]{:S(2)}) collective-permute-start(bf16[512,128]{1,0:T(8,128)(2,1)} %get-tuple-element.235), channel_id=1, source_target_pairs={{0,2},{1,3},{2,0},{3,1},{4,6},{5,7},{6,4},{7,5},{8,10},{9,11},{10,... | collective-permute-start | bytes 393224 | tf_op jit(solution)/shard_map/ppermute | solution.py:87
  160.7 11.6 %collective-permute-start.31 = (bf16[512,128]{1,0:T(8,128)(2,1)}, bf16[512,128]{1,0:T(8,128)(2,1)S(1)}, u32[]{:S(2)}, u32[]{:S(2)}) collective-permute-start(bf16[512,128]{1,0:T(8,128)(2,1)} %get-tuple-element.236), channel_id=1, source_target_pairs={{0,1},{1,2},{2,3},{3,0},{4,5},{5,6},{6,7},{7,4},{8,9},{9,10},{10,1... | collective-permute-start | bytes 393224 | tf_op jit(solution)/shard_map/ppermute | solution.py:87
  172.3 13.6 %collective-permute-start.33 = (bf16[512,128]{1,0:T(8,128)(2,1)}, bf16[512,128]{1,0:T(8,128)(2,1)S(1)}, u32[]{:S(2)}, u32[]{:S(2)}) collective-permute-start(bf16[512,128]{1,0:T(8,128)(2,1)} %get-tuple-element.259), channel_id=1, source_target_pairs={{0,2},{1,3},{2,0},{3,1},{4,6},{5,7},{6,4},{7,5},{8,10},{9,11},{10,... | collective-permute-start | bytes 393224 | tf_op jit(solution)/shard_map/ppermute | solution.py:87
  173.6 12.3 %collective-permute-start.34 = (bf16[512,128]{1,0:T(8,128)(2,1)}, bf16[512,128]{1,0:T(8,128)(2,1)S(1)}, u32[]{:S(2)}, u32[]{:S(2)}) collective-permute-start(bf16[512,128]{1,0:T(8,128)(2,1)} %get-tuple-element.260), channel_id=1, source_target_pairs={{0,1},{1,2},{2,3},{3,0},{4,5},{5,6},{6,7},{7,4},{8,9},{9,10},{10,1... | collective-permute-start | bytes 393224 | tf_op jit(solution)/shard_map/ppermute | solution.py:87
  186.0 24.3 %collective-permute-start.36 = (bf16[512,128]{1,0:T(8,128)(2,1)S(1)}, bf16[512,128]{1,0:T(8,128)(2,1)S(1)}, u32[]{:S(2)}, u32[]{:S(2)}) collective-permute-start(bf16[512,128]{1,0:T(8,128)(2,1)S(1)} %copy-done.60), channel_id=1, source_target_pairs={{0,2},{1,3},{2,0},{3,1},{4,6},{5,7},{6,4},{7,5},{8,10},{9,11},{10,... | collective-permute-start | bytes 393224 | tf_op jit(solution)/shard_map/ppermute | solution.py:87
  186.9 23.4 %collective-permute-start.37 = (bf16[512,128]{1,0:T(8,128)(2,1)S(1)}, bf16[512,128]{1,0:T(8,128)(2,1)S(1)}, u32[]{:S(2)}, u32[]{:S(2)}) collective-permute-start(bf16[512,128]{1,0:T(8,128)(2,1)S(1)} %copy-done.59), channel_id=1, source_target_pairs={{0,1},{1,2},{2,3},{3,0},{4,5},{5,6},{6,7},{7,4},{8,9},{9,10},{10,1... | collective-permute-start | bytes 393224 | tf_op jit(solution)/shard_map/ppermute | solution.py:87
  188.8 21.5 %collective-permute-start.38 = (bf16[512,128]{1,0:T(8,128)(2,1)}, bf16[512,128]{1,0:T(8,128)(2,1)S(1)}, u32[]{:S(2)}, u32[]{:S(2)}) collective-permute-start(bf16[512,128]{1,0:T(8,128)(2,1)} %get-tuple-element.279), channel_id=1, source_target_pairs={{0,3},{1,0},{2,1},{3,2},{4,7},{5,4},{6,5},{7,6},{8,11},{9,8},{10,9... | collective-permute-start | bytes 393224 | tf_op jit(solution)/shard_map/ppermute | solution.py:87
  190.7 19.6 %collective-permute-start.39 = (bf16[512,128]{1,0:T(8,128)(2,1)}, bf16[512,128]{1,0:T(8,128)(2,1)S(1)}, u32[]{:S(2)}, u32[]{:S(2)}) collective-permute-start(bf16[512,128]{1,0:T(8,128)(2,1)} %get-tuple-element.281), channel_id=1, source_target_pairs={{0,2},{1,3},{2,0},{3,1},{4,6},{5,7},{6,4},{7,5},{8,10},{9,11},{10,... | collective-permute-start | bytes 393224 | tf_op jit(solution)/shard_map/ppermute | solution.py:87
  192.6 17.8 %collective-permute-start.40 = (bf16[512,128]{1,0:T(8,128)(2,1)}, bf16[512,128]{1,0:T(8,128)(2,1)S(1)}, u32[]{:S(2)}, u32[]{:S(2)}) collective-permute-start(bf16[512,128]{1,0:T(8,128)(2,1)} %get-tuple-element.283), channel_id=1, source_target_pairs={{0,1},{1,2},{2,3},{3,0},{4,5},{5,6},{6,7},{7,4},{8,9},{9,10},{10,1... | collective-permute-start | bytes 393224 | tf_op jit(solution)/shard_map/ppermute | solution.py:87
  210.4 23.7 %collective-permute-start.41 = (bf16[12288,128]{1,0:T(8,128)(2,1)}, bf16[12288,128]{1,0:T(8,128)(2,1)S(1)}, u32[]{:S(2)}, u32[]{:S(2)}) collective-permute-start(bf16[12288,128]{1,0:T(8,128)(2,1)} %get-tuple-element.285), channel_id=1, source_target_pairs={{0,4},{4,0},{8,12},{12,8},{16,20},{20,16},{24,28},{28,24},{1,5},{5... | collective-permute-start | bytes 9437192 | tf_op jit(solution)/shard_map/ppermute | solution.py:41
  219.3 14.0 %collective-permute-start.44 = (bf16[2048,128]{1,0:T(8,128)(2,1)S(1)}, bf16[2048,128]{1,0:T(8,128)(2,1)S(1)}, u32[]{:S(2)}, u32[]{:S(2)}) collective-permute-start(bf16[2048,128]{1,0:T(8,128)(2,1)S(1)} %get-tuple-element.345), channel_id=1, source_target_pairs={{0,16},{4,20},{8,0},{12,4},{24,8},{28,12},{16,24},{20,28},{1,17},{... | collective-permute-start | bytes 1572872 | tf_op jit(solution)/shard_map/ppermute | solution.py:38
  220.4 13.7 %collective-permute-start.43 = (bf16[2048,128]{1,0:T(8,128)(2,1)S(1)}, bf16[2048,128]{1,0:T(8,128)(2,1)S(1)}, u32[]{:S(2)}, u32[]{:S(2)}) collective-permute-start(bf16[2048,128]{1,0:T(8,128)(2,1)S(1)} %get-tuple-element.346), channel_id=1, source_target_pairs={{0,8},{4,12},{8,24},{12,28},{24,16},{28,20},{16,0},{20,4},{1,9},{5... | collective-permute-start | bytes 1572872 | tf_op jit(solution)/shard_map/ppermute | solution.py:38
  237.2 33.1 %collective-permute-start.45 = (bf16[4096,128]{1,0:T(8,128)(2,1)}, bf16[4096,128]{1,0:T(8,128)(2,1)S(1)}, u32[]{:S(2)}, u32[]{:S(2)}) collective-permute-start(bf16[4096,128]{1,0:T(8,128)(2,1)} %pad_maximum_fusion.1), channel_id=1, source_target_pairs={{0,8},{4,12},{8,24},{12,28},{24,16},{28,20},{16,0},{20,4},{1,9},{5... | collective-permute-start | bytes 3145736 | tf_op jit(solution)/shard_map/ppermute | solution.py:38
  239.2 31.1 %collective-permute-start.46 = (bf16[4096,128]{1,0:T(8,128)(2,1)}, bf16[4096,128]{1,0:T(8,128)(2,1)}, u32[]{:S(2)}, u32[]{:S(2)}) collective-permute-start(bf16[4096,128]{1,0:T(8,128)(2,1)} %pad_maximum_fusion.2), channel_id=1, source_target_pairs={{0,16},{4,20},{8,0},{12,4},{24,8},{28,12},{16,24},{20,28},{1,17},{... | collective-permute-start | bytes 3145736 | tf_op jit(solution)/shard_map/ppermute | solution.py:38
  244.2 62.9 %reduce-scatter.5.cloned.1.call-start = ((), (), s32[]{:S(2)}) async-start(), calls=%async_computation.3 | async-start | bytes 327680 | tf_op jit(solution)/shard_map/reduce_scatter | solution.py:450
  245.4 20.5 %collective-permute-start.47 = (bf16[1024,256]{1,0:T(8,128)(2,1)S(1)}, bf16[1024,256]{1,0:T(8,128)(2,1)S(1)}, u32[]{:S(2)}, u32[]{:S(2)}) collective-permute-start(bf16[1024,256]{1,0:T(8,128)(2,1)S(1)} %get-tuple-element.294), channel_id=1, source_target_pairs={{0,3},{1,0},{2,1},{3,2},{4,7},{5,4},{6,5},{7,6},{8,11},{9,8},{10,9... | collective-permute-start | bytes 1572872 | tf_op jit(solution)/shard_map/ppermute | solution.py:87
  248.2 22.1 %collective-permute-start.48 = (bf16[1024,256]{1,0:T(8,128)(2,1)S(1)}, bf16[1024,256]{1,0:T(8,128)(2,1)S(1)}, u32[]{:S(2)}, u32[]{:S(2)}) collective-permute-start(bf16[1024,256]{1,0:T(8,128)(2,1)S(1)} %get-tuple-element.297), channel_id=1, source_target_pairs={{0,1},{1,2},{2,3},{3,0},{4,5},{5,6},{6,7},{7,4},{8,9},{9,10},{10,1... | collective-permute-start | bytes 1572872 | tf_op jit(solution)/shard_map/ppermute | solution.py:87
  271.4 39.0 %collective-permute-start.49 = (bf16[12288,128]{1,0:T(8,128)(2,1)}, bf16[12288,128]{1,0:T(8,128)(2,1)S(1)}, u32[]{:S(2)}, u32[]{:S(2)}) collective-permute-start(bf16[12288,128]{1,0:T(8,128)(2,1)} %get-tuple-element.321), channel_id=1, source_target_pairs={{0,4},{4,0},{8,12},{12,8},{16,20},{20,16},{24,28},{28,24},{1,5},{5... | collective-permute-start | bytes 9437192 | tf_op jit(solution)/shard_map/ppermute | solution.py:41
  271.4 15.6 %collective-permute-start.50 = (bf16[4096,128]{1,0:T(8,128)(2,1)}, bf16[4096,128]{1,0:T(8,128)(2,1)}, u32[]{:S(2)}, u32[]{:S(2)}) collective-permute-start(bf16[4096,128]{1,0:T(8,128)(2,1)} %get-tuple-element.323), channel_id=1, source_target_pairs={{0,4},{4,0},{8,12},{12,8},{16,20},{20,16},{24,28},{28,24},{1,5},{5... | collective-permute-start | bytes 3145736 | tf_op jit(solution)/shard_map/ppermute | solution.py:41
  272.8 37.7 %collective-permute-start.53 = (bf16[1024,256]{1,0:T(8,128)(2,1)}, bf16[1024,256]{1,0:T(8,128)(2,1)}, u32[]{:S(2)}, u32[]{:S(2)}) collective-permute-start(bf16[1024,256]{1,0:T(8,128)(2,1)} %pad_maximum_fusion.7), channel_id=1, source_target_pairs={{0,2},{1,3},{2,0},{3,1},{4,6},{5,7},{6,4},{7,5},{8,10},{9,11},{10,... | collective-permute-start | bytes 1572872 | tf_op jit(solution)/shard_map/ppermute | solution.py:87
  289.8 20.6 %collective-permute-start.52 = (bf16[2048,128]{1,0:T(8,128)(2,1)}, bf16[2048,128]{1,0:T(8,128)(2,1)}, u32[]{:S(2)}, u32[]{:S(2)}) collective-permute-start(bf16[2048,128]{1,0:T(8,128)(2,1)} %get-tuple-element.343), channel_id=1, source_target_pairs={{0,16},{4,20},{8,0},{12,4},{24,8},{28,12},{16,24},{20,28},{1,17},{... | collective-permute-start | bytes 1572872 | tf_op jit(solution)/shard_map/ppermute | solution.py:38
  291.3 19.2 %collective-permute-start.51 = (bf16[2048,128]{1,0:T(8,128)(2,1)}, bf16[2048,128]{1,0:T(8,128)(2,1)}, u32[]{:S(2)}, u32[]{:S(2)}) collective-permute-start(bf16[2048,128]{1,0:T(8,128)(2,1)} %get-tuple-element.344), channel_id=1, source_target_pairs={{0,8},{4,12},{8,24},{12,28},{24,16},{28,20},{16,0},{20,4},{1,9},{5... | collective-permute-start | bytes 1572872 | tf_op jit(solution)/shard_map/ppermute | solution.py:38
  316.1 23.6 %collective-permute-start.55 = (bf16[4096,128]{1,0:T(8,128)(2,1)S(1)}, bf16[4096,128]{1,0:T(8,128)(2,1)S(1)}, u32[]{:S(2)}, u32[]{:S(2)}) collective-permute-start(bf16[4096,128]{1,0:T(8,128)(2,1)S(1)} %pad_maximum_fusion.4), channel_id=1, source_target_pairs={{0,16},{4,20},{8,0},{12,4},{24,8},{28,12},{16,24},{20,28},{1,17},{... | collective-permute-start | bytes 3145736 | tf_op jit(solution)/shard_map/ppermute | solution.py:38
  317.7 23.2 %collective-permute-start.54 = (bf16[4096,128]{1,0:T(8,128)(2,1)S(1)}, bf16[4096,128]{1,0:T(8,128)(2,1)S(1)}, u32[]{:S(2)}, u32[]{:S(2)}) collective-permute-start(bf16[4096,128]{1,0:T(8,128)(2,1)S(1)} %pad_maximum_fusion.3), channel_id=1, source_target_pairs={{0,8},{4,12},{8,24},{12,28},{24,16},{28,20},{16,0},{20,4},{1,9},{5... | collective-permute-start | bytes 3145736 | tf_op jit(solution)/shard_map/ppermute | solution.py:38
  (79 other events, 864.8 us)
Sparse Core Ops, SparseCore 0:
  64.1 32.9 all-gather.1
  244.3 40.8 reduce-scatter.6
  287.5 19.5 reduce-scatter.4

commit v4 on v3

--- a/solution.py
+++ b/solution.py
@@ -264,10 +264,10 @@
     )(columns, counts, meta, tiles, *grads)
 
 
-def dense_kernel(parts, chunks, meta, *refs):
+def dense_kernel(parts, chunks, n_earlier, meta, *refs):
     n_mixed = parts * chunks
     mixed_refs, cot_refs, w_hbm = refs[:n_mixed], refs[n_mixed : n_mixed + parts], refs[n_mixed + parts]
-    outs = refs[n_mixed + parts + 1 :]
+    outs = refs[n_mixed + parts + 1 + n_earlier :]
     act_outs, mg_outs = outs[:parts], outs[parts : parts + n_mixed]
     mixed_out, grad_out, weight, sems = outs[parts + n_mixed :]
     f_wide, h_wide = weight.shape[0] // parts, weight.shape[1] // parts
@@ -307,29 +307,37 @@
         mg_outs[i][...] = back[:, i * width : (i + 1) * width]
 
 
-def dense(meta, mixed, cot, weight, rows, first):
+def dense(meta, mixed, cot, weight, rows, first, earlier):
     parts, chunks = len(mixed), len(mixed[0])
     width = mixed[0][0][0].shape[1]
     features, hidden = weight.shape
     h_wide = hidden // parts
+    all_rows = cot[0].shape[0]
     step = min(rows, 256)
+    flat = [m for row in mixed for m in row]
+    earlier = list(earlier)
 
     def spec(w, start=0):
         return pl.BlockSpec((step, w), lambda t, meta: (t + start // step, 0))
 
-    flat = [m for row in mixed for m in row]
+    kinds = [(h_wide, True)] * parts + [(width, c > 0) for _ in range(parts) for c in range(chunks)]
+    kinds += [(features, True), (hidden, True)]
+    whole_at = [i for i, (_, whole) in enumerate(kinds) if whole]
+    n_inputs = 1 + len(flat) + parts + 1
     outs = pl.pallas_call(
-        functools.partial(dense_kernel, parts, chunks),
+        functools.partial(dense_kernel, parts, chunks, len(earlier)),
         grid_spec=pltpu.PrefetchScalarGridSpec(
             num_scalar_prefetch=1,
             grid=(rows // step,),
-            in_specs=[spec(width, at) for _, at in flat] + [spec(h_wide, first)] * parts + [any_spec()],
-            out_specs=[spec(h_wide)] * parts + [spec(width)] * (parts * chunks) + [spec(features), spec(hidden)],
+            in_specs=[spec(width, at) for _, at in flat]
+            + [spec(h_wide, first)] * parts
+            + [any_spec()]
+            + [any_spec()] * len(earlier),
+            out_specs=[spec(w, first if whole else 0) for w, whole in kinds],
             scratch_shapes=[pltpu.VMEM((features, hidden), BF16), pltpu.SemaphoreType.DMA((parts * parts,))],
         ),
-        out_shape=[jax.ShapeDtypeStruct((rows, h_wide), BF16)] * parts
-        + [jax.ShapeDtypeStruct((rows, width), BF16)] * (parts * chunks)
-        + [jax.ShapeDtypeStruct((rows, features), BF16), jax.ShapeDtypeStruct((rows, hidden), BF16)],
+        out_shape=[jax.ShapeDtypeStruct((all_rows if whole else rows, w), BF16) for w, whole in kinds],
+        input_output_aliases={n_inputs + i: at for i, at in enumerate(whole_at)} if earlier else {},
         compiler_params=params(),
         cost_estimate=pl.CostEstimate(
             flops=4 * rows * features * hidden,
@@ -337,10 +345,16 @@
             transcendentals=rows * hidden,
         ),
         name="dense",
-    )(meta, *[m for m, _ in flat], *cot, weight)
+    )(meta, *[m for m, _ in flat], *cot, weight, *earlier)
     n = parts * chunks
     act, back = outs[:parts], outs[parts : parts + n]
-    return act, [back[u * chunks : (u + 1) * chunks] for u in range(parts)], outs[-2], outs[-1]
+    return (
+        act,
+        [back[u * chunks : (u + 1) * chunks] for u in range(parts)],
+        outs[-2],
+        outs[-1],
+        [outs[i] for i in whole_at],
+    )
 
 
 def local(features, tiles, columns, counts, weight, cotangent):
@@ -390,41 +404,41 @@
         other = [got_other[c, i] for i in range(len(offsets))]
         return spmm(tiles, columns, counts, spmm_meta, own + other, parts, cut, skip)
 
-    w.go(metas=(spmm_meta, spmm_t_meta, dense_meta))
+    cot_ends = send(cot_blocks, ends)
+    own_other = ring.sibling(features)
     for c in range(chunks):
-        if c == 0:
-            w.go(own=ring.sibling(features), cot_ends=send(cot_blocks, ends))
         got_own[c, 0] = xs[c]
+        got_other[c, 0] = own_other[:, c * width : (c + 1) * width]
         for step in range(1, middle):
             name = f"{c}_{step}"
             w.go(**{"up" + name: ring.hop(up, 1), "down" + name: ring.hop(down, -1)})
             if c and step == 1:
-                for i in (-2, -1):
-                    got_other[c - 1, len(offsets) + i] = ring.sibling(got_own[c - 1, len(offsets) + i])
+                for i in range(1, len(offsets)):
+                    got_other[c - 1, i] = ring.sibling(got_own[c - 1, i])
                 w.go(**{f"mixed{c - 1}": run_spmm(c - 1, 1, 0)})
             w.close()
             up, down = w["up" + name], w["down" + name]
             got_own[c, 2 * step - 1], got_own[c, 2 * step] = up, down
-            w.go(**{"other_up" + name: ring.sibling(up), "other_down" + name: ring.sibling(down)})
         w.go(**{f"far_up{c}": ring.hop(up[:half], 1), f"far_down{c}": ring.hop(down[half:], -1)})
-        if c:
+        if c == 0:
+            w.go(cot_ends=cot_ends, own_other=own_other, metas=(spmm_meta, spmm_t_meta, dense_meta))
+        else:
             mixed[c - 1] = w[f"mixed{c - 1}"]
-            w.go(**{f"mixed_ends{c - 1}": send(mixed[c - 1], ends)})
+        if c == last:
+            for step in range(1, middle):
+                for i in (2 * step - 1, 2 * step):
+                    got_other[c, i] = ring.sibling(got_own[c, i])
+                    w.go(**{f"other{c}_{i}": got_other[c, i]})
         w.close()
         if c == 0:
             spmm_meta, spmm_t_meta, dense_meta = w["metas"]
-        if c == 0:
             w.go(cot_inner=send([w.gate(b) for b in cot_blocks], inner))
-            w_full = lax.all_gather(w.gate(w_share), "row", axis=0, tiled=True)
         else:
-            w.go(**{f"mixed_inner{c - 1}": send(mixed[c - 1], inner)})
+            w.go(**{f"mixed_got{c - 1}": send(mixed[c - 1], ends + inner)})
         got_own[c, len(offsets) - 2], got_own[c, len(offsets) - 1] = w[f"far_up{c}"], w[f"far_down{c}"]
-        got_other[c, 0] = w["own"][:, c * width : (c + 1) * width]
-        for step in range(1, middle):
-            name = f"{c}_{step}"
-            got_other[c, 2 * step - 1], got_other[c, 2 * step] = w["other_up" + name], w["other_down" + name]
         if c < last:
             up = down = w.gate(xs[c + 1])
+    w_full = lax.all_gather(w.gate(w_share), "row", axis=0, tiled=True)
     for i in (-2, -1):
         got_other[last, len(offsets) + i] = ring.sibling(got_own[last, len(offsets) + i])
 
@@ -434,37 +448,43 @@
         w.go(**{f"half_got{h}": send(w[f"half{h}"], ends + inner)})
 
     cot = ordered(cot_blocks[0], w["cot_ends"], w["cot_inner"])
-    whole = [ordered(mixed[c][0], w[f"mixed_ends{c}"], w[f"mixed_inner{c}"]) for c in range(last)]
-    sums = 0.0
+    whole = [ordered(mixed[c][0], w[f"mixed_got{c}"]) for c in range(last)]
+    earlier = ()
     for h in range(halves):
         part = ordered(w[f"half{h}"][0], w[f"half_got{h}"])
         blocks = [[(whole[c][u], h * half_rows) for c in range(last)] + [(part[u], 0)] for u in range(parts)]
-        act, back, mixed_rows, grad_rows = dense(dense_meta, blocks, cot, w_full, half_rows, h * half_rows)
-        sums += lax.dot_general(mixed_rows, grad_rows, (((0,), (0,)), ((), ())), preferred_element_type=F32)
-        w.go(**{f"act{h}": act, f"back{h}": back})
+        act, back, mixed_rows, grad_rows, earlier = dense(
+            dense_meta, blocks, cot, w_full, half_rows, h * half_rows, earlier
+        )
+        w.go(**{f"back{h}": [b[0] for b in back]})
+        if h == halves - 1:
+            w.go(whole=(act, back, mixed_rows, grad_rows))
         w.close()
-        w.go(**{f"back_got0_{h}": send([b[0] for b in w[f"back{h}"]], ends + inner)})
+        w.go(**{f"back_got{h}": send(w[f"back{h}"], ends + inner)})
+    act, back, mixed_rows, grad_rows = w["whole"]
+    sums = lax.dot_general(mixed_rows, grad_rows, (((0,), (0,)), ((), ())), preferred_element_type=F32)
+    w.go(sums=sums.astype(BF16))
     w.close()
-
-    weight_terms = lax.psum_scatter(sums.astype(BF16), "row", scatter_dimension=1, tiled=True)
-    weight_grad = lax.psum_scatter(weight_terms, "rep", scatter_dimension=0, tiled=True).astype(F32)
-
-    act_blocks = [jnp.concatenate([w[f"act{h}"][u] for h in range(halves)]) for u in range(parts)]
+    weight_terms = lax.psum_scatter(w["sums"], "row", scatter_dimension=1, tiled=True)
+
     feature_grad = []
     for c in range(chunks):
-        grads = [
-            ordered(w[f"back{h}"][0][c], w[f"back_got{c}_{h}"])[u] for u in range(parts) for h in range(halves)
-        ]
         if c:
-            grads = [w.gate(g) for g in grads]
+            grads = [w.gate(g) for g in ordered(back[0][c], w[f"rest_ends{c}"], w[f"rest_inner{c}"])]
+        else:
+            parts_got = [ordered(w[f"back{h}"][0], w[f"back_got{h}"]) for h in range(halves)]
+            grads = [parts_got[h][u] for u in range(parts) for h in range(halves)]
         w.go(**{f"terms{c}": spmm_t(tiles, columns, counts, spmm_t_meta, grads, parts, held, rows, rows * row_size)})
         if c < last:
-            for h in range(halves):
-                w.go(**{f"back_got{c + 1}_{h}": send([w.gate(b[c + 1]) for b in w[f"back{h}"]], ends + inner)})
+            rest = [w.gate(b[c + 1]) for b in back]
+            w.go(**{f"rest_ends{c + 1}": send(rest, ends)})
         w.close()
+        if c < last:
+            w.go(**{f"rest_inner{c + 1}": send(rest, inner)})
         terms = w[f"terms{c}"]
         own_far, own_near, other_far, other_near = terms[0], terms[1:-2], terms[-2], terms[-1]
         got_far = ring.sibling(other_far)
+        other_near = lax.optimization_barrier((other_near, got_far))[0]
         w.go(**{f"got_near{c}": ring.sibling(other_near)})
 
         def far(start):
@@ -474,7 +494,7 @@
         down = ring.hop(far(half).astype(BF16), -1)
         w.go(**{f"sum{c}_{middle}": (up, down)})
         if c == last:
-            w.go(act_inner=send(act_blocks, inner))
+            w.go(act_inner=send(act, inner))
         w.close()
         got_near = w[f"got_near{c}"]
 
@@ -493,18 +513,19 @@
             to_up, to_down = to_up.astype(BF16), to_down.astype(BF16)
             w.go(**{f"sum{c}_{step}": (ring.hop(to_up, 1), ring.hop(to_down, -1))})
             if c == 0 and step == middle - 1:
-                w.go(act_ends=send([w.gate(a) for a in act_blocks], ends))
+                w.go(act_ends=send([w.gate(a) for a in act], ends))
             if step > 1:
                 w.close()
-            elif c < last:
+            else:
                 w.token = to_up[:8]
         up, down = (w.pending if f"sum{c}_1" in w.pending else w.done)[f"sum{c}_1"]
         if middle == 1:
             feature_grad.append((near_sum(0) + jnp.concatenate([up, down]).astype(F32)).astype(BF16))
         else:
             feature_grad.append((near_sum(0) + up.astype(F32) + down.astype(F32)).astype(BF16))
-    act = {**w.pending, **w.done}
-    act = ordered(act_blocks[0], act["act_ends"], act["act_inner"])
+    weight_grad = lax.psum_scatter(w.gate(weight_terms), "rep", scatter_dimension=0, tiled=True).astype(F32)
+    got = {**w.pending, **w.done}
+    act = ordered(act[0], got["act_ends"], got["act_inner"])
     feature_grad = jnp.concatenate(feature_grad, axis=1)
     activations = jnp.zeros((rows, h_wide), BF16)
     for u in range(parts):

time: 352 us -> 368 us (1.045)
  waiting for transfers between devices: 121 us -> 132 us
  starting transfers between devices: 52.1 us -> 56.6 us
  other arithmetic: 21.2 us -> 17.1 us
    unnamed x4, waiting for transfers between devices: 11.1 us -> 37.2 us
    ppermute x27 -> x24, waiting for transfers between devices: 52 us -> 41.1 us  [send(): lax.ppermute(blocks[s], 'rep', [(i, (i + s) % size) for i in range(size)])]
    ppermute x13, waiting for transfers between devices: 9.03 us -> 2.89 us  [sibling(): return lax.ppermute(value, 'row', [(d, d ^ 1) for d in range(self.devices)])]
    ppermute x27 -> x24, starting transfers between devices: 31.2 us -> 35.4 us  [send(): lax.ppermute(blocks[s], 'rep', [(i, (i + s) % size) for i in range(size)])]
    unnamed x139 -> x97, local copies, waits for them, and re-layouts: 10.7 us -> 10.4 us
  transfers between devices with their start and end apart: 59 -> 56, of which waited for: 23 -> 17; matrix products, arithmetic and copies ran while one was open for 11% -> 12% of each run, Pallas kernels for 24% -> 23%
where the time goes in v4:
time: 368 us; the launch traced here: 367 us
  waiting for transfers between devices  132 us (36%)
  Pallas kernels  85.2 us (23%)
  starting transfers between devices  56.6 us (15%)
  local copies, waits for them, and re-layouts  33.1 us (9%)
  between operations  22.3 us (6%)
  other arithmetic  17.1 us (5%)
  blocking collectives  14.6 us (4%)
  matrix products  5.96 us (2%)
    ppermute x24, waiting for transfers between devices, send(): lax.ppermute(blocks[s], 'rep', [(i, (i + s) % size) for i in range(size)])  41.1 us
    ppermute x16, waiting for transfers between devices, hop(): return lax.ppermute(value, 'row', self.perm(step))  37.4 us
    unnamed x4, waiting for transfers between devices  37.2 us
    pallas_call x3, Pallas kernels, spmm(): pl.pallas_call(functools.partial(spmm_kernel, len(pieces), per_part, skip...  36.5 us
    ppermute x24, starting transfers between devices, send(): lax.ppermute(blocks[s], 'rep', [(i, (i + s) % size) for i in range(size)])  35.4 us
    pallas_call x2, Pallas kernels, spmm_t(): pl.pallas_call(functools.partial(spmm_t_kernel, len(grads), per_part, len...  34.4 us
    ppermute x16, starting transfers between devices, hop(): return lax.ppermute(value, 'row', self.perm(step))  18.2 us
    all_gather x1, blocking collectives, local(): w_share = lax.all_gather(w_share, 'rep', axis=1, tiled=True)  14.6 us
  transfers between devices with their start and end apart: 56, of which 17 were waited for; matrix products, arithmetic and copies ran while one was open for 12% of the time, Pallas kernels for 23%

profile of v4, /device:TPU:0, one launch (start us, length us, event | category | flops | bytes accessed | tf_op | source)
XLA Modules:
  0.0 366.5 jit_solution(9349100828576014814)
XLA Ops:
  7.7 1.7 fusion.5
  9.4 2.6 collective-permute-start
  12.1 2.7 constant_dynamic-slice_fusion
  14.8 4.1 %collective-permute-start.4 = (bf16[1024,256]{1,0:T(8,128)(2,1)S(1)}, bf16[1024,256]{1,0:T(8,128)(2,1)}, u32[]{:S(2)}, u32[]{:S(2)}) collective-permute-start(bf16[1024,256]{1,0:T(8,128)(2,1)S(1)} %get-tuple-element.312), channel_id=1, source_target_pairs={{0,3},{1,0},{2,1},{3,2},{4,7},{5,4},{6,5},{7,6},{8,11},{9,8},{10,9... | collective-permute-start | bytes 1572872 | tf_op jit(solution)/shard_map/ppermute | solution.py:87
  18.9 17.0 %collective-permute-done.refs_1_ = bf16[4096,128]{1,0:T(8,128)(2,1)} collective-permute-done((bf16[4096,128]{1,0:T(8,128)(2,1)S(1)}, bf16[4096,128]{1,0:T(8,128)(2,1)}, u32[]{:S(2)}, u32[]{:S(2)}) %collective-permute-start) | collective-permute-done | bytes 1048608 | tf_op jit(solution)/shard_map/ppermute | solution.py:38
  37.9 1.9 slice.100
  40.9 1.6 collective-permute-start.2
  58.8 2.7 collective-permute-start.7
  61.5 3.0 fusion.4
  65.4 14.4 %spmm.3 = (bf16[1024,128]{1,0:T(8,128)(2,1)}, bf16[1024,128]{1,0:T(8,128)(2,1)}, bf16[1024,128]{1,0:T(8,128)(2,1)}, bf16[1024,128]{1,0:T(8,128)(2,1)}) custom-call(s32[32,16]{1,0:T(8,128)} %copy.60.cols, s32[32]{0:T(128)} %counts.9, s32[11]{0:T(128)} %stack.75.meta, bf16[32,16,128,128]{3,2,1,0:T(8,128)(2,1)} %tiles.9, bf16[4096,128]{1,0:T(8,128)(2,1)} %copy-done.5, ...), custom_call_target="tpu_custom_call" | custom-call | flops 2147483648 | bytes 25165824 | tf_op jit(solution)/shard_map/spmm/pallas_call | solution.py:158
  79.9 5.6 %collective-permute-done.7.refs_10_ = bf16[1024,256]{1,0:T(8,128)(2,1)S(1)} collective-permute-done((bf16[1024,256]{1,0:T(8,128)(2,1)}, bf16[1024,256]{1,0:T(8,128)(2,1)S(1)}, u32[]{:S(2)}, u32[]{:S(2)}) %collective-permute-start.7) | collective-permute-done | bytes 524320 | tf_op jit(solution)/shard_map/ppermute | solution.py:87
  86.9 1.9 slice.105
  90.9 14.6 %all_gather.6 = bf16[128,1024]{1,0:T(8,128)(2,1)} all-gather(bf16[128,256]{1,0:T(8,128)(2,1)S(1)} %constant_dynamic-slice_fusion.1), channel_id=1, replica_groups=mesh['row'=8,'rep'=4] {'rep'}, dimensions={1}, use_global_device_ids=true | all-gather | bytes 327680 | tf_op jit(solution)/shard_map/all_gather | solution.py:393
  106.1 4.2 %collective-permute-start.14 = (bf16[1024,128]{1,0:T(8,128)(2,1)}, bf16[1024,128]{1,0:T(8,128)(2,1)S(1)}, u32[]{:S(2)}, u32[]{:S(2)}) collective-permute-start(bf16[1024,128]{1,0:T(8,128)(2,1)} %get-tuple-element.164), channel_id=1, source_target_pairs={{0,3},{1,0},{2,1},{3,2},{4,7},{5,4},{6,5},{7,6},{8,11},{9,8},{10,9... | collective-permute-start | bytes 786440 | tf_op jit(solution)/shard_map/ppermute | solution.py:87
  112.0 11.1 %spmm.4 = (bf16[512,128]{1,0:T(8,128)(2,1)}, bf16[512,128]{1,0:T(8,128)(2,1)}, bf16[512,128]{1,0:T(8,128)(2,1)}, bf16[512,128]{1,0:T(8,128)(2,1)}) custom-call(s32[32,16]{1,0:T(8,128)} %copy.60.cols, s32[32]{0:T(128)} %counts.9, s32[11]{0:T(128)} %stack.75.meta, bf16[32,16,128,128]{3,2,1,0:T(8,128)(2,1)} %tiles.9, bf16[4096,128]{1,0:T(8,128)(2,1)} %copy-done.2, ...), custom_call_target="tpu_custom_call" | custom-call | flops 1073741824 | bytes 16777216 | tf_op jit(solution)/shard_map/spmm/pallas_call | solution.py:158
  123.1 10.2 %collective-permute-done.15.refs_4_ = bf16[1024,128]{1,0:T(8,128)(2,1)S(1)} collective-permute-done((bf16[1024,128]{1,0:T(8,128)(2,1)}, bf16[1024,128]{1,0:T(8,128)(2,1)S(1)}, u32[]{:S(2)}, u32[]{:S(2)}) %collective-permute-start.15) | collective-permute-done | bytes 262176 | tf_op jit(solution)/shard_map/ppermute | solution.py:87
  133.3 2.4 collective-permute-start.24
  135.7 2.0 collective-permute-start.25
  137.8 11.0 %spmm.5 = (bf16[512,128]{1,0:T(8,128)(2,1)}, bf16[512,128]{1,0:T(8,128)(2,1)}, bf16[512,128]{1,0:T(8,128)(2,1)}, bf16[512,128]{1,0:T(8,128)(2,1)}) custom-call(s32[32,16]{1,0:T(8,128)} %copy.60.cols, s32[32]{0:T(128)} %counts.9, s32[11]{0:T(128)} %stack.75.meta, bf16[32,16,128,128]{3,2,1,0:T(8,128)(2,1)} %tiles.9, bf16[4096,128]{1,0:T(8,128)(2,1)} %copy-done.2, ...), custom_call_target="tpu_custom_call" | custom-call | flops 1073741824 | bytes 16777216 | tf_op jit(solution)/shard_map/spmm/pallas_call | solution.py:158
  148.8 1.9 collective-permute-start.26
  151.4 7.1 %dense.2 = (bf16[1024,256]{1,0:T(8,128)(2,1)}, bf16[1024,256]{1,0:T(8,128)(2,1)}, bf16[1024,256]{1,0:T(8,128)(2,1)}, bf16[1024,256]{1,0:T(8,128)(2,1)}, bf16[512...) custom-call(s32[1]{0:T(128)} %bitcast.meta, ...), custom_call_target="tpu_custom_call" | custom-call | flops 2147483648 | bytes 8388608 | tf_op jit(solution)/shard_map/dense/pallas_call | solution.py:327
  158.6 3.4 collective-permute-done.27.refs_5_
  163.5 2.0 collective-permute-start.31
  165.6 7.2 %dense.3 = (bf16[1024,256]{1,0:T(8,128)(2,1)}, bf16[1024,256]{1,0:T(8,128)(2,1)}, bf16[1024,256]{1,0:T(8,128)(2,1)}, bf16[1024,256]{1,0:T(8,128)(2,1)}, bf16[512...) custom-call(s32[1]{0:T(128)} %bitcast.meta, ...), custom_call_target="tpu_custom_call", output_to_operand_aliasing={{0}: (14, {}), {1}: (15, {}), {2}: (16, {}), {3}: (17, {}),... | custom-call | flops 2147483648 | bytes 8388608 | tf_op jit(solution)/shard_map/dense/pallas_call | solution.py:327
  172.8 2.2 collective-permute-done.30.refs_4_
  176.3 2.0 collective-permute-start.34
  178.3 6.0 %convolution_convert_fusion = bf16[1024,1024]{1,0:T(8,128)(2,1)} fusion(bf16[1024,1024]{1,0:T(8,128)(2,1)} %get-tuple-element.241, bf16[1024,1024]{1,0:T(8,128)(2,1)} %get-tuple-element.242), kind=kOutput, calls=%fused_computation.7 | convolution fusion | flops 2148532224 | bytes 6291456 | tf_op jit(solution)/shard_map/dot_general | solution.py:465
  184.3 4.1 %collective-permute-done.33.refs_5_ = bf16[512,128]{1,0:T(8,128)(2,1)S(1)} collective-permute-done((bf16[512,128]{1,0:T(8,128)(2,1)}, bf16[512,128]{1,0:T(8,128)(2,1)S(1)}, u32[]{:S(2)}, u32[]{:S(2)}) %collective-permute-start.33) | collective-permute-done | bytes 131104 | tf_op jit(solution)/shard_map/ppermute | solution.py:87
  188.5 3.8 %collective-permute-start.35 = (bf16[1024,128]{1,0:T(8,128)(2,1)S(1)}, bf16[1024,128]{1,0:T(8,128)(2,1)S(1)}, u32[]{:S(2)}, u32[]{:S(2)}) collective-permute-start(bf16[1024,128]{1,0:T(8,128)(2,1)S(1)} %copy-done.29), channel_id=1, source_target_pairs={{0,3},{1,0},{2,1},{3,2},{4,7},{5,4},{6,5},{7,6},{8,11},{9,8},{10,9... | collective-permute-start | bytes 786440 | tf_op jit(solution)/shard_map/ppermute | solution.py:87
  192.3 17.2 %spmm_t.2 = (bf16[4096,128]{1,0:T(8,128)(2,1)}, bf16[4096,128]{1,0:T(8,128)(2,1)}, bf16[4096,128]{1,0:T(8,128)(2,1)}, bf16[4096,128]{1,0:T(8,128)(2,1)}, bf16[40...) custom-call(s32[32,16]{1,0:T(8,128)} %copy.60.cols, s32[32]{0:T(128)} %counts.9, s32[9]{0:T(128)} %stack.84.meta, ...), custom_call_target="tpu_custom_call" | custom-call | flops 2147483648 | bytes 25165824 | tf_op jit(solution)/shard_map/spmm_t/pallas_call | solution.py:241
  209.6 2.9 collective-permute-done.38
  216.2 12.2 %collective-permute-done.37.refs_2_ = bf16[1024,128]{1,0:T(8,128)(2,1)S(1)} collective-permute-done((bf16[1024,128]{1,0:T(8,128)(2,1)S(1)}, bf16[1024,128]{1,0:T(8,128)(2,1)S(1)}, u32[]{:S(2)}, u32[]{:S(2)}) %collective-permute-start.37) | collective-permute-done | bytes 262176 | tf_op jit(solution)/shard_map/ppermute | solution.py:87
  232.1 3.7 %collective-permute-start.44 = (bf16[1024,256]{1,0:T(8,128)(2,1)S(1)}, bf16[1024,256]{1,0:T(8,128)(2,1)S(1)}, u32[]{:S(2)}, u32[]{:S(2)}) collective-permute-start(bf16[1024,256]{1,0:T(8,128)(2,1)S(1)} %copy-done.18), channel_id=1, source_target_pairs={{0,3},{1,0},{2,1},{3,2},{4,7},{5,4},{6,5},{7,6},{8,11},{9,8},{10,9... | collective-permute-start | bytes 1572872 | tf_op jit(solution)/shard_map/ppermute | solution.py:87
  235.8 17.2 %spmm_t.3 = (bf16[4096,128]{1,0:T(8,128)(2,1)}, bf16[4096,128]{1,0:T(8,128)(2,1)}, bf16[4096,128]{1,0:T(8,128)(2,1)}, bf16[4096,128]{1,0:T(8,128)(2,1)}, bf16[40...) custom-call(s32[32,16]{1,0:T(8,128)} %copy.60.cols, s32[32]{0:T(128)} %counts.9, s32[9]{0:T(128)} %stack.84.meta, ...), custom_call_target="tpu_custom_call" | custom-call | flops 2147483648 | bytes 25165824 | tf_op jit(solution)/shard_map/spmm_t/pallas_call | solution.py:241
  253.0 3.4 collective-permute-done.44
  257.2 3.9 %copy.65 = bf16[1024,1024]{0,1:T(8,128)(2,1)} copy(bf16[1024,1024]{1,0:T(8,128)(2,1)} %convolution_convert_fusion) | data formatting | bytes 4194304
  261.8 2.3 collective-permute-start.50
  264.1 37.2 %reduce-scatter.7.cloned.1.call-done = bf16[128,1024]{1,0:T(8,128)(2,1)} async-done(((bf16[1024,1024]{1,0:T(8,128)(2,1)}), bf16[128,1024]{1,0:T(8,128)(2,1)}) %reduce-scatter.7.cloned.1.call-update) | async-done | bytes 262160
  301.3 1.8 copy.66
  303.1 2.8 add_convert_fusion.2
  310.3 13.1 %reduce-scatter.5.cloned.1.call-done = bf16[256,128]{1,0:T(8,128)(2,1)} async-done(((bf16[1024,128]{1,0:T(8,128)(2,1)}), bf16[256,128]{1,0:T(8,128)(2,1)}) %reduce-scatter.5.cloned.1.call-update) | async-done | bytes 65552 | tf_op jit(solution)/shard_map/reduce_scatter | solution.py:526
  324.9 1.9 constant_dynamic-update-slice_fusion.1
  326.8 2.6 convert_add_fusion.1
  334.2 2.1 add_convert_fusion.1
  336.3 2.0 constant_dynamic-update-slice_fusion.2
  339.1 14.9 %collective-permute-done.51 = bf16[4096,128]{1,0:T(8,128)(2,1)S(1)} collective-permute-done((bf16[4096,128]{1,0:T(8,128)(2,1)S(1)}, bf16[4096,128]{1,0:T(8,128)(2,1)S(1)}, u32[]{:S(2)}, u32[]{:S(2)}) %collective-permute-start.51) | collective-permute-done | bytes 1048608 | tf_op jit(solution)/shard_map/ppermute | solution.py:38
  353.9 2.7 collective-permute-done.52
  356.6 1.8 add_convert_fusion
  (210 shorter events, 44.6 us)
Async XLA Ops:
  7.2 144.2 %all-gather.2.cloned.1.call-start = ((), (), s32[]{:S(2)}) async-start(), calls=%async_computation.2 | async-start | bytes 2359296 | tf_op jit(solution)/shard_map/all_gather | solution.py:441
  7.2 48.8 %collective-permute-start.6 = (bf16[4096,256]{1,0:T(8,128)(2,1)}, bf16[4096,256]{1,0:T(8,128)(2,1)}, u32[]{:S(2)}, u32[]{:S(2)}) collective-permute-start(bf16[4096,256]{1,0:T(8,128)(2,1)} %param.42), channel_id=1, source_target_pairs={{0,4},{4,0},{8,12},{12,8},{16,20},{20,16},{24,28},{28,24},{1,5},{5... | collective-permute-start | bytes 6291464 | tf_op jit(solution)/shard_map/ppermute | solution.py:41
  9.4 26.5 %collective-permute-start = (bf16[4096,128]{1,0:T(8,128)(2,1)S(1)}, bf16[4096,128]{1,0:T(8,128)(2,1)}, u32[]{:S(2)}, u32[]{:S(2)}) collective-permute-start(bf16[4096,128]{1,0:T(8,128)(2,1)S(1)} %get-tuple-element.318.refs_0_), channel_id=1, source_target_pairs={{0,8},{4,12},{8,24},{12,28},{24,16},{28,20},{16,0},{20,4},{1,9},{5... | collective-permute-start | bytes 3145736 | tf_op jit(solution)/shard_map/ppermute | solution.py:38
  12.0 25.4 %collective-permute-start.1 = (bf16[4096,128]{1,0:T(8,128)(2,1)S(1)}, bf16[4096,128]{1,0:T(8,128)(2,1)}, u32[]{:S(2)}, u32[]{:S(2)}) collective-permute-start(bf16[4096,128]{1,0:T(8,128)(2,1)S(1)} %get-tuple-element.318.refs_0_), channel_id=1, source_target_pairs={{0,16},{4,20},{8,0},{12,4},{24,8},{28,12},{16,24},{20,28},{1,17},{... | collective-permute-start | bytes 3145736 | tf_op jit(solution)/shard_map/ppermute | solution.py:38
  14.8 26.0 %collective-permute-start.4 = (bf16[1024,256]{1,0:T(8,128)(2,1)S(1)}, bf16[1024,256]{1,0:T(8,128)(2,1)}, u32[]{:S(2)}, u32[]{:S(2)}) collective-permute-start(bf16[1024,256]{1,0:T(8,128)(2,1)S(1)} %get-tuple-element.312), channel_id=1, source_target_pairs={{0,3},{1,0},{2,1},{3,2},{4,7},{5,4},{6,5},{7,6},{8,11},{9,8},{10,9... | collective-permute-start | bytes 1572872 | tf_op jit(solution)/shard_map/ppermute | solution.py:87
  18.9 23.5 %collective-permute-start.5 = (bf16[1024,256]{1,0:T(8,128)(2,1)S(1)}, bf16[1024,256]{1,0:T(8,128)(2,1)}, u32[]{:S(2)}, u32[]{:S(2)}) collective-permute-start(bf16[1024,256]{1,0:T(8,128)(2,1)S(1)} %get-tuple-element.314), channel_id=1, source_target_pairs={{0,1},{1,2},{2,3},{3,0},{4,5},{5,6},{6,7},{7,4},{8,9},{9,10},{10,1... | collective-permute-start | bytes 1572872 | tf_op jit(solution)/shard_map/ppermute | solution.py:87
  37.4 21.4 %collective-permute-start.10 = (bf16[4096,128]{1,0:T(8,128)(2,1)}, bf16[4096,128]{1,0:T(8,128)(2,1)}, u32[]{:S(2)}, u32[]{:S(2)}) collective-permute-start(bf16[4096,128]{1,0:T(8,128)(2,1)} %collective-permute-done.refs_1_), channel_id=1, source_target_pairs={{0,4},{4,0},{8,12},{12,8},{16,20},{20,16},{24,28},{28,24},{1,5},{5... | collective-permute-start | bytes 3145736 | tf_op jit(solution)/shard_map/ppermute | solution.py:41
  37.4 21.4 %collective-permute-start.11 = (bf16[4096,128]{1,0:T(8,128)(2,1)}, bf16[4096,128]{1,0:T(8,128)(2,1)}, u32[]{:S(2)}, u32[]{:S(2)}) collective-permute-start(bf16[4096,128]{1,0:T(8,128)(2,1)} %collective-permute-done.1.refs_2_), channel_id=1, source_target_pairs={{0,4},{4,0},{8,12},{12,8},{16,20},{20,16},{24,28},{28,24},{1,5},{5... | collective-permute-start | bytes 3145736 | tf_op jit(solution)/shard_map/ppermute | solution.py:41
  40.9 14.1 %collective-permute-start.2 = (bf16[2048,128]{1,0:T(8,128)(2,1)}, bf16[2048,128]{1,0:T(8,128)(2,1)S(1)}, u32[]{:S(2)}, u32[]{:S(2)}) collective-permute-start(bf16[2048,128]{1,0:T(8,128)(2,1)} %slice.100), channel_id=1, source_target_pairs={{0,8},{4,12},{8,24},{12,28},{24,16},{28,20},{16,0},{20,4},{1,9},{5... | collective-permute-start | bytes 1572872 | tf_op jit(solution)/shard_map/ppermute | solution.py:38
  42.4 13.6 %collective-permute-start.3 = (bf16[2048,128]{1,0:T(8,128)(2,1)S(1)}, bf16[2048,128]{1,0:T(8,128)(2,1)S(1)}, u32[]{:S(2)}, u32[]{:S(2)}) collective-permute-start(bf16[2048,128]{1,0:T(8,128)(2,1)S(1)} %slice.101), channel_id=1, source_target_pairs={{0,16},{4,20},{8,0},{12,4},{24,8},{28,12},{16,24},{20,28},{1,17},{... | collective-permute-start | bytes 1572872 | tf_op jit(solution)/shard_map/ppermute | solution.py:38
  56.8 28.7 %collective-permute-start.8 = (bf16[4096,128]{1,0:T(8,128)(2,1)S(1)}, bf16[4096,128]{1,0:T(8,128)(2,1)S(1)}, u32[]{:S(2)}, u32[]{:S(2)}) collective-permute-start(bf16[4096,128]{1,0:T(8,128)(2,1)S(1)} %get-tuple-element.157.refs_0_), channel_id=1, source_target_pairs={{0,8},{4,12},{8,24},{12,28},{24,16},{28,20},{16,0},{20,4},{1,9},{5... | collective-permute-start | bytes 3145736 | tf_op jit(solution)/shard_map/ppermute | solution.py:38
  57.6 28.0 %collective-permute-start.9 = (bf16[4096,128]{1,0:T(8,128)(2,1)S(1)}, bf16[4096,128]{1,0:T(8,128)(2,1)}, u32[]{:S(2)}, u32[]{:S(2)}) collective-permute-start(bf16[4096,128]{1,0:T(8,128)(2,1)S(1)} %get-tuple-element.157.refs_0_), channel_id=1, source_target_pairs={{0,16},{4,20},{8,0},{12,4},{24,8},{28,12},{16,24},{20,28},{1,17},{... | collective-permute-start | bytes 3145736 | tf_op jit(solution)/shard_map/ppermute | solution.py:38
  58.8 26.7 %collective-permute-start.7 = (bf16[1024,256]{1,0:T(8,128)(2,1)}, bf16[1024,256]{1,0:T(8,128)(2,1)S(1)}, u32[]{:S(2)}, u32[]{:S(2)}) collective-permute-start(bf16[1024,256]{1,0:T(8,128)(2,1)} %get-tuple-element.156), channel_id=1, source_target_pairs={{0,2},{1,3},{2,0},{3,1},{4,6},{5,7},{6,4},{7,5},{8,10},{9,11},{10,... | collective-permute-start | bytes 1572872 | tf_op jit(solution)/shard_map/ppermute | solution.py:87
  85.5 19.9 %collective-permute-start.19 = (bf16[4096,128]{1,0:T(8,128)(2,1)S(1)}, bf16[4096,128]{1,0:T(8,128)(2,1)S(1)}, u32[]{:S(2)}, u32[]{:S(2)}) collective-permute-start(bf16[4096,128]{1,0:T(8,128)(2,1)S(1)} %collective-permute-done.8.refs_1_), channel_id=1, source_target_pairs={{0,4},{4,0},{8,12},{12,8},{16,20},{20,16},{24,28},{28,24},{1,5},{5... | collective-permute-start | bytes 3145736 | tf_op jit(solution)/shard_map/ppermute | solution.py:41
  85.6 19.9 %collective-permute-start.20 = (bf16[4096,128]{1,0:T(8,128)(2,1)}, bf16[4096,128]{1,0:T(8,128)(2,1)}, u32[]{:S(2)}, u32[]{:S(2)}) collective-permute-start(bf16[4096,128]{1,0:T(8,128)(2,1)} %collective-permute-done.9.refs_2_), channel_id=1, source_target_pairs={{0,4},{4,0},{8,12},{12,8},{16,20},{20,16},{24,28},{28,24},{1,5},{5... | collective-permute-start | bytes 3145736 | tf_op jit(solution)/shard_map/ppermute | solution.py:41
  88.8 16.6 %collective-permute-start.17 = (bf16[2048,128]{1,0:T(8,128)(2,1)}, bf16[2048,128]{1,0:T(8,128)(2,1)S(1)}, u32[]{:S(2)}, u32[]{:S(2)}) collective-permute-start(bf16[2048,128]{1,0:T(8,128)(2,1)} %slice.104), channel_id=1, source_target_pairs={{0,8},{4,12},{8,24},{12,28},{24,16},{28,20},{16,0},{20,4},{1,9},{5... | collective-permute-start | bytes 1572872 | tf_op jit(solution)/shard_map/ppermute | solution.py:38
  89.6 15.8 %collective-permute-start.18 = (bf16[2048,128]{1,0:T(8,128)(2,1)}, bf16[2048,128]{1,0:T(8,128)(2,1)}, u32[]{:S(2)}, u32[]{:S(2)}) collective-permute-start(bf16[2048,128]{1,0:T(8,128)(2,1)} %slice.105), channel_id=1, source_target_pairs={{0,16},{4,20},{8,0},{12,4},{24,8},{28,12},{16,24},{20,28},{1,17},{... | collective-permute-start | bytes 1572872 | tf_op jit(solution)/shard_map/ppermute | solution.py:38
  105.5 195.8 %reduce-scatter.7.cloned.1.call-start = ((), (), s32[]{:S(2)}) async-start(), calls=%async_computation.4 | async-start | bytes 2359296
  106.1 16.9 %collective-permute-start.14 = (bf16[1024,128]{1,0:T(8,128)(2,1)}, bf16[1024,128]{1,0:T(8,128)(2,1)S(1)}, u32[]{:S(2)}, u32[]{:S(2)}) collective-permute-start(bf16[1024,128]{1,0:T(8,128)(2,1)} %get-tuple-element.164), channel_id=1, source_target_pairs={{0,3},{1,0},{2,1},{3,2},{4,7},{5,4},{6,5},{7,6},{8,11},{9,8},{10,9... | collective-permute-start | bytes 786440 | tf_op jit(solution)/shard_map/ppermute | solution.py:87
  110.3 22.9 %collective-permute-start.15 = (bf16[1024,128]{1,0:T(8,128)(2,1)}, bf16[1024,128]{1,0:T(8,128)(2,1)S(1)}, u32[]{:S(2)}, u32[]{:S(2)}) collective-permute-start(bf16[1024,128]{1,0:T(8,128)(2,1)} %get-tuple-element.165), channel_id=1, source_target_pairs={{0,2},{1,3},{2,0},{3,1},{4,6},{5,7},{6,4},{7,5},{8,10},{9,11},{10,... | collective-permute-start | bytes 786440 | tf_op jit(solution)/shard_map/ppermute | solution.py:87
  110.3 22.9 %collective-permute-start.16 = (bf16[1024,128]{1,0:T(8,128)(2,1)}, bf16[1024,128]{1,0:T(8,128)(2,1)S(1)}, u32[]{:S(2)}, u32[]{:S(2)}) collective-permute-start(bf16[1024,128]{1,0:T(8,128)(2,1)} %get-tuple-element.166), channel_id=1, source_target_pairs={{0,1},{1,2},{2,3},{3,0},{4,5},{5,6},{6,7},{7,4},{8,9},{9,10},{10,1... | collective-permute-start | bytes 786440 | tf_op jit(solution)/shard_map/ppermute | solution.py:87
  133.2 15.5 %collective-permute-start.23 = (bf16[512,128]{1,0:T(8,128)(2,1)}, bf16[512,128]{1,0:T(8,128)(2,1)S(1)}, u32[]{:S(2)}, u32[]{:S(2)}) collective-permute-start(bf16[512,128]{1,0:T(8,128)(2,1)} %get-tuple-element.175), channel_id=1, source_target_pairs={{0,3},{1,0},{2,1},{3,2},{4,7},{5,4},{6,5},{7,6},{8,11},{9,8},{10,9... | collective-permute-start | bytes 393224 | tf_op jit(solution)/shard_map/ppermute | solution.py:87
  133.3 15.5 %collective-permute-start.24 = (bf16[512,128]{1,0:T(8,128)(2,1)}, bf16[512,128]{1,0:T(8,128)(2,1)S(1)}, u32[]{:S(2)}, u32[]{:S(2)}) collective-permute-start(bf16[512,128]{1,0:T(8,128)(2,1)} %get-tuple-element.176), channel_id=1, source_target_pairs={{0,2},{1,3},{2,0},{3,1},{4,6},{5,7},{6,4},{7,5},{8,10},{9,11},{10,... | collective-permute-start | bytes 393224 | tf_op jit(solution)/shard_map/ppermute | solution.py:87
  135.7 13.1 %collective-permute-start.25 = (bf16[512,128]{1,0:T(8,128)(2,1)}, bf16[512,128]{1,0:T(8,128)(2,1)S(1)}, u32[]{:S(2)}, u32[]{:S(2)}) collective-permute-start(bf16[512,128]{1,0:T(8,128)(2,1)} %get-tuple-element.177), channel_id=1, source_target_pairs={{0,1},{1,2},{2,3},{3,0},{4,5},{5,6},{6,7},{7,4},{8,9},{9,10},{10,1... | collective-permute-start | bytes 393224 | tf_op jit(solution)/shard_map/ppermute | solution.py:87
  150.7 11.2 %collective-permute-start.27 = (bf16[512,128]{1,0:T(8,128)(2,1)}, bf16[512,128]{1,0:T(8,128)(2,1)S(1)}, u32[]{:S(2)}, u32[]{:S(2)}) collective-permute-start(bf16[512,128]{1,0:T(8,128)(2,1)} %get-tuple-element.183), channel_id=1, source_target_pairs={{0,2},{1,3},{2,0},{3,1},{4,6},{5,7},{6,4},{7,5},{8,10},{9,11},{10,... | collective-permute-start | bytes 393224 | tf_op jit(solution)/shard_map/ppermute | solution.py:87
  150.7 11.2 %collective-permute-start.28 = (bf16[512,128]{1,0:T(8,128)(2,1)}, bf16[512,128]{1,0:T(8,128)(2,1)S(1)}, u32[]{:S(2)}, u32[]{:S(2)}) collective-permute-start(bf16[512,128]{1,0:T(8,128)(2,1)} %get-tuple-element.184), channel_id=1, source_target_pairs={{0,1},{1,2},{2,3},{3,0},{4,5},{5,6},{6,7},{7,4},{8,9},{9,10},{10,1... | collective-permute-start | bytes 393224 | tf_op jit(solution)/shard_map/ppermute | solution.py:87
  161.9 10.8 %collective-permute-start.29 = (bf16[512,128]{1,0:T(8,128)(2,1)}, bf16[512,128]{1,0:T(8,128)(2,1)S(1)}, u32[]{:S(2)}, u32[]{:S(2)}) collective-permute-start(bf16[512,128]{1,0:T(8,128)(2,1)} %get-tuple-element.202), channel_id=1, source_target_pairs={{0,3},{1,0},{2,1},{3,2},{4,7},{5,4},{6,5},{7,6},{8,11},{9,8},{10,9... | collective-permute-start | bytes 393224 | tf_op jit(solution)/shard_map/ppermute | solution.py:87
  162.7 12.3 %collective-permute-start.30 = (bf16[512,128]{1,0:T(8,128)(2,1)}, bf16[512,128]{1,0:T(8,128)(2,1)S(1)}, u32[]{:S(2)}, u32[]{:S(2)}) collective-permute-start(bf16[512,128]{1,0:T(8,128)(2,1)} %get-tuple-element.203), channel_id=1, source_target_pairs={{0,2},{1,3},{2,0},{3,1},{4,6},{5,7},{6,4},{7,5},{8,10},{9,11},{10,... | collective-permute-start | bytes 393224 | tf_op jit(solution)/shard_map/ppermute | solution.py:87
  163.5 11.4 %collective-permute-start.31 = (bf16[512,128]{1,0:T(8,128)(2,1)}, bf16[512,128]{1,0:T(8,128)(2,1)S(1)}, u32[]{:S(2)}, u32[]{:S(2)}) collective-permute-start(bf16[512,128]{1,0:T(8,128)(2,1)} %get-tuple-element.204), channel_id=1, source_target_pairs={{0,1},{1,2},{2,3},{3,0},{4,5},{5,6},{6,7},{7,4},{8,9},{9,10},{10,1... | collective-permute-start | bytes 393224 | tf_op jit(solution)/shard_map/ppermute | solution.py:87
  175.0 13.3 %collective-permute-start.33 = (bf16[512,128]{1,0:T(8,128)(2,1)}, bf16[512,128]{1,0:T(8,128)(2,1)S(1)}, u32[]{:S(2)}, u32[]{:S(2)}) collective-permute-start(bf16[512,128]{1,0:T(8,128)(2,1)} %get-tuple-element.239), channel_id=1, source_target_pairs={{0,2},{1,3},{2,0},{3,1},{4,6},{5,7},{6,4},{7,5},{8,10},{9,11},{10,... | collective-permute-start | bytes 393224 | tf_op jit(solution)/shard_map/ppermute | solution.py:87
  176.3 12.1 %collective-permute-start.34 = (bf16[512,128]{1,0:T(8,128)(2,1)}, bf16[512,128]{1,0:T(8,128)(2,1)S(1)}, u32[]{:S(2)}, u32[]{:S(2)}) collective-permute-start(bf16[512,128]{1,0:T(8,128)(2,1)} %get-tuple-element.240), channel_id=1, source_target_pairs={{0,1},{1,2},{2,3},{3,0},{4,5},{5,6},{6,7},{7,4},{8,9},{9,10},{10,1... | collective-permute-start | bytes 393224 | tf_op jit(solution)/shard_map/ppermute | solution.py:87
  188.4 21.1 %collective-permute-start.36 = (bf16[1024,128]{1,0:T(8,128)(2,1)S(1)}, bf16[1024,128]{1,0:T(8,128)(2,1)S(1)}, u32[]{:S(2)}, u32[]{:S(2)}) collective-permute-start(bf16[1024,128]{1,0:T(8,128)(2,1)S(1)} %copy-done.27), channel_id=1, source_target_pairs={{0,1},{1,2},{2,3},{3,0},{4,5},{5,6},{6,7},{7,4},{8,9},{9,10},{10,1... | collective-permute-start | bytes 786440 | tf_op jit(solution)/shard_map/ppermute | solution.py:87
  188.5 21.1 %collective-permute-start.35 = (bf16[1024,128]{1,0:T(8,128)(2,1)S(1)}, bf16[1024,128]{1,0:T(8,128)(2,1)S(1)}, u32[]{:S(2)}, u32[]{:S(2)}) collective-permute-start(bf16[1024,128]{1,0:T(8,128)(2,1)S(1)} %copy-done.29), channel_id=1, source_target_pairs={{0,3},{1,0},{2,1},{3,2},{4,7},{5,4},{6,5},{7,6},{8,11},{9,8},{10,9... | collective-permute-start | bytes 786440 | tf_op jit(solution)/shard_map/ppermute | solution.py:87
  212.5 16.2 %collective-permute-start.39 = (bf16[12288,128]{1,0:T(8,128)(2,1)}, bf16[12288,128]{1,0:T(8,128)(2,1)S(1)}, u32[]{:S(2)}, u32[]{:S(2)}) collective-permute-start(bf16[12288,128]{1,0:T(8,128)(2,1)} %get-tuple-element.263), channel_id=1, source_target_pairs={{0,4},{4,0},{8,12},{12,8},{16,20},{20,16},{24,28},{28,24},{1,5},{5... | collective-permute-start | bytes 9437192 | tf_op jit(solution)/shard_map/ppermute | solution.py:41
  214.1 14.3 %collective-permute-start.40 = (bf16[2048,128]{1,0:T(8,128)(2,1)S(1)}, bf16[2048,128]{1,0:T(8,128)(2,1)S(1)}, u32[]{:S(2)}, u32[]{:S(2)}) collective-permute-start(bf16[2048,128]{1,0:T(8,128)(2,1)S(1)} %get-tuple-element.310), channel_id=1, source_target_pairs={{0,8},{4,12},{8,24},{12,28},{24,16},{28,20},{16,0},{20,4},{1,9},{5... | collective-permute-start | bytes 1572872 | tf_op jit(solution)/shard_map/ppermute | solution.py:38
  214.8 13.9 %collective-permute-start.41 = (bf16[2048,128]{1,0:T(8,128)(2,1)S(1)}, bf16[2048,128]{1,0:T(8,128)(2,1)S(1)}, u32[]{:S(2)}, u32[]{:S(2)}) collective-permute-start(bf16[2048,128]{1,0:T(8,128)(2,1)S(1)} %get-tuple-element.309), channel_id=1, source_target_pairs={{0,16},{4,20},{8,0},{12,4},{24,8},{28,12},{16,24},{20,28},{1,17},{... | collective-permute-start | bytes 1572872 | tf_op jit(solution)/shard_map/ppermute | solution.py:38
  216.2 12.2 %collective-permute-start.37 = (bf16[1024,128]{1,0:T(8,128)(2,1)S(1)}, bf16[1024,128]{1,0:T(8,128)(2,1)S(1)}, u32[]{:S(2)}, u32[]{:S(2)}) collective-permute-start(bf16[1024,128]{1,0:T(8,128)(2,1)S(1)} %copy-done.28), channel_id=1, source_target_pairs={{0,2},{1,3},{2,0},{3,1},{4,6},{5,7},{6,4},{7,5},{8,10},{9,11},{10,... | collective-permute-start | bytes 786440 | tf_op jit(solution)/shard_map/ppermute | solution.py:87
  229.4 27.0 %collective-permute-start.43 = (bf16[4096,128]{1,0:T(8,128)(2,1)S(1)}, bf16[4096,128]{1,0:T(8,128)(2,1)}, u32[]{:S(2)}, u32[]{:S(2)}) collective-permute-start(bf16[4096,128]{1,0:T(8,128)(2,1)S(1)} %pad_maximum_fusion.2), channel_id=1, source_target_pairs={{0,16},{4,20},{8,0},{12,4},{24,8},{28,12},{16,24},{20,28},{1,17},{... | collective-permute-start | bytes 3145736 | tf_op jit(solution)/shard_map/ppermute | solution.py:38
  231.2 25.2 %collective-permute-start.42 = (bf16[4096,128]{1,0:T(8,128)(2,1)S(1)}, bf16[4096,128]{1,0:T(8,128)(2,1)}, u32[]{:S(2)}, u32[]{:S(2)}) collective-permute-start(bf16[4096,128]{1,0:T(8,128)(2,1)S(1)} %pad_maximum_fusion.1), channel_id=1, source_target_pairs={{0,8},{4,12},{8,24},{12,28},{24,16},{28,20},{16,0},{20,4},{1,9},{5... | collective-permute-start | bytes 3145736 | tf_op jit(solution)/shard_map/ppermute | solution.py:38
  232.0 21.0 %collective-permute-start.45 = (bf16[1024,256]{1,0:T(8,128)(2,1)S(1)}, bf16[1024,256]{1,0:T(8,128)(2,1)S(1)}, u32[]{:S(2)}, u32[]{:S(2)}) collective-permute-start(bf16[1024,256]{1,0:T(8,128)(2,1)S(1)} %copy-done.17), channel_id=1, source_target_pairs={{0,1},{1,2},{2,3},{3,0},{4,5},{5,6},{6,7},{7,4},{8,9},{9,10},{10,1... | collective-permute-start | bytes 1572872 | tf_op jit(solution)/shard_map/ppermute | solution.py:87
  232.1 24.2 %collective-permute-start.44 = (bf16[1024,256]{1,0:T(8,128)(2,1)S(1)}, bf16[1024,256]{1,0:T(8,128)(2,1)S(1)}, u32[]{:S(2)}, u32[]{:S(2)}) collective-permute-start(bf16[1024,256]{1,0:T(8,128)(2,1)S(1)} %copy-done.18), channel_id=1, source_target_pairs={{0,3},{1,0},{2,1},{3,2},{4,7},{5,4},{6,5},{7,6},{8,11},{9,8},{10,9... | collective-permute-start | bytes 1572872 | tf_op jit(solution)/shard_map/ppermute | solution.py:87
  261.1 62.2 %reduce-scatter.5.cloned.1.call-start = ((), (), s32[]{:S(2)}) async-start(), calls=%async_computation.3 | async-start | bytes 327680 | tf_op jit(solution)/shard_map/reduce_scatter | solution.py:526
  261.2 65.6 %collective-permute-start.47 = (bf16[12288,128]{1,0:T(8,128)(2,1)}, bf16[12288,128]{1,0:T(8,128)(2,1)}, u32[]{:S(2)}, u32[]{:S(2)}) collective-permute-start(bf16[12288,128]{1,0:T(8,128)(2,1)} %get-tuple-element.290), channel_id=1, source_target_pairs={{0,4},{4,0},{8,12},{12,8},{16,20},{20,16},{24,28},{28,24},{1,5},{5... | collective-permute-start | bytes 9437192 | tf_op jit(solution)/shard_map/ppermute | solution.py:41
  261.8 65.0 %collective-permute-start.50 = (bf16[1024,256]{1,0:T(8,128)(2,1)}, bf16[1024,256]{1,0:T(8,128)(2,1)}, u32[]{:S(2)}, u32[]{:S(2)}) collective-permute-start(bf16[1024,256]{1,0:T(8,128)(2,1)} %get-tuple-element.292), channel_id=1, source_target_pairs={{0,2},{1,3},{2,0},{3,1},{4,6},{5,7},{6,4},{7,5},{8,10},{9,11},{10,... | collective-permute-start | bytes 1572872 | tf_op jit(solution)/shard_map/ppermute | solution.py:87
  305.9 20.8 %collective-permute-start.48 = (bf16[2048,128]{1,0:T(8,128)(2,1)}, bf16[2048,128]{1,0:T(8,128)(2,1)}, u32[]{:S(2)}, u32[]{:S(2)}) collective-permute-start(bf16[2048,128]{1,0:T(8,128)(2,1)} %get-tuple-element.308), channel_id=1, source_target_pairs={{0,8},{4,12},{8,24},{12,28},{24,16},{28,20},{16,0},{20,4},{1,9},{5... | collective-permute-start | bytes 1572872 | tf_op jit(solution)/shard_map/ppermute | solution.py:38
  307.4 19.4 %collective-permute-start.49 = (bf16[2048,128]{1,0:T(8,128)(2,1)}, bf16[2048,128]{1,0:T(8,128)(2,1)}, u32[]{:S(2)}, u32[]{:S(2)}) collective-permute-start(bf16[2048,128]{1,0:T(8,128)(2,1)} %get-tuple-element.307), channel_id=1, source_target_pairs={{0,16},{4,20},{8,0},{12,4},{24,8},{28,12},{16,24},{20,28},{1,17},{... | collective-permute-start | bytes 1572872 | tf_op jit(solution)/shard_map/ppermute | solution.py:38
  330.7 23.3 %collective-permute-start.51 = (bf16[4096,128]{1,0:T(8,128)(2,1)S(1)}, bf16[4096,128]{1,0:T(8,128)(2,1)S(1)}, u32[]{:S(2)}, u32[]{:S(2)}) collective-permute-start(bf16[4096,128]{1,0:T(8,128)(2,1)S(1)} %pad_maximum_fusion.3), channel_id=1, source_target_pairs={{0,8},{4,12},{8,24},{12,28},{24,16},{28,20},{16,0},{20,4},{1,9},{5... | collective-permute-start | bytes 3145736 | tf_op jit(solution)/shard_map/ppermute | solution.py:38
  333.6 23.0 %collective-permute-start.52 = (bf16[4096,128]{1,0:T(8,128)(2,1)S(1)}, bf16[4096,128]{1,0:T(8,128)(2,1)S(1)}, u32[]{:S(2)}, u32[]{:S(2)}) collective-permute-start(bf16[4096,128]{1,0:T(8,128)(2,1)S(1)} %pad_maximum_fusion.4), channel_id=1, source_target_pairs={{0,16},{4,20},{8,0},{12,4},{24,8},{28,12},{16,24},{20,28},{1,17},{... | collective-permute-start | bytes 3145736 | tf_op jit(solution)/shard_map/ppermute | solution.py:38
  (55 other events, 586.7 us)
Sparse Core Ops, SparseCore 0:
  105.6 27.8 all-gather.1
  261.3 39.9 reduce-scatter.6
  303.7 19.6 reduce-scatter.4

commit v5 on v4

--- a/solution.py
+++ b/solution.py
@@ -422,19 +422,23 @@
         w.go(**{f"far_up{c}": ring.hop(up[:half], 1), f"far_down{c}": ring.hop(down[half:], -1)})
         if c == 0:
             w.go(cot_ends=cot_ends, own_other=own_other, metas=(spmm_meta, spmm_t_meta, dense_meta))
-        else:
-            mixed[c - 1] = w[f"mixed{c - 1}"]
+        seen = []
         if c == last:
             for step in range(1, middle):
                 for i in (2 * step - 1, 2 * step):
                     got_other[c, i] = ring.sibling(got_own[c, i])
                     w.go(**{f"other{c}_{i}": got_other[c, i]})
+                    seen.append(got_other[c, i])
+        if c:
+            mixed[c - 1] = w[f"mixed{c - 1}"]
+            ready = [lax.optimization_barrier((b, *seen))[0] for b in mixed[c - 1]]
+            w.go(**{f"mixed_ends{c - 1}": send(ready, ends)})
         w.close()
         if c == 0:
             spmm_meta, spmm_t_meta, dense_meta = w["metas"]
             w.go(cot_inner=send([w.gate(b) for b in cot_blocks], inner))
         else:
-            w.go(**{f"mixed_got{c - 1}": send(mixed[c - 1], ends + inner)})
+            w.go(**{f"mixed_inner{c - 1}": send([w.gate(b) for b in mixed[c - 1]], inner)})
         got_own[c, len(offsets) - 2], got_own[c, len(offsets) - 1] = w[f"far_up{c}"], w[f"far_down{c}"]
         if c < last:
             up = down = w.gate(xs[c + 1])
@@ -448,7 +452,7 @@
         w.go(**{f"half_got{h}": send(w[f"half{h}"], ends + inner)})
 
     cot = ordered(cot_blocks[0], w["cot_ends"], w["cot_inner"])
-    whole = [ordered(mixed[c][0], w[f"mixed_got{c}"]) for c in range(last)]
+    whole = [ordered(mixed[c][0], w[f"mixed_ends{c}"], w[f"mixed_inner{c}"]) for c in range(last)]
     earlier = ()
     for h in range(halves):
         part = ordered(w[f"half{h}"][0], w[f"half_got{h}"])
@@ -462,46 +466,48 @@
         w.close()
         w.go(**{f"back_got{h}": send(w[f"back{h}"], ends + inner)})
     act, back, mixed_rows, grad_rows = w["whole"]
-    sums = lax.dot_general(mixed_rows, grad_rows, (((0,), (0,)), ((), ())), preferred_element_type=F32)
-    w.go(sums=sums.astype(BF16))
+    by_row = grad_rows.reshape(part_rows, row_size, -1)
+    sums = jnp.einsum("nf,nrh->rfh", mixed_rows, by_row, preferred_element_type=F32).astype(BF16)
+    w.go(sums=sums)
     w.close()
-    weight_terms = lax.psum_scatter(w["sums"], "row", scatter_dimension=1, tiled=True)
-
-    feature_grad = []
+    weight_terms = lax.psum_scatter(w["sums"], "row", scatter_dimension=0, tiled=True)[0]
+
+    def run_spmm_t(c, grads):
+        return spmm_t(tiles, columns, counts, spmm_t_meta, grads, parts, held, rows, rows * row_size)
+
+    parts_got = [ordered(w[f"back{h}"][0], w[f"back_got{h}"]) for h in range(halves)]
+    w.go(terms0=run_spmm_t(0, [parts_got[h][u] for u in range(parts) for h in range(halves)]))
+    for c in range(1, chunks):
+        w.go(**{f"rest_got{c}": send([w.gate(b[c]) for b in back], ends + inner)})
+    w.close()
+
+    near_sums = []
     for c in range(chunks):
-        if c:
-            grads = [w.gate(g) for g in ordered(back[0][c], w[f"rest_ends{c}"], w[f"rest_inner{c}"])]
-        else:
-            parts_got = [ordered(w[f"back{h}"][0], w[f"back_got{h}"]) for h in range(halves)]
-            grads = [parts_got[h][u] for u in range(parts) for h in range(halves)]
-        w.go(**{f"terms{c}": spmm_t(tiles, columns, counts, spmm_t_meta, grads, parts, held, rows, rows * row_size)})
-        if c < last:
-            rest = [w.gate(b[c + 1]) for b in back]
-            w.go(**{f"rest_ends{c + 1}": send(rest, ends)})
-        w.close()
-        if c < last:
-            w.go(**{f"rest_inner{c + 1}": send(rest, inner)})
         terms = w[f"terms{c}"]
         own_far, own_near, other_far, other_near = terms[0], terms[1:-2], terms[-2], terms[-1]
         got_far = ring.sibling(other_far)
-        other_near = lax.optimization_barrier((other_near, got_far))[0]
-        w.go(**{f"got_near{c}": ring.sibling(other_near)})
-
-        def far(start):
-            return own_far[start : start + half].astype(F32) + got_far[start : start + half].astype(F32)
-
-        up = ring.hop(far(0).astype(BF16), 1)
-        down = ring.hop(far(half).astype(BF16), -1)
-        w.go(**{f"sum{c}_{middle}": (up, down)})
-        if c == last:
-            w.go(act_inner=send(act, inner))
+        got_near = ring.sibling(lax.optimization_barrier((other_near, got_far))[0])
+        far = [
+            (own_far[at : at + half].astype(F32) + got_far[at : at + half].astype(F32)).astype(BF16)
+            for at in (0, half)
+        ]
+        w.go(**{f"got_near{c}": got_near, f"sum{c}_{middle}": (ring.hop(far[0], 1), ring.hop(far[1], -1))})
+        if c < last:
+            grads = ordered(back[0][c + 1], w[f"rest_got{c + 1}"])
+            grads = lax.optimization_barrier((grads, far[0][:8], far[1][:8]))[0]
+            w.go(**{f"terms{c + 1}": run_spmm_t(c + 1, grads)})
+        if c == 0:
+            w.go(weight_terms=weight_terms)
         w.close()
-        got_near = w[f"got_near{c}"]
-
-        def near_sum(offset):
+        if c == 0:
+            weight_terms = lax.psum_scatter(w["weight_terms"], "rep", scatter_dimension=0, tiled=True)
+            w.go(act_ends=send([w.gate(a) for a in act], ends))
+
+        def near_sum(offset, got=w[f"got_near{c}"], own=own_near):
             at = near.index(offset % ring.chips)
-            return own_near[at].astype(F32) + got_near[at * rows : (at + 1) * rows].astype(F32)
-
+            return own[at].astype(F32) + got[at * rows : (at + 1) * rows].astype(F32)
+
+        near_sums.append(near_sum)
         for step in range(middle - 1, 0, -1):
             up, down = w[f"sum{c}_{step + 1}"]
             to_up, to_down = near_sum(step), near_sum(-step)
@@ -512,19 +518,19 @@
                 to_up, to_down = to_up + up.astype(F32), to_down + down.astype(F32)
             to_up, to_down = to_up.astype(BF16), to_down.astype(BF16)
             w.go(**{f"sum{c}_{step}": (ring.hop(to_up, 1), ring.hop(to_down, -1))})
-            if c == 0 and step == middle - 1:
-                w.go(act_ends=send([w.gate(a) for a in act], ends))
             if step > 1:
                 w.close()
             else:
                 w.token = to_up[:8]
-        up, down = (w.pending if f"sum{c}_1" in w.pending else w.done)[f"sum{c}_1"]
+    got = {**w.done, **w.pending, "act_inner": send([w.gate(a) for a in act], inner)}
+    feature_grad = []
+    for c, near_sum in enumerate(near_sums):
+        up, down = got[f"sum{c}_1"]
         if middle == 1:
             feature_grad.append((near_sum(0) + jnp.concatenate([up, down]).astype(F32)).astype(BF16))
         else:
             feature_grad.append((near_sum(0) + up.astype(F32) + down.astype(F32)).astype(BF16))
-    weight_grad = lax.psum_scatter(w.gate(weight_terms), "rep", scatter_dimension=0, tiled=True).astype(F32)
-    got = {**w.pending, **w.done}
+    weight_grad = w.gate(weight_terms).astype(F32)
     act = ordered(act[0], got["act_ends"], got["act_inner"])
     feature_grad = jnp.concatenate(feature_grad, axis=1)
     activations = jnp.zeros((rows, h_wide), BF16)

time: 368 us -> 362 us (0.984)
  waiting for transfers between devices: 132 us -> 113 us
  blocking collectives: 14.6 us -> 21.6 us
  other arithmetic: 17.1 us -> 21.2 us
    unnamed x4 -> x3, waiting for transfers between devices: 37.2 us -> 0.05 us
    ppermute x24, waiting for transfers between devices: 41.1 us -> 54.5 us  [send(): lax.ppermute(blocks[s], 'rep', [(i, (i + s) % size) for i in range(size)])]
    reduce_scatter x1 -> x2, waiting for transfers between devices: 13.1 us -> 22.1 us  [the longest x1 22.1 us: local(): lax.psum_scatter(w['sums'], 'row', scatter_dimension=0, tiled=True)[0]]
    ppermute x16, waiting for transfers between devices: 37.4 us -> 29.1 us  [hop(): return lax.ppermute(value, 'row', self.perm(step))]
    all_gather x1, blocking collectives: 14.6 us -> 21.6 us  [local(): w_share = lax.all_gather(w_share, 'rep', axis=1, tiled=True)]
    ppermute x13, waiting for transfers between devices: 2.89 us -> 7.51 us  [sibling(): return lax.ppermute(value, 'row', [(d, d ^ 1) for d in range(self.devices)])]
    reshape x0 -> x1, local copies, waits for them, and re-layouts: none -> 4.09 us  [local(): by_row = grad_rows.reshape(part_rows, row_size, -1)]
    unnamed x97 -> x106, local copies, waits for them, and re-layouts: 10.4 us -> 10.2 us
  transfers between devices with their start and end apart: 56 -> 56, of which waited for: 17 -> 18; matrix products, arithmetic and copies ran while one was open for 12% -> 13% of each run, Pallas kernels for 23% -> 24%
where the time goes in v5:
time: 362 us; the launch traced here: 360 us
  waiting for transfers between devices  113 us (31%)
  Pallas kernels  85.7 us (24%)
  starting transfers between devices  54.9 us (15%)
  local copies, waits for them, and re-layouts  35.9 us (10%)
  between operations  22.3 us (6%)
  blocking collectives  21.6 us (6%)
  other arithmetic  21.2 us (6%)
  matrix products  5.31 us (1%)
    ppermute x24, waiting for transfers between devices, send(): lax.ppermute(blocks[s], 'rep', [(i, (i + s) % size) for i in range(size)])  54.5 us
    pallas_call x3, Pallas kernels, spmm(): pl.pallas_call(functools.partial(spmm_kernel, len(pieces), per_part, skip...  36.5 us
    pallas_call x2, Pallas kernels, spmm_t(): pl.pallas_call(functools.partial(spmm_t_kernel, len(grads), per_part, len...  34.9 us
    ppermute x24, starting transfers between devices, send(): lax.ppermute(blocks[s], 'rep', [(i, (i + s) % size) for i in range(size)])  33.6 us
    ppermute x16, waiting for transfers between devices, hop(): return lax.ppermute(value, 'row', self.perm(step))  29.1 us
    reduce_scatter x1, waiting for transfers between devices, local(): lax.psum_scatter(w['sums'], 'row', scatter_dimension=0, tiled=True)[0]  22.1 us
    all_gather x1, blocking collectives, local(): w_share = lax.all_gather(w_share, 'rep', axis=1, tiled=True)  21.6 us
    ppermute x16, starting transfers between devices, hop(): return lax.ppermute(value, 'row', self.perm(step))  18.8 us
  transfers between devices with their start and end apart: 56, of which 18 were waited for; matrix products, arithmetic and copies ran while one was open for 13% of the time, Pallas kernels for 24%

profile of v5, /device:TPU:0, one launch (start us, length us, event | category | flops | bytes accessed | tf_op | source)
XLA Modules:
  0.0 360.2 jit_solution(4592257573984340143)
XLA Ops:
  7.7 1.7 fusion.9
  9.4 2.6 collective-permute-start
  12.1 2.6 constant_dynamic-slice_fusion
  14.8 4.1 %collective-permute-start.4 = (bf16[1024,256]{1,0:T(8,128)(2,1)S(1)}, bf16[1024,256]{1,0:T(8,128)(2,1)}, u32[]{:S(2)}, u32[]{:S(2)}) collective-permute-start(bf16[1024,256]{1,0:T(8,128)(2,1)S(1)} %get-tuple-element.329), channel_id=1, source_target_pairs={{0,3},{1,0},{2,1},{3,2},{4,7},{5,4},{6,5},{7,6},{8,11},{9,8},{10,9... | collective-permute-start | bytes 1572872 | tf_op jit(solution)/shard_map/ppermute | solution.py:87
  18.9 17.1 %collective-permute-done.refs_1_ = bf16[4096,128]{1,0:T(8,128)(2,1)} collective-permute-done((bf16[4096,128]{1,0:T(8,128)(2,1)S(1)}, bf16[4096,128]{1,0:T(8,128)(2,1)}, u32[]{:S(2)}, u32[]{:S(2)}) %collective-permute-start) | collective-permute-done | bytes 1048608 | tf_op jit(solution)/shard_map/ppermute | solution.py:38
  37.9 1.9 slice.101
  40.9 1.6 collective-permute-start.2
  58.9 2.7 collective-permute-start.7
  61.5 3.0 fusion.8
  65.5 14.4 %spmm.3 = (bf16[1024,128]{1,0:T(8,128)(2,1)}, bf16[1024,128]{1,0:T(8,128)(2,1)}, bf16[1024,128]{1,0:T(8,128)(2,1)}, bf16[1024,128]{1,0:T(8,128)(2,1)}) custom-call(s32[32,16]{1,0:T(8,128)} %copy.55.cols, s32[32]{0:T(128)} %counts.9, s32[11]{0:T(128)} %stack.75.meta, bf16[32,16,128,128]{3,2,1,0:T(8,128)(2,1)} %tiles.9, bf16[4096,128]{1,0:T(8,128)(2,1)} %copy-done.7, ...), custom_call_target="tpu_custom_call" | custom-call | flops 2147483648 | bytes 25165824 | tf_op jit(solution)/shard_map/spmm/pallas_call | solution.py:158
  79.9 5.6 %collective-permute-done.7.refs_10_ = bf16[1024,256]{1,0:T(8,128)(2,1)S(1)} collective-permute-done((bf16[1024,256]{1,0:T(8,128)(2,1)}, bf16[1024,256]{1,0:T(8,128)(2,1)S(1)}, u32[]{:S(2)}, u32[]{:S(2)}) %collective-permute-start.7) | collective-permute-done | bytes 524320 | tf_op jit(solution)/shard_map/ppermute | solution.py:87
  92.7 3.0 collective-permute-start.18
  95.8 21.6 %all_gather.6 = bf16[128,1024]{1,0:T(8,128)(2,1)} all-gather(bf16[128,256]{1,0:T(8,128)(2,1)S(1)} %constant_dynamic-slice_fusion.1), channel_id=1, replica_groups=mesh['row'=8,'rep'=4] {'rep'}, dimensions={1}, use_global_device_ids=true | all-gather | bytes 327680 | tf_op jit(solution)/shard_map/all_gather | solution.py:393
  121.3 11.0 %spmm.4 = (bf16[512,128]{1,0:T(8,128)(2,1)}, bf16[512,128]{1,0:T(8,128)(2,1)}, bf16[512,128]{1,0:T(8,128)(2,1)}, bf16[512,128]{1,0:T(8,128)(2,1)}) custom-call(s32[32,16]{1,0:T(8,128)} %copy.55.cols, s32[32]{0:T(128)} %counts.9, s32[11]{0:T(128)} %stack.75.meta, bf16[32,16,128,128]{3,2,1,0:T(8,128)(2,1)} %tiles.9, bf16[4096,128]{1,0:T(8,128)(2,1)} %copy-done.2, ...), custom_call_target="tpu_custom_call" | custom-call | flops 1073741824 | bytes 16777216 | tf_op jit(solution)/shard_map/spmm/pallas_call | solution.py:158
  132.5 2.2 collective-permute-start.23
  135.3 11.1 %spmm.5 = (bf16[512,128]{1,0:T(8,128)(2,1)}, bf16[512,128]{1,0:T(8,128)(2,1)}, bf16[512,128]{1,0:T(8,128)(2,1)}, bf16[512,128]{1,0:T(8,128)(2,1)}) custom-call(s32[32,16]{1,0:T(8,128)} %copy.55.cols, s32[32]{0:T(128)} %counts.9, s32[11]{0:T(128)} %stack.75.meta, bf16[32,16,128,128]{3,2,1,0:T(8,128)(2,1)} %tiles.9, bf16[4096,128]{1,0:T(8,128)(2,1)} %copy-done.2, ...), custom_call_target="tpu_custom_call" | custom-call | flops 1073741824 | bytes 16777216 | tf_op jit(solution)/shard_map/spmm/pallas_call | solution.py:158
  146.4 3.2 collective-permute-start.26
  150.9 7.1 %dense.2 = (bf16[1024,256]{1,0:T(8,128)(2,1)}, bf16[1024,256]{1,0:T(8,128)(2,1)}, bf16[1024,256]{1,0:T(8,128)(2,1)}, bf16[1024,256]{1,0:T(8,128)(2,1)}, bf16[512...) custom-call(s32[1]{0:T(128)} %bitcast.meta, ...), custom_call_target="tpu_custom_call" | custom-call | flops 2147483648 | bytes 8388608 | tf_op jit(solution)/shard_map/dense/pallas_call | solution.py:327
  158.0 4.0 %collective-permute-done.27.refs_5_ = bf16[512,128]{1,0:T(8,128)(2,1)S(1)} collective-permute-done((bf16[512,128]{1,0:T(8,128)(2,1)}, bf16[512,128]{1,0:T(8,128)(2,1)S(1)}, u32[]{:S(2)}, u32[]{:S(2)}) %collective-permute-start.27) | collective-permute-done | bytes 131104 | tf_op jit(solution)/shard_map/ppermute | solution.py:87
  163.5 2.0 collective-permute-start.31
  165.5 7.2 %dense.3 = (bf16[1024,256]{1,0:T(8,128)(2,1)}, bf16[1024,256]{1,0:T(8,128)(2,1)}, bf16[1024,256]{1,0:T(8,128)(2,1)}, bf16[1024,256]{1,0:T(8,128)(2,1)}, bf16[512...) custom-call(s32[1]{0:T(128)} %bitcast.meta, ...), custom_call_target="tpu_custom_call", output_to_operand_aliasing={{0}: (14, {}), {1}: (15, {}), {2}: (16, {}), {3}: (17, {}),... | custom-call | flops 2147483648 | bytes 8388608 | tf_op jit(solution)/shard_map/dense/pallas_call | solution.py:327
  172.7 2.4 collective-permute-done.30.refs_4_
  175.8 4.1 %copy.62 = bf16[1024,1024]{0,1:T(8,128)(2,1)} copy(bf16[1024,1024]{1,0:T(8,128)(2,1)} %get-tuple-element.252) | data formatting | bytes 4194304 | tf_op jit(solution)/shard_map/reshape | solution.py:469
  181.2 2.0 collective-permute-start.34
  183.1 5.3 %convert_bitcast_fusion = bf16[8,1024,128]{1,2,0:T(8,128)(2,1)} fusion(bf16[1024,8,128]{0,2,1:T(8,128)(2,1)} %bitcast.33, bf16[1024,1024]{1,0:T(8,128)(2,1)S(1)} %copy-done.9), kind=kOutput, calls=%fused_computation.9 | convolution fusion | flops 2148532224 | bytes 6291456 | tf_op jit(solution)/shard_map/nf,nrh->rfh/dot_general | solution.py:470
  188.5 4.9 %collective-permute-done.33.refs_5_ = bf16[512,128]{1,0:T(8,128)(2,1)S(1)} collective-permute-done((bf16[512,128]{1,0:T(8,128)(2,1)S(1)}, bf16[512,128]{1,0:T(8,128)(2,1)S(1)}, u32[]{:S(2)}, u32[]{:S(2)}) %collective-permute-start.33) | collective-permute-done | bytes 131104 | tf_op jit(solution)/shard_map/ppermute | solution.py:87
  195.2 2.9 collective-permute-start.35
  198.0 17.1 %spmm_t.2 = (bf16[4096,128]{1,0:T(8,128)(2,1)}, bf16[4096,128]{1,0:T(8,128)(2,1)}, bf16[4096,128]{1,0:T(8,128)(2,1)}, bf16[4096,128]{1,0:T(8,128)(2,1)}, bf16[40...) custom-call(s32[32,16]{1,0:T(8,128)} %copy.55.cols, s32[32]{0:T(128)} %counts.9, s32[9]{0:T(128)} %stack.84.meta, ...), custom_call_target="tpu_custom_call" | custom-call | flops 2147483648 | bytes 25165824 | tf_op jit(solution)/shard_map/spmm_t/pallas_call | solution.py:241
  216.1 2.9 collective-permute-done.38
  219.2 1.8 add_convert_fusion.4
  223.1 17.7 %spmm_t.3 = (bf16[4096,128]{1,0:T(8,128)(2,1)}, bf16[4096,128]{1,0:T(8,128)(2,1)}, bf16[4096,128]{1,0:T(8,128)(2,1)}, bf16[4096,128]{1,0:T(8,128)(2,1)}, bf16[40...) custom-call(s32[32,16]{1,0:T(8,128)} %copy.55.cols, s32[32]{0:T(128)} %counts.9, s32[9]{0:T(128)} %stack.84.meta, ...), custom_call_target="tpu_custom_call" | custom-call | flops 2147483648 | bytes 25165824 | tf_op jit(solution)/shard_map/spmm_t/pallas_call | solution.py:241
  240.8 22.1 %reduce-scatter.3.cloned.1.call-done = bf16[1,1024,128]{1,2,0:T(8,128)(2,1)} async-done(((bf16[8,1024,128]{1,2,0:T(8,128)(2,1)}), bf16[1,1024,128]{1,2,0:T(8,128)(2,1)}) %reduce-scatter.3.cloned.1.call-update) | async-done | bytes 262160 | tf_op jit(solution)/shard_map/reduce_scatter | solution.py:473
  262.9 2.9 collective-permute-done.46
  265.9 1.9 convert_add_fusion.2
  276.1 2.3 collective-permute-start.42
  279.7 11.6 %collective-permute-done.43 = bf16[1024,256]{1,0:T(8,128)(2,1)S(1)} collective-permute-done((bf16[1024,256]{1,0:T(8,128)(2,1)S(1)}, bf16[1024,256]{1,0:T(8,128)(2,1)S(1)}, u32[]{:S(2)}, u32[]{:S(2)}) %collective-permute-start.43) | collective-permute-done | bytes 524320 | tf_op jit(solution)/shard_map/ppermute | solution.py:87
  292.7 8.0 %collective-permute-done.42 = bf16[1024,256]{1,0:T(8,128)(2,1)S(1)} collective-permute-done((bf16[1024,256]{1,0:T(8,128)(2,1)S(1)}, bf16[1024,256]{1,0:T(8,128)(2,1)S(1)}, u32[]{:S(2)}, u32[]{:S(2)}) %collective-permute-start.42) | collective-permute-done | bytes 524320 | tf_op jit(solution)/shard_map/ppermute | solution.py:87
  305.2 5.4 %collective-permute-done.48 = bf16[2048,128]{1,0:T(8,128)(2,1)} collective-permute-done((bf16[2048,128]{1,0:T(8,128)(2,1)}, bf16[2048,128]{1,0:T(8,128)(2,1)}, u32[]{:S(2)}, u32[]{:S(2)}) %collective-permute-start.48) | collective-permute-done | bytes 524320 | tf_op jit(solution)/shard_map/ppermute | solution.py:38
  310.7 4.2 %collective-permute-done.49 = bf16[2048,128]{1,0:T(8,128)(2,1)S(1)} collective-permute-done((bf16[2048,128]{1,0:T(8,128)(2,1)}, bf16[2048,128]{1,0:T(8,128)(2,1)S(1)}, u32[]{:S(2)}, u32[]{:S(2)}) %collective-permute-start.49) | collective-permute-done | bytes 524320 | tf_op jit(solution)/shard_map/ppermute | solution.py:38
  314.9 2.6 convert_add_fusion
  319.8 1.5 collective-permute-start.51
  323.8 1.8 add_convert_fusion.1
  325.6 1.7 copy.61
  327.3 1.9 constant_dynamic-update-slice_fusion.1
  329.2 17.8 %collective-permute-done.50 = bf16[1024,256]{1,0:T(8,128)(2,1)} collective-permute-done((bf16[1024,256]{1,0:T(8,128)(2,1)S(1)}, bf16[1024,256]{1,0:T(8,128)(2,1)}, u32[]{:S(2)}, u32[]{:S(2)}) %collective-permute-start.50) | collective-permute-done | bytes 524320 | tf_op jit(solution)/shard_map/ppermute | solution.py:87
  347.0 1.9 constant_dynamic-update-slice_fusion.2
  349.7 2.5 add_convert_fusion
  352.1 1.5 pad_maximum_fusion
  (219 shorter events, 55.5 us)
Async XLA Ops:
  7.2 143.7 %all-gather.2.cloned.1.call-start = ((), (), s32[]{:S(2)}) async-start(), calls=%async_computation.2 | async-start | bytes 2359296 | tf_op jit(solution)/shard_map/all_gather | solution.py:445
  7.2 48.8 %collective-permute-start.6 = (bf16[4096,256]{1,0:T(8,128)(2,1)}, bf16[4096,256]{1,0:T(8,128)(2,1)}, u32[]{:S(2)}, u32[]{:S(2)}) collective-permute-start(bf16[4096,256]{1,0:T(8,128)(2,1)} %param.42), channel_id=1, source_target_pairs={{0,4},{4,0},{8,12},{12,8},{16,20},{20,16},{24,28},{28,24},{1,5},{5... | collective-permute-start | bytes 6291464 | tf_op jit(solution)/shard_map/ppermute | solution.py:41
  9.4 26.5 %collective-permute-start = (bf16[4096,128]{1,0:T(8,128)(2,1)S(1)}, bf16[4096,128]{1,0:T(8,128)(2,1)}, u32[]{:S(2)}, u32[]{:S(2)}) collective-permute-start(bf16[4096,128]{1,0:T(8,128)(2,1)S(1)} %get-tuple-element.335.refs_0_), channel_id=1, source_target_pairs={{0,8},{4,12},{8,24},{12,28},{24,16},{28,20},{16,0},{20,4},{1,9},{5... | collective-permute-start | bytes 3145736 | tf_op jit(solution)/shard_map/ppermute | solution.py:38
  12.0 25.4 %collective-permute-start.1 = (bf16[4096,128]{1,0:T(8,128)(2,1)S(1)}, bf16[4096,128]{1,0:T(8,128)(2,1)}, u32[]{:S(2)}, u32[]{:S(2)}) collective-permute-start(bf16[4096,128]{1,0:T(8,128)(2,1)S(1)} %get-tuple-element.335.refs_0_), channel_id=1, source_target_pairs={{0,16},{4,20},{8,0},{12,4},{24,8},{28,12},{16,24},{20,28},{1,17},{... | collective-permute-start | bytes 3145736 | tf_op jit(solution)/shard_map/ppermute | solution.py:38
  14.8 26.1 %collective-permute-start.4 = (bf16[1024,256]{1,0:T(8,128)(2,1)S(1)}, bf16[1024,256]{1,0:T(8,128)(2,1)}, u32[]{:S(2)}, u32[]{:S(2)}) collective-permute-start(bf16[1024,256]{1,0:T(8,128)(2,1)S(1)} %get-tuple-element.329), channel_id=1, source_target_pairs={{0,3},{1,0},{2,1},{3,2},{4,7},{5,4},{6,5},{7,6},{8,11},{9,8},{10,9... | collective-permute-start | bytes 1572872 | tf_op jit(solution)/shard_map/ppermute | solution.py:87
  18.9 23.6 %collective-permute-start.5 = (bf16[1024,256]{1,0:T(8,128)(2,1)S(1)}, bf16[1024,256]{1,0:T(8,128)(2,1)}, u32[]{:S(2)}, u32[]{:S(2)}) collective-permute-start(bf16[1024,256]{1,0:T(8,128)(2,1)S(1)} %get-tuple-element.331), channel_id=1, source_target_pairs={{0,1},{1,2},{2,3},{3,0},{4,5},{5,6},{6,7},{7,4},{8,9},{9,10},{10,1... | collective-permute-start | bytes 1572872 | tf_op jit(solution)/shard_map/ppermute | solution.py:87
  37.4 21.5 %collective-permute-start.10 = (bf16[4096,128]{1,0:T(8,128)(2,1)}, bf16[4096,128]{1,0:T(8,128)(2,1)}, u32[]{:S(2)}, u32[]{:S(2)}) collective-permute-start(bf16[4096,128]{1,0:T(8,128)(2,1)} %collective-permute-done.refs_1_), channel_id=1, source_target_pairs={{0,4},{4,0},{8,12},{12,8},{16,20},{20,16},{24,28},{28,24},{1,5},{5... | collective-permute-start | bytes 3145736 | tf_op jit(solution)/shard_map/ppermute | solution.py:41
  37.4 21.5 %collective-permute-start.11 = (bf16[4096,128]{1,0:T(8,128)(2,1)}, bf16[4096,128]{1,0:T(8,128)(2,1)}, u32[]{:S(2)}, u32[]{:S(2)}) collective-permute-start(bf16[4096,128]{1,0:T(8,128)(2,1)} %collective-permute-done.1.refs_2_), channel_id=1, source_target_pairs={{0,4},{4,0},{8,12},{12,8},{16,20},{20,16},{24,28},{28,24},{1,5},{5... | collective-permute-start | bytes 3145736 | tf_op jit(solution)/shard_map/ppermute | solution.py:41
  40.9 14.2 %collective-permute-start.2 = (bf16[2048,128]{1,0:T(8,128)(2,1)}, bf16[2048,128]{1,0:T(8,128)(2,1)S(1)}, u32[]{:S(2)}, u32[]{:S(2)}) collective-permute-start(bf16[2048,128]{1,0:T(8,128)(2,1)} %slice.101), channel_id=1, source_target_pairs={{0,8},{4,12},{8,24},{12,28},{24,16},{28,20},{16,0},{20,4},{1,9},{5... | collective-permute-start | bytes 1572872 | tf_op jit(solution)/shard_map/ppermute | solution.py:38
  42.4 13.6 %collective-permute-start.3 = (bf16[2048,128]{1,0:T(8,128)(2,1)S(1)}, bf16[2048,128]{1,0:T(8,128)(2,1)S(1)}, u32[]{:S(2)}, u32[]{:S(2)}) collective-permute-start(bf16[2048,128]{1,0:T(8,128)(2,1)S(1)} %slice.102), channel_id=1, source_target_pairs={{0,16},{4,20},{8,0},{12,4},{24,8},{28,12},{16,24},{20,28},{1,17},{... | collective-permute-start | bytes 1572872 | tf_op jit(solution)/shard_map/ppermute | solution.py:38
  56.8 28.7 %collective-permute-start.8 = (bf16[4096,128]{1,0:T(8,128)(2,1)S(1)}, bf16[4096,128]{1,0:T(8,128)(2,1)S(1)}, u32[]{:S(2)}, u32[]{:S(2)}) collective-permute-start(bf16[4096,128]{1,0:T(8,128)(2,1)S(1)} %get-tuple-element.164.refs_0_), channel_id=1, source_target_pairs={{0,8},{4,12},{8,24},{12,28},{24,16},{28,20},{16,0},{20,4},{1,9},{5... | collective-permute-start | bytes 3145736 | tf_op jit(solution)/shard_map/ppermute | solution.py:38
  57.6 28.0 %collective-permute-start.9 = (bf16[4096,128]{1,0:T(8,128)(2,1)S(1)}, bf16[4096,128]{1,0:T(8,128)(2,1)S(1)}, u32[]{:S(2)}, u32[]{:S(2)}) collective-permute-start(bf16[4096,128]{1,0:T(8,128)(2,1)S(1)} %get-tuple-element.164.refs_0_), channel_id=1, source_target_pairs={{0,16},{4,20},{8,0},{12,4},{24,8},{28,12},{16,24},{20,28},{1,17},{... | collective-permute-start | bytes 3145736 | tf_op jit(solution)/shard_map/ppermute | solution.py:38
  58.9 26.7 %collective-permute-start.7 = (bf16[1024,256]{1,0:T(8,128)(2,1)}, bf16[1024,256]{1,0:T(8,128)(2,1)S(1)}, u32[]{:S(2)}, u32[]{:S(2)}) collective-permute-start(bf16[1024,256]{1,0:T(8,128)(2,1)} %get-tuple-element.163), channel_id=1, source_target_pairs={{0,2},{1,3},{2,0},{3,1},{4,6},{5,7},{6,4},{7,5},{8,10},{9,11},{10,... | collective-permute-start | bytes 1572872 | tf_op jit(solution)/shard_map/ppermute | solution.py:87
  88.9 28.5 %collective-permute-start.14 = (bf16[2048,128]{1,0:T(8,128)(2,1)}, bf16[2048,128]{1,0:T(8,128)(2,1)S(1)}, u32[]{:S(2)}, u32[]{:S(2)}) collective-permute-start(bf16[2048,128]{1,0:T(8,128)(2,1)} %slice.105), channel_id=1, source_target_pairs={{0,8},{4,12},{8,24},{12,28},{24,16},{28,20},{16,0},{20,4},{1,9},{5... | collective-permute-start | bytes 1572872 | tf_op jit(solution)/shard_map/ppermute | solution.py:38
  89.6 27.8 %collective-permute-start.15 = (bf16[2048,128]{1,0:T(8,128)(2,1)}, bf16[2048,128]{1,0:T(8,128)(2,1)}, u32[]{:S(2)}, u32[]{:S(2)}) collective-permute-start(bf16[2048,128]{1,0:T(8,128)(2,1)} %slice.106), channel_id=1, source_target_pairs={{0,16},{4,20},{8,0},{12,4},{24,8},{28,12},{16,24},{20,28},{1,17},{... | collective-permute-start | bytes 1572872 | tf_op jit(solution)/shard_map/ppermute | solution.py:38
  92.0 25.5 %collective-permute-start.19 = (bf16[1024,128]{1,0:T(8,128)(2,1)}, bf16[1024,128]{1,0:T(8,128)(2,1)S(1)}, u32[]{:S(2)}, u32[]{:S(2)}) collective-permute-start(bf16[1024,128]{1,0:T(8,128)(2,1)} %get-tuple-element.177), channel_id=1, source_target_pairs={{0,1},{1,2},{2,3},{3,0},{4,5},{5,6},{6,7},{7,4},{8,9},{9,10},{10,1... | collective-permute-start | bytes 786440 | tf_op jit(solution)/shard_map/ppermute | solution.py:87
  92.7 24.7 %collective-permute-start.18 = (bf16[1024,128]{1,0:T(8,128)(2,1)}, bf16[1024,128]{1,0:T(8,128)(2,1)}, u32[]{:S(2)}, u32[]{:S(2)}) collective-permute-start(bf16[1024,128]{1,0:T(8,128)(2,1)} %get-tuple-element.175), channel_id=1, source_target_pairs={{0,3},{1,0},{2,1},{3,2},{4,7},{5,4},{6,5},{7,6},{8,11},{9,8},{10,9... | collective-permute-start | bytes 786440 | tf_op jit(solution)/shard_map/ppermute | solution.py:87
  117.5 145.4 %reduce-scatter.3.cloned.1.call-start = ((), (), s32[]{:S(2)}) async-start(), calls=%async_computation.3 | async-start | bytes 2359296 | tf_op jit(solution)/shard_map/reduce_scatter | solution.py:473
  118.1 14.4 %collective-permute-start.20 = (bf16[1024,128]{1,0:T(8,128)(2,1)}, bf16[1024,128]{1,0:T(8,128)(2,1)S(1)}, u32[]{:S(2)}, u32[]{:S(2)}) collective-permute-start(bf16[1024,128]{1,0:T(8,128)(2,1)} %get-tuple-element.179), channel_id=1, source_target_pairs={{0,2},{1,3},{2,0},{3,1},{4,6},{5,7},{6,4},{7,5},{8,10},{9,11},{10,... | collective-permute-start | bytes 786440 | tf_op jit(solution)/shard_map/ppermute | solution.py:87
  132.5 13.9 %collective-permute-start.23 = (bf16[512,128]{1,0:T(8,128)(2,1)}, bf16[512,128]{1,0:T(8,128)(2,1)S(1)}, u32[]{:S(2)}, u32[]{:S(2)}) collective-permute-start(bf16[512,128]{1,0:T(8,128)(2,1)} %get-tuple-element.185), channel_id=1, source_target_pairs={{0,3},{1,0},{2,1},{3,2},{4,7},{5,4},{6,5},{7,6},{8,11},{9,8},{10,9... | collective-permute-start | bytes 393224 | tf_op jit(solution)/shard_map/ppermute | solution.py:87
  134.7 11.8 %collective-permute-start.24 = (bf16[512,128]{1,0:T(8,128)(2,1)}, bf16[512,128]{1,0:T(8,128)(2,1)S(1)}, u32[]{:S(2)}, u32[]{:S(2)}) collective-permute-start(bf16[512,128]{1,0:T(8,128)(2,1)} %get-tuple-element.186), channel_id=1, source_target_pairs={{0,2},{1,3},{2,0},{3,1},{4,6},{5,7},{6,4},{7,5},{8,10},{9,11},{10,... | collective-permute-start | bytes 393224 | tf_op jit(solution)/shard_map/ppermute | solution.py:87
  134.7 11.8 %collective-permute-start.25 = (bf16[512,128]{1,0:T(8,128)(2,1)}, bf16[512,128]{1,0:T(8,128)(2,1)S(1)}, u32[]{:S(2)}, u32[]{:S(2)}) collective-permute-start(bf16[512,128]{1,0:T(8,128)(2,1)} %get-tuple-element.187), channel_id=1, source_target_pairs={{0,1},{1,2},{2,3},{3,0},{4,5},{5,6},{6,7},{7,4},{8,9},{9,10},{10,1... | collective-permute-start | bytes 393224 | tf_op jit(solution)/shard_map/ppermute | solution.py:87
  146.4 11.6 %collective-permute-start.26 = (bf16[512,128]{1,0:T(8,128)(2,1)}, bf16[512,128]{1,0:T(8,128)(2,1)S(1)}, u32[]{:S(2)}, u32[]{:S(2)}) collective-permute-start(bf16[512,128]{1,0:T(8,128)(2,1)} %get-tuple-element.192), channel_id=1, source_target_pairs={{0,3},{1,0},{2,1},{3,2},{4,7},{5,4},{6,5},{7,6},{8,11},{9,8},{10,9... | collective-permute-start | bytes 393224 | tf_op jit(solution)/shard_map/ppermute | solution.py:87
  149.7 12.3 %collective-permute-start.27 = (bf16[512,128]{1,0:T(8,128)(2,1)}, bf16[512,128]{1,0:T(8,128)(2,1)S(1)}, u32[]{:S(2)}, u32[]{:S(2)}) collective-permute-start(bf16[512,128]{1,0:T(8,128)(2,1)} %get-tuple-element.193), channel_id=1, source_target_pairs={{0,2},{1,3},{2,0},{3,1},{4,6},{5,7},{6,4},{7,5},{8,10},{9,11},{10,... | collective-permute-start | bytes 393224 | tf_op jit(solution)/shard_map/ppermute | solution.py:87
  150.9 11.2 %collective-permute-start.28 = (bf16[512,128]{1,0:T(8,128)(2,1)}, bf16[512,128]{1,0:T(8,128)(2,1)S(1)}, u32[]{:S(2)}, u32[]{:S(2)}) collective-permute-start(bf16[512,128]{1,0:T(8,128)(2,1)} %get-tuple-element.194), channel_id=1, source_target_pairs={{0,1},{1,2},{2,3},{3,0},{4,5},{5,6},{6,7},{7,4},{8,9},{9,10},{10,1... | collective-permute-start | bytes 393224 | tf_op jit(solution)/shard_map/ppermute | solution.py:87
  162.0 10.6 %collective-permute-start.29 = (bf16[512,128]{1,0:T(8,128)(2,1)}, bf16[512,128]{1,0:T(8,128)(2,1)S(1)}, u32[]{:S(2)}, u32[]{:S(2)}) collective-permute-start(bf16[512,128]{1,0:T(8,128)(2,1)} %get-tuple-element.212), channel_id=1, source_target_pairs={{0,3},{1,0},{2,1},{3,2},{4,7},{5,4},{6,5},{7,6},{8,11},{9,8},{10,9... | collective-permute-start | bytes 393224 | tf_op jit(solution)/shard_map/ppermute | solution.py:87
  162.4 12.7 %collective-permute-start.30 = (bf16[512,128]{1,0:T(8,128)(2,1)}, bf16[512,128]{1,0:T(8,128)(2,1)S(1)}, u32[]{:S(2)}, u32[]{:S(2)}) collective-permute-start(bf16[512,128]{1,0:T(8,128)(2,1)} %get-tuple-element.213), channel_id=1, source_target_pairs={{0,2},{1,3},{2,0},{3,1},{4,6},{5,7},{6,4},{7,5},{8,10},{9,11},{10,... | collective-permute-start | bytes 393224 | tf_op jit(solution)/shard_map/ppermute | solution.py:87
  163.5 11.6 %collective-permute-start.31 = (bf16[512,128]{1,0:T(8,128)(2,1)}, bf16[512,128]{1,0:T(8,128)(2,1)S(1)}, u32[]{:S(2)}, u32[]{:S(2)}) collective-permute-start(bf16[512,128]{1,0:T(8,128)(2,1)} %get-tuple-element.214), channel_id=1, source_target_pairs={{0,1},{1,2},{2,3},{3,0},{4,5},{5,6},{6,7},{7,4},{8,9},{9,10},{10,1... | collective-permute-start | bytes 393224 | tf_op jit(solution)/shard_map/ppermute | solution.py:87
  179.9 8.5 %collective-permute-start.32 = (bf16[512,128]{1,0:T(8,128)(2,1)}, bf16[512,128]{1,0:T(8,128)(2,1)S(1)}, u32[]{:S(2)}, u32[]{:S(2)}) collective-permute-start(bf16[512,128]{1,0:T(8,128)(2,1)} %get-tuple-element.249), channel_id=1, source_target_pairs={{0,3},{1,0},{2,1},{3,2},{4,7},{5,4},{6,5},{7,6},{8,11},{9,8},{10,9... | collective-permute-start | bytes 393224 | tf_op jit(solution)/shard_map/ppermute | solution.py:87
  179.9 13.5 %collective-permute-start.33 = (bf16[512,128]{1,0:T(8,128)(2,1)S(1)}, bf16[512,128]{1,0:T(8,128)(2,1)S(1)}, u32[]{:S(2)}, u32[]{:S(2)}) collective-permute-start(bf16[512,128]{1,0:T(8,128)(2,1)S(1)} %copy-done.49), channel_id=1, source_target_pairs={{0,2},{1,3},{2,0},{3,1},{4,6},{5,7},{6,4},{7,5},{8,10},{9,11},{10,... | collective-permute-start | bytes 393224 | tf_op jit(solution)/shard_map/ppermute | solution.py:87
  181.2 12.2 %collective-permute-start.34 = (bf16[512,128]{1,0:T(8,128)(2,1)S(1)}, bf16[512,128]{1,0:T(8,128)(2,1)S(1)}, u32[]{:S(2)}, u32[]{:S(2)}) collective-permute-start(bf16[512,128]{1,0:T(8,128)(2,1)S(1)} %copy-done.47), channel_id=1, source_target_pairs={{0,1},{1,2},{2,3},{3,0},{4,5},{5,6},{6,7},{7,4},{8,9},{9,10},{10,1... | collective-permute-start | bytes 393224 | tf_op jit(solution)/shard_map/ppermute | solution.py:87
  194.1 21.1 %collective-permute-start.37 = (bf16[1024,128]{1,0:T(8,128)(2,1)S(1)}, bf16[1024,128]{1,0:T(8,128)(2,1)S(1)}, u32[]{:S(2)}, u32[]{:S(2)}) collective-permute-start(bf16[1024,128]{1,0:T(8,128)(2,1)S(1)} %copy-done.30), channel_id=1, source_target_pairs={{0,1},{1,2},{2,3},{3,0},{4,5},{5,6},{6,7},{7,4},{8,9},{9,10},{10,1... | collective-permute-start | bytes 786440 | tf_op jit(solution)/shard_map/ppermute | solution.py:87
  194.1 21.1 %collective-permute-start.36 = (bf16[1024,128]{1,0:T(8,128)(2,1)S(1)}, bf16[1024,128]{1,0:T(8,128)(2,1)S(1)}, u32[]{:S(2)}, u32[]{:S(2)}) collective-permute-start(bf16[1024,128]{1,0:T(8,128)(2,1)S(1)} %copy-done.31), channel_id=1, source_target_pairs={{0,2},{1,3},{2,0},{3,1},{4,6},{5,7},{6,4},{7,5},{8,10},{9,11},{10,... | collective-permute-start | bytes 786440 | tf_op jit(solution)/shard_map/ppermute | solution.py:87
  195.2 20.1 %collective-permute-start.35 = (bf16[1024,128]{1,0:T(8,128)(2,1)S(1)}, bf16[1024,128]{1,0:T(8,128)(2,1)S(1)}, u32[]{:S(2)}, u32[]{:S(2)}) collective-permute-start(bf16[1024,128]{1,0:T(8,128)(2,1)S(1)} %copy-done.32), channel_id=1, source_target_pairs={{0,3},{1,0},{2,1},{3,2},{4,7},{5,4},{6,5},{7,6},{8,11},{9,8},{10,9... | collective-permute-start | bytes 786440 | tf_op jit(solution)/shard_map/ppermute | solution.py:87
  216.1 109.6 %reduce-scatter.5.cloned.1.call-start = ((), (), s32[]{:S(2)}) async-start(), calls=%async_computation.4 | async-start | bytes 327680 | tf_op jit(solution)/shard_map/reduce_scatter | solution.py:503
  219.0 43.9 %collective-permute-start.39 = (bf16[12288,128]{1,0:T(8,128)(2,1)}, bf16[12288,128]{1,0:T(8,128)(2,1)S(1)}, u32[]{:S(2)}, u32[]{:S(2)}) collective-permute-start(bf16[12288,128]{1,0:T(8,128)(2,1)} %get-tuple-element.273), channel_id=1, source_target_pairs={{0,4},{4,0},{8,12},{12,8},{16,20},{20,16},{24,28},{28,24},{1,5},{5... | collective-permute-start | bytes 9437192 | tf_op jit(solution)/shard_map/ppermute | solution.py:41
  221.0 19.8 %collective-permute-start.40 = (bf16[2048,128]{1,0:T(8,128)(2,1)S(1)}, bf16[2048,128]{1,0:T(8,128)(2,1)}, u32[]{:S(2)}, u32[]{:S(2)}) collective-permute-start(bf16[2048,128]{1,0:T(8,128)(2,1)S(1)} %get-tuple-element.327), channel_id=1, source_target_pairs={{0,8},{4,12},{8,24},{12,28},{24,16},{28,20},{16,0},{20,4},{1,9},{5... | collective-permute-start | bytes 1572872 | tf_op jit(solution)/shard_map/ppermute | solution.py:38
  221.7 19.1 %collective-permute-start.41 = (bf16[2048,128]{1,0:T(8,128)(2,1)S(1)}, bf16[2048,128]{1,0:T(8,128)(2,1)}, u32[]{:S(2)}, u32[]{:S(2)}) collective-permute-start(bf16[2048,128]{1,0:T(8,128)(2,1)S(1)} %get-tuple-element.326), channel_id=1, source_target_pairs={{0,16},{4,20},{8,0},{12,4},{24,8},{28,12},{16,24},{20,28},{1,17},{... | collective-permute-start | bytes 1572872 | tf_op jit(solution)/shard_map/ppermute | solution.py:38
  265.8 49.1 %collective-permute-start.47 = (bf16[12288,128]{1,0:T(8,128)(2,1)}, bf16[12288,128]{1,0:T(8,128)(2,1)}, u32[]{:S(2)}, u32[]{:S(2)}) collective-permute-start(bf16[12288,128]{1,0:T(8,128)(2,1)} %get-tuple-element.300), channel_id=1, source_target_pairs={{0,4},{4,0},{8,12},{12,8},{16,20},{20,16},{24,28},{28,24},{1,5},{5... | collective-permute-start | bytes 9437192 | tf_op jit(solution)/shard_map/ppermute | solution.py:41
  270.1 35.1 %collective-permute-start.45 = (bf16[4096,128]{1,0:T(8,128)(2,1)}, bf16[4096,128]{1,0:T(8,128)(2,1)S(1)}, u32[]{:S(2)}, u32[]{:S(2)}) collective-permute-start(bf16[4096,128]{1,0:T(8,128)(2,1)} %pad_maximum_fusion.2), channel_id=1, source_target_pairs={{0,16},{4,20},{8,0},{12,4},{24,8},{28,12},{16,24},{20,28},{1,17},{... | collective-permute-start | bytes 3145736 | tf_op jit(solution)/shard_map/ppermute | solution.py:38
  274.0 31.2 %collective-permute-start.44 = (bf16[4096,128]{1,0:T(8,128)(2,1)}, bf16[4096,128]{1,0:T(8,128)(2,1)S(1)}, u32[]{:S(2)}, u32[]{:S(2)}) collective-permute-start(bf16[4096,128]{1,0:T(8,128)(2,1)} %pad_maximum_fusion.1), channel_id=1, source_target_pairs={{0,8},{4,12},{8,24},{12,28},{24,16},{28,20},{16,0},{20,4},{1,9},{5... | collective-permute-start | bytes 3145736 | tf_op jit(solution)/shard_map/ppermute | solution.py:38
  274.6 16.7 %collective-permute-start.43 = (bf16[1024,256]{1,0:T(8,128)(2,1)S(1)}, bf16[1024,256]{1,0:T(8,128)(2,1)S(1)}, u32[]{:S(2)}, u32[]{:S(2)}) collective-permute-start(bf16[1024,256]{1,0:T(8,128)(2,1)S(1)} %copy-done.22), channel_id=1, source_target_pairs={{0,1},{1,2},{2,3},{3,0},{4,5},{5,6},{6,7},{7,4},{8,9},{9,10},{10,1... | collective-permute-start | bytes 1572872 | tf_op jit(solution)/shard_map/ppermute | solution.py:87
  276.1 24.6 %collective-permute-start.42 = (bf16[1024,256]{1,0:T(8,128)(2,1)S(1)}, bf16[1024,256]{1,0:T(8,128)(2,1)S(1)}, u32[]{:S(2)}, u32[]{:S(2)}) collective-permute-start(bf16[1024,256]{1,0:T(8,128)(2,1)S(1)} %copy-done.24), channel_id=1, source_target_pairs={{0,3},{1,0},{2,1},{3,2},{4,7},{5,4},{6,5},{7,6},{8,11},{9,8},{10,9... | collective-permute-start | bytes 1572872 | tf_op jit(solution)/shard_map/ppermute | solution.py:87
  291.3 19.4 %collective-permute-start.48 = (bf16[2048,128]{1,0:T(8,128)(2,1)}, bf16[2048,128]{1,0:T(8,128)(2,1)}, u32[]{:S(2)}, u32[]{:S(2)}) collective-permute-start(bf16[2048,128]{1,0:T(8,128)(2,1)} %get-tuple-element.325), channel_id=1, source_target_pairs={{0,8},{4,12},{8,24},{12,28},{24,16},{28,20},{16,0},{20,4},{1,9},{5... | collective-permute-start | bytes 1572872 | tf_op jit(solution)/shard_map/ppermute | solution.py:38
  301.5 13.4 %collective-permute-start.49 = (bf16[2048,128]{1,0:T(8,128)(2,1)}, bf16[2048,128]{1,0:T(8,128)(2,1)S(1)}, u32[]{:S(2)}, u32[]{:S(2)}) collective-permute-start(bf16[2048,128]{1,0:T(8,128)(2,1)} %get-tuple-element.324), channel_id=1, source_target_pairs={{0,16},{4,20},{8,0},{12,4},{24,8},{28,12},{16,24},{20,28},{1,17},{... | collective-permute-start | bytes 1572872 | tf_op jit(solution)/shard_map/ppermute | solution.py:38
  319.8 29.9 %collective-permute-start.51 = (bf16[4096,128]{1,0:T(8,128)(2,1)}, bf16[4096,128]{1,0:T(8,128)(2,1)}, u32[]{:S(2)}, u32[]{:S(2)}) collective-permute-start(bf16[4096,128]{1,0:T(8,128)(2,1)} %pad_maximum_fusion.3), channel_id=1, source_target_pairs={{0,8},{4,12},{8,24},{12,28},{24,16},{28,20},{16,0},{20,4},{1,9},{5... | collective-permute-start | bytes 3145736 | tf_op jit(solution)/shard_map/ppermute | solution.py:38
  322.5 27.1 %collective-permute-start.52 = (bf16[4096,128]{1,0:T(8,128)(2,1)}, bf16[4096,128]{1,0:T(8,128)(2,1)}, u32[]{:S(2)}, u32[]{:S(2)}) collective-permute-start(bf16[4096,128]{1,0:T(8,128)(2,1)} %pad_maximum_fusion.4), channel_id=1, source_target_pairs={{0,16},{4,20},{8,0},{12,4},{24,8},{28,12},{16,24},{20,28},{1,17},{... | collective-permute-start | bytes 3145736 | tf_op jit(solution)/shard_map/ppermute | solution.py:38
  323.0 23.9 %collective-permute-start.50 = (bf16[1024,256]{1,0:T(8,128)(2,1)S(1)}, bf16[1024,256]{1,0:T(8,128)(2,1)}, u32[]{:S(2)}, u32[]{:S(2)}) collective-permute-start(bf16[1024,256]{1,0:T(8,128)(2,1)S(1)} %copy-done.23), channel_id=1, source_target_pairs={{0,2},{1,3},{2,0},{3,1},{4,6},{5,7},{6,4},{7,5},{8,10},{9,11},{10,... | collective-permute-start | bytes 1572872 | tf_op jit(solution)/shard_map/ppermute | solution.py:87
  (60 other events, 562.6 us)
Sparse Core Ops, SparseCore 0:
  117.6 25.7 all-gather.1
  216.2 46.6 reduce-scatter.2
  305.3 18.3 reduce-scatter.4

commit v6 on v5

--- a/solution.py
+++ b/solution.py
@@ -281,11 +281,9 @@
     def _():
         copies = []
         for i in range(parts):
-            for j in range(parts):
-                src = w_hbm.at[aligned(place(i) * f_wide, f_wide, f_wide), aligned(place(j) * h_wide, h_wide, h_wide)]
-                dst = weight.at[pl.ds(i * f_wide, f_wide), pl.ds(j * h_wide, h_wide)]
-                copies.append(pltpu.make_async_copy(src, dst, sems.at[i * parts + j]))
-                copies[-1].start()
+            src = w_hbm.at[aligned(place(i) * f_wide, f_wide, f_wide)]
+            copies.append(pltpu.make_async_copy(src, weight.at[pl.ds(i * f_wide, f_wide)], sems.at[i]))
+            copies[-1].start()
         for copy in copies:
             copy.wait()
 
@@ -334,7 +332,7 @@
             + [any_spec()]
             + [any_spec()] * len(earlier),
             out_specs=[spec(w, first if whole else 0) for w, whole in kinds],
-            scratch_shapes=[pltpu.VMEM((features, hidden), BF16), pltpu.SemaphoreType.DMA((parts * parts,))],
+            scratch_shapes=[pltpu.VMEM((features, hidden), BF16), pltpu.SemaphoreType.DMA((parts,))],
         ),
         out_shape=[jax.ShapeDtypeStruct((all_rows if whole else rows, w), BF16) for w, whole in kinds],
         input_output_aliases={n_inputs + i: at for i, at in enumerate(whole_at)} if earlier else {},
@@ -357,6 +355,131 @@
     )
 
 
+def total_of(*values):
+    return functools.reduce(lambda a, b: a + b, [v.astype(F32) for v in values]).astype(BF16)
+
+
+def step_kernel(low_blocks, own_up, got_up, up, own_down, got_down, down, to_up, to_down):
+    low = pl.program_id(0) < low_blocks
+
+    def put(out, own, got, more, with_more):
+        both = own[...].astype(F32) + got[...].astype(F32)
+
+        @pl.when(with_more)
+        def _():
+            out[...] = (both + more[...].astype(F32)).astype(BF16)
+
+        @pl.when(jnp.logical_not(with_more))
+        def _():
+            out[...] = both.astype(BF16)
+
+    put(to_up, own_up, got_up, up, low)
+    put(to_down, own_down, got_down, down, jnp.logical_not(low))
+
+
+def step_sums(own_up, at_up, up, own_down, at_down, down, got):
+    rows, width = own_up.shape
+    step = min(rows // 2, 512)
+    blocks = rows // step
+    low = blocks // 2
+
+    def spec(index):
+        return pl.BlockSpec((step, width), lambda t: (index(t), 0))
+
+    here = spec(lambda t: t)
+    return pl.pallas_call(
+        functools.partial(step_kernel, low),
+        grid=(blocks,),
+        in_specs=[
+            here,
+            spec(lambda t: t + at_up * blocks),
+            spec(lambda t: jnp.minimum(t, low - 1)),
+            here,
+            spec(lambda t: t + at_down * blocks),
+            spec(lambda t: jnp.maximum(t - low, 0)),
+        ],
+        out_specs=[here, here],
+        out_shape=[jax.ShapeDtypeStruct((rows, width), BF16)] * 2,
+        compiler_params=params(),
+        cost_estimate=pl.CostEstimate(flops=4 * rows * width, bytes_accessed=14 * rows * width, transcendentals=0),
+        name="step_sums",
+    )(own_up, got, up, own_down, got, down)
+
+
+def result_kernel(n_ready, *refs):
+    ready, (own, got, up, down, out) = refs[:n_ready], refs[n_ready:]
+    width = own.shape[1]
+    for c, ref in enumerate(ready):
+        out[:, c * width : (c + 1) * width] = ref[...]
+    out[:, n_ready * width :] = (
+        own[...].astype(F32) + got[...].astype(F32) + up[...].astype(F32) + down[...].astype(F32)
+    ).astype(BF16)
+
+
+def result_of(ready, own, got, at, up, down):
+    rows, width = own.shape
+    step = min(rows, 512)
+    blocks = rows // step
+    here = pl.BlockSpec((step, width), lambda t: (t, 0))
+    there = pl.BlockSpec((step, width), lambda t: (t + at * blocks, 0))
+    wide = width * (len(ready) + 1)
+    return pl.pallas_call(
+        functools.partial(result_kernel, len(ready)),
+        grid=(blocks,),
+        in_specs=[here] * (len(ready) + 1) + [there, here, here],
+        out_specs=pl.BlockSpec((step, wide), lambda t: (t, 0)),
+        out_shape=jax.ShapeDtypeStruct((rows, wide), BF16),
+        compiler_params=params(),
+        cost_estimate=pl.CostEstimate(flops=4 * rows * width, bytes_accessed=14 * rows * width, transcendentals=0),
+        name="feature_grad",
+    )(*ready, own, got, up, down)
+
+
+class Reduction:
+    def __init__(self, ring, own_far, own_near, other_far, other_near):
+        self.ring, self.middle = ring, ring.chips // 2
+        self.near = [o for o in range(ring.chips) if o != self.middle]
+        self.own_far, self.own_near, self.other_far, self.other_near = own_far, own_near, other_far, other_near
+        self.rows = own_far.shape[0]
+
+    def far_swap(self):
+        return self.ring.sibling(self.other_far)
+
+    def near_swap(self, after):
+        return self.ring.sibling(lax.optimization_barrier((self.other_near, after))[0])
+
+    def far_sums(self, got):
+        half = self.rows // 2
+        return [total_of(self.own_far[at : at + half], got[at : at + half]) for at in (0, half)]
+
+    def hops(self, up, down):
+        return self.ring.hop(up, 1), self.ring.hop(down, -1)
+
+    def place(self, offset):
+        return self.near.index(offset % self.ring.chips)
+
+    def near_terms(self, offset, got):
+        at = self.place(offset)
+        return self.own_near[at], got[at * self.rows : (at + 1) * self.rows]
+
+    def sums(self, step, got, up, down, kernel):
+        if step < self.middle - 1:
+            return total_of(*self.near_terms(step, got), up), total_of(*self.near_terms(-step, got), down)
+        at_up, at_down = self.place(step), self.place(-step)
+        if kernel:
+            return step_sums(self.own_near[at_up], at_up, up, self.own_near[at_down], at_down, down, got)
+        zeros = jnp.zeros_like(up)
+        return (
+            total_of(*self.near_terms(step, got), jnp.concatenate([up, zeros])),
+            total_of(*self.near_terms(-step, got), jnp.concatenate([zeros, down])),
+        )
+
+    def last(self, up, down):
+        if self.middle > 1:
+            return up, down
+        return jnp.concatenate([up, jnp.zeros_like(up)]), jnp.concatenate([jnp.zeros_like(down), down])
+
+
 def local(features, tiles, columns, counts, weight, cotangent):
     rows, f_wide = features.shape
     h_wide = cotangent.shape[1]
@@ -390,7 +513,6 @@
 
     share = weight.shape[0] // row_size
     w_share = lax.dynamic_slice_in_dim(weight, lax.axis_index("row") * share, share, 0)
-    w_share = lax.all_gather(w_share, "rep", axis=1, tiled=True)
 
     cot_blocks = [part_of(cotangent, u) for u in range(parts)]
     xs = [features[:, c * width : (c + 1) * width] for c in range(chunks)]
@@ -422,6 +544,7 @@
         w.go(**{f"far_up{c}": ring.hop(up[:half], 1), f"far_down{c}": ring.hop(down[half:], -1)})
         if c == 0:
             w.go(cot_ends=cot_ends, own_other=own_other, metas=(spmm_meta, spmm_t_meta, dense_meta))
+            w.go(shares=send([w.gate(w_share)] * parts, ends + inner))
         seen = []
         if c == last:
             for step in range(1, middle):
@@ -442,7 +565,8 @@
         got_own[c, len(offsets) - 2], got_own[c, len(offsets) - 1] = w[f"far_up{c}"], w[f"far_down{c}"]
         if c < last:
             up = down = w.gate(xs[c + 1])
-    w_full = lax.all_gather(w.gate(w_share), "row", axis=0, tiled=True)
+    w_rows = jnp.concatenate(ordered(w_share, w["shares"]), axis=1)
+    w_full = lax.all_gather(w.gate(w_rows), "row", axis=0, tiled=True)
     for i in (-2, -1):
         got_other[last, len(offsets) + i] = ring.sibling(got_own[last, len(offsets) + i])
 
@@ -466,11 +590,24 @@
         w.close()
         w.go(**{f"back_got{h}": send(w[f"back{h}"], ends + inner)})
     act, back, mixed_rows, grad_rows = w["whole"]
-    by_row = grad_rows.reshape(part_rows, row_size, -1)
-    sums = jnp.einsum("nf,nrh->rfh", mixed_rows, by_row, preferred_element_type=F32).astype(BF16)
-    w.go(sums=sums)
+    sums = lax.dot_general(grad_rows, mixed_rows, (((0,), (0,)), ((), ())), preferred_element_type=F32).astype(BF16)
+    share = sums.shape[0] // row_size
+
+    def sums_for(offset, other):
+        return lax.dynamic_slice_in_dim(sums, ring.device_at(offset, other) * share, share, 0)
+
+    wg = Reduction(
+        ring,
+        sums_for(middle, False),
+        [sums_for(o, False) for o in near],
+        sums_for(middle, True),
+        jnp.concatenate([sums_for(o, True) for o in near]),
+    )
+    wg_far = wg.far_swap()
+    w.go(wg_own=(wg.own_far, wg.own_near), wg_far=wg_far, wg_near=wg.near_swap(wg_far))
     w.close()
-    weight_terms = lax.psum_scatter(w["sums"], "row", scatter_dimension=0, tiled=True)[0]
+    wg.own_far, wg.own_near = w["wg_own"]
+    w.go(wg_up_down=wg.hops(*wg.far_sums(w["wg_far"])))
 
     def run_spmm_t(c, grads):
         return spmm_t(tiles, columns, counts, spmm_t_meta, grads, parts, held, rows, rows * row_size)
@@ -481,58 +618,54 @@
         w.go(**{f"rest_got{c}": send([w.gate(b[c]) for b in back], ends + inner)})
     w.close()
 
-    near_sums = []
+    def wg_steps(first, until):
+        up, down = w["wg_up_down"]
+        for step in range(first, until, -1):
+            up, down = wg.hops(*wg.sums(step, w["wg_near"], up, down, False))
+        return up, down
+
+    reductions = []
     for c in range(chunks):
         terms = w[f"terms{c}"]
-        own_far, own_near, other_far, other_near = terms[0], terms[1:-2], terms[-2], terms[-1]
-        got_far = ring.sibling(other_far)
-        got_near = ring.sibling(lax.optimization_barrier((other_near, got_far))[0])
-        far = [
-            (own_far[at : at + half].astype(F32) + got_far[at : at + half].astype(F32)).astype(BF16)
-            for at in (0, half)
-        ]
-        w.go(**{f"got_near{c}": got_near, f"sum{c}_{middle}": (ring.hop(far[0], 1), ring.hop(far[1], -1))})
+        red = Reduction(ring, terms[0], terms[1:-2], terms[-2], terms[-1])
+        reductions.append(red)
+        got_far = red.far_swap()
+        got_near = red.near_swap(got_far)
+        far = red.far_sums(got_far)
+        w.go(**{f"got_near{c}": got_near, f"sum{c}_{middle}": red.hops(*far)})
         if c < last:
             grads = ordered(back[0][c + 1], w[f"rest_got{c + 1}"])
             grads = lax.optimization_barrier((grads, far[0][:8], far[1][:8]))[0]
             w.go(**{f"terms{c + 1}": run_spmm_t(c + 1, grads)})
         if c == 0:
-            w.go(weight_terms=weight_terms)
+            w.go(wg_last=wg_steps(middle - 1, 0))
+        if c == last:
+            w.go(act_inner=send([lax.optimization_barrier((a, got_near))[0] for a in act], inner))
         w.close()
         if c == 0:
-            weight_terms = lax.psum_scatter(w["weight_terms"], "rep", scatter_dimension=0, tiled=True)
-            w.go(act_ends=send([w.gate(a) for a in act], ends))
-
-        def near_sum(offset, got=w[f"got_near{c}"], own=own_near):
-            at = near.index(offset % ring.chips)
-            return own[at].astype(F32) + got[at * rows : (at + 1) * rows].astype(F32)
-
-        near_sums.append(near_sum)
+            block = total_of(*wg.near_terms(0, w["wg_near"]), *wg.last(*w["wg_last"]))
+            cuts = [
+                lax.dynamic_slice_in_dim(block, lax.rem(rep + u, parts) * f_wide, f_wide, 1) for u in range(parts)
+            ]
+            wg_got = send(cuts, ends + inner)
+            w.go(weight_grad=functools.reduce(lambda a, b: a + b, [v.astype(F32) for v in [cuts[0], *wg_got.values()]]))
         for step in range(middle - 1, 0, -1):
-            up, down = w[f"sum{c}_{step + 1}"]
-            to_up, to_down = near_sum(step), near_sum(-step)
-            if step == middle - 1:
-                to_up = jnp.concatenate([to_up[:half] + up.astype(F32), to_up[half:]])
-                to_down = jnp.concatenate([to_down[:half], to_down[half:] + down.astype(F32)])
-            else:
-                to_up, to_down = to_up + up.astype(F32), to_down + down.astype(F32)
-            to_up, to_down = to_up.astype(BF16), to_down.astype(BF16)
-            w.go(**{f"sum{c}_{step}": (ring.hop(to_up, 1), ring.hop(to_down, -1))})
+            to_up, to_down = red.sums(step, w[f"got_near{c}"], *w[f"sum{c}_{step + 1}"], True)
+            w.go(**{f"sum{c}_{step}": red.hops(to_up, to_down)})
             if step > 1:
                 w.close()
             else:
                 w.token = to_up[:8]
-    got = {**w.done, **w.pending, "act_inner": send([w.gate(a) for a in act], inner)}
-    feature_grad = []
-    for c, near_sum in enumerate(near_sums):
-        up, down = got[f"sum{c}_1"]
-        if middle == 1:
-            feature_grad.append((near_sum(0) + jnp.concatenate([up, down]).astype(F32)).astype(BF16))
-        else:
-            feature_grad.append((near_sum(0) + up.astype(F32) + down.astype(F32)).astype(BF16))
-    weight_grad = w.gate(weight_terms).astype(F32)
+    got = {**w.done, **w.pending, "act_ends": send([w.gate(a) for a in act], ends)}
+    ready = [
+        total_of(*red.near_terms(0, got[f"got_near{c}"]), *red.last(*got[f"sum{c}_1"]))
+        for c, red in enumerate(reductions[:-1])
+    ]
+    red = reductions[-1]
+    at = red.place(0)
+    feature_grad = result_of(ready, red.own_near[at], got[f"got_near{last}"], at, *red.last(*got[f"sum{last}_1"]))
+    weight_grad = got["weight_grad"].T
     act = ordered(act[0], got["act_ends"], got["act_inner"])
-    feature_grad = jnp.concatenate(feature_grad, axis=1)
     activations = jnp.zeros((rows, h_wide), BF16)
     for u in range(parts):
         activations = lax.dynamic_update_slice_in_dim(activations, act[u], lax.rem(rep + u, parts) * part_rows, 0)

time: 362 us -> 346 us (0.956)
  blocking collectives: 21.6 us -> 0 us
  Pallas kernels: 85.7 us -> 106 us
  starting transfers between devices: 54.9 us -> 69.1 us
  other arithmetic: 21.2 us -> 9.51 us
  waiting for transfers between devices: 113 us -> 102 us
  local copies, waits for them, and re-layouts: 35.9 us -> 29.7 us
    reduce_scatter x2 -> x0, waiting for transfers between devices: 22.1 us -> none  [the longest x1 22.1 us: local(): lax.psum_scatter(w['sums'], 'row', scatter_dimension=0, tiled=True)[0]]
    all_gather x1 -> x0, blocking collectives: 21.6 us -> none  [local(): w_share = lax.all_gather(w_share, 'rep', axis=1, tiled=True)]
    pallas_call x0 -> x3, Pallas kernels: none -> 21 us  [the longest x2 13.6 us: step_sums(): pl.pallas_call(functools.partial(step_kernel, low), grid=(blocks,), in_sp...]
    ppermute x16 -> x20, waiting for transfers between devices: 29.1 us -> 47.4 us  [hop(): return lax.ppermute(value, 'row', self.perm(step))]
    ppermute x24 -> x30, starting transfers between devices: 33.6 us -> 43.8 us  [send(): lax.ppermute(blocks[s], 'rep', [(i, (i + s) % size) for i in range(size)])]
    concatenate x5 -> x2, other arithmetic: 5.71 us -> 0.79 us  [the longest x1 0.73 us: local(): w_rows = jnp.concatenate(ordered(w_share, w['shares']), axis=1)]
    ppermute x24 -> x30, waiting for transfers between devices: 54.5 us -> 50.1 us  [send(): lax.ppermute(blocks[s], 'rep', [(i, (i + s) % size) for i in range(size)])]
    reshape x1 -> x0, local copies, waits for them, and re-layouts: 4.09 us -> none  [local(): by_row = grad_rows.reshape(part_rows, row_size, -1)]
  transfers between devices with their start and end apart: 56 -> 66, of which waited for: 18 -> 27; matrix products, arithmetic and copies ran while one was open for 13% -> 8% of each run, Pallas kernels for 24% -> 27%
where the time goes in v6:
time: 346 us; the launch traced here: 344 us
  Pallas kernels  106 us (31%)
  waiting for transfers between devices  102 us (29%)
  starting transfers between devices  69.1 us (20%)
  local copies, waits for them, and re-layouts  29.7 us (9%)
  between operations  22.8 us (7%)
  other arithmetic  9.51 us (3%)
  matrix products  4.7 us (1%)
    ppermute x30, waiting for transfers between devices, send(): lax.ppermute(blocks[s], 'rep', [(i, (i + s) % size) for i in range(size)])  50.1 us
    ppermute x20, waiting for transfers between devices, hop(): return lax.ppermute(value, 'row', self.perm(step))  47.4 us
    ppermute x30, starting transfers between devices, send(): lax.ppermute(blocks[s], 'rep', [(i, (i + s) % size) for i in range(size)])  43.8 us
    pallas_call x3, Pallas kernels, spmm(): pl.pallas_call(functools.partial(spmm_kernel, len(pieces), per_part, skip...  36.7 us
    pallas_call x2, Pallas kernels, spmm_t(): pl.pallas_call(functools.partial(spmm_t_kernel, len(grads), per_part, len...  34.6 us
    ppermute x20, starting transfers between devices, hop(): return lax.ppermute(value, 'row', self.perm(step))  22.5 us
    pallas_call x2, Pallas kernels, dense(): pl.pallas_call(functools.partial(dense_kernel, parts, chunks, len(earlier...  14.1 us
    pallas_call x2, Pallas kernels, step_sums(): pl.pallas_call(functools.partial(step_kernel, low), grid=(blocks,), in_sp...  13.6 us
  transfers between devices with their start and end apart: 66, of which 27 were waited for; matrix products, arithmetic and copies ran while one was open for 8% of the time, Pallas kernels for 27%

profile of v6, /device:TPU:0, one launch (start us, length us, event | category | flops | bytes accessed | tf_op | source)
XLA Modules:
  0.0 344.5 jit_solution(8127164869513736078)
XLA Ops:
  7.7 1.7 fusion.1
  9.4 2.6 collective-permute-start
  12.1 2.9 constant_dynamic-slice_fusion.2
  15.0 4.1 %collective-permute-start.4 = (bf16[1024,256]{1,0:T(8,128)(2,1)}, bf16[1024,256]{1,0:T(8,128)(2,1)S(1)}, u32[]{:S(2)}, u32[]{:S(2)}) collective-permute-start(bf16[1024,256]{1,0:T(8,128)(2,1)} %get-tuple-element.365), channel_id=1, source_target_pairs={{0,3},{1,0},{2,1},{3,2},{4,7},{5,4},{6,5},{7,6},{8,11},{9,8},{10,9... | collective-permute-start | bytes 1572872 | tf_op jit(solution)/shard_map/ppermute | solution.py:87
  19.1 16.8 %collective-permute-done.refs_1_ = bf16[4096,128]{1,0:T(8,128)(2,1)} collective-permute-done((bf16[4096,128]{1,0:T(8,128)(2,1)S(1)}, bf16[4096,128]{1,0:T(8,128)(2,1)}, u32[]{:S(2)}, u32[]{:S(2)}) %collective-permute-start) | collective-permute-done | bytes 1048608 | tf_op jit(solution)/shard_map/ppermute | solution.py:38
  37.9 3.7 %collective-permute-start.7 = (bf16[128,256]{1,0:T(8,128)(2,1)S(1)}, bf16[128,256]{1,0:T(8,128)(2,1)S(1)}, u32[]{:S(2)}, u32[]{:S(2)}) collective-permute-start(bf16[128,256]{1,0:T(8,128)(2,1)S(1)} %constant_dynamic-slice_fusion.4), channel_id=1, source_target_pairs={{0,3},{1,0},{2,1},{3,2},{4,7},{5,4},{6,5},{7,6},{8,11},{9,8},{10,9... | collective-permute-start | bytes 196616 | tf_op jit(solution)/shard_map/ppermute | solution.py:87
  50.6 1.8 collective-permute-start.3
  66.5 3.0 fusion
  70.5 14.4 %spmm.3 = (bf16[1024,128]{1,0:T(8,128)(2,1)}, bf16[1024,128]{1,0:T(8,128)(2,1)}, bf16[1024,128]{1,0:T(8,128)(2,1)}, bf16[1024,128]{1,0:T(8,128)(2,1)}) custom-call(s32[32,16]{1,0:T(8,128)} %copy.71.cols, s32[32]{0:T(128)} %counts.9, s32[11]{0:T(128)} %stack.75.meta, bf16[32,16,128,128]{3,2,1,0:T(8,128)(2,1)} %tiles.9, bf16[4096,128]{1,0:T(8,128)(2,1)} %copy-done.9, ...), custom_call_target="tpu_custom_call" | custom-call | flops 2147483648 | bytes 25165824 | tf_op jit(solution)/shard_map/spmm/pallas_call | solution.py:158
  85.0 6.7 %collective-permute-done.10.refs_10_ = bf16[1024,256]{1,0:T(8,128)(2,1)S(1)} collective-permute-done((bf16[1024,256]{1,0:T(8,128)(2,1)}, bf16[1024,256]{1,0:T(8,128)(2,1)S(1)}, u32[]{:S(2)}, u32[]{:S(2)}) %collective-permute-start.10) | collective-permute-done | bytes 524320 | tf_op jit(solution)/shard_map/ppermute | solution.py:87
  98.2 3.8 %collective-permute-start.21 = (bf16[1024,128]{1,0:T(8,128)(2,1)}, bf16[1024,128]{1,0:T(8,128)(2,1)}, u32[]{:S(2)}, u32[]{:S(2)}) collective-permute-start(bf16[1024,128]{1,0:T(8,128)(2,1)} %get-tuple-element.192), channel_id=1, source_target_pairs={{0,3},{1,0},{2,1},{3,2},{4,7},{5,4},{6,5},{7,6},{8,11},{9,8},{10,9... | collective-permute-start | bytes 786440 | tf_op jit(solution)/shard_map/ppermute | solution.py:87
  102.7 6.5 %collective-permute-done.17.refs_3_ = bf16[2048,128]{1,0:T(8,128)(2,1)S(1)} collective-permute-done((bf16[2048,128]{1,0:T(8,128)(2,1)}, bf16[2048,128]{1,0:T(8,128)(2,1)S(1)}, u32[]{:S(2)}, u32[]{:S(2)}) %collective-permute-start.17) | collective-permute-done | bytes 524320 | tf_op jit(solution)/shard_map/ppermute | solution.py:38
  110.5 1.9 collective-permute-done.21.refs_2_
  113.0 2.4 collective-permute-start.23
  116.4 11.2 %spmm.4 = (bf16[512,128]{1,0:T(8,128)(2,1)}, bf16[512,128]{1,0:T(8,128)(2,1)}, bf16[512,128]{1,0:T(8,128)(2,1)}, bf16[512,128]{1,0:T(8,128)(2,1)}) custom-call(s32[32,16]{1,0:T(8,128)} %copy.71.cols, s32[32]{0:T(128)} %counts.9, s32[11]{0:T(128)} %stack.75.meta, bf16[32,16,128,128]{3,2,1,0:T(8,128)(2,1)} %tiles.9, bf16[4096,128]{1,0:T(8,128)(2,1)} %copy-done.4, ...), custom_call_target="tpu_custom_call" | custom-call | flops 1073741824 | bytes 16777216 | tf_op jit(solution)/shard_map/spmm/pallas_call | solution.py:158
  128.7 2.2 collective-permute-start.26
  132.4 11.1 %spmm.5 = (bf16[512,128]{1,0:T(8,128)(2,1)}, bf16[512,128]{1,0:T(8,128)(2,1)}, bf16[512,128]{1,0:T(8,128)(2,1)}, bf16[512,128]{1,0:T(8,128)(2,1)}) custom-call(s32[32,16]{1,0:T(8,128)} %copy.71.cols, s32[32]{0:T(128)} %counts.9, s32[11]{0:T(128)} %stack.75.meta, bf16[32,16,128,128]{3,2,1,0:T(8,128)(2,1)} %tiles.9, bf16[4096,128]{1,0:T(8,128)(2,1)} %copy-done.4, ...), custom_call_target="tpu_custom_call" | custom-call | flops 1073741824 | bytes 16777216 | tf_op jit(solution)/shard_map/spmm/pallas_call | solution.py:158
  143.5 2.5 collective-permute-start.29
  147.1 7.0 %dense.2 = (bf16[1024,256]{1,0:T(8,128)(2,1)}, bf16[1024,256]{1,0:T(8,128)(2,1)}, bf16[1024,256]{1,0:T(8,128)(2,1)}, bf16[1024,256]{1,0:T(8,128)(2,1)}, bf16[512...) custom-call(s32[1]{0:T(128)} %bitcast.meta, ...), custom_call_target="tpu_custom_call" | custom-call | flops 2147483648 | bytes 8388608 | tf_op jit(solution)/shard_map/dense/pallas_call | solution.py:325
  154.2 4.2 %collective-permute-done.30.refs_5_ = bf16[512,128]{1,0:T(8,128)(2,1)S(1)} collective-permute-done((bf16[512,128]{1,0:T(8,128)(2,1)}, bf16[512,128]{1,0:T(8,128)(2,1)S(1)}, u32[]{:S(2)}, u32[]{:S(2)}) %collective-permute-start.30) | collective-permute-done | bytes 131104 | tf_op jit(solution)/shard_map/ppermute | solution.py:87
  158.5 1.6 collective-permute-start.33
  160.1 2.0 collective-permute-start.34
  162.2 7.1 %dense.3 = (bf16[1024,256]{1,0:T(8,128)(2,1)}, bf16[1024,256]{1,0:T(8,128)(2,1)}, bf16[1024,256]{1,0:T(8,128)(2,1)}, bf16[1024,256]{1,0:T(8,128)(2,1)}, bf16[512...) custom-call(s32[1]{0:T(128)} %bitcast.meta, ...), custom_call_target="tpu_custom_call", output_to_operand_aliasing={{0}: (14, {}), {1}: (15, {}), {2}: (16, {}), {3}: (17, {}),... | custom-call | flops 2147483648 | bytes 8388608 | tf_op jit(solution)/shard_map/dense/pallas_call | solution.py:325
  169.3 3.2 collective-permute-done.33.refs_4_
  172.4 4.7 %convolution_convert_fusion = bf16[1024,1024]{1,0:T(8,128)(2,1)S(1)} fusion(bf16[1024,1024]{1,0:T(8,128)(2,1)} %get-tuple-element.268, bf16[1024,1024]{1,0:T(8,128)(2,1)} %get-tuple-element.269), kind=kOutput, calls=%fused_computation.1 | convolution fusion | flops 2148532224 | bytes 6291456 | tf_op jit(solution)/shard_map/dot_general | solution.py:593
  180.0 2.0 collective-permute-start.37
  182.0 4.3 %collective-permute-done.35.refs_3_ = bf16[512,128]{1,0:T(8,128)(2,1)S(1)} collective-permute-done((bf16[512,128]{1,0:T(8,128)(2,1)S(1)}, bf16[512,128]{1,0:T(8,128)(2,1)S(1)}, u32[]{:S(2)}, u32[]{:S(2)}) %collective-permute-start.35) | collective-permute-done | bytes 131104 | tf_op jit(solution)/shard_map/ppermute | solution.py:87
  186.3 6.1 %collective-permute-done.36.refs_5_ = bf16[512,128]{1,0:T(8,128)(2,1)S(1)} collective-permute-done((bf16[512,128]{1,0:T(8,128)(2,1)S(1)}, bf16[512,128]{1,0:T(8,128)(2,1)S(1)}, u32[]{:S(2)}, u32[]{:S(2)}) %collective-permute-start.36) | collective-permute-done | bytes 131104 | tf_op jit(solution)/shard_map/ppermute | solution.py:87
  192.7 2.0 collective-permute-start.43
  194.7 2.8 collective-permute-start.42
  197.6 1.5 collective-permute-start.40
  199.7 17.2 %spmm_t.2 = (bf16[4096,128]{1,0:T(8,128)(2,1)}, bf16[4096,128]{1,0:T(8,128)(2,1)}, bf16[4096,128]{1,0:T(8,128)(2,1)}, bf16[4096,128]{1,0:T(8,128)(2,1)}, bf16[40...) custom-call(s32[32,16]{1,0:T(8,128)} %copy.71.cols, s32[32]{0:T(128)} %counts.9, s32[9]{0:T(128)} %stack.84.meta, ...), custom_call_target="tpu_custom_call" | custom-call | flops 2147483648 | bytes 25165824 | tf_op jit(solution)/shard_map/spmm_t/pallas_call | solution.py:241
  217.7 2.4 collective-permute-done.45
  221.6 1.5 collective-permute-start.47
  224.0 1.5 collective-permute-start.49
  226.1 17.4 %spmm_t.3 = (bf16[4096,128]{1,0:T(8,128)(2,1)}, bf16[4096,128]{1,0:T(8,128)(2,1)}, bf16[4096,128]{1,0:T(8,128)(2,1)}, bf16[4096,128]{1,0:T(8,128)(2,1)}, bf16[40...) custom-call(s32[32,16]{1,0:T(8,128)} %copy.71.cols, s32[32]{0:T(128)} %counts.9, s32[9]{0:T(128)} %stack.84.meta, ...), custom_call_target="tpu_custom_call" | custom-call | flops 2147483648 | bytes 25165824 | tf_op jit(solution)/shard_map/spmm_t/pallas_call | solution.py:241
  247.6 6.9 %step_sums.2 = (bf16[4096,128]{1,0:T(8,128)(2,1)}, bf16[4096,128]{1,0:T(8,128)(2,1)}) custom-call(bf16[4096,128]{1,0:T(8,128)(2,1)} %get-tuple-element.321.own_up, bf16[12288,128]{1,0:T(8,128)(2,1)} %copy-done.3, bf16[2048,128]{1,0:T(8,128)(2,1)} %copy-done.27, bf16[4096,128]{1,0:T(8,128)(2,1)} %get-tuple-element.324.own_down, bf16[12288,128]{1,0:T(8,128)(2,1)} %copy-done.3, ...), custom_call_target="tpu_custom_call" | custom-call | flops 2097152 | bytes 7340032 | tf_op jit(solution)/shard_map/step_sums/pallas_call | solution.py:390
  254.5 1.5 collective-permute-start.54
  257.7 2.0 collective-permute-start.51
  259.7 1.9 collective-permute-start.52
  262.0 1.6 add_convert_fusion.1
  271.4 9.4 %collective-permute-done.54 = bf16[4096,128]{1,0:T(8,128)(2,1)} collective-permute-done((bf16[4096,128]{1,0:T(8,128)(2,1)}, bf16[4096,128]{1,0:T(8,128)(2,1)}, u32[]{:S(2)}, u32[]{:S(2)}) %collective-permute-start.54) | collective-permute-done | bytes 1048608 | tf_op jit(solution)/shard_map/ppermute | solution.py:38
  282.3 9.2 %collective-permute-done.58.up = bf16[2048,128]{1,0:T(8,128)(2,1)} collective-permute-done((bf16[2048,128]{1,0:T(8,128)(2,1)}, bf16[2048,128]{1,0:T(8,128)(2,1)}, u32[]{:S(2)}, u32[]{:S(2)}) %collective-permute-start.58) | collective-permute-done | bytes 524320 | tf_op jit(solution)/shard_map/ppermute | solution.py:38
  293.5 6.8 %step_sums.3 = (bf16[4096,128]{1,0:T(8,128)(2,1)}, bf16[4096,128]{1,0:T(8,128)(2,1)}) custom-call(bf16[4096,128]{1,0:T(8,128)(2,1)} %get-tuple-element.317.own_up, bf16[12288,128]{1,0:T(8,128)(2,1)} %copy-done.2, bf16[2048,128]{1,0:T(8,128)(2,1)} %collective-permute-done.58.up, bf16[4096,128]{1,0:T(8,128)(2,1)} %get-tuple-element.336.own_down, ...), custom_call_target="tpu_custom_call" | custom-call | flops 2097152 | bytes 7340032 | tf_op jit(solution)/shard_map/step_sums/pallas_call | solution.py:390
  303.4 2.7 collective-permute-start.61
  306.1 3.4 add_convert_fusion.refs_0_
  310.3 16.7 %collective-permute-done.61 = bf16[1024,256]{1,0:T(8,128)(2,1)} collective-permute-done((bf16[1024,256]{1,0:T(8,128)(2,1)S(1)}, bf16[1024,256]{1,0:T(8,128)(2,1)}, u32[]{:S(2)}, u32[]{:S(2)}) %collective-permute-start.61) | collective-permute-done | bytes 524320 | tf_op jit(solution)/shard_map/ppermute | solution.py:87
  330.3 7.4 %feature_grad.1 = bf16[4096,256]{1,0:T(8,128)(2,1)} custom-call(bf16[4096,128]{1,0:T(8,128)(2,1)} %add_convert_fusion.refs_0_, bf16[4096,128]{1,0:T(8,128)(2,1)} %get-tuple-element.346.refs_1_, bf16[12288,128]{1,0:T(8,128)(2,1)} %copy-done.2, bf16[4096,128]{1,0:T(8,128)(2,1)} %collective-permute-done.63.refs_3_, ...), custom_call_target="tpu_custom_call" | custom-call | flops 2097152 | bytes 7340032 | tf_op jit(solution)/shard_map/feature_grad/pallas_call | solution.py:426
  (262 shorter events, 64.4 us)
Async XLA Ops:
  7.2 139.9 %all-gather.2.cloned.1.call-start = ((), (), s32[]{:S(2)}) async-start(), calls=%async_computation | async-start | bytes 2359296 | tf_op jit(solution)/shard_map/all_gather | solution.py:569
  7.2 56.3 %collective-permute-start.6 = (bf16[4096,256]{1,0:T(8,128)(2,1)}, bf16[4096,256]{1,0:T(8,128)(2,1)}, u32[]{:S(2)}, u32[]{:S(2)}) collective-permute-start(bf16[4096,256]{1,0:T(8,128)(2,1)} %param.58), channel_id=1, source_target_pairs={{0,4},{4,0},{8,12},{12,8},{16,20},{20,16},{24,28},{28,24},{1,5},{5... | collective-permute-start | bytes 6291464 | tf_op jit(solution)/shard_map/ppermute | solution.py:41
  9.4 26.5 %collective-permute-start = (bf16[4096,128]{1,0:T(8,128)(2,1)S(1)}, bf16[4096,128]{1,0:T(8,128)(2,1)}, u32[]{:S(2)}, u32[]{:S(2)}) collective-permute-start(bf16[4096,128]{1,0:T(8,128)(2,1)S(1)} %get-tuple-element.371.refs_0_), channel_id=1, source_target_pairs={{0,8},{4,12},{8,24},{12,28},{24,16},{28,20},{16,0},{20,4},{1,9},{5... | collective-permute-start | bytes 3145736 | tf_op jit(solution)/shard_map/ppermute | solution.py:38
  12.0 25.4 %collective-permute-start.1 = (bf16[4096,128]{1,0:T(8,128)(2,1)S(1)}, bf16[4096,128]{1,0:T(8,128)(2,1)}, u32[]{:S(2)}, u32[]{:S(2)}) collective-permute-start(bf16[4096,128]{1,0:T(8,128)(2,1)S(1)} %get-tuple-element.371.refs_0_), channel_id=1, source_target_pairs={{0,16},{4,20},{8,0},{12,4},{24,8},{28,12},{16,24},{20,28},{1,17},{... | collective-permute-start | bytes 3145736 | tf_op jit(solution)/shard_map/ppermute | solution.py:38
  15.0 22.9 %collective-permute-start.4 = (bf16[1024,256]{1,0:T(8,128)(2,1)}, bf16[1024,256]{1,0:T(8,128)(2,1)S(1)}, u32[]{:S(2)}, u32[]{:S(2)}) collective-permute-start(bf16[1024,256]{1,0:T(8,128)(2,1)} %get-tuple-element.365), channel_id=1, source_target_pairs={{0,3},{1,0},{2,1},{3,2},{4,7},{5,4},{6,5},{7,6},{8,11},{9,8},{10,9... | collective-permute-start | bytes 1572872 | tf_op jit(solution)/shard_map/ppermute | solution.py:87
  19.1 23.9 %collective-permute-start.5 = (bf16[1024,256]{1,0:T(8,128)(2,1)}, bf16[1024,256]{1,0:T(8,128)(2,1)}, u32[]{:S(2)}, u32[]{:S(2)}) collective-permute-start(bf16[1024,256]{1,0:T(8,128)(2,1)} %get-tuple-element.367), channel_id=1, source_target_pairs={{0,1},{1,2},{2,3},{3,0},{4,5},{5,6},{6,7},{7,4},{8,9},{9,10},{10,1... | collective-permute-start | bytes 1572872 | tf_op jit(solution)/shard_map/ppermute | solution.py:87
  37.4 28.3 %collective-permute-start.13 = (bf16[4096,128]{1,0:T(8,128)(2,1)}, bf16[4096,128]{1,0:T(8,128)(2,1)}, u32[]{:S(2)}, u32[]{:S(2)}) collective-permute-start(bf16[4096,128]{1,0:T(8,128)(2,1)} %collective-permute-done.refs_1_), channel_id=1, source_target_pairs={{0,4},{4,0},{8,12},{12,8},{16,20},{20,16},{24,28},{28,24},{1,5},{5... | collective-permute-start | bytes 3145736 | tf_op jit(solution)/shard_map/ppermute | solution.py:41
  37.4 28.4 %collective-permute-start.14 = (bf16[4096,128]{1,0:T(8,128)(2,1)}, bf16[4096,128]{1,0:T(8,128)(2,1)}, u32[]{:S(2)}, u32[]{:S(2)}) collective-permute-start(bf16[4096,128]{1,0:T(8,128)(2,1)} %collective-permute-done.1.refs_2_), channel_id=1, source_target_pairs={{0,4},{4,0},{8,12},{12,8},{16,20},{20,16},{24,28},{28,24},{1,5},{5... | collective-permute-start | bytes 3145736 | tf_op jit(solution)/shard_map/ppermute | solution.py:41
  48.1 15.3 %collective-permute-start.2 = (bf16[2048,128]{1,0:T(8,128)(2,1)S(1)}, bf16[2048,128]{1,0:T(8,128)(2,1)S(1)}, u32[]{:S(2)}, u32[]{:S(2)}) collective-permute-start(bf16[2048,128]{1,0:T(8,128)(2,1)S(1)} %slice.78), channel_id=1, source_target_pairs={{0,8},{4,12},{8,24},{12,28},{24,16},{28,20},{16,0},{20,4},{1,9},{5... | collective-permute-start | bytes 1572872 | tf_op jit(solution)/shard_map/ppermute | solution.py:38
  50.6 13.0 %collective-permute-start.3 = (bf16[2048,128]{1,0:T(8,128)(2,1)S(1)}, bf16[2048,128]{1,0:T(8,128)(2,1)}, u32[]{:S(2)}, u32[]{:S(2)}) collective-permute-start(bf16[2048,128]{1,0:T(8,128)(2,1)S(1)} %slice.79), channel_id=1, source_target_pairs={{0,16},{4,20},{8,0},{12,4},{24,8},{28,12},{16,24},{20,28},{1,17},{... | collective-permute-start | bytes 1572872 | tf_op jit(solution)/shard_map/ppermute | solution.py:38
  63.6 28.1 %collective-permute-start.11 = (bf16[4096,128]{1,0:T(8,128)(2,1)S(1)}, bf16[4096,128]{1,0:T(8,128)(2,1)S(1)}, u32[]{:S(2)}, u32[]{:S(2)}) collective-permute-start(bf16[4096,128]{1,0:T(8,128)(2,1)S(1)} %get-tuple-element.181.refs_0_), channel_id=1, source_target_pairs={{0,8},{4,12},{8,24},{12,28},{24,16},{28,20},{16,0},{20,4},{1,9},{5... | collective-permute-start | bytes 3145736 | tf_op jit(solution)/shard_map/ppermute | solution.py:38
  65.1 26.6 %collective-permute-start.12 = (bf16[4096,128]{1,0:T(8,128)(2,1)S(1)}, bf16[4096,128]{1,0:T(8,128)(2,1)S(1)}, u32[]{:S(2)}, u32[]{:S(2)}) collective-permute-start(bf16[4096,128]{1,0:T(8,128)(2,1)S(1)} %get-tuple-element.181.refs_0_), channel_id=1, source_target_pairs={{0,16},{4,20},{8,0},{12,4},{24,8},{28,12},{16,24},{20,28},{1,17},{... | collective-permute-start | bytes 3145736 | tf_op jit(solution)/shard_map/ppermute | solution.py:38
  65.8 25.9 %collective-permute-start.10 = (bf16[1024,256]{1,0:T(8,128)(2,1)}, bf16[1024,256]{1,0:T(8,128)(2,1)S(1)}, u32[]{:S(2)}, u32[]{:S(2)}) collective-permute-start(bf16[1024,256]{1,0:T(8,128)(2,1)} %get-tuple-element.180), channel_id=1, source_target_pairs={{0,2},{1,3},{2,0},{3,1},{4,6},{5,7},{6,4},{7,5},{8,10},{9,11},{10,... | collective-permute-start | bytes 1572872 | tf_op jit(solution)/shard_map/ppermute | solution.py:87
  95.0 14.2 %collective-permute-start.17 = (bf16[2048,128]{1,0:T(8,128)(2,1)}, bf16[2048,128]{1,0:T(8,128)(2,1)S(1)}, u32[]{:S(2)}, u32[]{:S(2)}) collective-permute-start(bf16[2048,128]{1,0:T(8,128)(2,1)} %slice.82), channel_id=1, source_target_pairs={{0,8},{4,12},{8,24},{12,28},{24,16},{28,20},{16,0},{20,4},{1,9},{5... | collective-permute-start | bytes 1572872 | tf_op jit(solution)/shard_map/ppermute | solution.py:38
  96.5 14.0 %collective-permute-start.18 = (bf16[2048,128]{1,0:T(8,128)(2,1)}, bf16[2048,128]{1,0:T(8,128)(2,1)S(1)}, u32[]{:S(2)}, u32[]{:S(2)}) collective-permute-start(bf16[2048,128]{1,0:T(8,128)(2,1)} %slice.83), channel_id=1, source_target_pairs={{0,16},{4,20},{8,0},{12,4},{24,8},{28,12},{16,24},{20,28},{1,17},{... | collective-permute-start | bytes 1572872 | tf_op jit(solution)/shard_map/ppermute | solution.py:38
  98.2 12.3 %collective-permute-start.22 = (bf16[1024,128]{1,0:T(8,128)(2,1)}, bf16[1024,128]{1,0:T(8,128)(2,1)S(1)}, u32[]{:S(2)}, u32[]{:S(2)}) collective-permute-start(bf16[1024,128]{1,0:T(8,128)(2,1)} %get-tuple-element.194), channel_id=1, source_target_pairs={{0,1},{1,2},{2,3},{3,0},{4,5},{5,6},{6,7},{7,4},{8,9},{9,10},{10,1... | collective-permute-start | bytes 786440 | tf_op jit(solution)/shard_map/ppermute | solution.py:87
  98.2 14.2 %collective-permute-start.21 = (bf16[1024,128]{1,0:T(8,128)(2,1)}, bf16[1024,128]{1,0:T(8,128)(2,1)}, u32[]{:S(2)}, u32[]{:S(2)}) collective-permute-start(bf16[1024,128]{1,0:T(8,128)(2,1)} %get-tuple-element.192), channel_id=1, source_target_pairs={{0,3},{1,0},{2,1},{3,2},{4,7},{5,4},{6,5},{7,6},{8,11},{9,8},{10,9... | collective-permute-start | bytes 786440 | tf_op jit(solution)/shard_map/ppermute | solution.py:87
  113.0 15.0 %collective-permute-start.23 = (bf16[1024,128]{1,0:T(8,128)(2,1)}, bf16[1024,128]{1,0:T(8,128)(2,1)S(1)}, u32[]{:S(2)}, u32[]{:S(2)}) collective-permute-start(bf16[1024,128]{1,0:T(8,128)(2,1)} %get-tuple-element.196), channel_id=1, source_target_pairs={{0,2},{1,3},{2,0},{3,1},{4,6},{5,7},{6,4},{7,5},{8,10},{9,11},{10,... | collective-permute-start | bytes 786440 | tf_op jit(solution)/shard_map/ppermute | solution.py:87
  128.7 14.7 %collective-permute-start.26 = (bf16[512,128]{1,0:T(8,128)(2,1)}, bf16[512,128]{1,0:T(8,128)(2,1)S(1)}, u32[]{:S(2)}, u32[]{:S(2)}) collective-permute-start(bf16[512,128]{1,0:T(8,128)(2,1)} %get-tuple-element.202), channel_id=1, source_target_pairs={{0,3},{1,0},{2,1},{3,2},{4,7},{5,4},{6,5},{7,6},{8,11},{9,8},{10,9... | collective-permute-start | bytes 393224 | tf_op jit(solution)/shard_map/ppermute | solution.py:87
  130.9 12.5 %collective-permute-start.27 = (bf16[512,128]{1,0:T(8,128)(2,1)}, bf16[512,128]{1,0:T(8,128)(2,1)S(1)}, u32[]{:S(2)}, u32[]{:S(2)}) collective-permute-start(bf16[512,128]{1,0:T(8,128)(2,1)} %get-tuple-element.203), channel_id=1, source_target_pairs={{0,2},{1,3},{2,0},{3,1},{4,6},{5,7},{6,4},{7,5},{8,10},{9,11},{10,... | collective-permute-start | bytes 393224 | tf_op jit(solution)/shard_map/ppermute | solution.py:87
  130.9 12.6 %collective-permute-start.28 = (bf16[512,128]{1,0:T(8,128)(2,1)}, bf16[512,128]{1,0:T(8,128)(2,1)S(1)}, u32[]{:S(2)}, u32[]{:S(2)}) collective-permute-start(bf16[512,128]{1,0:T(8,128)(2,1)} %get-tuple-element.204), channel_id=1, source_target_pairs={{0,1},{1,2},{2,3},{3,0},{4,5},{5,6},{6,7},{7,4},{8,9},{9,10},{10,1... | collective-permute-start | bytes 393224 | tf_op jit(solution)/shard_map/ppermute | solution.py:87
  146.0 12.5 %collective-permute-start.30 = (bf16[512,128]{1,0:T(8,128)(2,1)}, bf16[512,128]{1,0:T(8,128)(2,1)S(1)}, u32[]{:S(2)}, u32[]{:S(2)}) collective-permute-start(bf16[512,128]{1,0:T(8,128)(2,1)} %get-tuple-element.210), channel_id=1, source_target_pairs={{0,2},{1,3},{2,0},{3,1},{4,6},{5,7},{6,4},{7,5},{8,10},{9,11},{10,... | collective-permute-start | bytes 393224 | tf_op jit(solution)/shard_map/ppermute | solution.py:87
  147.1 11.4 %collective-permute-start.31 = (bf16[512,128]{1,0:T(8,128)(2,1)}, bf16[512,128]{1,0:T(8,128)(2,1)S(1)}, u32[]{:S(2)}, u32[]{:S(2)}) collective-permute-start(bf16[512,128]{1,0:T(8,128)(2,1)} %get-tuple-element.211), channel_id=1, source_target_pairs={{0,1},{1,2},{2,3},{3,0},{4,5},{5,6},{6,7},{7,4},{8,9},{9,10},{10,1... | collective-permute-start | bytes 393224 | tf_op jit(solution)/shard_map/ppermute | solution.py:87
  158.5 13.9 %collective-permute-start.33 = (bf16[512,128]{1,0:T(8,128)(2,1)}, bf16[512,128]{1,0:T(8,128)(2,1)S(1)}, u32[]{:S(2)}, u32[]{:S(2)}) collective-permute-start(bf16[512,128]{1,0:T(8,128)(2,1)} %get-tuple-element.233), channel_id=1, source_target_pairs={{0,2},{1,3},{2,0},{3,1},{4,6},{5,7},{6,4},{7,5},{8,10},{9,11},{10,... | collective-permute-start | bytes 393224 | tf_op jit(solution)/shard_map/ppermute | solution.py:87
  160.1 12.3 %collective-permute-start.34 = (bf16[512,128]{1,0:T(8,128)(2,1)}, bf16[512,128]{1,0:T(8,128)(2,1)S(1)}, u32[]{:S(2)}, u32[]{:S(2)}) collective-permute-start(bf16[512,128]{1,0:T(8,128)(2,1)} %get-tuple-element.234), channel_id=1, source_target_pairs={{0,1},{1,2},{2,3},{3,0},{4,5},{5,6},{6,7},{7,4},{8,9},{9,10},{10,1... | collective-permute-start | bytes 393224 | tf_op jit(solution)/shard_map/ppermute | solution.py:87
  179.1 13.3 %collective-permute-start.39 = (bf16[384,1024]{1,0:T(8,128)(2,1)S(1)}, bf16[384,1024]{1,0:T(8,128)(2,1)S(1)}, u32[]{:S(2)}, u32[]{:S(2)}) collective-permute-start(bf16[384,1024]{1,0:T(8,128)(2,1)S(1)} %pad_maximum_fusion), channel_id=1, source_target_pairs={{0,4},{4,0},{8,12},{12,8},{16,20},{20,16},{24,28},{28,24},{1,5},{5... | collective-permute-start | bytes 2359304 | tf_op jit(solution)/shard_map/ppermute | solution.py:41
  179.2 13.2 %collective-permute-start.36 = (bf16[512,128]{1,0:T(8,128)(2,1)S(1)}, bf16[512,128]{1,0:T(8,128)(2,1)S(1)}, u32[]{:S(2)}, u32[]{:S(2)}) collective-permute-start(bf16[512,128]{1,0:T(8,128)(2,1)S(1)} %copy-done.66), channel_id=1, source_target_pairs={{0,2},{1,3},{2,0},{3,1},{4,6},{5,7},{6,4},{7,5},{8,10},{9,11},{10,... | collective-permute-start | bytes 393224 | tf_op jit(solution)/shard_map/ppermute | solution.py:87
  180.0 12.4 %collective-permute-start.37 = (bf16[512,128]{1,0:T(8,128)(2,1)S(1)}, bf16[512,128]{1,0:T(8,128)(2,1)S(1)}, u32[]{:S(2)}, u32[]{:S(2)}) collective-permute-start(bf16[512,128]{1,0:T(8,128)(2,1)S(1)} %copy-done.65), channel_id=1, source_target_pairs={{0,1},{1,2},{2,3},{3,0},{4,5},{5,6},{6,7},{7,4},{8,9},{9,10},{10,1... | collective-permute-start | bytes 393224 | tf_op jit(solution)/shard_map/ppermute | solution.py:87
  192.4 24.6 %collective-permute-start.44 = (bf16[1024,128]{1,0:T(8,128)(2,1)S(1)}, bf16[1024,128]{1,0:T(8,128)(2,1)S(1)}, u32[]{:S(2)}, u32[]{:S(2)}) collective-permute-start(bf16[1024,128]{1,0:T(8,128)(2,1)S(1)} %copy-done.39), channel_id=1, source_target_pairs={{0,1},{1,2},{2,3},{3,0},{4,5},{5,6},{6,7},{7,4},{8,9},{9,10},{10,1... | collective-permute-start | bytes 786440 | tf_op jit(solution)/shard_map/ppermute | solution.py:87
  192.7 24.3 %collective-permute-start.43 = (bf16[1024,128]{1,0:T(8,128)(2,1)S(1)}, bf16[1024,128]{1,0:T(8,128)(2,1)S(1)}, u32[]{:S(2)}, u32[]{:S(2)}) collective-permute-start(bf16[1024,128]{1,0:T(8,128)(2,1)S(1)} %copy-done.40), channel_id=1, source_target_pairs={{0,2},{1,3},{2,0},{3,1},{4,6},{5,7},{6,4},{7,5},{8,10},{9,11},{10,... | collective-permute-start | bytes 786440 | tf_op jit(solution)/shard_map/ppermute | solution.py:87
  194.7 22.3 %collective-permute-start.42 = (bf16[1024,128]{1,0:T(8,128)(2,1)S(1)}, bf16[1024,128]{1,0:T(8,128)(2,1)S(1)}, u32[]{:S(2)}, u32[]{:S(2)}) collective-permute-start(bf16[1024,128]{1,0:T(8,128)(2,1)S(1)} %copy-done.41), channel_id=1, source_target_pairs={{0,3},{1,0},{2,1},{3,2},{4,7},{5,4},{6,5},{7,6},{8,11},{9,8},{10,9... | collective-permute-start | bytes 786440 | tf_op jit(solution)/shard_map/ppermute | solution.py:87
  197.6 19.3 %collective-permute-start.40 = (bf16[64,1024]{1,0:T(8,128)(2,1)S(1)}, bf16[64,1024]{1,0:T(8,128)(2,1)S(1)}, u32[]{:S(2)}, u32[]{:S(2)}) collective-permute-start(bf16[64,1024]{1,0:T(8,128)(2,1)S(1)} %get-tuple-element.375), channel_id=1, source_target_pairs={{0,8},{4,12},{8,24},{12,28},{24,16},{28,20},{16,0},{20,4},{1,9},{5... | collective-permute-start | bytes 393224 | tf_op jit(solution)/shard_map/ppermute | solution.py:38
  199.2 17.8 %collective-permute-start.41 = (bf16[64,1024]{1,0:T(8,128)(2,1)S(1)}, bf16[64,1024]{1,0:T(8,128)(2,1)S(1)}, u32[]{:S(2)}, u32[]{:S(2)}) collective-permute-start(bf16[64,1024]{1,0:T(8,128)(2,1)S(1)} %get-tuple-element.374), channel_id=1, source_target_pairs={{0,16},{4,20},{8,0},{12,4},{24,8},{28,12},{16,24},{20,28},{1,17},{... | collective-permute-start | bytes 393224 | tf_op jit(solution)/shard_map/ppermute | solution.py:38
  220.0 23.5 %collective-permute-start.46 = (bf16[12288,128]{1,0:T(8,128)(2,1)}, bf16[12288,128]{1,0:T(8,128)(2,1)S(1)}, u32[]{:S(2)}, u32[]{:S(2)}) collective-permute-start(bf16[12288,128]{1,0:T(8,128)(2,1)} %get-tuple-element.296), channel_id=1, source_target_pairs={{0,4},{4,0},{8,12},{12,8},{16,20},{20,16},{24,28},{28,24},{1,5},{5... | collective-permute-start | bytes 9437192 | tf_op jit(solution)/shard_map/ppermute | solution.py:41
  221.6 21.8 %collective-permute-start.47 = (bf16[2048,128]{1,0:T(8,128)(2,1)S(1)}, bf16[2048,128]{1,0:T(8,128)(2,1)S(1)}, u32[]{:S(2)}, u32[]{:S(2)}) collective-permute-start(bf16[2048,128]{1,0:T(8,128)(2,1)S(1)} %get-tuple-element.355), channel_id=1, source_target_pairs={{0,8},{4,12},{8,24},{12,28},{24,16},{28,20},{16,0},{20,4},{1,9},{5... | collective-permute-start | bytes 1572872 | tf_op jit(solution)/shard_map/ppermute | solution.py:38
  223.2 20.3 %collective-permute-start.48 = (bf16[2048,128]{1,0:T(8,128)(2,1)S(1)}, bf16[2048,128]{1,0:T(8,128)(2,1)S(1)}, u32[]{:S(2)}, u32[]{:S(2)}) collective-permute-start(bf16[2048,128]{1,0:T(8,128)(2,1)S(1)} %get-tuple-element.354), channel_id=1, source_target_pairs={{0,16},{4,20},{8,0},{12,4},{24,8},{28,12},{16,24},{20,28},{1,17},{... | collective-permute-start | bytes 1572872 | tf_op jit(solution)/shard_map/ppermute | solution.py:38
  224.0 19.4 %collective-permute-start.49 = (bf16[128,1024]{1,0:T(8,128)(2,1)S(1)}, bf16[128,1024]{1,0:T(8,128)(2,1)S(1)}, u32[]{:S(2)}, u32[]{:S(2)}) collective-permute-start(bf16[128,1024]{1,0:T(8,128)(2,1)S(1)} %get-tuple-element.373), channel_id=1, source_target_pairs={{0,8},{4,12},{8,24},{12,28},{24,16},{28,20},{16,0},{20,4},{1,9},{5... | collective-permute-start | bytes 786440 | tf_op jit(solution)/shard_map/ppermute | solution.py:38
  225.5 17.9 %collective-permute-start.50 = (bf16[128,1024]{1,0:T(8,128)(2,1)S(1)}, bf16[128,1024]{1,0:T(8,128)(2,1)S(1)}, u32[]{:S(2)}, u32[]{:S(2)}) collective-permute-start(bf16[128,1024]{1,0:T(8,128)(2,1)S(1)} %get-tuple-element.372), channel_id=1, source_target_pairs={{0,16},{4,20},{8,0},{12,4},{24,8},{28,12},{16,24},{20,28},{1,17},{... | collective-permute-start | bytes 786440 | tf_op jit(solution)/shard_map/ppermute | solution.py:38
  247.4 14.2 %collective-permute-start.57 = (bf16[12288,128]{1,0:T(8,128)(2,1)}, bf16[12288,128]{1,0:T(8,128)(2,1)S(1)}, u32[]{:S(2)}, u32[]{:S(2)}) collective-permute-start(bf16[12288,128]{1,0:T(8,128)(2,1)} %get-tuple-element.330), channel_id=1, source_target_pairs={{0,4},{4,0},{8,12},{12,8},{16,20},{20,16},{24,28},{28,24},{1,5},{5... | collective-permute-start | bytes 9437192 | tf_op jit(solution)/shard_map/ppermute | solution.py:41
  254.5 26.4 %collective-permute-start.54 = (bf16[4096,128]{1,0:T(8,128)(2,1)}, bf16[4096,128]{1,0:T(8,128)(2,1)}, u32[]{:S(2)}, u32[]{:S(2)}) collective-permute-start(bf16[4096,128]{1,0:T(8,128)(2,1)} %get-tuple-element.326), channel_id=1, source_target_pairs={{0,8},{4,12},{8,24},{12,28},{24,16},{28,20},{16,0},{20,4},{1,9},{5... | collective-permute-start | bytes 3145736 | tf_op jit(solution)/shard_map/ppermute | solution.py:38
  256.0 26.3 %collective-permute-start.55 = (bf16[4096,128]{1,0:T(8,128)(2,1)}, bf16[4096,128]{1,0:T(8,128)(2,1)}, u32[]{:S(2)}, u32[]{:S(2)}) collective-permute-start(bf16[4096,128]{1,0:T(8,128)(2,1)} %get-tuple-element.327), channel_id=1, source_target_pairs={{0,16},{4,20},{8,0},{12,4},{24,8},{28,12},{16,24},{20,28},{1,17},{... | collective-permute-start | bytes 3145736 | tf_op jit(solution)/shard_map/ppermute | solution.py:38
  264.2 27.3 %collective-permute-start.58 = (bf16[2048,128]{1,0:T(8,128)(2,1)}, bf16[2048,128]{1,0:T(8,128)(2,1)}, u32[]{:S(2)}, u32[]{:S(2)}) collective-permute-start(bf16[2048,128]{1,0:T(8,128)(2,1)} %get-tuple-element.353), channel_id=1, source_target_pairs={{0,8},{4,12},{8,24},{12,28},{24,16},{28,20},{16,0},{20,4},{1,9},{5... | collective-permute-start | bytes 1572872 | tf_op jit(solution)/shard_map/ppermute | solution.py:38
  265.7 27.0 %collective-permute-start.59 = (bf16[2048,128]{1,0:T(8,128)(2,1)}, bf16[2048,128]{1,0:T(8,128)(2,1)}, u32[]{:S(2)}, u32[]{:S(2)}) collective-permute-start(bf16[2048,128]{1,0:T(8,128)(2,1)} %get-tuple-element.352), channel_id=1, source_target_pairs={{0,16},{4,20},{8,0},{12,4},{24,8},{28,12},{16,24},{20,28},{1,17},{... | collective-permute-start | bytes 1572872 | tf_op jit(solution)/shard_map/ppermute | solution.py:38
  267.6 25.9 %collective-permute-start.60 = (bf16[1024,256]{1,0:T(8,128)(2,1)}, bf16[1024,256]{1,0:T(8,128)(2,1)}, u32[]{:S(2)}, u32[]{:S(2)}) collective-permute-start(bf16[1024,256]{1,0:T(8,128)(2,1)} %get-tuple-element.333), channel_id=1, source_target_pairs={{0,2},{1,3},{2,0},{3,1},{4,6},{5,7},{6,4},{7,5},{8,10},{9,11},{10,... | collective-permute-start | bytes 1572872 | tf_op jit(solution)/shard_map/ppermute | solution.py:87
  300.3 30.0 %collective-permute-start.63 = (bf16[4096,128]{1,0:T(8,128)(2,1)}, bf16[4096,128]{1,0:T(8,128)(2,1)}, u32[]{:S(2)}, u32[]{:S(2)}) collective-permute-start(bf16[4096,128]{1,0:T(8,128)(2,1)} %get-tuple-element.338), channel_id=1, source_target_pairs={{0,8},{4,12},{8,24},{12,28},{24,16},{28,20},{16,0},{20,4},{1,9},{5... | collective-permute-start | bytes 3145736 | tf_op jit(solution)/shard_map/ppermute | solution.py:38
  301.7 28.5 %collective-permute-start.64 = (bf16[4096,128]{1,0:T(8,128)(2,1)}, bf16[4096,128]{1,0:T(8,128)(2,1)}, u32[]{:S(2)}, u32[]{:S(2)}) collective-permute-start(bf16[4096,128]{1,0:T(8,128)(2,1)} %get-tuple-element.347), channel_id=1, source_target_pairs={{0,16},{4,20},{8,0},{12,4},{24,8},{28,12},{16,24},{20,28},{1,17},{... | collective-permute-start | bytes 3145736 | tf_op jit(solution)/shard_map/ppermute | solution.py:38
  302.3 26.8 %collective-permute-start.62 = (bf16[1024,256]{1,0:T(8,128)(2,1)S(1)}, bf16[1024,256]{1,0:T(8,128)(2,1)}, u32[]{:S(2)}, u32[]{:S(2)}) collective-permute-start(bf16[1024,256]{1,0:T(8,128)(2,1)S(1)} %copy-done.29), channel_id=1, source_target_pairs={{0,1},{1,2},{2,3},{3,0},{4,5},{5,6},{6,7},{7,4},{8,9},{9,10},{10,1... | collective-permute-start | bytes 1572872 | tf_op jit(solution)/shard_map/ppermute | solution.py:87
  303.4 23.6 %collective-permute-start.61 = (bf16[1024,256]{1,0:T(8,128)(2,1)S(1)}, bf16[1024,256]{1,0:T(8,128)(2,1)}, u32[]{:S(2)}, u32[]{:S(2)}) collective-permute-start(bf16[1024,256]{1,0:T(8,128)(2,1)S(1)} %copy-done.30), channel_id=1, source_target_pairs={{0,3},{1,0},{2,1},{3,2},{4,7},{5,4},{6,5},{7,6},{8,11},{9,8},{10,9... | collective-permute-start | bytes 1572872 | tf_op jit(solution)/shard_map/ppermute | solution.py:87
  (86 other events, 853.5 us)
Sparse Core Ops, SparseCore 0:
  112.5 28.2 all-gather.1

commit v7 on v5

--- a/solution.py
+++ b/solution.py
@@ -264,97 +264,212 @@
     )(columns, counts, meta, tiles, *grads)
 
 
-def dense_kernel(parts, chunks, n_earlier, meta, *refs):
+def dense_kernel(parts, chunks, n_earlier, is_first, is_last, meta, *refs):
     n_mixed = parts * chunks
     mixed_refs, cot_refs, w_hbm = refs[:n_mixed], refs[n_mixed : n_mixed + parts], refs[n_mixed + parts]
-    outs = refs[n_mixed + parts + 1 + n_earlier :]
+    refs = refs[n_mixed + parts + 1 :]
+    if not is_first:
+        sums_hbm, refs = refs[0], refs[1:]
+    outs = refs[n_earlier:]
     act_outs, mg_outs = outs[:parts], outs[parts : parts + n_mixed]
-    mixed_out, grad_out, weight, sems = outs[parts + n_mixed :]
+    sums_out, weight, sums, sems, sums_sem = outs[parts + n_mixed :]
     f_wide, h_wide = weight.shape[0] // parts, weight.shape[1] // parts
     width = f_wide // chunks
     me = meta[0]
+    t = pl.program_id(0)
 
     def place(u):
         return lax.rem(me + u, parts)
 
-    @pl.when(pl.program_id(0) == 0)
+    @pl.when(t == 0)
     def _():
         copies = []
         for i in range(parts):
             for j in range(parts):
-                src = w_hbm.at[aligned(place(i) * f_wide, f_wide, f_wide), aligned(place(j) * h_wide, h_wide, h_wide)]
+                src = w_hbm.at[place(j), aligned(place(i) * f_wide, f_wide, f_wide)]
                 dst = weight.at[pl.ds(i * f_wide, f_wide), pl.ds(j * h_wide, h_wide)]
                 copies.append(pltpu.make_async_copy(src, dst, sems.at[i * parts + j]))
                 copies[-1].start()
         for copy in copies:
             copy.wait()
+        if is_first:
+            sums[...] = jnp.zeros_like(sums)
+        else:
+            load = pltpu.make_async_copy(sums_hbm, sums, sums_sem)
+            load.start()
+            load.wait()
 
     mixed = jnp.concatenate([ref[...] for ref in mixed_refs], axis=1)
-    for u in range(parts):
-        at = pl.ds(pl.multiple_of(place(u) * f_wide, f_wide), f_wide)
-        mixed_out[:, at] = mixed[:, u * f_wide : (u + 1) * f_wide]
     grads = []
     for u in range(parts):
         preact = jnp.dot(mixed, weight[:, u * h_wide : (u + 1) * h_wide], preferred_element_type=F32)
         sig = jax.nn.sigmoid(preact)
         act_outs[u][...] = (preact * sig).astype(BF16)
         grads.append((cot_refs[u][...].astype(F32) * sig * (1.0 + preact * (1.0 - sig))).astype(BF16))
-        at = pl.ds(pl.multiple_of(place(u) * h_wide, h_wide), h_wide)
-        grad_out[:, at] = grads[u]
     grad = jnp.concatenate(grads, axis=1)
     back = lax.dot_general(grad, weight[...], (((1,), (1,)), ((), ())), preferred_element_type=F32).astype(BF16)
     for i in range(n_mixed):
         mg_outs[i][...] = back[:, i * width : (i + 1) * width]
+    for u in range(parts):
+        sums[u * h_wide : (u + 1) * h_wide, :] += lax.dot_general(
+            grads[u], mixed, (((0,), (0,)), ((), ())), preferred_element_type=F32
+        )
+
+    @pl.when(t == pl.num_programs(0) - 1)
+    def _():
+        if is_last:
+            for u in range(parts):
+                to = aligned(place(u) * h_wide, h_wide, h_wide)
+                sums_out[to, :] = sums[u * h_wide : (u + 1) * h_wide, :].astype(BF16)
+        else:
+            store = pltpu.make_async_copy(sums, sums_out, sums_sem)
+            store.start()
+            store.wait()
 
 
 def dense(meta, mixed, cot, weight, rows, first, earlier):
     parts, chunks = len(mixed), len(mixed[0])
     width = mixed[0][0][0].shape[1]
-    features, hidden = weight.shape
-    h_wide = hidden // parts
+    _, features, h_wide = weight.shape
+    hidden = parts * h_wide
     all_rows = cot[0].shape[0]
     step = min(rows, 256)
     flat = [m for row in mixed for m in row]
-    earlier = list(earlier)
+    earlier_whole, earlier_sums = earlier if earlier else ([], [])
+    is_first, is_last = not earlier, first + rows == all_rows
 
     def spec(w, start=0):
         return pl.BlockSpec((step, w), lambda t, meta: (t + start // step, 0))
 
     kinds = [(h_wide, True)] * parts + [(width, c > 0) for _ in range(parts) for c in range(chunks)]
-    kinds += [(features, True), (hidden, True)]
     whole_at = [i for i, (_, whole) in enumerate(kinds) if whole]
-    n_inputs = 1 + len(flat) + parts + 1
+    n_inputs = 1 + len(flat) + parts + 1 + len(earlier_sums)
+    sums_spec = pl.BlockSpec((hidden, features), lambda t, meta: (0, 0)) if is_last else any_spec()
     outs = pl.pallas_call(
-        functools.partial(dense_kernel, parts, chunks, len(earlier)),
+        functools.partial(dense_kernel, parts, chunks, len(earlier_whole), is_first, is_last),
         grid_spec=pltpu.PrefetchScalarGridSpec(
             num_scalar_prefetch=1,
             grid=(rows // step,),
             in_specs=[spec(width, at) for _, at in flat]
             + [spec(h_wide, first)] * parts
-            + [any_spec()]
-            + [any_spec()] * len(earlier),
-            out_specs=[spec(w, first if whole else 0) for w, whole in kinds],
-            scratch_shapes=[pltpu.VMEM((features, hidden), BF16), pltpu.SemaphoreType.DMA((parts * parts,))],
+            + [any_spec()] * (1 + len(earlier_sums) + len(earlier_whole)),
+            out_specs=[spec(w, first if whole else 0) for w, whole in kinds] + [sums_spec],
+            scratch_shapes=[
+                pltpu.VMEM((features, hidden), BF16),
+                pltpu.VMEM((hidden, features), F32),
+                pltpu.SemaphoreType.DMA((parts * parts,)),
+                pltpu.SemaphoreType.DMA,
+            ],
         ),
-        out_shape=[jax.ShapeDtypeStruct((all_rows if whole else rows, w), BF16) for w, whole in kinds],
+        out_shape=[jax.ShapeDtypeStruct((all_rows if whole else rows, w), BF16) for w, whole in kinds]
+        + [jax.ShapeDtypeStruct((hidden, features), BF16 if is_last else F32)],
         input_output_aliases={n_inputs + i: at for i, at in enumerate(whole_at)} if earlier else {},
         compiler_params=params(),
         cost_estimate=pl.CostEstimate(
-            flops=4 * rows * features * hidden,
-            bytes_accessed=2 * (features * hidden + 6 * rows * hidden),
+            flops=6 * rows * features * hidden,
+            bytes_accessed=2 * (3 * features * hidden + 4 * rows * hidden),
             transcendentals=rows * hidden,
         ),
         name="dense",
-    )(meta, *[m for m, _ in flat], *cot, weight, *earlier)
+    )(meta, *[m for m, _ in flat], *cot, weight, *earlier_sums, *earlier_whole)
     n = parts * chunks
     act, back = outs[:parts], outs[parts : parts + n]
     return (
         act,
         [back[u * chunks : (u + 1) * chunks] for u in range(parts)],
-        outs[-2],
         outs[-1],
-        [outs[i] for i in whole_at],
+        ([outs[i] for i in whole_at], [outs[-1]]),
     )
+
+
+def total_of(*values):
+    return functools.reduce(lambda a, b: a + b, [v.astype(F32) for v in values]).astype(BF16)
+
+
+def result_kernel(n_ready, low_blocks, *refs):
+    ready, (own, got, up_low, up_high, down_low, down_high, out) = refs[:n_ready], refs[n_ready:]
+    width = own.shape[1]
+    low = pl.program_id(0) < low_blocks
+    for c, ref in enumerate(ready):
+        out[:, c * width : (c + 1) * width] = ref[...]
+
+    def put(up, down):
+        total = own[...].astype(F32) + got[...].astype(F32) + up[...].astype(F32) + down[...].astype(F32)
+        out[:, n_ready * width :] = total.astype(BF16)
+
+    @pl.when(low)
+    def _():
+        put(up_low, down_low)
+
+    @pl.when(jnp.logical_not(low))
+    def _():
+        put(up_high, down_high)
+
+
+def result_of(ready, own, got, up, down):
+    rows, width = own.shape
+    step = min(rows // 2, 1024)
+    blocks = rows // step
+    low = blocks // 2
+    here = pl.BlockSpec((step, width), lambda t: (t, 0))
+    lower = pl.BlockSpec((step, width), lambda t: (jnp.minimum(t, low - 1), 0))
+    upper = pl.BlockSpec((step, width), lambda t: (jnp.maximum(t - low, 0), 0))
+    wide = width * (len(ready) + 1)
+    return pl.pallas_call(
+        functools.partial(result_kernel, len(ready), low),
+        grid=(blocks,),
+        in_specs=[here] * (len(ready) + 2) + [lower, upper] * 2,
+        out_specs=pl.BlockSpec((step, wide), lambda t: (t, 0)),
+        out_shape=jax.ShapeDtypeStruct((rows, wide), BF16),
+        compiler_params=params(),
+        cost_estimate=pl.CostEstimate(flops=4 * rows * width, bytes_accessed=14 * rows * width, transcendentals=0),
+        name="feature_grad",
+    )(*ready, own, got, *up, *down)
+
+
+class Reduction:
+    def __init__(self, ring, own_far, own_zero, own_near, other_far, other_zero, other_near):
+        self.ring, self.middle = ring, ring.chips // 2
+        self.near = near_places(ring)
+        self.own_far, self.own_zero, self.own_near = own_far, own_zero, own_near
+        self.other_far, self.other_zero, self.other_near = other_far, other_zero, other_near
+        self.rows = own_far.shape[0]
+        self.half = self.rows // 2
+
+    def swaps(self):
+        far = self.ring.sibling(self.other_far)
+        self.got_near = self.ring.sibling(lax.optimization_barrier((self.other_near, far))[0])
+        self.got_zero = self.ring.sibling(lax.optimization_barrier((self.other_zero, self.got_near))[0])
+        return far
+
+    def far_sums(self, got):
+        return [total_of(self.own_far[at : at + self.half], got[at : at + self.half]) for at in (0, self.half)]
+
+    def near_sum(self, offset, upper, *more):
+        at = self.near.index(offset % self.ring.chips)
+        start = upper * self.half
+        own = self.own_near[at][start : start + self.half]
+        start += at * self.rows
+        return total_of(own, self.got_near[start : start + self.half], *more)
+
+    def hops(self, up, down):
+        return self.ring.hop(up, 1), self.ring.hop(down, -1)
+
+    def free_sums(self):
+        return self.near_sum(self.middle - 1, 1), self.near_sum(1 - self.middle, 0)
+
+    def bound_sums(self, far):
+        return self.near_sum(self.middle - 1, 0, far[0]), self.near_sum(1 - self.middle, 1, far[1])
+
+    def finish(self, free, bound):
+        for step in range(self.middle - 2, 0, -1):
+            free = self.hops(self.near_sum(step, 1, free[0]), self.near_sum(-step, 0, free[1]))
+            bound = self.hops(self.near_sum(step, 0, bound[0]), self.near_sum(-step, 1, bound[1]))
+        return (bound[0], free[0]), (free[1], bound[1])
+
+
+def near_places(ring):
+    return [o for o in range(1, ring.chips) if o != ring.chips // 2]
 
 
 def local(features, tiles, columns, counts, weight, cotangent):
@@ -370,7 +485,7 @@
     halves = 2
     half_rows = part_rows // halves
     middle = ring.chips // 2
-    near = [o for o in range(ring.chips) if o != middle]
+    near = near_places(ring)
     ends, inner = shift_groups(parts)
     last = chunks - 1
     w = Waves()
@@ -379,8 +494,8 @@
     own_meta = [ring.device_at(o, False) * rows + at for o, at in offsets]
     other_meta = [ring.device_at(o, True) * rows + at for o, at in offsets]
     spmm_meta = jnp.stack([rep] + own_meta + other_meta).astype(jnp.int32)
-    held = [1] + [1] * len(near) + [1, len(near)]
-    order = [middle] + near
+    held = [1, 1] + [1] * len(near) + [1, 1, len(near)]
+    order = [middle, 0] + near
     terms_at = [ring.device_at(o, other) * rows for other in (False, True) for o in order]
     spmm_t_meta = jnp.stack([rep] + terms_at).astype(jnp.int32)
     dense_meta = rep[None].astype(jnp.int32)
@@ -388,9 +503,7 @@
     def part_of(x, u):
         return lax.dynamic_slice_in_dim(x, lax.rem(rep + u, parts) * part_rows, part_rows, 0)
 
-    share = weight.shape[0] // row_size
-    w_share = lax.dynamic_slice_in_dim(weight, lax.axis_index("row") * share, share, 0)
-    w_share = lax.all_gather(w_share, "rep", axis=1, tiled=True)
+    w_full = lax.all_gather(weight, "rep", axis=0, tiled=False)
 
     cot_blocks = [part_of(cotangent, u) for u in range(parts)]
     xs = [features[:, c * width : (c + 1) * width] for c in range(chunks)]
@@ -416,12 +529,14 @@
                 for i in range(1, len(offsets)):
                     got_other[c - 1, i] = ring.sibling(got_own[c - 1, i])
                 w.go(**{f"mixed{c - 1}": run_spmm(c - 1, 1, 0)})
+            if c == 0 and step == 1:
+                w.go(metas=(spmm_meta, spmm_t_meta, dense_meta))
             w.close()
             up, down = w["up" + name], w["down" + name]
             got_own[c, 2 * step - 1], got_own[c, 2 * step] = up, down
         w.go(**{f"far_up{c}": ring.hop(up[:half], 1), f"far_down{c}": ring.hop(down[half:], -1)})
         if c == 0:
-            w.go(cot_ends=cot_ends, own_other=own_other, metas=(spmm_meta, spmm_t_meta, dense_meta))
+            w.go(cot_ends=cot_ends, own_other=own_other)
         seen = []
         if c == last:
             for step in range(1, middle):
@@ -442,7 +557,6 @@
         got_own[c, len(offsets) - 2], got_own[c, len(offsets) - 1] = w[f"far_up{c}"], w[f"far_down{c}"]
         if c < last:
             up = down = w.gate(xs[c + 1])
-    w_full = lax.all_gather(w.gate(w_share), "row", axis=0, tiled=True)
     for i in (-2, -1):
         got_other[last, len(offsets) + i] = ring.sibling(got_own[last, len(offsets) + i])
 
@@ -457,20 +571,33 @@
     for h in range(halves):
         part = ordered(w[f"half{h}"][0], w[f"half_got{h}"])
         blocks = [[(whole[c][u], h * half_rows) for c in range(last)] + [(part[u], 0)] for u in range(parts)]
-        act, back, mixed_rows, grad_rows, earlier = dense(
-            dense_meta, blocks, cot, w_full, half_rows, h * half_rows, earlier
-        )
+        act, back, sums, earlier = dense(dense_meta, blocks, cot, w_full, half_rows, h * half_rows, earlier)
         w.go(**{f"back{h}": [b[0] for b in back]})
         if h == halves - 1:
-            w.go(whole=(act, back, mixed_rows, grad_rows))
+            w.go(whole=(act, back, sums))
         w.close()
         w.go(**{f"back_got{h}": send(w[f"back{h}"], ends + inner)})
-    act, back, mixed_rows, grad_rows = w["whole"]
-    by_row = grad_rows.reshape(part_rows, row_size, -1)
-    sums = jnp.einsum("nf,nrh->rfh", mixed_rows, by_row, preferred_element_type=F32).astype(BF16)
-    w.go(sums=sums)
+    act, back, sums = w["whole"]
+
+    share = sums.shape[0] // row_size
+
+    def sums_for(offset, other):
+        return lax.dynamic_slice_in_dim(sums, ring.device_at(offset, other) * share, share, 0)
+
+    wg = Reduction(
+        ring,
+        sums_for(middle, False),
+        sums_for(0, False),
+        [sums_for(o, False) for o in near],
+        sums_for(middle, True),
+        sums_for(0, True),
+        jnp.concatenate([sums_for(o, True) for o in near]),
+    )
+    wg_far = wg.swaps()
+    w.go(wg=(wg.own_zero, wg.own_near, wg.got_near, wg.got_zero, wg.far_sums(wg_far)))
     w.close()
-    weight_terms = lax.psum_scatter(w["sums"], "row", scatter_dimension=0, tiled=True)[0]
+    wg.own_zero, wg.own_near, wg.got_near, wg.got_zero, wg_far = w["wg"]
+    w.go(wg_far=wg.hops(*wg_far))
 
     def run_spmm_t(c, grads):
         return spmm_t(tiles, columns, counts, spmm_t_meta, grads, parts, held, rows, rows * row_size)
@@ -480,59 +607,59 @@
     for c in range(1, chunks):
         w.go(**{f"rest_got{c}": send([w.gate(b[c]) for b in back], ends + inner)})
     w.close()
-
-    near_sums = []
+    wg_bound = wg.bound_sums(w["wg_far"])
+    wg_free = wg.free_sums()
+    wg_got = wg.hops(jnp.concatenate([wg_bound[0], wg_free[0]]), jnp.concatenate([wg_free[1], wg_bound[1]]))
+    wg_got = wg.finish(
+        (wg_got[0][wg.half :], wg_got[1][: wg.half]), (wg_got[0][: wg.half], wg_got[1][wg.half :])
+    )
+
+    reductions = []
     for c in range(chunks):
         terms = w[f"terms{c}"]
-        own_far, own_near, other_far, other_near = terms[0], terms[1:-2], terms[-2], terms[-1]
-        got_far = ring.sibling(other_far)
-        got_near = ring.sibling(lax.optimization_barrier((other_near, got_far))[0])
-        far = [
-            (own_far[at : at + half].astype(F32) + got_far[at : at + half].astype(F32)).astype(BF16)
-            for at in (0, half)
-        ]
-        w.go(**{f"got_near{c}": got_near, f"sum{c}_{middle}": (ring.hop(far[0], 1), ring.hop(far[1], -1))})
+        red = Reduction(ring, terms[0], terms[1], terms[2:-3], terms[-3], terms[-2], terms[-1])
+        reductions.append(red)
+        far = red.far_sums(red.swaps())
+        free = red.free_sums()
+        if c == 0:
+            free = lax.optimization_barrier((free, wg_got))[0]
+        far_hops, free_hops = red.hops(*far), red.hops(*free)
+        w.go(**{f"far{c}": far_hops, f"zero{c}": red.got_zero})
         if c < last:
             grads = ordered(back[0][c + 1], w[f"rest_got{c + 1}"])
-            grads = lax.optimization_barrier((grads, far[0][:8], far[1][:8]))[0]
-            w.go(**{f"terms{c + 1}": run_spmm_t(c + 1, grads)})
+            grads = lax.optimization_barrier((grads, free[0][:8], free[1][:8]))[0]
+            w.go(**{f"terms{c + 1}": run_spmm_t(c + 1, grads), f"free{c}": free_hops})
         if c == 0:
-            w.go(weight_terms=weight_terms)
+            act_inner = send([lax.optimization_barrier((a, free[0][:8]))[0] for a in act], inner)
+        if c == last:
+            w.go(act_inner=act_inner)
+            low_end = send([lax.optimization_barrier((a, *act_inner.values()))[0] for a in act], ends[:1])
+            w.go(low_end=low_end)
         w.close()
         if c == 0:
-            weight_terms = lax.psum_scatter(w["weight_terms"], "rep", scatter_dimension=0, tiled=True)
-            w.go(act_ends=send([w.gate(a) for a in act], ends))
-
-        def near_sum(offset, got=w[f"got_near{c}"], own=own_near):
-            at = near.index(offset % ring.chips)
-            return own[at].astype(F32) + got[at * rows : (at + 1) * rows].astype(F32)
-
-        near_sums.append(near_sum)
-        for step in range(middle - 1, 0, -1):
-            up, down = w[f"sum{c}_{step + 1}"]
-            to_up, to_down = near_sum(step), near_sum(-step)
-            if step == middle - 1:
-                to_up = jnp.concatenate([to_up[:half] + up.astype(F32), to_up[half:]])
-                to_down = jnp.concatenate([to_down[:half], to_down[half:] + down.astype(F32)])
-            else:
-                to_up, to_down = to_up + up.astype(F32), to_down + down.astype(F32)
-            to_up, to_down = to_up.astype(BF16), to_down.astype(BF16)
-            w.go(**{f"sum{c}_{step}": (ring.hop(to_up, 1), ring.hop(to_down, -1))})
-            if step > 1:
-                w.close()
-            else:
-                w.token = to_up[:8]
-    got = {**w.done, **w.pending, "act_inner": send([w.gate(a) for a in act], inner)}
-    feature_grad = []
-    for c, near_sum in enumerate(near_sums):
-        up, down = got[f"sum{c}_1"]
-        if middle == 1:
-            feature_grad.append((near_sum(0) + jnp.concatenate([up, down]).astype(F32)).astype(BF16))
-        else:
-            feature_grad.append((near_sum(0) + up.astype(F32) + down.astype(F32)).astype(BF16))
-    weight_grad = w.gate(weight_terms).astype(F32)
+            up, down = (jnp.concatenate(halves_of) for halves_of in wg_got)
+            block = total_of(wg.own_zero, wg.got_zero, up, down)
+            cuts = [w.gate(block[:, u * f_wide : (u + 1) * f_wide]) for u in range(parts)]
+            cuts_got = send(cuts, ends + inner)
+            weight_grad = functools.reduce(
+                lambda a, b: a + b, [v.astype(F32) for v in [cuts[0], *cuts_got.values()]]
+            )
+        red.free_hops = w[f"free{c}"] if c < last else free_hops
+        bound = red.bound_sums(w[f"far{c}"])
+        red.bound_hops = red.hops(*bound)
+        if c < last:
+            w.go(**{f"bound{c}": red.bound_hops})
+    high_end = send([lax.optimization_barrier((a, bound[0][:8]))[0] for a in act], ends[1:])
+
+    feature_grad = ()
+    for c, red in enumerate(reductions):
+        bound_hops = w[f"bound{c}"] if c < last else red.bound_hops
+        up, down = red.finish(red.free_hops, bound_hops)
+        feature_grad = (result_of(feature_grad, red.own_zero, w[f"zero{c}"], up, down),)
+    feature_grad = feature_grad[0]
+    weight_grad = weight_grad.T
+    got = {"act_ends": {**w["low_end"], **high_end}, "act_inner": w["act_inner"]}
     act = ordered(act[0], got["act_ends"], got["act_inner"])
-    feature_grad = jnp.concatenate(feature_grad, axis=1)
     activations = jnp.zeros((rows, h_wide), BF16)
     for u in range(parts):
         activations = lax.dynamic_update_slice_in_dim(activations, act[u], lax.rem(rep + u, parts) * part_rows, 0)

time: 362 us -> 374 us (1.033)
  waiting for transfers between devices: 113 us -> 144 us
  blocking collectives: 21.6 us -> 0 us
  starting transfers between devices: 54.9 us -> 72.3 us
  Pallas kernels: 85.7 us -> 102 us
  local copies, waits for them, and re-layouts: 35.9 us -> 22.1 us
  other arithmetic: 21.2 us -> 9.93 us
  matrix products: 5.31 us -> 0 us
    ppermute x16 -> x24, waiting for transfers between devices: 29.1 us -> 53.6 us  [hop(): return lax.ppermute(value, 'row', self.perm(step))]
    reduce_scatter x2 -> x0, waiting for transfers between devices: 22.1 us -> none  [the longest x1 22.1 us: local(): lax.psum_scatter(w['sums'], 'row', scatter_dimension=0, tiled=True)[0]]
    all_gather x1 -> x0, blocking collectives: 21.6 us -> none  [local(): w_share = lax.all_gather(w_share, 'rep', axis=1, tiled=True)]
    ppermute x24 -> x27, waiting for transfers between devices: 54.5 us -> 75.5 us  [send(): lax.ppermute(blocks[s], 'rep', [(i, (i + s) % size) for i in range(size)])]
    ppermute x24 -> x27, starting transfers between devices: 33.6 us -> 43.3 us  [send(): lax.ppermute(blocks[s], 'rep', [(i, (i + s) % size) for i in range(size)])]
    pallas_call x0 -> x2, Pallas kernels: none -> 9.07 us  [result_of(): pl.pallas_call(functools.partial(result_kernel, len(ready), low), grid=(b...]
    pallas_call x2, Pallas kernels: 14.3 us -> 21.8 us  [dense(): pl.pallas_call(functools.partial(dense_kernel, parts, chunks, len(earlier...]
    ppermute x16 -> x24, starting transfers between devices: 18.8 us -> 26.1 us  [hop(): return lax.ppermute(value, 'row', self.perm(step))]
  transfers between devices with their start and end apart: 56 -> 70, of which waited for: 18 -> 26; matrix products, arithmetic and copies ran while one was open for 13% -> 7% of each run, Pallas kernels for 24% -> 26%
where the time goes in v7:
time: 374 us; the launch traced here: 373 us
  waiting for transfers between devices  144 us (39%)
  Pallas kernels  102 us (27%)
  starting transfers between devices  72.3 us (19%)
  between operations  22.8 us (6%)
  local copies, waits for them, and re-layouts  22.1 us (6%)
  other arithmetic  9.93 us (3%)
    ppermute x27, waiting for transfers between devices, send(): lax.ppermute(blocks[s], 'rep', [(i, (i + s) % size) for i in range(size)])  75.5 us
    ppermute x24, waiting for transfers between devices, hop(): return lax.ppermute(value, 'row', self.perm(step))  53.6 us
    ppermute x27, starting transfers between devices, send(): lax.ppermute(blocks[s], 'rep', [(i, (i + s) % size) for i in range(size)])  43.3 us
    pallas_call x3, Pallas kernels, spmm(): pl.pallas_call(functools.partial(spmm_kernel, len(pieces), per_part, skip...  36.5 us
    pallas_call x2, Pallas kernels, spmm_t(): pl.pallas_call(functools.partial(spmm_t_kernel, len(grads), per_part, len...  34.5 us
    ppermute x24, starting transfers between devices, hop(): return lax.ppermute(value, 'row', self.perm(step))  26.1 us
    pallas_call x2, Pallas kernels, dense(): pl.pallas_call(functools.partial(dense_kernel, parts, chunks, len(earlier...  21.8 us
    ppermute x18, waiting for transfers between devices, sibling(): return lax.ppermute(value, 'row', [(d, d ^ 1) for d in range(self.devices)])  14.7 us
  transfers between devices with their start and end apart: 70, of which 26 were waited for; matrix products, arithmetic and copies ran while one was open for 7% of the time, Pallas kernels for 26%

profile of v7, /device:TPU:0, one launch (start us, length us, event | category | flops | bytes accessed | tf_op | source)
XLA Modules:
  0.0 372.7 jit_solution(15856971085031270226)
XLA Ops:
  9.4 2.6 collective-permute-start
  12.1 2.9 constant_dynamic-slice_fusion.9
  15.0 4.0 %collective-permute-start.4 = (bf16[1024,256]{1,0:T(8,128)(2,1)}, bf16[1024,256]{1,0:T(8,128)(2,1)}, u32[]{:S(2)}, u32[]{:S(2)}) collective-permute-start(bf16[1024,256]{1,0:T(8,128)(2,1)} %get-tuple-element.378), channel_id=1, source_target_pairs={{0,3},{1,0},{2,1},{3,2},{4,7},{5,4},{6,5},{7,6},{8,11},{9,8},{10,9... | collective-permute-start | bytes 1572872 | tf_op jit(solution)/shard_map/ppermute | solution.py:87
  29.5 6.4 %collective-permute-done.refs_1_ = bf16[4096,128]{1,0:T(8,128)(2,1)} collective-permute-done((bf16[4096,128]{1,0:T(8,128)(2,1)S(1)}, bf16[4096,128]{1,0:T(8,128)(2,1)}, u32[]{:S(2)}, u32[]{:S(2)}) %collective-permute-start) | collective-permute-done | bytes 1048608 | tf_op jit(solution)/shard_map/ppermute | solution.py:38
  37.9 1.9 slice.157
  39.7 1.9 slice.158
  45.0 10.7 %collective-permute-done.2.refs_3_ = bf16[2048,128]{1,0:T(8,128)(2,1)} collective-permute-done((bf16[2048,128]{1,0:T(8,128)(2,1)}, bf16[2048,128]{1,0:T(8,128)(2,1)}, u32[]{:S(2)}, u32[]{:S(2)}) %collective-permute-start.2) | collective-permute-done | bytes 524320 | tf_op jit(solution)/shard_map/ppermute | solution.py:38
  59.1 2.7 collective-permute-start.7
  61.7 3.0 fusion
  65.8 14.5 %spmm.3 = (bf16[1024,128]{1,0:T(8,128)(2,1)}, bf16[1024,128]{1,0:T(8,128)(2,1)}, bf16[1024,128]{1,0:T(8,128)(2,1)}, bf16[1024,128]{1,0:T(8,128)(2,1)}) custom-call(s32[32,16]{1,0:T(8,128)} %copy.69.cols, s32[32]{0:T(128)} %counts.9, s32[11]{0:T(128)} %stack.75.meta, bf16[32,16,128,128]{3,2,1,0:T(8,128)(2,1)} %tiles.9, bf16[4096,128]{1,0:T(8,128)(2,1)} %copy-done.5, ...), custom_call_target="tpu_custom_call" | custom-call | flops 2147483648 | bytes 25165824 | tf_op jit(solution)/shard_map/spmm/pallas_call | solution.py:158
  80.3 29.7 %collective-permute-done.7.refs_10_ = bf16[1024,256]{1,0:T(8,128)(2,1)S(1)} collective-permute-done((bf16[1024,256]{1,0:T(8,128)(2,1)}, bf16[1024,256]{1,0:T(8,128)(2,1)S(1)}, u32[]{:S(2)}, u32[]{:S(2)}) %collective-permute-start.7) | collective-permute-done | bytes 524320 | tf_op jit(solution)/shard_map/ppermute | solution.py:87
  115.1 3.8 %collective-permute-start.18 = (bf16[1024,128]{1,0:T(8,128)(2,1)S(1)}, bf16[1024,128]{1,0:T(8,128)(2,1)S(1)}, u32[]{:S(2)}, u32[]{:S(2)}) collective-permute-start(bf16[1024,128]{1,0:T(8,128)(2,1)S(1)} %copy-done.64), channel_id=1, source_target_pairs={{0,3},{1,0},{2,1},{3,2},{4,7},{5,4},{6,5},{7,6},{8,11},{9,8},{10,9... | collective-permute-start | bytes 786440 | tf_op jit(solution)/shard_map/ppermute | solution.py:87
  118.9 6.5 %collective-permute-done.14.refs_3_ = bf16[2048,128]{1,0:T(8,128)(2,1)S(1)} collective-permute-done((bf16[2048,128]{1,0:T(8,128)(2,1)S(1)}, bf16[2048,128]{1,0:T(8,128)(2,1)S(1)}, u32[]{:S(2)}, u32[]{:S(2)}) %collective-permute-start.14) | collective-permute-done | bytes 524320 | tf_op jit(solution)/shard_map/ppermute | solution.py:38
  126.6 2.5 collective-permute-done.18.refs_2_
  129.6 2.3 collective-permute-start.20
  132.9 11.0 %spmm.4 = (bf16[512,128]{1,0:T(8,128)(2,1)}, bf16[512,128]{1,0:T(8,128)(2,1)}, bf16[512,128]{1,0:T(8,128)(2,1)}, bf16[512,128]{1,0:T(8,128)(2,1)}) custom-call(s32[32,16]{1,0:T(8,128)} %copy.69.cols, s32[32]{0:T(128)} %counts.9, s32[11]{0:T(128)} %stack.75.meta, bf16[32,16,128,128]{3,2,1,0:T(8,128)(2,1)} %tiles.9, bf16[4096,128]{1,0:T(8,128)(2,1)} %copy-done, ...), custom_call_target="tpu_custom_call" | custom-call | flops 1073741824 | bytes 16777216 | tf_op jit(solution)/shard_map/spmm/pallas_call | solution.py:158
  144.3 2.0 collective-permute-start.23
  146.4 1.7 collective-permute-start.25
  148.0 11.0 %spmm.5 = (bf16[512,128]{1,0:T(8,128)(2,1)}, bf16[512,128]{1,0:T(8,128)(2,1)}, bf16[512,128]{1,0:T(8,128)(2,1)}, bf16[512,128]{1,0:T(8,128)(2,1)}) custom-call(s32[32,16]{1,0:T(8,128)} %copy.69.cols, s32[32]{0:T(128)} %counts.9, s32[11]{0:T(128)} %stack.75.meta, bf16[32,16,128,128]{3,2,1,0:T(8,128)(2,1)} %tiles.9, bf16[4096,128]{1,0:T(8,128)(2,1)} %copy-done, ...), custom_call_target="tpu_custom_call" | custom-call | flops 1073741824 | bytes 16777216 | tf_op jit(solution)/shard_map/spmm/pallas_call | solution.py:158
  159.1 2.2 collective-permute-start.26
  162.8 10.4 %dense.2 = (bf16[1024,256]{1,0:T(8,128)(2,1)}, bf16[1024,256]{1,0:T(8,128)(2,1)}, bf16[1024,256]{1,0:T(8,128)(2,1)}, bf16[1024,256]{1,0:T(8,128)(2,1)}, bf16[512...) custom-call(s32[1]{0:T(128)} %bitcast.meta, ...), custom_call_target="tpu_custom_call" | custom-call | flops 3221225472 | bytes 10485760 | tf_op jit(solution)/shard_map/dense/pallas_call | solution.py:348
  173.9 2.9 collective-permute-start.29
  177.6 11.3 %dense.3 = (bf16[1024,256]{1,0:T(8,128)(2,1)}, bf16[1024,256]{1,0:T(8,128)(2,1)}, bf16[1024,256]{1,0:T(8,128)(2,1)}, bf16[1024,256]{1,0:T(8,128)(2,1)}, bf16[512...) custom-call(s32[1]{0:T(128)} %bitcast.meta, ...), custom_call_target="tpu_custom_call", output_to_operand_aliasing={{0}: (15, {}), {1}: (16, {}), {2}: (17, {}), {3}: (18, {}),... | custom-call | flops 3221225472 | bytes 10485760 | tf_op jit(solution)/shard_map/dense/pallas_call | solution.py:348
  189.0 1.8 constant_dynamic-slice_fusion.8
  192.5 1.8 collective-permute-done.37
  194.4 3.1 collective-permute-start.33
  199.7 2.1 collective-permute-done.33.refs_3_
  201.7 9.2 %collective-permute-done.34.refs_5_ = bf16[512,128]{1,0:T(8,128)(2,1)S(1)} collective-permute-done((bf16[512,128]{1,0:T(8,128)(2,1)}, bf16[512,128]{1,0:T(8,128)(2,1)S(1)}, u32[]{:S(2)}, u32[]{:S(2)}) %collective-permute-start.34) | collective-permute-done | bytes 131104 | tf_op jit(solution)/shard_map/ppermute | solution.py:87
  212.4 2.8 collective-permute-start.41
  217.3 17.2 %spmm_t.2 = (bf16[4096,128]{1,0:T(8,128)(2,1)}, bf16[4096,128]{1,0:T(8,128)(2,1)}, bf16[4096,128]{1,0:T(8,128)(2,1)}, bf16[4096,128]{1,0:T(8,128)(2,1)}, bf16[40...) custom-call(s32[32,16]{1,0:T(8,128)} %copy.69.cols, s32[32]{0:T(128)} %counts.9, ...), custom_call_target="tpu_custom_call" | custom-call | flops 2147483648 | bytes 25165824 | tf_op jit(solution)/shard_map/spmm_t/pallas_call | solution.py:241
  234.7 2.9 collective-permute-done.44
  237.7 4.2 %collective-permute-done.45 = bf16[8192,128]{1,0:T(8,128)(2,1)S(1)} collective-permute-done((bf16[8192,128]{1,0:T(8,128)(2,1)}, bf16[8192,128]{1,0:T(8,128)(2,1)S(1)}, u32[]{:S(2)}, u32[]{:S(2)}) %collective-permute-start.45) | collective-permute-done | bytes 2097184 | tf_op jit(solution)/shard_map/ppermute | solution.py:41
  242.0 2.5 add_convert_fusion.10
  249.9 17.3 %spmm_t.3 = (bf16[4096,128]{1,0:T(8,128)(2,1)}, bf16[4096,128]{1,0:T(8,128)(2,1)}, bf16[4096,128]{1,0:T(8,128)(2,1)}, bf16[4096,128]{1,0:T(8,128)(2,1)}, bf16[40...) custom-call(s32[32,16]{1,0:T(8,128)} %copy.69.cols, s32[32]{0:T(128)} %counts.9, ...), custom_call_target="tpu_custom_call" | custom-call | flops 2147483648 | bytes 25165824 | tf_op jit(solution)/shard_map/spmm_t/pallas_call | solution.py:241
  267.3 2.9 collective-permute-done.49.refs_3_
  271.3 2.9 collective-permute-done.53
  274.3 1.7 collective-permute-start.58
  279.4 21.3 %collective-permute-done.58 = bf16[1024,256]{1,0:T(8,128)(2,1)S(1)} collective-permute-done((bf16[1024,256]{1,0:T(8,128)(2,1)S(1)}, bf16[1024,256]{1,0:T(8,128)(2,1)S(1)}, u32[]{:S(2)}, u32[]{:S(2)}) %collective-permute-start.58) | collective-permute-done | bytes 524320 | tf_op jit(solution)/shard_map/ppermute | solution.py:87
  307.1 9.6 %collective-permute-done.59 = bf16[1024,256]{1,0:T(8,128)(2,1)S(1)} collective-permute-done((bf16[1024,256]{1,0:T(8,128)(2,1)S(1)}, bf16[1024,256]{1,0:T(8,128)(2,1)S(1)}, u32[]{:S(2)}, u32[]{:S(2)}) %collective-permute-start.59) | collective-permute-done | bytes 524320 | tf_op jit(solution)/shard_map/ppermute | solution.py:87
  318.6 3.3 collective-permute-start.32
  321.9 5.9 %collective-permute-done.54 = bf16[2048,128]{1,0:T(8,128)(2,1)S(1)} collective-permute-done((bf16[2048,128]{1,0:T(8,128)(2,1)S(1)}, bf16[2048,128]{1,0:T(8,128)(2,1)S(1)}, u32[]{:S(2)}, u32[]{:S(2)}) %collective-permute-start.54) | collective-permute-done | bytes 524320 | tf_op jit(solution)/shard_map/ppermute | solution.py:38
  327.8 3.5 collective-permute-start.67
  331.3 2.4 collective-permute-start.68
  333.8 1.9 add_convert_fusion
  340.6 4.4 %feature_grad.2.refs_0_ = bf16[4096,128]{1,0:T(8,128)(2,1)} custom-call(bf16[4096,128]{1,0:T(8,128)(2,1)} %get-tuple-element.328.refs_0_, bf16[4096,128]{1,0:T(8,128)(2,1)} %copy-done.12, bf16[2048,128]{1,0:T(8,128)(2,1)} %copy-done.29, bf16[2048,128]{1,0:T(8,128)(2,1)} %copy-done.25, bf16[2048,128]{1,0:T(8,128)(2,1)} %copy-done.26, bf16[2048,128]{1,0:T(8,128)(2,1)} %copy-done.30), custom_call_target="tpu_custom_call" | custom-call | flops 2097152 | bytes 7340032 | tf_op jit(solution)/shard_map/feature_grad/pallas_call | solution.py:418
  345.1 5.7 %collective-permute-done.60.refs_3_ = bf16[2048,128]{1,0:T(8,128)(2,1)S(1)} collective-permute-done((bf16[2048,128]{1,0:T(8,128)(2,1)}, bf16[2048,128]{1,0:T(8,128)(2,1)S(1)}, u32[]{:S(2)}, u32[]{:S(2)}) %collective-permute-start.60) | collective-permute-done | bytes 524320 | tf_op jit(solution)/shard_map/ppermute | solution.py:38
  350.7 9.6 %collective-permute-done.61.refs_4_ = bf16[2048,128]{1,0:T(8,128)(2,1)S(1)} collective-permute-done((bf16[2048,128]{1,0:T(8,128)(2,1)}, bf16[2048,128]{1,0:T(8,128)(2,1)S(1)}, u32[]{:S(2)}, u32[]{:S(2)}) %collective-permute-start.61) | collective-permute-done | bytes 524320 | tf_op jit(solution)/shard_map/ppermute | solution.py:38
  361.2 4.7 %feature_grad.3 = bf16[4096,256]{1,0:T(8,128)(2,1)} custom-call(bf16[4096,128]{1,0:T(8,128)(2,1)} %feature_grad.2.refs_0_, bf16[4096,128]{1,0:T(8,128)(2,1)} %get-tuple-element.334.refs_1_, bf16[4096,128]{1,0:T(8,128)(2,1)} %copy-done.15, bf16[2048,128]{1,0:T(8,128)(2,1)} %copy-done.22, bf16[2048,128]{1,0:T(8,128)(2,1)} %copy-done.23, ...), custom_call_target="tpu_custom_call" | custom-call | flops 2097152 | bytes 7340032 | tf_op jit(solution)/shard_map/feature_grad/pallas_call | solution.py:418
  (272 shorter events, 57.3 us)
Async XLA Ops:
  7.2 155.6 %all-gather.3.cloned.1.call-start = ((), (), s32[]{:S(2)}) async-start(), calls=%async_computation | async-start | bytes 2621440 | tf_op jit(solution)/shard_map/all_gather | solution.py:506
  7.2 49.8 %collective-permute-start.6 = (bf16[4096,256]{1,0:T(8,128)(2,1)}, bf16[4096,256]{1,0:T(8,128)(2,1)}, u32[]{:S(2)}, u32[]{:S(2)}) collective-permute-start(bf16[4096,256]{1,0:T(8,128)(2,1)} %param.58), channel_id=1, source_target_pairs={{0,4},{4,0},{8,12},{12,8},{16,20},{20,16},{24,28},{28,24},{1,5},{5... | collective-permute-start | bytes 6291464 | tf_op jit(solution)/shard_map/ppermute | solution.py:41
  9.4 26.5 %collective-permute-start = (bf16[4096,128]{1,0:T(8,128)(2,1)S(1)}, bf16[4096,128]{1,0:T(8,128)(2,1)}, u32[]{:S(2)}, u32[]{:S(2)}) collective-permute-start(bf16[4096,128]{1,0:T(8,128)(2,1)S(1)} %get-tuple-element.384.refs_0_), channel_id=1, source_target_pairs={{0,8},{4,12},{8,24},{12,28},{24,16},{28,20},{16,0},{20,4},{1,9},{5... | collective-permute-start | bytes 3145736 | tf_op jit(solution)/shard_map/ppermute | solution.py:38
  12.0 25.4 %collective-permute-start.1 = (bf16[4096,128]{1,0:T(8,128)(2,1)S(1)}, bf16[4096,128]{1,0:T(8,128)(2,1)}, u32[]{:S(2)}, u32[]{:S(2)}) collective-permute-start(bf16[4096,128]{1,0:T(8,128)(2,1)S(1)} %get-tuple-element.384.refs_0_), channel_id=1, source_target_pairs={{0,16},{4,20},{8,0},{12,4},{24,8},{28,12},{16,24},{20,28},{1,17},{... | collective-permute-start | bytes 3145736 | tf_op jit(solution)/shard_map/ppermute | solution.py:38
  15.0 26.6 %collective-permute-start.4 = (bf16[1024,256]{1,0:T(8,128)(2,1)}, bf16[1024,256]{1,0:T(8,128)(2,1)}, u32[]{:S(2)}, u32[]{:S(2)}) collective-permute-start(bf16[1024,256]{1,0:T(8,128)(2,1)} %get-tuple-element.378), channel_id=1, source_target_pairs={{0,3},{1,0},{2,1},{3,2},{4,7},{5,4},{6,5},{7,6},{8,11},{9,8},{10,9... | collective-permute-start | bytes 1572872 | tf_op jit(solution)/shard_map/ppermute | solution.py:87
  19.1 24.1 %collective-permute-start.5 = (bf16[1024,256]{1,0:T(8,128)(2,1)}, bf16[1024,256]{1,0:T(8,128)(2,1)}, u32[]{:S(2)}, u32[]{:S(2)}) collective-permute-start(bf16[1024,256]{1,0:T(8,128)(2,1)} %get-tuple-element.380), channel_id=1, source_target_pairs={{0,1},{1,2},{2,3},{3,0},{4,5},{5,6},{6,7},{7,4},{8,9},{9,10},{10,1... | collective-permute-start | bytes 1572872 | tf_op jit(solution)/shard_map/ppermute | solution.py:87
  37.4 21.7 %collective-permute-start.10 = (bf16[4096,128]{1,0:T(8,128)(2,1)}, bf16[4096,128]{1,0:T(8,128)(2,1)S(1)}, u32[]{:S(2)}, u32[]{:S(2)}) collective-permute-start(bf16[4096,128]{1,0:T(8,128)(2,1)} %collective-permute-done.refs_1_), channel_id=1, source_target_pairs={{0,4},{4,0},{8,12},{12,8},{16,20},{20,16},{24,28},{28,24},{1,5},{5... | collective-permute-start | bytes 3145736 | tf_op jit(solution)/shard_map/ppermute | solution.py:41
  37.4 21.7 %collective-permute-start.11 = (bf16[4096,128]{1,0:T(8,128)(2,1)}, bf16[4096,128]{1,0:T(8,128)(2,1)S(1)}, u32[]{:S(2)}, u32[]{:S(2)}) collective-permute-start(bf16[4096,128]{1,0:T(8,128)(2,1)} %collective-permute-done.1.refs_2_), channel_id=1, source_target_pairs={{0,4},{4,0},{8,12},{12,8},{16,20},{20,16},{24,28},{28,24},{1,5},{5... | collective-permute-start | bytes 3145736 | tf_op jit(solution)/shard_map/ppermute | solution.py:41
  41.6 14.1 %collective-permute-start.2 = (bf16[2048,128]{1,0:T(8,128)(2,1)}, bf16[2048,128]{1,0:T(8,128)(2,1)}, u32[]{:S(2)}, u32[]{:S(2)}) collective-permute-start(bf16[2048,128]{1,0:T(8,128)(2,1)} %slice.157), channel_id=1, source_target_pairs={{0,8},{4,12},{8,24},{12,28},{24,16},{28,20},{16,0},{20,4},{1,9},{5... | collective-permute-start | bytes 1572872 | tf_op jit(solution)/shard_map/ppermute | solution.py:38
  43.1 13.9 %collective-permute-start.3 = (bf16[2048,128]{1,0:T(8,128)(2,1)}, bf16[2048,128]{1,0:T(8,128)(2,1)}, u32[]{:S(2)}, u32[]{:S(2)}) collective-permute-start(bf16[2048,128]{1,0:T(8,128)(2,1)} %slice.158), channel_id=1, source_target_pairs={{0,16},{4,20},{8,0},{12,4},{24,8},{28,12},{16,24},{20,28},{1,17},{... | collective-permute-start | bytes 1572872 | tf_op jit(solution)/shard_map/ppermute | solution.py:38
  57.0 53.0 %collective-permute-start.8 = (bf16[4096,128]{1,0:T(8,128)(2,1)S(1)}, bf16[4096,128]{1,0:T(8,128)(2,1)S(1)}, u32[]{:S(2)}, u32[]{:S(2)}) collective-permute-start(bf16[4096,128]{1,0:T(8,128)(2,1)S(1)} %get-tuple-element.181.refs_0_), channel_id=1, source_target_pairs={{0,8},{4,12},{8,24},{12,28},{24,16},{28,20},{16,0},{20,4},{1,9},{5... | collective-permute-start | bytes 3145736 | tf_op jit(solution)/shard_map/ppermute | solution.py:38
  57.5 52.5 %collective-permute-start.9 = (bf16[4096,128]{1,0:T(8,128)(2,1)S(1)}, bf16[4096,128]{1,0:T(8,128)(2,1)S(1)}, u32[]{:S(2)}, u32[]{:S(2)}) collective-permute-start(bf16[4096,128]{1,0:T(8,128)(2,1)S(1)} %get-tuple-element.181.refs_0_), channel_id=1, source_target_pairs={{0,16},{4,20},{8,0},{12,4},{24,8},{28,12},{16,24},{20,28},{1,17},{... | collective-permute-start | bytes 3145736 | tf_op jit(solution)/shard_map/ppermute | solution.py:38
  59.1 51.0 %collective-permute-start.7 = (bf16[1024,256]{1,0:T(8,128)(2,1)}, bf16[1024,256]{1,0:T(8,128)(2,1)S(1)}, u32[]{:S(2)}, u32[]{:S(2)}) collective-permute-start(bf16[1024,256]{1,0:T(8,128)(2,1)} %get-tuple-element.180), channel_id=1, source_target_pairs={{0,2},{1,3},{2,0},{3,1},{4,6},{5,7},{6,4},{7,5},{8,10},{9,11},{10,... | collective-permute-start | bytes 1572872 | tf_op jit(solution)/shard_map/ppermute | solution.py:87
  111.5 13.9 %collective-permute-start.14 = (bf16[2048,128]{1,0:T(8,128)(2,1)S(1)}, bf16[2048,128]{1,0:T(8,128)(2,1)S(1)}, u32[]{:S(2)}, u32[]{:S(2)}) collective-permute-start(bf16[2048,128]{1,0:T(8,128)(2,1)S(1)} %slice.161), channel_id=1, source_target_pairs={{0,8},{4,12},{8,24},{12,28},{24,16},{28,20},{16,0},{20,4},{1,9},{5... | collective-permute-start | bytes 1572872 | tf_op jit(solution)/shard_map/ppermute | solution.py:38
  112.8 13.8 %collective-permute-start.15 = (bf16[2048,128]{1,0:T(8,128)(2,1)S(1)}, bf16[2048,128]{1,0:T(8,128)(2,1)S(1)}, u32[]{:S(2)}, u32[]{:S(2)}) collective-permute-start(bf16[2048,128]{1,0:T(8,128)(2,1)S(1)} %slice.162), channel_id=1, source_target_pairs={{0,16},{4,20},{8,0},{12,4},{24,8},{28,12},{16,24},{20,28},{1,17},{... | collective-permute-start | bytes 1572872 | tf_op jit(solution)/shard_map/ppermute | solution.py:38
  115.1 14.0 %collective-permute-start.18 = (bf16[1024,128]{1,0:T(8,128)(2,1)S(1)}, bf16[1024,128]{1,0:T(8,128)(2,1)S(1)}, u32[]{:S(2)}, u32[]{:S(2)}) collective-permute-start(bf16[1024,128]{1,0:T(8,128)(2,1)S(1)} %copy-done.64), channel_id=1, source_target_pairs={{0,3},{1,0},{2,1},{3,2},{4,7},{5,4},{6,5},{7,6},{8,11},{9,8},{10,9... | collective-permute-start | bytes 786440 | tf_op jit(solution)/shard_map/ppermute | solution.py:87
  129.6 14.7 %collective-permute-start.20 = (bf16[1024,128]{1,0:T(8,128)(2,1)S(1)}, bf16[1024,128]{1,0:T(8,128)(2,1)S(1)}, u32[]{:S(2)}, u32[]{:S(2)}) collective-permute-start(bf16[1024,128]{1,0:T(8,128)(2,1)S(1)} %copy-done.63), channel_id=1, source_target_pairs={{0,2},{1,3},{2,0},{3,1},{4,6},{5,7},{6,4},{7,5},{8,10},{9,11},{10,... | collective-permute-start | bytes 786440 | tf_op jit(solution)/shard_map/ppermute | solution.py:87
  144.3 14.7 %collective-permute-start.23 = (bf16[512,128]{1,0:T(8,128)(2,1)}, bf16[512,128]{1,0:T(8,128)(2,1)S(1)}, u32[]{:S(2)}, u32[]{:S(2)}) collective-permute-start(bf16[512,128]{1,0:T(8,128)(2,1)} %get-tuple-element.202), channel_id=1, source_target_pairs={{0,3},{1,0},{2,1},{3,2},{4,7},{5,4},{6,5},{7,6},{8,11},{9,8},{10,9... | collective-permute-start | bytes 393224 | tf_op jit(solution)/shard_map/ppermute | solution.py:87
  159.1 14.1 %collective-permute-start.26 = (bf16[512,128]{1,0:T(8,128)(2,1)}, bf16[512,128]{1,0:T(8,128)(2,1)S(1)}, u32[]{:S(2)}, u32[]{:S(2)}) collective-permute-start(bf16[512,128]{1,0:T(8,128)(2,1)} %get-tuple-element.209), channel_id=1, source_target_pairs={{0,3},{1,0},{2,1},{3,2},{4,7},{5,4},{6,5},{7,6},{8,11},{9,8},{10,9... | collective-permute-start | bytes 393224 | tf_op jit(solution)/shard_map/ppermute | solution.py:87
  173.9 15.1 %collective-permute-start.29 = (bf16[512,128]{1,0:T(8,128)(2,1)}, bf16[512,128]{1,0:T(8,128)(2,1)S(1)}, u32[]{:S(2)}, u32[]{:S(2)}) collective-permute-start(bf16[512,128]{1,0:T(8,128)(2,1)} %get-tuple-element.228), channel_id=1, source_target_pairs={{0,3},{1,0},{2,1},{3,2},{4,7},{5,4},{6,5},{7,6},{8,11},{9,8},{10,9... | collective-permute-start | bytes 393224 | tf_op jit(solution)/shard_map/ppermute | solution.py:87
  194.3 16.7 %collective-permute-start.38 = (bf16[128,1024]{1,0:T(8,128)(2,1)S(1)}, bf16[128,1024]{1,0:T(8,128)(2,1)S(1)}, u32[]{:S(2)}, u32[]{:S(2)}) collective-permute-start(bf16[128,1024]{1,0:T(8,128)(2,1)S(1)} %get-tuple-element.264), channel_id=1, source_target_pairs={{0,4},{4,0},{8,12},{12,8},{16,20},{20,16},{24,28},{28,24},{1,5},{5... | collective-permute-start | bytes 786440 | tf_op jit(solution)/shard_map/ppermute | solution.py:41
  197.5 13.5 %collective-permute-start.34 = (bf16[512,128]{1,0:T(8,128)(2,1)}, bf16[512,128]{1,0:T(8,128)(2,1)S(1)}, u32[]{:S(2)}, u32[]{:S(2)}) collective-permute-start(bf16[512,128]{1,0:T(8,128)(2,1)} %get-tuple-element.260), channel_id=1, source_target_pairs={{0,2},{1,3},{2,0},{3,1},{4,6},{5,7},{6,4},{7,5},{8,10},{9,11},{10,... | collective-permute-start | bytes 393224 | tf_op jit(solution)/shard_map/ppermute | solution.py:87
  211.0 23.5 %collective-permute-start.43 = (bf16[1024,128]{1,0:T(8,128)(2,1)S(1)}, bf16[1024,128]{1,0:T(8,128)(2,1)S(1)}, u32[]{:S(2)}, u32[]{:S(2)}) collective-permute-start(bf16[1024,128]{1,0:T(8,128)(2,1)S(1)} %copy-done.45), channel_id=1, source_target_pairs={{0,1},{1,2},{2,3},{3,0},{4,5},{5,6},{6,7},{7,4},{8,9},{9,10},{10,1... | collective-permute-start | bytes 786440 | tf_op jit(solution)/shard_map/ppermute | solution.py:87
  211.1 23.5 %collective-permute-start.42 = (bf16[1024,128]{1,0:T(8,128)(2,1)S(1)}, bf16[1024,128]{1,0:T(8,128)(2,1)S(1)}, u32[]{:S(2)}, u32[]{:S(2)}) collective-permute-start(bf16[1024,128]{1,0:T(8,128)(2,1)S(1)} %copy-done.46), channel_id=1, source_target_pairs={{0,2},{1,3},{2,0},{3,1},{4,6},{5,7},{6,4},{7,5},{8,10},{9,11},{10,... | collective-permute-start | bytes 786440 | tf_op jit(solution)/shard_map/ppermute | solution.py:87
  212.4 22.2 %collective-permute-start.41 = (bf16[1024,128]{1,0:T(8,128)(2,1)S(1)}, bf16[1024,128]{1,0:T(8,128)(2,1)S(1)}, u32[]{:S(2)}, u32[]{:S(2)}) collective-permute-start(bf16[1024,128]{1,0:T(8,128)(2,1)S(1)} %copy-done.47), channel_id=1, source_target_pairs={{0,3},{1,0},{2,1},{3,2},{4,7},{5,4},{6,5},{7,6},{8,11},{9,8},{10,9... | collective-permute-start | bytes 786440 | tf_op jit(solution)/shard_map/ppermute | solution.py:87
  215.2 19.3 %collective-permute-start.39 = (bf16[64,1024]{1,0:T(8,128)(2,1)S(1)}, bf16[64,1024]{1,0:T(8,128)(2,1)S(1)}, u32[]{:S(2)}, u32[]{:S(2)}) collective-permute-start(bf16[64,1024]{1,0:T(8,128)(2,1)S(1)} %get-tuple-element.265), channel_id=1, source_target_pairs={{0,8},{4,12},{8,24},{12,28},{24,16},{28,20},{16,0},{20,4},{1,9},{5... | collective-permute-start | bytes 393224 | tf_op jit(solution)/shard_map/ppermute | solution.py:38
  216.6 17.9 %collective-permute-start.40 = (bf16[64,1024]{1,0:T(8,128)(2,1)S(1)}, bf16[64,1024]{1,0:T(8,128)(2,1)}, u32[]{:S(2)}, u32[]{:S(2)}) collective-permute-start(bf16[64,1024]{1,0:T(8,128)(2,1)S(1)} %get-tuple-element.266), channel_id=1, source_target_pairs={{0,16},{4,20},{8,0},{12,4},{24,8},{28,12},{16,24},{20,28},{1,17},{... | collective-permute-start | bytes 393224 | tf_op jit(solution)/shard_map/ppermute | solution.py:38
  241.9 29.3 %collective-permute-start.48 = (bf16[4096,128]{1,0:T(8,128)(2,1)}, bf16[4096,128]{1,0:T(8,128)(2,1)S(1)}, u32[]{:S(2)}, u32[]{:S(2)}) collective-permute-start(bf16[4096,128]{1,0:T(8,128)(2,1)} %get-tuple-element.295), channel_id=1, source_target_pairs={{0,4},{4,0},{8,12},{12,8},{16,20},{20,16},{24,28},{28,24},{1,5},{5... | collective-permute-start | bytes 3145736 | tf_op jit(solution)/shard_map/ppermute | solution.py:41
  244.5 22.7 %collective-permute-start.46 = (bf16[2048,128]{1,0:T(8,128)(2,1)}, bf16[2048,128]{1,0:T(8,128)(2,1)}, u32[]{:S(2)}, u32[]{:S(2)}) collective-permute-start(bf16[2048,128]{1,0:T(8,128)(2,1)} %get-tuple-element.369), channel_id=1, source_target_pairs={{0,8},{4,12},{8,24},{12,28},{24,16},{28,20},{16,0},{20,4},{1,9},{5... | collective-permute-start | bytes 1572872 | tf_op jit(solution)/shard_map/ppermute | solution.py:38
  245.9 21.4 %collective-permute-start.47 = (bf16[2048,128]{1,0:T(8,128)(2,1)}, bf16[2048,128]{1,0:T(8,128)(2,1)}, u32[]{:S(2)}, u32[]{:S(2)}) collective-permute-start(bf16[2048,128]{1,0:T(8,128)(2,1)} %get-tuple-element.368), channel_id=1, source_target_pairs={{0,16},{4,20},{8,0},{12,4},{24,8},{28,12},{16,24},{20,28},{1,17},{... | collective-permute-start | bytes 1572872 | tf_op jit(solution)/shard_map/ppermute | solution.py:38
  247.8 22.4 %collective-permute-start.49 = (bf16[2048,128]{1,0:T(8,128)(2,1)}, bf16[2048,128]{1,0:T(8,128)(2,1)S(1)}, u32[]{:S(2)}, u32[]{:S(2)}) collective-permute-start(bf16[2048,128]{1,0:T(8,128)(2,1)} %get-tuple-element.301), channel_id=1, source_target_pairs={{0,8},{4,12},{8,24},{12,28},{24,16},{28,20},{16,0},{20,4},{1,9},{5... | collective-permute-start | bytes 1572872 | tf_op jit(solution)/shard_map/ppermute | solution.py:38
  249.2 22.0 %collective-permute-start.50 = (bf16[2048,128]{1,0:T(8,128)(2,1)}, bf16[2048,128]{1,0:T(8,128)(2,1)S(1)}, u32[]{:S(2)}, u32[]{:S(2)}) collective-permute-start(bf16[2048,128]{1,0:T(8,128)(2,1)} %get-tuple-element.313), channel_id=1, source_target_pairs={{0,16},{4,20},{8,0},{12,4},{24,8},{28,12},{16,24},{20,28},{1,17},{... | collective-permute-start | bytes 1572872 | tf_op jit(solution)/shard_map/ppermute | solution.py:38
  274.2 30.5 %collective-permute-start.56 = (bf16[8192,128]{1,0:T(8,128)(2,1)}, bf16[8192,128]{1,0:T(8,128)(2,1)S(1)}, u32[]{:S(2)}, u32[]{:S(2)}) collective-permute-start(bf16[8192,128]{1,0:T(8,128)(2,1)} %get-tuple-element.320), channel_id=1, source_target_pairs={{0,4},{4,0},{8,12},{12,8},{16,20},{20,16},{24,28},{28,24},{1,5},{5... | collective-permute-start | bytes 6291464 | tf_op jit(solution)/shard_map/ppermute | solution.py:41
  274.3 26.3 %collective-permute-start.58 = (bf16[1024,256]{1,0:T(8,128)(2,1)S(1)}, bf16[1024,256]{1,0:T(8,128)(2,1)S(1)}, u32[]{:S(2)}, u32[]{:S(2)}) collective-permute-start(bf16[1024,256]{1,0:T(8,128)(2,1)S(1)} %copy-done.32), channel_id=1, source_target_pairs={{0,2},{1,3},{2,0},{3,1},{4,6},{5,7},{6,4},{7,5},{8,10},{9,11},{10,... | collective-permute-start | bytes 1572872 | tf_op jit(solution)/shard_map/ppermute | solution.py:87
  277.2 27.8 %collective-permute-start.64 = (bf16[128,1024]{1,0:T(8,128)(2,1)S(1)}, bf16[128,1024]{1,0:T(8,128)(2,1)S(1)}, u32[]{:S(2)}, u32[]{:S(2)}) collective-permute-start(bf16[128,1024]{1,0:T(8,128)(2,1)S(1)} %pad_maximum_fusion.1), channel_id=1, source_target_pairs={{0,8},{4,12},{8,24},{12,28},{24,16},{28,20},{16,0},{20,4},{1,9},{5... | collective-permute-start | bytes 786440 | tf_op jit(solution)/shard_map/ppermute | solution.py:38
  278.8 26.8 %collective-permute-start.65 = (bf16[128,1024]{1,0:T(8,128)(2,1)S(1)}, bf16[128,1024]{1,0:T(8,128)(2,1)S(1)}, u32[]{:S(2)}, u32[]{:S(2)}) collective-permute-start(bf16[128,1024]{1,0:T(8,128)(2,1)S(1)} %pad_maximum_fusion.2), channel_id=1, source_target_pairs={{0,16},{4,20},{8,0},{12,4},{24,8},{28,12},{16,24},{20,28},{1,17},{... | collective-permute-start | bytes 786440 | tf_op jit(solution)/shard_map/ppermute | solution.py:38
  301.5 15.2 %collective-permute-start.59 = (bf16[1024,256]{1,0:T(8,128)(2,1)S(1)}, bf16[1024,256]{1,0:T(8,128)(2,1)S(1)}, u32[]{:S(2)}, u32[]{:S(2)}) collective-permute-start(bf16[1024,256]{1,0:T(8,128)(2,1)S(1)} %copy-done.31), channel_id=1, source_target_pairs={{0,1},{1,2},{2,3},{3,0},{4,5},{5,6},{6,7},{7,4},{8,9},{9,10},{10,1... | collective-permute-start | bytes 1572872 | tf_op jit(solution)/shard_map/ppermute | solution.py:87
  303.1 15.4 %collective-permute-start.51 = (bf16[2048,128]{1,0:T(8,128)(2,1)S(1)}, bf16[2048,128]{1,0:T(8,128)(2,1)S(1)}, u32[]{:S(2)}, u32[]{:S(2)}) collective-permute-start(bf16[2048,128]{1,0:T(8,128)(2,1)S(1)} %get-tuple-element.365), channel_id=1, source_target_pairs={{0,8},{4,12},{8,24},{12,28},{24,16},{28,20},{16,0},{20,4},{1,9},{5... | collective-permute-start | bytes 1572872 | tf_op jit(solution)/shard_map/ppermute | solution.py:38
  304.7 29.1 %collective-permute-start.57 = (bf16[4096,128]{1,0:T(8,128)(2,1)S(1)}, bf16[4096,128]{1,0:T(8,128)(2,1)S(1)}, u32[]{:S(2)}, u32[]{:S(2)}) collective-permute-start(bf16[4096,128]{1,0:T(8,128)(2,1)S(1)} %copy-done.62), channel_id=1, source_target_pairs={{0,4},{4,0},{8,12},{12,8},{16,20},{20,16},{24,28},{28,24},{1,5},{5... | collective-permute-start | bytes 3145736 | tf_op jit(solution)/shard_map/ppermute | solution.py:41
  305.0 16.9 %collective-permute-start.52 = (bf16[2048,128]{1,0:T(8,128)(2,1)S(1)}, bf16[2048,128]{1,0:T(8,128)(2,1)S(1)}, u32[]{:S(2)}, u32[]{:S(2)}) collective-permute-start(bf16[2048,128]{1,0:T(8,128)(2,1)S(1)} %get-tuple-element.364), channel_id=1, source_target_pairs={{0,16},{4,20},{8,0},{12,4},{24,8},{28,12},{16,24},{20,28},{1,17},{... | collective-permute-start | bytes 1572872 | tf_op jit(solution)/shard_map/ppermute | solution.py:38
  305.6 22.2 %collective-permute-start.54 = (bf16[2048,128]{1,0:T(8,128)(2,1)S(1)}, bf16[2048,128]{1,0:T(8,128)(2,1)S(1)}, u32[]{:S(2)}, u32[]{:S(2)}) collective-permute-start(bf16[2048,128]{1,0:T(8,128)(2,1)S(1)} %get-tuple-element.363), channel_id=1, source_target_pairs={{0,8},{4,12},{8,24},{12,28},{24,16},{28,20},{16,0},{20,4},{1,9},{5... | collective-permute-start | bytes 1572872 | tf_op jit(solution)/shard_map/ppermute | solution.py:38
  317.5 13.9 %collective-permute-start.55 = (bf16[2048,128]{1,0:T(8,128)(2,1)S(1)}, bf16[2048,128]{1,0:T(8,128)(2,1)S(1)}, u32[]{:S(2)}, u32[]{:S(2)}) collective-permute-start(bf16[2048,128]{1,0:T(8,128)(2,1)S(1)} %get-tuple-element.362), channel_id=1, source_target_pairs={{0,16},{4,20},{8,0},{12,4},{24,8},{28,12},{16,24},{20,28},{1,17},{... | collective-permute-start | bytes 1572872 | tf_op jit(solution)/shard_map/ppermute | solution.py:38
  318.6 17.6 %collective-permute-start.32 = (bf16[1024,256]{1,0:T(8,128)(2,1)S(1)}, bf16[1024,256]{1,0:T(8,128)(2,1)S(1)}, u32[]{:S(2)}, u32[]{:S(2)}) collective-permute-start(bf16[1024,256]{1,0:T(8,128)(2,1)S(1)} %copy-done.33), channel_id=1, source_target_pairs={{0,3},{1,0},{2,1},{3,2},{4,7},{5,4},{6,5},{7,6},{8,11},{9,8},{10,9... | collective-permute-start | bytes 1572872 | tf_op jit(solution)/shard_map/ppermute | solution.py:87
  321.9 15.0 %collective-permute-start.66 = (bf16[128,256]{1,0:T(8,128)(2,1)S(1)}, bf16[128,256]{1,0:T(8,128)(2,1)S(1)}, u32[]{:S(2)}, u32[]{:S(2)}) collective-permute-start(bf16[128,256]{1,0:T(8,128)(2,1)S(1)} %get-tuple-element.348), channel_id=1, source_target_pairs={{0,1},{1,2},{2,3},{3,0},{4,5},{5,6},{6,7},{7,4},{8,9},{9,10},{10,1... | collective-permute-start | bytes 196616 | tf_op jit(solution)/shard_map/ppermute | solution.py:87
  335.7 15.1 %collective-permute-start.60 = (bf16[2048,128]{1,0:T(8,128)(2,1)}, bf16[2048,128]{1,0:T(8,128)(2,1)S(1)}, u32[]{:S(2)}, u32[]{:S(2)}) collective-permute-start(bf16[2048,128]{1,0:T(8,128)(2,1)} %get-tuple-element.360), channel_id=1, source_target_pairs={{0,8},{4,12},{8,24},{12,28},{24,16},{28,20},{16,0},{20,4},{1,9},{5... | collective-permute-start | bytes 1572872 | tf_op jit(solution)/shard_map/ppermute | solution.py:38
  336.2 24.1 %collective-permute-start.61 = (bf16[2048,128]{1,0:T(8,128)(2,1)}, bf16[2048,128]{1,0:T(8,128)(2,1)S(1)}, u32[]{:S(2)}, u32[]{:S(2)}) collective-permute-start(bf16[2048,128]{1,0:T(8,128)(2,1)} %get-tuple-element.361), channel_id=1, source_target_pairs={{0,8},{4,12},{8,24},{12,28},{24,16},{28,20},{16,0},{20,4},{1,9},{5... | collective-permute-start | bytes 1572872 | tf_op jit(solution)/shard_map/ppermute | solution.py:38
  336.9 23.5 %collective-permute-start.62 = (bf16[2048,128]{1,0:T(8,128)(2,1)}, bf16[2048,128]{1,0:T(8,128)(2,1)}, u32[]{:S(2)}, u32[]{:S(2)}) collective-permute-start(bf16[2048,128]{1,0:T(8,128)(2,1)} %get-tuple-element.355), channel_id=1, source_target_pairs={{0,16},{4,20},{8,0},{12,4},{24,8},{28,12},{16,24},{20,28},{1,17},{... | collective-permute-start | bytes 1572872 | tf_op jit(solution)/shard_map/ppermute | solution.py:38
  338.3 22.9 %collective-permute-start.63 = (bf16[2048,128]{1,0:T(8,128)(2,1)}, bf16[2048,128]{1,0:T(8,128)(2,1)}, u32[]{:S(2)}, u32[]{:S(2)}) collective-permute-start(bf16[2048,128]{1,0:T(8,128)(2,1)} %get-tuple-element.354), channel_id=1, source_target_pairs={{0,16},{4,20},{8,0},{12,4},{24,8},{28,12},{16,24},{20,28},{1,17},{... | collective-permute-start | bytes 1572872 | tf_op jit(solution)/shard_map/ppermute | solution.py:38
  (91 other events, 1085.8 us)
Sparse Core Ops, SparseCore 0:
  44.5 67.8 all-gather.2

commit v8 on v7

--- a/solution.py
+++ b/solution.py
@@ -266,8 +266,9 @@
 
 def dense_kernel(parts, chunks, n_earlier, is_first, is_last, meta, *refs):
     n_mixed = parts * chunks
-    mixed_refs, cot_refs, w_hbm = refs[:n_mixed], refs[n_mixed : n_mixed + parts], refs[n_mixed + parts]
-    refs = refs[n_mixed + parts + 1 :]
+    mixed_refs, cot_refs = refs[:n_mixed], refs[n_mixed : n_mixed + parts]
+    w_halves = refs[n_mixed + parts : n_mixed + parts + CORES]
+    refs = refs[n_mixed + parts + CORES :]
     if not is_first:
         sums_hbm, refs = refs[0], refs[1:]
     outs = refs[n_earlier:]
@@ -285,9 +286,12 @@
     def _():
         copies = []
         for i in range(parts):
+            half, at = i // (parts // CORES), i % (parts // CORES)
+            whole_at = lax.rem(meta[1] + half, CORES) * (parts // CORES) + at
+            to = aligned(lax.rem(whole_at + parts - me, parts) * f_wide, f_wide, f_wide)
             for j in range(parts):
-                src = w_hbm.at[place(j), aligned(place(i) * f_wide, f_wide, f_wide)]
-                dst = weight.at[pl.ds(i * f_wide, f_wide), pl.ds(j * h_wide, h_wide)]
+                src = w_halves[half].at[place(j), pl.ds(at * f_wide, f_wide)]
+                dst = weight.at[to, pl.ds(j * h_wide, h_wide)]
                 copies.append(pltpu.make_async_copy(src, dst, sems.at[i * parts + j]))
                 copies[-1].start()
         for copy in copies:
@@ -330,7 +334,7 @@
 def dense(meta, mixed, cot, weight, rows, first, earlier):
     parts, chunks = len(mixed), len(mixed[0])
     width = mixed[0][0][0].shape[1]
-    _, features, h_wide = weight.shape
+    features, h_wide = CORES * weight[0].shape[1], weight[0].shape[2]
     hidden = parts * h_wide
     all_rows = cot[0].shape[0]
     step = min(rows, 256)
@@ -343,7 +347,7 @@
 
     kinds = [(h_wide, True)] * parts + [(width, c > 0) for _ in range(parts) for c in range(chunks)]
     whole_at = [i for i, (_, whole) in enumerate(kinds) if whole]
-    n_inputs = 1 + len(flat) + parts + 1 + len(earlier_sums)
+    n_inputs = 1 + len(flat) + parts + CORES + len(earlier_sums)
     sums_spec = pl.BlockSpec((hidden, features), lambda t, meta: (0, 0)) if is_last else any_spec()
     outs = pl.pallas_call(
         functools.partial(dense_kernel, parts, chunks, len(earlier_whole), is_first, is_last),
@@ -352,7 +356,7 @@
             grid=(rows // step,),
             in_specs=[spec(width, at) for _, at in flat]
             + [spec(h_wide, first)] * parts
-            + [any_spec()] * (1 + len(earlier_sums) + len(earlier_whole)),
+            + [any_spec()] * (CORES + len(earlier_sums) + len(earlier_whole)),
             out_specs=[spec(w, first if whole else 0) for w, whole in kinds] + [sums_spec],
             scratch_shapes=[
                 pltpu.VMEM((features, hidden), BF16),
@@ -371,7 +375,7 @@
             transcendentals=rows * hidden,
         ),
         name="dense",
-    )(meta, *[m for m, _ in flat], *cot, weight, *earlier_sums, *earlier_whole)
+    )(meta, *[m for m, _ in flat], *cot, *weight, *earlier_sums, *earlier_whole)
     n = parts * chunks
     act, back = outs[:parts], outs[parts : parts + n]
     return (
@@ -436,14 +440,13 @@
         self.rows = own_far.shape[0]
         self.half = self.rows // 2
 
-    def swaps(self):
-        far = self.ring.sibling(self.other_far)
-        self.got_near = self.ring.sibling(lax.optimization_barrier((self.other_near, far))[0])
+    def start(self):
+        got = self.ring.sibling(self.other_far)
+        far = [total_of(self.own_far[at : at + self.half], got[at : at + self.half]) for at in (0, self.half)]
+        far = lax.optimization_barrier(far)
+        self.got_near = self.ring.sibling(lax.optimization_barrier((self.other_near, *far))[0])
         self.got_zero = self.ring.sibling(lax.optimization_barrier((self.other_zero, self.got_near))[0])
         return far
-
-    def far_sums(self, got):
-        return [total_of(self.own_far[at : at + self.half], got[at : at + self.half]) for at in (0, self.half)]
 
     def near_sum(self, offset, upper, *more):
         at = self.near.index(offset % self.ring.chips)
@@ -498,12 +501,14 @@
     order = [middle, 0] + near
     terms_at = [ring.device_at(o, other) * rows for other in (False, True) for o in order]
     spmm_t_meta = jnp.stack([rep] + terms_at).astype(jnp.int32)
-    dense_meta = rep[None].astype(jnp.int32)
+    dense_meta = jnp.stack([rep, lax.rem(lax.axis_index("row"), CORES)]).astype(jnp.int32)
 
     def part_of(x, u):
         return lax.dynamic_slice_in_dim(x, lax.rem(rep + u, parts) * part_rows, part_rows, 0)
 
-    w_full = lax.all_gather(weight, "rep", axis=0, tiled=False)
+    w_rows = weight.shape[0] // CORES
+    core = lax.rem(lax.axis_index("row"), CORES)
+    w_half = lax.all_gather(lax.dynamic_slice_in_dim(weight, core * w_rows, w_rows, 0), "rep", axis=0, tiled=False)
 
     cot_blocks = [part_of(cotangent, u) for u in range(parts)]
     xs = [features[:, c * width : (c + 1) * width] for c in range(chunks)]
@@ -560,6 +565,7 @@
     for i in (-2, -1):
         got_other[last, len(offsets) + i] = ring.sibling(got_own[last, len(offsets) + i])
 
+    w.go(w_other=ring.sibling(w.gate(w_half)))
     for h in range(halves):
         w.go(**{f"half{h}": run_spmm(last, halves, h)})
         w.close()
@@ -571,7 +577,7 @@
     for h in range(halves):
         part = ordered(w[f"half{h}"][0], w[f"half_got{h}"])
         blocks = [[(whole[c][u], h * half_rows) for c in range(last)] + [(part[u], 0)] for u in range(parts)]
-        act, back, sums, earlier = dense(dense_meta, blocks, cot, w_full, half_rows, h * half_rows, earlier)
+        act, back, sums, earlier = dense(dense_meta, blocks, cot, (w_half, w["w_other"]), half_rows, h * half_rows, earlier)
         w.go(**{f"back{h}": [b[0] for b in back]})
         if h == halves - 1:
             w.go(whole=(act, back, sums))
@@ -580,6 +586,8 @@
     act, back, sums = w["whole"]
 
     share = sums.shape[0] // row_size
+    first_got = w.pending[f"back_got{halves - 1}"][1]
+    sums = lax.optimization_barrier((sums, first_got))[0]
 
     def sums_for(offset, other):
         return lax.dynamic_slice_in_dim(sums, ring.device_at(offset, other) * share, share, 0)
@@ -593,11 +601,12 @@
         sums_for(0, True),
         jnp.concatenate([sums_for(o, True) for o in near]),
     )
-    wg_far = wg.swaps()
-    w.go(wg=(wg.own_zero, wg.own_near, wg.got_near, wg.got_zero, wg.far_sums(wg_far)))
+    wg_far = wg.hops(*wg.start())
+    w.go(wg=(wg.own_zero, wg.own_near, wg.got_near, wg.got_zero, wg_far))
     w.close()
     wg.own_zero, wg.own_near, wg.got_near, wg.got_zero, wg_far = w["wg"]
-    w.go(wg_far=wg.hops(*wg_far))
+    wg_bound, wg_free = wg.bound_sums(wg_far), wg.free_sums()
+    w.go(wg_got=wg.hops(jnp.concatenate([wg_bound[0], wg_free[0]]), jnp.concatenate([wg_free[1], wg_bound[1]])))
 
     def run_spmm_t(c, grads):
         return spmm_t(tiles, columns, counts, spmm_t_meta, grads, parts, held, rows, rows * row_size)
@@ -607,49 +616,45 @@
     for c in range(1, chunks):
         w.go(**{f"rest_got{c}": send([w.gate(b[c]) for b in back], ends + inner)})
     w.close()
-    wg_bound = wg.bound_sums(w["wg_far"])
-    wg_free = wg.free_sums()
-    wg_got = wg.hops(jnp.concatenate([wg_bound[0], wg_free[0]]), jnp.concatenate([wg_free[1], wg_bound[1]]))
+    wg_got = w["wg_got"]
     wg_got = wg.finish(
         (wg_got[0][wg.half :], wg_got[1][: wg.half]), (wg_got[0][: wg.half], wg_got[1][wg.half :])
     )
+
+    def send_act(shifts, *after):
+        return send([lax.optimization_barrier((a, *after))[0] for a in act], shifts)
 
     reductions = []
     for c in range(chunks):
         terms = w[f"terms{c}"]
         red = Reduction(ring, terms[0], terms[1], terms[2:-3], terms[-3], terms[-2], terms[-1])
         reductions.append(red)
-        far = red.far_sums(red.swaps())
+        far = red.start()
+        w.go(**{f"far{c}": red.hops(*far), f"zero{c}": red.got_zero})
         free = red.free_sums()
-        if c == 0:
-            free = lax.optimization_barrier((free, wg_got))[0]
-        far_hops, free_hops = red.hops(*far), red.hops(*free)
-        w.go(**{f"far{c}": far_hops, f"zero{c}": red.got_zero})
         if c < last:
             grads = ordered(back[0][c + 1], w[f"rest_got{c + 1}"])
             grads = lax.optimization_barrier((grads, free[0][:8], free[1][:8]))[0]
-            w.go(**{f"terms{c + 1}": run_spmm_t(c + 1, grads), f"free{c}": free_hops})
+            w.go(**{f"terms{c + 1}": run_spmm_t(c + 1, grads), f"free{c}": red.hops(*free)})
         if c == 0:
-            act_inner = send([lax.optimization_barrier((a, free[0][:8]))[0] for a in act], inner)
+            w.go(act_inner=send_act(inner, free[0][:8]))
         if c == last:
-            w.go(act_inner=act_inner)
-            low_end = send([lax.optimization_barrier((a, *act_inner.values()))[0] for a in act], ends[:1])
-            w.go(low_end=low_end)
+            w.go(low_end=send_act(ends[:1], far[0][:8]))
         w.close()
-        if c == 0:
-            up, down = (jnp.concatenate(halves_of) for halves_of in wg_got)
-            block = total_of(wg.own_zero, wg.got_zero, up, down)
-            cuts = [w.gate(block[:, u * f_wide : (u + 1) * f_wide]) for u in range(parts)]
-            cuts_got = send(cuts, ends + inner)
-            weight_grad = functools.reduce(
-                lambda a, b: a + b, [v.astype(F32) for v in [cuts[0], *cuts_got.values()]]
-            )
-        red.free_hops = w[f"free{c}"] if c < last else free_hops
+        if c == last:
+            free = [w.gate(f) for f in free]
+        red.free_hops = w[f"free{c}"] if c < last else red.hops(*free)
         bound = red.bound_sums(w[f"far{c}"])
         red.bound_hops = red.hops(*bound)
         if c < last:
             w.go(**{f"bound{c}": red.bound_hops})
-    high_end = send([lax.optimization_barrier((a, bound[0][:8]))[0] for a in act], ends[1:])
+    high_end = send_act(ends[1:], bound[0][:8])
+
+    up, down = (jnp.concatenate(halves_of) for halves_of in wg_got)
+    block = total_of(wg.own_zero, wg.got_zero, up, down)
+    cuts = [lax.optimization_barrier((block, bound[0][:8]))[0][:, u * f_wide : (u + 1) * f_wide] for u in range(parts)]
+    cuts_got = send(cuts, ends + inner)
+    weight_grad = functools.reduce(lambda a, b: a + b, [v.astype(F32) for v in [cuts[0], *cuts_got.values()]])
 
     feature_grad = ()
     for c, red in enumerate(reductions):

time: 374 us -> 356 us (0.952)
  waiting for transfers between devices: 144 us -> 113 us
  starting transfers between devices: 72.3 us -> 80.1 us
    ppermute x27, waiting for transfers between devices: 75.5 us -> 40.1 us  [send(): lax.ppermute(blocks[s], 'rep', [(i, (i + s) % size) for i in range(size)])]
    ppermute x27, starting transfers between devices: 43.3 us -> 48.6 us  [send(): lax.ppermute(blocks[s], 'rep', [(i, (i + s) % size) for i in range(size)])]
    ppermute x18 -> x19, waiting for transfers between devices: 14.7 us -> 15.5 us  [sibling(): return lax.ppermute(value, 'row', [(d, d ^ 1) for d in range(self.devices)])]
  transfers between devices with their start and end apart: 70 -> 71, of which waited for: 26 -> 30; matrix products, arithmetic and copies ran while one was open for 7% -> 6% of each run, Pallas kernels for 26% -> 28%
where the time goes in v8:
time: 356 us; the launch traced here: 355 us
  waiting for transfers between devices  113 us (32%)
  Pallas kernels  103 us (29%)
  starting transfers between devices  80.1 us (22%)
  local copies, waits for them, and re-layouts  25.6 us (7%)
  between operations  22.9 us (6%)
  other arithmetic  10.4 us (3%)
    ppermute x24, waiting for transfers between devices, hop(): return lax.ppermute(value, 'row', self.perm(step))  57.2 us
    ppermute x27, starting transfers between devices, send(): lax.ppermute(blocks[s], 'rep', [(i, (i + s) % size) for i in range(size)])  48.6 us
    ppermute x27, waiting for transfers between devices, send(): lax.ppermute(blocks[s], 'rep', [(i, (i + s) % size) for i in range(size)])  40.1 us
    pallas_call x3, Pallas kernels, spmm(): pl.pallas_call(functools.partial(spmm_kernel, len(pieces), per_part, skip...  36.4 us
    pallas_call x2, Pallas kernels, spmm_t(): pl.pallas_call(functools.partial(spmm_t_kernel, len(grads), per_part, len...  34.5 us
    ppermute x24, starting transfers between devices, hop(): return lax.ppermute(value, 'row', self.perm(step))  28.2 us
    pallas_call x2, Pallas kernels, dense(): pl.pallas_call(functools.partial(dense_kernel, parts, chunks, len(earlier...  23.1 us
    ppermute x19, waiting for transfers between devices, sibling(): return lax.ppermute(value, 'row', [(d, d ^ 1) for d in range(self.devices)])  15.5 us
  transfers between devices with their start and end apart: 71, of which 30 were waited for; matrix products, arithmetic and copies ran while one was open for 6% of the time, Pallas kernels for 28%

profile of v8, /device:TPU:0, one launch (start us, length us, event | category | flops | bytes accessed | tf_op | source)
XLA Modules:
  0.0 354.8 jit_solution(10105059968099665540)
XLA Ops:
  9.4 2.6 collective-permute-start
  12.1 2.9 constant_dynamic-slice_fusion.1
  15.0 4.1 %collective-permute-start.4 = (bf16[1024,256]{1,0:T(8,128)(2,1)}, bf16[1024,256]{1,0:T(8,128)(2,1)S(1)}, u32[]{:S(2)}, u32[]{:S(2)}) collective-permute-start(bf16[1024,256]{1,0:T(8,128)(2,1)} %get-tuple-element.390), channel_id=1, source_target_pairs={{0,3},{1,0},{2,1},{3,2},{4,7},{5,4},{6,5},{7,6},{8,11},{9,8},{10,9... | collective-permute-start | bytes 1572872 | tf_op jit(solution)/shard_map/ppermute | solution.py:87
  30.2 5.8 %collective-permute-done.refs_1_ = bf16[4096,128]{1,0:T(8,128)(2,1)} collective-permute-done((bf16[4096,128]{1,0:T(8,128)(2,1)S(1)}, bf16[4096,128]{1,0:T(8,128)(2,1)}, u32[]{:S(2)}, u32[]{:S(2)}) %collective-permute-start) | collective-permute-done | bytes 1048608 | tf_op jit(solution)/shard_map/ppermute | solution.py:38
  37.9 1.9 slice.164
  45.7 9.3 %collective-permute-done.2.refs_3_ = bf16[2048,128]{1,0:T(8,128)(2,1)} collective-permute-done((bf16[2048,128]{1,0:T(8,128)(2,1)}, bf16[2048,128]{1,0:T(8,128)(2,1)}, u32[]{:S(2)}, u32[]{:S(2)}) %collective-permute-start.2) | collective-permute-done | bytes 524320 | tf_op jit(solution)/shard_map/ppermute | solution.py:38
  58.8 2.7 collective-permute-start.7
  61.5 3.0 fusion
  65.5 14.5 %spmm.3 = (bf16[1024,128]{1,0:T(8,128)(2,1)}, bf16[1024,128]{1,0:T(8,128)(2,1)}, bf16[1024,128]{1,0:T(8,128)(2,1)}, bf16[1024,128]{1,0:T(8,128)(2,1)}) custom-call(s32[32,16]{1,0:T(8,128)} %copy.69.cols, s32[32]{0:T(128)} %counts.9, s32[11]{0:T(128)} %stack.82.meta, bf16[32,16,128,128]{3,2,1,0:T(8,128)(2,1)} %tiles.9, bf16[4096,128]{1,0:T(8,128)(2,1)} %copy-done.7, ...), custom_call_target="tpu_custom_call" | custom-call | flops 2147483648 | bytes 25165824 | tf_op jit(solution)/shard_map/spmm/pallas_call | solution.py:158
  80.0 14.8 %collective-permute-done.7.refs_10_ = bf16[1024,256]{1,0:T(8,128)(2,1)S(1)} collective-permute-done((bf16[1024,256]{1,0:T(8,128)(2,1)}, bf16[1024,256]{1,0:T(8,128)(2,1)S(1)}, u32[]{:S(2)}, u32[]{:S(2)}) %collective-permute-start.7) | collective-permute-done | bytes 524320 | tf_op jit(solution)/shard_map/ppermute | solution.py:87
  100.0 3.8 %collective-permute-start.18 = (bf16[1024,128]{1,0:T(8,128)(2,1)S(1)}, bf16[1024,128]{1,0:T(8,128)(2,1)}, u32[]{:S(2)}, u32[]{:S(2)}) collective-permute-start(bf16[1024,128]{1,0:T(8,128)(2,1)S(1)} %copy-done.59), channel_id=1, source_target_pairs={{0,3},{1,0},{2,1},{3,2},{4,7},{5,4},{6,5},{7,6},{8,11},{9,8},{10,9... | collective-permute-start | bytes 786440 | tf_op jit(solution)/shard_map/ppermute | solution.py:87
  103.8 6.1 %collective-permute-done.14.refs_3_ = bf16[2048,128]{1,0:T(8,128)(2,1)S(1)} collective-permute-done((bf16[2048,128]{1,0:T(8,128)(2,1)S(1)}, bf16[2048,128]{1,0:T(8,128)(2,1)S(1)}, u32[]{:S(2)}, u32[]{:S(2)}) %collective-permute-start.14) | collective-permute-done | bytes 524320 | tf_op jit(solution)/shard_map/ppermute | solution.py:38
  111.0 3.1 collective-permute-done.18.refs_2_
  114.6 2.3 collective-permute-start.20
  119.1 11.0 %spmm.4 = (bf16[512,128]{1,0:T(8,128)(2,1)}, bf16[512,128]{1,0:T(8,128)(2,1)}, bf16[512,128]{1,0:T(8,128)(2,1)}, bf16[512,128]{1,0:T(8,128)(2,1)}) custom-call(s32[32,16]{1,0:T(8,128)} %copy.69.cols, s32[32]{0:T(128)} %counts.9, s32[11]{0:T(128)} %stack.82.meta, bf16[32,16,128,128]{3,2,1,0:T(8,128)(2,1)} %tiles.9, bf16[4096,128]{1,0:T(8,128)(2,1)} %copy-done.2, ...), custom_call_target="tpu_custom_call" | custom-call | flops 1073741824 | bytes 16777216 | tf_op jit(solution)/shard_map/spmm/pallas_call | solution.py:158
  130.1 2.1 collective-permute-start.24
  132.6 1.9 collective-permute-start.26
  134.5 11.0 %spmm.5 = (bf16[512,128]{1,0:T(8,128)(2,1)}, bf16[512,128]{1,0:T(8,128)(2,1)}, bf16[512,128]{1,0:T(8,128)(2,1)}, bf16[512,128]{1,0:T(8,128)(2,1)}) custom-call(s32[32,16]{1,0:T(8,128)} %copy.69.cols, s32[32]{0:T(128)} %counts.9, s32[11]{0:T(128)} %stack.82.meta, bf16[32,16,128,128]{3,2,1,0:T(8,128)(2,1)} %tiles.9, bf16[4096,128]{1,0:T(8,128)(2,1)} %copy-done.2, ...), custom_call_target="tpu_custom_call" | custom-call | flops 1073741824 | bytes 16777216 | tf_op jit(solution)/shard_map/spmm/pallas_call | solution.py:158
  145.6 1.9 collective-permute-start.27
  149.3 11.1 %dense.2 = (bf16[1024,256]{1,0:T(8,128)(2,1)}, bf16[1024,256]{1,0:T(8,128)(2,1)}, bf16[1024,256]{1,0:T(8,128)(2,1)}, bf16[1024,256]{1,0:T(8,128)(2,1)}, bf16[512...) custom-call(s32[2]{0:T(128)} %pad_add_fusion.meta, ...), custom_call_target="tpu_custom_call" | custom-call | flops 3221225472 | bytes 10485760 | tf_op jit(solution)/shard_map/dense/pallas_call | solution.py:352
  160.5 2.8 collective-permute-start.30
  164.1 12.0 %dense.3 = (bf16[1024,256]{1,0:T(8,128)(2,1)}, bf16[1024,256]{1,0:T(8,128)(2,1)}, bf16[1024,256]{1,0:T(8,128)(2,1)}, bf16[1024,256]{1,0:T(8,128)(2,1)}, bf16[512...) custom-call(s32[2]{0:T(128)} %pad_add_fusion.meta, ...), custom_call_target="tpu_custom_call", output_to_operand_aliasing={{0}: (16, {}), {1}: (17, {}), {2}: (18, {}), {3}: (19, {}),... | custom-call | flops 3221225472 | bytes 10485760 | tf_op jit(solution)/shard_map/dense/pallas_call | solution.py:352
  176.2 3.5 collective-permute-start.33
  179.7 2.8 collective-permute-done.33.refs_3_
  182.5 1.7 constant_dynamic-slice_fusion.10
  187.0 1.8 collective-permute-done.37
  190.0 3.6 %collective-permute-start.35 = (bf16[512,128]{1,0:T(8,128)(2,1)}, bf16[512,128]{1,0:T(8,128)(2,1)S(1)}, u32[]{:S(2)}, u32[]{:S(2)}) collective-permute-start(bf16[512,128]{1,0:T(8,128)(2,1)} %get-tuple-element.269), channel_id=1, source_target_pairs={{0,1},{1,2},{2,3},{3,0},{4,5},{5,6},{6,7},{7,4},{8,9},{9,10},{10,1... | collective-permute-start | bytes 393224 | tf_op jit(solution)/shard_map/ppermute | solution.py:87
  195.7 5.8 %collective-permute-done.34.refs_5_ = bf16[512,128]{1,0:T(8,128)(2,1)S(1)} collective-permute-done((bf16[512,128]{1,0:T(8,128)(2,1)}, bf16[512,128]{1,0:T(8,128)(2,1)S(1)}, u32[]{:S(2)}, u32[]{:S(2)}) %collective-permute-start.34) | collective-permute-done | bytes 131104 | tf_op jit(solution)/shard_map/ppermute | solution.py:87
  202.7 2.8 collective-permute-start.43
  208.0 17.2 %spmm_t.2 = (bf16[4096,128]{1,0:T(8,128)(2,1)}, bf16[4096,128]{1,0:T(8,128)(2,1)}, bf16[4096,128]{1,0:T(8,128)(2,1)}, bf16[4096,128]{1,0:T(8,128)(2,1)}, bf16[40...) custom-call(s32[32,16]{1,0:T(8,128)} %copy.69.cols, s32[32]{0:T(128)} %counts.9, ...), custom_call_target="tpu_custom_call" | custom-call | flops 2147483648 | bytes 25165824 | tf_op jit(solution)/shard_map/spmm_t/pallas_call | solution.py:241
  225.4 2.9 collective-permute-done.46
  228.2 2.3 add_convert_fusion.10
  232.1 2.8 collective-permute-done.49
  238.4 1.8 collective-permute-start.53
  240.3 5.1 %collective-permute-done.47 = bf16[2048,128]{1,0:T(8,128)(2,1)S(1)} collective-permute-done((bf16[2048,128]{1,0:T(8,128)(2,1)S(1)}, bf16[2048,128]{1,0:T(8,128)(2,1)S(1)}, u32[]{:S(2)}, u32[]{:S(2)}) %collective-permute-start.47) | collective-permute-done | bytes 524320 | tf_op jit(solution)/shard_map/ppermute | solution.py:38
  247.7 17.4 %spmm_t.3 = (bf16[4096,128]{1,0:T(8,128)(2,1)}, bf16[4096,128]{1,0:T(8,128)(2,1)}, bf16[4096,128]{1,0:T(8,128)(2,1)}, bf16[4096,128]{1,0:T(8,128)(2,1)}, bf16[40...) custom-call(s32[32,16]{1,0:T(8,128)} %copy.69.cols, s32[32]{0:T(128)} %counts.9, ...), custom_call_target="tpu_custom_call" | custom-call | flops 2147483648 | bytes 25165824 | tf_op jit(solution)/shard_map/spmm_t/pallas_call | solution.py:241
  265.3 2.9 collective-permute-done.54
  269.8 2.5 collective-permute-start.61
  278.1 7.7 %collective-permute-done.61 = bf16[1024,256]{1,0:T(8,128)(2,1)S(1)} collective-permute-done((bf16[1024,256]{1,0:T(8,128)(2,1)S(1)}, bf16[1024,256]{1,0:T(8,128)(2,1)S(1)}, u32[]{:S(2)}, u32[]{:S(2)}) %collective-permute-start.61) | collective-permute-done | bytes 524320 | tf_op jit(solution)/shard_map/ppermute | solution.py:87
  287.5 2.8 collective-permute-done.56.refs_2_
  290.9 10.1 %collective-permute-done.58 = bf16[2048,128]{1,0:T(8,128)(2,1)S(1)} collective-permute-done((bf16[2048,128]{1,0:T(8,128)(2,1)S(1)}, bf16[2048,128]{1,0:T(8,128)(2,1)S(1)}, u32[]{:S(2)}, u32[]{:S(2)}) %collective-permute-start.58) | collective-permute-done | bytes 524320 | tf_op jit(solution)/shard_map/ppermute | solution.py:38
  303.0 3.5 collective-permute-start.62
  306.5 3.8 %collective-permute-start.68 = (bf16[128,256]{1,0:T(8,128)(2,1)S(1)}, bf16[128,256]{1,0:T(8,128)(2,1)S(1)}, u32[]{:S(2)}, u32[]{:S(2)}) collective-permute-start(bf16[128,256]{1,0:T(8,128)(2,1)S(1)} %get-tuple-element.405), channel_id=1, source_target_pairs={{0,3},{1,0},{2,1},{3,2},{4,7},{5,4},{6,5},{7,6},{8,11},{9,8},{10,9... | collective-permute-start | bytes 196616 | tf_op jit(solution)/shard_map/ppermute | solution.py:87
  312.1 4.3 %feature_grad.2.refs_0_ = bf16[4096,128]{1,0:T(8,128)(2,1)} custom-call(bf16[4096,128]{1,0:T(8,128)(2,1)} %get-tuple-element.346.refs_0_, bf16[4096,128]{1,0:T(8,128)(2,1)} %copy-done.14, bf16[2048,128]{1,0:T(8,128)(2,1)} %copy-done.24, bf16[2048,128]{1,0:T(8,128)(2,1)} %copy-done.22, bf16[2048,128]{1,0:T(8,128)(2,1)} %copy-done.23, bf16[2048,128]{1,0:T(8,128)(2,1)} %copy-done.25), custom_call_target="tpu_custom_call" | custom-call | flops 2097152 | bytes 7340032 | tf_op jit(solution)/shard_map/feature_grad/pallas_call | solution.py:422
  316.3 4.6 %collective-permute-done.67 = bf16[128,256]{1,0:T(8,128)(2,1)S(1)} collective-permute-done((bf16[128,256]{1,0:T(8,128)(2,1)S(1)}, bf16[128,256]{1,0:T(8,128)(2,1)S(1)}, u32[]{:S(2)}, u32[]{:S(2)}) %collective-permute-start.67) | collective-permute-done | bytes 65568 | tf_op jit(solution)/shard_map/ppermute | solution.py:87
  329.5 6.6 %collective-permute-done.65.refs_5_ = bf16[2048,128]{1,0:T(8,128)(2,1)} collective-permute-done((bf16[2048,128]{1,0:T(8,128)(2,1)}, bf16[2048,128]{1,0:T(8,128)(2,1)}, u32[]{:S(2)}, u32[]{:S(2)}) %collective-permute-start.65) | collective-permute-done | bytes 524320 | tf_op jit(solution)/shard_map/ppermute | solution.py:38
  336.1 7.0 %collective-permute-done.66.refs_6_ = bf16[2048,128]{1,0:T(8,128)(2,1)} collective-permute-done((bf16[2048,128]{1,0:T(8,128)(2,1)S(1)}, bf16[2048,128]{1,0:T(8,128)(2,1)}, u32[]{:S(2)}, u32[]{:S(2)}) %collective-permute-start.66) | collective-permute-done | bytes 524320 | tf_op jit(solution)/shard_map/ppermute | solution.py:38
  343.2 4.7 %feature_grad.3 = bf16[4096,256]{1,0:T(8,128)(2,1)} custom-call(bf16[4096,128]{1,0:T(8,128)(2,1)} %feature_grad.2.refs_0_, bf16[4096,128]{1,0:T(8,128)(2,1)} %get-tuple-element.352.refs_1_, bf16[4096,128]{1,0:T(8,128)(2,1)} %collective-permute-done.60.refs_2_, bf16[2048,128]{1,0:T(8,128)(2,1)} %collective-permute-done.63.refs_3_, ...), custom_call_target="tpu_custom_call" | custom-call | flops 2097152 | bytes 7340032 | tf_op jit(solution)/shard_map/feature_grad/pallas_call | solution.py:422
  (266 shorter events, 69.5 us)
Async XLA Ops:
  7.2 106.9 %all-gather.3.cloned.1.call-start = ((), (), s32[]{:S(2)}) async-start(), calls=%async_computation | async-start | bytes 1310720 | tf_op jit(solution)/shard_map/all_gather | solution.py:511
  7.2 48.8 %collective-permute-start.6 = (bf16[4096,256]{1,0:T(8,128)(2,1)}, bf16[4096,256]{1,0:T(8,128)(2,1)}, u32[]{:S(2)}, u32[]{:S(2)}) collective-permute-start(bf16[4096,256]{1,0:T(8,128)(2,1)} %param.58), channel_id=1, source_target_pairs={{0,4},{4,0},{8,12},{12,8},{16,20},{20,16},{24,28},{28,24},{1,5},{5... | collective-permute-start | bytes 6291464 | tf_op jit(solution)/shard_map/ppermute | solution.py:41
  9.4 26.5 %collective-permute-start = (bf16[4096,128]{1,0:T(8,128)(2,1)S(1)}, bf16[4096,128]{1,0:T(8,128)(2,1)}, u32[]{:S(2)}, u32[]{:S(2)}) collective-permute-start(bf16[4096,128]{1,0:T(8,128)(2,1)S(1)} %get-tuple-element.396.refs_0_), channel_id=1, source_target_pairs={{0,8},{4,12},{8,24},{12,28},{24,16},{28,20},{16,0},{20,4},{1,9},{5... | collective-permute-start | bytes 3145736 | tf_op jit(solution)/shard_map/ppermute | solution.py:38
  12.0 25.4 %collective-permute-start.1 = (bf16[4096,128]{1,0:T(8,128)(2,1)S(1)}, bf16[4096,128]{1,0:T(8,128)(2,1)}, u32[]{:S(2)}, u32[]{:S(2)}) collective-permute-start(bf16[4096,128]{1,0:T(8,128)(2,1)S(1)} %get-tuple-element.396.refs_0_), channel_id=1, source_target_pairs={{0,16},{4,20},{8,0},{12,4},{24,8},{28,12},{16,24},{20,28},{1,17},{... | collective-permute-start | bytes 3145736 | tf_op jit(solution)/shard_map/ppermute | solution.py:38
  15.0 25.8 %collective-permute-start.4 = (bf16[1024,256]{1,0:T(8,128)(2,1)}, bf16[1024,256]{1,0:T(8,128)(2,1)S(1)}, u32[]{:S(2)}, u32[]{:S(2)}) collective-permute-start(bf16[1024,256]{1,0:T(8,128)(2,1)} %get-tuple-element.390), channel_id=1, source_target_pairs={{0,3},{1,0},{2,1},{3,2},{4,7},{5,4},{6,5},{7,6},{8,11},{9,8},{10,9... | collective-permute-start | bytes 1572872 | tf_op jit(solution)/shard_map/ppermute | solution.py:87
  19.1 23.7 %collective-permute-start.5 = (bf16[1024,256]{1,0:T(8,128)(2,1)}, bf16[1024,256]{1,0:T(8,128)(2,1)}, u32[]{:S(2)}, u32[]{:S(2)}) collective-permute-start(bf16[1024,256]{1,0:T(8,128)(2,1)} %get-tuple-element.392), channel_id=1, source_target_pairs={{0,1},{1,2},{2,3},{3,0},{4,5},{5,6},{6,7},{7,4},{8,9},{9,10},{10,1... | collective-permute-start | bytes 1572872 | tf_op jit(solution)/shard_map/ppermute | solution.py:87
  37.4 21.5 %collective-permute-start.10 = (bf16[4096,128]{1,0:T(8,128)(2,1)}, bf16[4096,128]{1,0:T(8,128)(2,1)}, u32[]{:S(2)}, u32[]{:S(2)}) collective-permute-start(bf16[4096,128]{1,0:T(8,128)(2,1)} %collective-permute-done.refs_1_), channel_id=1, source_target_pairs={{0,4},{4,0},{8,12},{12,8},{16,20},{20,16},{24,28},{28,24},{1,5},{5... | collective-permute-start | bytes 3145736 | tf_op jit(solution)/shard_map/ppermute | solution.py:41
  37.4 21.5 %collective-permute-start.11 = (bf16[4096,128]{1,0:T(8,128)(2,1)}, bf16[4096,128]{1,0:T(8,128)(2,1)}, u32[]{:S(2)}, u32[]{:S(2)}) collective-permute-start(bf16[4096,128]{1,0:T(8,128)(2,1)} %collective-permute-done.1.refs_2_), channel_id=1, source_target_pairs={{0,4},{4,0},{8,12},{12,8},{16,20},{20,16},{24,28},{28,24},{1,5},{5... | collective-permute-start | bytes 3145736 | tf_op jit(solution)/shard_map/ppermute | solution.py:41
  40.9 14.2 %collective-permute-start.2 = (bf16[2048,128]{1,0:T(8,128)(2,1)}, bf16[2048,128]{1,0:T(8,128)(2,1)}, u32[]{:S(2)}, u32[]{:S(2)}) collective-permute-start(bf16[2048,128]{1,0:T(8,128)(2,1)} %slice.164), channel_id=1, source_target_pairs={{0,8},{4,12},{8,24},{12,28},{24,16},{28,20},{16,0},{20,4},{1,9},{5... | collective-permute-start | bytes 1572872 | tf_op jit(solution)/shard_map/ppermute | solution.py:38
  42.8 13.2 %collective-permute-start.3 = (bf16[2048,128]{1,0:T(8,128)(2,1)S(1)}, bf16[2048,128]{1,0:T(8,128)(2,1)S(1)}, u32[]{:S(2)}, u32[]{:S(2)}) collective-permute-start(bf16[2048,128]{1,0:T(8,128)(2,1)S(1)} %slice.165), channel_id=1, source_target_pairs={{0,16},{4,20},{8,0},{12,4},{24,8},{28,12},{16,24},{20,28},{1,17},{... | collective-permute-start | bytes 1572872 | tf_op jit(solution)/shard_map/ppermute | solution.py:38
  56.8 38.0 %collective-permute-start.8 = (bf16[4096,128]{1,0:T(8,128)(2,1)S(1)}, bf16[4096,128]{1,0:T(8,128)(2,1)S(1)}, u32[]{:S(2)}, u32[]{:S(2)}) collective-permute-start(bf16[4096,128]{1,0:T(8,128)(2,1)S(1)} %get-tuple-element.187.refs_0_), channel_id=1, source_target_pairs={{0,8},{4,12},{8,24},{12,28},{24,16},{28,20},{16,0},{20,4},{1,9},{5... | collective-permute-start | bytes 3145736 | tf_op jit(solution)/shard_map/ppermute | solution.py:38
  58.0 36.8 %collective-permute-start.9 = (bf16[4096,128]{1,0:T(8,128)(2,1)S(1)}, bf16[4096,128]{1,0:T(8,128)(2,1)S(1)}, u32[]{:S(2)}, u32[]{:S(2)}) collective-permute-start(bf16[4096,128]{1,0:T(8,128)(2,1)S(1)} %get-tuple-element.187.refs_0_), channel_id=1, source_target_pairs={{0,16},{4,20},{8,0},{12,4},{24,8},{28,12},{16,24},{20,28},{1,17},{... | collective-permute-start | bytes 3145736 | tf_op jit(solution)/shard_map/ppermute | solution.py:38
  58.8 35.9 %collective-permute-start.7 = (bf16[1024,256]{1,0:T(8,128)(2,1)}, bf16[1024,256]{1,0:T(8,128)(2,1)S(1)}, u32[]{:S(2)}, u32[]{:S(2)}) collective-permute-start(bf16[1024,256]{1,0:T(8,128)(2,1)} %get-tuple-element.186), channel_id=1, source_target_pairs={{0,2},{1,3},{2,0},{3,1},{4,6},{5,7},{6,4},{7,5},{8,10},{9,11},{10,... | collective-permute-start | bytes 1572872 | tf_op jit(solution)/shard_map/ppermute | solution.py:87
  96.0 13.9 %collective-permute-start.14 = (bf16[2048,128]{1,0:T(8,128)(2,1)S(1)}, bf16[2048,128]{1,0:T(8,128)(2,1)S(1)}, u32[]{:S(2)}, u32[]{:S(2)}) collective-permute-start(bf16[2048,128]{1,0:T(8,128)(2,1)S(1)} %slice.168), channel_id=1, source_target_pairs={{0,8},{4,12},{8,24},{12,28},{24,16},{28,20},{16,0},{20,4},{1,9},{5... | collective-permute-start | bytes 1572872 | tf_op jit(solution)/shard_map/ppermute | solution.py:38
  97.5 13.5 %collective-permute-start.15 = (bf16[2048,128]{1,0:T(8,128)(2,1)S(1)}, bf16[2048,128]{1,0:T(8,128)(2,1)S(1)}, u32[]{:S(2)}, u32[]{:S(2)}) collective-permute-start(bf16[2048,128]{1,0:T(8,128)(2,1)S(1)} %slice.169), channel_id=1, source_target_pairs={{0,16},{4,20},{8,0},{12,4},{24,8},{28,12},{16,24},{20,28},{1,17},{... | collective-permute-start | bytes 1572872 | tf_op jit(solution)/shard_map/ppermute | solution.py:38
  100.0 14.1 %collective-permute-start.18 = (bf16[1024,128]{1,0:T(8,128)(2,1)S(1)}, bf16[1024,128]{1,0:T(8,128)(2,1)}, u32[]{:S(2)}, u32[]{:S(2)}) collective-permute-start(bf16[1024,128]{1,0:T(8,128)(2,1)S(1)} %copy-done.59), channel_id=1, source_target_pairs={{0,3},{1,0},{2,1},{3,2},{4,7},{5,4},{6,5},{7,6},{8,11},{9,8},{10,9... | collective-permute-start | bytes 786440 | tf_op jit(solution)/shard_map/ppermute | solution.py:87
  114.1 16.0 %collective-permute-start.21 = (bf16[4,512,256]{2,1,0:T(8,128)(2,1)}, bf16[4,512,256]{2,1,0:T(8,128)(2,1)S(1)}, u32[]{:S(2)}, u32[]{:S(2)}) collective-permute-start(bf16[4,512,256]{2,1,0:T(8,128)(2,1)} %bitcast.27), channel_id=1, source_target_pairs={{0,4},{4,0},{8,12},{12,8},{16,20},{20,16},{24,28},{28,24},{1,5},{5... | collective-permute-start | bytes 3145736 | tf_op jit(solution)/shard_map/ppermute | solution.py:41
  114.6 15.4 %collective-permute-start.20 = (bf16[1024,128]{1,0:T(8,128)(2,1)}, bf16[1024,128]{1,0:T(8,128)(2,1)S(1)}, u32[]{:S(2)}, u32[]{:S(2)}) collective-permute-start(bf16[1024,128]{1,0:T(8,128)(2,1)} %get-tuple-element.202), channel_id=1, source_target_pairs={{0,2},{1,3},{2,0},{3,1},{4,6},{5,7},{6,4},{7,5},{8,10},{9,11},{10,... | collective-permute-start | bytes 786440 | tf_op jit(solution)/shard_map/ppermute | solution.py:87
  130.1 15.4 %collective-permute-start.24 = (bf16[512,128]{1,0:T(8,128)(2,1)}, bf16[512,128]{1,0:T(8,128)(2,1)S(1)}, u32[]{:S(2)}, u32[]{:S(2)}) collective-permute-start(bf16[512,128]{1,0:T(8,128)(2,1)} %get-tuple-element.209), channel_id=1, source_target_pairs={{0,3},{1,0},{2,1},{3,2},{4,7},{5,4},{6,5},{7,6},{8,11},{9,8},{10,9... | collective-permute-start | bytes 393224 | tf_op jit(solution)/shard_map/ppermute | solution.py:87
  132.2 13.4 %collective-permute-start.25 = (bf16[512,128]{1,0:T(8,128)(2,1)}, bf16[512,128]{1,0:T(8,128)(2,1)S(1)}, u32[]{:S(2)}, u32[]{:S(2)}) collective-permute-start(bf16[512,128]{1,0:T(8,128)(2,1)} %get-tuple-element.210), channel_id=1, source_target_pairs={{0,2},{1,3},{2,0},{3,1},{4,6},{5,7},{6,4},{7,5},{8,10},{9,11},{10,... | collective-permute-start | bytes 393224 | tf_op jit(solution)/shard_map/ppermute | solution.py:87
  132.6 13.0 %collective-permute-start.26 = (bf16[512,128]{1,0:T(8,128)(2,1)}, bf16[512,128]{1,0:T(8,128)(2,1)S(1)}, u32[]{:S(2)}, u32[]{:S(2)}) collective-permute-start(bf16[512,128]{1,0:T(8,128)(2,1)} %get-tuple-element.211), channel_id=1, source_target_pairs={{0,1},{1,2},{2,3},{3,0},{4,5},{5,6},{6,7},{7,4},{8,9},{9,10},{10,1... | collective-permute-start | bytes 393224 | tf_op jit(solution)/shard_map/ppermute | solution.py:87
  145.6 14.8 %collective-permute-start.27 = (bf16[512,128]{1,0:T(8,128)(2,1)}, bf16[512,128]{1,0:T(8,128)(2,1)S(1)}, u32[]{:S(2)}, u32[]{:S(2)}) collective-permute-start(bf16[512,128]{1,0:T(8,128)(2,1)} %get-tuple-element.216), channel_id=1, source_target_pairs={{0,3},{1,0},{2,1},{3,2},{4,7},{5,4},{6,5},{7,6},{8,11},{9,8},{10,9... | collective-permute-start | bytes 393224 | tf_op jit(solution)/shard_map/ppermute | solution.py:87
  160.5 15.6 %collective-permute-start.30 = (bf16[512,128]{1,0:T(8,128)(2,1)}, bf16[512,128]{1,0:T(8,128)(2,1)S(1)}, u32[]{:S(2)}, u32[]{:S(2)}) collective-permute-start(bf16[512,128]{1,0:T(8,128)(2,1)} %get-tuple-element.236), channel_id=1, source_target_pairs={{0,3},{1,0},{2,1},{3,2},{4,7},{5,4},{6,5},{7,6},{8,11},{9,8},{10,9... | collective-permute-start | bytes 393224 | tf_op jit(solution)/shard_map/ppermute | solution.py:87
  201.5 23.7 %collective-permute-start.45 = (bf16[1024,128]{1,0:T(8,128)(2,1)S(1)}, bf16[1024,128]{1,0:T(8,128)(2,1)S(1)}, u32[]{:S(2)}, u32[]{:S(2)}) collective-permute-start(bf16[1024,128]{1,0:T(8,128)(2,1)S(1)} %copy-done.41), channel_id=1, source_target_pairs={{0,1},{1,2},{2,3},{3,0},{4,5},{5,6},{6,7},{7,4},{8,9},{9,10},{10,1... | collective-permute-start | bytes 786440 | tf_op jit(solution)/shard_map/ppermute | solution.py:87
  201.6 23.6 %collective-permute-start.44 = (bf16[1024,128]{1,0:T(8,128)(2,1)S(1)}, bf16[1024,128]{1,0:T(8,128)(2,1)S(1)}, u32[]{:S(2)}, u32[]{:S(2)}) collective-permute-start(bf16[1024,128]{1,0:T(8,128)(2,1)S(1)} %copy-done.42), channel_id=1, source_target_pairs={{0,2},{1,3},{2,0},{3,1},{4,6},{5,7},{6,4},{7,5},{8,10},{9,11},{10,... | collective-permute-start | bytes 786440 | tf_op jit(solution)/shard_map/ppermute | solution.py:87
  202.7 22.5 %collective-permute-start.43 = (bf16[1024,128]{1,0:T(8,128)(2,1)S(1)}, bf16[1024,128]{1,0:T(8,128)(2,1)S(1)}, u32[]{:S(2)}, u32[]{:S(2)}) collective-permute-start(bf16[1024,128]{1,0:T(8,128)(2,1)S(1)} %copy-done.43), channel_id=1, source_target_pairs={{0,3},{1,0},{2,1},{3,2},{4,7},{5,4},{6,5},{7,6},{8,11},{9,8},{10,9... | collective-permute-start | bytes 786440 | tf_op jit(solution)/shard_map/ppermute | solution.py:87
  205.8 19.4 %collective-permute-start.42 = (bf16[128,1024]{1,0:T(8,128)(2,1)S(1)}, bf16[128,1024]{1,0:T(8,128)(2,1)S(1)}, u32[]{:S(2)}, u32[]{:S(2)}) collective-permute-start(bf16[128,1024]{1,0:T(8,128)(2,1)S(1)} %pad_maximum_fusion.2), channel_id=1, source_target_pairs={{0,16},{4,20},{8,0},{12,4},{24,8},{28,12},{16,24},{20,28},{1,17},{... | collective-permute-start | bytes 786440 | tf_op jit(solution)/shard_map/ppermute | solution.py:38
  207.4 17.9 %collective-permute-start.41 = (bf16[128,1024]{1,0:T(8,128)(2,1)S(1)}, bf16[128,1024]{1,0:T(8,128)(2,1)S(1)}, u32[]{:S(2)}, u32[]{:S(2)}) collective-permute-start(bf16[128,1024]{1,0:T(8,128)(2,1)S(1)} %pad_maximum_fusion.1), channel_id=1, source_target_pairs={{0,8},{4,12},{8,24},{12,28},{24,16},{28,20},{16,0},{20,4},{1,9},{5... | collective-permute-start | bytes 786440 | tf_op jit(solution)/shard_map/ppermute | solution.py:38
  230.6 14.8 %collective-permute-start.47 = (bf16[2048,128]{1,0:T(8,128)(2,1)S(1)}, bf16[2048,128]{1,0:T(8,128)(2,1)S(1)}, u32[]{:S(2)}, u32[]{:S(2)}) collective-permute-start(bf16[2048,128]{1,0:T(8,128)(2,1)S(1)} %get-tuple-element.305), channel_id=1, source_target_pairs={{0,8},{4,12},{8,24},{12,28},{24,16},{28,20},{16,0},{20,4},{1,9},{5... | collective-permute-start | bytes 1572872 | tf_op jit(solution)/shard_map/ppermute | solution.py:38
  234.9 30.3 %collective-permute-start.50 = (bf16[4096,128]{1,0:T(8,128)(2,1)}, bf16[4096,128]{1,0:T(8,128)(2,1)S(1)}, u32[]{:S(2)}, u32[]{:S(2)}) collective-permute-start(bf16[4096,128]{1,0:T(8,128)(2,1)} %get-tuple-element.310), channel_id=1, source_target_pairs={{0,4},{4,0},{8,12},{12,8},{16,20},{20,16},{24,28},{28,24},{1,5},{5... | collective-permute-start | bytes 3145736 | tf_op jit(solution)/shard_map/ppermute | solution.py:41
  235.0 30.1 %collective-permute-start.48 = (bf16[2048,128]{1,0:T(8,128)(2,1)}, bf16[2048,128]{1,0:T(8,128)(2,1)}, u32[]{:S(2)}, u32[]{:S(2)}) collective-permute-start(bf16[2048,128]{1,0:T(8,128)(2,1)} %get-tuple-element.306), channel_id=1, source_target_pairs={{0,16},{4,20},{8,0},{12,4},{24,8},{28,12},{16,24},{20,28},{1,17},{... | collective-permute-start | bytes 1572872 | tf_op jit(solution)/shard_map/ppermute | solution.py:38
  237.8 27.3 %collective-permute-start.51 = (bf16[2048,128]{1,0:T(8,128)(2,1)}, bf16[2048,128]{1,0:T(8,128)(2,1)S(1)}, u32[]{:S(2)}, u32[]{:S(2)}) collective-permute-start(bf16[2048,128]{1,0:T(8,128)(2,1)} %get-tuple-element.379), channel_id=1, source_target_pairs={{0,8},{4,12},{8,24},{12,28},{24,16},{28,20},{16,0},{20,4},{1,9},{5... | collective-permute-start | bytes 1572872 | tf_op jit(solution)/shard_map/ppermute | solution.py:38
  238.4 26.7 %collective-permute-start.53 = (bf16[1024,256]{1,0:T(8,128)(2,1)S(1)}, bf16[1024,256]{1,0:T(8,128)(2,1)S(1)}, u32[]{:S(2)}, u32[]{:S(2)}) collective-permute-start(bf16[1024,256]{1,0:T(8,128)(2,1)S(1)} %copy-done.28), channel_id=1, source_target_pairs={{0,2},{1,3},{2,0},{3,1},{4,6},{5,7},{6,4},{7,5},{8,10},{9,11},{10,... | collective-permute-start | bytes 1572872 | tf_op jit(solution)/shard_map/ppermute | solution.py:87
  246.2 18.9 %collective-permute-start.52 = (bf16[2048,128]{1,0:T(8,128)(2,1)}, bf16[2048,128]{1,0:T(8,128)(2,1)S(1)}, u32[]{:S(2)}, u32[]{:S(2)}) collective-permute-start(bf16[2048,128]{1,0:T(8,128)(2,1)} %get-tuple-element.378), channel_id=1, source_target_pairs={{0,16},{4,20},{8,0},{12,4},{24,8},{28,12},{16,24},{20,28},{1,17},{... | collective-permute-start | bytes 1572872 | tf_op jit(solution)/shard_map/ppermute | solution.py:38
  269.8 16.0 %collective-permute-start.61 = (bf16[1024,256]{1,0:T(8,128)(2,1)S(1)}, bf16[1024,256]{1,0:T(8,128)(2,1)S(1)}, u32[]{:S(2)}, u32[]{:S(2)}) collective-permute-start(bf16[1024,256]{1,0:T(8,128)(2,1)S(1)} %copy-done.27), channel_id=1, source_target_pairs={{0,1},{1,2},{2,3},{3,0},{4,5},{5,6},{6,7},{7,4},{8,9},{9,10},{10,1... | collective-permute-start | bytes 1572872 | tf_op jit(solution)/shard_map/ppermute | solution.py:87
  273.9 27.4 %collective-permute-start.60 = (bf16[4096,128]{1,0:T(8,128)(2,1)}, bf16[4096,128]{1,0:T(8,128)(2,1)}, u32[]{:S(2)}, u32[]{:S(2)}) collective-permute-start(bf16[4096,128]{1,0:T(8,128)(2,1)} %get-tuple-element.340), channel_id=1, source_target_pairs={{0,4},{4,0},{8,12},{12,8},{16,20},{20,16},{24,28},{28,24},{1,5},{5... | collective-permute-start | bytes 3145736 | tf_op jit(solution)/shard_map/ppermute | solution.py:41
  275.5 14.8 %collective-permute-start.56 = (bf16[2048,128]{1,0:T(8,128)(2,1)S(1)}, bf16[2048,128]{1,0:T(8,128)(2,1)S(1)}, u32[]{:S(2)}, u32[]{:S(2)}) collective-permute-start(bf16[2048,128]{1,0:T(8,128)(2,1)S(1)} %get-tuple-element.377), channel_id=1, source_target_pairs={{0,8},{4,12},{8,24},{12,28},{24,16},{28,20},{16,0},{20,4},{1,9},{5... | collective-permute-start | bytes 1572872 | tf_op jit(solution)/shard_map/ppermute | solution.py:38
  276.1 14.8 %collective-permute-start.57 = (bf16[2048,128]{1,0:T(8,128)(2,1)S(1)}, bf16[2048,128]{1,0:T(8,128)(2,1)S(1)}, u32[]{:S(2)}, u32[]{:S(2)}) collective-permute-start(bf16[2048,128]{1,0:T(8,128)(2,1)S(1)} %get-tuple-element.376), channel_id=1, source_target_pairs={{0,16},{4,20},{8,0},{12,4},{24,8},{28,12},{16,24},{20,28},{1,17},{... | collective-permute-start | bytes 1572872 | tf_op jit(solution)/shard_map/ppermute | solution.py:38
  277.6 23.4 %collective-permute-start.58 = (bf16[2048,128]{1,0:T(8,128)(2,1)S(1)}, bf16[2048,128]{1,0:T(8,128)(2,1)S(1)}, u32[]{:S(2)}, u32[]{:S(2)}) collective-permute-start(bf16[2048,128]{1,0:T(8,128)(2,1)S(1)} %get-tuple-element.334), channel_id=1, source_target_pairs={{0,8},{4,12},{8,24},{12,28},{24,16},{28,20},{16,0},{20,4},{1,9},{5... | collective-permute-start | bytes 1572872 | tf_op jit(solution)/shard_map/ppermute | solution.py:38
  285.8 15.4 %collective-permute-start.59 = (bf16[2048,128]{1,0:T(8,128)(2,1)S(1)}, bf16[2048,128]{1,0:T(8,128)(2,1)S(1)}, u32[]{:S(2)}, u32[]{:S(2)}) collective-permute-start(bf16[2048,128]{1,0:T(8,128)(2,1)S(1)} %get-tuple-element.335), channel_id=1, source_target_pairs={{0,16},{4,20},{8,0},{12,4},{24,8},{28,12},{16,24},{20,28},{1,17},{... | collective-permute-start | bytes 1572872 | tf_op jit(solution)/shard_map/ppermute | solution.py:38
  303.0 23.2 %collective-permute-start.62 = (bf16[1024,256]{1,0:T(8,128)(2,1)}, bf16[1024,256]{1,0:T(8,128)(2,1)}, u32[]{:S(2)}, u32[]{:S(2)}) collective-permute-start(bf16[1024,256]{1,0:T(8,128)(2,1)} %get-tuple-element.343), channel_id=1, source_target_pairs={{0,3},{1,0},{2,1},{3,2},{4,7},{5,4},{6,5},{7,6},{8,11},{9,8},{10,9... | collective-permute-start | bytes 1572872 | tf_op jit(solution)/shard_map/ppermute | solution.py:87
  306.5 14.5 %collective-permute-start.67 = (bf16[128,256]{1,0:T(8,128)(2,1)S(1)}, bf16[128,256]{1,0:T(8,128)(2,1)S(1)}, u32[]{:S(2)}, u32[]{:S(2)}) collective-permute-start(bf16[128,256]{1,0:T(8,128)(2,1)S(1)} %get-tuple-element.403), channel_id=1, source_target_pairs={{0,1},{1,2},{2,3},{3,0},{4,5},{5,6},{6,7},{7,4},{8,9},{9,10},{10,1... | collective-permute-start | bytes 196616 | tf_op jit(solution)/shard_map/ppermute | solution.py:87
  306.5 15.9 %collective-permute-start.68 = (bf16[128,256]{1,0:T(8,128)(2,1)S(1)}, bf16[128,256]{1,0:T(8,128)(2,1)S(1)}, u32[]{:S(2)}, u32[]{:S(2)}) collective-permute-start(bf16[128,256]{1,0:T(8,128)(2,1)S(1)} %get-tuple-element.405), channel_id=1, source_target_pairs={{0,3},{1,0},{2,1},{3,2},{4,7},{5,4},{6,5},{7,6},{8,11},{9,8},{10,9... | collective-permute-start | bytes 196616 | tf_op jit(solution)/shard_map/ppermute | solution.py:87
  310.3 13.6 %collective-permute-start.69 = (bf16[128,256]{1,0:T(8,128)(2,1)S(1)}, bf16[128,256]{1,0:T(8,128)(2,1)S(1)}, u32[]{:S(2)}, u32[]{:S(2)}) collective-permute-start(bf16[128,256]{1,0:T(8,128)(2,1)S(1)} %get-tuple-element.404), channel_id=1, source_target_pairs={{0,2},{1,3},{2,0},{3,1},{4,6},{5,7},{6,4},{7,5},{8,10},{9,11},{10,... | collective-permute-start | bytes 196616 | tf_op jit(solution)/shard_map/ppermute | solution.py:87
  310.5 25.6 %collective-permute-start.63 = (bf16[2048,128]{1,0:T(8,128)(2,1)}, bf16[2048,128]{1,0:T(8,128)(2,1)}, u32[]{:S(2)}, u32[]{:S(2)}) collective-permute-start(bf16[2048,128]{1,0:T(8,128)(2,1)} %get-tuple-element.372), channel_id=1, source_target_pairs={{0,8},{4,12},{8,24},{12,28},{24,16},{28,20},{16,0},{20,4},{1,9},{5... | collective-permute-start | bytes 1572872 | tf_op jit(solution)/shard_map/ppermute | solution.py:38
  320.9 15.2 %collective-permute-start.65 = (bf16[2048,128]{1,0:T(8,128)(2,1)}, bf16[2048,128]{1,0:T(8,128)(2,1)}, u32[]{:S(2)}, u32[]{:S(2)}) collective-permute-start(bf16[2048,128]{1,0:T(8,128)(2,1)} %get-tuple-element.356), channel_id=1, source_target_pairs={{0,16},{4,20},{8,0},{12,4},{24,8},{28,12},{16,24},{20,28},{1,17},{... | collective-permute-start | bytes 1572872 | tf_op jit(solution)/shard_map/ppermute | solution.py:38
  322.4 13.7 %collective-permute-start.64 = (bf16[2048,128]{1,0:T(8,128)(2,1)}, bf16[2048,128]{1,0:T(8,128)(2,1)}, u32[]{:S(2)}, u32[]{:S(2)}) collective-permute-start(bf16[2048,128]{1,0:T(8,128)(2,1)} %get-tuple-element.354), channel_id=1, source_target_pairs={{0,8},{4,12},{8,24},{12,28},{24,16},{28,20},{16,0},{20,4},{1,9},{5... | collective-permute-start | bytes 1572872 | tf_op jit(solution)/shard_map/ppermute | solution.py:38
  323.9 19.3 %collective-permute-start.66 = (bf16[2048,128]{1,0:T(8,128)(2,1)S(1)}, bf16[2048,128]{1,0:T(8,128)(2,1)}, u32[]{:S(2)}, u32[]{:S(2)}) collective-permute-start(bf16[2048,128]{1,0:T(8,128)(2,1)S(1)} %get-tuple-element.366), channel_id=1, source_target_pairs={{0,16},{4,20},{8,0},{12,4},{24,8},{28,12},{16,24},{20,28},{1,17},{... | collective-permute-start | bytes 1572872 | tf_op jit(solution)/shard_map/ppermute | solution.py:38
  (87 other events, 931.4 us)
Sparse Core Ops, SparseCore 0:
  45.2 43.2 all-gather.2

commit v9 on v8

--- a/solution.py
+++ b/solution.py
@@ -390,6 +390,58 @@
     return functools.reduce(lambda a, b: a + b, [v.astype(F32) for v in values]).astype(BF16)
 
 
+def first_kernel(low_blocks, own_far, got_far, own_up, got_up, own_down, got_down, to_up, to_down):
+    low = pl.program_id(0) < low_blocks
+
+    def put(out, own, got):
+        out[...] = (own[...].astype(F32) + got[...].astype(F32)).astype(BF16)
+
+    @pl.when(low)
+    def _():
+        put(to_up, own_far, got_far)
+        put(to_down, own_down, got_down)
+
+    @pl.when(jnp.logical_not(low))
+    def _():
+        put(to_up, own_up, got_up)
+        put(to_down, own_far, got_far)
+
+
+def first_sums(own_far, own_up, own_down, got, at_far, at_up, at_down):
+    rows, width = own_far.shape
+    step = min(rows // 2, 1024)
+    blocks = rows // step
+    low = blocks // 2
+
+    def spec(index):
+        return pl.BlockSpec((step, width), lambda t: (index(t), 0))
+
+    def upper(t):
+        return jnp.maximum(t, low)
+
+    def lower(t):
+        return jnp.minimum(t, low - 1)
+
+    here = spec(lambda t: t)
+    return pl.pallas_call(
+        functools.partial(first_kernel, low),
+        grid=(blocks,),
+        in_specs=[
+            here,
+            spec(lambda t: t + at_far * blocks),
+            spec(upper),
+            spec(lambda t: upper(t) + at_up * blocks),
+            spec(lower),
+            spec(lambda t: lower(t) + at_down * blocks),
+        ],
+        out_specs=[here, here],
+        out_shape=[jax.ShapeDtypeStruct((rows, width), BF16)] * 2,
+        compiler_params=params(),
+        cost_estimate=pl.CostEstimate(flops=2 * rows * width, bytes_accessed=12 * rows * width, transcendentals=0),
+        name="first_sums",
+    )(own_far, got, own_up, got, own_down, got)
+
+
 def result_kernel(n_ready, low_blocks, *refs):
     ready, (own, got, up_low, up_high, down_low, down_high, out) = refs[:n_ready], refs[n_ready:]
     width = own.shape[1]
@@ -417,12 +469,16 @@
     low = blocks // 2
     here = pl.BlockSpec((step, width), lambda t: (t, 0))
     lower = pl.BlockSpec((step, width), lambda t: (jnp.minimum(t, low - 1), 0))
-    upper = pl.BlockSpec((step, width), lambda t: (jnp.maximum(t - low, 0), 0))
+
+    def upper(value):
+        skip = low if value.shape[0] < rows else 0
+        return pl.BlockSpec((step, width), lambda t: (jnp.maximum(t, low) - skip, 0))
+
     wide = width * (len(ready) + 1)
     return pl.pallas_call(
         functools.partial(result_kernel, len(ready), low),
         grid=(blocks,),
-        in_specs=[here] * (len(ready) + 2) + [lower, upper] * 2,
+        in_specs=[here] * (len(ready) + 2) + [lower, upper(up[1]), lower, upper(down[1])],
         out_specs=pl.BlockSpec((step, wide), lambda t: (t, 0)),
         out_shape=jax.ShapeDtypeStruct((rows, wide), BF16),
         compiler_params=params(),
@@ -432,39 +488,49 @@
 
 
 class Reduction:
-    def __init__(self, ring, own_far, own_zero, own_near, other_far, other_zero, other_near):
+    def __init__(self, ring, own_far, own_zero, own_near, other, other_zero):
         self.ring, self.middle = ring, ring.chips // 2
         self.near = near_places(ring)
         self.own_far, self.own_zero, self.own_near = own_far, own_zero, own_near
-        self.other_far, self.other_zero, self.other_near = other_far, other_zero, other_near
+        self.other, self.other_zero = other, other_zero
         self.rows = own_far.shape[0]
         self.half = self.rows // 2
 
-    def start(self):
-        got = self.ring.sibling(self.other_far)
-        far = [total_of(self.own_far[at : at + self.half], got[at : at + self.half]) for at in (0, self.half)]
-        far = lax.optimization_barrier(far)
-        self.got_near = self.ring.sibling(lax.optimization_barrier((self.other_near, *far))[0])
-        self.got_zero = self.ring.sibling(lax.optimization_barrier((self.other_zero, self.got_near))[0])
-        return far
+    def place(self, offset):
+        return self.near.index(offset % self.ring.chips)
 
     def near_sum(self, offset, upper, *more):
-        at = self.near.index(offset % self.ring.chips)
+        at = self.place(offset)
         start = upper * self.half
         own = self.own_near[at][start : start + self.half]
-        start += at * self.rows
-        return total_of(own, self.got_near[start : start + self.half], *more)
+        start += (1 + at) * self.rows
+        return total_of(own, self.got[start : start + self.half], *more)
 
     def hops(self, up, down):
         return self.ring.hop(up, 1), self.ring.hop(down, -1)
 
-    def free_sums(self):
-        return self.near_sum(self.middle - 1, 1), self.near_sum(1 - self.middle, 0)
-
-    def bound_sums(self, far):
-        return self.near_sum(self.middle - 1, 0, far[0]), self.near_sum(1 - self.middle, 1, far[1])
-
-    def finish(self, free, bound):
+    def first(self, kernel):
+        at_up, at_down = self.place(self.middle - 1), self.place(1 - self.middle)
+        if kernel:
+            own_up, own_down = self.own_near[at_up], self.own_near[at_down]
+            return first_sums(self.own_far, own_up, own_down, self.got, 0, 1 + at_up, 1 + at_down)
+        far = total_of(self.own_far, self.got[: self.rows])
+        return (
+            jnp.concatenate([far[: self.half], self.near_sum(self.middle - 1, 1)]),
+            jnp.concatenate([self.near_sum(1 - self.middle, 0), far[self.half :]]),
+        )
+
+    def second(self, got_first):
+        up, down = got_first
+        return (
+            self.near_sum(self.middle - 1, 0, up[: self.half]),
+            self.near_sum(1 - self.middle, 1, down[self.half :]),
+        )
+
+    def finish(self, got_first, bound):
+        if self.middle == 2:
+            return (bound[0], got_first[0]), (got_first[1], bound[1])
+        free = got_first[0][self.half :], got_first[1][: self.half]
         for step in range(self.middle - 2, 0, -1):
             free = self.hops(self.near_sum(step, 1, free[0]), self.near_sum(-step, 0, free[1]))
             bound = self.hops(self.near_sum(step, 0, bound[0]), self.near_sum(-step, 1, bound[1]))
@@ -497,9 +563,9 @@
     own_meta = [ring.device_at(o, False) * rows + at for o, at in offsets]
     other_meta = [ring.device_at(o, True) * rows + at for o, at in offsets]
     spmm_meta = jnp.stack([rep] + own_meta + other_meta).astype(jnp.int32)
-    held = [1, 1] + [1] * len(near) + [1, 1, len(near)]
-    order = [middle, 0] + near
-    terms_at = [ring.device_at(o, other) * rows for other in (False, True) for o in order]
+    held = [1] * (2 + len(near)) + [1 + len(near), 1]
+    terms_at = [ring.device_at(o, False) * rows for o in [middle, 0] + near]
+    terms_at += [ring.device_at(o, True) * rows for o in [middle] + near + [0]]
     spmm_t_meta = jnp.stack([rep] + terms_at).astype(jnp.int32)
     dense_meta = jnp.stack([rep, lax.rem(lax.axis_index("row"), CORES)]).astype(jnp.int32)
 
@@ -523,6 +589,7 @@
         return spmm(tiles, columns, counts, spmm_meta, own + other, parts, cut, skip)
 
     cot_ends = send(cot_blocks, ends)
+    later = {}
     own_other = ring.sibling(features)
     for c in range(chunks):
         got_own[c, 0] = xs[c]
@@ -552,20 +619,20 @@
         if c:
             mixed[c - 1] = w[f"mixed{c - 1}"]
             ready = [lax.optimization_barrier((b, *seen))[0] for b in mixed[c - 1]]
-            w.go(**{f"mixed_ends{c - 1}": send(ready, ends)})
+            later[f"mixed_ends{c - 1}"] = send(ready, ends)
         w.close()
         if c == 0:
             spmm_meta, spmm_t_meta, dense_meta = w["metas"]
-            w.go(cot_inner=send([w.gate(b) for b in cot_blocks], inner))
+            later["cot_inner"] = send([w.gate(b) for b in cot_blocks], inner)
         else:
-            w.go(**{f"mixed_inner{c - 1}": send([w.gate(b) for b in mixed[c - 1]], inner)})
+            later[f"mixed_inner{c - 1}"] = send([w.gate(b) for b in mixed[c - 1]], inner)
         got_own[c, len(offsets) - 2], got_own[c, len(offsets) - 1] = w[f"far_up{c}"], w[f"far_down{c}"]
         if c < last:
             up = down = w.gate(xs[c + 1])
     for i in (-2, -1):
         got_other[last, len(offsets) + i] = ring.sibling(got_own[last, len(offsets) + i])
 
-    w.go(w_other=ring.sibling(w.gate(w_half)))
+    w.go(w_other=ring.sibling(w.gate(w_half)), **later)
     for h in range(halves):
         w.go(**{f"half{h}": run_spmm(last, halves, h)})
         w.close()
@@ -586,40 +653,29 @@
     act, back, sums = w["whole"]
 
     share = sums.shape[0] // row_size
-    first_got = w.pending[f"back_got{halves - 1}"][1]
-    sums = lax.optimization_barrier((sums, first_got))[0]
 
     def sums_for(offset, other):
         return lax.dynamic_slice_in_dim(sums, ring.device_at(offset, other) * share, share, 0)
 
+    wg_other = jnp.concatenate([sums_for(o, True) for o in [middle] + near + [0]])
+    w.go(wg_got=ring.sibling(wg_other))
+    w.close()
+    wg_got = w["wg_got"]
     wg = Reduction(
-        ring,
-        sums_for(middle, False),
-        sums_for(0, False),
-        [sums_for(o, False) for o in near],
-        sums_for(middle, True),
-        sums_for(0, True),
-        jnp.concatenate([sums_for(o, True) for o in near]),
+        ring, sums_for(middle, False), sums_for(0, False), [sums_for(o, False) for o in near], None, None
     )
-    wg_far = wg.hops(*wg.start())
-    w.go(wg=(wg.own_zero, wg.own_near, wg.got_near, wg.got_zero, wg_far))
-    w.close()
-    wg.own_zero, wg.own_near, wg.got_near, wg.got_zero, wg_far = w["wg"]
-    wg_bound, wg_free = wg.bound_sums(wg_far), wg.free_sums()
-    w.go(wg_got=wg.hops(jnp.concatenate([wg_bound[0], wg_free[0]]), jnp.concatenate([wg_free[1], wg_bound[1]])))
+    wg.got, wg.got_zero = wg_got[:-share], wg_got[-share:]
 
     def run_spmm_t(c, grads):
         return spmm_t(tiles, columns, counts, spmm_t_meta, grads, parts, held, rows, rows * row_size)
 
     parts_got = [ordered(w[f"back{h}"][0], w[f"back_got{h}"]) for h in range(halves)]
+    w.go(wg_first=wg.hops(*wg.first(False)))
     w.go(terms0=run_spmm_t(0, [parts_got[h][u] for u in range(parts) for h in range(halves)]))
     for c in range(1, chunks):
         w.go(**{f"rest_got{c}": send([w.gate(b[c]) for b in back], ends + inner)})
     w.close()
-    wg_got = w["wg_got"]
-    wg_got = wg.finish(
-        (wg_got[0][wg.half :], wg_got[1][: wg.half]), (wg_got[0][: wg.half], wg_got[1][wg.half :])
-    )
+    wg_second = wg.hops(*wg.second(w["wg_first"]))
 
     def send_act(shifts, *after):
         return send([lax.optimization_barrier((a, *after))[0] for a in act], shifts)
@@ -627,44 +683,46 @@
     reductions = []
     for c in range(chunks):
         terms = w[f"terms{c}"]
-        red = Reduction(ring, terms[0], terms[1], terms[2:-3], terms[-3], terms[-2], terms[-1])
+        red = Reduction(ring, terms[0], terms[1], terms[2:-2], terms[-2], terms[-1])
         reductions.append(red)
-        far = red.start()
-        w.go(**{f"far{c}": red.hops(*far), f"zero{c}": red.got_zero})
-        free = red.free_sums()
+        red.got = ring.sibling(red.other)
+        if c == 0:
+            red.got = lax.optimization_barrier((red.got, wg_second))[0]
+        first = red.first(True)
+        red.got_zero = ring.sibling(lax.optimization_barrier((red.other_zero, first[0]))[0])
+        w.go(**{f"first{c}": red.hops(*first)})
         if c < last:
             grads = ordered(back[0][c + 1], w[f"rest_got{c + 1}"])
-            grads = lax.optimization_barrier((grads, free[0][:8], free[1][:8]))[0]
-            w.go(**{f"terms{c + 1}": run_spmm_t(c + 1, grads), f"free{c}": red.hops(*free)})
+            grads = lax.optimization_barrier((grads, first[0][:8], first[1][:8]))[0]
+            w.go(**{f"terms{c + 1}": run_spmm_t(c + 1, grads), f"zero{c}": red.got_zero})
         if c == 0:
-            w.go(act_inner=send_act(inner, free[0][:8]))
+            w.go(act_ends=send_act(ends, first[0][:8]))
         if c == last:
-            w.go(low_end=send_act(ends[:1], far[0][:8]))
+            w.go(act_inner=send_act(inner, first[0][:8]))
         w.close()
-        if c == last:
-            free = [w.gate(f) for f in free]
-        red.free_hops = w[f"free{c}"] if c < last else red.hops(*free)
-        bound = red.bound_sums(w[f"far{c}"])
-        red.bound_hops = red.hops(*bound)
+        second = red.second(w[f"first{c}"])
+        red.second_hops = red.hops(*second)
         if c < last:
-            w.go(**{f"bound{c}": red.bound_hops})
-    high_end = send_act(ends[1:], bound[0][:8])
-
-    up, down = (jnp.concatenate(halves_of) for halves_of in wg_got)
-    block = total_of(wg.own_zero, wg.got_zero, up, down)
-    cuts = [lax.optimization_barrier((block, bound[0][:8]))[0][:, u * f_wide : (u + 1) * f_wide] for u in range(parts)]
+            w.go(**{f"second{c}": red.second_hops})
+
+    up, down = wg.finish(w["wg_first"], wg_second)
+    if middle == 2:
+        up, down = (up[0], up[1][wg.half :]), (down[0][: wg.half], down[1])
+    block = total_of(wg.own_zero, wg.got_zero, jnp.concatenate(up), jnp.concatenate(down))
+    block = lax.optimization_barrier((block, second[0][:8]))[0]
+    cuts = [block[:, u * f_wide : (u + 1) * f_wide] for u in range(parts)]
     cuts_got = send(cuts, ends + inner)
     weight_grad = functools.reduce(lambda a, b: a + b, [v.astype(F32) for v in [cuts[0], *cuts_got.values()]])
 
     feature_grad = ()
     for c, red in enumerate(reductions):
-        bound_hops = w[f"bound{c}"] if c < last else red.bound_hops
-        up, down = red.finish(red.free_hops, bound_hops)
-        feature_grad = (result_of(feature_grad, red.own_zero, w[f"zero{c}"], up, down),)
+        second_hops = w[f"second{c}"] if c < last else red.second_hops
+        got_zero = w[f"zero{c}"] if c < last else red.got_zero
+        up, down = red.finish(w[f"first{c}"], second_hops)
+        feature_grad = (result_of(feature_grad, red.own_zero, got_zero, up, down),)
     feature_grad = feature_grad[0]
     weight_grad = weight_grad.T
-    got = {"act_ends": {**w["low_end"], **high_end}, "act_inner": w["act_inner"]}
-    act = ordered(act[0], got["act_ends"], got["act_inner"])
+    act = ordered(act[0], w["act_ends"], w["act_inner"])
     activations = jnp.zeros((rows, h_wide), BF16)
     for u in range(parts):
         activations = lax.dynamic_update_slice_in_dim(activations, act[u], lax.rem(rep + u, parts) * part_rows, 0)

time: 356 us -> 372 us (1.045)
  waiting for transfers between devices: 113 us -> 128 us
  starting transfers between devices: 80.1 us -> 65.3 us
  Pallas kernels: 103 us -> 112 us
  local copies, waits for them, and re-layouts: 25.6 us -> 30.4 us
    ppermute x27, waiting for transfers between devices: 40.1 us -> 58.6 us  [send(): lax.ppermute(blocks[s], 'rep', [(i, (i + s) % size) for i in range(size)])]
    ppermute x19 -> x15, waiting for transfers between devices: 15.5 us -> 5.59 us  [sibling(): return lax.ppermute(value, 'row', [(d, d ^ 1) for d in range(self.devices)])]
    pallas_call x0 -> x2, Pallas kernels: none -> 8.86 us  [first_sums(): pl.pallas_call(functools.partial(first_kernel, low), grid=(blocks,), in_s...]
    ppermute x24 -> x20, starting transfers between devices: 28.2 us -> 21.3 us  [hop(): return lax.ppermute(value, 'row', self.perm(step))]
    ppermute x24 -> x20, waiting for transfers between devices: 57.2 us -> 63.9 us  [hop(): return lax.ppermute(value, 'row', self.perm(step))]
    ppermute x27, starting transfers between devices: 48.6 us -> 42.2 us  [send(): lax.ppermute(blocks[s], 'rep', [(i, (i + s) % size) for i in range(size)])]
    unnamed x130 -> x142, local copies, waits for them, and re-layouts: 6.54 us -> 10.2 us
    convert_element_type x8 -> x6, other arithmetic: 9.6 us -> 10.5 us  [total_of(): functools.reduce(lambda a, b: a + b, [v.astype(F32) for v in values])]
  transfers between devices with their start and end apart: 71 -> 63, of which waited for: 30 -> 24; matrix products, arithmetic and copies ran while one was open for 6% -> 8% of each run, Pallas kernels for 28% -> 28%
where the time goes in v9:
time: 372 us; the launch traced here: 370 us
  waiting for transfers between devices  128 us (34%)
  Pallas kernels  112 us (30%)
  starting transfers between devices  65.3 us (18%)
  local copies, waits for them, and re-layouts  30.4 us (8%)
  between operations  23.1 us (6%)
  other arithmetic  11.2 us (3%)
    ppermute x20, waiting for transfers between devices, hop(): return lax.ppermute(value, 'row', self.perm(step))  63.9 us
    ppermute x27, waiting for transfers between devices, send(): lax.ppermute(blocks[s], 'rep', [(i, (i + s) % size) for i in range(size)])  58.6 us
    ppermute x27, starting transfers between devices, send(): lax.ppermute(blocks[s], 'rep', [(i, (i + s) % size) for i in range(size)])  42.2 us
    pallas_call x3, Pallas kernels, spmm(): pl.pallas_call(functools.partial(spmm_kernel, len(pieces), per_part, skip...  36.5 us
    pallas_call x2, Pallas kernels, spmm_t(): pl.pallas_call(functools.partial(spmm_t_kernel, len(grads), per_part, len...  34.4 us
    pallas_call x2, Pallas kernels, dense(): pl.pallas_call(functools.partial(dense_kernel, parts, chunks, len(earlier...  23.1 us
    ppermute x20, starting transfers between devices, hop(): return lax.ppermute(value, 'row', self.perm(step))  21.3 us
    convert_element_type x6, other arithmetic, total_of(): functools.reduce(lambda a, b: a + b, [v.astype(F32) for v in values])  10.5 us
  transfers between devices with their start and end apart: 63, of which 24 were waited for; matrix products, arithmetic and copies ran while one was open for 8% of the time, Pallas kernels for 28%

profile of v9, /device:TPU:0, one launch (start us, length us, event | category | flops | bytes accessed | tf_op | source)
XLA Modules:
  0.0 370.2 jit_solution(1362180477461730407)
XLA Ops:
  9.4 2.6 collective-permute-start.1
  12.1 2.9 constant_dynamic-slice_fusion.1
  15.0 2.1 collective-permute-start.5
  28.6 7.3 %collective-permute-done.1.refs_2_ = bf16[4096,128]{1,0:T(8,128)(2,1)} collective-permute-done((bf16[4096,128]{1,0:T(8,128)(2,1)S(1)}, bf16[4096,128]{1,0:T(8,128)(2,1)}, u32[]{:S(2)}, u32[]{:S(2)}) %collective-permute-start.1) | collective-permute-done | bytes 1048608 | tf_op jit(solution)/shard_map/ppermute | solution.py:38
  37.4 3.6 collective-permute-start.4
  41.0 1.9 slice.135
  42.9 1.9 slice.136
  46.8 6.4 %collective-permute-done.4.refs_9_ = bf16[1024,256]{1,0:T(8,128)(2,1)S(1)} collective-permute-done((bf16[1024,256]{1,0:T(8,128)(2,1)}, bf16[1024,256]{1,0:T(8,128)(2,1)S(1)}, u32[]{:S(2)}, u32[]{:S(2)}) %collective-permute-start.4) | collective-permute-done | bytes 524320 | tf_op jit(solution)/shard_map/ppermute | solution.py:87
  54.7 4.3 %collective-permute-done.3.refs_4_ = bf16[2048,128]{1,0:T(8,128)(2,1)S(1)} collective-permute-done((bf16[2048,128]{1,0:T(8,128)(2,1)}, bf16[2048,128]{1,0:T(8,128)(2,1)S(1)}, u32[]{:S(2)}, u32[]{:S(2)}) %collective-permute-start.3) | collective-permute-done | bytes 524320 | tf_op jit(solution)/shard_map/ppermute | solution.py:38
  62.5 3.1 fusion
  66.6 14.5 %spmm.3 = (bf16[1024,128]{1,0:T(8,128)(2,1)}, bf16[1024,128]{1,0:T(8,128)(2,1)}, bf16[1024,128]{1,0:T(8,128)(2,1)}, bf16[1024,128]{1,0:T(8,128)(2,1)}) custom-call(s32[32,16]{1,0:T(8,128)} %copy.69.cols, s32[32]{0:T(128)} %counts.9, s32[11]{0:T(128)} %stack.82.meta, bf16[32,16,128,128]{3,2,1,0:T(8,128)(2,1)} %tiles.9, bf16[4096,128]{1,0:T(8,128)(2,1)} %copy-done.8, ...), custom_call_target="tpu_custom_call" | custom-call | flops 2147483648 | bytes 25165824 | tf_op jit(solution)/shard_map/spmm/pallas_call | solution.py:158
  81.1 4.9 %collective-permute-done.8.refs_2_ = bf16[4096,128]{1,0:T(8,128)(2,1)S(1)} collective-permute-done((bf16[4096,128]{1,0:T(8,128)(2,1)S(1)}, bf16[4096,128]{1,0:T(8,128)(2,1)S(1)}, u32[]{:S(2)}, u32[]{:S(2)}) %collective-permute-start.8) | collective-permute-done | bytes 1048608 | tf_op jit(solution)/shard_map/ppermute | solution.py:38
  89.4 11.2 %collective-permute-done.14.refs_4_ = bf16[2048,128]{1,0:T(8,128)(2,1)S(1)} collective-permute-done((bf16[2048,128]{1,0:T(8,128)(2,1)S(1)}, bf16[2048,128]{1,0:T(8,128)(2,1)S(1)}, u32[]{:S(2)}, u32[]{:S(2)}) %collective-permute-start.14) | collective-permute-done | bytes 524320 | tf_op jit(solution)/shard_map/ppermute | solution.py:38
  101.6 2.9 collective-permute-start.21
  106.6 11.0 %spmm.4 = (bf16[512,128]{1,0:T(8,128)(2,1)}, bf16[512,128]{1,0:T(8,128)(2,1)}, bf16[512,128]{1,0:T(8,128)(2,1)}, bf16[512,128]{1,0:T(8,128)(2,1)}) custom-call(s32[32,16]{1,0:T(8,128)} %copy.69.cols, s32[32]{0:T(128)} %counts.9, s32[11]{0:T(128)} %stack.82.meta, bf16[32,16,128,128]{3,2,1,0:T(8,128)(2,1)} %tiles.9, bf16[4096,128]{1,0:T(8,128)(2,1)} %copy-done.4, ...), custom_call_target="tpu_custom_call" | custom-call | flops 1073741824 | bytes 16777216 | tf_op jit(solution)/shard_map/spmm/pallas_call | solution.py:158
  117.6 19.8 %collective-permute-done.18.refs_10_ = bf16[1024,256]{1,0:T(8,128)(2,1)} collective-permute-done((bf16[1024,256]{1,0:T(8,128)(2,1)}, bf16[1024,256]{1,0:T(8,128)(2,1)}, u32[]{:S(2)}, u32[]{:S(2)}) %collective-permute-start.18) | collective-permute-done | bytes 524320 | tf_op jit(solution)/shard_map/ppermute | solution.py:87
  137.4 5.5 %collective-permute-done.21.refs_4_ = bf16[1024,128]{1,0:T(8,128)(2,1)S(1)} collective-permute-done((bf16[1024,128]{1,0:T(8,128)(2,1)}, bf16[1024,128]{1,0:T(8,128)(2,1)S(1)}, u32[]{:S(2)}, u32[]{:S(2)}) %collective-permute-start.21) | collective-permute-done | bytes 262176 | tf_op jit(solution)/shard_map/ppermute | solution.py:87
  143.0 3.1 collective-permute-start.24
  146.1 7.1 %collective-permute-start.25 = (bf16[512,128]{1,0:T(8,128)(2,1)}, bf16[512,128]{1,0:T(8,128)(2,1)S(1)}, u32[]{:S(2)}, u32[]{:S(2)}) collective-permute-start(bf16[512,128]{1,0:T(8,128)(2,1)} %get-tuple-element.189), channel_id=1, source_target_pairs={{0,2},{1,3},{2,0},{3,1},{4,6},{5,7},{6,4},{7,5},{8,10},{9,11},{10,... | collective-permute-start | bytes 393224 | tf_op jit(solution)/shard_map/ppermute | solution.py:87
  153.2 2.0 collective-permute-start.26
  155.2 11.0 %spmm.5 = (bf16[512,128]{1,0:T(8,128)(2,1)}, bf16[512,128]{1,0:T(8,128)(2,1)}, bf16[512,128]{1,0:T(8,128)(2,1)}, bf16[512,128]{1,0:T(8,128)(2,1)}) custom-call(s32[32,16]{1,0:T(8,128)} %copy.69.cols, s32[32]{0:T(128)} %counts.9, s32[11]{0:T(128)} %stack.82.meta, bf16[32,16,128,128]{3,2,1,0:T(8,128)(2,1)} %tiles.9, bf16[4096,128]{1,0:T(8,128)(2,1)} %copy-done.4, ...), custom_call_target="tpu_custom_call" | custom-call | flops 1073741824 | bytes 16777216 | tf_op jit(solution)/shard_map/spmm/pallas_call | solution.py:158
  166.3 1.9 collective-permute-start.27
  168.8 11.1 %dense.2 = (bf16[1024,256]{1,0:T(8,128)(2,1)}, bf16[1024,256]{1,0:T(8,128)(2,1)}, bf16[1024,256]{1,0:T(8,128)(2,1)}, bf16[1024,256]{1,0:T(8,128)(2,1)}, bf16[512...) custom-call(s32[2]{0:T(128)} %pad_add_fusion.meta, ...), custom_call_target="tpu_custom_call" | custom-call | flops 3221225472 | bytes 10485760 | tf_op jit(solution)/shard_map/dense/pallas_call | solution.py:352
  179.9 3.2 collective-permute-start.30
  184.5 12.0 %dense.3 = (bf16[1024,256]{1,0:T(8,128)(2,1)}, bf16[1024,256]{1,0:T(8,128)(2,1)}, bf16[1024,256]{1,0:T(8,128)(2,1)}, bf16[1024,256]{1,0:T(8,128)(2,1)}, bf16[512...) custom-call(s32[2]{0:T(128)} %pad_add_fusion.meta, ...), custom_call_target="tpu_custom_call", output_to_operand_aliasing={{0}: (16, {}), {1}: (17, {}), {2}: (18, {}), {3}: (19, {}),... | custom-call | flops 3221225472 | bytes 10485760 | tf_op jit(solution)/shard_map/dense/pallas_call | solution.py:352
  198.3 3.7 collective-permute-start.33
  202.6 3.6 collective-permute-done.33.refs_3_
  206.2 8.2 %collective-permute-done.34.refs_5_ = bf16[512,128]{1,0:T(8,128)(2,1)S(1)} collective-permute-done((bf16[512,128]{1,0:T(8,128)(2,1)S(1)}, bf16[512,128]{1,0:T(8,128)(2,1)S(1)}, u32[]{:S(2)}, u32[]{:S(2)}) %collective-permute-start.34) | collective-permute-done | bytes 131104 | tf_op jit(solution)/shard_map/ppermute | solution.py:87
  220.8 2.0 collective-permute-start.41
  222.8 17.3 %spmm_t.2 = (bf16[4096,128]{1,0:T(8,128)(2,1)}, bf16[4096,128]{1,0:T(8,128)(2,1)}, bf16[4096,128]{1,0:T(8,128)(2,1)}, bf16[4096,128]{1,0:T(8,128)(2,1)}, bf16[12...) custom-call(s32[32,16]{1,0:T(8,128)} %copy.69.cols, s32[32]{0:T(128)} %counts.9, s32[9]{0:T(128)} %stack.91.meta, ...), custom_call_target="tpu_custom_call" | custom-call | flops 2147483648 | bytes 25165824 | tf_op jit(solution)/shard_map/spmm_t/pallas_call | solution.py:241
  240.1 2.9 collective-permute-done.40.refs_2_
  247.2 3.9 %collective-permute-done.44 = bf16[64,1024]{1,0:T(8,128)(2,1)S(1)} collective-permute-done((bf16[64,1024]{1,0:T(8,128)(2,1)S(1)}, bf16[64,1024]{1,0:T(8,128)(2,1)S(1)}, u32[]{:S(2)}, u32[]{:S(2)}) %collective-permute-start.44) | collective-permute-done | bytes 131104 | tf_op jit(solution)/shard_map/ppermute | solution.py:38
  252.3 1.7 copy-done.2
  254.1 4.4 %first_sums.2 = (bf16[4096,128]{1,0:T(8,128)(2,1)}, bf16[4096,128]{1,0:T(8,128)(2,1)}) custom-call(bf16[4096,128]{1,0:T(8,128)(2,1)} %get-tuple-element.271.own_far, bf16[12288,128]{1,0:T(8,128)(2,1)} %copy-done.2, bf16[4096,128]{1,0:T(8,128)(2,1)} %get-tuple-element.276.own_up, bf16[12288,128]{1,0:T(8,128)(2,1)} %copy-done.2, ...), custom_call_target="tpu_custom_call" | custom-call | flops 1048576 | bytes 6291456 | tf_op jit(solution)/shard_map/first_sums/pallas_call | solution.py:426
  260.7 2.0 collective-permute-start.49
  262.7 17.2 %spmm_t.3 = (bf16[4096,128]{1,0:T(8,128)(2,1)}, bf16[4096,128]{1,0:T(8,128)(2,1)}, bf16[4096,128]{1,0:T(8,128)(2,1)}, bf16[4096,128]{1,0:T(8,128)(2,1)}, bf16[12...) custom-call(s32[32,16]{1,0:T(8,128)} %copy.69.cols, s32[32]{0:T(128)} %counts.9, s32[9]{0:T(128)} %stack.91.meta, ...), custom_call_target="tpu_custom_call" | custom-call | flops 2147483648 | bytes 25165824 | tf_op jit(solution)/shard_map/spmm_t/pallas_call | solution.py:241
  279.9 6.5 %collective-permute-done.49 = bf16[1024,256]{1,0:T(8,128)(2,1)S(1)} collective-permute-done((bf16[1024,256]{1,0:T(8,128)(2,1)S(1)}, bf16[1024,256]{1,0:T(8,128)(2,1)S(1)}, u32[]{:S(2)}, u32[]{:S(2)}) %collective-permute-start.49) | collective-permute-done | bytes 524320 | tf_op jit(solution)/shard_map/ppermute | solution.py:87
  288.7 5.4 %collective-permute-done.52.got_far.got_up.got_down = bf16[12288,128]{1,0:T(8,128)(2,1)S(1)} collective-permute-done((bf16[12288,128]{1,0:T(8,128)(2,1)}, bf16[12288,128]{1,0:T(8,128)(2,1)S(1)}, u32[]{:S(2)}, u32[]{:S(2)}) %collective-permute-start.52) | collective-permute-done | bytes 3145760 | tf_op jit(solution)/shard_map/ppermute | solution.py:41
  294.1 1.7 copy-done.3
  295.8 4.4 %first_sums.3 = (bf16[4096,128]{1,0:T(8,128)(2,1)}, bf16[4096,128]{1,0:T(8,128)(2,1)}) custom-call(bf16[4096,128]{1,0:T(8,128)(2,1)} %get-tuple-element.303.own_far, bf16[12288,128]{1,0:T(8,128)(2,1)} %copy-done.3, bf16[4096,128]{1,0:T(8,128)(2,1)} %get-tuple-element.305.own_up, bf16[12288,128]{1,0:T(8,128)(2,1)} %copy-done.3, ...), custom_call_target="tpu_custom_call" | custom-call | flops 1048576 | bytes 6291456 | tf_op jit(solution)/shard_map/first_sums/pallas_call | solution.py:426
  306.3 2.0 add_convert_fusion.4
  308.3 5.7 %collective-permute-done.55 = bf16[1024,256]{1,0:T(8,128)(2,1)S(1)} collective-permute-done((bf16[1024,256]{1,0:T(8,128)(2,1)}, bf16[1024,256]{1,0:T(8,128)(2,1)S(1)}, u32[]{:S(2)}, u32[]{:S(2)}) %collective-permute-start.55) | collective-permute-done | bytes 524320 | tf_op jit(solution)/shard_map/ppermute | solution.py:87
  314.0 22.9 %collective-permute-done.51.refs_5_ = bf16[2048,128]{1,0:T(8,128)(2,1)S(1)} collective-permute-done((bf16[2048,128]{1,0:T(8,128)(2,1)S(1)}, bf16[2048,128]{1,0:T(8,128)(2,1)S(1)}, u32[]{:S(2)}, u32[]{:S(2)}) %collective-permute-start.51) | collective-permute-done | bytes 524320 | tf_op jit(solution)/shard_map/ppermute | solution.py:38
  339.4 3.3 add_convert_fusion
  345.7 1.9 constant_dynamic-update-slice_fusion.1
  347.5 4.4 %feature_grad.2.refs_0_ = bf16[4096,128]{1,0:T(8,128)(2,1)} custom-call(bf16[4096,128]{1,0:T(8,128)(2,1)} %get-tuple-element.312.refs_0_, bf16[4096,128]{1,0:T(8,128)(2,1)} %copy-done.26, bf16[2048,128]{1,0:T(8,128)(2,1)} %copy-done.30, bf16[4096,128]{1,0:T(8,128)(2,1)} %copy-done.15, bf16[4096,128]{1,0:T(8,128)(2,1)} %copy-done.13, bf16[2048,128]{1,0:T(8,128)(2,1)} %copy-done.29), custom_call_target="tpu_custom_call" | custom-call | flops 2097152 | bytes 7340032 | tf_op jit(solution)/shard_map/feature_grad/pallas_call | solution.py:478
  353.6 3.4 collective-permute-done.58.refs_6_
  358.6 4.8 %feature_grad.3 = bf16[4096,256]{1,0:T(8,128)(2,1)} custom-call(bf16[4096,128]{1,0:T(8,128)(2,1)} %feature_grad.2.refs_0_, bf16[4096,128]{1,0:T(8,128)(2,1)} %get-tuple-element.316.refs_1_, bf16[4096,128]{1,0:T(8,128)(2,1)} %collective-permute-done.56.refs_2_, bf16[2048,128]{1,0:T(8,128)(2,1)} %copy-done.35, bf16[4096,128]{1,0:T(8,128)(2,1)} %copy-done.18, ...), custom_call_target="tpu_custom_call" | custom-call | flops 2097152 | bytes 7340032 | tf_op jit(solution)/shard_map/feature_grad/pallas_call | solution.py:478
  (265 shorter events, 56.7 us)
Async XLA Ops:
  7.2 93.8 %all-gather.3.cloned.1.call-start = ((), (), s32[]{:S(2)}) async-start(), calls=%async_computation | async-start | bytes 1310720 | tf_op jit(solution)/shard_map/all_gather | solution.py:577
  7.2 53.2 %collective-permute-start.6 = (bf16[4096,256]{1,0:T(8,128)(2,1)}, bf16[4096,256]{1,0:T(8,128)(2,1)}, u32[]{:S(2)}, u32[]{:S(2)}) collective-permute-start(bf16[4096,256]{1,0:T(8,128)(2,1)} %param.58), channel_id=1, source_target_pairs={{0,4},{4,0},{8,12},{12,8},{16,20},{20,16},{24,28},{28,24},{1,5},{5... | collective-permute-start | bytes 6291464 | tf_op jit(solution)/shard_map/ppermute | solution.py:41
  9.4 26.5 %collective-permute-start.1 = (bf16[4096,128]{1,0:T(8,128)(2,1)S(1)}, bf16[4096,128]{1,0:T(8,128)(2,1)}, u32[]{:S(2)}, u32[]{:S(2)}) collective-permute-start(bf16[4096,128]{1,0:T(8,128)(2,1)S(1)} %get-tuple-element.342.refs_0_), channel_id=1, source_target_pairs={{0,16},{4,20},{8,0},{12,4},{24,8},{28,12},{16,24},{20,28},{1,17},{... | collective-permute-start | bytes 3145736 | tf_op jit(solution)/shard_map/ppermute | solution.py:38
  12.1 25.4 %collective-permute-start = (bf16[4096,128]{1,0:T(8,128)(2,1)S(1)}, bf16[4096,128]{1,0:T(8,128)(2,1)}, u32[]{:S(2)}, u32[]{:S(2)}) collective-permute-start(bf16[4096,128]{1,0:T(8,128)(2,1)S(1)} %get-tuple-element.342.refs_0_), channel_id=1, source_target_pairs={{0,8},{4,12},{8,24},{12,28},{24,16},{28,20},{16,0},{20,4},{1,9},{5... | collective-permute-start | bytes 3145736 | tf_op jit(solution)/shard_map/ppermute | solution.py:38
  15.0 31.3 %collective-permute-start.5 = (bf16[1024,256]{1,0:T(8,128)(2,1)}, bf16[1024,256]{1,0:T(8,128)(2,1)S(1)}, u32[]{:S(2)}, u32[]{:S(2)}) collective-permute-start(bf16[1024,256]{1,0:T(8,128)(2,1)} %get-tuple-element.337), channel_id=1, source_target_pairs={{0,1},{1,2},{2,3},{3,0},{4,5},{5,6},{6,7},{7,4},{8,9},{9,10},{10,1... | collective-permute-start | bytes 1572872 | tf_op jit(solution)/shard_map/ppermute | solution.py:87
  37.4 25.1 %collective-permute-start.9 = (bf16[4096,128]{1,0:T(8,128)(2,1)}, bf16[4096,128]{1,0:T(8,128)(2,1)}, u32[]{:S(2)}, u32[]{:S(2)}) collective-permute-start(bf16[4096,128]{1,0:T(8,128)(2,1)} %collective-permute-done.refs_1_), channel_id=1, source_target_pairs={{0,4},{4,0},{8,12},{12,8},{16,20},{20,16},{24,28},{28,24},{1,5},{5... | collective-permute-start | bytes 3145736 | tf_op jit(solution)/shard_map/ppermute | solution.py:41
  37.4 15.8 %collective-permute-start.4 = (bf16[1024,256]{1,0:T(8,128)(2,1)}, bf16[1024,256]{1,0:T(8,128)(2,1)S(1)}, u32[]{:S(2)}, u32[]{:S(2)}) collective-permute-start(bf16[1024,256]{1,0:T(8,128)(2,1)} %get-tuple-element.338), channel_id=1, source_target_pairs={{0,3},{1,0},{2,1},{3,2},{4,7},{5,4},{6,5},{7,6},{8,11},{9,8},{10,9... | collective-permute-start | bytes 1572872 | tf_op jit(solution)/shard_map/ppermute | solution.py:87
  44.8 14.3 %collective-permute-start.3 = (bf16[2048,128]{1,0:T(8,128)(2,1)}, bf16[2048,128]{1,0:T(8,128)(2,1)S(1)}, u32[]{:S(2)}, u32[]{:S(2)}) collective-permute-start(bf16[2048,128]{1,0:T(8,128)(2,1)} %slice.136), channel_id=1, source_target_pairs={{0,16},{4,20},{8,0},{12,4},{24,8},{28,12},{16,24},{20,28},{1,17},{... | collective-permute-start | bytes 1572872 | tf_op jit(solution)/shard_map/ppermute | solution.py:38
  46.3 14.1 %collective-permute-start.2 = (bf16[2048,128]{1,0:T(8,128)(2,1)}, bf16[2048,128]{1,0:T(8,128)(2,1)}, u32[]{:S(2)}, u32[]{:S(2)}) collective-permute-start(bf16[2048,128]{1,0:T(8,128)(2,1)} %slice.135), channel_id=1, source_target_pairs={{0,8},{4,12},{8,24},{12,28},{24,16},{28,20},{16,0},{20,4},{1,9},{5... | collective-permute-start | bytes 1572872 | tf_op jit(solution)/shard_map/ppermute | solution.py:38
  60.4 25.6 %collective-permute-start.8 = (bf16[4096,128]{1,0:T(8,128)(2,1)S(1)}, bf16[4096,128]{1,0:T(8,128)(2,1)S(1)}, u32[]{:S(2)}, u32[]{:S(2)}) collective-permute-start(bf16[4096,128]{1,0:T(8,128)(2,1)S(1)} %get-tuple-element.165.refs_0_), channel_id=1, source_target_pairs={{0,16},{4,20},{8,0},{12,4},{24,8},{28,12},{16,24},{20,28},{1,17},{... | collective-permute-start | bytes 3145736 | tf_op jit(solution)/shard_map/ppermute | solution.py:38
  61.4 24.8 %collective-permute-start.7 = (bf16[4096,128]{1,0:T(8,128)(2,1)S(1)}, bf16[4096,128]{1,0:T(8,128)(2,1)S(1)}, u32[]{:S(2)}, u32[]{:S(2)}) collective-permute-start(bf16[4096,128]{1,0:T(8,128)(2,1)S(1)} %get-tuple-element.165.refs_0_), channel_id=1, source_target_pairs={{0,8},{4,12},{8,24},{12,28},{24,16},{28,20},{16,0},{20,4},{1,9},{5... | collective-permute-start | bytes 3145736 | tf_op jit(solution)/shard_map/ppermute | solution.py:38
  86.2 14.7 %collective-permute-start.15 = (bf16[4096,128]{1,0:T(8,128)(2,1)S(1)}, bf16[4096,128]{1,0:T(8,128)(2,1)S(1)}, u32[]{:S(2)}, u32[]{:S(2)}) collective-permute-start(bf16[4096,128]{1,0:T(8,128)(2,1)S(1)} %collective-permute-done.7.refs_1_), channel_id=1, source_target_pairs={{0,4},{4,0},{8,12},{12,8},{16,20},{20,16},{24,28},{28,24},{1,5},{5... | collective-permute-start | bytes 3145736 | tf_op jit(solution)/shard_map/ppermute | solution.py:41
  86.2 14.7 %collective-permute-start.16 = (bf16[4096,128]{1,0:T(8,128)(2,1)S(1)}, bf16[4096,128]{1,0:T(8,128)(2,1)}, u32[]{:S(2)}, u32[]{:S(2)}) collective-permute-start(bf16[4096,128]{1,0:T(8,128)(2,1)S(1)} %collective-permute-done.8.refs_2_), channel_id=1, source_target_pairs={{0,4},{4,0},{8,12},{12,8},{16,20},{20,16},{24,28},{28,24},{1,5},{5... | collective-permute-start | bytes 3145736 | tf_op jit(solution)/shard_map/ppermute | solution.py:41
  87.4 13.3 %collective-permute-start.14 = (bf16[2048,128]{1,0:T(8,128)(2,1)S(1)}, bf16[2048,128]{1,0:T(8,128)(2,1)S(1)}, u32[]{:S(2)}, u32[]{:S(2)}) collective-permute-start(bf16[2048,128]{1,0:T(8,128)(2,1)S(1)} %slice.139), channel_id=1, source_target_pairs={{0,16},{4,20},{8,0},{12,4},{24,8},{28,12},{16,24},{20,28},{1,17},{... | collective-permute-start | bytes 1572872 | tf_op jit(solution)/shard_map/ppermute | solution.py:38
  87.9 13.0 %collective-permute-start.13 = (bf16[2048,128]{1,0:T(8,128)(2,1)S(1)}, bf16[2048,128]{1,0:T(8,128)(2,1)S(1)}, u32[]{:S(2)}, u32[]{:S(2)}) collective-permute-start(bf16[2048,128]{1,0:T(8,128)(2,1)S(1)} %slice.138), channel_id=1, source_target_pairs={{0,8},{4,12},{8,24},{12,28},{24,16},{28,20},{16,0},{20,4},{1,9},{5... | collective-permute-start | bytes 1572872 | tf_op jit(solution)/shard_map/ppermute | solution.py:38
  101.0 42.0 %collective-permute-start.17 = (bf16[4,512,256]{2,1,0:T(8,128)(2,1)}, bf16[4,512,256]{2,1,0:T(8,128)(2,1)}, u32[]{:S(2)}, u32[]{:S(2)}) collective-permute-start(bf16[4,512,256]{2,1,0:T(8,128)(2,1)} %bitcast.27), channel_id=1, source_target_pairs={{0,4},{4,0},{8,12},{12,8},{16,20},{20,16},{24,28},{28,24},{1,5},{5... | collective-permute-start | bytes 3145736 | tf_op jit(solution)/shard_map/ppermute | solution.py:41
  101.6 35.8 %collective-permute-start.18 = (bf16[1024,256]{1,0:T(8,128)(2,1)}, bf16[1024,256]{1,0:T(8,128)(2,1)}, u32[]{:S(2)}, u32[]{:S(2)}) collective-permute-start(bf16[1024,256]{1,0:T(8,128)(2,1)} %get-tuple-element.176), channel_id=1, source_target_pairs={{0,2},{1,3},{2,0},{3,1},{4,6},{5,7},{6,4},{7,5},{8,10},{9,11},{10,... | collective-permute-start | bytes 1572872 | tf_op jit(solution)/shard_map/ppermute | solution.py:87
  101.6 41.3 %collective-permute-start.21 = (bf16[1024,128]{1,0:T(8,128)(2,1)}, bf16[1024,128]{1,0:T(8,128)(2,1)S(1)}, u32[]{:S(2)}, u32[]{:S(2)}) collective-permute-start(bf16[1024,128]{1,0:T(8,128)(2,1)} %get-tuple-element.182), channel_id=1, source_target_pairs={{0,2},{1,3},{2,0},{3,1},{4,6},{5,7},{6,4},{7,5},{8,10},{9,11},{10,... | collective-permute-start | bytes 786440 | tf_op jit(solution)/shard_map/ppermute | solution.py:87
  104.6 38.4 %collective-permute-start.19 = (bf16[1024,128]{1,0:T(8,128)(2,1)}, bf16[1024,128]{1,0:T(8,128)(2,1)}, u32[]{:S(2)}, u32[]{:S(2)}) collective-permute-start(bf16[1024,128]{1,0:T(8,128)(2,1)} %get-tuple-element.178), channel_id=1, source_target_pairs={{0,3},{1,0},{2,1},{3,2},{4,7},{5,4},{6,5},{7,6},{8,11},{9,8},{10,9... | collective-permute-start | bytes 786440 | tf_op jit(solution)/shard_map/ppermute | solution.py:87
  105.2 37.7 %collective-permute-start.20 = (bf16[1024,128]{1,0:T(8,128)(2,1)}, bf16[1024,128]{1,0:T(8,128)(2,1)}, u32[]{:S(2)}, u32[]{:S(2)}) collective-permute-start(bf16[1024,128]{1,0:T(8,128)(2,1)} %get-tuple-element.180), channel_id=1, source_target_pairs={{0,1},{1,2},{2,3},{3,0},{4,5},{5,6},{6,7},{7,4},{8,9},{9,10},{10,1... | collective-permute-start | bytes 786440 | tf_op jit(solution)/shard_map/ppermute | solution.py:87
  143.0 23.3 %collective-permute-start.24 = (bf16[512,128]{1,0:T(8,128)(2,1)}, bf16[512,128]{1,0:T(8,128)(2,1)S(1)}, u32[]{:S(2)}, u32[]{:S(2)}) collective-permute-start(bf16[512,128]{1,0:T(8,128)(2,1)} %get-tuple-element.188), channel_id=1, source_target_pairs={{0,3},{1,0},{2,1},{3,2},{4,7},{5,4},{6,5},{7,6},{8,11},{9,8},{10,9... | collective-permute-start | bytes 393224 | tf_op jit(solution)/shard_map/ppermute | solution.py:87
  146.1 20.2 %collective-permute-start.25 = (bf16[512,128]{1,0:T(8,128)(2,1)}, bf16[512,128]{1,0:T(8,128)(2,1)S(1)}, u32[]{:S(2)}, u32[]{:S(2)}) collective-permute-start(bf16[512,128]{1,0:T(8,128)(2,1)} %get-tuple-element.189), channel_id=1, source_target_pairs={{0,2},{1,3},{2,0},{3,1},{4,6},{5,7},{6,4},{7,5},{8,10},{9,11},{10,... | collective-permute-start | bytes 393224 | tf_op jit(solution)/shard_map/ppermute | solution.py:87
  153.2 13.1 %collective-permute-start.26 = (bf16[512,128]{1,0:T(8,128)(2,1)}, bf16[512,128]{1,0:T(8,128)(2,1)S(1)}, u32[]{:S(2)}, u32[]{:S(2)}) collective-permute-start(bf16[512,128]{1,0:T(8,128)(2,1)} %get-tuple-element.190), channel_id=1, source_target_pairs={{0,1},{1,2},{2,3},{3,0},{4,5},{5,6},{6,7},{7,4},{8,9},{9,10},{10,1... | collective-permute-start | bytes 393224 | tf_op jit(solution)/shard_map/ppermute | solution.py:87
  166.3 13.6 %collective-permute-start.27 = (bf16[512,128]{1,0:T(8,128)(2,1)}, bf16[512,128]{1,0:T(8,128)(2,1)S(1)}, u32[]{:S(2)}, u32[]{:S(2)}) collective-permute-start(bf16[512,128]{1,0:T(8,128)(2,1)} %get-tuple-element.195), channel_id=1, source_target_pairs={{0,3},{1,0},{2,1},{3,2},{4,7},{5,4},{6,5},{7,6},{8,11},{9,8},{10,9... | collective-permute-start | bytes 393224 | tf_op jit(solution)/shard_map/ppermute | solution.py:87
  179.9 16.6 %collective-permute-start.30 = (bf16[512,128]{1,0:T(8,128)(2,1)}, bf16[512,128]{1,0:T(8,128)(2,1)S(1)}, u32[]{:S(2)}, u32[]{:S(2)}) collective-permute-start(bf16[512,128]{1,0:T(8,128)(2,1)} %get-tuple-element.215), channel_id=1, source_target_pairs={{0,3},{1,0},{2,1},{3,2},{4,7},{5,4},{6,5},{7,6},{8,11},{9,8},{10,9... | collective-permute-start | bytes 393224 | tf_op jit(solution)/shard_map/ppermute | solution.py:87
  183.2 13.4 %collective-permute-start.31 = (bf16[512,128]{1,0:T(8,128)(2,1)}, bf16[512,128]{1,0:T(8,128)(2,1)S(1)}, u32[]{:S(2)}, u32[]{:S(2)}) collective-permute-start(bf16[512,128]{1,0:T(8,128)(2,1)} %get-tuple-element.216), channel_id=1, source_target_pairs={{0,2},{1,3},{2,0},{3,1},{4,6},{5,7},{6,4},{7,5},{8,10},{9,11},{10,... | collective-permute-start | bytes 393224 | tf_op jit(solution)/shard_map/ppermute | solution.py:87
  198.2 16.2 %collective-permute-start.36 = (bf16[512,1024]{1,0:T(8,128)(2,1)S(1)}, bf16[512,1024]{1,0:T(8,128)(2,1)S(1)}, u32[]{:S(2)}, u32[]{:S(2)}) collective-permute-start(bf16[512,1024]{1,0:T(8,128)(2,1)S(1)} %pad_maximum_fusion), channel_id=1, source_target_pairs={{0,4},{4,0},{8,12},{12,8},{16,20},{20,16},{24,28},{28,24},{1,5},{5... | collective-permute-start | bytes 3145736 | tf_op jit(solution)/shard_map/ppermute | solution.py:41
  202.0 12.5 %collective-permute-start.34 = (bf16[512,128]{1,0:T(8,128)(2,1)S(1)}, bf16[512,128]{1,0:T(8,128)(2,1)S(1)}, u32[]{:S(2)}, u32[]{:S(2)}) collective-permute-start(bf16[512,128]{1,0:T(8,128)(2,1)S(1)} %copy-done.66), channel_id=1, source_target_pairs={{0,2},{1,3},{2,0},{3,1},{4,6},{5,7},{6,4},{7,5},{8,10},{9,11},{10,... | collective-permute-start | bytes 393224 | tf_op jit(solution)/shard_map/ppermute | solution.py:87
  202.0 12.4 %collective-permute-start.35 = (bf16[512,128]{1,0:T(8,128)(2,1)S(1)}, bf16[512,128]{1,0:T(8,128)(2,1)S(1)}, u32[]{:S(2)}, u32[]{:S(2)}) collective-permute-start(bf16[512,128]{1,0:T(8,128)(2,1)S(1)} %copy-done.65), channel_id=1, source_target_pairs={{0,1},{1,2},{2,3},{3,0},{4,5},{5,6},{6,7},{7,4},{8,9},{9,10},{10,1... | collective-permute-start | bytes 393224 | tf_op jit(solution)/shard_map/ppermute | solution.py:87
  216.8 23.3 %collective-permute-start.37 = (bf16[128,1024]{1,0:T(8,128)(2,1)S(1)}, bf16[128,1024]{1,0:T(8,128)(2,1)S(1)}, u32[]{:S(2)}, u32[]{:S(2)}) collective-permute-start(bf16[128,1024]{1,0:T(8,128)(2,1)S(1)} %pad_maximum_fusion.1), channel_id=1, source_target_pairs={{0,8},{4,12},{8,24},{12,28},{24,16},{28,20},{16,0},{20,4},{1,9},{5... | collective-permute-start | bytes 786440 | tf_op jit(solution)/shard_map/ppermute | solution.py:38
  218.3 21.7 %collective-permute-start.38 = (bf16[128,1024]{1,0:T(8,128)(2,1)S(1)}, bf16[128,1024]{1,0:T(8,128)(2,1)S(1)}, u32[]{:S(2)}, u32[]{:S(2)}) collective-permute-start(bf16[128,1024]{1,0:T(8,128)(2,1)S(1)} %pad_maximum_fusion.2), channel_id=1, source_target_pairs={{0,16},{4,20},{8,0},{12,4},{24,8},{28,12},{16,24},{20,28},{1,17},{... | collective-permute-start | bytes 786440 | tf_op jit(solution)/shard_map/ppermute | solution.py:38
  218.9 21.2 %collective-permute-start.39 = (bf16[1024,128]{1,0:T(8,128)(2,1)S(1)}, bf16[1024,128]{1,0:T(8,128)(2,1)S(1)}, u32[]{:S(2)}, u32[]{:S(2)}) collective-permute-start(bf16[1024,128]{1,0:T(8,128)(2,1)S(1)} %copy-done.46), channel_id=1, source_target_pairs={{0,3},{1,0},{2,1},{3,2},{4,7},{5,4},{6,5},{7,6},{8,11},{9,8},{10,9... | collective-permute-start | bytes 786440 | tf_op jit(solution)/shard_map/ppermute | solution.py:87
  219.5 23.6 %collective-permute-start.40 = (bf16[1024,128]{1,0:T(8,128)(2,1)S(1)}, bf16[1024,128]{1,0:T(8,128)(2,1)S(1)}, u32[]{:S(2)}, u32[]{:S(2)}) collective-permute-start(bf16[1024,128]{1,0:T(8,128)(2,1)S(1)} %copy-done.45), channel_id=1, source_target_pairs={{0,2},{1,3},{2,0},{3,1},{4,6},{5,7},{6,4},{7,5},{8,10},{9,11},{10,... | collective-permute-start | bytes 786440 | tf_op jit(solution)/shard_map/ppermute | solution.py:87
  220.8 22.2 %collective-permute-start.41 = (bf16[1024,128]{1,0:T(8,128)(2,1)S(1)}, bf16[1024,128]{1,0:T(8,128)(2,1)S(1)}, u32[]{:S(2)}, u32[]{:S(2)}) collective-permute-start(bf16[1024,128]{1,0:T(8,128)(2,1)S(1)} %copy-done.44), channel_id=1, source_target_pairs={{0,1},{1,2},{2,3},{3,0},{4,5},{5,6},{6,7},{7,4},{8,9},{9,10},{10,1... | collective-permute-start | bytes 786440 | tf_op jit(solution)/shard_map/ppermute | solution.py:87
  258.5 27.9 %collective-permute-start.47 = (bf16[4096,128]{1,0:T(8,128)(2,1)}, bf16[4096,128]{1,0:T(8,128)(2,1)S(1)}, u32[]{:S(2)}, u32[]{:S(2)}) collective-permute-start(bf16[4096,128]{1,0:T(8,128)(2,1)} %get-tuple-element.295), channel_id=1, source_target_pairs={{0,4},{4,0},{8,12},{12,8},{16,20},{20,16},{24,28},{28,24},{1,5},{5... | collective-permute-start | bytes 3145736 | tf_op jit(solution)/shard_map/ppermute | solution.py:41
  258.6 27.8 %collective-permute-start.46 = (bf16[4096,128]{1,0:T(8,128)(2,1)}, bf16[4096,128]{1,0:T(8,128)(2,1)S(1)}, u32[]{:S(2)}, u32[]{:S(2)}) collective-permute-start(bf16[4096,128]{1,0:T(8,128)(2,1)} %get-tuple-element.279), channel_id=1, source_target_pairs={{0,16},{4,20},{8,0},{12,4},{24,8},{28,12},{16,24},{20,28},{1,17},{... | collective-permute-start | bytes 3145736 | tf_op jit(solution)/shard_map/ppermute | solution.py:38
  260.1 26.3 %collective-permute-start.45 = (bf16[4096,128]{1,0:T(8,128)(2,1)}, bf16[4096,128]{1,0:T(8,128)(2,1)S(1)}, u32[]{:S(2)}, u32[]{:S(2)}) collective-permute-start(bf16[4096,128]{1,0:T(8,128)(2,1)} %get-tuple-element.278), channel_id=1, source_target_pairs={{0,8},{4,12},{8,24},{12,28},{24,16},{28,20},{16,0},{20,4},{1,9},{5... | collective-permute-start | bytes 3145736 | tf_op jit(solution)/shard_map/ppermute | solution.py:38
  260.7 19.2 %collective-permute-start.48 = (bf16[1024,256]{1,0:T(8,128)(2,1)S(1)}, bf16[1024,256]{1,0:T(8,128)(2,1)S(1)}, u32[]{:S(2)}, u32[]{:S(2)}) collective-permute-start(bf16[1024,256]{1,0:T(8,128)(2,1)S(1)} %copy-done.33), channel_id=1, source_target_pairs={{0,3},{1,0},{2,1},{3,2},{4,7},{5,4},{6,5},{7,6},{8,11},{9,8},{10,9... | collective-permute-start | bytes 1572872 | tf_op jit(solution)/shard_map/ppermute | solution.py:87
  260.7 25.7 %collective-permute-start.49 = (bf16[1024,256]{1,0:T(8,128)(2,1)S(1)}, bf16[1024,256]{1,0:T(8,128)(2,1)S(1)}, u32[]{:S(2)}, u32[]{:S(2)}) collective-permute-start(bf16[1024,256]{1,0:T(8,128)(2,1)S(1)} %copy-done.32), channel_id=1, source_target_pairs={{0,1},{1,2},{2,3},{3,0},{4,5},{5,6},{6,7},{7,4},{8,9},{9,10},{10,1... | collective-permute-start | bytes 1572872 | tf_op jit(solution)/shard_map/ppermute | solution.py:87
  288.2 25.7 %collective-permute-start.55 = (bf16[1024,256]{1,0:T(8,128)(2,1)}, bf16[1024,256]{1,0:T(8,128)(2,1)S(1)}, u32[]{:S(2)}, u32[]{:S(2)}) collective-permute-start(bf16[1024,256]{1,0:T(8,128)(2,1)} %get-tuple-element.309), channel_id=1, source_target_pairs={{0,2},{1,3},{2,0},{3,1},{4,6},{5,7},{6,4},{7,5},{8,10},{9,11},{10,... | collective-permute-start | bytes 1572872 | tf_op jit(solution)/shard_map/ppermute | solution.py:87
  300.2 39.2 %collective-permute-start.54 = (bf16[4096,128]{1,0:T(8,128)(2,1)}, bf16[4096,128]{1,0:T(8,128)(2,1)S(1)}, u32[]{:S(2)}, u32[]{:S(2)}) collective-permute-start(bf16[4096,128]{1,0:T(8,128)(2,1)} %get-tuple-element.308), channel_id=1, source_target_pairs={{0,16},{4,20},{8,0},{12,4},{24,8},{28,12},{16,24},{20,28},{1,17},{... | collective-permute-start | bytes 3145736 | tf_op jit(solution)/shard_map/ppermute | solution.py:38
  301.7 37.7 %collective-permute-start.53 = (bf16[4096,128]{1,0:T(8,128)(2,1)}, bf16[4096,128]{1,0:T(8,128)(2,1)S(1)}, u32[]{:S(2)}, u32[]{:S(2)}) collective-permute-start(bf16[4096,128]{1,0:T(8,128)(2,1)} %get-tuple-element.307), channel_id=1, source_target_pairs={{0,8},{4,12},{8,24},{12,28},{24,16},{28,20},{16,0},{20,4},{1,9},{5... | collective-permute-start | bytes 3145736 | tf_op jit(solution)/shard_map/ppermute | solution.py:38
  303.9 33.0 %collective-permute-start.51 = (bf16[2048,128]{1,0:T(8,128)(2,1)S(1)}, bf16[2048,128]{1,0:T(8,128)(2,1)S(1)}, u32[]{:S(2)}, u32[]{:S(2)}) collective-permute-start(bf16[2048,128]{1,0:T(8,128)(2,1)S(1)} %get-tuple-element.326), channel_id=1, source_target_pairs={{0,16},{4,20},{8,0},{12,4},{24,8},{28,12},{16,24},{20,28},{1,17},{... | collective-permute-start | bytes 1572872 | tf_op jit(solution)/shard_map/ppermute | solution.py:38
  305.4 32.6 %collective-permute-start.50 = (bf16[2048,128]{1,0:T(8,128)(2,1)S(1)}, bf16[2048,128]{1,0:T(8,128)(2,1)S(1)}, u32[]{:S(2)}, u32[]{:S(2)}) collective-permute-start(bf16[2048,128]{1,0:T(8,128)(2,1)S(1)} %get-tuple-element.327), channel_id=1, source_target_pairs={{0,8},{4,12},{8,24},{12,28},{24,16},{28,20},{16,0},{20,4},{1,9},{5... | collective-permute-start | bytes 1572872 | tf_op jit(solution)/shard_map/ppermute | solution.py:38
  314.0 29.8 %collective-permute-start.59 = (bf16[128,256]{1,0:T(8,128)(2,1)S(1)}, bf16[128,256]{1,0:T(8,128)(2,1)S(1)}, u32[]{:S(2)}, u32[]{:S(2)}) collective-permute-start(bf16[128,256]{1,0:T(8,128)(2,1)S(1)} %get-tuple-element.344), channel_id=1, source_target_pairs={{0,1},{1,2},{2,3},{3,0},{4,5},{5,6},{6,7},{7,4},{8,9},{9,10},{10,1... | collective-permute-start | bytes 196616 | tf_op jit(solution)/shard_map/ppermute | solution.py:87
  339.4 14.2 %collective-permute-start.56 = (bf16[4096,128]{1,0:T(8,128)(2,1)}, bf16[4096,128]{1,0:T(8,128)(2,1)}, u32[]{:S(2)}, u32[]{:S(2)}) collective-permute-start(bf16[4096,128]{1,0:T(8,128)(2,1)} %get-tuple-element.318), channel_id=1, source_target_pairs={{0,4},{4,0},{8,12},{12,8},{16,20},{20,16},{24,28},{28,24},{1,5},{5... | collective-permute-start | bytes 3145736 | tf_op jit(solution)/shard_map/ppermute | solution.py:41
  342.8 14.2 %collective-permute-start.58 = (bf16[2048,128]{1,0:T(8,128)(2,1)}, bf16[2048,128]{1,0:T(8,128)(2,1)S(1)}, u32[]{:S(2)}, u32[]{:S(2)}) collective-permute-start(bf16[2048,128]{1,0:T(8,128)(2,1)} %get-tuple-element.324), channel_id=1, source_target_pairs={{0,16},{4,20},{8,0},{12,4},{24,8},{28,12},{16,24},{20,28},{1,17},{... | collective-permute-start | bytes 1572872 | tf_op jit(solution)/shard_map/ppermute | solution.py:38
  343.7 13.9 %collective-permute-start.57 = (bf16[2048,128]{1,0:T(8,128)(2,1)}, bf16[2048,128]{1,0:T(8,128)(2,1)S(1)}, u32[]{:S(2)}, u32[]{:S(2)}) collective-permute-start(bf16[2048,128]{1,0:T(8,128)(2,1)} %get-tuple-element.325), channel_id=1, source_target_pairs={{0,8},{4,12},{8,24},{12,28},{24,16},{28,20},{16,0},{20,4},{1,9},{5... | collective-permute-start | bytes 1572872 | tf_op jit(solution)/shard_map/ppermute | solution.py:38
  (85 other events, 792.1 us)
Sparse Core Ops, SparseCore 0:
  54.1 28.8 all-gather.2

commit v10 on v8

--- a/solution.py
+++ b/solution.py
@@ -267,8 +267,7 @@
 def dense_kernel(parts, chunks, n_earlier, is_first, is_last, meta, *refs):
     n_mixed = parts * chunks
     mixed_refs, cot_refs = refs[:n_mixed], refs[n_mixed : n_mixed + parts]
-    w_halves = refs[n_mixed + parts : n_mixed + parts + CORES]
-    refs = refs[n_mixed + parts + CORES :]
+    w_hbm, refs = refs[n_mixed + parts], refs[n_mixed + parts + 1 :]
     if not is_first:
         sums_hbm, refs = refs[0], refs[1:]
     outs = refs[n_earlier:]
@@ -286,14 +285,9 @@
     def _():
         copies = []
         for i in range(parts):
-            half, at = i // (parts // CORES), i % (parts // CORES)
-            whole_at = lax.rem(meta[1] + half, CORES) * (parts // CORES) + at
-            to = aligned(lax.rem(whole_at + parts - me, parts) * f_wide, f_wide, f_wide)
-            for j in range(parts):
-                src = w_halves[half].at[place(j), pl.ds(at * f_wide, f_wide)]
-                dst = weight.at[to, pl.ds(j * h_wide, h_wide)]
-                copies.append(pltpu.make_async_copy(src, dst, sems.at[i * parts + j]))
-                copies[-1].start()
+            src = w_hbm.at[aligned(place(i) * f_wide, f_wide, f_wide)]
+            copies.append(pltpu.make_async_copy(src, weight.at[pl.ds(i * f_wide, f_wide)], sems.at[i]))
+            copies[-1].start()
         for copy in copies:
             copy.wait()
         if is_first:
@@ -334,8 +328,8 @@
 def dense(meta, mixed, cot, weight, rows, first, earlier):
     parts, chunks = len(mixed), len(mixed[0])
     width = mixed[0][0][0].shape[1]
-    features, h_wide = CORES * weight[0].shape[1], weight[0].shape[2]
-    hidden = parts * h_wide
+    features, hidden = weight.shape
+    h_wide = hidden // parts
     all_rows = cot[0].shape[0]
     step = min(rows, 256)
     flat = [m for row in mixed for m in row]
@@ -347,7 +341,7 @@
 
     kinds = [(h_wide, True)] * parts + [(width, c > 0) for _ in range(parts) for c in range(chunks)]
     whole_at = [i for i, (_, whole) in enumerate(kinds) if whole]
-    n_inputs = 1 + len(flat) + parts + CORES + len(earlier_sums)
+    n_inputs = 1 + len(flat) + parts + 1 + len(earlier_sums)
     sums_spec = pl.BlockSpec((hidden, features), lambda t, meta: (0, 0)) if is_last else any_spec()
     outs = pl.pallas_call(
         functools.partial(dense_kernel, parts, chunks, len(earlier_whole), is_first, is_last),
@@ -356,12 +350,12 @@
             grid=(rows // step,),
             in_specs=[spec(width, at) for _, at in flat]
             + [spec(h_wide, first)] * parts
-            + [any_spec()] * (CORES + len(earlier_sums) + len(earlier_whole)),
+            + [any_spec()] * (1 + len(earlier_sums) + len(earlier_whole)),
             out_specs=[spec(w, first if whole else 0) for w, whole in kinds] + [sums_spec],
             scratch_shapes=[
                 pltpu.VMEM((features, hidden), BF16),
                 pltpu.VMEM((hidden, features), F32),
-                pltpu.SemaphoreType.DMA((parts * parts,)),
+                pltpu.SemaphoreType.DMA((parts,)),
                 pltpu.SemaphoreType.DMA,
             ],
         ),
@@ -375,7 +369,7 @@
             transcendentals=rows * hidden,
         ),
         name="dense",
-    )(meta, *[m for m, _ in flat], *cot, *weight, *earlier_sums, *earlier_whole)
+    )(meta, *[m for m, _ in flat], *cot, weight, *earlier_sums, *earlier_whole)
     n = parts * chunks
     act, back = outs[:parts], outs[parts : parts + n]
     return (
@@ -410,7 +404,7 @@
         put(up_high, down_high)
 
 
-def result_of(ready, own, got, up, down):
+def result_of(ready, own, got, at, up, down):
     rows, width = own.shape
     step = min(rows // 2, 1024)
     blocks = rows // step
@@ -418,11 +412,12 @@
     here = pl.BlockSpec((step, width), lambda t: (t, 0))
     lower = pl.BlockSpec((step, width), lambda t: (jnp.minimum(t, low - 1), 0))
     upper = pl.BlockSpec((step, width), lambda t: (jnp.maximum(t - low, 0), 0))
+    there = pl.BlockSpec((step, width), lambda t: (t + at * blocks, 0))
     wide = width * (len(ready) + 1)
     return pl.pallas_call(
         functools.partial(result_kernel, len(ready), low),
         grid=(blocks,),
-        in_specs=[here] * (len(ready) + 2) + [lower, upper] * 2,
+        in_specs=[here] * (len(ready) + 1) + [there] + [lower, upper] * 2,
         out_specs=pl.BlockSpec((step, wide), lambda t: (t, 0)),
         out_shape=jax.ShapeDtypeStruct((rows, wide), BF16),
         compiler_params=params(),
@@ -432,20 +427,20 @@
 
 
 class Reduction:
-    def __init__(self, ring, own_far, own_zero, own_near, other_far, other_zero, other_near):
+    def __init__(self, ring, own_far, own_zero, own_near, other_far, other_rest):
         self.ring, self.middle = ring, ring.chips // 2
         self.near = near_places(ring)
         self.own_far, self.own_zero, self.own_near = own_far, own_zero, own_near
-        self.other_far, self.other_zero, self.other_near = other_far, other_zero, other_near
+        self.other_far, self.other_rest = other_far, other_rest
         self.rows = own_far.shape[0]
         self.half = self.rows // 2
 
+    def far_sums(self, got):
+        return [total_of(self.own_far[at : at + self.half], got[at : at + self.half]) for at in (0, self.half)]
+
     def start(self):
-        got = self.ring.sibling(self.other_far)
-        far = [total_of(self.own_far[at : at + self.half], got[at : at + self.half]) for at in (0, self.half)]
-        far = lax.optimization_barrier(far)
-        self.got_near = self.ring.sibling(lax.optimization_barrier((self.other_near, *far))[0])
-        self.got_zero = self.ring.sibling(lax.optimization_barrier((self.other_zero, self.got_near))[0])
+        far = lax.optimization_barrier(self.far_sums(self.ring.sibling(self.other_far)))
+        self.got = self.ring.sibling(lax.optimization_barrier((self.other_rest, *far))[0])
         return far
 
     def near_sum(self, offset, upper, *more):
@@ -453,7 +448,7 @@
         start = upper * self.half
         own = self.own_near[at][start : start + self.half]
         start += at * self.rows
-        return total_of(own, self.got_near[start : start + self.half], *more)
+        return total_of(own, self.got[start : start + self.half], *more)
 
     def hops(self, up, down):
         return self.ring.hop(up, 1), self.ring.hop(down, -1)
@@ -497,18 +492,17 @@
     own_meta = [ring.device_at(o, False) * rows + at for o, at in offsets]
     other_meta = [ring.device_at(o, True) * rows + at for o, at in offsets]
     spmm_meta = jnp.stack([rep] + own_meta + other_meta).astype(jnp.int32)
-    held = [1, 1] + [1] * len(near) + [1, 1, len(near)]
-    order = [middle, 0] + near
-    terms_at = [ring.device_at(o, other) * rows for other in (False, True) for o in order]
+    held = [1] * (2 + len(near)) + [1, len(near) + 1]
+    terms_at = [ring.device_at(o, False) * rows for o in [middle, 0] + near]
+    terms_at += [ring.device_at(o, True) * rows for o in [middle] + near + [0]]
     spmm_t_meta = jnp.stack([rep] + terms_at).astype(jnp.int32)
-    dense_meta = jnp.stack([rep, lax.rem(lax.axis_index("row"), CORES)]).astype(jnp.int32)
+    dense_meta = rep[None].astype(jnp.int32)
 
     def part_of(x, u):
         return lax.dynamic_slice_in_dim(x, lax.rem(rep + u, parts) * part_rows, part_rows, 0)
 
-    w_rows = weight.shape[0] // CORES
-    core = lax.rem(lax.axis_index("row"), CORES)
-    w_half = lax.all_gather(lax.dynamic_slice_in_dim(weight, core * w_rows, w_rows, 0), "rep", axis=0, tiled=False)
+    w_rows = weight.shape[0] // row_size
+    w_share = lax.dynamic_slice_in_dim(weight, lax.axis_index("row") * w_rows, w_rows, 0)
 
     cot_blocks = [part_of(cotangent, u) for u in range(parts)]
     xs = [features[:, c * width : (c + 1) * width] for c in range(chunks)]
@@ -539,9 +533,12 @@
             w.close()
             up, down = w["up" + name], w["down" + name]
             got_own[c, 2 * step - 1], got_own[c, 2 * step] = up, down
-        w.go(**{f"far_up{c}": ring.hop(up[:half], 1), f"far_down{c}": ring.hop(down[half:], -1)})
+        far_up, far_down = up[:half], down[half:]
+        w.go(**{f"far_up{c}": ring.hop(far_up, 1), f"far_down{c}": ring.hop(far_down, -1)})
         if c == 0:
             w.go(cot_ends=cot_ends, own_other=own_other)
+            w_ready = lax.optimization_barrier((w_share, far_up[:8], far_down[:8]))[0]
+            w.go(shares=send([w_ready] * parts, ends + inner))
         seen = []
         if c == last:
             for step in range(1, middle):
@@ -565,7 +562,8 @@
     for i in (-2, -1):
         got_other[last, len(offsets) + i] = ring.sibling(got_own[last, len(offsets) + i])
 
-    w.go(w_other=ring.sibling(w.gate(w_half)))
+    w_full = jnp.concatenate(ordered(w_share, w["shares"]), axis=1)
+    w_full = lax.all_gather(w.gate(w_full), "row", axis=0, tiled=True)
     for h in range(halves):
         w.go(**{f"half{h}": run_spmm(last, halves, h)})
         w.close()
@@ -577,7 +575,7 @@
     for h in range(halves):
         part = ordered(w[f"half{h}"][0], w[f"half_got{h}"])
         blocks = [[(whole[c][u], h * half_rows) for c in range(last)] + [(part[u], 0)] for u in range(parts)]
-        act, back, sums, earlier = dense(dense_meta, blocks, cot, (w_half, w["w_other"]), half_rows, h * half_rows, earlier)
+        act, back, sums, earlier = dense(dense_meta, blocks, cot, w_full, half_rows, h * half_rows, earlier)
         w.go(**{f"back{h}": [b[0] for b in back]})
         if h == halves - 1:
             w.go(whole=(act, back, sums))
@@ -586,27 +584,17 @@
     act, back, sums = w["whole"]
 
     share = sums.shape[0] // row_size
-    first_got = w.pending[f"back_got{halves - 1}"][1]
-    sums = lax.optimization_barrier((sums, first_got))[0]
 
     def sums_for(offset, other):
         return lax.dynamic_slice_in_dim(sums, ring.device_at(offset, other) * share, share, 0)
 
-    wg = Reduction(
-        ring,
-        sums_for(middle, False),
-        sums_for(0, False),
-        [sums_for(o, False) for o in near],
-        sums_for(middle, True),
-        sums_for(0, True),
-        jnp.concatenate([sums_for(o, True) for o in near]),
-    )
-    wg_far = wg.hops(*wg.start())
-    w.go(wg=(wg.own_zero, wg.own_near, wg.got_near, wg.got_zero, wg_far))
+    w.go(wg_got=ring.sibling(jnp.concatenate([sums_for(o, True) for o in [middle] + near + [0]])))
     w.close()
-    wg.own_zero, wg.own_near, wg.got_near, wg.got_zero, wg_far = w["wg"]
-    wg_bound, wg_free = wg.bound_sums(wg_far), wg.free_sums()
-    w.go(wg_got=wg.hops(jnp.concatenate([wg_bound[0], wg_free[0]]), jnp.concatenate([wg_free[1], wg_bound[1]])))
+    wg_got = w["wg_got"]
+    wg = Reduction(ring, sums_for(middle, False), sums_for(0, False), [sums_for(o, False) for o in near], None, None)
+    wg.got = wg_got[share:]
+    wg_far, wg_free = wg.far_sums(wg_got[:share]), wg.free_sums()
+    w.go(wg_first=wg.hops(jnp.concatenate([wg_far[0], wg_free[0]]), jnp.concatenate([wg_free[1], wg_far[1]])))
 
     def run_spmm_t(c, grads):
         return spmm_t(tiles, columns, counts, spmm_t_meta, grads, parts, held, rows, rows * row_size)
@@ -616,10 +604,9 @@
     for c in range(1, chunks):
         w.go(**{f"rest_got{c}": send([w.gate(b[c]) for b in back], ends + inner)})
     w.close()
-    wg_got = w["wg_got"]
-    wg_got = wg.finish(
-        (wg_got[0][wg.half :], wg_got[1][: wg.half]), (wg_got[0][: wg.half], wg_got[1][wg.half :])
-    )
+    up, down = w["wg_first"]
+    wg_free = up[wg.half :], down[: wg.half]
+    wg_bound = wg.bound_sums((up[: wg.half], down[wg.half :]))
 
     def send_act(shifts, *after):
         return send([lax.optimization_barrier((a, *after))[0] for a in act], shifts)
@@ -627,10 +614,10 @@
     reductions = []
     for c in range(chunks):
         terms = w[f"terms{c}"]
-        red = Reduction(ring, terms[0], terms[1], terms[2:-3], terms[-3], terms[-2], terms[-1])
+        red = Reduction(ring, terms[0], terms[1], terms[2:-2], terms[-2], terms[-1])
         reductions.append(red)
         far = red.start()
-        w.go(**{f"far{c}": red.hops(*far), f"zero{c}": red.got_zero})
+        w.go(**{f"far{c}": red.hops(*far)})
         free = red.free_sums()
         if c < last:
             grads = ordered(back[0][c + 1], w[f"rest_got{c + 1}"])
@@ -645,23 +632,34 @@
             free = [w.gate(f) for f in free]
         red.free_hops = w[f"free{c}"] if c < last else red.hops(*free)
         bound = red.bound_sums(w[f"far{c}"])
+        if c == 0:
+            bound = [jnp.concatenate([b, v.reshape(-1, width)]) for b, v in zip(bound, wg_bound)]
         red.bound_hops = red.hops(*bound)
         if c < last:
             w.go(**{f"bound{c}": red.bound_hops})
-    high_end = send_act(ends[1:], bound[0][:8])
-
-    up, down = (jnp.concatenate(halves_of) for halves_of in wg_got)
-    block = total_of(wg.own_zero, wg.got_zero, up, down)
-    cuts = [lax.optimization_barrier((block, bound[0][:8]))[0][:, u * f_wide : (u + 1) * f_wide] for u in range(parts)]
-    cuts_got = send(cuts, ends + inner)
-    weight_grad = functools.reduce(lambda a, b: a + b, [v.astype(F32) for v in [cuts[0], *cuts_got.values()]])
 
     feature_grad = ()
     for c, red in enumerate(reductions):
         bound_hops = w[f"bound{c}"] if c < last else red.bound_hops
+        if c == 0:
+            wg_bound = [v[red.half :].reshape(wg.half, -1) for v in bound_hops]
+            if middle > 2:
+                bound_hops = [v[: red.half] for v in bound_hops]
         up, down = red.finish(red.free_hops, bound_hops)
-        feature_grad = (result_of(feature_grad, red.own_zero, w[f"zero{c}"], up, down),)
+        at = len(near)
+        feature_grad = (result_of(feature_grad, red.own_zero, red.got, at, up, down),)
+        if c == 0:
+            early = feature_grad[0][:8]
     feature_grad = feature_grad[0]
+
+    up, down = (jnp.concatenate(halves_of) for halves_of in wg.finish(wg_free, wg_bound))
+    block = total_of(wg.own_zero, wg.got[len(near) * share :], up, down)
+    if chunks > 1:
+        block, early = lax.optimization_barrier((block, early))
+    cuts = [block[:, u * f_wide : (u + 1) * f_wide] for u in range(parts)]
+    cuts_got = send(cuts, ends + inner)
+    weight_grad = functools.reduce(lambda a, b: a + b, [v.astype(F32) for v in [cuts[0], *cuts_got.values()]])
+    high_end = send_act(ends[1:], early if chunks > 1 else bound[0][:8])
     weight_grad = weight_grad.T
     got = {"act_ends": {**w["low_end"], **high_end}, "act_inner": w["act_inner"]}
     act = ordered(act[0], got["act_ends"], got["act_inner"])

time: 356 us -> 362 us (1.017)
  local copies, waits for them, and re-layouts: 25.6 us -> 40.4 us
  waiting for transfers between devices: 113 us -> 104 us
  other arithmetic: 10.4 us -> 18.8 us
  starting transfers between devices: 80.1 us -> 72 us
    ppermute x24 -> x22, waiting for transfers between devices: 57.2 us -> 36.5 us  [hop(): return lax.ppermute(value, 'row', self.perm(step))]
    ppermute x27 -> x30, waiting for transfers between devices: 40.1 us -> 57.5 us  [send(): lax.ppermute(blocks[s], 'rep', [(i, (i + s) % size) for i in range(size)])]
    convert_element_type x8, other arithmetic: 9.6 us -> 16.1 us  [total_of(): functools.reduce(lambda a, b: a + b, [v.astype(F32) for v in values])]
    slice x5 -> x9, local copies, waits for them, and re-layouts: 3.03 us -> 9.48 us  [the longest x4 5.4 us: local(): far_up, far_down = (up[:half], down[half:])]
    ppermute x19 -> x14, waiting for transfers between devices: 15.5 us -> 9.85 us  [sibling(): return lax.ppermute(value, 'row', [(d, d ^ 1) for d in range(self.devices)])]
    ppermute x24 -> x22, starting transfers between devices: 28.2 us -> 23.3 us  [hop(): return lax.ppermute(value, 'row', self.perm(step))]
    unnamed x130 -> x136, local copies, waits for them, and re-layouts: 6.54 us -> 9.94 us
    ppermute x27 -> x30, starting transfers between devices: 48.6 us -> 46.4 us  [send(): lax.ppermute(blocks[s], 'rep', [(i, (i + s) % size) for i in range(size)])]
  transfers between devices with their start and end apart: 71 -> 67, of which waited for: 30 -> 24; matrix products, arithmetic and copies ran while one was open for 6% -> 12% of each run, Pallas kernels for 28% -> 27%
where the time goes in v10:
time: 362 us; the launch traced here: 360 us
  waiting for transfers between devices  104 us (29%)
  Pallas kernels  102 us (28%)
  starting transfers between devices  72 us (20%)
  local copies, waits for them, and re-layouts  40.4 us (11%)
  between operations  22.8 us (6%)
  other arithmetic  18.8 us (5%)
    ppermute x30, waiting for transfers between devices, send(): lax.ppermute(blocks[s], 'rep', [(i, (i + s) % size) for i in range(size)])  57.5 us
    ppermute x30, starting transfers between devices, send(): lax.ppermute(blocks[s], 'rep', [(i, (i + s) % size) for i in range(size)])  46.4 us
    pallas_call x3, Pallas kernels, spmm(): pl.pallas_call(functools.partial(spmm_kernel, len(pieces), per_part, skip...  36.6 us
    ppermute x22, waiting for transfers between devices, hop(): return lax.ppermute(value, 'row', self.perm(step))  36.5 us
    pallas_call x2, Pallas kernels, spmm_t(): pl.pallas_call(functools.partial(spmm_t_kernel, len(grads), per_part, len...  34.6 us
    ppermute x22, starting transfers between devices, hop(): return lax.ppermute(value, 'row', self.perm(step))  23.3 us
    pallas_call x2, Pallas kernels, dense(): pl.pallas_call(functools.partial(dense_kernel, parts, chunks, len(earlier...  21.6 us
    convert_element_type x8, other arithmetic, total_of(): functools.reduce(lambda a, b: a + b, [v.astype(F32) for v in values])  16.1 us
  transfers between devices with their start and end apart: 67, of which 24 were waited for; matrix products, arithmetic and copies ran while one was open for 12% of the time, Pallas kernels for 27%

profile of v10, /device:TPU:0, one launch (start us, length us, event | category | flops | bytes accessed | tf_op | source)
XLA Modules:
  0.0 359.8 jit_solution(4358159879720311)
XLA Ops:
  9.0 3.0 collective-permute-start
  12.1 4.1 %collective-permute-start.7 = (bf16[128,256]{1,0:T(8,128)(2,1)S(1)}, bf16[128,256]{1,0:T(8,128)(2,1)S(1)}, u32[]{:S(2)}, u32[]{:S(2)}) collective-permute-start(bf16[128,256]{1,0:T(8,128)(2,1)S(1)} %constant_dynamic-slice_fusion.3), channel_id=1, source_target_pairs={{0,3},{1,0},{2,1},{3,2},{4,7},{5,4},{6,5},{7,6},{8,11},{9,8},{10,9... | collective-permute-start | bytes 196616 | tf_op jit(solution)/shard_map/ppermute | solution.py:87
  16.2 2.4 collective-permute-done.7
  18.7 2.7 constant_dynamic-slice_fusion.1
  30.5 4.7 %collective-permute-done.refs_1_ = bf16[4096,128]{1,0:T(8,128)(2,1)} collective-permute-done((bf16[4096,128]{1,0:T(8,128)(2,1)S(1)}, bf16[4096,128]{1,0:T(8,128)(2,1)}, u32[]{:S(2)}, u32[]{:S(2)}) %collective-permute-start) | collective-permute-done | bytes 1048608 | tf_op jit(solution)/shard_map/ppermute | solution.py:38
  35.3 3.8 %collective-permute-start.4 = (bf16[1024,256]{1,0:T(8,128)(2,1)S(1)}, bf16[1024,256]{1,0:T(8,128)(2,1)S(1)}, u32[]{:S(2)}, u32[]{:S(2)}) collective-permute-start(bf16[1024,256]{1,0:T(8,128)(2,1)S(1)} %get-tuple-element.353), channel_id=1, source_target_pairs={{0,3},{1,0},{2,1},{3,2},{4,7},{5,4},{6,5},{7,6},{8,11},{9,8},{10,9... | collective-permute-start | bytes 1572872 | tf_op jit(solution)/shard_map/ppermute | solution.py:87
  40.9 1.9 slice.186
  42.8 1.9 slice.187
  44.6 6.8 %collective-permute-done.4.refs_9_ = bf16[1024,256]{1,0:T(8,128)(2,1)S(1)} collective-permute-done((bf16[1024,256]{1,0:T(8,128)(2,1)S(1)}, bf16[1024,256]{1,0:T(8,128)(2,1)S(1)}, u32[]{:S(2)}, u32[]{:S(2)}) %collective-permute-start.4) | collective-permute-done | bytes 524320 | tf_op jit(solution)/shard_map/ppermute | solution.py:87
  53.0 8.6 %collective-permute-done.5.refs_11_ = bf16[1024,256]{1,0:T(8,128)(2,1)S(1)} collective-permute-done((bf16[1024,256]{1,0:T(8,128)(2,1)}, bf16[1024,256]{1,0:T(8,128)(2,1)S(1)}, u32[]{:S(2)}, u32[]{:S(2)}) %collective-permute-start.5) | collective-permute-done | bytes 524320 | tf_op jit(solution)/shard_map/ppermute | solution.py:87
  63.7 9.9 %collective-permute-done.3.refs_4_ = bf16[2048,128]{1,0:T(8,128)(2,1)S(1)} collective-permute-done((bf16[2048,128]{1,0:T(8,128)(2,1)}, bf16[2048,128]{1,0:T(8,128)(2,1)S(1)}, u32[]{:S(2)}, u32[]{:S(2)}) %collective-permute-start.3) | collective-permute-done | bytes 524320 | tf_op jit(solution)/shard_map/ppermute | solution.py:38
  76.5 2.8 collective-permute-start.10
  79.3 3.0 fusion
  83.3 14.4 %spmm.3 = (bf16[1024,128]{1,0:T(8,128)(2,1)}, bf16[1024,128]{1,0:T(8,128)(2,1)}, bf16[1024,128]{1,0:T(8,128)(2,1)}, bf16[1024,128]{1,0:T(8,128)(2,1)}) custom-call(s32[32,16]{1,0:T(8,128)} %copy.69.cols, s32[32]{0:T(128)} %counts.9, s32[11]{0:T(128)} %stack.75.meta, bf16[32,16,128,128]{3,2,1,0:T(8,128)(2,1)} %tiles.9, bf16[4096,128]{1,0:T(8,128)(2,1)} %copy-done.8, ...), custom_call_target="tpu_custom_call" | custom-call | flops 2147483648 | bytes 25165824 | tf_op jit(solution)/shard_map/spmm/pallas_call | solution.py:158
  97.8 5.5 %collective-permute-done.10.refs_10_ = bf16[1024,256]{1,0:T(8,128)(2,1)S(1)} collective-permute-done((bf16[1024,256]{1,0:T(8,128)(2,1)}, bf16[1024,256]{1,0:T(8,128)(2,1)S(1)}, u32[]{:S(2)}, u32[]{:S(2)}) %collective-permute-start.10) | collective-permute-done | bytes 524320 | tf_op jit(solution)/shard_map/ppermute | solution.py:87
  110.5 3.0 collective-permute-start.21
  114.2 6.4 %collective-permute-done.17.refs_3_ = bf16[2048,128]{1,0:T(8,128)(2,1)S(1)} collective-permute-done((bf16[2048,128]{1,0:T(8,128)(2,1)}, bf16[2048,128]{1,0:T(8,128)(2,1)S(1)}, u32[]{:S(2)}, u32[]{:S(2)}) %collective-permute-start.17) | collective-permute-done | bytes 524320 | tf_op jit(solution)/shard_map/ppermute | solution.py:38
  121.9 2.5 collective-permute-done.21.refs_2_
  128.0 11.2 %spmm.4 = (bf16[512,128]{1,0:T(8,128)(2,1)}, bf16[512,128]{1,0:T(8,128)(2,1)}, bf16[512,128]{1,0:T(8,128)(2,1)}, bf16[512,128]{1,0:T(8,128)(2,1)}) custom-call(s32[32,16]{1,0:T(8,128)} %copy.69.cols, s32[32]{0:T(128)} %counts.9, s32[11]{0:T(128)} %stack.75.meta, bf16[32,16,128,128]{3,2,1,0:T(8,128)(2,1)} %tiles.9, bf16[4096,128]{1,0:T(8,128)(2,1)} %copy-done.2, ...), custom_call_target="tpu_custom_call" | custom-call | flops 1073741824 | bytes 16777216 | tf_op jit(solution)/shard_map/spmm/pallas_call | solution.py:158
  140.7 2.8 collective-permute-start.26
  144.0 11.1 %spmm.5 = (bf16[512,128]{1,0:T(8,128)(2,1)}, bf16[512,128]{1,0:T(8,128)(2,1)}, bf16[512,128]{1,0:T(8,128)(2,1)}, bf16[512,128]{1,0:T(8,128)(2,1)}) custom-call(s32[32,16]{1,0:T(8,128)} %copy.69.cols, s32[32]{0:T(128)} %counts.9, s32[11]{0:T(128)} %stack.75.meta, bf16[32,16,128,128]{3,2,1,0:T(8,128)(2,1)} %tiles.9, bf16[4096,128]{1,0:T(8,128)(2,1)} %copy-done.2, ...), custom_call_target="tpu_custom_call" | custom-call | flops 1073741824 | bytes 16777216 | tf_op jit(solution)/shard_map/spmm/pallas_call | solution.py:158
  155.3 3.2 collective-permute-start.29
  159.7 10.3 %dense.2 = (bf16[1024,256]{1,0:T(8,128)(2,1)}, bf16[1024,256]{1,0:T(8,128)(2,1)}, bf16[1024,256]{1,0:T(8,128)(2,1)}, bf16[1024,256]{1,0:T(8,128)(2,1)}, bf16[512...) custom-call(s32[1]{0:T(128)} %bitcast.meta, ...), custom_call_target="tpu_custom_call" | custom-call | flops 3221225472 | bytes 10485760 | tf_op jit(solution)/shard_map/dense/pallas_call | solution.py:346
  170.8 3.1 collective-permute-start.32
  174.6 11.3 %dense.3 = (bf16[1024,256]{1,0:T(8,128)(2,1)}, bf16[1024,256]{1,0:T(8,128)(2,1)}, bf16[1024,256]{1,0:T(8,128)(2,1)}, bf16[1024,256]{1,0:T(8,128)(2,1)}, bf16[512...) custom-call(s32[1]{0:T(128)} %bitcast.meta, ...), custom_call_target="tpu_custom_call", output_to_operand_aliasing={{0}: (15, {}), {1}: (16, {}), {2}: (17, {}), {3}: (18, {}),... | custom-call | flops 3221225472 | bytes 10485760 | tf_op jit(solution)/shard_map/dense/pallas_call | solution.py:346
  187.7 3.2 collective-permute-start.36
  192.0 3.1 collective-permute-done.36.refs_3_
  195.1 9.4 %collective-permute-done.37.refs_5_ = bf16[512,128]{1,0:T(8,128)(2,1)S(1)} collective-permute-done((bf16[512,128]{1,0:T(8,128)(2,1)S(1)}, bf16[512,128]{1,0:T(8,128)(2,1)S(1)}, u32[]{:S(2)}, u32[]{:S(2)}) %collective-permute-start.37) | collective-permute-done | bytes 131104 | tf_op jit(solution)/shard_map/ppermute | solution.py:87
  206.3 3.4 collective-permute-start.42
  213.2 17.4 %spmm_t.2 = (bf16[4096,128]{1,0:T(8,128)(2,1)}, bf16[4096,128]{1,0:T(8,128)(2,1)}, bf16[4096,128]{1,0:T(8,128)(2,1)}, bf16[4096,128]{1,0:T(8,128)(2,1)}, bf16[40...) custom-call(s32[32,16]{1,0:T(8,128)} %copy.69.cols, s32[32]{0:T(128)} %counts.9, s32[9]{0:T(128)} %stack.84.meta, ...), custom_call_target="tpu_custom_call" | custom-call | flops 2147483648 | bytes 25165824 | tf_op jit(solution)/shard_map/spmm_t/pallas_call | solution.py:241
  230.8 2.9 collective-permute-done.45
  237.4 3.8 %collective-permute-done.48.refs_1_ = bf16[12288,128]{1,0:T(8,128)(2,1)} collective-permute-done((bf16[12288,128]{1,0:T(8,128)(2,1)}, bf16[12288,128]{1,0:T(8,128)(2,1)}, u32[]{:S(2)}, u32[]{:S(2)}) %collective-permute-start.48) | collective-permute-done | bytes 3145760 | tf_op jit(solution)/shard_map/ppermute | solution.py:41
  244.3 2.0 collective-permute-start.51
  246.8 17.3 %spmm_t.3 = (bf16[4096,128]{1,0:T(8,128)(2,1)}, bf16[4096,128]{1,0:T(8,128)(2,1)}, bf16[4096,128]{1,0:T(8,128)(2,1)}, bf16[4096,128]{1,0:T(8,128)(2,1)}, bf16[40...) custom-call(s32[32,16]{1,0:T(8,128)} %copy.69.cols, s32[32]{0:T(128)} %counts.9, s32[9]{0:T(128)} %stack.84.meta, ...), custom_call_target="tpu_custom_call" | custom-call | flops 2147483648 | bytes 25165824 | tf_op jit(solution)/shard_map/spmm_t/pallas_call | solution.py:241
  264.1 6.0 %collective-permute-done.51 = bf16[1024,256]{1,0:T(8,128)(2,1)S(1)} collective-permute-done((bf16[1024,256]{1,0:T(8,128)(2,1)S(1)}, bf16[1024,256]{1,0:T(8,128)(2,1)S(1)}, u32[]{:S(2)}, u32[]{:S(2)}) %collective-permute-start.51) | collective-permute-done | bytes 524320 | tf_op jit(solution)/shard_map/ppermute | solution.py:87
  270.2 2.9 collective-permute-done.54
  273.1 2.4 add_convert_fusion.4
  277.2 2.2 add_convert_fusion.6
  283.7 8.4 %collective-permute-done.57 = bf16[1024,256]{1,0:T(8,128)(2,1)} collective-permute-done((bf16[1024,256]{1,0:T(8,128)(2,1)}, bf16[1024,256]{1,0:T(8,128)(2,1)}, u32[]{:S(2)}, u32[]{:S(2)}) %collective-permute-start.57) | collective-permute-done | bytes 524320 | tf_op jit(solution)/shard_map/ppermute | solution.py:87
  295.8 2.5 collective-permute-done.53.refs_5_
  298.3 3.9 %collective-permute-start.35 = (bf16[1024,256]{1,0:T(8,128)(2,1)}, bf16[1024,256]{1,0:T(8,128)(2,1)}, u32[]{:S(2)}, u32[]{:S(2)}) collective-permute-start(bf16[1024,256]{1,0:T(8,128)(2,1)} %get-tuple-element.249), channel_id=1, source_target_pairs={{0,3},{1,0},{2,1},{3,2},{4,7},{5,4},{6,5},{7,6},{8,11},{9,8},{10,9... | collective-permute-start | bytes 1572872 | tf_op jit(solution)/shard_map/ppermute | solution.py:87
  302.1 7.9 %collective-permute-done.55 = bf16[2048,128]{1,0:T(8,128)(2,1)} collective-permute-done((bf16[2048,128]{1,0:T(8,128)(2,1)}, bf16[2048,128]{1,0:T(8,128)(2,1)}, u32[]{:S(2)}, u32[]{:S(2)}) %collective-permute-start.55) | collective-permute-done | bytes 524320 | tf_op jit(solution)/shard_map/ppermute | solution.py:38
  317.5 4.5 %add_convert_fusion = (bf16[2048,128]{1,0:T(8,128)(2,1)}, bf16[2048,128]{1,0:T(8,128)(2,1)}, bf16[2048,128]{1,0:T(8,128)(2,1)}, bf16[2048,128]{1,0:T(8,128)(2,1)}) fusion(bf16[2048,128]{1,0:T(8,128)(2,1)} %collective-permute-done.56, bf16[12288,128]{1,0:T(8,128)(2,1)S(1)} %collective-permute-done.58.refs_2_, bf16[4096,128]{1,0:T(8,128)(2,1)} %get-tuple-element.322, ...), kind=kLoop, calls=%fused_computation.1 | loop fusion | flops 5242880 | bytes 7340032 | tf_op jit(solution)/shard_map/convert_element_type | solution.py:384
  327.9 3.8 %collective-permute-start.64 = (bf16[128,256]{1,0:T(8,128)(2,1)S(1)}, bf16[128,256]{1,0:T(8,128)(2,1)S(1)}, u32[]{:S(2)}, u32[]{:S(2)}) collective-permute-start(bf16[128,256]{1,0:T(8,128)(2,1)S(1)} %get-tuple-element.362), channel_id=1, source_target_pairs={{0,3},{1,0},{2,1},{3,2},{4,7},{5,4},{6,5},{7,6},{8,11},{9,8},{10,9... | collective-permute-start | bytes 196616 | tf_op jit(solution)/shard_map/ppermute | solution.py:87
  332.6 4.3 %feature_grad.2.refs_0_ = bf16[4096,128]{1,0:T(8,128)(2,1)} custom-call(bf16[4096,128]{1,0:T(8,128)(2,1)} %get-tuple-element.311.refs_0_, bf16[12288,128]{1,0:T(8,128)(2,1)} %collective-permute-done.48.refs_1_, bf16[2560,128]{1,0:T(8,128)(2,1)} %collective-permute-done.52.refs_2_, bf16[2048,128]{1,0:T(8,128)(2,1)} %copy-done.34, ...), custom_call_target="tpu_custom_call" | custom-call | flops 2097152 | bytes 7340032 | tf_op jit(solution)/shard_map/feature_grad/pallas_call | solution.py:417
  339.0 3.0 collective-permute-done.65
  342.9 3.8 %collective-permute-done.59.refs_3_ = bf16[2048,128]{1,0:T(8,128)(2,1)S(1)} collective-permute-done((bf16[2048,128]{1,0:T(8,128)(2,1)}, bf16[2048,128]{1,0:T(8,128)(2,1)S(1)}, u32[]{:S(2)}, u32[]{:S(2)}) %collective-permute-start.59) | collective-permute-done | bytes 524320 | tf_op jit(solution)/shard_map/ppermute | solution.py:38
  348.2 4.8 %feature_grad.3 = bf16[4096,256]{1,0:T(8,128)(2,1)} custom-call(bf16[4096,128]{1,0:T(8,128)(2,1)} %feature_grad.2.refs_0_, bf16[4096,128]{1,0:T(8,128)(2,1)} %get-tuple-element.316.refs_1_, bf16[12288,128]{1,0:T(8,128)(2,1)} %copy-done.3, bf16[2048,128]{1,0:T(8,128)(2,1)} %copy-done.23, bf16[2048,128]{1,0:T(8,128)(2,1)} %copy-done.22, ...), custom_call_target="tpu_custom_call" | custom-call | flops 2097152 | bytes 7340032 | tf_op jit(solution)/shard_map/feature_grad/pallas_call | solution.py:417
  (274 shorter events, 74.0 us)
Async XLA Ops:
  7.2 152.5 %all-gather.2.cloned.1.call-start = ((), (), s32[]{:S(2)}) async-start(), calls=%async_computation | async-start | bytes 2359296 | tf_op jit(solution)/shard_map/all_gather | solution.py:566
  9.0 26.3 %collective-permute-start = (bf16[4096,128]{1,0:T(8,128)(2,1)S(1)}, bf16[4096,128]{1,0:T(8,128)(2,1)}, u32[]{:S(2)}, u32[]{:S(2)}) collective-permute-start(bf16[4096,128]{1,0:T(8,128)(2,1)S(1)} %get-tuple-element.359.refs_0_), channel_id=1, source_target_pairs={{0,8},{4,12},{8,24},{12,28},{24,16},{28,20},{16,0},{20,4},{1,9},{5... | collective-permute-start | bytes 3145736 | tf_op jit(solution)/shard_map/ppermute | solution.py:38
  12.0 27.1 %collective-permute-start.1 = (bf16[4096,128]{1,0:T(8,128)(2,1)S(1)}, bf16[4096,128]{1,0:T(8,128)(2,1)}, u32[]{:S(2)}, u32[]{:S(2)}) collective-permute-start(bf16[4096,128]{1,0:T(8,128)(2,1)S(1)} %get-tuple-element.359.refs_0_), channel_id=1, source_target_pairs={{0,16},{4,20},{8,0},{12,4},{24,8},{28,12},{16,24},{20,28},{1,17},{... | collective-permute-start | bytes 3145736 | tf_op jit(solution)/shard_map/ppermute | solution.py:38
  12.1 61.6 %collective-permute-start.6 = (bf16[4096,256]{1,0:T(8,128)(2,1)}, bf16[4096,256]{1,0:T(8,128)(2,1)}, u32[]{:S(2)}, u32[]{:S(2)}) collective-permute-start(bf16[4096,256]{1,0:T(8,128)(2,1)} %param.58), channel_id=1, source_target_pairs={{0,4},{4,0},{8,12},{12,8},{16,20},{20,16},{24,28},{28,24},{1,5},{5... | collective-permute-start | bytes 6291464 | tf_op jit(solution)/shard_map/ppermute | solution.py:41
  16.2 24.2 %collective-permute-start.8 = (bf16[128,256]{1,0:T(8,128)(2,1)S(1)}, bf16[128,256]{1,0:T(8,128)(2,1)S(1)}, u32[]{:S(2)}, u32[]{:S(2)}) collective-permute-start(bf16[128,256]{1,0:T(8,128)(2,1)S(1)} %constant_dynamic-slice_fusion.3), channel_id=1, source_target_pairs={{0,2},{1,3},{2,0},{3,1},{4,6},{5,7},{6,4},{7,5},{8,10},{9,11},{10,... | collective-permute-start | bytes 196616 | tf_op jit(solution)/shard_map/ppermute | solution.py:87
  18.6 21.8 %collective-permute-start.9 = (bf16[128,256]{1,0:T(8,128)(2,1)S(1)}, bf16[128,256]{1,0:T(8,128)(2,1)S(1)}, u32[]{:S(2)}, u32[]{:S(2)}) collective-permute-start(bf16[128,256]{1,0:T(8,128)(2,1)S(1)} %constant_dynamic-slice_fusion.3), channel_id=1, source_target_pairs={{0,1},{1,2},{2,3},{3,0},{4,5},{5,6},{6,7},{7,4},{8,9},{9,10},{10,1... | collective-permute-start | bytes 196616 | tf_op jit(solution)/shard_map/ppermute | solution.py:87
  35.3 16.2 %collective-permute-start.4 = (bf16[1024,256]{1,0:T(8,128)(2,1)S(1)}, bf16[1024,256]{1,0:T(8,128)(2,1)S(1)}, u32[]{:S(2)}, u32[]{:S(2)}) collective-permute-start(bf16[1024,256]{1,0:T(8,128)(2,1)S(1)} %get-tuple-element.353), channel_id=1, source_target_pairs={{0,3},{1,0},{2,1},{3,2},{4,7},{5,4},{6,5},{7,6},{8,11},{9,8},{10,9... | collective-permute-start | bytes 1572872 | tf_op jit(solution)/shard_map/ppermute | solution.py:87
  39.1 22.4 %collective-permute-start.5 = (bf16[1024,256]{1,0:T(8,128)(2,1)}, bf16[1024,256]{1,0:T(8,128)(2,1)S(1)}, u32[]{:S(2)}, u32[]{:S(2)}) collective-permute-start(bf16[1024,256]{1,0:T(8,128)(2,1)} %get-tuple-element.355), channel_id=1, source_target_pairs={{0,1},{1,2},{2,3},{3,0},{4,5},{5,6},{6,7},{7,4},{8,9},{9,10},{10,1... | collective-permute-start | bytes 1572872 | tf_op jit(solution)/shard_map/ppermute | solution.py:87
  40.4 36.1 %collective-permute-start.13 = (bf16[4096,128]{1,0:T(8,128)(2,1)}, bf16[4096,128]{1,0:T(8,128)(2,1)}, u32[]{:S(2)}, u32[]{:S(2)}) collective-permute-start(bf16[4096,128]{1,0:T(8,128)(2,1)} %collective-permute-done.refs_1_), channel_id=1, source_target_pairs={{0,4},{4,0},{8,12},{12,8},{16,20},{20,16},{24,28},{28,24},{1,5},{5... | collective-permute-start | bytes 3145736 | tf_op jit(solution)/shard_map/ppermute | solution.py:41
  40.4 36.0 %collective-permute-start.14 = (bf16[4096,128]{1,0:T(8,128)(2,1)}, bf16[4096,128]{1,0:T(8,128)(2,1)}, u32[]{:S(2)}, u32[]{:S(2)}) collective-permute-start(bf16[4096,128]{1,0:T(8,128)(2,1)} %collective-permute-done.1.refs_2_), channel_id=1, source_target_pairs={{0,4},{4,0},{8,12},{12,8},{16,20},{20,16},{24,28},{28,24},{1,5},{5... | collective-permute-start | bytes 3145736 | tf_op jit(solution)/shard_map/ppermute | solution.py:41
  51.5 12.3 %collective-permute-start.2 = (bf16[2048,128]{1,0:T(8,128)(2,1)}, bf16[2048,128]{1,0:T(8,128)(2,1)S(1)}, u32[]{:S(2)}, u32[]{:S(2)}) collective-permute-start(bf16[2048,128]{1,0:T(8,128)(2,1)} %slice.186), channel_id=1, source_target_pairs={{0,8},{4,12},{8,24},{12,28},{24,16},{28,20},{16,0},{20,4},{1,9},{5... | collective-permute-start | bytes 1572872 | tf_op jit(solution)/shard_map/ppermute | solution.py:38
  61.5 12.1 %collective-permute-start.3 = (bf16[2048,128]{1,0:T(8,128)(2,1)}, bf16[2048,128]{1,0:T(8,128)(2,1)S(1)}, u32[]{:S(2)}, u32[]{:S(2)}) collective-permute-start(bf16[2048,128]{1,0:T(8,128)(2,1)} %slice.187), channel_id=1, source_target_pairs={{0,16},{4,20},{8,0},{12,4},{24,8},{28,12},{16,24},{20,28},{1,17},{... | collective-permute-start | bytes 1572872 | tf_op jit(solution)/shard_map/ppermute | solution.py:38
  74.4 28.8 %collective-permute-start.11 = (bf16[4096,128]{1,0:T(8,128)(2,1)S(1)}, bf16[4096,128]{1,0:T(8,128)(2,1)S(1)}, u32[]{:S(2)}, u32[]{:S(2)}) collective-permute-start(bf16[4096,128]{1,0:T(8,128)(2,1)S(1)} %get-tuple-element.168.refs_0_), channel_id=1, source_target_pairs={{0,8},{4,12},{8,24},{12,28},{24,16},{28,20},{16,0},{20,4},{1,9},{5... | collective-permute-start | bytes 3145736 | tf_op jit(solution)/shard_map/ppermute | solution.py:38
  75.9 27.4 %collective-permute-start.12 = (bf16[4096,128]{1,0:T(8,128)(2,1)S(1)}, bf16[4096,128]{1,0:T(8,128)(2,1)S(1)}, u32[]{:S(2)}, u32[]{:S(2)}) collective-permute-start(bf16[4096,128]{1,0:T(8,128)(2,1)S(1)} %get-tuple-element.168.refs_0_), channel_id=1, source_target_pairs={{0,16},{4,20},{8,0},{12,4},{24,8},{28,12},{16,24},{20,28},{1,17},{... | collective-permute-start | bytes 3145736 | tf_op jit(solution)/shard_map/ppermute | solution.py:38
  76.5 26.8 %collective-permute-start.10 = (bf16[1024,256]{1,0:T(8,128)(2,1)}, bf16[1024,256]{1,0:T(8,128)(2,1)S(1)}, u32[]{:S(2)}, u32[]{:S(2)}) collective-permute-start(bf16[1024,256]{1,0:T(8,128)(2,1)} %get-tuple-element.167), channel_id=1, source_target_pairs={{0,2},{1,3},{2,0},{3,1},{4,6},{5,7},{6,4},{7,5},{8,10},{9,11},{10,... | collective-permute-start | bytes 1572872 | tf_op jit(solution)/shard_map/ppermute | solution.py:87
  106.6 14.0 %collective-permute-start.17 = (bf16[2048,128]{1,0:T(8,128)(2,1)}, bf16[2048,128]{1,0:T(8,128)(2,1)S(1)}, u32[]{:S(2)}, u32[]{:S(2)}) collective-permute-start(bf16[2048,128]{1,0:T(8,128)(2,1)} %slice.190), channel_id=1, source_target_pairs={{0,8},{4,12},{8,24},{12,28},{24,16},{28,20},{16,0},{20,4},{1,9},{5... | collective-permute-start | bytes 1572872 | tf_op jit(solution)/shard_map/ppermute | solution.py:38
  108.2 13.8 %collective-permute-start.18 = (bf16[2048,128]{1,0:T(8,128)(2,1)}, bf16[2048,128]{1,0:T(8,128)(2,1)S(1)}, u32[]{:S(2)}, u32[]{:S(2)}) collective-permute-start(bf16[2048,128]{1,0:T(8,128)(2,1)} %slice.191), channel_id=1, source_target_pairs={{0,16},{4,20},{8,0},{12,4},{24,8},{28,12},{16,24},{20,28},{1,17},{... | collective-permute-start | bytes 1572872 | tf_op jit(solution)/shard_map/ppermute | solution.py:38
  109.7 12.3 %collective-permute-start.22 = (bf16[1024,128]{1,0:T(8,128)(2,1)}, bf16[1024,128]{1,0:T(8,128)(2,1)S(1)}, u32[]{:S(2)}, u32[]{:S(2)}) collective-permute-start(bf16[1024,128]{1,0:T(8,128)(2,1)} %get-tuple-element.181), channel_id=1, source_target_pairs={{0,1},{1,2},{2,3},{3,0},{4,5},{5,6},{6,7},{7,4},{8,9},{9,10},{10,1... | collective-permute-start | bytes 786440 | tf_op jit(solution)/shard_map/ppermute | solution.py:87
  110.5 13.9 %collective-permute-start.21 = (bf16[1024,128]{1,0:T(8,128)(2,1)}, bf16[1024,128]{1,0:T(8,128)(2,1)}, u32[]{:S(2)}, u32[]{:S(2)}) collective-permute-start(bf16[1024,128]{1,0:T(8,128)(2,1)} %get-tuple-element.179), channel_id=1, source_target_pairs={{0,3},{1,0},{2,1},{3,2},{4,7},{5,4},{6,5},{7,6},{8,11},{9,8},{10,9... | collective-permute-start | bytes 786440 | tf_op jit(solution)/shard_map/ppermute | solution.py:87
  125.0 15.0 %collective-permute-start.23 = (bf16[1024,128]{1,0:T(8,128)(2,1)}, bf16[1024,128]{1,0:T(8,128)(2,1)S(1)}, u32[]{:S(2)}, u32[]{:S(2)}) collective-permute-start(bf16[1024,128]{1,0:T(8,128)(2,1)} %get-tuple-element.183), channel_id=1, source_target_pairs={{0,2},{1,3},{2,0},{3,1},{4,6},{5,7},{6,4},{7,5},{8,10},{9,11},{10,... | collective-permute-start | bytes 786440 | tf_op jit(solution)/shard_map/ppermute | solution.py:87
  140.7 14.4 %collective-permute-start.26 = (bf16[512,128]{1,0:T(8,128)(2,1)}, bf16[512,128]{1,0:T(8,128)(2,1)S(1)}, u32[]{:S(2)}, u32[]{:S(2)}) collective-permute-start(bf16[512,128]{1,0:T(8,128)(2,1)} %get-tuple-element.189), channel_id=1, source_target_pairs={{0,3},{1,0},{2,1},{3,2},{4,7},{5,4},{6,5},{7,6},{8,11},{9,8},{10,9... | collective-permute-start | bytes 393224 | tf_op jit(solution)/shard_map/ppermute | solution.py:87
  155.3 14.7 %collective-permute-start.29 = (bf16[512,128]{1,0:T(8,128)(2,1)}, bf16[512,128]{1,0:T(8,128)(2,1)S(1)}, u32[]{:S(2)}, u32[]{:S(2)}) collective-permute-start(bf16[512,128]{1,0:T(8,128)(2,1)} %get-tuple-element.196), channel_id=1, source_target_pairs={{0,3},{1,0},{2,1},{3,2},{4,7},{5,4},{6,5},{7,6},{8,11},{9,8},{10,9... | collective-permute-start | bytes 393224 | tf_op jit(solution)/shard_map/ppermute | solution.py:87
  158.5 12.3 %collective-permute-start.30 = (bf16[512,128]{1,0:T(8,128)(2,1)}, bf16[512,128]{1,0:T(8,128)(2,1)S(1)}, u32[]{:S(2)}, u32[]{:S(2)}) collective-permute-start(bf16[512,128]{1,0:T(8,128)(2,1)} %get-tuple-element.197), channel_id=1, source_target_pairs={{0,2},{1,3},{2,0},{3,1},{4,6},{5,7},{6,4},{7,5},{8,10},{9,11},{10,... | collective-permute-start | bytes 393224 | tf_op jit(solution)/shard_map/ppermute | solution.py:87
  170.8 15.0 %collective-permute-start.32 = (bf16[512,128]{1,0:T(8,128)(2,1)}, bf16[512,128]{1,0:T(8,128)(2,1)S(1)}, u32[]{:S(2)}, u32[]{:S(2)}) collective-permute-start(bf16[512,128]{1,0:T(8,128)(2,1)} %get-tuple-element.219), channel_id=1, source_target_pairs={{0,3},{1,0},{2,1},{3,2},{4,7},{5,4},{6,5},{7,6},{8,11},{9,8},{10,9... | collective-permute-start | bytes 393224 | tf_op jit(solution)/shard_map/ppermute | solution.py:87
  187.6 18.2 %collective-permute-start.39 = (bf16[512,1024]{1,0:T(8,128)(2,1)S(1)}, bf16[512,1024]{1,0:T(8,128)(2,1)S(1)}, u32[]{:S(2)}, u32[]{:S(2)}) collective-permute-start(bf16[512,1024]{1,0:T(8,128)(2,1)S(1)} %pad_maximum_fusion), channel_id=1, source_target_pairs={{0,4},{4,0},{8,12},{12,8},{16,20},{20,16},{24,28},{28,24},{1,5},{5... | collective-permute-start | bytes 3145736 | tf_op jit(solution)/shard_map/ppermute | solution.py:41
  190.9 13.6 %collective-permute-start.37 = (bf16[512,128]{1,0:T(8,128)(2,1)S(1)}, bf16[512,128]{1,0:T(8,128)(2,1)S(1)}, u32[]{:S(2)}, u32[]{:S(2)}) collective-permute-start(bf16[512,128]{1,0:T(8,128)(2,1)S(1)} %copy-done.63), channel_id=1, source_target_pairs={{0,2},{1,3},{2,0},{3,1},{4,6},{5,7},{6,4},{7,5},{8,10},{9,11},{10,... | collective-permute-start | bytes 393224 | tf_op jit(solution)/shard_map/ppermute | solution.py:87
  192.0 12.5 %collective-permute-start.38 = (bf16[512,128]{1,0:T(8,128)(2,1)S(1)}, bf16[512,128]{1,0:T(8,128)(2,1)S(1)}, u32[]{:S(2)}, u32[]{:S(2)}) collective-permute-start(bf16[512,128]{1,0:T(8,128)(2,1)S(1)} %copy-done.62), channel_id=1, source_target_pairs={{0,1},{1,2},{2,3},{3,0},{4,5},{5,6},{6,7},{7,4},{8,9},{9,10},{10,1... | collective-permute-start | bytes 393224 | tf_op jit(solution)/shard_map/ppermute | solution.py:87
  205.8 24.8 %collective-permute-start.44 = (bf16[1024,128]{1,0:T(8,128)(2,1)S(1)}, bf16[1024,128]{1,0:T(8,128)(2,1)S(1)}, u32[]{:S(2)}, u32[]{:S(2)}) collective-permute-start(bf16[1024,128]{1,0:T(8,128)(2,1)S(1)} %copy-done.38), channel_id=1, source_target_pairs={{0,1},{1,2},{2,3},{3,0},{4,5},{5,6},{6,7},{7,4},{8,9},{9,10},{10,1... | collective-permute-start | bytes 786440 | tf_op jit(solution)/shard_map/ppermute | solution.py:87
  205.9 24.8 %collective-permute-start.43 = (bf16[1024,128]{1,0:T(8,128)(2,1)S(1)}, bf16[1024,128]{1,0:T(8,128)(2,1)S(1)}, u32[]{:S(2)}, u32[]{:S(2)}) collective-permute-start(bf16[1024,128]{1,0:T(8,128)(2,1)S(1)} %copy-done.39), channel_id=1, source_target_pairs={{0,2},{1,3},{2,0},{3,1},{4,6},{5,7},{6,4},{7,5},{8,10},{9,11},{10,... | collective-permute-start | bytes 786440 | tf_op jit(solution)/shard_map/ppermute | solution.py:87
  206.3 24.3 %collective-permute-start.42 = (bf16[1024,128]{1,0:T(8,128)(2,1)S(1)}, bf16[1024,128]{1,0:T(8,128)(2,1)S(1)}, u32[]{:S(2)}, u32[]{:S(2)}) collective-permute-start(bf16[1024,128]{1,0:T(8,128)(2,1)S(1)} %copy-done.40), channel_id=1, source_target_pairs={{0,3},{1,0},{2,1},{3,2},{4,7},{5,4},{6,5},{7,6},{8,11},{9,8},{10,9... | collective-permute-start | bytes 786440 | tf_op jit(solution)/shard_map/ppermute | solution.py:87
  211.0 19.6 %collective-permute-start.41 = (bf16[128,1024]{1,0:T(8,128)(2,1)S(1)}, bf16[128,1024]{1,0:T(8,128)(2,1)S(1)}, u32[]{:S(2)}, u32[]{:S(2)}) collective-permute-start(bf16[128,1024]{1,0:T(8,128)(2,1)S(1)} %pad_maximum_fusion.5), channel_id=1, source_target_pairs={{0,16},{4,20},{8,0},{12,4},{24,8},{28,12},{16,24},{20,28},{1,17},{... | collective-permute-start | bytes 786440 | tf_op jit(solution)/shard_map/ppermute | solution.py:38
  211.5 19.2 %collective-permute-start.40 = (bf16[128,1024]{1,0:T(8,128)(2,1)S(1)}, bf16[128,1024]{1,0:T(8,128)(2,1)S(1)}, u32[]{:S(2)}, u32[]{:S(2)}) collective-permute-start(bf16[128,1024]{1,0:T(8,128)(2,1)S(1)} %pad_maximum_fusion.4), channel_id=1, source_target_pairs={{0,8},{4,12},{8,24},{12,28},{24,16},{28,20},{16,0},{20,4},{1,9},{5... | collective-permute-start | bytes 786440 | tf_op jit(solution)/shard_map/ppermute | solution.py:38
  235.3 28.7 %collective-permute-start.46 = (bf16[2048,128]{1,0:T(8,128)(2,1)S(1)}, bf16[2048,128]{1,0:T(8,128)(2,1)S(1)}, u32[]{:S(2)}, u32[]{:S(2)}) collective-permute-start(bf16[2048,128]{1,0:T(8,128)(2,1)S(1)} %get-tuple-element.278), channel_id=1, source_target_pairs={{0,8},{4,12},{8,24},{12,28},{24,16},{28,20},{16,0},{20,4},{1,9},{5... | collective-permute-start | bytes 1572872 | tf_op jit(solution)/shard_map/ppermute | solution.py:38
  236.9 27.2 %collective-permute-start.47 = (bf16[2048,128]{1,0:T(8,128)(2,1)S(1)}, bf16[2048,128]{1,0:T(8,128)(2,1)S(1)}, u32[]{:S(2)}, u32[]{:S(2)}) collective-permute-start(bf16[2048,128]{1,0:T(8,128)(2,1)S(1)} %get-tuple-element.279), channel_id=1, source_target_pairs={{0,16},{4,20},{8,0},{12,4},{24,8},{28,12},{16,24},{20,28},{1,17},{... | collective-permute-start | bytes 1572872 | tf_op jit(solution)/shard_map/ppermute | solution.py:38
  242.7 27.4 %collective-permute-start.49 = (bf16[2048,128]{1,0:T(8,128)(2,1)S(1)}, bf16[2048,128]{1,0:T(8,128)(2,1)S(1)}, u32[]{:S(2)}, u32[]{:S(2)}) collective-permute-start(bf16[2048,128]{1,0:T(8,128)(2,1)S(1)} %get-tuple-element.339), channel_id=1, source_target_pairs={{0,8},{4,12},{8,24},{12,28},{24,16},{28,20},{16,0},{20,4},{1,9},{5... | collective-permute-start | bytes 1572872 | tf_op jit(solution)/shard_map/ppermute | solution.py:38
  244.3 25.8 %collective-permute-start.51 = (bf16[1024,256]{1,0:T(8,128)(2,1)S(1)}, bf16[1024,256]{1,0:T(8,128)(2,1)S(1)}, u32[]{:S(2)}, u32[]{:S(2)}) collective-permute-start(bf16[1024,256]{1,0:T(8,128)(2,1)S(1)} %copy-done.24), channel_id=1, source_target_pairs={{0,2},{1,3},{2,0},{3,1},{4,6},{5,7},{6,4},{7,5},{8,10},{9,11},{10,... | collective-permute-start | bytes 1572872 | tf_op jit(solution)/shard_map/ppermute | solution.py:87
  246.3 23.9 %collective-permute-start.50 = (bf16[2048,128]{1,0:T(8,128)(2,1)S(1)}, bf16[2048,128]{1,0:T(8,128)(2,1)S(1)}, u32[]{:S(2)}, u32[]{:S(2)}) collective-permute-start(bf16[2048,128]{1,0:T(8,128)(2,1)S(1)} %get-tuple-element.338), channel_id=1, source_target_pairs={{0,16},{4,20},{8,0},{12,4},{24,8},{28,12},{16,24},{20,28},{1,17},{... | collective-permute-start | bytes 1572872 | tf_op jit(solution)/shard_map/ppermute | solution.py:38
  275.6 41.9 %collective-permute-start.58 = (bf16[12288,128]{1,0:T(8,128)(2,1)}, bf16[12288,128]{1,0:T(8,128)(2,1)S(1)}, u32[]{:S(2)}, u32[]{:S(2)}) collective-permute-start(bf16[12288,128]{1,0:T(8,128)(2,1)} %get-tuple-element.318), channel_id=1, source_target_pairs={{0,4},{4,0},{8,12},{12,8},{16,20},{20,16},{24,28},{28,24},{1,5},{5... | collective-permute-start | bytes 9437192 | tf_op jit(solution)/shard_map/ppermute | solution.py:41
  275.8 16.3 %collective-permute-start.57 = (bf16[1024,256]{1,0:T(8,128)(2,1)}, bf16[1024,256]{1,0:T(8,128)(2,1)}, u32[]{:S(2)}, u32[]{:S(2)}) collective-permute-start(bf16[1024,256]{1,0:T(8,128)(2,1)} %get-tuple-element.309), channel_id=1, source_target_pairs={{0,1},{1,2},{2,3},{3,0},{4,5},{5,6},{6,7},{7,4},{8,9},{9,10},{10,1... | collective-permute-start | bytes 1572872 | tf_op jit(solution)/shard_map/ppermute | solution.py:87
  280.4 17.9 %collective-permute-start.53 = (bf16[2560,128]{1,0:T(8,128)(2,1)}, bf16[2560,128]{1,0:T(8,128)(2,1)}, u32[]{:S(2)}, u32[]{:S(2)}) collective-permute-start(bf16[2560,128]{1,0:T(8,128)(2,1)} %pad_maximum_fusion.2), channel_id=1, source_target_pairs={{0,16},{4,20},{8,0},{12,4},{24,8},{28,12},{16,24},{20,28},{1,17},{... | collective-permute-start | bytes 1966088 | tf_op jit(solution)/shard_map/ppermute | solution.py:38
  281.8 20.3 %collective-permute-start.52 = (bf16[2560,128]{1,0:T(8,128)(2,1)}, bf16[2560,128]{1,0:T(8,128)(2,1)}, u32[]{:S(2)}, u32[]{:S(2)}) collective-permute-start(bf16[2560,128]{1,0:T(8,128)(2,1)} %pad_maximum_fusion.1), channel_id=1, source_target_pairs={{0,8},{4,12},{8,24},{12,28},{24,16},{28,20},{16,0},{20,4},{1,9},{5... | collective-permute-start | bytes 1966088 | tf_op jit(solution)/shard_map/ppermute | solution.py:38
  283.3 26.7 %collective-permute-start.55 = (bf16[2048,128]{1,0:T(8,128)(2,1)}, bf16[2048,128]{1,0:T(8,128)(2,1)}, u32[]{:S(2)}, u32[]{:S(2)}) collective-permute-start(bf16[2048,128]{1,0:T(8,128)(2,1)} %get-tuple-element.307), channel_id=1, source_target_pairs={{0,8},{4,12},{8,24},{12,28},{24,16},{28,20},{16,0},{20,4},{1,9},{5... | collective-permute-start | bytes 1572872 | tf_op jit(solution)/shard_map/ppermute | solution.py:38
  292.1 18.0 %collective-permute-start.56 = (bf16[2048,128]{1,0:T(8,128)(2,1)}, bf16[2048,128]{1,0:T(8,128)(2,1)}, u32[]{:S(2)}, u32[]{:S(2)}) collective-permute-start(bf16[2048,128]{1,0:T(8,128)(2,1)} %get-tuple-element.308), channel_id=1, source_target_pairs={{0,16},{4,20},{8,0},{12,4},{24,8},{28,12},{16,24},{20,28},{1,17},{... | collective-permute-start | bytes 1572872 | tf_op jit(solution)/shard_map/ppermute | solution.py:38
  298.3 27.3 %collective-permute-start.35 = (bf16[1024,256]{1,0:T(8,128)(2,1)}, bf16[1024,256]{1,0:T(8,128)(2,1)}, u32[]{:S(2)}, u32[]{:S(2)}) collective-permute-start(bf16[1024,256]{1,0:T(8,128)(2,1)} %get-tuple-element.249), channel_id=1, source_target_pairs={{0,3},{1,0},{2,1},{3,2},{4,7},{5,4},{6,5},{7,6},{8,11},{9,8},{10,9... | collective-permute-start | bytes 1572872 | tf_op jit(solution)/shard_map/ppermute | solution.py:87
  322.0 20.8 %collective-permute-start.61 = (bf16[2048,128]{1,0:T(8,128)(2,1)}, bf16[2048,128]{1,0:T(8,128)(2,1)S(1)}, u32[]{:S(2)}, u32[]{:S(2)}) collective-permute-start(bf16[2048,128]{1,0:T(8,128)(2,1)} %get-tuple-element.323), channel_id=1, source_target_pairs={{0,16},{4,20},{8,0},{12,4},{24,8},{28,12},{16,24},{20,28},{1,17},{... | collective-permute-start | bytes 1572872 | tf_op jit(solution)/shard_map/ppermute | solution.py:38
  322.4 20.4 %collective-permute-start.60 = (bf16[2048,128]{1,0:T(8,128)(2,1)}, bf16[2048,128]{1,0:T(8,128)(2,1)S(1)}, u32[]{:S(2)}, u32[]{:S(2)}) collective-permute-start(bf16[2048,128]{1,0:T(8,128)(2,1)} %get-tuple-element.321), channel_id=1, source_target_pairs={{0,8},{4,12},{8,24},{12,28},{24,16},{28,20},{16,0},{20,4},{1,9},{5... | collective-permute-start | bytes 1572872 | tf_op jit(solution)/shard_map/ppermute | solution.py:38
  324.0 22.6 %collective-permute-start.59 = (bf16[2048,128]{1,0:T(8,128)(2,1)}, bf16[2048,128]{1,0:T(8,128)(2,1)S(1)}, u32[]{:S(2)}, u32[]{:S(2)}) collective-permute-start(bf16[2048,128]{1,0:T(8,128)(2,1)} %get-tuple-element.332), channel_id=1, source_target_pairs={{0,8},{4,12},{8,24},{12,28},{24,16},{28,20},{16,0},{20,4},{1,9},{5... | collective-permute-start | bytes 1572872 | tf_op jit(solution)/shard_map/ppermute | solution.py:38
  325.6 21.1 %collective-permute-start.62 = (bf16[2048,128]{1,0:T(8,128)(2,1)}, bf16[2048,128]{1,0:T(8,128)(2,1)S(1)}, u32[]{:S(2)}, u32[]{:S(2)}) collective-permute-start(bf16[2048,128]{1,0:T(8,128)(2,1)} %get-tuple-element.328), channel_id=1, source_target_pairs={{0,16},{4,20},{8,0},{12,4},{24,8},{28,12},{16,24},{20,28},{1,17},{... | collective-permute-start | bytes 1572872 | tf_op jit(solution)/shard_map/ppermute | solution.py:38
  (86 other events, 846.0 us)
Sparse Core Ops, SparseCore 0:
  124.5 27.5 all-gather.1

commit v11 on v6

--- a/solution.py
+++ b/solution.py
@@ -379,7 +379,7 @@
 
 def step_sums(own_up, at_up, up, own_down, at_down, down, got):
     rows, width = own_up.shape
-    step = min(rows // 2, 512)
+    step = min(rows // 2, 1024)
     blocks = rows // step
     low = blocks // 2
 
@@ -418,7 +418,7 @@
 
 def result_of(ready, own, got, at, up, down):
     rows, width = own.shape
-    step = min(rows, 512)
+    step = min(rows // 2, 1024)
     blocks = rows // step
     here = pl.BlockSpec((step, width), lambda t: (t, 0))
     there = pl.BlockSpec((step, width), lambda t: (t + at * blocks, 0))
@@ -435,6 +435,96 @@
     )(*ready, own, got, up, down)
 
 
+def halves_kernel(low_blocks, own_far, got_far, own_up, got_up, own_down, got_down, to_up, to_down):
+    low = pl.program_id(0) < low_blocks
+
+    def put(out, own, got):
+        out[...] = (own[...].astype(F32) + got[...].astype(F32)).astype(BF16)
+
+    @pl.when(low)
+    def _():
+        put(to_up, own_far, got_far)
+        put(to_down, own_down, got_down)
+
+    @pl.when(jnp.logical_not(low))
+    def _():
+        put(to_up, own_up, got_up)
+        put(to_down, own_far, got_far)
+
+
+def halves_sums(own_far, got_far, own_up, at_up, own_down, at_down, got):
+    rows, width = own_far.shape
+    step = min(rows // 2, 1024)
+    blocks = rows // step
+    low = blocks // 2
+
+    def spec(index):
+        return pl.BlockSpec((step, width), lambda t: (index(t), 0))
+
+    here = spec(lambda t: t)
+    return pl.pallas_call(
+        functools.partial(halves_kernel, low),
+        grid=(blocks,),
+        in_specs=[
+            here,
+            here,
+            spec(lambda t: jnp.maximum(t, low)),
+            spec(lambda t: jnp.maximum(t, low) + at_up * blocks),
+            spec(lambda t: jnp.minimum(t, low - 1)),
+            spec(lambda t: jnp.minimum(t, low - 1) + at_down * blocks),
+        ],
+        out_specs=[here, here],
+        out_shape=[jax.ShapeDtypeStruct((rows, width), BF16)] * 2,
+        compiler_params=params(),
+        cost_estimate=pl.CostEstimate(flops=2 * rows * width, bytes_accessed=12 * rows * width, transcendentals=0),
+        name="halves_sums",
+    )(own_far, got_far, own_up, got, own_down, got)
+
+
+def joined_kernel(low_blocks, own, got, up_low, up_high, down_low, down_high, out):
+    low = pl.program_id(0) < low_blocks
+
+    def put(up, down):
+        total = own[...].astype(F32) + got[...].astype(F32) + up[...].astype(F32) + down[...].astype(F32)
+        out[...] = total.astype(BF16)
+
+    @pl.when(low)
+    def _():
+        put(up_low, down_low)
+
+    @pl.when(jnp.logical_not(low))
+    def _():
+        put(up_high, down_high)
+
+
+def joined(own, got, at, up_low, up, down, down_high):
+    rows, width = own.shape
+    step = min(rows // 2, 1024)
+    blocks = rows // step
+    low = blocks // 2
+
+    def spec(index):
+        return pl.BlockSpec((step, width), lambda t: (index(t), 0))
+
+    return pl.pallas_call(
+        functools.partial(joined_kernel, low),
+        grid=(blocks,),
+        in_specs=[
+            spec(lambda t: t),
+            spec(lambda t: t + at * blocks),
+            spec(lambda t: jnp.minimum(t, low - 1)),
+            spec(lambda t: jnp.maximum(t, low)),
+            spec(lambda t: jnp.minimum(t, low - 1)),
+            spec(lambda t: jnp.maximum(t - low, 0)),
+        ],
+        out_specs=spec(lambda t: t),
+        out_shape=jax.ShapeDtypeStruct((rows, width), BF16),
+        compiler_params=params(),
+        cost_estimate=pl.CostEstimate(flops=3 * rows * width, bytes_accessed=10 * rows * width, transcendentals=0),
+        name="joined",
+    )(own, got, up_low, up, down, down_high)
+
+
 class Reduction:
     def __init__(self, ring, own_far, own_near, other_far, other_near):
         self.ring, self.middle = ring, ring.chips // 2
@@ -473,6 +563,15 @@
             total_of(*self.near_terms(step, got), jnp.concatenate([up, zeros])),
             total_of(*self.near_terms(-step, got), jnp.concatenate([zeros, down])),
         )
+
+    def halves(self, got_far, got):
+        at_up, at_down = self.place(1), self.place(-1)
+        return halves_sums(self.own_far, got_far, self.own_near[at_up], at_up, self.own_near[at_down], at_down, got)
+
+    def other_halves(self, got, up, down):
+        half = self.rows // 2
+        (own_up, got_up), (own_down, got_down) = self.near_terms(1, got), self.near_terms(-1, got)
+        return total_of(own_up[:half], got_up[:half], up[:half]), total_of(own_down[half:], got_down[half:], down[half:])
 
     def last(self, up, down):
         if self.middle > 1:
@@ -538,13 +637,14 @@
                 for i in range(1, len(offsets)):
                     got_other[c - 1, i] = ring.sibling(got_own[c - 1, i])
                 w.go(**{f"mixed{c - 1}": run_spmm(c - 1, 1, 0)})
+            if c == 0 and step == 1:
+                w.go(metas=(spmm_meta, spmm_t_meta, dense_meta))
             w.close()
             up, down = w["up" + name], w["down" + name]
             got_own[c, 2 * step - 1], got_own[c, 2 * step] = up, down
         w.go(**{f"far_up{c}": ring.hop(up[:half], 1), f"far_down{c}": ring.hop(down[half:], -1)})
         if c == 0:
-            w.go(cot_ends=cot_ends, own_other=own_other, metas=(spmm_meta, spmm_t_meta, dense_meta))
-            w.go(shares=send([w.gate(w_share)] * parts, ends + inner))
+            w.go(cot_ends=cot_ends, own_other=own_other)
         seen = []
         if c == last:
             for step in range(1, middle):
@@ -560,12 +660,13 @@
         if c == 0:
             spmm_meta, spmm_t_meta, dense_meta = w["metas"]
             w.go(cot_inner=send([w.gate(b) for b in cot_blocks], inner))
+            w.go(shares=send([w.gate(w_share)] * parts, ends + inner))
         else:
             w.go(**{f"mixed_inner{c - 1}": send([w.gate(b) for b in mixed[c - 1]], inner)})
         got_own[c, len(offsets) - 2], got_own[c, len(offsets) - 1] = w[f"far_up{c}"], w[f"far_down{c}"]
         if c < last:
             up = down = w.gate(xs[c + 1])
-    w_rows = jnp.concatenate(ordered(w_share, w["shares"]), axis=1)
+    w_rows = jnp.concatenate(ordered(w_share, {**w.done, **w.pending}["shares"]), axis=1)
     w_full = lax.all_gather(w.gate(w_rows), "row", axis=0, tiled=True)
     for i in (-2, -1):
         got_other[last, len(offsets) + i] = ring.sibling(got_own[last, len(offsets) + i])
@@ -624,45 +725,61 @@
             up, down = wg.hops(*wg.sums(step, w["wg_near"], up, down, False))
         return up, down
 
+    def send_act(shifts):
+        return send([w.gate(a) for a in act], shifts)
+
     reductions = []
     for c in range(chunks):
         terms = w[f"terms{c}"]
         red = Reduction(ring, terms[0], terms[1:-2], terms[-2], terms[-1])
         reductions.append(red)
+        combined = c < last and middle == 2
         got_far = red.far_swap()
         got_near = red.near_swap(got_far)
-        far = red.far_sums(got_far)
-        w.go(**{f"got_near{c}": got_near, f"sum{c}_{middle}": red.hops(*far)})
+        if c == 0:
+            wg_last = wg_steps(middle - 1, 0)
+            w.go(wg_last=wg_last)
+        sums = red.halves(got_far, got_near) if combined else red.far_sums(got_far)
+        w.go(**{f"got_near{c}": got_near})
         if c < last:
             grads = ordered(back[0][c + 1], w[f"rest_got{c + 1}"])
-            grads = lax.optimization_barrier((grads, far[0][:8], far[1][:8]))[0]
+            grads, sums = lax.optimization_barrier((grads, sums))
             w.go(**{f"terms{c + 1}": run_spmm_t(c + 1, grads)})
+        w.go(**{f"sum{c}_{middle}": red.hops(*sums)})
         if c == 0:
-            w.go(wg_last=wg_steps(middle - 1, 0))
-        if c == last:
-            w.go(act_inner=send([lax.optimization_barrier((a, got_near))[0] for a in act], inner))
+            w.go(act_inner=send_act(inner))
         w.close()
         if c == 0:
             block = total_of(*wg.near_terms(0, w["wg_near"]), *wg.last(*w["wg_last"]))
+        if c == last:
             cuts = [
-                lax.dynamic_slice_in_dim(block, lax.rem(rep + u, parts) * f_wide, f_wide, 1) for u in range(parts)
+                w.gate(lax.dynamic_slice_in_dim(block, lax.rem(rep + u, parts) * f_wide, f_wide, 1))
+                for u in range(parts)
             ]
-            wg_got = send(cuts, ends + inner)
-            w.go(weight_grad=functools.reduce(lambda a, b: a + b, [v.astype(F32) for v in [cuts[0], *wg_got.values()]]))
+        if combined:
+            w.go(**{f"sum{c}_1": red.hops(*red.other_halves(w[f"got_near{c}"], *w[f"sum{c}_{middle}"]))})
+            continue
         for step in range(middle - 1, 0, -1):
             to_up, to_down = red.sums(step, w[f"got_near{c}"], *w[f"sum{c}_{step + 1}"], True)
+            if step == 1 and c == last:
+                cuts, act, to_up, to_down = lax.optimization_barrier((cuts, act, to_up, to_down))
             w.go(**{f"sum{c}_{step}": red.hops(to_up, to_down)})
             if step > 1:
                 w.close()
-            else:
-                w.token = to_up[:8]
-    got = {**w.done, **w.pending, "act_ends": send([w.gate(a) for a in act], ends)}
-    ready = [
-        total_of(*red.near_terms(0, got[f"got_near{c}"]), *red.last(*got[f"sum{c}_1"]))
-        for c, red in enumerate(reductions[:-1])
-    ]
+    w.go(act_ends=send(act, ends))
+    cuts_got = send(cuts, ends + inner)
+    got = {**w.done, **w.pending}
+    got["weight_grad"] = functools.reduce(lambda a, b: a + b, [v.astype(F32) for v in [cuts[0], *cuts_got.values()]])
+    ready = []
+    at = near.index(0)
+    for c, red in enumerate(reductions[:-1]):
+        up, down = got[f"sum{c}_1"]
+        if middle == 2:
+            whole_up, whole_down = got[f"sum{c}_2"]
+            ready.append(joined(red.own_near[at], got[f"got_near{c}"], at, up, whole_up, whole_down, down))
+        else:
+            ready.append(total_of(*red.near_terms(0, got[f"got_near{c}"]), *red.last(up, down)))
     red = reductions[-1]
-    at = red.place(0)
     feature_grad = result_of(ready, red.own_near[at], got[f"got_near{last}"], at, *red.last(*got[f"sum{last}_1"]))
     weight_grad = got["weight_grad"].T
     act = ordered(act[0], got["act_ends"], got["act_inner"])

time: 346 us -> 354 us (1.023)
  waiting for transfers between devices: 102 us -> 119 us
    pallas_call x2 -> x1, Pallas kernels: 13.6 us -> 4.85 us  [step_sums(): pl.pallas_call(functools.partial(step_kernel, low), grid=(blocks,), in_sp...]
    pallas_call x0 -> x2, Pallas kernels: none -> 8.75 us  [the longest x1 4.42 us: halves_sums(): pl.pallas_call(functools.partial(halves_kernel, low), grid=(blocks,), in_...]
    ppermute x20, waiting for transfers between devices: 47.4 us -> 55.2 us  [hop(): return lax.ppermute(value, 'row', self.perm(step))]
    ppermute x15, waiting for transfers between devices: 4.71 us -> 12.3 us  [sibling(): return lax.ppermute(value, 'row', [(d, d ^ 1) for d in range(self.devices)])]
    unnamed x138 -> x116, local copies, waits for them, and re-layouts: 12.2 us -> 10.1 us
    convert_element_type x6 -> x5, other arithmetic: 7.85 us -> 6.3 us  [total_of(): functools.reduce(lambda a, b: a + b, [v.astype(F32) for v in values])]
  transfers between devices with their start and end apart: 66 -> 66, of which waited for: 27 -> 28; matrix products, arithmetic and copies ran while one was open for 8% -> 7% of each run, Pallas kernels for 27% -> 25%
where the time goes in v11:
time: 354 us; the launch traced here: 352 us
  waiting for transfers between devices  119 us (34%)
  Pallas kernels  104 us (29%)
  starting transfers between devices  68.1 us (19%)
  local copies, waits for them, and re-layouts  26.6 us (8%)
  between operations  22.7 us (6%)
  other arithmetic  7.11 us (2%)
  matrix products  4.7 us (1%)
    ppermute x20, waiting for transfers between devices, hop(): return lax.ppermute(value, 'row', self.perm(step))  55.2 us
    ppermute x30, waiting for transfers between devices, send(): lax.ppermute(blocks[s], 'rep', [(i, (i + s) % size) for i in range(size)])  51.1 us
    ppermute x30, starting transfers between devices, send(): lax.ppermute(blocks[s], 'rep', [(i, (i + s) % size) for i in range(size)])  43.2 us
    pallas_call x3, Pallas kernels, spmm(): pl.pallas_call(functools.partial(spmm_kernel, len(pieces), per_part, skip...  36.6 us
    pallas_call x2, Pallas kernels, spmm_t(): pl.pallas_call(functools.partial(spmm_t_kernel, len(grads), per_part, len...  34.5 us
    ppermute x20, starting transfers between devices, hop(): return lax.ppermute(value, 'row', self.perm(step))  22.2 us
    pallas_call x2, Pallas kernels, dense(): pl.pallas_call(functools.partial(dense_kernel, parts, chunks, len(earlier...  14.1 us
    ppermute x15, waiting for transfers between devices, sibling(): return lax.ppermute(value, 'row', [(d, d ^ 1) for d in range(self.devices)])  12.3 us
  transfers between devices with their start and end apart: 66, of which 28 were waited for; matrix products, arithmetic and copies ran while one was open for 7% of the time, Pallas kernels for 25%

profile of v11, /device:TPU:0, one launch (start us, length us, event | category | flops | bytes accessed | tf_op | source)
XLA Modules:
  0.0 352.0 jit_solution(8081729807203561203)
XLA Ops:
  7.7 1.7 fusion.1
  9.4 2.6 collective-permute-start
  12.1 2.9 constant_dynamic-slice_fusion.5
  15.0 4.0 %collective-permute-start.4 = (bf16[1024,256]{1,0:T(8,128)(2,1)}, bf16[1024,256]{1,0:T(8,128)(2,1)S(1)}, u32[]{:S(2)}, u32[]{:S(2)}) collective-permute-start(bf16[1024,256]{1,0:T(8,128)(2,1)} %get-tuple-element.389), channel_id=1, source_target_pairs={{0,3},{1,0},{2,1},{3,2},{4,7},{5,4},{6,5},{7,6},{8,11},{9,8},{10,9... | collective-permute-start | bytes 1572872 | tf_op jit(solution)/shard_map/ppermute | solution.py:87
  29.5 6.5 %collective-permute-done.refs_1_ = bf16[4096,128]{1,0:T(8,128)(2,1)} collective-permute-done((bf16[4096,128]{1,0:T(8,128)(2,1)S(1)}, bf16[4096,128]{1,0:T(8,128)(2,1)}, u32[]{:S(2)}, u32[]{:S(2)}) %collective-permute-start) | collective-permute-done | bytes 1048608 | tf_op jit(solution)/shard_map/ppermute | solution.py:38
  44.3 9.8 %collective-permute-done.2.refs_3_ = bf16[2048,128]{1,0:T(8,128)(2,1)} collective-permute-done((bf16[2048,128]{1,0:T(8,128)(2,1)S(1)}, bf16[2048,128]{1,0:T(8,128)(2,1)}, u32[]{:S(2)}, u32[]{:S(2)}) %collective-permute-start.2) | collective-permute-done | bytes 524320 | tf_op jit(solution)/shard_map/ppermute | solution.py:38
  60.1 1.7 collective-permute-done.10
  62.3 3.0 fusion
  65.3 1.8 collective-permute-start.8
  68.3 14.4 %spmm.3 = (bf16[1024,128]{1,0:T(8,128)(2,1)}, bf16[1024,128]{1,0:T(8,128)(2,1)}, bf16[1024,128]{1,0:T(8,128)(2,1)}, bf16[1024,128]{1,0:T(8,128)(2,1)}) custom-call(s32[32,16]{1,0:T(8,128)} %copy.71.cols, s32[32]{0:T(128)} %counts.9, s32[11]{0:T(128)} %stack.75.meta, bf16[32,16,128,128]{3,2,1,0:T(8,128)(2,1)} %tiles.9, bf16[4096,128]{1,0:T(8,128)(2,1)} %copy-done.9, ...), custom_call_target="tpu_custom_call" | custom-call | flops 2147483648 | bytes 25165824 | tf_op jit(solution)/shard_map/spmm/pallas_call | solution.py:158
  82.7 8.3 %collective-permute-done.9 = bf16[128,256]{1,0:T(8,128)(2,1)S(1)} collective-permute-done((bf16[128,256]{1,0:T(8,128)(2,1)S(1)}, bf16[128,256]{1,0:T(8,128)(2,1)S(1)}, u32[]{:S(2)}, u32[]{:S(2)}) %collective-permute-start.9) | collective-permute-done | bytes 65568 | tf_op jit(solution)/shard_map/ppermute | solution.py:87
  97.5 3.8 %collective-permute-start.21 = (bf16[1024,128]{1,0:T(8,128)(2,1)}, bf16[1024,128]{1,0:T(8,128)(2,1)}, u32[]{:S(2)}, u32[]{:S(2)}) collective-permute-start(bf16[1024,128]{1,0:T(8,128)(2,1)} %get-tuple-element.204), channel_id=1, source_target_pairs={{0,3},{1,0},{2,1},{3,2},{4,7},{5,4},{6,5},{7,6},{8,11},{9,8},{10,9... | collective-permute-start | bytes 786440 | tf_op jit(solution)/shard_map/ppermute | solution.py:87
  102.0 6.4 %collective-permute-done.17.refs_3_ = bf16[2048,128]{1,0:T(8,128)(2,1)S(1)} collective-permute-done((bf16[2048,128]{1,0:T(8,128)(2,1)}, bf16[2048,128]{1,0:T(8,128)(2,1)S(1)}, u32[]{:S(2)}, u32[]{:S(2)}) %collective-permute-start.17) | collective-permute-done | bytes 524320 | tf_op jit(solution)/shard_map/ppermute | solution.py:38
  109.2 2.5 collective-permute-done.21.refs_2_
  112.3 2.4 collective-permute-start.23
  115.7 11.2 %spmm.4 = (bf16[512,128]{1,0:T(8,128)(2,1)}, bf16[512,128]{1,0:T(8,128)(2,1)}, bf16[512,128]{1,0:T(8,128)(2,1)}, bf16[512,128]{1,0:T(8,128)(2,1)}) custom-call(s32[32,16]{1,0:T(8,128)} %copy.71.cols, s32[32]{0:T(128)} %counts.9, s32[11]{0:T(128)} %stack.75.meta, bf16[32,16,128,128]{3,2,1,0:T(8,128)(2,1)} %tiles.9, bf16[4096,128]{1,0:T(8,128)(2,1)} %copy-done.4, ...), custom_call_target="tpu_custom_call" | custom-call | flops 1073741824 | bytes 16777216 | tf_op jit(solution)/shard_map/spmm/pallas_call | solution.py:158
  128.0 2.2 collective-permute-start.26
  131.6 11.0 %spmm.5 = (bf16[512,128]{1,0:T(8,128)(2,1)}, bf16[512,128]{1,0:T(8,128)(2,1)}, bf16[512,128]{1,0:T(8,128)(2,1)}, bf16[512,128]{1,0:T(8,128)(2,1)}) custom-call(s32[32,16]{1,0:T(8,128)} %copy.71.cols, s32[32]{0:T(128)} %counts.9, s32[11]{0:T(128)} %stack.75.meta, bf16[32,16,128,128]{3,2,1,0:T(8,128)(2,1)} %tiles.9, bf16[4096,128]{1,0:T(8,128)(2,1)} %copy-done.4, ...), custom_call_target="tpu_custom_call" | custom-call | flops 1073741824 | bytes 16777216 | tf_op jit(solution)/shard_map/spmm/pallas_call | solution.py:158
  142.7 2.5 collective-permute-start.29
  146.4 7.0 %dense.2 = (bf16[1024,256]{1,0:T(8,128)(2,1)}, bf16[1024,256]{1,0:T(8,128)(2,1)}, bf16[1024,256]{1,0:T(8,128)(2,1)}, bf16[1024,256]{1,0:T(8,128)(2,1)}, bf16[512...) custom-call(s32[1]{0:T(128)} %bitcast.meta, ...), custom_call_target="tpu_custom_call" | custom-call | flops 2147483648 | bytes 8388608 | tf_op jit(solution)/shard_map/dense/pallas_call | solution.py:325
  153.5 4.0 %collective-permute-done.30.refs_5_ = bf16[512,128]{1,0:T(8,128)(2,1)S(1)} collective-permute-done((bf16[512,128]{1,0:T(8,128)(2,1)}, bf16[512,128]{1,0:T(8,128)(2,1)S(1)}, u32[]{:S(2)}, u32[]{:S(2)}) %collective-permute-start.30) | collective-permute-done | bytes 131104 | tf_op jit(solution)/shard_map/ppermute | solution.py:87
  159.2 2.0 collective-permute-start.34
  161.2 7.1 %dense.3 = (bf16[1024,256]{1,0:T(8,128)(2,1)}, bf16[1024,256]{1,0:T(8,128)(2,1)}, bf16[1024,256]{1,0:T(8,128)(2,1)}, bf16[1024,256]{1,0:T(8,128)(2,1)}, bf16[512...) custom-call(s32[1]{0:T(128)} %bitcast.meta, ...), custom_call_target="tpu_custom_call", output_to_operand_aliasing={{0}: (14, {}), {1}: (15, {}), {2}: (16, {}), {3}: (17, {}),... | custom-call | flops 2147483648 | bytes 8388608 | tf_op jit(solution)/shard_map/dense/pallas_call | solution.py:325
  168.4 3.2 collective-permute-done.33.refs_4_
  171.5 4.7 %convolution_convert_fusion = bf16[1024,1024]{1,0:T(8,128)(2,1)S(1)} fusion(bf16[1024,1024]{1,0:T(8,128)(2,1)} %get-tuple-element.278, bf16[1024,1024]{1,0:T(8,128)(2,1)} %get-tuple-element.279), kind=kOutput, calls=%fused_computation | convolution fusion | flops 2148532224 | bytes 6291456 | tf_op jit(solution)/shard_map/dot_general | solution.py:694
  179.1 2.0 collective-permute-start.37
  181.1 4.3 %collective-permute-done.35.refs_3_ = bf16[512,128]{1,0:T(8,128)(2,1)S(1)} collective-permute-done((bf16[512,128]{1,0:T(8,128)(2,1)S(1)}, bf16[512,128]{1,0:T(8,128)(2,1)S(1)}, u32[]{:S(2)}, u32[]{:S(2)}) %collective-permute-start.35) | collective-permute-done | bytes 131104 | tf_op jit(solution)/shard_map/ppermute | solution.py:87
  185.3 6.1 %collective-permute-done.36.refs_5_ = bf16[512,128]{1,0:T(8,128)(2,1)S(1)} collective-permute-done((bf16[512,128]{1,0:T(8,128)(2,1)S(1)}, bf16[512,128]{1,0:T(8,128)(2,1)S(1)}, u32[]{:S(2)}, u32[]{:S(2)}) %collective-permute-start.36) | collective-permute-done | bytes 131104 | tf_op jit(solution)/shard_map/ppermute | solution.py:87
  191.8 2.0 collective-permute-start.43
  193.8 2.8 collective-permute-start.42
  198.8 17.1 %spmm_t.2 = (bf16[4096,128]{1,0:T(8,128)(2,1)}, bf16[4096,128]{1,0:T(8,128)(2,1)}, bf16[4096,128]{1,0:T(8,128)(2,1)}, bf16[4096,128]{1,0:T(8,128)(2,1)}, bf16[40...) custom-call(s32[32,16]{1,0:T(8,128)} %copy.71.cols, s32[32]{0:T(128)} %counts.9, s32[9]{0:T(128)} %stack.84.meta, ...), custom_call_target="tpu_custom_call" | custom-call | flops 2147483648 | bytes 25165824 | tf_op jit(solution)/shard_map/spmm_t/pallas_call | solution.py:241
  216.7 2.9 collective-permute-done.47.got_far
  219.7 5.7 %collective-permute-done.48.got_up.got_down.got = bf16[12288,128]{1,0:T(8,128)(2,1)S(1)} collective-permute-done((bf16[12288,128]{1,0:T(8,128)(2,1)}, bf16[12288,128]{1,0:T(8,128)(2,1)S(1)}, u32[]{:S(2)}, u32[]{:S(2)}) %collective-permute-start.48) | collective-permute-done | bytes 3145760 | tf_op jit(solution)/shard_map/ppermute | solution.py:41
  225.4 1.7 copy-done.2
  227.1 4.4 %halves_sums.1 = (bf16[4096,128]{1,0:T(8,128)(2,1)}, bf16[4096,128]{1,0:T(8,128)(2,1)}) custom-call(bf16[4096,128]{1,0:T(8,128)(2,1)} %get-tuple-element.317.own_far, bf16[4096,128]{1,0:T(8,128)(2,1)} %copy-done.21, bf16[4096,128]{1,0:T(8,128)(2,1)} %get-tuple-element.318.own_up, bf16[12288,128]{1,0:T(8,128)(2,1)} %copy-done.2, ...), custom_call_target="tpu_custom_call" | custom-call | flops 1048576 | bytes 6291456 | tf_op jit(solution)/shard_map/halves_sums/pallas_call | solution.py:465
  237.6 17.4 %spmm_t.3 = (bf16[4096,128]{1,0:T(8,128)(2,1)}, bf16[4096,128]{1,0:T(8,128)(2,1)}, bf16[4096,128]{1,0:T(8,128)(2,1)}, bf16[4096,128]{1,0:T(8,128)(2,1)}, bf16[40...) custom-call(s32[32,16]{1,0:T(8,128)} %copy.71.cols, s32[32]{0:T(128)} %counts.9, s32[9]{0:T(128)} %stack.84.meta, ...), custom_call_target="tpu_custom_call" | custom-call | flops 2147483648 | bytes 25165824 | tf_op jit(solution)/shard_map/spmm_t/pallas_call | solution.py:241
  254.9 7.7 %collective-permute-done.45 = bf16[128,1024]{1,0:T(8,128)(2,1)S(1)} collective-permute-done((bf16[128,1024]{1,0:T(8,128)(2,1)S(1)}, bf16[128,1024]{1,0:T(8,128)(2,1)S(1)}, u32[]{:S(2)}, u32[]{:S(2)}) %collective-permute-start.45) | collective-permute-done | bytes 262176 | tf_op jit(solution)/shard_map/ppermute | solution.py:38
  264.4 2.2 collective-permute-done.54
  266.7 2.6 add_convert_fusion.2
  276.0 8.4 %collective-permute-done.52.up_low = bf16[2048,128]{1,0:T(8,128)(2,1)} collective-permute-done((bf16[2048,128]{1,0:T(8,128)(2,1)}, bf16[2048,128]{1,0:T(8,128)(2,1)}, u32[]{:S(2)}, u32[]{:S(2)}) %collective-permute-start.52) | collective-permute-done | bytes 524320 | tf_op jit(solution)/shard_map/ppermute | solution.py:38
  285.6 9.4 %collective-permute-done.56.up = bf16[2048,128]{1,0:T(8,128)(2,1)} collective-permute-done((bf16[2048,128]{1,0:T(8,128)(2,1)}, bf16[2048,128]{1,0:T(8,128)(2,1)}, u32[]{:S(2)}, u32[]{:S(2)}) %collective-permute-start.56) | collective-permute-done | bytes 524320 | tf_op jit(solution)/shard_map/ppermute | solution.py:38
  297.7 4.9 %step_sums.1 = (bf16[4096,128]{1,0:T(8,128)(2,1)}, bf16[4096,128]{1,0:T(8,128)(2,1)}) custom-call(bf16[4096,128]{1,0:T(8,128)(2,1)} %get-tuple-element.353.own_up, bf16[12288,128]{1,0:T(8,128)(2,1)} %copy-done.3, bf16[2048,128]{1,0:T(8,128)(2,1)} %collective-permute-done.56.up, bf16[4096,128]{1,0:T(8,128)(2,1)} %get-tuple-element.356.own_down, ...), custom_call_target="tpu_custom_call" | custom-call | flops 2097152 | bytes 7340032 | tf_op jit(solution)/shard_map/step_sums/pallas_call | solution.py:390
  304.6 3.2 collective-permute-start.58
  307.8 3.8 %collective-permute-start.63 = (bf16[128,256]{1,0:T(8,128)(2,1)S(1)}, bf16[128,256]{1,0:T(8,128)(2,1)S(1)}, u32[]{:S(2)}, u32[]{:S(2)}) collective-permute-start(bf16[128,256]{1,0:T(8,128)(2,1)S(1)} %get-tuple-element.371), channel_id=1, source_target_pairs={{0,3},{1,0},{2,1},{3,2},{4,7},{5,4},{6,5},{7,6},{8,11},{9,8},{10,9... | collective-permute-start | bytes 196616 | tf_op jit(solution)/shard_map/ppermute | solution.py:87
  311.6 9.9 %collective-permute-done.62 = bf16[128,256]{1,0:T(8,128)(2,1)S(1)} collective-permute-done((bf16[128,256]{1,0:T(8,128)(2,1)S(1)}, bf16[128,256]{1,0:T(8,128)(2,1)S(1)}, u32[]{:S(2)}, u32[]{:S(2)}) %collective-permute-start.62) | collective-permute-done | bytes 65568 | tf_op jit(solution)/shard_map/ppermute | solution.py:87
  324.2 4.3 %joined.1.refs_0_ = bf16[4096,128]{1,0:T(8,128)(2,1)} custom-call(bf16[4096,128]{1,0:T(8,128)(2,1)} %get-tuple-element.364.own, bf16[12288,128]{1,0:T(8,128)(2,1)} %copy-done.2, bf16[2048,128]{1,0:T(8,128)(2,1)} %collective-permute-done.52.up_low, bf16[4096,128]{1,0:T(8,128)(2,1)} %copy-done.12, bf16[4096,128]{1,0:T(8,128)(2,1)} %copy-done.13, ...), custom_call_target="tpu_custom_call" | custom-call | flops 1572864 | bytes 5242880 | tf_op jit(solution)/shard_map/joined/pallas_call | solution.py:509
  328.5 8.1 %collective-permute-done.64 = bf16[128,256]{1,0:T(8,128)(2,1)S(1)} collective-permute-done((bf16[128,256]{1,0:T(8,128)(2,1)S(1)}, bf16[128,256]{1,0:T(8,128)(2,1)S(1)}, u32[]{:S(2)}, u32[]{:S(2)}) %collective-permute-start.64) | collective-permute-done | bytes 65568 | tf_op jit(solution)/shard_map/ppermute | solution.py:87
  339.8 5.3 %feature_grad.1 = bf16[4096,256]{1,0:T(8,128)(2,1)} custom-call(bf16[4096,128]{1,0:T(8,128)(2,1)} %joined.1.refs_0_, bf16[4096,128]{1,0:T(8,128)(2,1)} %get-tuple-element.366.refs_1_, bf16[12288,128]{1,0:T(8,128)(2,1)} %copy-done.3, bf16[4096,128]{1,0:T(8,128)(2,1)} %collective-permute-done.60.refs_3_, bf16[4096,128]{1,0:T(8,128)(2,1)} %collective-permute-done.61.refs_4_), custom_call_target="tpu_custom_call" | custom-call | flops 2097152 | bytes 7340032 | tf_op jit(solution)/shard_map/feature_grad/pallas_call | solution.py:426
  (240 shorter events, 66.4 us)
Async XLA Ops:
  7.2 139.2 %all-gather.2.cloned.1.call-start = ((), (), s32[]{:S(2)}) async-start(), calls=%async_computation | async-start | bytes 2359296 | tf_op jit(solution)/shard_map/all_gather | solution.py:670
  7.2 48.5 %collective-permute-start.6 = (bf16[4096,256]{1,0:T(8,128)(2,1)}, bf16[4096,256]{1,0:T(8,128)(2,1)}, u32[]{:S(2)}, u32[]{:S(2)}) collective-permute-start(bf16[4096,256]{1,0:T(8,128)(2,1)} %param.58), channel_id=1, source_target_pairs={{0,4},{4,0},{8,12},{12,8},{16,20},{20,16},{24,28},{28,24},{1,5},{5... | collective-permute-start | bytes 6291464 | tf_op jit(solution)/shard_map/ppermute | solution.py:41
  9.4 26.5 %collective-permute-start = (bf16[4096,128]{1,0:T(8,128)(2,1)S(1)}, bf16[4096,128]{1,0:T(8,128)(2,1)}, u32[]{:S(2)}, u32[]{:S(2)}) collective-permute-start(bf16[4096,128]{1,0:T(8,128)(2,1)S(1)} %get-tuple-element.395.refs_0_), channel_id=1, source_target_pairs={{0,8},{4,12},{8,24},{12,28},{24,16},{28,20},{16,0},{20,4},{1,9},{5... | collective-permute-start | bytes 3145736 | tf_op jit(solution)/shard_map/ppermute | solution.py:38
  12.0 25.4 %collective-permute-start.1 = (bf16[4096,128]{1,0:T(8,128)(2,1)S(1)}, bf16[4096,128]{1,0:T(8,128)(2,1)}, u32[]{:S(2)}, u32[]{:S(2)}) collective-permute-start(bf16[4096,128]{1,0:T(8,128)(2,1)S(1)} %get-tuple-element.395.refs_0_), channel_id=1, source_target_pairs={{0,16},{4,20},{8,0},{12,4},{24,8},{28,12},{16,24},{20,28},{1,17},{... | collective-permute-start | bytes 3145736 | tf_op jit(solution)/shard_map/ppermute | solution.py:38
  15.0 25.0 %collective-permute-start.4 = (bf16[1024,256]{1,0:T(8,128)(2,1)}, bf16[1024,256]{1,0:T(8,128)(2,1)S(1)}, u32[]{:S(2)}, u32[]{:S(2)}) collective-permute-start(bf16[1024,256]{1,0:T(8,128)(2,1)} %get-tuple-element.389), channel_id=1, source_target_pairs={{0,3},{1,0},{2,1},{3,2},{4,7},{5,4},{6,5},{7,6},{8,11},{9,8},{10,9... | collective-permute-start | bytes 1572872 | tf_op jit(solution)/shard_map/ppermute | solution.py:87
  19.1 23.7 %collective-permute-start.5 = (bf16[1024,256]{1,0:T(8,128)(2,1)}, bf16[1024,256]{1,0:T(8,128)(2,1)}, u32[]{:S(2)}, u32[]{:S(2)}) collective-permute-start(bf16[1024,256]{1,0:T(8,128)(2,1)} %get-tuple-element.391), channel_id=1, source_target_pairs={{0,1},{1,2},{2,3},{3,0},{4,5},{5,6},{6,7},{7,4},{8,9},{9,10},{10,1... | collective-permute-start | bytes 1572872 | tf_op jit(solution)/shard_map/ppermute | solution.py:87
  37.4 22.2 %collective-permute-start.13 = (bf16[4096,128]{1,0:T(8,128)(2,1)}, bf16[4096,128]{1,0:T(8,128)(2,1)}, u32[]{:S(2)}, u32[]{:S(2)}) collective-permute-start(bf16[4096,128]{1,0:T(8,128)(2,1)} %collective-permute-done.refs_1_), channel_id=1, source_target_pairs={{0,4},{4,0},{8,12},{12,8},{16,20},{20,16},{24,28},{28,24},{1,5},{5... | collective-permute-start | bytes 3145736 | tf_op jit(solution)/shard_map/ppermute | solution.py:41
  37.4 22.7 %collective-permute-start.14 = (bf16[4096,128]{1,0:T(8,128)(2,1)}, bf16[4096,128]{1,0:T(8,128)(2,1)}, u32[]{:S(2)}, u32[]{:S(2)}) collective-permute-start(bf16[4096,128]{1,0:T(8,128)(2,1)} %collective-permute-done.1.refs_2_), channel_id=1, source_target_pairs={{0,4},{4,0},{8,12},{12,8},{16,20},{20,16},{24,28},{28,24},{1,5},{5... | collective-permute-start | bytes 3145736 | tf_op jit(solution)/shard_map/ppermute | solution.py:41
  40.1 14.0 %collective-permute-start.2 = (bf16[2048,128]{1,0:T(8,128)(2,1)S(1)}, bf16[2048,128]{1,0:T(8,128)(2,1)}, u32[]{:S(2)}, u32[]{:S(2)}) collective-permute-start(bf16[2048,128]{1,0:T(8,128)(2,1)S(1)} %slice.80), channel_id=1, source_target_pairs={{0,8},{4,12},{8,24},{12,28},{24,16},{28,20},{16,0},{20,4},{1,9},{5... | collective-permute-start | bytes 1572872 | tf_op jit(solution)/shard_map/ppermute | solution.py:38
  42.8 13.0 %collective-permute-start.3 = (bf16[2048,128]{1,0:T(8,128)(2,1)S(1)}, bf16[2048,128]{1,0:T(8,128)(2,1)}, u32[]{:S(2)}, u32[]{:S(2)}) collective-permute-start(bf16[2048,128]{1,0:T(8,128)(2,1)S(1)} %slice.81), channel_id=1, source_target_pairs={{0,16},{4,20},{8,0},{12,4},{24,8},{28,12},{16,24},{20,28},{1,17},{... | collective-permute-start | bytes 1572872 | tf_op jit(solution)/shard_map/ppermute | solution.py:38
  58.1 32.9 %collective-permute-start.11 = (bf16[4096,128]{1,0:T(8,128)(2,1)S(1)}, bf16[4096,128]{1,0:T(8,128)(2,1)S(1)}, u32[]{:S(2)}, u32[]{:S(2)}) collective-permute-start(bf16[4096,128]{1,0:T(8,128)(2,1)S(1)} %get-tuple-element.193.refs_0_), channel_id=1, source_target_pairs={{0,8},{4,12},{8,24},{12,28},{24,16},{28,20},{16,0},{20,4},{1,9},{5... | collective-permute-start | bytes 3145736 | tf_op jit(solution)/shard_map/ppermute | solution.py:38
  59.6 31.5 %collective-permute-start.12 = (bf16[4096,128]{1,0:T(8,128)(2,1)S(1)}, bf16[4096,128]{1,0:T(8,128)(2,1)S(1)}, u32[]{:S(2)}, u32[]{:S(2)}) collective-permute-start(bf16[4096,128]{1,0:T(8,128)(2,1)S(1)} %get-tuple-element.193.refs_0_), channel_id=1, source_target_pairs={{0,16},{4,20},{8,0},{12,4},{24,8},{28,12},{16,24},{20,28},{1,17},{... | collective-permute-start | bytes 3145736 | tf_op jit(solution)/shard_map/ppermute | solution.py:38
  61.8 29.2 %collective-permute-start.7 = (bf16[1024,256]{1,0:T(8,128)(2,1)}, bf16[1024,256]{1,0:T(8,128)(2,1)S(1)}, u32[]{:S(2)}, u32[]{:S(2)}) collective-permute-start(bf16[1024,256]{1,0:T(8,128)(2,1)} %get-tuple-element.191), channel_id=1, source_target_pairs={{0,2},{1,3},{2,0},{3,1},{4,6},{5,7},{6,4},{7,5},{8,10},{9,11},{10,... | collective-permute-start | bytes 1572872 | tf_op jit(solution)/shard_map/ppermute | solution.py:87
  65.3 17.5 %collective-permute-start.8 = (bf16[128,256]{1,0:T(8,128)(2,1)S(1)}, bf16[128,256]{1,0:T(8,128)(2,1)S(1)}, u32[]{:S(2)}, u32[]{:S(2)}) collective-permute-start(bf16[128,256]{1,0:T(8,128)(2,1)S(1)} %constant_dynamic-slice_fusion.7), channel_id=1, source_target_pairs={{0,3},{1,0},{2,1},{3,2},{4,7},{5,4},{6,5},{7,6},{8,11},{9,8},{10,9... | collective-permute-start | bytes 196616 | tf_op jit(solution)/shard_map/ppermute | solution.py:87
  67.1 23.9 %collective-permute-start.9 = (bf16[128,256]{1,0:T(8,128)(2,1)S(1)}, bf16[128,256]{1,0:T(8,128)(2,1)S(1)}, u32[]{:S(2)}, u32[]{:S(2)}) collective-permute-start(bf16[128,256]{1,0:T(8,128)(2,1)S(1)} %constant_dynamic-slice_fusion.7), channel_id=1, source_target_pairs={{0,2},{1,3},{2,0},{3,1},{4,6},{5,7},{6,4},{7,5},{8,10},{9,11},{10,... | collective-permute-start | bytes 196616 | tf_op jit(solution)/shard_map/ppermute | solution.py:87
  94.4 14.0 %collective-permute-start.17 = (bf16[2048,128]{1,0:T(8,128)(2,1)}, bf16[2048,128]{1,0:T(8,128)(2,1)S(1)}, u32[]{:S(2)}, u32[]{:S(2)}) collective-permute-start(bf16[2048,128]{1,0:T(8,128)(2,1)} %slice.84), channel_id=1, source_target_pairs={{0,8},{4,12},{8,24},{12,28},{24,16},{28,20},{16,0},{20,4},{1,9},{5... | collective-permute-start | bytes 1572872 | tf_op jit(solution)/shard_map/ppermute | solution.py:38
  95.4 13.8 %collective-permute-start.18 = (bf16[2048,128]{1,0:T(8,128)(2,1)}, bf16[2048,128]{1,0:T(8,128)(2,1)S(1)}, u32[]{:S(2)}, u32[]{:S(2)}) collective-permute-start(bf16[2048,128]{1,0:T(8,128)(2,1)} %slice.85), channel_id=1, source_target_pairs={{0,16},{4,20},{8,0},{12,4},{24,8},{28,12},{16,24},{20,28},{1,17},{... | collective-permute-start | bytes 1572872 | tf_op jit(solution)/shard_map/ppermute | solution.py:38
  97.5 14.2 %collective-permute-start.21 = (bf16[1024,128]{1,0:T(8,128)(2,1)}, bf16[1024,128]{1,0:T(8,128)(2,1)}, u32[]{:S(2)}, u32[]{:S(2)}) collective-permute-start(bf16[1024,128]{1,0:T(8,128)(2,1)} %get-tuple-element.204), channel_id=1, source_target_pairs={{0,3},{1,0},{2,1},{3,2},{4,7},{5,4},{6,5},{7,6},{8,11},{9,8},{10,9... | collective-permute-start | bytes 786440 | tf_op jit(solution)/shard_map/ppermute | solution.py:87
  112.3 15.0 %collective-permute-start.23 = (bf16[1024,128]{1,0:T(8,128)(2,1)}, bf16[1024,128]{1,0:T(8,128)(2,1)S(1)}, u32[]{:S(2)}, u32[]{:S(2)}) collective-permute-start(bf16[1024,128]{1,0:T(8,128)(2,1)} %get-tuple-element.208), channel_id=1, source_target_pairs={{0,2},{1,3},{2,0},{3,1},{4,6},{5,7},{6,4},{7,5},{8,10},{9,11},{10,... | collective-permute-start | bytes 786440 | tf_op jit(solution)/shard_map/ppermute | solution.py:87
  128.0 14.6 %collective-permute-start.26 = (bf16[512,128]{1,0:T(8,128)(2,1)}, bf16[512,128]{1,0:T(8,128)(2,1)S(1)}, u32[]{:S(2)}, u32[]{:S(2)}) collective-permute-start(bf16[512,128]{1,0:T(8,128)(2,1)} %get-tuple-element.214), channel_id=1, source_target_pairs={{0,3},{1,0},{2,1},{3,2},{4,7},{5,4},{6,5},{7,6},{8,11},{9,8},{10,9... | collective-permute-start | bytes 393224 | tf_op jit(solution)/shard_map/ppermute | solution.py:87
  130.2 12.5 %collective-permute-start.27 = (bf16[512,128]{1,0:T(8,128)(2,1)}, bf16[512,128]{1,0:T(8,128)(2,1)S(1)}, u32[]{:S(2)}, u32[]{:S(2)}) collective-permute-start(bf16[512,128]{1,0:T(8,128)(2,1)} %get-tuple-element.215), channel_id=1, source_target_pairs={{0,2},{1,3},{2,0},{3,1},{4,6},{5,7},{6,4},{7,5},{8,10},{9,11},{10,... | collective-permute-start | bytes 393224 | tf_op jit(solution)/shard_map/ppermute | solution.py:87
  130.2 12.5 %collective-permute-start.28 = (bf16[512,128]{1,0:T(8,128)(2,1)}, bf16[512,128]{1,0:T(8,128)(2,1)S(1)}, u32[]{:S(2)}, u32[]{:S(2)}) collective-permute-start(bf16[512,128]{1,0:T(8,128)(2,1)} %get-tuple-element.216), channel_id=1, source_target_pairs={{0,1},{1,2},{2,3},{3,0},{4,5},{5,6},{6,7},{7,4},{8,9},{9,10},{10,1... | collective-permute-start | bytes 393224 | tf_op jit(solution)/shard_map/ppermute | solution.py:87
  157.6 14.0 %collective-permute-start.33 = (bf16[512,128]{1,0:T(8,128)(2,1)}, bf16[512,128]{1,0:T(8,128)(2,1)S(1)}, u32[]{:S(2)}, u32[]{:S(2)}) collective-permute-start(bf16[512,128]{1,0:T(8,128)(2,1)} %get-tuple-element.245), channel_id=1, source_target_pairs={{0,2},{1,3},{2,0},{3,1},{4,6},{5,7},{6,4},{7,5},{8,10},{9,11},{10,... | collective-permute-start | bytes 393224 | tf_op jit(solution)/shard_map/ppermute | solution.py:87
  178.1 13.3 %collective-permute-start.39 = (bf16[384,1024]{1,0:T(8,128)(2,1)S(1)}, bf16[384,1024]{1,0:T(8,128)(2,1)S(1)}, u32[]{:S(2)}, u32[]{:S(2)}) collective-permute-start(bf16[384,1024]{1,0:T(8,128)(2,1)S(1)} %pad_maximum_fusion), channel_id=1, source_target_pairs={{0,4},{4,0},{8,12},{12,8},{16,20},{20,16},{24,28},{28,24},{1,5},{5... | collective-permute-start | bytes 2359304 | tf_op jit(solution)/shard_map/ppermute | solution.py:41
  178.3 13.2 %collective-permute-start.36 = (bf16[512,128]{1,0:T(8,128)(2,1)S(1)}, bf16[512,128]{1,0:T(8,128)(2,1)S(1)}, u32[]{:S(2)}, u32[]{:S(2)}) collective-permute-start(bf16[512,128]{1,0:T(8,128)(2,1)S(1)} %copy-done.55), channel_id=1, source_target_pairs={{0,2},{1,3},{2,0},{3,1},{4,6},{5,7},{6,4},{7,5},{8,10},{9,11},{10,... | collective-permute-start | bytes 393224 | tf_op jit(solution)/shard_map/ppermute | solution.py:87
  179.1 12.4 %collective-permute-start.37 = (bf16[512,128]{1,0:T(8,128)(2,1)S(1)}, bf16[512,128]{1,0:T(8,128)(2,1)S(1)}, u32[]{:S(2)}, u32[]{:S(2)}) collective-permute-start(bf16[512,128]{1,0:T(8,128)(2,1)S(1)} %copy-done.54), channel_id=1, source_target_pairs={{0,1},{1,2},{2,3},{3,0},{4,5},{5,6},{6,7},{7,4},{8,9},{9,10},{10,1... | collective-permute-start | bytes 393224 | tf_op jit(solution)/shard_map/ppermute | solution.py:87
  191.5 24.5 %collective-permute-start.44 = (bf16[1024,128]{1,0:T(8,128)(2,1)S(1)}, bf16[1024,128]{1,0:T(8,128)(2,1)S(1)}, u32[]{:S(2)}, u32[]{:S(2)}) collective-permute-start(bf16[1024,128]{1,0:T(8,128)(2,1)S(1)} %copy-done.33), channel_id=1, source_target_pairs={{0,1},{1,2},{2,3},{3,0},{4,5},{5,6},{6,7},{7,4},{8,9},{9,10},{10,1... | collective-permute-start | bytes 786440 | tf_op jit(solution)/shard_map/ppermute | solution.py:87
  191.8 24.2 %collective-permute-start.43 = (bf16[1024,128]{1,0:T(8,128)(2,1)S(1)}, bf16[1024,128]{1,0:T(8,128)(2,1)S(1)}, u32[]{:S(2)}, u32[]{:S(2)}) collective-permute-start(bf16[1024,128]{1,0:T(8,128)(2,1)S(1)} %copy-done.34), channel_id=1, source_target_pairs={{0,2},{1,3},{2,0},{3,1},{4,6},{5,7},{6,4},{7,5},{8,10},{9,11},{10,... | collective-permute-start | bytes 786440 | tf_op jit(solution)/shard_map/ppermute | solution.py:87
  193.8 22.2 %collective-permute-start.42 = (bf16[1024,128]{1,0:T(8,128)(2,1)S(1)}, bf16[1024,128]{1,0:T(8,128)(2,1)S(1)}, u32[]{:S(2)}, u32[]{:S(2)}) collective-permute-start(bf16[1024,128]{1,0:T(8,128)(2,1)S(1)} %copy-done.35), channel_id=1, source_target_pairs={{0,3},{1,0},{2,1},{3,2},{4,7},{5,4},{6,5},{7,6},{8,11},{9,8},{10,9... | collective-permute-start | bytes 786440 | tf_op jit(solution)/shard_map/ppermute | solution.py:87
  196.7 19.2 %collective-permute-start.40 = (bf16[64,1024]{1,0:T(8,128)(2,1)S(1)}, bf16[64,1024]{1,0:T(8,128)(2,1)S(1)}, u32[]{:S(2)}, u32[]{:S(2)}) collective-permute-start(bf16[64,1024]{1,0:T(8,128)(2,1)S(1)} %get-tuple-element.399), channel_id=1, source_target_pairs={{0,8},{4,12},{8,24},{12,28},{24,16},{28,20},{16,0},{20,4},{1,9},{5... | collective-permute-start | bytes 393224 | tf_op jit(solution)/shard_map/ppermute | solution.py:38
  198.1 17.9 %collective-permute-start.41 = (bf16[64,1024]{1,0:T(8,128)(2,1)S(1)}, bf16[64,1024]{1,0:T(8,128)(2,1)S(1)}, u32[]{:S(2)}, u32[]{:S(2)}) collective-permute-start(bf16[64,1024]{1,0:T(8,128)(2,1)S(1)} %get-tuple-element.398), channel_id=1, source_target_pairs={{0,16},{4,20},{8,0},{12,4},{24,8},{28,12},{16,24},{20,28},{1,17},{... | collective-permute-start | bytes 393224 | tf_op jit(solution)/shard_map/ppermute | solution.py:38
  231.5 32.1 %collective-permute-start.49 = (bf16[4096,128]{1,0:T(8,128)(2,1)}, bf16[4096,128]{1,0:T(8,128)(2,1)S(1)}, u32[]{:S(2)}, u32[]{:S(2)}) collective-permute-start(bf16[4096,128]{1,0:T(8,128)(2,1)} %get-tuple-element.332), channel_id=1, source_target_pairs={{0,8},{4,12},{8,24},{12,28},{24,16},{28,20},{16,0},{20,4},{1,9},{5... | collective-permute-start | bytes 3145736 | tf_op jit(solution)/shard_map/ppermute | solution.py:38
  232.8 30.8 %collective-permute-start.50 = (bf16[4096,128]{1,0:T(8,128)(2,1)}, bf16[4096,128]{1,0:T(8,128)(2,1)S(1)}, u32[]{:S(2)}, u32[]{:S(2)}) collective-permute-start(bf16[4096,128]{1,0:T(8,128)(2,1)} %get-tuple-element.333), channel_id=1, source_target_pairs={{0,16},{4,20},{8,0},{12,4},{24,8},{28,12},{16,24},{20,28},{1,17},{... | collective-permute-start | bytes 3145736 | tf_op jit(solution)/shard_map/ppermute | solution.py:38
  233.6 30.0 %collective-permute-start.51 = (bf16[1024,256]{1,0:T(8,128)(2,1)}, bf16[1024,256]{1,0:T(8,128)(2,1)S(1)}, u32[]{:S(2)}, u32[]{:S(2)}) collective-permute-start(bf16[1024,256]{1,0:T(8,128)(2,1)} %get-tuple-element.335), channel_id=1, source_target_pairs={{0,2},{1,3},{2,0},{3,1},{4,6},{5,7},{6,4},{7,5},{8,10},{9,11},{10,... | collective-permute-start | bytes 1572872 | tf_op jit(solution)/shard_map/ppermute | solution.py:87
  235.5 27.1 %collective-permute-start.45 = (bf16[128,1024]{1,0:T(8,128)(2,1)S(1)}, bf16[128,1024]{1,0:T(8,128)(2,1)S(1)}, u32[]{:S(2)}, u32[]{:S(2)}) collective-permute-start(bf16[128,1024]{1,0:T(8,128)(2,1)S(1)} %get-tuple-element.397), channel_id=1, source_target_pairs={{0,8},{4,12},{8,24},{12,28},{24,16},{28,20},{16,0},{20,4},{1,9},{5... | collective-permute-start | bytes 786440 | tf_op jit(solution)/shard_map/ppermute | solution.py:38
  236.8 26.8 %collective-permute-start.46 = (bf16[128,1024]{1,0:T(8,128)(2,1)S(1)}, bf16[128,1024]{1,0:T(8,128)(2,1)S(1)}, u32[]{:S(2)}, u32[]{:S(2)}) collective-permute-start(bf16[128,1024]{1,0:T(8,128)(2,1)S(1)} %get-tuple-element.396), channel_id=1, source_target_pairs={{0,16},{4,20},{8,0},{12,4},{24,8},{28,12},{16,24},{20,28},{1,17},{... | collective-permute-start | bytes 786440 | tf_op jit(solution)/shard_map/ppermute | solution.py:38
  266.6 29.4 %collective-permute-start.55 = (bf16[12288,128]{1,0:T(8,128)(2,1)}, bf16[12288,128]{1,0:T(8,128)(2,1)S(1)}, u32[]{:S(2)}, u32[]{:S(2)}) collective-permute-start(bf16[12288,128]{1,0:T(8,128)(2,1)} %get-tuple-element.343), channel_id=1, source_target_pairs={{0,4},{4,0},{8,12},{12,8},{16,20},{20,16},{24,28},{28,24},{1,5},{5... | collective-permute-start | bytes 9437192 | tf_op jit(solution)/shard_map/ppermute | solution.py:41
  269.3 15.1 %collective-permute-start.52 = (bf16[2048,128]{1,0:T(8,128)(2,1)}, bf16[2048,128]{1,0:T(8,128)(2,1)}, u32[]{:S(2)}, u32[]{:S(2)}) collective-permute-start(bf16[2048,128]{1,0:T(8,128)(2,1)} %get-tuple-element.377), channel_id=1, source_target_pairs={{0,8},{4,12},{8,24},{12,28},{24,16},{28,20},{16,0},{20,4},{1,9},{5... | collective-permute-start | bytes 1572872 | tf_op jit(solution)/shard_map/ppermute | solution.py:38
  270.5 15.1 %collective-permute-start.53 = (bf16[2048,128]{1,0:T(8,128)(2,1)}, bf16[2048,128]{1,0:T(8,128)(2,1)}, u32[]{:S(2)}, u32[]{:S(2)}) collective-permute-start(bf16[2048,128]{1,0:T(8,128)(2,1)} %get-tuple-element.376), channel_id=1, source_target_pairs={{0,16},{4,20},{8,0},{12,4},{24,8},{28,12},{16,24},{20,28},{1,17},{... | collective-permute-start | bytes 1572872 | tf_op jit(solution)/shard_map/ppermute | solution.py:38
  272.6 22.5 %collective-permute-start.56 = (bf16[2048,128]{1,0:T(8,128)(2,1)}, bf16[2048,128]{1,0:T(8,128)(2,1)}, u32[]{:S(2)}, u32[]{:S(2)}) collective-permute-start(bf16[2048,128]{1,0:T(8,128)(2,1)} %get-tuple-element.379), channel_id=1, source_target_pairs={{0,8},{4,12},{8,24},{12,28},{24,16},{28,20},{16,0},{20,4},{1,9},{5... | collective-permute-start | bytes 1572872 | tf_op jit(solution)/shard_map/ppermute | solution.py:38
  273.8 22.2 %collective-permute-start.57 = (bf16[2048,128]{1,0:T(8,128)(2,1)}, bf16[2048,128]{1,0:T(8,128)(2,1)}, u32[]{:S(2)}, u32[]{:S(2)}) collective-permute-start(bf16[2048,128]{1,0:T(8,128)(2,1)} %get-tuple-element.378), channel_id=1, source_target_pairs={{0,16},{4,20},{8,0},{12,4},{24,8},{28,12},{16,24},{20,28},{1,17},{... | collective-permute-start | bytes 1572872 | tf_op jit(solution)/shard_map/ppermute | solution.py:38
  302.5 37.2 %collective-permute-start.60 = (bf16[4096,128]{1,0:T(8,128)(2,1)}, bf16[4096,128]{1,0:T(8,128)(2,1)}, u32[]{:S(2)}, u32[]{:S(2)}) collective-permute-start(bf16[4096,128]{1,0:T(8,128)(2,1)} %get-tuple-element.367), channel_id=1, source_target_pairs={{0,8},{4,12},{8,24},{12,28},{24,16},{28,20},{16,0},{20,4},{1,9},{5... | collective-permute-start | bytes 3145736 | tf_op jit(solution)/shard_map/ppermute | solution.py:38
  303.4 36.4 %collective-permute-start.61 = (bf16[4096,128]{1,0:T(8,128)(2,1)}, bf16[4096,128]{1,0:T(8,128)(2,1)}, u32[]{:S(2)}, u32[]{:S(2)}) collective-permute-start(bf16[4096,128]{1,0:T(8,128)(2,1)} %get-tuple-element.368), channel_id=1, source_target_pairs={{0,16},{4,20},{8,0},{12,4},{24,8},{28,12},{16,24},{20,28},{1,17},{... | collective-permute-start | bytes 3145736 | tf_op jit(solution)/shard_map/ppermute | solution.py:38
  304.6 32.9 %collective-permute-start.58 = (bf16[1024,256]{1,0:T(8,128)(2,1)}, bf16[1024,256]{1,0:T(8,128)(2,1)}, u32[]{:S(2)}, u32[]{:S(2)}) collective-permute-start(bf16[1024,256]{1,0:T(8,128)(2,1)} %get-tuple-element.361), channel_id=1, source_target_pairs={{0,3},{1,0},{2,1},{3,2},{4,7},{5,4},{6,5},{7,6},{8,11},{9,8},{10,9... | collective-permute-start | bytes 1572872 | tf_op jit(solution)/shard_map/ppermute | solution.py:87
  307.8 13.8 %collective-permute-start.62 = (bf16[128,256]{1,0:T(8,128)(2,1)S(1)}, bf16[128,256]{1,0:T(8,128)(2,1)S(1)}, u32[]{:S(2)}, u32[]{:S(2)}) collective-permute-start(bf16[128,256]{1,0:T(8,128)(2,1)S(1)} %get-tuple-element.370), channel_id=1, source_target_pairs={{0,1},{1,2},{2,3},{3,0},{4,5},{5,6},{6,7},{7,4},{8,9},{9,10},{10,1... | collective-permute-start | bytes 196616 | tf_op jit(solution)/shard_map/ppermute | solution.py:87
  307.8 15.2 %collective-permute-start.63 = (bf16[128,256]{1,0:T(8,128)(2,1)S(1)}, bf16[128,256]{1,0:T(8,128)(2,1)S(1)}, u32[]{:S(2)}, u32[]{:S(2)}) collective-permute-start(bf16[128,256]{1,0:T(8,128)(2,1)S(1)} %get-tuple-element.371), channel_id=1, source_target_pairs={{0,3},{1,0},{2,1},{3,2},{4,7},{5,4},{6,5},{7,6},{8,11},{9,8},{10,9... | collective-permute-start | bytes 196616 | tf_op jit(solution)/shard_map/ppermute | solution.py:87
  321.5 15.2 %collective-permute-start.64 = (bf16[128,256]{1,0:T(8,128)(2,1)S(1)}, bf16[128,256]{1,0:T(8,128)(2,1)S(1)}, u32[]{:S(2)}, u32[]{:S(2)}) collective-permute-start(bf16[128,256]{1,0:T(8,128)(2,1)S(1)} %get-tuple-element.372), channel_id=1, source_target_pairs={{0,2},{1,3},{2,0},{3,1},{4,6},{5,7},{6,4},{7,5},{8,10},{9,11},{10,... | collective-permute-start | bytes 196616 | tf_op jit(solution)/shard_map/ppermute | solution.py:87
  322.9 15.7 %collective-permute-start.59 = (bf16[1024,256]{1,0:T(8,128)(2,1)}, bf16[1024,256]{1,0:T(8,128)(2,1)}, u32[]{:S(2)}, u32[]{:S(2)}) collective-permute-start(bf16[1024,256]{1,0:T(8,128)(2,1)} %get-tuple-element.363), channel_id=1, source_target_pairs={{0,1},{1,2},{2,3},{3,0},{4,5},{5,6},{6,7},{7,4},{8,9},{9,10},{10,1... | collective-permute-start | bytes 1572872 | tf_op jit(solution)/shard_map/ppermute | solution.py:87
  (75 other events, 754.2 us)
Sparse Core Ops, SparseCore 0:
  111.8 27.4 all-gather.1

commit v12 on v11

--- a/solution.py
+++ b/solution.py
@@ -736,10 +736,12 @@
         combined = c < last and middle == 2
         got_far = red.far_swap()
         got_near = red.near_swap(got_far)
+        if c == last and c:
+            got_near, cuts = lax.optimization_barrier((got_near, cuts))
+            w.go(cuts_got=send(cuts, ends + inner))
+        sums = red.halves(got_far, got_near) if combined else red.far_sums(got_far)
         if c == 0:
-            wg_last = wg_steps(middle - 1, 0)
-            w.go(wg_last=wg_last)
-        sums = red.halves(got_far, got_near) if combined else red.far_sums(got_far)
+            sums, wg_last = lax.optimization_barrier((sums, wg_steps(middle - 1, 0)))
         w.go(**{f"got_near{c}": got_near})
         if c < last:
             grads = ordered(back[0][c + 1], w[f"rest_got{c + 1}"])
@@ -750,8 +752,7 @@
             w.go(act_inner=send_act(inner))
         w.close()
         if c == 0:
-            block = total_of(*wg.near_terms(0, w["wg_near"]), *wg.last(*w["wg_last"]))
-        if c == last:
+            block = total_of(*wg.near_terms(0, w["wg_near"]), *wg.last(*wg_last))
             cuts = [
                 w.gate(lax.dynamic_slice_in_dim(block, lax.rem(rep + u, parts) * f_wide, f_wide, 1))
                 for u in range(parts)
@@ -762,13 +763,15 @@
         for step in range(middle - 1, 0, -1):
             to_up, to_down = red.sums(step, w[f"got_near{c}"], *w[f"sum{c}_{step + 1}"], True)
             if step == 1 and c == last:
-                cuts, act, to_up, to_down = lax.optimization_barrier((cuts, act, to_up, to_down))
+                act, to_up, to_down = lax.optimization_barrier((act, to_up, to_down))
             w.go(**{f"sum{c}_{step}": red.hops(to_up, to_down)})
             if step > 1:
                 w.close()
     w.go(act_ends=send(act, ends))
-    cuts_got = send(cuts, ends + inner)
+    if last == 0:
+        w.go(cuts_got=send(cuts, ends + inner))
     got = {**w.done, **w.pending}
+    cuts_got = got["cuts_got"]
     got["weight_grad"] = functools.reduce(lambda a, b: a + b, [v.astype(F32) for v in [cuts[0], *cuts_got.values()]])
     ready = []
     at = near.index(0)

time: 354 us -> 339 us (0.958)
  waiting for transfers between devices: 119 us -> 106 us
    ppermute x20, waiting for transfers between devices: 55.2 us -> 42.5 us  [hop(): return lax.ppermute(value, 'row', self.perm(step))]
    unnamed x116 -> x120, local copies, waits for them, and re-layouts: 10.1 us -> 11.5 us
  transfers between devices with their start and end apart: 66 -> 66, of which waited for: 28 -> 26; matrix products, arithmetic and copies ran while one was open for 7% -> 7% of each run, Pallas kernels for 25% -> 28%
where the time goes in v12:
time: 339 us; the launch traced here: 337 us
  waiting for transfers between devices  106 us (31%)
  Pallas kernels  103 us (30%)
  starting transfers between devices  66.7 us (20%)
  local copies, waits for them, and re-layouts  27 us (8%)
  between operations  22.6 us (7%)
  other arithmetic  6.23 us (2%)
  matrix products  4.7 us (1%)
    ppermute x30, waiting for transfers between devices, send(): lax.ppermute(blocks[s], 'rep', [(i, (i + s) % size) for i in range(size)])  53.8 us
    ppermute x20, waiting for transfers between devices, hop(): return lax.ppermute(value, 'row', self.perm(step))  42.5 us
    ppermute x30, starting transfers between devices, send(): lax.ppermute(blocks[s], 'rep', [(i, (i + s) % size) for i in range(size)])  41.8 us
    pallas_call x3, Pallas kernels, spmm(): pl.pallas_call(functools.partial(spmm_kernel, len(pieces), per_part, skip...  36.7 us
    pallas_call x2, Pallas kernels, spmm_t(): pl.pallas_call(functools.partial(spmm_t_kernel, len(grads), per_part, len...  34.5 us
    ppermute x20, starting transfers between devices, hop(): return lax.ppermute(value, 'row', self.perm(step))  22.1 us
    pallas_call x2, Pallas kernels, dense(): pl.pallas_call(functools.partial(dense_kernel, parts, chunks, len(earlier...  14.1 us
    unnamed x120, local copies, waits for them, and re-layouts  11.5 us
  transfers between devices with their start and end apart: 66, of which 26 were waited for; matrix products, arithmetic and copies ran while one was open for 7% of the time, Pallas kernels for 28%

profile of v12, /device:TPU:0, one launch (start us, length us, event | category | flops | bytes accessed | tf_op | source)
XLA Modules:
  0.0 337.0 jit_solution(15796851485596744120)
XLA Ops:
  7.7 1.7 fusion.1
  9.4 2.6 collective-permute-start
  12.1 2.9 constant_dynamic-slice_fusion.5
  15.0 4.0 %collective-permute-start.4 = (bf16[1024,256]{1,0:T(8,128)(2,1)}, bf16[1024,256]{1,0:T(8,128)(2,1)S(1)}, u32[]{:S(2)}, u32[]{:S(2)}) collective-permute-start(bf16[1024,256]{1,0:T(8,128)(2,1)} %get-tuple-element.401), channel_id=1, source_target_pairs={{0,3},{1,0},{2,1},{3,2},{4,7},{5,4},{6,5},{7,6},{8,11},{9,8},{10,9... | collective-permute-start | bytes 1572872 | tf_op jit(solution)/shard_map/ppermute | solution.py:87
  29.5 6.5 %collective-permute-done.refs_1_ = bf16[4096,128]{1,0:T(8,128)(2,1)} collective-permute-done((bf16[4096,128]{1,0:T(8,128)(2,1)S(1)}, bf16[4096,128]{1,0:T(8,128)(2,1)}, u32[]{:S(2)}, u32[]{:S(2)}) %collective-permute-start) | collective-permute-done | bytes 1048608 | tf_op jit(solution)/shard_map/ppermute | solution.py:38
  44.3 9.8 %collective-permute-done.2.refs_3_ = bf16[2048,128]{1,0:T(8,128)(2,1)} collective-permute-done((bf16[2048,128]{1,0:T(8,128)(2,1)S(1)}, bf16[2048,128]{1,0:T(8,128)(2,1)}, u32[]{:S(2)}, u32[]{:S(2)}) %collective-permute-start.2) | collective-permute-done | bytes 524320 | tf_op jit(solution)/shard_map/ppermute | solution.py:38
  54.1 1.7 collective-permute-done.3.refs_4_
  60.1 1.7 collective-permute-done.10
  62.3 3.0 fusion
  65.3 1.8 collective-permute-start.8
  68.3 14.5 %spmm.3 = (bf16[1024,128]{1,0:T(8,128)(2,1)}, bf16[1024,128]{1,0:T(8,128)(2,1)}, bf16[1024,128]{1,0:T(8,128)(2,1)}, bf16[1024,128]{1,0:T(8,128)(2,1)}) custom-call(s32[32,16]{1,0:T(8,128)} %copy.71.cols, s32[32]{0:T(128)} %counts.9, s32[11]{0:T(128)} %stack.75.meta, bf16[32,16,128,128]{3,2,1,0:T(8,128)(2,1)} %tiles.9, bf16[4096,128]{1,0:T(8,128)(2,1)} %copy-done.9, ...), custom_call_target="tpu_custom_call" | custom-call | flops 2147483648 | bytes 25165824 | tf_op jit(solution)/shard_map/spmm/pallas_call | solution.py:158
  82.8 8.3 %collective-permute-done.9 = bf16[128,256]{1,0:T(8,128)(2,1)S(1)} collective-permute-done((bf16[128,256]{1,0:T(8,128)(2,1)S(1)}, bf16[128,256]{1,0:T(8,128)(2,1)S(1)}, u32[]{:S(2)}, u32[]{:S(2)}) %collective-permute-start.9) | collective-permute-done | bytes 65568 | tf_op jit(solution)/shard_map/ppermute | solution.py:87
  97.5 3.8 %collective-permute-start.21 = (bf16[1024,128]{1,0:T(8,128)(2,1)}, bf16[1024,128]{1,0:T(8,128)(2,1)}, u32[]{:S(2)}, u32[]{:S(2)}) collective-permute-start(bf16[1024,128]{1,0:T(8,128)(2,1)} %get-tuple-element.210), channel_id=1, source_target_pairs={{0,3},{1,0},{2,1},{3,2},{4,7},{5,4},{6,5},{7,6},{8,11},{9,8},{10,9... | collective-permute-start | bytes 786440 | tf_op jit(solution)/shard_map/ppermute | solution.py:87
  102.1 6.4 %collective-permute-done.17.refs_3_ = bf16[2048,128]{1,0:T(8,128)(2,1)S(1)} collective-permute-done((bf16[2048,128]{1,0:T(8,128)(2,1)}, bf16[2048,128]{1,0:T(8,128)(2,1)S(1)}, u32[]{:S(2)}, u32[]{:S(2)}) %collective-permute-start.17) | collective-permute-done | bytes 524320 | tf_op jit(solution)/shard_map/ppermute | solution.py:38
  109.2 2.5 collective-permute-done.21.refs_2_
  112.3 2.4 collective-permute-start.23
  115.7 11.2 %spmm.4 = (bf16[512,128]{1,0:T(8,128)(2,1)}, bf16[512,128]{1,0:T(8,128)(2,1)}, bf16[512,128]{1,0:T(8,128)(2,1)}, bf16[512,128]{1,0:T(8,128)(2,1)}) custom-call(s32[32,16]{1,0:T(8,128)} %copy.71.cols, s32[32]{0:T(128)} %counts.9, s32[11]{0:T(128)} %stack.75.meta, bf16[32,16,128,128]{3,2,1,0:T(8,128)(2,1)} %tiles.9, bf16[4096,128]{1,0:T(8,128)(2,1)} %copy-done.4, ...), custom_call_target="tpu_custom_call" | custom-call | flops 1073741824 | bytes 16777216 | tf_op jit(solution)/shard_map/spmm/pallas_call | solution.py:158
  128.0 2.2 collective-permute-start.26
  131.6 11.0 %spmm.5 = (bf16[512,128]{1,0:T(8,128)(2,1)}, bf16[512,128]{1,0:T(8,128)(2,1)}, bf16[512,128]{1,0:T(8,128)(2,1)}, bf16[512,128]{1,0:T(8,128)(2,1)}) custom-call(s32[32,16]{1,0:T(8,128)} %copy.71.cols, s32[32]{0:T(128)} %counts.9, s32[11]{0:T(128)} %stack.75.meta, bf16[32,16,128,128]{3,2,1,0:T(8,128)(2,1)} %tiles.9, bf16[4096,128]{1,0:T(8,128)(2,1)} %copy-done.4, ...), custom_call_target="tpu_custom_call" | custom-call | flops 1073741824 | bytes 16777216 | tf_op jit(solution)/shard_map/spmm/pallas_call | solution.py:158
  142.8 2.5 collective-permute-start.29
  146.5 7.0 %dense.2 = (bf16[1024,256]{1,0:T(8,128)(2,1)}, bf16[1024,256]{1,0:T(8,128)(2,1)}, bf16[1024,256]{1,0:T(8,128)(2,1)}, bf16[1024,256]{1,0:T(8,128)(2,1)}, bf16[512...) custom-call(s32[1]{0:T(128)} %bitcast.meta, ...), custom_call_target="tpu_custom_call" | custom-call | flops 2147483648 | bytes 8388608 | tf_op jit(solution)/shard_map/dense/pallas_call | solution.py:325
  153.5 4.0 %collective-permute-done.30.refs_5_ = bf16[512,128]{1,0:T(8,128)(2,1)S(1)} collective-permute-done((bf16[512,128]{1,0:T(8,128)(2,1)}, bf16[512,128]{1,0:T(8,128)(2,1)S(1)}, u32[]{:S(2)}, u32[]{:S(2)}) %collective-permute-start.30) | collective-permute-done | bytes 131104 | tf_op jit(solution)/shard_map/ppermute | solution.py:87
  159.3 2.0 collective-permute-start.34
  161.3 7.1 %dense.3 = (bf16[1024,256]{1,0:T(8,128)(2,1)}, bf16[1024,256]{1,0:T(8,128)(2,1)}, bf16[1024,256]{1,0:T(8,128)(2,1)}, bf16[1024,256]{1,0:T(8,128)(2,1)}, bf16[512...) custom-call(s32[1]{0:T(128)} %bitcast.meta, ...), custom_call_target="tpu_custom_call", output_to_operand_aliasing={{0}: (14, {}), {1}: (15, {}), {2}: (16, {}), {3}: (17, {}),... | custom-call | flops 2147483648 | bytes 8388608 | tf_op jit(solution)/shard_map/dense/pallas_call | solution.py:325
  168.4 3.2 collective-permute-done.33.refs_4_
  171.6 4.7 %convolution_convert_fusion = bf16[1024,1024]{1,0:T(8,128)(2,1)S(1)} fusion(bf16[1024,1024]{1,0:T(8,128)(2,1)} %get-tuple-element.288, bf16[1024,1024]{1,0:T(8,128)(2,1)} %get-tuple-element.289), kind=kOutput, calls=%fused_computation | convolution fusion | flops 2148532224 | bytes 6291456 | tf_op jit(solution)/shard_map/dot_general | solution.py:694
  179.2 2.0 collective-permute-start.37
  181.1 4.3 %collective-permute-done.35.refs_3_ = bf16[512,128]{1,0:T(8,128)(2,1)S(1)} collective-permute-done((bf16[512,128]{1,0:T(8,128)(2,1)S(1)}, bf16[512,128]{1,0:T(8,128)(2,1)S(1)}, u32[]{:S(2)}, u32[]{:S(2)}) %collective-permute-start.35) | collective-permute-done | bytes 131104 | tf_op jit(solution)/shard_map/ppermute | solution.py:87
  185.4 6.1 %collective-permute-done.36.refs_5_ = bf16[512,128]{1,0:T(8,128)(2,1)S(1)} collective-permute-done((bf16[512,128]{1,0:T(8,128)(2,1)S(1)}, bf16[512,128]{1,0:T(8,128)(2,1)S(1)}, u32[]{:S(2)}, u32[]{:S(2)}) %collective-permute-start.36) | collective-permute-done | bytes 131104 | tf_op jit(solution)/shard_map/ppermute | solution.py:87
  191.9 2.0 collective-permute-start.43
  193.9 2.8 collective-permute-start.42
  198.9 17.2 %spmm_t.2 = (bf16[4096,128]{1,0:T(8,128)(2,1)}, bf16[4096,128]{1,0:T(8,128)(2,1)}, bf16[4096,128]{1,0:T(8,128)(2,1)}, bf16[4096,128]{1,0:T(8,128)(2,1)}, bf16[40...) custom-call(s32[32,16]{1,0:T(8,128)} %copy.71.cols, s32[32]{0:T(128)} %counts.9, s32[9]{0:T(128)} %stack.84.meta, ...), custom_call_target="tpu_custom_call" | custom-call | flops 2147483648 | bytes 25165824 | tf_op jit(solution)/shard_map/spmm_t/pallas_call | solution.py:241
  216.2 2.9 collective-permute-done.45.got_far
  221.5 3.5 %collective-permute-done.46.got_up.got_down.got = bf16[12288,128]{1,0:T(8,128)(2,1)S(1)} collective-permute-done((bf16[12288,128]{1,0:T(8,128)(2,1)}, bf16[12288,128]{1,0:T(8,128)(2,1)S(1)}, u32[]{:S(2)}, u32[]{:S(2)}) %collective-permute-start.46) | collective-permute-done | bytes 3145760 | tf_op jit(solution)/shard_map/ppermute | solution.py:41
  226.7 4.4 %halves_sums.1 = (bf16[4096,128]{1,0:T(8,128)(2,1)}, bf16[4096,128]{1,0:T(8,128)(2,1)}) custom-call(bf16[4096,128]{1,0:T(8,128)(2,1)} %get-tuple-element.321.own_far, bf16[4096,128]{1,0:T(8,128)(2,1)} %copy-done.23, bf16[4096,128]{1,0:T(8,128)(2,1)} %get-tuple-element.322.own_up, bf16[12288,128]{1,0:T(8,128)(2,1)} %copy-done.2, ...), custom_call_target="tpu_custom_call" | custom-call | flops 1048576 | bytes 6291456 | tf_op jit(solution)/shard_map/halves_sums/pallas_call | solution.py:465
  234.9 17.4 %spmm_t.3 = (bf16[4096,128]{1,0:T(8,128)(2,1)}, bf16[4096,128]{1,0:T(8,128)(2,1)}, bf16[4096,128]{1,0:T(8,128)(2,1)}, bf16[4096,128]{1,0:T(8,128)(2,1)}, bf16[40...) custom-call(s32[32,16]{1,0:T(8,128)} %copy.71.cols, s32[32]{0:T(128)} %counts.9, s32[9]{0:T(128)} %stack.84.meta, ...), custom_call_target="tpu_custom_call" | custom-call | flops 2147483648 | bytes 25165824 | tf_op jit(solution)/shard_map/spmm_t/pallas_call | solution.py:241
  252.3 7.2 %collective-permute-done.51 = bf16[1024,256]{1,0:T(8,128)(2,1)S(1)} collective-permute-done((bf16[1024,256]{1,0:T(8,128)(2,1)S(1)}, bf16[1024,256]{1,0:T(8,128)(2,1)S(1)}, u32[]{:S(2)}, u32[]{:S(2)}) %collective-permute-start.51) | collective-permute-done | bytes 524320 | tf_op jit(solution)/shard_map/ppermute | solution.py:87
  260.3 2.2 collective-permute-done.54
  262.6 2.6 add_convert_fusion.2
  271.9 2.5 collective-permute-start.56
  274.3 5.9 %collective-permute-done.52.up_low = bf16[2048,128]{1,0:T(8,128)(2,1)} collective-permute-done((bf16[2048,128]{1,0:T(8,128)(2,1)}, bf16[2048,128]{1,0:T(8,128)(2,1)}, u32[]{:S(2)}, u32[]{:S(2)}) %collective-permute-start.52) | collective-permute-done | bytes 524320 | tf_op jit(solution)/shard_map/ppermute | solution.py:38
  283.2 7.7 %collective-permute-done.59.up = bf16[2048,128]{1,0:T(8,128)(2,1)} collective-permute-done((bf16[2048,128]{1,0:T(8,128)(2,1)}, bf16[2048,128]{1,0:T(8,128)(2,1)}, u32[]{:S(2)}, u32[]{:S(2)}) %collective-permute-start.59) | collective-permute-done | bytes 524320 | tf_op jit(solution)/shard_map/ppermute | solution.py:38
  292.0 4.9 %step_sums.1 = (bf16[4096,128]{1,0:T(8,128)(2,1)}, bf16[4096,128]{1,0:T(8,128)(2,1)}) custom-call(bf16[4096,128]{1,0:T(8,128)(2,1)} %get-tuple-element.346.own_up, bf16[12288,128]{1,0:T(8,128)(2,1)} %copy-done.3, bf16[2048,128]{1,0:T(8,128)(2,1)} %collective-permute-done.59.up, bf16[4096,128]{1,0:T(8,128)(2,1)} %get-tuple-element.367.own_down, ...), custom_call_target="tpu_custom_call" | custom-call | flops 2097152 | bytes 7340032 | tf_op jit(solution)/shard_map/step_sums/pallas_call | solution.py:390
  298.9 2.3 collective-permute-start.61
  302.0 4.2 %joined.1.refs_0_ = bf16[4096,128]{1,0:T(8,128)(2,1)} custom-call(bf16[4096,128]{1,0:T(8,128)(2,1)} %get-tuple-element.375.own, bf16[12288,128]{1,0:T(8,128)(2,1)} %copy-done.2, bf16[2048,128]{1,0:T(8,128)(2,1)} %collective-permute-done.52.up_low, bf16[4096,128]{1,0:T(8,128)(2,1)} %copy-done.12, bf16[4096,128]{1,0:T(8,128)(2,1)} %copy-done.13, ...), custom_call_target="tpu_custom_call" | custom-call | flops 1572864 | bytes 5242880 | tf_op jit(solution)/shard_map/joined/pallas_call | solution.py:509
  307.4 6.6 %collective-permute-done.61 = bf16[1024,256]{1,0:T(8,128)(2,1)} collective-permute-done((bf16[1024,256]{1,0:T(8,128)(2,1)}, bf16[1024,256]{1,0:T(8,128)(2,1)}, u32[]{:S(2)}, u32[]{:S(2)}) %collective-permute-start.61) | collective-permute-done | bytes 524320 | tf_op jit(solution)/shard_map/ppermute | solution.py:87
  315.1 8.4 %collective-permute-done.62 = bf16[1024,256]{1,0:T(8,128)(2,1)S(1)} collective-permute-done((bf16[1024,256]{1,0:T(8,128)(2,1)}, bf16[1024,256]{1,0:T(8,128)(2,1)S(1)}, u32[]{:S(2)}, u32[]{:S(2)}) %collective-permute-start.62) | collective-permute-done | bytes 524320 | tf_op jit(solution)/shard_map/ppermute | solution.py:87
  325.5 4.6 %feature_grad.1 = bf16[4096,256]{1,0:T(8,128)(2,1)} custom-call(bf16[4096,128]{1,0:T(8,128)(2,1)} %joined.1.refs_0_, bf16[4096,128]{1,0:T(8,128)(2,1)} %get-tuple-element.378.refs_1_, bf16[12288,128]{1,0:T(8,128)(2,1)} %copy-done.3, bf16[4096,128]{1,0:T(8,128)(2,1)} %copy-done.20, bf16[4096,128]{1,0:T(8,128)(2,1)} %copy-done.21), custom_call_target="tpu_custom_call" | custom-call | flops 2097152 | bytes 7340032 | tf_op jit(solution)/shard_map/feature_grad/pallas_call | solution.py:426
  (244 shorter events, 64.5 us)
Async XLA Ops:
  7.2 139.3 %all-gather.2.cloned.1.call-start = ((), (), s32[]{:S(2)}) async-start(), calls=%async_computation | async-start | bytes 2359296 | tf_op jit(solution)/shard_map/all_gather | solution.py:670
  7.2 48.5 %collective-permute-start.6 = (bf16[4096,256]{1,0:T(8,128)(2,1)}, bf16[4096,256]{1,0:T(8,128)(2,1)}, u32[]{:S(2)}, u32[]{:S(2)}) collective-permute-start(bf16[4096,256]{1,0:T(8,128)(2,1)} %param.58), channel_id=1, source_target_pairs={{0,4},{4,0},{8,12},{12,8},{16,20},{20,16},{24,28},{28,24},{1,5},{5... | collective-permute-start | bytes 6291464 | tf_op jit(solution)/shard_map/ppermute | solution.py:41
  9.4 26.5 %collective-permute-start = (bf16[4096,128]{1,0:T(8,128)(2,1)S(1)}, bf16[4096,128]{1,0:T(8,128)(2,1)}, u32[]{:S(2)}, u32[]{:S(2)}) collective-permute-start(bf16[4096,128]{1,0:T(8,128)(2,1)S(1)} %get-tuple-element.407.refs_0_), channel_id=1, source_target_pairs={{0,8},{4,12},{8,24},{12,28},{24,16},{28,20},{16,0},{20,4},{1,9},{5... | collective-permute-start | bytes 3145736 | tf_op jit(solution)/shard_map/ppermute | solution.py:38
  12.0 25.4 %collective-permute-start.1 = (bf16[4096,128]{1,0:T(8,128)(2,1)S(1)}, bf16[4096,128]{1,0:T(8,128)(2,1)}, u32[]{:S(2)}, u32[]{:S(2)}) collective-permute-start(bf16[4096,128]{1,0:T(8,128)(2,1)S(1)} %get-tuple-element.407.refs_0_), channel_id=1, source_target_pairs={{0,16},{4,20},{8,0},{12,4},{24,8},{28,12},{16,24},{20,28},{1,17},{... | collective-permute-start | bytes 3145736 | tf_op jit(solution)/shard_map/ppermute | solution.py:38
  15.0 25.0 %collective-permute-start.4 = (bf16[1024,256]{1,0:T(8,128)(2,1)}, bf16[1024,256]{1,0:T(8,128)(2,1)S(1)}, u32[]{:S(2)}, u32[]{:S(2)}) collective-permute-start(bf16[1024,256]{1,0:T(8,128)(2,1)} %get-tuple-element.401), channel_id=1, source_target_pairs={{0,3},{1,0},{2,1},{3,2},{4,7},{5,4},{6,5},{7,6},{8,11},{9,8},{10,9... | collective-permute-start | bytes 1572872 | tf_op jit(solution)/shard_map/ppermute | solution.py:87
  19.1 23.7 %collective-permute-start.5 = (bf16[1024,256]{1,0:T(8,128)(2,1)}, bf16[1024,256]{1,0:T(8,128)(2,1)}, u32[]{:S(2)}, u32[]{:S(2)}) collective-permute-start(bf16[1024,256]{1,0:T(8,128)(2,1)} %get-tuple-element.403), channel_id=1, source_target_pairs={{0,1},{1,2},{2,3},{3,0},{4,5},{5,6},{6,7},{7,4},{8,9},{9,10},{10,1... | collective-permute-start | bytes 1572872 | tf_op jit(solution)/shard_map/ppermute | solution.py:87
  37.4 22.2 %collective-permute-start.13 = (bf16[4096,128]{1,0:T(8,128)(2,1)}, bf16[4096,128]{1,0:T(8,128)(2,1)}, u32[]{:S(2)}, u32[]{:S(2)}) collective-permute-start(bf16[4096,128]{1,0:T(8,128)(2,1)} %collective-permute-done.refs_1_), channel_id=1, source_target_pairs={{0,4},{4,0},{8,12},{12,8},{16,20},{20,16},{24,28},{28,24},{1,5},{5... | collective-permute-start | bytes 3145736 | tf_op jit(solution)/shard_map/ppermute | solution.py:41
  37.4 22.7 %collective-permute-start.14 = (bf16[4096,128]{1,0:T(8,128)(2,1)}, bf16[4096,128]{1,0:T(8,128)(2,1)}, u32[]{:S(2)}, u32[]{:S(2)}) collective-permute-start(bf16[4096,128]{1,0:T(8,128)(2,1)} %collective-permute-done.1.refs_2_), channel_id=1, source_target_pairs={{0,4},{4,0},{8,12},{12,8},{16,20},{20,16},{24,28},{28,24},{1,5},{5... | collective-permute-start | bytes 3145736 | tf_op jit(solution)/shard_map/ppermute | solution.py:41
  40.1 14.0 %collective-permute-start.2 = (bf16[2048,128]{1,0:T(8,128)(2,1)S(1)}, bf16[2048,128]{1,0:T(8,128)(2,1)}, u32[]{:S(2)}, u32[]{:S(2)}) collective-permute-start(bf16[2048,128]{1,0:T(8,128)(2,1)S(1)} %slice.80), channel_id=1, source_target_pairs={{0,8},{4,12},{8,24},{12,28},{24,16},{28,20},{16,0},{20,4},{1,9},{5... | collective-permute-start | bytes 1572872 | tf_op jit(solution)/shard_map/ppermute | solution.py:38
  42.8 13.0 %collective-permute-start.3 = (bf16[2048,128]{1,0:T(8,128)(2,1)S(1)}, bf16[2048,128]{1,0:T(8,128)(2,1)}, u32[]{:S(2)}, u32[]{:S(2)}) collective-permute-start(bf16[2048,128]{1,0:T(8,128)(2,1)S(1)} %slice.81), channel_id=1, source_target_pairs={{0,16},{4,20},{8,0},{12,4},{24,8},{28,12},{16,24},{20,28},{1,17},{... | collective-permute-start | bytes 1572872 | tf_op jit(solution)/shard_map/ppermute | solution.py:38
  58.1 32.9 %collective-permute-start.11 = (bf16[4096,128]{1,0:T(8,128)(2,1)S(1)}, bf16[4096,128]{1,0:T(8,128)(2,1)S(1)}, u32[]{:S(2)}, u32[]{:S(2)}) collective-permute-start(bf16[4096,128]{1,0:T(8,128)(2,1)S(1)} %get-tuple-element.199.refs_0_), channel_id=1, source_target_pairs={{0,8},{4,12},{8,24},{12,28},{24,16},{28,20},{16,0},{20,4},{1,9},{5... | collective-permute-start | bytes 3145736 | tf_op jit(solution)/shard_map/ppermute | solution.py:38
  59.6 31.5 %collective-permute-start.12 = (bf16[4096,128]{1,0:T(8,128)(2,1)S(1)}, bf16[4096,128]{1,0:T(8,128)(2,1)S(1)}, u32[]{:S(2)}, u32[]{:S(2)}) collective-permute-start(bf16[4096,128]{1,0:T(8,128)(2,1)S(1)} %get-tuple-element.199.refs_0_), channel_id=1, source_target_pairs={{0,16},{4,20},{8,0},{12,4},{24,8},{28,12},{16,24},{20,28},{1,17},{... | collective-permute-start | bytes 3145736 | tf_op jit(solution)/shard_map/ppermute | solution.py:38
  61.8 29.2 %collective-permute-start.7 = (bf16[1024,256]{1,0:T(8,128)(2,1)}, bf16[1024,256]{1,0:T(8,128)(2,1)S(1)}, u32[]{:S(2)}, u32[]{:S(2)}) collective-permute-start(bf16[1024,256]{1,0:T(8,128)(2,1)} %get-tuple-element.197), channel_id=1, source_target_pairs={{0,2},{1,3},{2,0},{3,1},{4,6},{5,7},{6,4},{7,5},{8,10},{9,11},{10,... | collective-permute-start | bytes 1572872 | tf_op jit(solution)/shard_map/ppermute | solution.py:87
  65.3 17.5 %collective-permute-start.8 = (bf16[128,256]{1,0:T(8,128)(2,1)S(1)}, bf16[128,256]{1,0:T(8,128)(2,1)S(1)}, u32[]{:S(2)}, u32[]{:S(2)}) collective-permute-start(bf16[128,256]{1,0:T(8,128)(2,1)S(1)} %constant_dynamic-slice_fusion.7), channel_id=1, source_target_pairs={{0,3},{1,0},{2,1},{3,2},{4,7},{5,4},{6,5},{7,6},{8,11},{9,8},{10,9... | collective-permute-start | bytes 196616 | tf_op jit(solution)/shard_map/ppermute | solution.py:87
  67.1 23.9 %collective-permute-start.9 = (bf16[128,256]{1,0:T(8,128)(2,1)S(1)}, bf16[128,256]{1,0:T(8,128)(2,1)S(1)}, u32[]{:S(2)}, u32[]{:S(2)}) collective-permute-start(bf16[128,256]{1,0:T(8,128)(2,1)S(1)} %constant_dynamic-slice_fusion.7), channel_id=1, source_target_pairs={{0,2},{1,3},{2,0},{3,1},{4,6},{5,7},{6,4},{7,5},{8,10},{9,11},{10,... | collective-permute-start | bytes 196616 | tf_op jit(solution)/shard_map/ppermute | solution.py:87
  94.4 14.0 %collective-permute-start.17 = (bf16[2048,128]{1,0:T(8,128)(2,1)}, bf16[2048,128]{1,0:T(8,128)(2,1)S(1)}, u32[]{:S(2)}, u32[]{:S(2)}) collective-permute-start(bf16[2048,128]{1,0:T(8,128)(2,1)} %slice.84), channel_id=1, source_target_pairs={{0,8},{4,12},{8,24},{12,28},{24,16},{28,20},{16,0},{20,4},{1,9},{5... | collective-permute-start | bytes 1572872 | tf_op jit(solution)/shard_map/ppermute | solution.py:38
  95.5 13.8 %collective-permute-start.18 = (bf16[2048,128]{1,0:T(8,128)(2,1)}, bf16[2048,128]{1,0:T(8,128)(2,1)S(1)}, u32[]{:S(2)}, u32[]{:S(2)}) collective-permute-start(bf16[2048,128]{1,0:T(8,128)(2,1)} %slice.85), channel_id=1, source_target_pairs={{0,16},{4,20},{8,0},{12,4},{24,8},{28,12},{16,24},{20,28},{1,17},{... | collective-permute-start | bytes 1572872 | tf_op jit(solution)/shard_map/ppermute | solution.py:38
  97.5 11.7 %collective-permute-start.22 = (bf16[1024,128]{1,0:T(8,128)(2,1)}, bf16[1024,128]{1,0:T(8,128)(2,1)S(1)}, u32[]{:S(2)}, u32[]{:S(2)}) collective-permute-start(bf16[1024,128]{1,0:T(8,128)(2,1)} %get-tuple-element.212), channel_id=1, source_target_pairs={{0,1},{1,2},{2,3},{3,0},{4,5},{5,6},{6,7},{7,4},{8,9},{9,10},{10,1... | collective-permute-start | bytes 786440 | tf_op jit(solution)/shard_map/ppermute | solution.py:87
  97.5 14.2 %collective-permute-start.21 = (bf16[1024,128]{1,0:T(8,128)(2,1)}, bf16[1024,128]{1,0:T(8,128)(2,1)}, u32[]{:S(2)}, u32[]{:S(2)}) collective-permute-start(bf16[1024,128]{1,0:T(8,128)(2,1)} %get-tuple-element.210), channel_id=1, source_target_pairs={{0,3},{1,0},{2,1},{3,2},{4,7},{5,4},{6,5},{7,6},{8,11},{9,8},{10,9... | collective-permute-start | bytes 786440 | tf_op jit(solution)/shard_map/ppermute | solution.py:87
  112.3 15.0 %collective-permute-start.23 = (bf16[1024,128]{1,0:T(8,128)(2,1)}, bf16[1024,128]{1,0:T(8,128)(2,1)S(1)}, u32[]{:S(2)}, u32[]{:S(2)}) collective-permute-start(bf16[1024,128]{1,0:T(8,128)(2,1)} %get-tuple-element.214), channel_id=1, source_target_pairs={{0,2},{1,3},{2,0},{3,1},{4,6},{5,7},{6,4},{7,5},{8,10},{9,11},{10,... | collective-permute-start | bytes 786440 | tf_op jit(solution)/shard_map/ppermute | solution.py:87
  128.0 14.7 %collective-permute-start.26 = (bf16[512,128]{1,0:T(8,128)(2,1)}, bf16[512,128]{1,0:T(8,128)(2,1)S(1)}, u32[]{:S(2)}, u32[]{:S(2)}) collective-permute-start(bf16[512,128]{1,0:T(8,128)(2,1)} %get-tuple-element.220), channel_id=1, source_target_pairs={{0,3},{1,0},{2,1},{3,2},{4,7},{5,4},{6,5},{7,6},{8,11},{9,8},{10,9... | collective-permute-start | bytes 393224 | tf_op jit(solution)/shard_map/ppermute | solution.py:87
  130.2 12.5 %collective-permute-start.27 = (bf16[512,128]{1,0:T(8,128)(2,1)}, bf16[512,128]{1,0:T(8,128)(2,1)S(1)}, u32[]{:S(2)}, u32[]{:S(2)}) collective-permute-start(bf16[512,128]{1,0:T(8,128)(2,1)} %get-tuple-element.221), channel_id=1, source_target_pairs={{0,2},{1,3},{2,0},{3,1},{4,6},{5,7},{6,4},{7,5},{8,10},{9,11},{10,... | collective-permute-start | bytes 393224 | tf_op jit(solution)/shard_map/ppermute | solution.py:87
  130.2 12.5 %collective-permute-start.28 = (bf16[512,128]{1,0:T(8,128)(2,1)}, bf16[512,128]{1,0:T(8,128)(2,1)S(1)}, u32[]{:S(2)}, u32[]{:S(2)}) collective-permute-start(bf16[512,128]{1,0:T(8,128)(2,1)} %get-tuple-element.222), channel_id=1, source_target_pairs={{0,1},{1,2},{2,3},{3,0},{4,5},{5,6},{6,7},{7,4},{8,9},{9,10},{10,1... | collective-permute-start | bytes 393224 | tf_op jit(solution)/shard_map/ppermute | solution.py:87
  145.2 12.3 %collective-permute-start.30 = (bf16[512,128]{1,0:T(8,128)(2,1)}, bf16[512,128]{1,0:T(8,128)(2,1)S(1)}, u32[]{:S(2)}, u32[]{:S(2)}) collective-permute-start(bf16[512,128]{1,0:T(8,128)(2,1)} %get-tuple-element.228), channel_id=1, source_target_pairs={{0,2},{1,3},{2,0},{3,1},{4,6},{5,7},{6,4},{7,5},{8,10},{9,11},{10,... | collective-permute-start | bytes 393224 | tf_op jit(solution)/shard_map/ppermute | solution.py:87
  157.6 14.0 %collective-permute-start.33 = (bf16[512,128]{1,0:T(8,128)(2,1)}, bf16[512,128]{1,0:T(8,128)(2,1)S(1)}, u32[]{:S(2)}, u32[]{:S(2)}) collective-permute-start(bf16[512,128]{1,0:T(8,128)(2,1)} %get-tuple-element.251), channel_id=1, source_target_pairs={{0,2},{1,3},{2,0},{3,1},{4,6},{5,7},{6,4},{7,5},{8,10},{9,11},{10,... | collective-permute-start | bytes 393224 | tf_op jit(solution)/shard_map/ppermute | solution.py:87
  159.3 12.3 %collective-permute-start.34 = (bf16[512,128]{1,0:T(8,128)(2,1)}, bf16[512,128]{1,0:T(8,128)(2,1)S(1)}, u32[]{:S(2)}, u32[]{:S(2)}) collective-permute-start(bf16[512,128]{1,0:T(8,128)(2,1)} %get-tuple-element.252), channel_id=1, source_target_pairs={{0,1},{1,2},{2,3},{3,0},{4,5},{5,6},{6,7},{7,4},{8,9},{9,10},{10,1... | collective-permute-start | bytes 393224 | tf_op jit(solution)/shard_map/ppermute | solution.py:87
  178.2 13.3 %collective-permute-start.39 = (bf16[384,1024]{1,0:T(8,128)(2,1)S(1)}, bf16[384,1024]{1,0:T(8,128)(2,1)S(1)}, u32[]{:S(2)}, u32[]{:S(2)}) collective-permute-start(bf16[384,1024]{1,0:T(8,128)(2,1)S(1)} %pad_maximum_fusion), channel_id=1, source_target_pairs={{0,4},{4,0},{8,12},{12,8},{16,20},{20,16},{24,28},{28,24},{1,5},{5... | collective-permute-start | bytes 2359304 | tf_op jit(solution)/shard_map/ppermute | solution.py:41
  178.3 13.2 %collective-permute-start.36 = (bf16[512,128]{1,0:T(8,128)(2,1)S(1)}, bf16[512,128]{1,0:T(8,128)(2,1)S(1)}, u32[]{:S(2)}, u32[]{:S(2)}) collective-permute-start(bf16[512,128]{1,0:T(8,128)(2,1)S(1)} %copy-done.57), channel_id=1, source_target_pairs={{0,2},{1,3},{2,0},{3,1},{4,6},{5,7},{6,4},{7,5},{8,10},{9,11},{10,... | collective-permute-start | bytes 393224 | tf_op jit(solution)/shard_map/ppermute | solution.py:87
  179.2 12.4 %collective-permute-start.37 = (bf16[512,128]{1,0:T(8,128)(2,1)S(1)}, bf16[512,128]{1,0:T(8,128)(2,1)S(1)}, u32[]{:S(2)}, u32[]{:S(2)}) collective-permute-start(bf16[512,128]{1,0:T(8,128)(2,1)S(1)} %copy-done.56), channel_id=1, source_target_pairs={{0,1},{1,2},{2,3},{3,0},{4,5},{5,6},{6,7},{7,4},{8,9},{9,10},{10,1... | collective-permute-start | bytes 393224 | tf_op jit(solution)/shard_map/ppermute | solution.py:87
  191.6 24.5 %collective-permute-start.44 = (bf16[1024,128]{1,0:T(8,128)(2,1)S(1)}, bf16[1024,128]{1,0:T(8,128)(2,1)S(1)}, u32[]{:S(2)}, u32[]{:S(2)}) collective-permute-start(bf16[1024,128]{1,0:T(8,128)(2,1)S(1)} %copy-done.36), channel_id=1, source_target_pairs={{0,1},{1,2},{2,3},{3,0},{4,5},{5,6},{6,7},{7,4},{8,9},{9,10},{10,1... | collective-permute-start | bytes 786440 | tf_op jit(solution)/shard_map/ppermute | solution.py:87
  191.9 24.2 %collective-permute-start.43 = (bf16[1024,128]{1,0:T(8,128)(2,1)S(1)}, bf16[1024,128]{1,0:T(8,128)(2,1)S(1)}, u32[]{:S(2)}, u32[]{:S(2)}) collective-permute-start(bf16[1024,128]{1,0:T(8,128)(2,1)S(1)} %copy-done.37), channel_id=1, source_target_pairs={{0,2},{1,3},{2,0},{3,1},{4,6},{5,7},{6,4},{7,5},{8,10},{9,11},{10,... | collective-permute-start | bytes 786440 | tf_op jit(solution)/shard_map/ppermute | solution.py:87
  193.9 22.2 %collective-permute-start.42 = (bf16[1024,128]{1,0:T(8,128)(2,1)S(1)}, bf16[1024,128]{1,0:T(8,128)(2,1)S(1)}, u32[]{:S(2)}, u32[]{:S(2)}) collective-permute-start(bf16[1024,128]{1,0:T(8,128)(2,1)S(1)} %copy-done.38), channel_id=1, source_target_pairs={{0,3},{1,0},{2,1},{3,2},{4,7},{5,4},{6,5},{7,6},{8,11},{9,8},{10,9... | collective-permute-start | bytes 786440 | tf_op jit(solution)/shard_map/ppermute | solution.py:87
  196.8 19.2 %collective-permute-start.40 = (bf16[64,1024]{1,0:T(8,128)(2,1)S(1)}, bf16[64,1024]{1,0:T(8,128)(2,1)S(1)}, u32[]{:S(2)}, u32[]{:S(2)}) collective-permute-start(bf16[64,1024]{1,0:T(8,128)(2,1)S(1)} %get-tuple-element.411), channel_id=1, source_target_pairs={{0,8},{4,12},{8,24},{12,28},{24,16},{28,20},{16,0},{20,4},{1,9},{5... | collective-permute-start | bytes 393224 | tf_op jit(solution)/shard_map/ppermute | solution.py:38
  198.1 17.9 %collective-permute-start.41 = (bf16[64,1024]{1,0:T(8,128)(2,1)S(1)}, bf16[64,1024]{1,0:T(8,128)(2,1)S(1)}, u32[]{:S(2)}, u32[]{:S(2)}) collective-permute-start(bf16[64,1024]{1,0:T(8,128)(2,1)S(1)} %get-tuple-element.410), channel_id=1, source_target_pairs={{0,16},{4,20},{8,0},{12,4},{24,8},{28,12},{16,24},{20,28},{1,17},{... | collective-permute-start | bytes 393224 | tf_op jit(solution)/shard_map/ppermute | solution.py:38
  219.4 11.7 %collective-permute-start.47 = (bf16[128,1024]{1,0:T(8,128)(2,1)S(1)}, bf16[128,1024]{1,0:T(8,128)(2,1)S(1)}, u32[]{:S(2)}, u32[]{:S(2)}) collective-permute-start(bf16[128,1024]{1,0:T(8,128)(2,1)S(1)} %get-tuple-element.409), channel_id=1, source_target_pairs={{0,8},{4,12},{8,24},{12,28},{24,16},{28,20},{16,0},{20,4},{1,9},{5... | collective-permute-start | bytes 786440 | tf_op jit(solution)/shard_map/ppermute | solution.py:38
  231.9 27.6 %collective-permute-start.49 = (bf16[4096,128]{1,0:T(8,128)(2,1)}, bf16[4096,128]{1,0:T(8,128)(2,1)S(1)}, u32[]{:S(2)}, u32[]{:S(2)}) collective-permute-start(bf16[4096,128]{1,0:T(8,128)(2,1)} %get-tuple-element.343), channel_id=1, source_target_pairs={{0,8},{4,12},{8,24},{12,28},{24,16},{28,20},{16,0},{20,4},{1,9},{5... | collective-permute-start | bytes 3145736 | tf_op jit(solution)/shard_map/ppermute | solution.py:38
  233.2 26.3 %collective-permute-start.50 = (bf16[4096,128]{1,0:T(8,128)(2,1)}, bf16[4096,128]{1,0:T(8,128)(2,1)S(1)}, u32[]{:S(2)}, u32[]{:S(2)}) collective-permute-start(bf16[4096,128]{1,0:T(8,128)(2,1)} %get-tuple-element.344), channel_id=1, source_target_pairs={{0,16},{4,20},{8,0},{12,4},{24,8},{28,12},{16,24},{20,28},{1,17},{... | collective-permute-start | bytes 3145736 | tf_op jit(solution)/shard_map/ppermute | solution.py:38
  233.9 25.5 %collective-permute-start.51 = (bf16[1024,256]{1,0:T(8,128)(2,1)S(1)}, bf16[1024,256]{1,0:T(8,128)(2,1)S(1)}, u32[]{:S(2)}, u32[]{:S(2)}) collective-permute-start(bf16[1024,256]{1,0:T(8,128)(2,1)S(1)} %copy-done.27), channel_id=1, source_target_pairs={{0,2},{1,3},{2,0},{3,1},{4,6},{5,7},{6,4},{7,5},{8,10},{9,11},{10,... | collective-permute-start | bytes 1572872 | tf_op jit(solution)/shard_map/ppermute | solution.py:87
  265.2 15.1 %collective-permute-start.52 = (bf16[2048,128]{1,0:T(8,128)(2,1)}, bf16[2048,128]{1,0:T(8,128)(2,1)}, u32[]{:S(2)}, u32[]{:S(2)}) collective-permute-start(bf16[2048,128]{1,0:T(8,128)(2,1)} %get-tuple-element.389), channel_id=1, source_target_pairs={{0,8},{4,12},{8,24},{12,28},{24,16},{28,20},{16,0},{20,4},{1,9},{5... | collective-permute-start | bytes 1572872 | tf_op jit(solution)/shard_map/ppermute | solution.py:38
  266.5 15.1 %collective-permute-start.53 = (bf16[2048,128]{1,0:T(8,128)(2,1)}, bf16[2048,128]{1,0:T(8,128)(2,1)}, u32[]{:S(2)}, u32[]{:S(2)}) collective-permute-start(bf16[2048,128]{1,0:T(8,128)(2,1)} %get-tuple-element.388), channel_id=1, source_target_pairs={{0,16},{4,20},{8,0},{12,4},{24,8},{28,12},{16,24},{20,28},{1,17},{... | collective-permute-start | bytes 1572872 | tf_op jit(solution)/shard_map/ppermute | solution.py:38
  268.5 22.5 %collective-permute-start.59 = (bf16[2048,128]{1,0:T(8,128)(2,1)}, bf16[2048,128]{1,0:T(8,128)(2,1)}, u32[]{:S(2)}, u32[]{:S(2)}) collective-permute-start(bf16[2048,128]{1,0:T(8,128)(2,1)} %get-tuple-element.391), channel_id=1, source_target_pairs={{0,8},{4,12},{8,24},{12,28},{24,16},{28,20},{16,0},{20,4},{1,9},{5... | collective-permute-start | bytes 1572872 | tf_op jit(solution)/shard_map/ppermute | solution.py:38
  269.8 22.2 %collective-permute-start.60 = (bf16[2048,128]{1,0:T(8,128)(2,1)}, bf16[2048,128]{1,0:T(8,128)(2,1)}, u32[]{:S(2)}, u32[]{:S(2)}) collective-permute-start(bf16[2048,128]{1,0:T(8,128)(2,1)} %get-tuple-element.390), channel_id=1, source_target_pairs={{0,16},{4,20},{8,0},{12,4},{24,8},{28,12},{16,24},{20,28},{1,17},{... | collective-permute-start | bytes 1572872 | tf_op jit(solution)/shard_map/ppermute | solution.py:38
  271.9 20.1 %collective-permute-start.56 = (bf16[128,256]{1,0:T(8,128)(2,1)S(1)}, bf16[128,256]{1,0:T(8,128)(2,1)S(1)}, u32[]{:S(2)}, u32[]{:S(2)}) collective-permute-start(bf16[128,256]{1,0:T(8,128)(2,1)S(1)} %get-tuple-element.360), channel_id=1, source_target_pairs={{0,3},{1,0},{2,1},{3,2},{4,7},{5,4},{6,5},{7,6},{8,11},{9,8},{10,9... | collective-permute-start | bytes 196616 | tf_op jit(solution)/shard_map/ppermute | solution.py:87
  280.3 11.7 %collective-permute-start.57 = (bf16[128,256]{1,0:T(8,128)(2,1)S(1)}, bf16[128,256]{1,0:T(8,128)(2,1)S(1)}, u32[]{:S(2)}, u32[]{:S(2)}) collective-permute-start(bf16[128,256]{1,0:T(8,128)(2,1)S(1)} %get-tuple-element.361), channel_id=1, source_target_pairs={{0,2},{1,3},{2,0},{3,1},{4,6},{5,7},{6,4},{7,5},{8,10},{9,11},{10,... | collective-permute-start | bytes 196616 | tf_op jit(solution)/shard_map/ppermute | solution.py:87
  296.9 26.6 %collective-permute-start.63 = (bf16[4096,128]{1,0:T(8,128)(2,1)}, bf16[4096,128]{1,0:T(8,128)(2,1)S(1)}, u32[]{:S(2)}, u32[]{:S(2)}) collective-permute-start(bf16[4096,128]{1,0:T(8,128)(2,1)} %get-tuple-element.379), channel_id=1, source_target_pairs={{0,8},{4,12},{8,24},{12,28},{24,16},{28,20},{16,0},{20,4},{1,9},{5... | collective-permute-start | bytes 3145736 | tf_op jit(solution)/shard_map/ppermute | solution.py:38
  298.1 25.4 %collective-permute-start.64 = (bf16[4096,128]{1,0:T(8,128)(2,1)}, bf16[4096,128]{1,0:T(8,128)(2,1)S(1)}, u32[]{:S(2)}, u32[]{:S(2)}) collective-permute-start(bf16[4096,128]{1,0:T(8,128)(2,1)} %get-tuple-element.380), channel_id=1, source_target_pairs={{0,16},{4,20},{8,0},{12,4},{24,8},{28,12},{16,24},{20,28},{1,17},{... | collective-permute-start | bytes 3145736 | tf_op jit(solution)/shard_map/ppermute | solution.py:38
  298.9 15.0 %collective-permute-start.61 = (bf16[1024,256]{1,0:T(8,128)(2,1)}, bf16[1024,256]{1,0:T(8,128)(2,1)}, u32[]{:S(2)}, u32[]{:S(2)}) collective-permute-start(bf16[1024,256]{1,0:T(8,128)(2,1)} %get-tuple-element.372), channel_id=1, source_target_pairs={{0,3},{1,0},{2,1},{3,2},{4,7},{5,4},{6,5},{7,6},{8,11},{9,8},{10,9... | collective-permute-start | bytes 1572872 | tf_op jit(solution)/shard_map/ppermute | solution.py:87
  301.2 22.2 %collective-permute-start.62 = (bf16[1024,256]{1,0:T(8,128)(2,1)}, bf16[1024,256]{1,0:T(8,128)(2,1)S(1)}, u32[]{:S(2)}, u32[]{:S(2)}) collective-permute-start(bf16[1024,256]{1,0:T(8,128)(2,1)} %get-tuple-element.374), channel_id=1, source_target_pairs={{0,1},{1,2},{2,3},{3,0},{4,5},{5,6},{6,7},{7,4},{8,9},{9,10},{10,1... | collective-permute-start | bytes 1572872 | tf_op jit(solution)/shard_map/ppermute | solution.py:87
  (77 other events, 693.6 us)
Sparse Core Ops, SparseCore 0:
  111.9 27.4 all-gather.1

commit v13 on v12

--- a/solution.py
+++ b/solution.py
@@ -728,45 +728,60 @@
     def send_act(shifts):
         return send([w.gate(a) for a in act], shifts)
 
+    def reduction(terms):
+        red = Reduction(ring, terms[0], terms[1:-2], terms[-2], terms[-1])
+        got_far = red.far_swap()
+        return red, got_far, red.near_swap(got_far)
+
     reductions = []
+    combined_before = False
+    red, got_far, got_near = reduction(w["terms0"])
     for c in range(chunks):
-        terms = w[f"terms{c}"]
-        red = Reduction(ring, terms[0], terms[1:-2], terms[-2], terms[-1])
         reductions.append(red)
         combined = c < last and middle == 2
-        got_far = red.far_swap()
-        got_near = red.near_swap(got_far)
         if c == last and c:
             got_near, cuts = lax.optimization_barrier((got_near, cuts))
             w.go(cuts_got=send(cuts, ends + inner))
-        sums = red.halves(got_far, got_near) if combined else red.far_sums(got_far)
+        if c == 0 or not combined_before:
+            sums = red.halves(got_far, got_near) if combined else red.far_sums(got_far)
         if c == 0:
             sums, wg_last = lax.optimization_barrier((sums, wg_steps(middle - 1, 0)))
         w.go(**{f"got_near{c}": got_near})
         if c < last:
             grads = ordered(back[0][c + 1], w[f"rest_got{c + 1}"])
             grads, sums = lax.optimization_barrier((grads, sums))
-            w.go(**{f"terms{c + 1}": run_spmm_t(c + 1, grads)})
-        w.go(**{f"sum{c}_{middle}": red.hops(*sums)})
+            following = reduction(run_spmm_t(c + 1, grads))
+            w.go(following=following[1:], following_sums=following[0].far_sums(following[1]) if combined else ())
+        first = red.hops(*sums)
+        w.go(**{f"sum{c}_{middle}": first})
         if c == 0:
             w.go(act_inner=send_act(inner))
-        w.close()
+        if c < last or not combined_before:
+            w.close()
         if c == 0:
             block = total_of(*wg.near_terms(0, w["wg_near"]), *wg.last(*wg_last))
             cuts = [
                 w.gate(lax.dynamic_slice_in_dim(block, lax.rem(rep + u, parts) * f_wide, f_wide, 1))
                 for u in range(parts)
             ]
+        combined_before = combined
         if combined:
-            w.go(**{f"sum{c}_1": red.hops(*red.other_halves(w[f"got_near{c}"], *w[f"sum{c}_{middle}"]))})
+            halves_next = red.other_halves(w[f"got_near{c}"], *w[f"sum{c}_{middle}"])
+            red, (got_far, got_near), sums = following[0], w.done.pop("following"), w.done.pop("following_sums")
+            w.go(**{f"sum{c}_1": red.hops(*halves_next)})
             continue
+        now = {**w.done, **w.pending}
         for step in range(middle - 1, 0, -1):
-            to_up, to_down = red.sums(step, w[f"got_near{c}"], *w[f"sum{c}_{step + 1}"], True)
+            to_up, to_down = red.sums(step, now[f"got_near{c}"], *now[f"sum{c}_{step + 1}"], True)
             if step == 1 and c == last:
                 act, to_up, to_down = lax.optimization_barrier((act, to_up, to_down))
             w.go(**{f"sum{c}_{step}": red.hops(to_up, to_down)})
             if step > 1:
                 w.close()
+            now = {**w.done, **w.pending}
+        if c < last:
+            red, (got_far, got_near) = following[0], w.done.pop("following")
+            w.done.pop("following_sums")
     w.go(act_ends=send(act, ends))
     if last == 0:
         w.go(cuts_got=send(cuts, ends + inner))

time: 339 us -> 358 us (1.056)
  waiting for transfers between devices: 106 us -> 117 us
  starting transfers between devices: 66.7 us -> 73 us
    ppermute x30, waiting for transfers between devices: 53.8 us -> 60.9 us  [send(): lax.ppermute(blocks[s], 'rep', [(i, (i + s) % size) for i in range(size)])]
    ppermute x30, starting transfers between devices: 41.8 us -> 47.8 us  [send(): lax.ppermute(blocks[s], 'rep', [(i, (i + s) % size) for i in range(size)])]
    unnamed x120 -> x122, local copies, waits for them, and re-layouts: 11.5 us -> 10.4 us
  transfers between devices with their start and end apart: 66 -> 66, of which waited for: 26 -> 24; matrix products, arithmetic and copies ran while one was open for 7% -> 7% of each run, Pallas kernels for 28% -> 23%
where the time goes in v13:
time: 358 us; the launch traced here: 356 us
  waiting for transfers between devices  117 us (33%)
  Pallas kernels  103 us (29%)
  starting transfers between devices  73 us (20%)
  local copies, waits for them, and re-layouts  28.8 us (8%)
  between operations  22.5 us (6%)
  other arithmetic  6.88 us (2%)
  matrix products  4.7 us (1%)
    ppermute x30, waiting for transfers between devices, send(): lax.ppermute(blocks[s], 'rep', [(i, (i + s) % size) for i in range(size)])  60.9 us
    ppermute x30, starting transfers between devices, send(): lax.ppermute(blocks[s], 'rep', [(i, (i + s) % size) for i in range(size)])  47.8 us
    ppermute x20, waiting for transfers between devices, hop(): return lax.ppermute(value, 'row', self.perm(step))  45.4 us
    pallas_call x3, Pallas kernels, spmm(): pl.pallas_call(functools.partial(spmm_kernel, len(pieces), per_part, skip...  36.7 us
    pallas_call x2, Pallas kernels, spmm_t(): pl.pallas_call(functools.partial(spmm_t_kernel, len(grads), per_part, len...  34.5 us
    ppermute x20, starting transfers between devices, hop(): return lax.ppermute(value, 'row', self.perm(step))  22.2 us
    pallas_call x2, Pallas kernels, dense(): pl.pallas_call(functools.partial(dense_kernel, parts, chunks, len(earlier...  14.1 us
    ppermute x15, waiting for transfers between devices, sibling(): return lax.ppermute(value, 'row', [(d, d ^ 1) for d in range(self.devices)])  10.6 us
  transfers between devices with their start and end apart: 66, of which 24 were waited for; matrix products, arithmetic and copies ran while one was open for 7% of the time, Pallas kernels for 23%

profile of v13, /device:TPU:0, one launch (start us, length us, event | category | flops | bytes accessed | tf_op | source)
XLA Modules:
  0.0 356.3 jit_solution(1045993925477233140)
XLA Ops:
  7.7 1.7 fusion.1
  9.4 2.6 collective-permute-start
  12.1 2.9 constant_dynamic-slice_fusion.5
  15.0 4.0 %collective-permute-start.4 = (bf16[1024,256]{1,0:T(8,128)(2,1)}, bf16[1024,256]{1,0:T(8,128)(2,1)S(1)}, u32[]{:S(2)}, u32[]{:S(2)}) collective-permute-start(bf16[1024,256]{1,0:T(8,128)(2,1)} %get-tuple-element.379), channel_id=1, source_target_pairs={{0,3},{1,0},{2,1},{3,2},{4,7},{5,4},{6,5},{7,6},{8,11},{9,8},{10,9... | collective-permute-start | bytes 1572872 | tf_op jit(solution)/shard_map/ppermute | solution.py:87
  29.3 6.7 %collective-permute-done.refs_1_ = bf16[4096,128]{1,0:T(8,128)(2,1)} collective-permute-done((bf16[4096,128]{1,0:T(8,128)(2,1)S(1)}, bf16[4096,128]{1,0:T(8,128)(2,1)}, u32[]{:S(2)}, u32[]{:S(2)}) %collective-permute-start) | collective-permute-done | bytes 1048608 | tf_op jit(solution)/shard_map/ppermute | solution.py:38
  37.9 1.9 slice.80
  44.3 10.8 %collective-permute-done.2.refs_3_ = bf16[2048,128]{1,0:T(8,128)(2,1)} collective-permute-done((bf16[2048,128]{1,0:T(8,128)(2,1)}, bf16[2048,128]{1,0:T(8,128)(2,1)}, u32[]{:S(2)}, u32[]{:S(2)}) %collective-permute-start.2) | collective-permute-done | bytes 524320 | tf_op jit(solution)/shard_map/ppermute | solution.py:38
  60.3 1.8 collective-permute-done.10
  63.0 3.0 fusion
  69.0 14.5 %spmm.3 = (bf16[1024,128]{1,0:T(8,128)(2,1)}, bf16[1024,128]{1,0:T(8,128)(2,1)}, bf16[1024,128]{1,0:T(8,128)(2,1)}, bf16[1024,128]{1,0:T(8,128)(2,1)}) custom-call(s32[32,16]{1,0:T(8,128)} %copy.71.cols, s32[32]{0:T(128)} %counts.9, s32[11]{0:T(128)} %stack.75.meta, bf16[32,16,128,128]{3,2,1,0:T(8,128)(2,1)} %tiles.9, bf16[4096,128]{1,0:T(8,128)(2,1)} %copy-done.9, ...), custom_call_target="tpu_custom_call" | custom-call | flops 2147483648 | bytes 25165824 | tf_op jit(solution)/shard_map/spmm/pallas_call | solution.py:158
  83.4 7.8 %collective-permute-done.9 = bf16[128,256]{1,0:T(8,128)(2,1)S(1)} collective-permute-done((bf16[128,256]{1,0:T(8,128)(2,1)S(1)}, bf16[128,256]{1,0:T(8,128)(2,1)S(1)}, u32[]{:S(2)}, u32[]{:S(2)}) %collective-permute-start.9) | collective-permute-done | bytes 65568 | tf_op jit(solution)/shard_map/ppermute | solution.py:87
  97.7 3.8 %collective-permute-start.21 = (bf16[1024,128]{1,0:T(8,128)(2,1)}, bf16[1024,128]{1,0:T(8,128)(2,1)}, u32[]{:S(2)}, u32[]{:S(2)}) collective-permute-start(bf16[1024,128]{1,0:T(8,128)(2,1)} %get-tuple-element.199), channel_id=1, source_target_pairs={{0,3},{1,0},{2,1},{3,2},{4,7},{5,4},{6,5},{7,6},{8,11},{9,8},{10,9... | collective-permute-start | bytes 786440 | tf_op jit(solution)/shard_map/ppermute | solution.py:87
  102.3 6.4 %collective-permute-done.17.refs_3_ = bf16[2048,128]{1,0:T(8,128)(2,1)S(1)} collective-permute-done((bf16[2048,128]{1,0:T(8,128)(2,1)}, bf16[2048,128]{1,0:T(8,128)(2,1)S(1)}, u32[]{:S(2)}, u32[]{:S(2)}) %collective-permute-start.17) | collective-permute-done | bytes 524320 | tf_op jit(solution)/shard_map/ppermute | solution.py:38
  109.6 2.3 collective-permute-done.21.refs_2_
  112.5 2.4 collective-permute-start.23
  115.9 11.2 %spmm.4 = (bf16[512,128]{1,0:T(8,128)(2,1)}, bf16[512,128]{1,0:T(8,128)(2,1)}, bf16[512,128]{1,0:T(8,128)(2,1)}, bf16[512,128]{1,0:T(8,128)(2,1)}) custom-call(s32[32,16]{1,0:T(8,128)} %copy.71.cols, s32[32]{0:T(128)} %counts.9, s32[11]{0:T(128)} %stack.75.meta, bf16[32,16,128,128]{3,2,1,0:T(8,128)(2,1)} %tiles.9, bf16[4096,128]{1,0:T(8,128)(2,1)} %copy-done.4, ...), custom_call_target="tpu_custom_call" | custom-call | flops 1073741824 | bytes 16777216 | tf_op jit(solution)/shard_map/spmm/pallas_call | solution.py:158
  128.2 2.2 collective-permute-start.26
  131.8 11.1 %spmm.5 = (bf16[512,128]{1,0:T(8,128)(2,1)}, bf16[512,128]{1,0:T(8,128)(2,1)}, bf16[512,128]{1,0:T(8,128)(2,1)}, bf16[512,128]{1,0:T(8,128)(2,1)}) custom-call(s32[32,16]{1,0:T(8,128)} %copy.71.cols, s32[32]{0:T(128)} %counts.9, s32[11]{0:T(128)} %stack.75.meta, bf16[32,16,128,128]{3,2,1,0:T(8,128)(2,1)} %tiles.9, bf16[4096,128]{1,0:T(8,128)(2,1)} %copy-done.4, ...), custom_call_target="tpu_custom_call" | custom-call | flops 1073741824 | bytes 16777216 | tf_op jit(solution)/shard_map/spmm/pallas_call | solution.py:158
  142.9 2.5 collective-permute-start.29
  146.7 7.0 %dense.2 = (bf16[1024,256]{1,0:T(8,128)(2,1)}, bf16[1024,256]{1,0:T(8,128)(2,1)}, bf16[1024,256]{1,0:T(8,128)(2,1)}, bf16[1024,256]{1,0:T(8,128)(2,1)}, bf16[512...) custom-call(s32[1]{0:T(128)} %bitcast.meta, ...), custom_call_target="tpu_custom_call" | custom-call | flops 2147483648 | bytes 8388608 | tf_op jit(solution)/shard_map/dense/pallas_call | solution.py:325
  153.8 4.0 %collective-permute-done.30.refs_5_ = bf16[512,128]{1,0:T(8,128)(2,1)S(1)} collective-permute-done((bf16[512,128]{1,0:T(8,128)(2,1)}, bf16[512,128]{1,0:T(8,128)(2,1)S(1)}, u32[]{:S(2)}, u32[]{:S(2)}) %collective-permute-start.30) | collective-permute-done | bytes 131104 | tf_op jit(solution)/shard_map/ppermute | solution.py:87
  159.5 2.0 collective-permute-start.34
  161.5 7.1 %dense.3 = (bf16[1024,256]{1,0:T(8,128)(2,1)}, bf16[1024,256]{1,0:T(8,128)(2,1)}, bf16[1024,256]{1,0:T(8,128)(2,1)}, bf16[1024,256]{1,0:T(8,128)(2,1)}, bf16[512...) custom-call(s32[1]{0:T(128)} %bitcast.meta, ...), custom_call_target="tpu_custom_call", output_to_operand_aliasing={{0}: (14, {}), {1}: (15, {}), {2}: (16, {}), {3}: (17, {}),... | custom-call | flops 2147483648 | bytes 8388608 | tf_op jit(solution)/shard_map/dense/pallas_call | solution.py:325
  168.6 3.2 collective-permute-done.33.refs_4_
  171.8 4.7 %convolution_convert_fusion = bf16[1024,1024]{1,0:T(8,128)(2,1)S(1)} fusion(bf16[1024,1024]{1,0:T(8,128)(2,1)} %get-tuple-element.279, bf16[1024,1024]{1,0:T(8,128)(2,1)} %get-tuple-element.280), kind=kOutput, calls=%fused_computation | convolution fusion | flops 2148532224 | bytes 6291456 | tf_op jit(solution)/shard_map/dot_general | solution.py:694
  179.4 2.0 collective-permute-start.37
  181.3 4.3 %collective-permute-done.35.refs_3_ = bf16[512,128]{1,0:T(8,128)(2,1)S(1)} collective-permute-done((bf16[512,128]{1,0:T(8,128)(2,1)S(1)}, bf16[512,128]{1,0:T(8,128)(2,1)S(1)}, u32[]{:S(2)}, u32[]{:S(2)}) %collective-permute-start.35) | collective-permute-done | bytes 131104 | tf_op jit(solution)/shard_map/ppermute | solution.py:87
  185.6 6.1 %collective-permute-done.36.refs_5_ = bf16[512,128]{1,0:T(8,128)(2,1)S(1)} collective-permute-done((bf16[512,128]{1,0:T(8,128)(2,1)S(1)}, bf16[512,128]{1,0:T(8,128)(2,1)S(1)}, u32[]{:S(2)}, u32[]{:S(2)}) %collective-permute-start.36) | collective-permute-done | bytes 131104 | tf_op jit(solution)/shard_map/ppermute | solution.py:87
  192.1 2.0 collective-permute-start.43
  194.1 2.8 collective-permute-start.42
  199.1 17.2 %spmm_t.2 = (bf16[4096,128]{1,0:T(8,128)(2,1)}, bf16[4096,128]{1,0:T(8,128)(2,1)}, bf16[4096,128]{1,0:T(8,128)(2,1)}, bf16[4096,128]{1,0:T(8,128)(2,1)}, bf16[40...) custom-call(s32[32,16]{1,0:T(8,128)} %copy.71.cols, s32[32]{0:T(128)} %counts.9, s32[9]{0:T(128)} %stack.84.meta, ...), custom_call_target="tpu_custom_call" | custom-call | flops 2147483648 | bytes 25165824 | tf_op jit(solution)/shard_map/spmm_t/pallas_call | solution.py:241
  216.4 2.9 collective-permute-done.45.got_far
  221.7 3.4 collective-permute-done.46.got_up.got_down.got
  225.1 1.7 copy-done.2
  226.8 4.4 %halves_sums.1 = (bf16[4096,128]{1,0:T(8,128)(2,1)}, bf16[4096,128]{1,0:T(8,128)(2,1)}) custom-call(bf16[4096,128]{1,0:T(8,128)(2,1)} %get-tuple-element.307.own_far, bf16[4096,128]{1,0:T(8,128)(2,1)} %copy-done.20, bf16[4096,128]{1,0:T(8,128)(2,1)} %get-tuple-element.309.own_up, bf16[12288,128]{1,0:T(8,128)(2,1)} %copy-done.2, ...), custom_call_target="tpu_custom_call" | custom-call | flops 1048576 | bytes 6291456 | tf_op jit(solution)/shard_map/halves_sums/pallas_call | solution.py:465
  231.3 17.3 %spmm_t.3 = (bf16[4096,128]{1,0:T(8,128)(2,1)}, bf16[4096,128]{1,0:T(8,128)(2,1)}, bf16[4096,128]{1,0:T(8,128)(2,1)}, bf16[4096,128]{1,0:T(8,128)(2,1)}, bf16[40...) custom-call(s32[32,16]{1,0:T(8,128)} %copy.71.cols, s32[32]{0:T(128)} %counts.9, s32[9]{0:T(128)} %stack.84.meta, ...), custom_call_target="tpu_custom_call" | custom-call | flops 2147483648 | bytes 25165824 | tf_op jit(solution)/shard_map/spmm_t/pallas_call | solution.py:241
  248.9 2.9 collective-permute-done.49
  254.9 1.9 add_convert_fusion.2
  256.9 23.1 %collective-permute-done.53 = bf16[1024,256]{1,0:T(8,128)(2,1)} collective-permute-done((bf16[1024,256]{1,0:T(8,128)(2,1)}, bf16[1024,256]{1,0:T(8,128)(2,1)}, u32[]{:S(2)}, u32[]{:S(2)}) %collective-permute-start.53) | collective-permute-done | bytes 524320 | tf_op jit(solution)/shard_map/ppermute | solution.py:87
  282.1 2.7 add_convert_fusion
  287.9 7.1 %collective-permute-done.54.up = bf16[2048,128]{1,0:T(8,128)(2,1)S(1)} collective-permute-done((bf16[2048,128]{1,0:T(8,128)(2,1)S(1)}, bf16[2048,128]{1,0:T(8,128)(2,1)S(1)}, u32[]{:S(2)}, u32[]{:S(2)}) %collective-permute-start.54) | collective-permute-done | bytes 524320 | tf_op jit(solution)/shard_map/ppermute | solution.py:38
  295.9 4.9 %step_sums.1 = (bf16[4096,128]{1,0:T(8,128)(2,1)}, bf16[4096,128]{1,0:T(8,128)(2,1)}) custom-call(bf16[4096,128]{1,0:T(8,128)(2,1)} %get-tuple-element.326.own_up, bf16[12288,128]{1,0:T(8,128)(2,1)} %copy-done.3, bf16[2048,128]{1,0:T(8,128)(2,1)} %copy-done.28, bf16[4096,128]{1,0:T(8,128)(2,1)} %get-tuple-element.345.own_down, bf16[12288,128]{1,0:T(8,128)(2,1)} %copy-done.3, ...), custom_call_target="tpu_custom_call" | custom-call | flops 2097152 | bytes 7340032 | tf_op jit(solution)/shard_map/step_sums/pallas_call | solution.py:390
  302.9 2.2 collective-permute-start.63
  307.8 6.0 %collective-permute-done.64 = bf16[128,256]{1,0:T(8,128)(2,1)S(1)} collective-permute-done((bf16[128,256]{1,0:T(8,128)(2,1)S(1)}, bf16[128,256]{1,0:T(8,128)(2,1)S(1)}, u32[]{:S(2)}, u32[]{:S(2)}) %collective-permute-start.64) | collective-permute-done | bytes 65568 | tf_op jit(solution)/shard_map/ppermute | solution.py:87
  313.8 8.8 %collective-permute-start.56 = (bf16[1024,256]{1,0:T(8,128)(2,1)}, bf16[1024,256]{1,0:T(8,128)(2,1)}, u32[]{:S(2)}, u32[]{:S(2)}) collective-permute-start(bf16[1024,256]{1,0:T(8,128)(2,1)} %get-tuple-element.350), channel_id=1, source_target_pairs={{0,3},{1,0},{2,1},{3,2},{4,7},{5,4},{6,5},{7,6},{8,11},{9,8},{10,9... | collective-permute-start | bytes 1572872 | tf_op jit(solution)/shard_map/ppermute | solution.py:87
  323.6 11.2 %collective-permute-done.59.down_high = bf16[2048,128]{1,0:T(8,128)(2,1)} collective-permute-done((bf16[2048,128]{1,0:T(8,128)(2,1)}, bf16[2048,128]{1,0:T(8,128)(2,1)}, u32[]{:S(2)}, u32[]{:S(2)}) %collective-permute-start.59) | collective-permute-done | bytes 524320 | tf_op jit(solution)/shard_map/ppermute | solution.py:38
  334.8 4.3 %joined.1.refs_0_ = bf16[4096,128]{1,0:T(8,128)(2,1)} custom-call(bf16[4096,128]{1,0:T(8,128)(2,1)} %get-tuple-element.353.own, bf16[12288,128]{1,0:T(8,128)(2,1)} %copy-done.2, bf16[2048,128]{1,0:T(8,128)(2,1)} %copy-done.24, bf16[4096,128]{1,0:T(8,128)(2,1)} %collective-permute-done.51.up_high, bf16[4096,128]{1,0:T(8,128)(2,1)} %collective-permute-done.52.down_low, ...), custom_call_target="tpu_custom_call" | custom-call | flops 1572864 | bytes 5242880 | tf_op jit(solution)/shard_map/joined/pallas_call | solution.py:509
  344.8 4.6 %feature_grad.1 = bf16[4096,256]{1,0:T(8,128)(2,1)} custom-call(bf16[4096,128]{1,0:T(8,128)(2,1)} %joined.1.refs_0_, bf16[4096,128]{1,0:T(8,128)(2,1)} %get-tuple-element.356.refs_1_, bf16[12288,128]{1,0:T(8,128)(2,1)} %copy-done.3, bf16[4096,128]{1,0:T(8,128)(2,1)} %copy-done.18, bf16[4096,128]{1,0:T(8,128)(2,1)} %copy-done.19), custom_call_target="tpu_custom_call" | custom-call | flops 2097152 | bytes 7340032 | tf_op jit(solution)/shard_map/feature_grad/pallas_call | solution.py:426
  (246 shorter events, 62.7 us)
Async XLA Ops:
  7.2 139.5 %all-gather.2.cloned.1.call-start = ((), (), s32[]{:S(2)}) async-start(), calls=%async_computation | async-start | bytes 2359296 | tf_op jit(solution)/shard_map/all_gather | solution.py:670
  7.2 48.8 %collective-permute-start.6 = (bf16[4096,256]{1,0:T(8,128)(2,1)}, bf16[4096,256]{1,0:T(8,128)(2,1)}, u32[]{:S(2)}, u32[]{:S(2)}) collective-permute-start(bf16[4096,256]{1,0:T(8,128)(2,1)} %param.58), channel_id=1, source_target_pairs={{0,4},{4,0},{8,12},{12,8},{16,20},{20,16},{24,28},{28,24},{1,5},{5... | collective-permute-start | bytes 6291464 | tf_op jit(solution)/shard_map/ppermute | solution.py:41
  9.4 26.5 %collective-permute-start = (bf16[4096,128]{1,0:T(8,128)(2,1)S(1)}, bf16[4096,128]{1,0:T(8,128)(2,1)}, u32[]{:S(2)}, u32[]{:S(2)}) collective-permute-start(bf16[4096,128]{1,0:T(8,128)(2,1)S(1)} %get-tuple-element.385.refs_0_), channel_id=1, source_target_pairs={{0,8},{4,12},{8,24},{12,28},{24,16},{28,20},{16,0},{20,4},{1,9},{5... | collective-permute-start | bytes 3145736 | tf_op jit(solution)/shard_map/ppermute | solution.py:38
  12.0 25.4 %collective-permute-start.1 = (bf16[4096,128]{1,0:T(8,128)(2,1)S(1)}, bf16[4096,128]{1,0:T(8,128)(2,1)}, u32[]{:S(2)}, u32[]{:S(2)}) collective-permute-start(bf16[4096,128]{1,0:T(8,128)(2,1)S(1)} %get-tuple-element.385.refs_0_), channel_id=1, source_target_pairs={{0,16},{4,20},{8,0},{12,4},{24,8},{28,12},{16,24},{20,28},{1,17},{... | collective-permute-start | bytes 3145736 | tf_op jit(solution)/shard_map/ppermute | solution.py:38
  15.0 25.8 %collective-permute-start.4 = (bf16[1024,256]{1,0:T(8,128)(2,1)}, bf16[1024,256]{1,0:T(8,128)(2,1)S(1)}, u32[]{:S(2)}, u32[]{:S(2)}) collective-permute-start(bf16[1024,256]{1,0:T(8,128)(2,1)} %get-tuple-element.379), channel_id=1, source_target_pairs={{0,3},{1,0},{2,1},{3,2},{4,7},{5,4},{6,5},{7,6},{8,11},{9,8},{10,9... | collective-permute-start | bytes 1572872 | tf_op jit(solution)/shard_map/ppermute | solution.py:87
  19.1 23.7 %collective-permute-start.5 = (bf16[1024,256]{1,0:T(8,128)(2,1)}, bf16[1024,256]{1,0:T(8,128)(2,1)}, u32[]{:S(2)}, u32[]{:S(2)}) collective-permute-start(bf16[1024,256]{1,0:T(8,128)(2,1)} %get-tuple-element.381), channel_id=1, source_target_pairs={{0,1},{1,2},{2,3},{3,0},{4,5},{5,6},{6,7},{7,4},{8,9},{9,10},{10,1... | collective-permute-start | bytes 1572872 | tf_op jit(solution)/shard_map/ppermute | solution.py:87
  37.4 22.1 %collective-permute-start.13 = (bf16[4096,128]{1,0:T(8,128)(2,1)}, bf16[4096,128]{1,0:T(8,128)(2,1)}, u32[]{:S(2)}, u32[]{:S(2)}) collective-permute-start(bf16[4096,128]{1,0:T(8,128)(2,1)} %collective-permute-done.refs_1_), channel_id=1, source_target_pairs={{0,4},{4,0},{8,12},{12,8},{16,20},{20,16},{24,28},{28,24},{1,5},{5... | collective-permute-start | bytes 3145736 | tf_op jit(solution)/shard_map/ppermute | solution.py:41
  37.4 22.9 %collective-permute-start.14 = (bf16[4096,128]{1,0:T(8,128)(2,1)}, bf16[4096,128]{1,0:T(8,128)(2,1)}, u32[]{:S(2)}, u32[]{:S(2)}) collective-permute-start(bf16[4096,128]{1,0:T(8,128)(2,1)} %collective-permute-done.1.refs_2_), channel_id=1, source_target_pairs={{0,4},{4,0},{8,12},{12,8},{16,20},{20,16},{24,28},{28,24},{1,5},{5... | collective-permute-start | bytes 3145736 | tf_op jit(solution)/shard_map/ppermute | solution.py:41
  40.9 14.2 %collective-permute-start.2 = (bf16[2048,128]{1,0:T(8,128)(2,1)}, bf16[2048,128]{1,0:T(8,128)(2,1)}, u32[]{:S(2)}, u32[]{:S(2)}) collective-permute-start(bf16[2048,128]{1,0:T(8,128)(2,1)} %slice.80), channel_id=1, source_target_pairs={{0,8},{4,12},{8,24},{12,28},{24,16},{28,20},{16,0},{20,4},{1,9},{5... | collective-permute-start | bytes 1572872 | tf_op jit(solution)/shard_map/ppermute | solution.py:38
  42.8 13.2 %collective-permute-start.3 = (bf16[2048,128]{1,0:T(8,128)(2,1)S(1)}, bf16[2048,128]{1,0:T(8,128)(2,1)S(1)}, u32[]{:S(2)}, u32[]{:S(2)}) collective-permute-start(bf16[2048,128]{1,0:T(8,128)(2,1)S(1)} %slice.81), channel_id=1, source_target_pairs={{0,16},{4,20},{8,0},{12,4},{24,8},{28,12},{16,24},{20,28},{1,17},{... | collective-permute-start | bytes 1572872 | tf_op jit(solution)/shard_map/ppermute | solution.py:38
  58.3 32.9 %collective-permute-start.11 = (bf16[4096,128]{1,0:T(8,128)(2,1)S(1)}, bf16[4096,128]{1,0:T(8,128)(2,1)S(1)}, u32[]{:S(2)}, u32[]{:S(2)}) collective-permute-start(bf16[4096,128]{1,0:T(8,128)(2,1)S(1)} %get-tuple-element.188.refs_0_), channel_id=1, source_target_pairs={{0,8},{4,12},{8,24},{12,28},{24,16},{28,20},{16,0},{20,4},{1,9},{5... | collective-permute-start | bytes 3145736 | tf_op jit(solution)/shard_map/ppermute | solution.py:38
  59.5 31.7 %collective-permute-start.12 = (bf16[4096,128]{1,0:T(8,128)(2,1)S(1)}, bf16[4096,128]{1,0:T(8,128)(2,1)S(1)}, u32[]{:S(2)}, u32[]{:S(2)}) collective-permute-start(bf16[4096,128]{1,0:T(8,128)(2,1)S(1)} %get-tuple-element.188.refs_0_), channel_id=1, source_target_pairs={{0,16},{4,20},{8,0},{12,4},{24,8},{28,12},{16,24},{20,28},{1,17},{... | collective-permute-start | bytes 3145736 | tf_op jit(solution)/shard_map/ppermute | solution.py:38
  62.1 29.1 %collective-permute-start.7 = (bf16[1024,256]{1,0:T(8,128)(2,1)}, bf16[1024,256]{1,0:T(8,128)(2,1)S(1)}, u32[]{:S(2)}, u32[]{:S(2)}) collective-permute-start(bf16[1024,256]{1,0:T(8,128)(2,1)} %get-tuple-element.186), channel_id=1, source_target_pairs={{0,2},{1,3},{2,0},{3,1},{4,6},{5,7},{6,4},{7,5},{8,10},{9,11},{10,... | collective-permute-start | bytes 1572872 | tf_op jit(solution)/shard_map/ppermute | solution.py:87
  66.0 17.5 %collective-permute-start.8 = (bf16[128,256]{1,0:T(8,128)(2,1)S(1)}, bf16[128,256]{1,0:T(8,128)(2,1)S(1)}, u32[]{:S(2)}, u32[]{:S(2)}) collective-permute-start(bf16[128,256]{1,0:T(8,128)(2,1)S(1)} %constant_dynamic-slice_fusion.7), channel_id=1, source_target_pairs={{0,3},{1,0},{2,1},{3,2},{4,7},{5,4},{6,5},{7,6},{8,11},{9,8},{10,9... | collective-permute-start | bytes 196616 | tf_op jit(solution)/shard_map/ppermute | solution.py:87
  67.4 23.8 %collective-permute-start.9 = (bf16[128,256]{1,0:T(8,128)(2,1)S(1)}, bf16[128,256]{1,0:T(8,128)(2,1)S(1)}, u32[]{:S(2)}, u32[]{:S(2)}) collective-permute-start(bf16[128,256]{1,0:T(8,128)(2,1)S(1)} %constant_dynamic-slice_fusion.7), channel_id=1, source_target_pairs={{0,2},{1,3},{2,0},{3,1},{4,6},{5,7},{6,4},{7,5},{8,10},{9,11},{10,... | collective-permute-start | bytes 196616 | tf_op jit(solution)/shard_map/ppermute | solution.py:87
  94.6 14.0 %collective-permute-start.17 = (bf16[2048,128]{1,0:T(8,128)(2,1)}, bf16[2048,128]{1,0:T(8,128)(2,1)S(1)}, u32[]{:S(2)}, u32[]{:S(2)}) collective-permute-start(bf16[2048,128]{1,0:T(8,128)(2,1)} %slice.84), channel_id=1, source_target_pairs={{0,8},{4,12},{8,24},{12,28},{24,16},{28,20},{16,0},{20,4},{1,9},{5... | collective-permute-start | bytes 1572872 | tf_op jit(solution)/shard_map/ppermute | solution.py:38
  95.8 13.8 %collective-permute-start.18 = (bf16[2048,128]{1,0:T(8,128)(2,1)}, bf16[2048,128]{1,0:T(8,128)(2,1)S(1)}, u32[]{:S(2)}, u32[]{:S(2)}) collective-permute-start(bf16[2048,128]{1,0:T(8,128)(2,1)} %slice.85), channel_id=1, source_target_pairs={{0,16},{4,20},{8,0},{12,4},{24,8},{28,12},{16,24},{20,28},{1,17},{... | collective-permute-start | bytes 1572872 | tf_op jit(solution)/shard_map/ppermute | solution.py:38
  97.7 11.9 %collective-permute-start.22 = (bf16[1024,128]{1,0:T(8,128)(2,1)}, bf16[1024,128]{1,0:T(8,128)(2,1)S(1)}, u32[]{:S(2)}, u32[]{:S(2)}) collective-permute-start(bf16[1024,128]{1,0:T(8,128)(2,1)} %get-tuple-element.201), channel_id=1, source_target_pairs={{0,1},{1,2},{2,3},{3,0},{4,5},{5,6},{6,7},{7,4},{8,9},{9,10},{10,1... | collective-permute-start | bytes 786440 | tf_op jit(solution)/shard_map/ppermute | solution.py:87
  97.7 14.2 %collective-permute-start.21 = (bf16[1024,128]{1,0:T(8,128)(2,1)}, bf16[1024,128]{1,0:T(8,128)(2,1)}, u32[]{:S(2)}, u32[]{:S(2)}) collective-permute-start(bf16[1024,128]{1,0:T(8,128)(2,1)} %get-tuple-element.199), channel_id=1, source_target_pairs={{0,3},{1,0},{2,1},{3,2},{4,7},{5,4},{6,5},{7,6},{8,11},{9,8},{10,9... | collective-permute-start | bytes 786440 | tf_op jit(solution)/shard_map/ppermute | solution.py:87
  112.5 15.0 %collective-permute-start.23 = (bf16[1024,128]{1,0:T(8,128)(2,1)}, bf16[1024,128]{1,0:T(8,128)(2,1)S(1)}, u32[]{:S(2)}, u32[]{:S(2)}) collective-permute-start(bf16[1024,128]{1,0:T(8,128)(2,1)} %get-tuple-element.203), channel_id=1, source_target_pairs={{0,2},{1,3},{2,0},{3,1},{4,6},{5,7},{6,4},{7,5},{8,10},{9,11},{10,... | collective-permute-start | bytes 786440 | tf_op jit(solution)/shard_map/ppermute | solution.py:87
  128.2 14.7 %collective-permute-start.26 = (bf16[512,128]{1,0:T(8,128)(2,1)}, bf16[512,128]{1,0:T(8,128)(2,1)S(1)}, u32[]{:S(2)}, u32[]{:S(2)}) collective-permute-start(bf16[512,128]{1,0:T(8,128)(2,1)} %get-tuple-element.209), channel_id=1, source_target_pairs={{0,3},{1,0},{2,1},{3,2},{4,7},{5,4},{6,5},{7,6},{8,11},{9,8},{10,9... | collective-permute-start | bytes 393224 | tf_op jit(solution)/shard_map/ppermute | solution.py:87
  130.4 12.5 %collective-permute-start.27 = (bf16[512,128]{1,0:T(8,128)(2,1)}, bf16[512,128]{1,0:T(8,128)(2,1)S(1)}, u32[]{:S(2)}, u32[]{:S(2)}) collective-permute-start(bf16[512,128]{1,0:T(8,128)(2,1)} %get-tuple-element.210), channel_id=1, source_target_pairs={{0,2},{1,3},{2,0},{3,1},{4,6},{5,7},{6,4},{7,5},{8,10},{9,11},{10,... | collective-permute-start | bytes 393224 | tf_op jit(solution)/shard_map/ppermute | solution.py:87
  130.4 12.5 %collective-permute-start.28 = (bf16[512,128]{1,0:T(8,128)(2,1)}, bf16[512,128]{1,0:T(8,128)(2,1)S(1)}, u32[]{:S(2)}, u32[]{:S(2)}) collective-permute-start(bf16[512,128]{1,0:T(8,128)(2,1)} %get-tuple-element.211), channel_id=1, source_target_pairs={{0,1},{1,2},{2,3},{3,0},{4,5},{5,6},{6,7},{7,4},{8,9},{9,10},{10,1... | collective-permute-start | bytes 393224 | tf_op jit(solution)/shard_map/ppermute | solution.py:87
  145.4 12.4 %collective-permute-start.30 = (bf16[512,128]{1,0:T(8,128)(2,1)}, bf16[512,128]{1,0:T(8,128)(2,1)S(1)}, u32[]{:S(2)}, u32[]{:S(2)}) collective-permute-start(bf16[512,128]{1,0:T(8,128)(2,1)} %get-tuple-element.217), channel_id=1, source_target_pairs={{0,2},{1,3},{2,0},{3,1},{4,6},{5,7},{6,4},{7,5},{8,10},{9,11},{10,... | collective-permute-start | bytes 393224 | tf_op jit(solution)/shard_map/ppermute | solution.py:87
  157.8 13.9 %collective-permute-start.33 = (bf16[512,128]{1,0:T(8,128)(2,1)}, bf16[512,128]{1,0:T(8,128)(2,1)S(1)}, u32[]{:S(2)}, u32[]{:S(2)}) collective-permute-start(bf16[512,128]{1,0:T(8,128)(2,1)} %get-tuple-element.240), channel_id=1, source_target_pairs={{0,2},{1,3},{2,0},{3,1},{4,6},{5,7},{6,4},{7,5},{8,10},{9,11},{10,... | collective-permute-start | bytes 393224 | tf_op jit(solution)/shard_map/ppermute | solution.py:87
  159.5 12.3 %collective-permute-start.34 = (bf16[512,128]{1,0:T(8,128)(2,1)}, bf16[512,128]{1,0:T(8,128)(2,1)S(1)}, u32[]{:S(2)}, u32[]{:S(2)}) collective-permute-start(bf16[512,128]{1,0:T(8,128)(2,1)} %get-tuple-element.241), channel_id=1, source_target_pairs={{0,1},{1,2},{2,3},{3,0},{4,5},{5,6},{6,7},{7,4},{8,9},{9,10},{10,1... | collective-permute-start | bytes 393224 | tf_op jit(solution)/shard_map/ppermute | solution.py:87
  178.4 13.3 %collective-permute-start.39 = (bf16[384,1024]{1,0:T(8,128)(2,1)S(1)}, bf16[384,1024]{1,0:T(8,128)(2,1)S(1)}, u32[]{:S(2)}, u32[]{:S(2)}) collective-permute-start(bf16[384,1024]{1,0:T(8,128)(2,1)S(1)} %pad_maximum_fusion), channel_id=1, source_target_pairs={{0,4},{4,0},{8,12},{12,8},{16,20},{20,16},{24,28},{28,24},{1,5},{5... | collective-permute-start | bytes 2359304 | tf_op jit(solution)/shard_map/ppermute | solution.py:41
  178.5 13.2 %collective-permute-start.36 = (bf16[512,128]{1,0:T(8,128)(2,1)S(1)}, bf16[512,128]{1,0:T(8,128)(2,1)S(1)}, u32[]{:S(2)}, u32[]{:S(2)}) collective-permute-start(bf16[512,128]{1,0:T(8,128)(2,1)S(1)} %copy-done.58), channel_id=1, source_target_pairs={{0,2},{1,3},{2,0},{3,1},{4,6},{5,7},{6,4},{7,5},{8,10},{9,11},{10,... | collective-permute-start | bytes 393224 | tf_op jit(solution)/shard_map/ppermute | solution.py:87
  179.4 12.4 %collective-permute-start.37 = (bf16[512,128]{1,0:T(8,128)(2,1)S(1)}, bf16[512,128]{1,0:T(8,128)(2,1)S(1)}, u32[]{:S(2)}, u32[]{:S(2)}) collective-permute-start(bf16[512,128]{1,0:T(8,128)(2,1)S(1)} %copy-done.57), channel_id=1, source_target_pairs={{0,1},{1,2},{2,3},{3,0},{4,5},{5,6},{6,7},{7,4},{8,9},{9,10},{10,1... | collective-permute-start | bytes 393224 | tf_op jit(solution)/shard_map/ppermute | solution.py:87
  191.8 24.5 %collective-permute-start.44 = (bf16[1024,128]{1,0:T(8,128)(2,1)S(1)}, bf16[1024,128]{1,0:T(8,128)(2,1)S(1)}, u32[]{:S(2)}, u32[]{:S(2)}) collective-permute-start(bf16[1024,128]{1,0:T(8,128)(2,1)S(1)} %copy-done.37), channel_id=1, source_target_pairs={{0,1},{1,2},{2,3},{3,0},{4,5},{5,6},{6,7},{7,4},{8,9},{9,10},{10,1... | collective-permute-start | bytes 786440 | tf_op jit(solution)/shard_map/ppermute | solution.py:87
  192.1 24.2 %collective-permute-start.43 = (bf16[1024,128]{1,0:T(8,128)(2,1)S(1)}, bf16[1024,128]{1,0:T(8,128)(2,1)S(1)}, u32[]{:S(2)}, u32[]{:S(2)}) collective-permute-start(bf16[1024,128]{1,0:T(8,128)(2,1)S(1)} %copy-done.38), channel_id=1, source_target_pairs={{0,2},{1,3},{2,0},{3,1},{4,6},{5,7},{6,4},{7,5},{8,10},{9,11},{10,... | collective-permute-start | bytes 786440 | tf_op jit(solution)/shard_map/ppermute | solution.py:87
  194.1 22.2 %collective-permute-start.42 = (bf16[1024,128]{1,0:T(8,128)(2,1)S(1)}, bf16[1024,128]{1,0:T(8,128)(2,1)S(1)}, u32[]{:S(2)}, u32[]{:S(2)}) collective-permute-start(bf16[1024,128]{1,0:T(8,128)(2,1)S(1)} %copy-done.39), channel_id=1, source_target_pairs={{0,3},{1,0},{2,1},{3,2},{4,7},{5,4},{6,5},{7,6},{8,11},{9,8},{10,9... | collective-permute-start | bytes 786440 | tf_op jit(solution)/shard_map/ppermute | solution.py:87
  197.0 19.3 %collective-permute-start.40 = (bf16[64,1024]{1,0:T(8,128)(2,1)S(1)}, bf16[64,1024]{1,0:T(8,128)(2,1)S(1)}, u32[]{:S(2)}, u32[]{:S(2)}) collective-permute-start(bf16[64,1024]{1,0:T(8,128)(2,1)S(1)} %get-tuple-element.389), channel_id=1, source_target_pairs={{0,8},{4,12},{8,24},{12,28},{24,16},{28,20},{16,0},{20,4},{1,9},{5... | collective-permute-start | bytes 393224 | tf_op jit(solution)/shard_map/ppermute | solution.py:38
  198.3 18.0 %collective-permute-start.41 = (bf16[64,1024]{1,0:T(8,128)(2,1)S(1)}, bf16[64,1024]{1,0:T(8,128)(2,1)S(1)}, u32[]{:S(2)}, u32[]{:S(2)}) collective-permute-start(bf16[64,1024]{1,0:T(8,128)(2,1)S(1)} %get-tuple-element.388), channel_id=1, source_target_pairs={{0,16},{4,20},{8,0},{12,4},{24,8},{28,12},{16,24},{20,28},{1,17},{... | collective-permute-start | bytes 393224 | tf_op jit(solution)/shard_map/ppermute | solution.py:38
  219.6 11.7 %collective-permute-start.47 = (bf16[128,1024]{1,0:T(8,128)(2,1)S(1)}, bf16[128,1024]{1,0:T(8,128)(2,1)S(1)}, u32[]{:S(2)}, u32[]{:S(2)}) collective-permute-start(bf16[128,1024]{1,0:T(8,128)(2,1)S(1)} %get-tuple-element.387), channel_id=1, source_target_pairs={{0,8},{4,12},{8,24},{12,28},{24,16},{28,20},{16,0},{20,4},{1,9},{5... | collective-permute-start | bytes 786440 | tf_op jit(solution)/shard_map/ppermute | solution.py:38
  251.8 28.3 %collective-permute-start.50 = (bf16[12288,128]{1,0:T(8,128)(2,1)}, bf16[12288,128]{1,0:T(8,128)(2,1)S(1)}, u32[]{:S(2)}, u32[]{:S(2)}) collective-permute-start(bf16[12288,128]{1,0:T(8,128)(2,1)} %get-tuple-element.329), channel_id=1, source_target_pairs={{0,4},{4,0},{8,12},{12,8},{16,20},{20,16},{24,28},{28,24},{1,5},{5... | collective-permute-start | bytes 9437192 | tf_op jit(solution)/shard_map/ppermute | solution.py:41
  251.9 28.1 %collective-permute-start.51 = (bf16[4096,128]{1,0:T(8,128)(2,1)}, bf16[4096,128]{1,0:T(8,128)(2,1)}, u32[]{:S(2)}, u32[]{:S(2)}) collective-permute-start(bf16[4096,128]{1,0:T(8,128)(2,1)} %get-tuple-element.331), channel_id=1, source_target_pairs={{0,8},{4,12},{8,24},{12,28},{24,16},{28,20},{16,0},{20,4},{1,9},{5... | collective-permute-start | bytes 3145736 | tf_op jit(solution)/shard_map/ppermute | solution.py:38
  253.1 26.9 %collective-permute-start.52 = (bf16[4096,128]{1,0:T(8,128)(2,1)}, bf16[4096,128]{1,0:T(8,128)(2,1)}, u32[]{:S(2)}, u32[]{:S(2)}) collective-permute-start(bf16[4096,128]{1,0:T(8,128)(2,1)} %get-tuple-element.332), channel_id=1, source_target_pairs={{0,16},{4,20},{8,0},{12,4},{24,8},{28,12},{16,24},{20,28},{1,17},{... | collective-permute-start | bytes 3145736 | tf_op jit(solution)/shard_map/ppermute | solution.py:38
  253.9 26.1 %collective-permute-start.53 = (bf16[1024,256]{1,0:T(8,128)(2,1)}, bf16[1024,256]{1,0:T(8,128)(2,1)}, u32[]{:S(2)}, u32[]{:S(2)}) collective-permute-start(bf16[1024,256]{1,0:T(8,128)(2,1)} %get-tuple-element.333), channel_id=1, source_target_pairs={{0,2},{1,3},{2,0},{3,1},{4,6},{5,7},{6,4},{7,5},{8,10},{9,11},{10,... | collective-permute-start | bytes 1572872 | tf_op jit(solution)/shard_map/ppermute | solution.py:87
  280.1 14.9 %collective-permute-start.54 = (bf16[2048,128]{1,0:T(8,128)(2,1)S(1)}, bf16[2048,128]{1,0:T(8,128)(2,1)S(1)}, u32[]{:S(2)}, u32[]{:S(2)}) collective-permute-start(bf16[2048,128]{1,0:T(8,128)(2,1)S(1)} %get-tuple-element.344), channel_id=1, source_target_pairs={{0,8},{4,12},{8,24},{12,28},{24,16},{28,20},{16,0},{20,4},{1,9},{5... | collective-permute-start | bytes 1572872 | tf_op jit(solution)/shard_map/ppermute | solution.py:38
  281.3 13.6 %collective-permute-start.55 = (bf16[2048,128]{1,0:T(8,128)(2,1)S(1)}, bf16[2048,128]{1,0:T(8,128)(2,1)S(1)}, u32[]{:S(2)}, u32[]{:S(2)}) collective-permute-start(bf16[2048,128]{1,0:T(8,128)(2,1)S(1)} %get-tuple-element.346), channel_id=1, source_target_pairs={{0,16},{4,20},{8,0},{12,4},{24,8},{28,12},{16,24},{20,28},{1,17},{... | collective-permute-start | bytes 1572872 | tf_op jit(solution)/shard_map/ppermute | solution.py:38
  284.9 37.8 %collective-permute-start.58 = (bf16[2048,128]{1,0:T(8,128)(2,1)S(1)}, bf16[2048,128]{1,0:T(8,128)(2,1)S(1)}, u32[]{:S(2)}, u32[]{:S(2)}) collective-permute-start(bf16[2048,128]{1,0:T(8,128)(2,1)S(1)} %get-tuple-element.367), channel_id=1, source_target_pairs={{0,8},{4,12},{8,24},{12,28},{24,16},{28,20},{16,0},{20,4},{1,9},{5... | collective-permute-start | bytes 1572872 | tf_op jit(solution)/shard_map/ppermute | solution.py:38
  287.3 17.8 %collective-permute-start.62 = (bf16[128,256]{1,0:T(8,128)(2,1)S(1)}, bf16[128,256]{1,0:T(8,128)(2,1)S(1)}, u32[]{:S(2)}, u32[]{:S(2)}) collective-permute-start(bf16[128,256]{1,0:T(8,128)(2,1)S(1)} %get-tuple-element.360), channel_id=1, source_target_pairs={{0,1},{1,2},{2,3},{3,0},{4,5},{5,6},{6,7},{7,4},{8,9},{9,10},{10,1... | collective-permute-start | bytes 196616 | tf_op jit(solution)/shard_map/ppermute | solution.py:87
  300.8 42.6 %collective-permute-start.60 = (bf16[4096,128]{1,0:T(8,128)(2,1)}, bf16[4096,128]{1,0:T(8,128)(2,1)S(1)}, u32[]{:S(2)}, u32[]{:S(2)}) collective-permute-start(bf16[4096,128]{1,0:T(8,128)(2,1)} %get-tuple-element.357), channel_id=1, source_target_pairs={{0,8},{4,12},{8,24},{12,28},{24,16},{28,20},{16,0},{20,4},{1,9},{5... | collective-permute-start | bytes 3145736 | tf_op jit(solution)/shard_map/ppermute | solution.py:38
  302.1 41.4 %collective-permute-start.61 = (bf16[4096,128]{1,0:T(8,128)(2,1)}, bf16[4096,128]{1,0:T(8,128)(2,1)S(1)}, u32[]{:S(2)}, u32[]{:S(2)}) collective-permute-start(bf16[4096,128]{1,0:T(8,128)(2,1)} %get-tuple-element.358), channel_id=1, source_target_pairs={{0,16},{4,20},{8,0},{12,4},{24,8},{28,12},{16,24},{20,28},{1,17},{... | collective-permute-start | bytes 3145736 | tf_op jit(solution)/shard_map/ppermute | solution.py:38
  305.0 29.7 %collective-permute-start.59 = (bf16[2048,128]{1,0:T(8,128)(2,1)}, bf16[2048,128]{1,0:T(8,128)(2,1)}, u32[]{:S(2)}, u32[]{:S(2)}) collective-permute-start(bf16[2048,128]{1,0:T(8,128)(2,1)} %get-tuple-element.366), channel_id=1, source_target_pairs={{0,16},{4,20},{8,0},{12,4},{24,8},{28,12},{16,24},{20,28},{1,17},{... | collective-permute-start | bytes 1572872 | tf_op jit(solution)/shard_map/ppermute | solution.py:38
  313.8 26.3 %collective-permute-start.56 = (bf16[1024,256]{1,0:T(8,128)(2,1)}, bf16[1024,256]{1,0:T(8,128)(2,1)}, u32[]{:S(2)}, u32[]{:S(2)}) collective-permute-start(bf16[1024,256]{1,0:T(8,128)(2,1)} %get-tuple-element.350), channel_id=1, source_target_pairs={{0,3},{1,0},{2,1},{3,2},{4,7},{5,4},{6,5},{7,6},{8,11},{9,8},{10,9... | collective-permute-start | bytes 1572872 | tf_op jit(solution)/shard_map/ppermute | solution.py:87
  322.7 19.6 %collective-permute-start.57 = (bf16[1024,256]{1,0:T(8,128)(2,1)S(1)}, bf16[1024,256]{1,0:T(8,128)(2,1)}, u32[]{:S(2)}, u32[]{:S(2)}) collective-permute-start(bf16[1024,256]{1,0:T(8,128)(2,1)S(1)} %copy-done.26), channel_id=1, source_target_pairs={{0,1},{1,2},{2,3},{3,0},{4,5},{5,6},{6,7},{7,4},{8,9},{9,10},{10,1... | collective-permute-start | bytes 1572872 | tf_op jit(solution)/shard_map/ppermute | solution.py:87
  (78 other events, 733.7 us)
Sparse Core Ops, SparseCore 0:
  112.0 27.2 all-gather.1

commit v14 on v12

--- a/solution.py
+++ b/solution.py
@@ -705,7 +705,7 @@
         jnp.concatenate([sums_for(o, True) for o in near]),
     )
     wg_far = wg.far_swap()
-    w.go(wg_own=(wg.own_far, wg.own_near), wg_far=wg_far, wg_near=wg.near_swap(wg_far))
+    w.go(wg_own=(wg.own_far, wg.own_near), wg_far=wg_far, wg_near=ring.sibling(wg.other_near))
     w.close()
     wg.own_far, wg.own_near = w["wg_own"]
     w.go(wg_up_down=wg.hops(*wg.far_sums(w["wg_far"])))

time: 339 us -> 337 us (level)
  transfers between devices with their start and end apart: 66 -> 66, of which waited for: 26 -> 25; matrix products, arithmetic and copies ran while one was open for 7% -> 7% of each run, Pallas kernels for 28% -> 28%
where the time goes in v14:
time: 337 us; the launch traced here: 336 us
  waiting for transfers between devices  106 us (31%)
  Pallas kernels  103 us (31%)
  starting transfers between devices  65.2 us (19%)
  local copies, waits for them, and re-layouts  27.7 us (8%)
  between operations  22.6 us (7%)
  other arithmetic  6.23 us (2%)
  matrix products  4.7 us (1%)
    ppermute x30, waiting for transfers between devices, send(): lax.ppermute(blocks[s], 'rep', [(i, (i + s) % size) for i in range(size)])  53.5 us
    ppermute x20, waiting for transfers between devices, hop(): return lax.ppermute(value, 'row', self.perm(step))  43.7 us
    ppermute x30, starting transfers between devices, send(): lax.ppermute(blocks[s], 'rep', [(i, (i + s) % size) for i in range(size)])  40 us
    pallas_call x3, Pallas kernels, spmm(): pl.pallas_call(functools.partial(spmm_kernel, len(pieces), per_part, skip...  36.7 us
    pallas_call x2, Pallas kernels, spmm_t(): pl.pallas_call(functools.partial(spmm_t_kernel, len(grads), per_part, len...  34.5 us
    ppermute x20, starting transfers between devices, hop(): return lax.ppermute(value, 'row', self.perm(step))  22.1 us
    pallas_call x2, Pallas kernels, dense(): pl.pallas_call(functools.partial(dense_kernel, parts, chunks, len(earlier...  14.1 us
    unnamed x120, local copies, waits for them, and re-layouts  12.2 us
  transfers between devices with their start and end apart: 66, of which 25 were waited for; matrix products, arithmetic and copies ran while one was open for 7% of the time, Pallas kernels for 28%

profile of v14, /device:TPU:0, one launch (start us, length us, event | category | flops | bytes accessed | tf_op | source)
XLA Modules:
  0.0 335.6 jit_solution(16908377178522870356)
XLA Ops:
  7.7 1.7 fusion.1
  9.4 2.6 collective-permute-start
  12.1 2.9 constant_dynamic-slice_fusion.5
  15.0 4.0 %collective-permute-start.4 = (bf16[1024,256]{1,0:T(8,128)(2,1)}, bf16[1024,256]{1,0:T(8,128)(2,1)S(1)}, u32[]{:S(2)}, u32[]{:S(2)}) collective-permute-start(bf16[1024,256]{1,0:T(8,128)(2,1)} %get-tuple-element.399), channel_id=1, source_target_pairs={{0,3},{1,0},{2,1},{3,2},{4,7},{5,4},{6,5},{7,6},{8,11},{9,8},{10,9... | collective-permute-start | bytes 1572872 | tf_op jit(solution)/shard_map/ppermute | solution.py:87
  29.5 6.5 %collective-permute-done.refs_1_ = bf16[4096,128]{1,0:T(8,128)(2,1)} collective-permute-done((bf16[4096,128]{1,0:T(8,128)(2,1)S(1)}, bf16[4096,128]{1,0:T(8,128)(2,1)}, u32[]{:S(2)}, u32[]{:S(2)}) %collective-permute-start) | collective-permute-done | bytes 1048608 | tf_op jit(solution)/shard_map/ppermute | solution.py:38
  44.3 9.8 %collective-permute-done.2.refs_3_ = bf16[2048,128]{1,0:T(8,128)(2,1)} collective-permute-done((bf16[2048,128]{1,0:T(8,128)(2,1)S(1)}, bf16[2048,128]{1,0:T(8,128)(2,1)}, u32[]{:S(2)}, u32[]{:S(2)}) %collective-permute-start.2) | collective-permute-done | bytes 524320 | tf_op jit(solution)/shard_map/ppermute | solution.py:38
  54.1 1.7 collective-permute-done.3.refs_4_
  60.1 1.7 collective-permute-done.10
  62.3 3.0 fusion
  65.3 1.8 collective-permute-start.8
  68.3 14.5 %spmm.3 = (bf16[1024,128]{1,0:T(8,128)(2,1)}, bf16[1024,128]{1,0:T(8,128)(2,1)}, bf16[1024,128]{1,0:T(8,128)(2,1)}, bf16[1024,128]{1,0:T(8,128)(2,1)}) custom-call(s32[32,16]{1,0:T(8,128)} %copy.71.cols, s32[32]{0:T(128)} %counts.9, s32[11]{0:T(128)} %stack.75.meta, bf16[32,16,128,128]{3,2,1,0:T(8,128)(2,1)} %tiles.9, bf16[4096,128]{1,0:T(8,128)(2,1)} %copy-done.9, ...), custom_call_target="tpu_custom_call" | custom-call | flops 2147483648 | bytes 25165824 | tf_op jit(solution)/shard_map/spmm/pallas_call | solution.py:158
  82.8 8.3 %collective-permute-done.9 = bf16[128,256]{1,0:T(8,128)(2,1)S(1)} collective-permute-done((bf16[128,256]{1,0:T(8,128)(2,1)S(1)}, bf16[128,256]{1,0:T(8,128)(2,1)S(1)}, u32[]{:S(2)}, u32[]{:S(2)}) %collective-permute-start.9) | collective-permute-done | bytes 65568 | tf_op jit(solution)/shard_map/ppermute | solution.py:87
  97.5 3.8 %collective-permute-start.21 = (bf16[1024,128]{1,0:T(8,128)(2,1)}, bf16[1024,128]{1,0:T(8,128)(2,1)}, u32[]{:S(2)}, u32[]{:S(2)}) collective-permute-start(bf16[1024,128]{1,0:T(8,128)(2,1)} %get-tuple-element.209), channel_id=1, source_target_pairs={{0,3},{1,0},{2,1},{3,2},{4,7},{5,4},{6,5},{7,6},{8,11},{9,8},{10,9... | collective-permute-start | bytes 786440 | tf_op jit(solution)/shard_map/ppermute | solution.py:87
  102.1 6.4 %collective-permute-done.17.refs_3_ = bf16[2048,128]{1,0:T(8,128)(2,1)S(1)} collective-permute-done((bf16[2048,128]{1,0:T(8,128)(2,1)}, bf16[2048,128]{1,0:T(8,128)(2,1)S(1)}, u32[]{:S(2)}, u32[]{:S(2)}) %collective-permute-start.17) | collective-permute-done | bytes 524320 | tf_op jit(solution)/shard_map/ppermute | solution.py:38
  109.2 2.5 collective-permute-done.21.refs_2_
  112.3 2.4 collective-permute-start.23
  115.7 11.2 %spmm.4 = (bf16[512,128]{1,0:T(8,128)(2,1)}, bf16[512,128]{1,0:T(8,128)(2,1)}, bf16[512,128]{1,0:T(8,128)(2,1)}, bf16[512,128]{1,0:T(8,128)(2,1)}) custom-call(s32[32,16]{1,0:T(8,128)} %copy.71.cols, s32[32]{0:T(128)} %counts.9, s32[11]{0:T(128)} %stack.75.meta, bf16[32,16,128,128]{3,2,1,0:T(8,128)(2,1)} %tiles.9, bf16[4096,128]{1,0:T(8,128)(2,1)} %copy-done.4, ...), custom_call_target="tpu_custom_call" | custom-call | flops 1073741824 | bytes 16777216 | tf_op jit(solution)/shard_map/spmm/pallas_call | solution.py:158
  128.0 2.2 collective-permute-start.26
  131.6 11.0 %spmm.5 = (bf16[512,128]{1,0:T(8,128)(2,1)}, bf16[512,128]{1,0:T(8,128)(2,1)}, bf16[512,128]{1,0:T(8,128)(2,1)}, bf16[512,128]{1,0:T(8,128)(2,1)}) custom-call(s32[32,16]{1,0:T(8,128)} %copy.71.cols, s32[32]{0:T(128)} %counts.9, s32[11]{0:T(128)} %stack.75.meta, bf16[32,16,128,128]{3,2,1,0:T(8,128)(2,1)} %tiles.9, bf16[4096,128]{1,0:T(8,128)(2,1)} %copy-done.4, ...), custom_call_target="tpu_custom_call" | custom-call | flops 1073741824 | bytes 16777216 | tf_op jit(solution)/shard_map/spmm/pallas_call | solution.py:158
  142.8 2.5 collective-permute-start.29
  146.5 7.0 %dense.2 = (bf16[1024,256]{1,0:T(8,128)(2,1)}, bf16[1024,256]{1,0:T(8,128)(2,1)}, bf16[1024,256]{1,0:T(8,128)(2,1)}, bf16[1024,256]{1,0:T(8,128)(2,1)}, bf16[512...) custom-call(s32[1]{0:T(128)} %bitcast.meta, ...), custom_call_target="tpu_custom_call" | custom-call | flops 2147483648 | bytes 8388608 | tf_op jit(solution)/shard_map/dense/pallas_call | solution.py:325
  153.5 4.0 %collective-permute-done.30.refs_5_ = bf16[512,128]{1,0:T(8,128)(2,1)S(1)} collective-permute-done((bf16[512,128]{1,0:T(8,128)(2,1)}, bf16[512,128]{1,0:T(8,128)(2,1)S(1)}, u32[]{:S(2)}, u32[]{:S(2)}) %collective-permute-start.30) | collective-permute-done | bytes 131104 | tf_op jit(solution)/shard_map/ppermute | solution.py:87
  159.3 2.0 collective-permute-start.34
  161.3 7.1 %dense.3 = (bf16[1024,256]{1,0:T(8,128)(2,1)}, bf16[1024,256]{1,0:T(8,128)(2,1)}, bf16[1024,256]{1,0:T(8,128)(2,1)}, bf16[1024,256]{1,0:T(8,128)(2,1)}, bf16[512...) custom-call(s32[1]{0:T(128)} %bitcast.meta, ...), custom_call_target="tpu_custom_call", output_to_operand_aliasing={{0}: (14, {}), {1}: (15, {}), {2}: (16, {}), {3}: (17, {}),... | custom-call | flops 2147483648 | bytes 8388608 | tf_op jit(solution)/shard_map/dense/pallas_call | solution.py:325
  168.4 3.2 collective-permute-done.33.refs_4_
  171.6 4.7 %convolution_convert_fusion = bf16[1024,1024]{1,0:T(8,128)(2,1)S(1)} fusion(bf16[1024,1024]{1,0:T(8,128)(2,1)} %get-tuple-element.287, bf16[1024,1024]{1,0:T(8,128)(2,1)} %get-tuple-element.288), kind=kOutput, calls=%fused_computation | convolution fusion | flops 2148532224 | bytes 6291456 | tf_op jit(solution)/shard_map/dot_general | solution.py:694
  178.0 2.0 collective-permute-start.37
  180.0 4.0 %collective-permute-done.35.refs_3_ = bf16[512,128]{1,0:T(8,128)(2,1)S(1)} collective-permute-done((bf16[512,128]{1,0:T(8,128)(2,1)S(1)}, bf16[512,128]{1,0:T(8,128)(2,1)S(1)}, u32[]{:S(2)}, u32[]{:S(2)}) %collective-permute-start.35) | collective-permute-done | bytes 131104 | tf_op jit(solution)/shard_map/ppermute | solution.py:87
  184.0 6.1 %collective-permute-done.36.refs_5_ = bf16[512,128]{1,0:T(8,128)(2,1)S(1)} collective-permute-done((bf16[512,128]{1,0:T(8,128)(2,1)S(1)}, bf16[512,128]{1,0:T(8,128)(2,1)S(1)}, u32[]{:S(2)}, u32[]{:S(2)}) %collective-permute-start.36) | collective-permute-done | bytes 131104 | tf_op jit(solution)/shard_map/ppermute | solution.py:87
  190.5 2.0 collective-permute-start.43
  192.5 2.8 collective-permute-start.42
  197.5 17.2 %spmm_t.2 = (bf16[4096,128]{1,0:T(8,128)(2,1)}, bf16[4096,128]{1,0:T(8,128)(2,1)}, bf16[4096,128]{1,0:T(8,128)(2,1)}, bf16[4096,128]{1,0:T(8,128)(2,1)}, bf16[40...) custom-call(s32[32,16]{1,0:T(8,128)} %copy.71.cols, s32[32]{0:T(128)} %counts.9, s32[9]{0:T(128)} %stack.84.meta, ...), custom_call_target="tpu_custom_call" | custom-call | flops 2147483648 | bytes 25165824 | tf_op jit(solution)/shard_map/spmm_t/pallas_call | solution.py:241
  215.4 2.9 collective-permute-done.45.got_far
  220.7 3.5 %collective-permute-done.46.got_up.got_down.got = bf16[12288,128]{1,0:T(8,128)(2,1)S(1)} collective-permute-done((bf16[12288,128]{1,0:T(8,128)(2,1)}, bf16[12288,128]{1,0:T(8,128)(2,1)S(1)}, u32[]{:S(2)}, u32[]{:S(2)}) %collective-permute-start.46) | collective-permute-done | bytes 3145760 | tf_op jit(solution)/shard_map/ppermute | solution.py:41
  225.9 4.4 %halves_sums.1 = (bf16[4096,128]{1,0:T(8,128)(2,1)}, bf16[4096,128]{1,0:T(8,128)(2,1)}) custom-call(bf16[4096,128]{1,0:T(8,128)(2,1)} %get-tuple-element.319.own_far, bf16[4096,128]{1,0:T(8,128)(2,1)} %copy-done.23, bf16[4096,128]{1,0:T(8,128)(2,1)} %get-tuple-element.320.own_up, bf16[12288,128]{1,0:T(8,128)(2,1)} %copy-done.2, ...), custom_call_target="tpu_custom_call" | custom-call | flops 1048576 | bytes 6291456 | tf_op jit(solution)/shard_map/halves_sums/pallas_call | solution.py:465
  233.9 17.4 %spmm_t.3 = (bf16[4096,128]{1,0:T(8,128)(2,1)}, bf16[4096,128]{1,0:T(8,128)(2,1)}, bf16[4096,128]{1,0:T(8,128)(2,1)}, bf16[4096,128]{1,0:T(8,128)(2,1)}, bf16[40...) custom-call(s32[32,16]{1,0:T(8,128)} %copy.71.cols, s32[32]{0:T(128)} %counts.9, s32[9]{0:T(128)} %stack.84.meta, ...), custom_call_target="tpu_custom_call" | custom-call | flops 2147483648 | bytes 25165824 | tf_op jit(solution)/shard_map/spmm_t/pallas_call | solution.py:241
  251.3 7.4 %collective-permute-done.51 = bf16[1024,256]{1,0:T(8,128)(2,1)S(1)} collective-permute-done((bf16[1024,256]{1,0:T(8,128)(2,1)S(1)}, bf16[1024,256]{1,0:T(8,128)(2,1)S(1)}, u32[]{:S(2)}, u32[]{:S(2)}) %collective-permute-start.51) | collective-permute-done | bytes 524320 | tf_op jit(solution)/shard_map/ppermute | solution.py:87
  259.5 2.2 collective-permute-done.54
  261.8 2.6 add_convert_fusion.2
  271.1 1.9 collective-permute-start.56
  272.9 6.5 %collective-permute-done.52.up_low = bf16[2048,128]{1,0:T(8,128)(2,1)} collective-permute-done((bf16[2048,128]{1,0:T(8,128)(2,1)}, bf16[2048,128]{1,0:T(8,128)(2,1)}, u32[]{:S(2)}, u32[]{:S(2)}) %collective-permute-start.52) | collective-permute-done | bytes 524320 | tf_op jit(solution)/shard_map/ppermute | solution.py:38
  281.9 8.3 %collective-permute-done.59.up = bf16[2048,128]{1,0:T(8,128)(2,1)} collective-permute-done((bf16[2048,128]{1,0:T(8,128)(2,1)}, bf16[2048,128]{1,0:T(8,128)(2,1)}, u32[]{:S(2)}, u32[]{:S(2)}) %collective-permute-start.59) | collective-permute-done | bytes 524320 | tf_op jit(solution)/shard_map/ppermute | solution.py:38
  291.2 4.9 %step_sums.1 = (bf16[4096,128]{1,0:T(8,128)(2,1)}, bf16[4096,128]{1,0:T(8,128)(2,1)}) custom-call(bf16[4096,128]{1,0:T(8,128)(2,1)} %get-tuple-element.344.own_up, bf16[12288,128]{1,0:T(8,128)(2,1)} %copy-done.3, bf16[2048,128]{1,0:T(8,128)(2,1)} %collective-permute-done.59.up, bf16[4096,128]{1,0:T(8,128)(2,1)} %get-tuple-element.365.own_down, ...), custom_call_target="tpu_custom_call" | custom-call | flops 2097152 | bytes 7340032 | tf_op jit(solution)/shard_map/step_sums/pallas_call | solution.py:390
  298.1 1.8 collective-permute-start.61
  300.9 4.2 %joined.1.refs_0_ = bf16[4096,128]{1,0:T(8,128)(2,1)} custom-call(bf16[4096,128]{1,0:T(8,128)(2,1)} %get-tuple-element.373.own, bf16[12288,128]{1,0:T(8,128)(2,1)} %copy-done.2, bf16[2048,128]{1,0:T(8,128)(2,1)} %collective-permute-done.52.up_low, bf16[4096,128]{1,0:T(8,128)(2,1)} %copy-done.12, bf16[4096,128]{1,0:T(8,128)(2,1)} %copy-done.13, ...), custom_call_target="tpu_custom_call" | custom-call | flops 1572864 | bytes 5242880 | tf_op jit(solution)/shard_map/joined/pallas_call | solution.py:509
  306.2 6.7 %collective-permute-done.61 = bf16[1024,256]{1,0:T(8,128)(2,1)} collective-permute-done((bf16[1024,256]{1,0:T(8,128)(2,1)}, bf16[1024,256]{1,0:T(8,128)(2,1)}, u32[]{:S(2)}, u32[]{:S(2)}) %collective-permute-start.61) | collective-permute-done | bytes 524320 | tf_op jit(solution)/shard_map/ppermute | solution.py:87
  314.1 7.9 %collective-permute-done.62 = bf16[1024,256]{1,0:T(8,128)(2,1)S(1)} collective-permute-done((bf16[1024,256]{1,0:T(8,128)(2,1)}, bf16[1024,256]{1,0:T(8,128)(2,1)S(1)}, u32[]{:S(2)}, u32[]{:S(2)}) %collective-permute-start.62) | collective-permute-done | bytes 524320 | tf_op jit(solution)/shard_map/ppermute | solution.py:87
  324.1 4.6 %feature_grad.1 = bf16[4096,256]{1,0:T(8,128)(2,1)} custom-call(bf16[4096,128]{1,0:T(8,128)(2,1)} %joined.1.refs_0_, bf16[4096,128]{1,0:T(8,128)(2,1)} %get-tuple-element.376.refs_1_, bf16[12288,128]{1,0:T(8,128)(2,1)} %copy-done.3, bf16[4096,128]{1,0:T(8,128)(2,1)} %copy-done.20, bf16[4096,128]{1,0:T(8,128)(2,1)} %copy-done.21), custom_call_target="tpu_custom_call" | custom-call | flops 2097152 | bytes 7340032 | tf_op jit(solution)/shard_map/feature_grad/pallas_call | solution.py:426
  (244 shorter events, 63.4 us)
Async XLA Ops:
  7.2 139.3 %all-gather.2.cloned.1.call-start = ((), (), s32[]{:S(2)}) async-start(), calls=%async_computation | async-start | bytes 2359296 | tf_op jit(solution)/shard_map/all_gather | solution.py:670
  7.2 48.5 %collective-permute-start.6 = (bf16[4096,256]{1,0:T(8,128)(2,1)}, bf16[4096,256]{1,0:T(8,128)(2,1)}, u32[]{:S(2)}, u32[]{:S(2)}) collective-permute-start(bf16[4096,256]{1,0:T(8,128)(2,1)} %param.58), channel_id=1, source_target_pairs={{0,4},{4,0},{8,12},{12,8},{16,20},{20,16},{24,28},{28,24},{1,5},{5... | collective-permute-start | bytes 6291464 | tf_op jit(solution)/shard_map/ppermute | solution.py:41
  9.4 26.5 %collective-permute-start = (bf16[4096,128]{1,0:T(8,128)(2,1)S(1)}, bf16[4096,128]{1,0:T(8,128)(2,1)}, u32[]{:S(2)}, u32[]{:S(2)}) collective-permute-start(bf16[4096,128]{1,0:T(8,128)(2,1)S(1)} %get-tuple-element.405.refs_0_), channel_id=1, source_target_pairs={{0,8},{4,12},{8,24},{12,28},{24,16},{28,20},{16,0},{20,4},{1,9},{5... | collective-permute-start | bytes 3145736 | tf_op jit(solution)/shard_map/ppermute | solution.py:38
  12.0 25.4 %collective-permute-start.1 = (bf16[4096,128]{1,0:T(8,128)(2,1)S(1)}, bf16[4096,128]{1,0:T(8,128)(2,1)}, u32[]{:S(2)}, u32[]{:S(2)}) collective-permute-start(bf16[4096,128]{1,0:T(8,128)(2,1)S(1)} %get-tuple-element.405.refs_0_), channel_id=1, source_target_pairs={{0,16},{4,20},{8,0},{12,4},{24,8},{28,12},{16,24},{20,28},{1,17},{... | collective-permute-start | bytes 3145736 | tf_op jit(solution)/shard_map/ppermute | solution.py:38
  15.0 25.0 %collective-permute-start.4 = (bf16[1024,256]{1,0:T(8,128)(2,1)}, bf16[1024,256]{1,0:T(8,128)(2,1)S(1)}, u32[]{:S(2)}, u32[]{:S(2)}) collective-permute-start(bf16[1024,256]{1,0:T(8,128)(2,1)} %get-tuple-element.399), channel_id=1, source_target_pairs={{0,3},{1,0},{2,1},{3,2},{4,7},{5,4},{6,5},{7,6},{8,11},{9,8},{10,9... | collective-permute-start | bytes 1572872 | tf_op jit(solution)/shard_map/ppermute | solution.py:87
  19.1 23.7 %collective-permute-start.5 = (bf16[1024,256]{1,0:T(8,128)(2,1)}, bf16[1024,256]{1,0:T(8,128)(2,1)}, u32[]{:S(2)}, u32[]{:S(2)}) collective-permute-start(bf16[1024,256]{1,0:T(8,128)(2,1)} %get-tuple-element.401), channel_id=1, source_target_pairs={{0,1},{1,2},{2,3},{3,0},{4,5},{5,6},{6,7},{7,4},{8,9},{9,10},{10,1... | collective-permute-start | bytes 1572872 | tf_op jit(solution)/shard_map/ppermute | solution.py:87
  37.4 22.2 %collective-permute-start.13 = (bf16[4096,128]{1,0:T(8,128)(2,1)}, bf16[4096,128]{1,0:T(8,128)(2,1)}, u32[]{:S(2)}, u32[]{:S(2)}) collective-permute-start(bf16[4096,128]{1,0:T(8,128)(2,1)} %collective-permute-done.refs_1_), channel_id=1, source_target_pairs={{0,4},{4,0},{8,12},{12,8},{16,20},{20,16},{24,28},{28,24},{1,5},{5... | collective-permute-start | bytes 3145736 | tf_op jit(solution)/shard_map/ppermute | solution.py:41
  37.4 22.7 %collective-permute-start.14 = (bf16[4096,128]{1,0:T(8,128)(2,1)}, bf16[4096,128]{1,0:T(8,128)(2,1)}, u32[]{:S(2)}, u32[]{:S(2)}) collective-permute-start(bf16[4096,128]{1,0:T(8,128)(2,1)} %collective-permute-done.1.refs_2_), channel_id=1, source_target_pairs={{0,4},{4,0},{8,12},{12,8},{16,20},{20,16},{24,28},{28,24},{1,5},{5... | collective-permute-start | bytes 3145736 | tf_op jit(solution)/shard_map/ppermute | solution.py:41
  40.1 14.0 %collective-permute-start.2 = (bf16[2048,128]{1,0:T(8,128)(2,1)S(1)}, bf16[2048,128]{1,0:T(8,128)(2,1)}, u32[]{:S(2)}, u32[]{:S(2)}) collective-permute-start(bf16[2048,128]{1,0:T(8,128)(2,1)S(1)} %slice.80), channel_id=1, source_target_pairs={{0,8},{4,12},{8,24},{12,28},{24,16},{28,20},{16,0},{20,4},{1,9},{5... | collective-permute-start | bytes 1572872 | tf_op jit(solution)/shard_map/ppermute | solution.py:38
  42.8 13.0 %collective-permute-start.3 = (bf16[2048,128]{1,0:T(8,128)(2,1)S(1)}, bf16[2048,128]{1,0:T(8,128)(2,1)}, u32[]{:S(2)}, u32[]{:S(2)}) collective-permute-start(bf16[2048,128]{1,0:T(8,128)(2,1)S(1)} %slice.81), channel_id=1, source_target_pairs={{0,16},{4,20},{8,0},{12,4},{24,8},{28,12},{16,24},{20,28},{1,17},{... | collective-permute-start | bytes 1572872 | tf_op jit(solution)/shard_map/ppermute | solution.py:38
  58.1 32.9 %collective-permute-start.11 = (bf16[4096,128]{1,0:T(8,128)(2,1)S(1)}, bf16[4096,128]{1,0:T(8,128)(2,1)S(1)}, u32[]{:S(2)}, u32[]{:S(2)}) collective-permute-start(bf16[4096,128]{1,0:T(8,128)(2,1)S(1)} %get-tuple-element.198.refs_0_), channel_id=1, source_target_pairs={{0,8},{4,12},{8,24},{12,28},{24,16},{28,20},{16,0},{20,4},{1,9},{5... | collective-permute-start | bytes 3145736 | tf_op jit(solution)/shard_map/ppermute | solution.py:38
  59.6 31.5 %collective-permute-start.12 = (bf16[4096,128]{1,0:T(8,128)(2,1)S(1)}, bf16[4096,128]{1,0:T(8,128)(2,1)S(1)}, u32[]{:S(2)}, u32[]{:S(2)}) collective-permute-start(bf16[4096,128]{1,0:T(8,128)(2,1)S(1)} %get-tuple-element.198.refs_0_), channel_id=1, source_target_pairs={{0,16},{4,20},{8,0},{12,4},{24,8},{28,12},{16,24},{20,28},{1,17},{... | collective-permute-start | bytes 3145736 | tf_op jit(solution)/shard_map/ppermute | solution.py:38
  61.8 29.2 %collective-permute-start.7 = (bf16[1024,256]{1,0:T(8,128)(2,1)}, bf16[1024,256]{1,0:T(8,128)(2,1)S(1)}, u32[]{:S(2)}, u32[]{:S(2)}) collective-permute-start(bf16[1024,256]{1,0:T(8,128)(2,1)} %get-tuple-element.196), channel_id=1, source_target_pairs={{0,2},{1,3},{2,0},{3,1},{4,6},{5,7},{6,4},{7,5},{8,10},{9,11},{10,... | collective-permute-start | bytes 1572872 | tf_op jit(solution)/shard_map/ppermute | solution.py:87
  65.3 17.5 %collective-permute-start.8 = (bf16[128,256]{1,0:T(8,128)(2,1)S(1)}, bf16[128,256]{1,0:T(8,128)(2,1)S(1)}, u32[]{:S(2)}, u32[]{:S(2)}) collective-permute-start(bf16[128,256]{1,0:T(8,128)(2,1)S(1)} %constant_dynamic-slice_fusion.7), channel_id=1, source_target_pairs={{0,3},{1,0},{2,1},{3,2},{4,7},{5,4},{6,5},{7,6},{8,11},{9,8},{10,9... | collective-permute-start | bytes 196616 | tf_op jit(solution)/shard_map/ppermute | solution.py:87
  67.1 23.9 %collective-permute-start.9 = (bf16[128,256]{1,0:T(8,128)(2,1)S(1)}, bf16[128,256]{1,0:T(8,128)(2,1)S(1)}, u32[]{:S(2)}, u32[]{:S(2)}) collective-permute-start(bf16[128,256]{1,0:T(8,128)(2,1)S(1)} %constant_dynamic-slice_fusion.7), channel_id=1, source_target_pairs={{0,2},{1,3},{2,0},{3,1},{4,6},{5,7},{6,4},{7,5},{8,10},{9,11},{10,... | collective-permute-start | bytes 196616 | tf_op jit(solution)/shard_map/ppermute | solution.py:87
  94.4 14.0 %collective-permute-start.17 = (bf16[2048,128]{1,0:T(8,128)(2,1)}, bf16[2048,128]{1,0:T(8,128)(2,1)S(1)}, u32[]{:S(2)}, u32[]{:S(2)}) collective-permute-start(bf16[2048,128]{1,0:T(8,128)(2,1)} %slice.84), channel_id=1, source_target_pairs={{0,8},{4,12},{8,24},{12,28},{24,16},{28,20},{16,0},{20,4},{1,9},{5... | collective-permute-start | bytes 1572872 | tf_op jit(solution)/shard_map/ppermute | solution.py:38
  95.5 13.8 %collective-permute-start.18 = (bf16[2048,128]{1,0:T(8,128)(2,1)}, bf16[2048,128]{1,0:T(8,128)(2,1)S(1)}, u32[]{:S(2)}, u32[]{:S(2)}) collective-permute-start(bf16[2048,128]{1,0:T(8,128)(2,1)} %slice.85), channel_id=1, source_target_pairs={{0,16},{4,20},{8,0},{12,4},{24,8},{28,12},{16,24},{20,28},{1,17},{... | collective-permute-start | bytes 1572872 | tf_op jit(solution)/shard_map/ppermute | solution.py:38
  97.5 11.7 %collective-permute-start.22 = (bf16[1024,128]{1,0:T(8,128)(2,1)}, bf16[1024,128]{1,0:T(8,128)(2,1)S(1)}, u32[]{:S(2)}, u32[]{:S(2)}) collective-permute-start(bf16[1024,128]{1,0:T(8,128)(2,1)} %get-tuple-element.211), channel_id=1, source_target_pairs={{0,1},{1,2},{2,3},{3,0},{4,5},{5,6},{6,7},{7,4},{8,9},{9,10},{10,1... | collective-permute-start | bytes 786440 | tf_op jit(solution)/shard_map/ppermute | solution.py:87
  97.5 14.2 %collective-permute-start.21 = (bf16[1024,128]{1,0:T(8,128)(2,1)}, bf16[1024,128]{1,0:T(8,128)(2,1)}, u32[]{:S(2)}, u32[]{:S(2)}) collective-permute-start(bf16[1024,128]{1,0:T(8,128)(2,1)} %get-tuple-element.209), channel_id=1, source_target_pairs={{0,3},{1,0},{2,1},{3,2},{4,7},{5,4},{6,5},{7,6},{8,11},{9,8},{10,9... | collective-permute-start | bytes 786440 | tf_op jit(solution)/shard_map/ppermute | solution.py:87
  112.3 15.0 %collective-permute-start.23 = (bf16[1024,128]{1,0:T(8,128)(2,1)}, bf16[1024,128]{1,0:T(8,128)(2,1)S(1)}, u32[]{:S(2)}, u32[]{:S(2)}) collective-permute-start(bf16[1024,128]{1,0:T(8,128)(2,1)} %get-tuple-element.213), channel_id=1, source_target_pairs={{0,2},{1,3},{2,0},{3,1},{4,6},{5,7},{6,4},{7,5},{8,10},{9,11},{10,... | collective-permute-start | bytes 786440 | tf_op jit(solution)/shard_map/ppermute | solution.py:87
  128.0 14.7 %collective-permute-start.26 = (bf16[512,128]{1,0:T(8,128)(2,1)}, bf16[512,128]{1,0:T(8,128)(2,1)S(1)}, u32[]{:S(2)}, u32[]{:S(2)}) collective-permute-start(bf16[512,128]{1,0:T(8,128)(2,1)} %get-tuple-element.219), channel_id=1, source_target_pairs={{0,3},{1,0},{2,1},{3,2},{4,7},{5,4},{6,5},{7,6},{8,11},{9,8},{10,9... | collective-permute-start | bytes 393224 | tf_op jit(solution)/shard_map/ppermute | solution.py:87
  130.2 12.5 %collective-permute-start.27 = (bf16[512,128]{1,0:T(8,128)(2,1)}, bf16[512,128]{1,0:T(8,128)(2,1)S(1)}, u32[]{:S(2)}, u32[]{:S(2)}) collective-permute-start(bf16[512,128]{1,0:T(8,128)(2,1)} %get-tuple-element.220), channel_id=1, source_target_pairs={{0,2},{1,3},{2,0},{3,1},{4,6},{5,7},{6,4},{7,5},{8,10},{9,11},{10,... | collective-permute-start | bytes 393224 | tf_op jit(solution)/shard_map/ppermute | solution.py:87
  130.2 12.5 %collective-permute-start.28 = (bf16[512,128]{1,0:T(8,128)(2,1)}, bf16[512,128]{1,0:T(8,128)(2,1)S(1)}, u32[]{:S(2)}, u32[]{:S(2)}) collective-permute-start(bf16[512,128]{1,0:T(8,128)(2,1)} %get-tuple-element.221), channel_id=1, source_target_pairs={{0,1},{1,2},{2,3},{3,0},{4,5},{5,6},{6,7},{7,4},{8,9},{9,10},{10,1... | collective-permute-start | bytes 393224 | tf_op jit(solution)/shard_map/ppermute | solution.py:87
  145.2 12.3 %collective-permute-start.30 = (bf16[512,128]{1,0:T(8,128)(2,1)}, bf16[512,128]{1,0:T(8,128)(2,1)S(1)}, u32[]{:S(2)}, u32[]{:S(2)}) collective-permute-start(bf16[512,128]{1,0:T(8,128)(2,1)} %get-tuple-element.227), channel_id=1, source_target_pairs={{0,2},{1,3},{2,0},{3,1},{4,6},{5,7},{6,4},{7,5},{8,10},{9,11},{10,... | collective-permute-start | bytes 393224 | tf_op jit(solution)/shard_map/ppermute | solution.py:87
  157.6 14.0 %collective-permute-start.33 = (bf16[512,128]{1,0:T(8,128)(2,1)}, bf16[512,128]{1,0:T(8,128)(2,1)S(1)}, u32[]{:S(2)}, u32[]{:S(2)}) collective-permute-start(bf16[512,128]{1,0:T(8,128)(2,1)} %get-tuple-element.250), channel_id=1, source_target_pairs={{0,2},{1,3},{2,0},{3,1},{4,6},{5,7},{6,4},{7,5},{8,10},{9,11},{10,... | collective-permute-start | bytes 393224 | tf_op jit(solution)/shard_map/ppermute | solution.py:87
  159.3 12.3 %collective-permute-start.34 = (bf16[512,128]{1,0:T(8,128)(2,1)}, bf16[512,128]{1,0:T(8,128)(2,1)S(1)}, u32[]{:S(2)}, u32[]{:S(2)}) collective-permute-start(bf16[512,128]{1,0:T(8,128)(2,1)} %get-tuple-element.251), channel_id=1, source_target_pairs={{0,1},{1,2},{2,3},{3,0},{4,5},{5,6},{6,7},{7,4},{8,9},{9,10},{10,1... | collective-permute-start | bytes 393224 | tf_op jit(solution)/shard_map/ppermute | solution.py:87
  176.6 13.5 %collective-permute-start.39 = (bf16[384,1024]{1,0:T(8,128)(2,1)S(1)}, bf16[384,1024]{1,0:T(8,128)(2,1)S(1)}, u32[]{:S(2)}, u32[]{:S(2)}) collective-permute-start(bf16[384,1024]{1,0:T(8,128)(2,1)S(1)} %pad_maximum_fusion), channel_id=1, source_target_pairs={{0,4},{4,0},{8,12},{12,8},{16,20},{20,16},{24,28},{28,24},{1,5},{5... | collective-permute-start | bytes 2359304 | tf_op jit(solution)/shard_map/ppermute | solution.py:41
  176.7 13.4 %collective-permute-start.38 = (bf16[128,1024]{1,0:T(8,128)(2,1)S(1)}, bf16[128,1024]{1,0:T(8,128)(2,1)S(1)}, u32[]{:S(2)}, u32[]{:S(2)}) collective-permute-start(bf16[128,1024]{1,0:T(8,128)(2,1)S(1)} %get-tuple-element.393), channel_id=1, source_target_pairs={{0,4},{4,0},{8,12},{12,8},{16,20},{20,16},{24,28},{28,24},{1,5},{5... | collective-permute-start | bytes 786440 | tf_op jit(solution)/shard_map/ppermute | solution.py:41
  177.3 12.8 %collective-permute-start.36 = (bf16[512,128]{1,0:T(8,128)(2,1)S(1)}, bf16[512,128]{1,0:T(8,128)(2,1)S(1)}, u32[]{:S(2)}, u32[]{:S(2)}) collective-permute-start(bf16[512,128]{1,0:T(8,128)(2,1)S(1)} %copy-done.57), channel_id=1, source_target_pairs={{0,2},{1,3},{2,0},{3,1},{4,6},{5,7},{6,4},{7,5},{8,10},{9,11},{10,... | collective-permute-start | bytes 393224 | tf_op jit(solution)/shard_map/ppermute | solution.py:87
  178.0 12.1 %collective-permute-start.37 = (bf16[512,128]{1,0:T(8,128)(2,1)S(1)}, bf16[512,128]{1,0:T(8,128)(2,1)S(1)}, u32[]{:S(2)}, u32[]{:S(2)}) collective-permute-start(bf16[512,128]{1,0:T(8,128)(2,1)S(1)} %copy-done.56), channel_id=1, source_target_pairs={{0,1},{1,2},{2,3},{3,0},{4,5},{5,6},{6,7},{7,4},{8,9},{9,10},{10,1... | collective-permute-start | bytes 393224 | tf_op jit(solution)/shard_map/ppermute | solution.py:87
  190.2 24.5 %collective-permute-start.44 = (bf16[1024,128]{1,0:T(8,128)(2,1)S(1)}, bf16[1024,128]{1,0:T(8,128)(2,1)S(1)}, u32[]{:S(2)}, u32[]{:S(2)}) collective-permute-start(bf16[1024,128]{1,0:T(8,128)(2,1)S(1)} %copy-done.36), channel_id=1, source_target_pairs={{0,1},{1,2},{2,3},{3,0},{4,5},{5,6},{6,7},{7,4},{8,9},{9,10},{10,1... | collective-permute-start | bytes 786440 | tf_op jit(solution)/shard_map/ppermute | solution.py:87
  190.5 24.2 %collective-permute-start.43 = (bf16[1024,128]{1,0:T(8,128)(2,1)S(1)}, bf16[1024,128]{1,0:T(8,128)(2,1)S(1)}, u32[]{:S(2)}, u32[]{:S(2)}) collective-permute-start(bf16[1024,128]{1,0:T(8,128)(2,1)S(1)} %copy-done.37), channel_id=1, source_target_pairs={{0,2},{1,3},{2,0},{3,1},{4,6},{5,7},{6,4},{7,5},{8,10},{9,11},{10,... | collective-permute-start | bytes 786440 | tf_op jit(solution)/shard_map/ppermute | solution.py:87
  192.5 22.2 %collective-permute-start.42 = (bf16[1024,128]{1,0:T(8,128)(2,1)S(1)}, bf16[1024,128]{1,0:T(8,128)(2,1)S(1)}, u32[]{:S(2)}, u32[]{:S(2)}) collective-permute-start(bf16[1024,128]{1,0:T(8,128)(2,1)S(1)} %copy-done.38), channel_id=1, source_target_pairs={{0,3},{1,0},{2,1},{3,2},{4,7},{5,4},{6,5},{7,6},{8,11},{9,8},{10,9... | collective-permute-start | bytes 786440 | tf_op jit(solution)/shard_map/ppermute | solution.py:87
  195.4 19.2 %collective-permute-start.40 = (bf16[64,1024]{1,0:T(8,128)(2,1)S(1)}, bf16[64,1024]{1,0:T(8,128)(2,1)S(1)}, u32[]{:S(2)}, u32[]{:S(2)}) collective-permute-start(bf16[64,1024]{1,0:T(8,128)(2,1)S(1)} %get-tuple-element.409), channel_id=1, source_target_pairs={{0,8},{4,12},{8,24},{12,28},{24,16},{28,20},{16,0},{20,4},{1,9},{5... | collective-permute-start | bytes 393224 | tf_op jit(solution)/shard_map/ppermute | solution.py:38
  196.7 17.9 %collective-permute-start.41 = (bf16[64,1024]{1,0:T(8,128)(2,1)S(1)}, bf16[64,1024]{1,0:T(8,128)(2,1)S(1)}, u32[]{:S(2)}, u32[]{:S(2)}) collective-permute-start(bf16[64,1024]{1,0:T(8,128)(2,1)S(1)} %get-tuple-element.408), channel_id=1, source_target_pairs={{0,16},{4,20},{8,0},{12,4},{24,8},{28,12},{16,24},{20,28},{1,17},{... | collective-permute-start | bytes 393224 | tf_op jit(solution)/shard_map/ppermute | solution.py:38
  231.1 27.6 %collective-permute-start.49 = (bf16[4096,128]{1,0:T(8,128)(2,1)}, bf16[4096,128]{1,0:T(8,128)(2,1)S(1)}, u32[]{:S(2)}, u32[]{:S(2)}) collective-permute-start(bf16[4096,128]{1,0:T(8,128)(2,1)} %get-tuple-element.341), channel_id=1, source_target_pairs={{0,8},{4,12},{8,24},{12,28},{24,16},{28,20},{16,0},{20,4},{1,9},{5... | collective-permute-start | bytes 3145736 | tf_op jit(solution)/shard_map/ppermute | solution.py:38
  232.4 26.3 %collective-permute-start.50 = (bf16[4096,128]{1,0:T(8,128)(2,1)}, bf16[4096,128]{1,0:T(8,128)(2,1)S(1)}, u32[]{:S(2)}, u32[]{:S(2)}) collective-permute-start(bf16[4096,128]{1,0:T(8,128)(2,1)} %get-tuple-element.342), channel_id=1, source_target_pairs={{0,16},{4,20},{8,0},{12,4},{24,8},{28,12},{16,24},{20,28},{1,17},{... | collective-permute-start | bytes 3145736 | tf_op jit(solution)/shard_map/ppermute | solution.py:38
  233.1 25.5 %collective-permute-start.51 = (bf16[1024,256]{1,0:T(8,128)(2,1)S(1)}, bf16[1024,256]{1,0:T(8,128)(2,1)S(1)}, u32[]{:S(2)}, u32[]{:S(2)}) collective-permute-start(bf16[1024,256]{1,0:T(8,128)(2,1)S(1)} %copy-done.27), channel_id=1, source_target_pairs={{0,2},{1,3},{2,0},{3,1},{4,6},{5,7},{6,4},{7,5},{8,10},{9,11},{10,... | collective-permute-start | bytes 1572872 | tf_op jit(solution)/shard_map/ppermute | solution.py:87
  264.4 15.1 %collective-permute-start.52 = (bf16[2048,128]{1,0:T(8,128)(2,1)}, bf16[2048,128]{1,0:T(8,128)(2,1)}, u32[]{:S(2)}, u32[]{:S(2)}) collective-permute-start(bf16[2048,128]{1,0:T(8,128)(2,1)} %get-tuple-element.387), channel_id=1, source_target_pairs={{0,8},{4,12},{8,24},{12,28},{24,16},{28,20},{16,0},{20,4},{1,9},{5... | collective-permute-start | bytes 1572872 | tf_op jit(solution)/shard_map/ppermute | solution.py:38
  265.7 15.1 %collective-permute-start.53 = (bf16[2048,128]{1,0:T(8,128)(2,1)}, bf16[2048,128]{1,0:T(8,128)(2,1)}, u32[]{:S(2)}, u32[]{:S(2)}) collective-permute-start(bf16[2048,128]{1,0:T(8,128)(2,1)} %get-tuple-element.386), channel_id=1, source_target_pairs={{0,16},{4,20},{8,0},{12,4},{24,8},{28,12},{16,24},{20,28},{1,17},{... | collective-permute-start | bytes 1572872 | tf_op jit(solution)/shard_map/ppermute | solution.py:38
  267.7 22.5 %collective-permute-start.59 = (bf16[2048,128]{1,0:T(8,128)(2,1)}, bf16[2048,128]{1,0:T(8,128)(2,1)}, u32[]{:S(2)}, u32[]{:S(2)}) collective-permute-start(bf16[2048,128]{1,0:T(8,128)(2,1)} %get-tuple-element.389), channel_id=1, source_target_pairs={{0,8},{4,12},{8,24},{12,28},{24,16},{28,20},{16,0},{20,4},{1,9},{5... | collective-permute-start | bytes 1572872 | tf_op jit(solution)/shard_map/ppermute | solution.py:38
  269.0 22.2 %collective-permute-start.60 = (bf16[2048,128]{1,0:T(8,128)(2,1)}, bf16[2048,128]{1,0:T(8,128)(2,1)}, u32[]{:S(2)}, u32[]{:S(2)}) collective-permute-start(bf16[2048,128]{1,0:T(8,128)(2,1)} %get-tuple-element.388), channel_id=1, source_target_pairs={{0,16},{4,20},{8,0},{12,4},{24,8},{28,12},{16,24},{20,28},{1,17},{... | collective-permute-start | bytes 1572872 | tf_op jit(solution)/shard_map/ppermute | solution.py:38
  271.1 20.1 %collective-permute-start.56 = (bf16[128,256]{1,0:T(8,128)(2,1)S(1)}, bf16[128,256]{1,0:T(8,128)(2,1)S(1)}, u32[]{:S(2)}, u32[]{:S(2)}) collective-permute-start(bf16[128,256]{1,0:T(8,128)(2,1)S(1)} %get-tuple-element.358), channel_id=1, source_target_pairs={{0,3},{1,0},{2,1},{3,2},{4,7},{5,4},{6,5},{7,6},{8,11},{9,8},{10,9... | collective-permute-start | bytes 196616 | tf_op jit(solution)/shard_map/ppermute | solution.py:87
  279.5 11.7 %collective-permute-start.57 = (bf16[128,256]{1,0:T(8,128)(2,1)S(1)}, bf16[128,256]{1,0:T(8,128)(2,1)S(1)}, u32[]{:S(2)}, u32[]{:S(2)}) collective-permute-start(bf16[128,256]{1,0:T(8,128)(2,1)S(1)} %get-tuple-element.359), channel_id=1, source_target_pairs={{0,2},{1,3},{2,0},{3,1},{4,6},{5,7},{6,4},{7,5},{8,10},{9,11},{10,... | collective-permute-start | bytes 196616 | tf_op jit(solution)/shard_map/ppermute | solution.py:87
  296.1 26.0 %collective-permute-start.63 = (bf16[4096,128]{1,0:T(8,128)(2,1)}, bf16[4096,128]{1,0:T(8,128)(2,1)S(1)}, u32[]{:S(2)}, u32[]{:S(2)}) collective-permute-start(bf16[4096,128]{1,0:T(8,128)(2,1)} %get-tuple-element.377), channel_id=1, source_target_pairs={{0,8},{4,12},{8,24},{12,28},{24,16},{28,20},{16,0},{20,4},{1,9},{5... | collective-permute-start | bytes 3145736 | tf_op jit(solution)/shard_map/ppermute | solution.py:38
  297.3 24.9 %collective-permute-start.64 = (bf16[4096,128]{1,0:T(8,128)(2,1)}, bf16[4096,128]{1,0:T(8,128)(2,1)S(1)}, u32[]{:S(2)}, u32[]{:S(2)}) collective-permute-start(bf16[4096,128]{1,0:T(8,128)(2,1)} %get-tuple-element.378), channel_id=1, source_target_pairs={{0,16},{4,20},{8,0},{12,4},{24,8},{28,12},{16,24},{20,28},{1,17},{... | collective-permute-start | bytes 3145736 | tf_op jit(solution)/shard_map/ppermute | solution.py:38
  298.1 14.9 %collective-permute-start.61 = (bf16[1024,256]{1,0:T(8,128)(2,1)}, bf16[1024,256]{1,0:T(8,128)(2,1)}, u32[]{:S(2)}, u32[]{:S(2)}) collective-permute-start(bf16[1024,256]{1,0:T(8,128)(2,1)} %get-tuple-element.370), channel_id=1, source_target_pairs={{0,3},{1,0},{2,1},{3,2},{4,7},{5,4},{6,5},{7,6},{8,11},{9,8},{10,9... | collective-permute-start | bytes 1572872 | tf_op jit(solution)/shard_map/ppermute | solution.py:87
  299.8 22.2 %collective-permute-start.62 = (bf16[1024,256]{1,0:T(8,128)(2,1)}, bf16[1024,256]{1,0:T(8,128)(2,1)S(1)}, u32[]{:S(2)}, u32[]{:S(2)}) collective-permute-start(bf16[1024,256]{1,0:T(8,128)(2,1)} %get-tuple-element.372), channel_id=1, source_target_pairs={{0,1},{1,2},{2,3},{3,0},{4,5},{5,6},{6,7},{7,4},{8,9},{9,10},{10,1... | collective-permute-start | bytes 1572872 | tf_op jit(solution)/shard_map/ppermute | solution.py:87
  (77 other events, 683.5 us)
Sparse Core Ops, SparseCore 0:
  111.9 27.4 all-gather.1

commit v15 on v14

--- a/solution.py
+++ b/solution.py
@@ -659,8 +659,9 @@
         w.close()
         if c == 0:
             spmm_meta, spmm_t_meta, dense_meta = w["metas"]
-            w.go(cot_inner=send([w.gate(b) for b in cot_blocks], inner))
-            w.go(shares=send([w.gate(w_share)] * parts, ends + inner))
+            shares = send([w.gate(w_share)] * parts, ends + inner)
+            blocks, shares = lax.optimization_barrier(([w.gate(b) for b in cot_blocks], shares))
+            w.go(cot_inner=send(blocks, inner), shares=shares)
         else:
             w.go(**{f"mixed_inner{c - 1}": send([w.gate(b) for b in mixed[c - 1]], inner)})
         got_own[c, len(offsets) - 2], got_own[c, len(offsets) - 1] = w[f"far_up{c}"], w[f"far_down{c}"]

time: 337 us -> 338 us (level)
    unnamed x120 -> x128, local copies, waits for them, and re-layouts: 12.2 us -> 13.2 us
  transfers between devices with their start and end apart: 66 -> 66, of which waited for: 25 -> 26; matrix products, arithmetic and copies ran while one was open for 7% -> 7% of each run, Pallas kernels for 28% -> 28%
where the time goes in v15:
time: 338 us; the launch traced here: 337 us
  waiting for transfers between devices  106 us (31%)
  Pallas kernels  103 us (30%)
  starting transfers between devices  65 us (19%)
  local copies, waits for them, and re-layouts  28.7 us (8%)
  between operations  22.6 us (7%)
  other arithmetic  6.24 us (2%)
  matrix products  4.7 us (1%)
    ppermute x30, waiting for transfers between devices, send(): lax.ppermute(blocks[s], 'rep', [(i, (i + s) % size) for i in range(size)])  54.2 us
    ppermute x20, waiting for transfers between devices, hop(): return lax.ppermute(value, 'row', self.perm(step))  43.4 us
    ppermute x30, starting transfers between devices, send(): lax.ppermute(blocks[s], 'rep', [(i, (i + s) % size) for i in range(size)])  39.5 us
    pallas_call x3, Pallas kernels, spmm(): pl.pallas_call(functools.partial(spmm_kernel, len(pieces), per_part, skip...  36.6 us
    pallas_call x2, Pallas kernels, spmm_t(): pl.pallas_call(functools.partial(spmm_t_kernel, len(grads), per_part, len...  34.5 us
    ppermute x20, starting transfers between devices, hop(): return lax.ppermute(value, 'row', self.perm(step))  22.4 us
    pallas_call x2, Pallas kernels, dense(): pl.pallas_call(functools.partial(dense_kernel, parts, chunks, len(earlier...  14.1 us
    unnamed x128, local copies, waits for them, and re-layouts  13.2 us
  transfers between devices with their start and end apart: 66, of which 26 were waited for; matrix products, arithmetic and copies ran while one was open for 7% of the time, Pallas kernels for 28%

profile of v15, /device:TPU:0, one launch (start us, length us, event | category | flops | bytes accessed | tf_op | source)
XLA Modules:
  0.0 336.9 jit_solution(6750669856606112124)
XLA Ops:
  7.7 1.7 fusion.1
  9.4 2.6 collective-permute-start
  12.1 2.9 constant_dynamic-slice_fusion.5
  15.0 4.1 %collective-permute-start.4 = (bf16[1024,256]{1,0:T(8,128)(2,1)}, bf16[1024,256]{1,0:T(8,128)(2,1)S(1)}, u32[]{:S(2)}, u32[]{:S(2)}) collective-permute-start(bf16[1024,256]{1,0:T(8,128)(2,1)} %get-tuple-element.407), channel_id=1, source_target_pairs={{0,3},{1,0},{2,1},{3,2},{4,7},{5,4},{6,5},{7,6},{8,11},{9,8},{10,9... | collective-permute-start | bytes 1572872 | tf_op jit(solution)/shard_map/ppermute | solution.py:87
  29.4 6.6 %collective-permute-done.refs_1_ = bf16[4096,128]{1,0:T(8,128)(2,1)} collective-permute-done((bf16[4096,128]{1,0:T(8,128)(2,1)S(1)}, bf16[4096,128]{1,0:T(8,128)(2,1)}, u32[]{:S(2)}, u32[]{:S(2)}) %collective-permute-start) | collective-permute-done | bytes 1048608 | tf_op jit(solution)/shard_map/ppermute | solution.py:38
  44.3 9.8 %collective-permute-done.2.refs_3_ = bf16[2048,128]{1,0:T(8,128)(2,1)} collective-permute-done((bf16[2048,128]{1,0:T(8,128)(2,1)S(1)}, bf16[2048,128]{1,0:T(8,128)(2,1)}, u32[]{:S(2)}, u32[]{:S(2)}) %collective-permute-start.2) | collective-permute-done | bytes 524320 | tf_op jit(solution)/shard_map/ppermute | solution.py:38
  54.1 1.7 collective-permute-done.3.refs_4_
  55.7 3.2 collective-permute-start.7
  60.8 3.3 collective-permute-done.8
  67.0 3.0 fusion
  71.1 14.4 %spmm.3 = (bf16[1024,128]{1,0:T(8,128)(2,1)}, bf16[1024,128]{1,0:T(8,128)(2,1)}, bf16[1024,128]{1,0:T(8,128)(2,1)}, bf16[1024,128]{1,0:T(8,128)(2,1)}) custom-call(s32[32,16]{1,0:T(8,128)} %copy.71.cols, s32[32]{0:T(128)} %counts.9, s32[11]{0:T(128)} %stack.75.meta, bf16[32,16,128,128]{3,2,1,0:T(8,128)(2,1)} %tiles.9, bf16[4096,128]{1,0:T(8,128)(2,1)} %copy-done.9, ...), custom_call_target="tpu_custom_call" | custom-call | flops 2147483648 | bytes 25165824 | tf_op jit(solution)/shard_map/spmm/pallas_call | solution.py:158
  85.5 7.1 %collective-permute-done.10.refs_10_ = bf16[1024,256]{1,0:T(8,128)(2,1)S(1)} collective-permute-done((bf16[1024,256]{1,0:T(8,128)(2,1)}, bf16[1024,256]{1,0:T(8,128)(2,1)S(1)}, u32[]{:S(2)}, u32[]{:S(2)}) %collective-permute-start.10) | collective-permute-done | bytes 524320 | tf_op jit(solution)/shard_map/ppermute | solution.py:87
  99.1 3.8 %collective-permute-start.21 = (bf16[1024,128]{1,0:T(8,128)(2,1)}, bf16[1024,128]{1,0:T(8,128)(2,1)}, u32[]{:S(2)}, u32[]{:S(2)}) collective-permute-start(bf16[1024,128]{1,0:T(8,128)(2,1)} %get-tuple-element.217), channel_id=1, source_target_pairs={{0,3},{1,0},{2,1},{3,2},{4,7},{5,4},{6,5},{7,6},{8,11},{9,8},{10,9... | collective-permute-start | bytes 786440 | tf_op jit(solution)/shard_map/ppermute | solution.py:87
  103.6 6.4 %collective-permute-done.17.refs_3_ = bf16[2048,128]{1,0:T(8,128)(2,1)S(1)} collective-permute-done((bf16[2048,128]{1,0:T(8,128)(2,1)}, bf16[2048,128]{1,0:T(8,128)(2,1)S(1)}, u32[]{:S(2)}, u32[]{:S(2)}) %collective-permute-start.17) | collective-permute-done | bytes 524320 | tf_op jit(solution)/shard_map/ppermute | solution.py:38
  110.4 2.8 collective-permute-done.21.refs_2_
  113.8 2.4 collective-permute-start.23
  117.2 11.1 %spmm.4 = (bf16[512,128]{1,0:T(8,128)(2,1)}, bf16[512,128]{1,0:T(8,128)(2,1)}, bf16[512,128]{1,0:T(8,128)(2,1)}, bf16[512,128]{1,0:T(8,128)(2,1)}) custom-call(s32[32,16]{1,0:T(8,128)} %copy.71.cols, s32[32]{0:T(128)} %counts.9, s32[11]{0:T(128)} %stack.75.meta, bf16[32,16,128,128]{3,2,1,0:T(8,128)(2,1)} %tiles.9, bf16[4096,128]{1,0:T(8,128)(2,1)} %copy-done.4, ...), custom_call_target="tpu_custom_call" | custom-call | flops 1073741824 | bytes 16777216 | tf_op jit(solution)/shard_map/spmm/pallas_call | solution.py:158
  129.6 2.1 collective-permute-start.26
  133.1 11.1 %spmm.5 = (bf16[512,128]{1,0:T(8,128)(2,1)}, bf16[512,128]{1,0:T(8,128)(2,1)}, bf16[512,128]{1,0:T(8,128)(2,1)}, bf16[512,128]{1,0:T(8,128)(2,1)}) custom-call(s32[32,16]{1,0:T(8,128)} %copy.71.cols, s32[32]{0:T(128)} %counts.9, s32[11]{0:T(128)} %stack.75.meta, bf16[32,16,128,128]{3,2,1,0:T(8,128)(2,1)} %tiles.9, bf16[4096,128]{1,0:T(8,128)(2,1)} %copy-done.4, ...), custom_call_target="tpu_custom_call" | custom-call | flops 1073741824 | bytes 16777216 | tf_op jit(solution)/shard_map/spmm/pallas_call | solution.py:158
  144.3 2.4 collective-permute-start.29
  148.0 7.0 %dense.2 = (bf16[1024,256]{1,0:T(8,128)(2,1)}, bf16[1024,256]{1,0:T(8,128)(2,1)}, bf16[1024,256]{1,0:T(8,128)(2,1)}, bf16[1024,256]{1,0:T(8,128)(2,1)}, bf16[512...) custom-call(s32[1]{0:T(128)} %bitcast.meta, ...), custom_call_target="tpu_custom_call" | custom-call | flops 2147483648 | bytes 8388608 | tf_op jit(solution)/shard_map/dense/pallas_call | solution.py:325
  155.1 3.9 %collective-permute-done.30.refs_5_ = bf16[512,128]{1,0:T(8,128)(2,1)S(1)} collective-permute-done((bf16[512,128]{1,0:T(8,128)(2,1)}, bf16[512,128]{1,0:T(8,128)(2,1)S(1)}, u32[]{:S(2)}, u32[]{:S(2)}) %collective-permute-start.30) | collective-permute-done | bytes 131104 | tf_op jit(solution)/shard_map/ppermute | solution.py:87
  160.7 2.0 collective-permute-start.34
  162.7 7.1 %dense.3 = (bf16[1024,256]{1,0:T(8,128)(2,1)}, bf16[1024,256]{1,0:T(8,128)(2,1)}, bf16[1024,256]{1,0:T(8,128)(2,1)}, bf16[1024,256]{1,0:T(8,128)(2,1)}, bf16[512...) custom-call(s32[1]{0:T(128)} %bitcast.meta, ...), custom_call_target="tpu_custom_call", output_to_operand_aliasing={{0}: (14, {}), {1}: (15, {}), {2}: (16, {}), {3}: (17, {}),... | custom-call | flops 2147483648 | bytes 8388608 | tf_op jit(solution)/shard_map/dense/pallas_call | solution.py:325
  169.8 3.2 collective-permute-done.33.refs_4_
  173.0 4.7 %convolution_convert_fusion = bf16[1024,1024]{1,0:T(8,128)(2,1)S(1)} fusion(bf16[1024,1024]{1,0:T(8,128)(2,1)} %get-tuple-element.295, bf16[1024,1024]{1,0:T(8,128)(2,1)} %get-tuple-element.296), kind=kOutput, calls=%fused_computation | convolution fusion | flops 2148532224 | bytes 6291456 | tf_op jit(solution)/shard_map/dot_general | solution.py:695
  179.5 2.0 collective-permute-start.37
  181.4 4.0 %collective-permute-done.35.refs_3_ = bf16[512,128]{1,0:T(8,128)(2,1)S(1)} collective-permute-done((bf16[512,128]{1,0:T(8,128)(2,1)S(1)}, bf16[512,128]{1,0:T(8,128)(2,1)S(1)}, u32[]{:S(2)}, u32[]{:S(2)}) %collective-permute-start.35) | collective-permute-done | bytes 131104 | tf_op jit(solution)/shard_map/ppermute | solution.py:87
  185.4 6.1 %collective-permute-done.36.refs_5_ = bf16[512,128]{1,0:T(8,128)(2,1)S(1)} collective-permute-done((bf16[512,128]{1,0:T(8,128)(2,1)S(1)}, bf16[512,128]{1,0:T(8,128)(2,1)S(1)}, u32[]{:S(2)}, u32[]{:S(2)}) %collective-permute-start.36) | collective-permute-done | bytes 131104 | tf_op jit(solution)/shard_map/ppermute | solution.py:87
  191.9 2.0 collective-permute-start.43
  193.9 2.8 collective-permute-start.42
  198.9 17.1 %spmm_t.2 = (bf16[4096,128]{1,0:T(8,128)(2,1)}, bf16[4096,128]{1,0:T(8,128)(2,1)}, bf16[4096,128]{1,0:T(8,128)(2,1)}, bf16[4096,128]{1,0:T(8,128)(2,1)}, bf16[40...) custom-call(s32[32,16]{1,0:T(8,128)} %copy.71.cols, s32[32]{0:T(128)} %counts.9, s32[9]{0:T(128)} %stack.84.meta, ...), custom_call_target="tpu_custom_call" | custom-call | flops 2147483648 | bytes 25165824 | tf_op jit(solution)/shard_map/spmm_t/pallas_call | solution.py:241
  216.8 2.9 collective-permute-done.45.got_far
  222.1 3.5 %collective-permute-done.46.got_up.got_down.got = bf16[12288,128]{1,0:T(8,128)(2,1)S(1)} collective-permute-done((bf16[12288,128]{1,0:T(8,128)(2,1)}, bf16[12288,128]{1,0:T(8,128)(2,1)S(1)}, u32[]{:S(2)}, u32[]{:S(2)}) %collective-permute-start.46) | collective-permute-done | bytes 3145760 | tf_op jit(solution)/shard_map/ppermute | solution.py:41
  225.6 1.7 copy-done.2
  227.3 4.4 %halves_sums.1 = (bf16[4096,128]{1,0:T(8,128)(2,1)}, bf16[4096,128]{1,0:T(8,128)(2,1)}) custom-call(bf16[4096,128]{1,0:T(8,128)(2,1)} %get-tuple-element.327.own_far, bf16[4096,128]{1,0:T(8,128)(2,1)} %copy-done.23, bf16[4096,128]{1,0:T(8,128)(2,1)} %get-tuple-element.328.own_up, bf16[12288,128]{1,0:T(8,128)(2,1)} %copy-done.2, ...), custom_call_target="tpu_custom_call" | custom-call | flops 1048576 | bytes 6291456 | tf_op jit(solution)/shard_map/halves_sums/pallas_call | solution.py:465
  235.3 17.4 %spmm_t.3 = (bf16[4096,128]{1,0:T(8,128)(2,1)}, bf16[4096,128]{1,0:T(8,128)(2,1)}, bf16[4096,128]{1,0:T(8,128)(2,1)}, bf16[4096,128]{1,0:T(8,128)(2,1)}, bf16[40...) custom-call(s32[32,16]{1,0:T(8,128)} %copy.71.cols, s32[32]{0:T(128)} %counts.9, s32[9]{0:T(128)} %stack.84.meta, ...), custom_call_target="tpu_custom_call" | custom-call | flops 2147483648 | bytes 25165824 | tf_op jit(solution)/shard_map/spmm_t/pallas_call | solution.py:241
  252.7 7.4 %collective-permute-done.51 = bf16[1024,256]{1,0:T(8,128)(2,1)S(1)} collective-permute-done((bf16[1024,256]{1,0:T(8,128)(2,1)S(1)}, bf16[1024,256]{1,0:T(8,128)(2,1)S(1)}, u32[]{:S(2)}, u32[]{:S(2)}) %collective-permute-start.51) | collective-permute-done | bytes 524320 | tf_op jit(solution)/shard_map/ppermute | solution.py:87
  260.9 2.2 collective-permute-done.54
  263.3 2.6 add_convert_fusion.2
  272.5 1.7 collective-permute-start.56
  274.3 6.7 %collective-permute-done.52.up_low = bf16[2048,128]{1,0:T(8,128)(2,1)} collective-permute-done((bf16[2048,128]{1,0:T(8,128)(2,1)}, bf16[2048,128]{1,0:T(8,128)(2,1)}, u32[]{:S(2)}, u32[]{:S(2)}) %collective-permute-start.52) | collective-permute-done | bytes 524320 | tf_op jit(solution)/shard_map/ppermute | solution.py:38
  283.2 8.4 %collective-permute-done.59.up = bf16[2048,128]{1,0:T(8,128)(2,1)} collective-permute-done((bf16[2048,128]{1,0:T(8,128)(2,1)}, bf16[2048,128]{1,0:T(8,128)(2,1)}, u32[]{:S(2)}, u32[]{:S(2)}) %collective-permute-start.59) | collective-permute-done | bytes 524320 | tf_op jit(solution)/shard_map/ppermute | solution.py:38
  292.5 4.8 %step_sums.1 = (bf16[4096,128]{1,0:T(8,128)(2,1)}, bf16[4096,128]{1,0:T(8,128)(2,1)}) custom-call(bf16[4096,128]{1,0:T(8,128)(2,1)} %get-tuple-element.352.own_up, bf16[12288,128]{1,0:T(8,128)(2,1)} %copy-done.3, bf16[2048,128]{1,0:T(8,128)(2,1)} %collective-permute-done.59.up, bf16[4096,128]{1,0:T(8,128)(2,1)} %get-tuple-element.373.own_down, ...), custom_call_target="tpu_custom_call" | custom-call | flops 2097152 | bytes 7340032 | tf_op jit(solution)/shard_map/step_sums/pallas_call | solution.py:390
  302.2 4.2 %joined.1.refs_0_ = bf16[4096,128]{1,0:T(8,128)(2,1)} custom-call(bf16[4096,128]{1,0:T(8,128)(2,1)} %get-tuple-element.381.own, bf16[12288,128]{1,0:T(8,128)(2,1)} %copy-done.2, bf16[2048,128]{1,0:T(8,128)(2,1)} %collective-permute-done.52.up_low, bf16[4096,128]{1,0:T(8,128)(2,1)} %copy-done.12, bf16[4096,128]{1,0:T(8,128)(2,1)} %copy-done.13, ...), custom_call_target="tpu_custom_call" | custom-call | flops 1572864 | bytes 5242880 | tf_op jit(solution)/shard_map/joined/pallas_call | solution.py:509
  307.5 6.8 %collective-permute-done.61 = bf16[1024,256]{1,0:T(8,128)(2,1)} collective-permute-done((bf16[1024,256]{1,0:T(8,128)(2,1)}, bf16[1024,256]{1,0:T(8,128)(2,1)}, u32[]{:S(2)}, u32[]{:S(2)}) %collective-permute-start.61) | collective-permute-done | bytes 524320 | tf_op jit(solution)/shard_map/ppermute | solution.py:87
  315.4 7.9 %collective-permute-done.62 = bf16[1024,256]{1,0:T(8,128)(2,1)S(1)} collective-permute-done((bf16[1024,256]{1,0:T(8,128)(2,1)}, bf16[1024,256]{1,0:T(8,128)(2,1)S(1)}, u32[]{:S(2)}, u32[]{:S(2)}) %collective-permute-start.62) | collective-permute-done | bytes 524320 | tf_op jit(solution)/shard_map/ppermute | solution.py:87
  325.4 4.6 %feature_grad.1 = bf16[4096,256]{1,0:T(8,128)(2,1)} custom-call(bf16[4096,128]{1,0:T(8,128)(2,1)} %joined.1.refs_0_, bf16[4096,128]{1,0:T(8,128)(2,1)} %get-tuple-element.384.refs_1_, bf16[12288,128]{1,0:T(8,128)(2,1)} %copy-done.3, bf16[4096,128]{1,0:T(8,128)(2,1)} %copy-done.20, bf16[4096,128]{1,0:T(8,128)(2,1)} %copy-done.21), custom_call_target="tpu_custom_call" | custom-call | flops 2097152 | bytes 7340032 | tf_op jit(solution)/shard_map/feature_grad/pallas_call | solution.py:426
  (252 shorter events, 62.8 us)
Async XLA Ops:
  7.2 140.8 %all-gather.2.cloned.1.call-start = ((), (), s32[]{:S(2)}) async-start(), calls=%async_computation | async-start | bytes 2359296 | tf_op jit(solution)/shard_map/all_gather | solution.py:671
  7.2 48.5 %collective-permute-start.6 = (bf16[4096,256]{1,0:T(8,128)(2,1)}, bf16[4096,256]{1,0:T(8,128)(2,1)}, u32[]{:S(2)}, u32[]{:S(2)}) collective-permute-start(bf16[4096,256]{1,0:T(8,128)(2,1)} %param.58), channel_id=1, source_target_pairs={{0,4},{4,0},{8,12},{12,8},{16,20},{20,16},{24,28},{28,24},{1,5},{5... | collective-permute-start | bytes 6291464 | tf_op jit(solution)/shard_map/ppermute | solution.py:41
  9.4 26.5 %collective-permute-start = (bf16[4096,128]{1,0:T(8,128)(2,1)S(1)}, bf16[4096,128]{1,0:T(8,128)(2,1)}, u32[]{:S(2)}, u32[]{:S(2)}) collective-permute-start(bf16[4096,128]{1,0:T(8,128)(2,1)S(1)} %get-tuple-element.413.refs_0_), channel_id=1, source_target_pairs={{0,8},{4,12},{8,24},{12,28},{24,16},{28,20},{16,0},{20,4},{1,9},{5... | collective-permute-start | bytes 3145736 | tf_op jit(solution)/shard_map/ppermute | solution.py:38
  12.0 25.4 %collective-permute-start.1 = (bf16[4096,128]{1,0:T(8,128)(2,1)S(1)}, bf16[4096,128]{1,0:T(8,128)(2,1)}, u32[]{:S(2)}, u32[]{:S(2)}) collective-permute-start(bf16[4096,128]{1,0:T(8,128)(2,1)S(1)} %get-tuple-element.413.refs_0_), channel_id=1, source_target_pairs={{0,16},{4,20},{8,0},{12,4},{24,8},{28,12},{16,24},{20,28},{1,17},{... | collective-permute-start | bytes 3145736 | tf_op jit(solution)/shard_map/ppermute | solution.py:38
  15.0 25.1 %collective-permute-start.4 = (bf16[1024,256]{1,0:T(8,128)(2,1)}, bf16[1024,256]{1,0:T(8,128)(2,1)S(1)}, u32[]{:S(2)}, u32[]{:S(2)}) collective-permute-start(bf16[1024,256]{1,0:T(8,128)(2,1)} %get-tuple-element.407), channel_id=1, source_target_pairs={{0,3},{1,0},{2,1},{3,2},{4,7},{5,4},{6,5},{7,6},{8,11},{9,8},{10,9... | collective-permute-start | bytes 1572872 | tf_op jit(solution)/shard_map/ppermute | solution.py:87
  19.1 23.7 %collective-permute-start.5 = (bf16[1024,256]{1,0:T(8,128)(2,1)}, bf16[1024,256]{1,0:T(8,128)(2,1)}, u32[]{:S(2)}, u32[]{:S(2)}) collective-permute-start(bf16[1024,256]{1,0:T(8,128)(2,1)} %get-tuple-element.409), channel_id=1, source_target_pairs={{0,1},{1,2},{2,3},{3,0},{4,5},{5,6},{6,7},{7,4},{8,9},{9,10},{10,1... | collective-permute-start | bytes 1572872 | tf_op jit(solution)/shard_map/ppermute | solution.py:87
  37.4 29.1 %collective-permute-start.13 = (bf16[4096,128]{1,0:T(8,128)(2,1)}, bf16[4096,128]{1,0:T(8,128)(2,1)}, u32[]{:S(2)}, u32[]{:S(2)}) collective-permute-start(bf16[4096,128]{1,0:T(8,128)(2,1)} %collective-permute-done.refs_1_), channel_id=1, source_target_pairs={{0,4},{4,0},{8,12},{12,8},{16,20},{20,16},{24,28},{28,24},{1,5},{5... | collective-permute-start | bytes 3145736 | tf_op jit(solution)/shard_map/ppermute | solution.py:41
  37.4 29.1 %collective-permute-start.14 = (bf16[4096,128]{1,0:T(8,128)(2,1)}, bf16[4096,128]{1,0:T(8,128)(2,1)}, u32[]{:S(2)}, u32[]{:S(2)}) collective-permute-start(bf16[4096,128]{1,0:T(8,128)(2,1)} %collective-permute-done.1.refs_2_), channel_id=1, source_target_pairs={{0,4},{4,0},{8,12},{12,8},{16,20},{20,16},{24,28},{28,24},{1,5},{5... | collective-permute-start | bytes 3145736 | tf_op jit(solution)/shard_map/ppermute | solution.py:41
  40.1 14.0 %collective-permute-start.2 = (bf16[2048,128]{1,0:T(8,128)(2,1)S(1)}, bf16[2048,128]{1,0:T(8,128)(2,1)}, u32[]{:S(2)}, u32[]{:S(2)}) collective-permute-start(bf16[2048,128]{1,0:T(8,128)(2,1)S(1)} %slice.80), channel_id=1, source_target_pairs={{0,8},{4,12},{8,24},{12,28},{24,16},{28,20},{16,0},{20,4},{1,9},{5... | collective-permute-start | bytes 1572872 | tf_op jit(solution)/shard_map/ppermute | solution.py:38
  42.8 13.0 %collective-permute-start.3 = (bf16[2048,128]{1,0:T(8,128)(2,1)S(1)}, bf16[2048,128]{1,0:T(8,128)(2,1)}, u32[]{:S(2)}, u32[]{:S(2)}) collective-permute-start(bf16[2048,128]{1,0:T(8,128)(2,1)S(1)} %slice.81), channel_id=1, source_target_pairs={{0,16},{4,20},{8,0},{12,4},{24,8},{28,12},{16,24},{20,28},{1,17},{... | collective-permute-start | bytes 1572872 | tf_op jit(solution)/shard_map/ppermute | solution.py:38
  64.1 28.5 %collective-permute-start.11 = (bf16[4096,128]{1,0:T(8,128)(2,1)S(1)}, bf16[4096,128]{1,0:T(8,128)(2,1)S(1)}, u32[]{:S(2)}, u32[]{:S(2)}) collective-permute-start(bf16[4096,128]{1,0:T(8,128)(2,1)S(1)} %get-tuple-element.206.refs_0_), channel_id=1, source_target_pairs={{0,8},{4,12},{8,24},{12,28},{24,16},{28,20},{16,0},{20,4},{1,9},{5... | collective-permute-start | bytes 3145736 | tf_op jit(solution)/shard_map/ppermute | solution.py:38
  65.1 27.5 %collective-permute-start.12 = (bf16[4096,128]{1,0:T(8,128)(2,1)S(1)}, bf16[4096,128]{1,0:T(8,128)(2,1)S(1)}, u32[]{:S(2)}, u32[]{:S(2)}) collective-permute-start(bf16[4096,128]{1,0:T(8,128)(2,1)S(1)} %get-tuple-element.206.refs_0_), channel_id=1, source_target_pairs={{0,16},{4,20},{8,0},{12,4},{24,8},{28,12},{16,24},{20,28},{1,17},{... | collective-permute-start | bytes 3145736 | tf_op jit(solution)/shard_map/ppermute | solution.py:38
  66.5 26.1 %collective-permute-start.10 = (bf16[1024,256]{1,0:T(8,128)(2,1)}, bf16[1024,256]{1,0:T(8,128)(2,1)S(1)}, u32[]{:S(2)}, u32[]{:S(2)}) collective-permute-start(bf16[1024,256]{1,0:T(8,128)(2,1)} %get-tuple-element.202), channel_id=1, source_target_pairs={{0,2},{1,3},{2,0},{3,1},{4,6},{5,7},{6,4},{7,5},{8,10},{9,11},{10,... | collective-permute-start | bytes 1572872 | tf_op jit(solution)/shard_map/ppermute | solution.py:87
  95.9 14.1 %collective-permute-start.17 = (bf16[2048,128]{1,0:T(8,128)(2,1)}, bf16[2048,128]{1,0:T(8,128)(2,1)S(1)}, u32[]{:S(2)}, u32[]{:S(2)}) collective-permute-start(bf16[2048,128]{1,0:T(8,128)(2,1)} %slice.84), channel_id=1, source_target_pairs={{0,8},{4,12},{8,24},{12,28},{24,16},{28,20},{16,0},{20,4},{1,9},{5... | collective-permute-start | bytes 1572872 | tf_op jit(solution)/shard_map/ppermute | solution.py:38
  96.6 13.8 %collective-permute-start.18 = (bf16[2048,128]{1,0:T(8,128)(2,1)}, bf16[2048,128]{1,0:T(8,128)(2,1)S(1)}, u32[]{:S(2)}, u32[]{:S(2)}) collective-permute-start(bf16[2048,128]{1,0:T(8,128)(2,1)} %slice.85), channel_id=1, source_target_pairs={{0,16},{4,20},{8,0},{12,4},{24,8},{28,12},{16,24},{20,28},{1,17},{... | collective-permute-start | bytes 1572872 | tf_op jit(solution)/shard_map/ppermute | solution.py:38
  99.1 11.3 %collective-permute-start.22 = (bf16[1024,128]{1,0:T(8,128)(2,1)}, bf16[1024,128]{1,0:T(8,128)(2,1)S(1)}, u32[]{:S(2)}, u32[]{:S(2)}) collective-permute-start(bf16[1024,128]{1,0:T(8,128)(2,1)} %get-tuple-element.219), channel_id=1, source_target_pairs={{0,1},{1,2},{2,3},{3,0},{4,5},{5,6},{6,7},{7,4},{8,9},{9,10},{10,1... | collective-permute-start | bytes 786440 | tf_op jit(solution)/shard_map/ppermute | solution.py:87
  99.1 14.2 %collective-permute-start.21 = (bf16[1024,128]{1,0:T(8,128)(2,1)}, bf16[1024,128]{1,0:T(8,128)(2,1)}, u32[]{:S(2)}, u32[]{:S(2)}) collective-permute-start(bf16[1024,128]{1,0:T(8,128)(2,1)} %get-tuple-element.217), channel_id=1, source_target_pairs={{0,3},{1,0},{2,1},{3,2},{4,7},{5,4},{6,5},{7,6},{8,11},{9,8},{10,9... | collective-permute-start | bytes 786440 | tf_op jit(solution)/shard_map/ppermute | solution.py:87
  113.8 15.0 %collective-permute-start.23 = (bf16[1024,128]{1,0:T(8,128)(2,1)}, bf16[1024,128]{1,0:T(8,128)(2,1)S(1)}, u32[]{:S(2)}, u32[]{:S(2)}) collective-permute-start(bf16[1024,128]{1,0:T(8,128)(2,1)} %get-tuple-element.221), channel_id=1, source_target_pairs={{0,2},{1,3},{2,0},{3,1},{4,6},{5,7},{6,4},{7,5},{8,10},{9,11},{10,... | collective-permute-start | bytes 786440 | tf_op jit(solution)/shard_map/ppermute | solution.py:87
  129.6 14.7 %collective-permute-start.26 = (bf16[512,128]{1,0:T(8,128)(2,1)}, bf16[512,128]{1,0:T(8,128)(2,1)S(1)}, u32[]{:S(2)}, u32[]{:S(2)}) collective-permute-start(bf16[512,128]{1,0:T(8,128)(2,1)} %get-tuple-element.227), channel_id=1, source_target_pairs={{0,3},{1,0},{2,1},{3,2},{4,7},{5,4},{6,5},{7,6},{8,11},{9,8},{10,9... | collective-permute-start | bytes 393224 | tf_op jit(solution)/shard_map/ppermute | solution.py:87
  131.7 12.6 %collective-permute-start.27 = (bf16[512,128]{1,0:T(8,128)(2,1)}, bf16[512,128]{1,0:T(8,128)(2,1)S(1)}, u32[]{:S(2)}, u32[]{:S(2)}) collective-permute-start(bf16[512,128]{1,0:T(8,128)(2,1)} %get-tuple-element.228), channel_id=1, source_target_pairs={{0,2},{1,3},{2,0},{3,1},{4,6},{5,7},{6,4},{7,5},{8,10},{9,11},{10,... | collective-permute-start | bytes 393224 | tf_op jit(solution)/shard_map/ppermute | solution.py:87
  131.7 12.6 %collective-permute-start.28 = (bf16[512,128]{1,0:T(8,128)(2,1)}, bf16[512,128]{1,0:T(8,128)(2,1)S(1)}, u32[]{:S(2)}, u32[]{:S(2)}) collective-permute-start(bf16[512,128]{1,0:T(8,128)(2,1)} %get-tuple-element.229), channel_id=1, source_target_pairs={{0,1},{1,2},{2,3},{3,0},{4,5},{5,6},{6,7},{7,4},{8,9},{9,10},{10,1... | collective-permute-start | bytes 393224 | tf_op jit(solution)/shard_map/ppermute | solution.py:87
  146.7 12.3 %collective-permute-start.30 = (bf16[512,128]{1,0:T(8,128)(2,1)}, bf16[512,128]{1,0:T(8,128)(2,1)S(1)}, u32[]{:S(2)}, u32[]{:S(2)}) collective-permute-start(bf16[512,128]{1,0:T(8,128)(2,1)} %get-tuple-element.235), channel_id=1, source_target_pairs={{0,2},{1,3},{2,0},{3,1},{4,6},{5,7},{6,4},{7,5},{8,10},{9,11},{10,... | collective-permute-start | bytes 393224 | tf_op jit(solution)/shard_map/ppermute | solution.py:87
  147.8 11.1 %collective-permute-start.31 = (bf16[512,128]{1,0:T(8,128)(2,1)}, bf16[512,128]{1,0:T(8,128)(2,1)S(1)}, u32[]{:S(2)}, u32[]{:S(2)}) collective-permute-start(bf16[512,128]{1,0:T(8,128)(2,1)} %get-tuple-element.236), channel_id=1, source_target_pairs={{0,1},{1,2},{2,3},{3,0},{4,5},{5,6},{6,7},{7,4},{8,9},{9,10},{10,1... | collective-permute-start | bytes 393224 | tf_op jit(solution)/shard_map/ppermute | solution.py:87
  159.0 14.0 %collective-permute-start.33 = (bf16[512,128]{1,0:T(8,128)(2,1)}, bf16[512,128]{1,0:T(8,128)(2,1)S(1)}, u32[]{:S(2)}, u32[]{:S(2)}) collective-permute-start(bf16[512,128]{1,0:T(8,128)(2,1)} %get-tuple-element.258), channel_id=1, source_target_pairs={{0,2},{1,3},{2,0},{3,1},{4,6},{5,7},{6,4},{7,5},{8,10},{9,11},{10,... | collective-permute-start | bytes 393224 | tf_op jit(solution)/shard_map/ppermute | solution.py:87
  160.7 12.3 %collective-permute-start.34 = (bf16[512,128]{1,0:T(8,128)(2,1)}, bf16[512,128]{1,0:T(8,128)(2,1)S(1)}, u32[]{:S(2)}, u32[]{:S(2)}) collective-permute-start(bf16[512,128]{1,0:T(8,128)(2,1)} %get-tuple-element.259), channel_id=1, source_target_pairs={{0,1},{1,2},{2,3},{3,0},{4,5},{5,6},{6,7},{7,4},{8,9},{9,10},{10,1... | collective-permute-start | bytes 393224 | tf_op jit(solution)/shard_map/ppermute | solution.py:87
  178.1 13.5 %collective-permute-start.39 = (bf16[384,1024]{1,0:T(8,128)(2,1)S(1)}, bf16[384,1024]{1,0:T(8,128)(2,1)S(1)}, u32[]{:S(2)}, u32[]{:S(2)}) collective-permute-start(bf16[384,1024]{1,0:T(8,128)(2,1)S(1)} %pad_maximum_fusion), channel_id=1, source_target_pairs={{0,4},{4,0},{8,12},{12,8},{16,20},{20,16},{24,28},{28,24},{1,5},{5... | collective-permute-start | bytes 2359304 | tf_op jit(solution)/shard_map/ppermute | solution.py:41
  178.2 13.4 %collective-permute-start.38 = (bf16[128,1024]{1,0:T(8,128)(2,1)S(1)}, bf16[128,1024]{1,0:T(8,128)(2,1)S(1)}, u32[]{:S(2)}, u32[]{:S(2)}) collective-permute-start(bf16[128,1024]{1,0:T(8,128)(2,1)S(1)} %get-tuple-element.401), channel_id=1, source_target_pairs={{0,4},{4,0},{8,12},{12,8},{16,20},{20,16},{24,28},{28,24},{1,5},{5... | collective-permute-start | bytes 786440 | tf_op jit(solution)/shard_map/ppermute | solution.py:41
  178.7 12.8 %collective-permute-start.36 = (bf16[512,128]{1,0:T(8,128)(2,1)S(1)}, bf16[512,128]{1,0:T(8,128)(2,1)S(1)}, u32[]{:S(2)}, u32[]{:S(2)}) collective-permute-start(bf16[512,128]{1,0:T(8,128)(2,1)S(1)} %copy-done.61), channel_id=1, source_target_pairs={{0,2},{1,3},{2,0},{3,1},{4,6},{5,7},{6,4},{7,5},{8,10},{9,11},{10,... | collective-permute-start | bytes 393224 | tf_op jit(solution)/shard_map/ppermute | solution.py:87
  179.5 12.1 %collective-permute-start.37 = (bf16[512,128]{1,0:T(8,128)(2,1)S(1)}, bf16[512,128]{1,0:T(8,128)(2,1)S(1)}, u32[]{:S(2)}, u32[]{:S(2)}) collective-permute-start(bf16[512,128]{1,0:T(8,128)(2,1)S(1)} %copy-done.60), channel_id=1, source_target_pairs={{0,1},{1,2},{2,3},{3,0},{4,5},{5,6},{6,7},{7,4},{8,9},{9,10},{10,1... | collective-permute-start | bytes 393224 | tf_op jit(solution)/shard_map/ppermute | solution.py:87
  191.6 24.5 %collective-permute-start.44 = (bf16[1024,128]{1,0:T(8,128)(2,1)S(1)}, bf16[1024,128]{1,0:T(8,128)(2,1)S(1)}, u32[]{:S(2)}, u32[]{:S(2)}) collective-permute-start(bf16[1024,128]{1,0:T(8,128)(2,1)S(1)} %copy-done.36), channel_id=1, source_target_pairs={{0,1},{1,2},{2,3},{3,0},{4,5},{5,6},{6,7},{7,4},{8,9},{9,10},{10,1... | collective-permute-start | bytes 786440 | tf_op jit(solution)/shard_map/ppermute | solution.py:87
  191.9 24.2 %collective-permute-start.43 = (bf16[1024,128]{1,0:T(8,128)(2,1)S(1)}, bf16[1024,128]{1,0:T(8,128)(2,1)S(1)}, u32[]{:S(2)}, u32[]{:S(2)}) collective-permute-start(bf16[1024,128]{1,0:T(8,128)(2,1)S(1)} %copy-done.37), channel_id=1, source_target_pairs={{0,2},{1,3},{2,0},{3,1},{4,6},{5,7},{6,4},{7,5},{8,10},{9,11},{10,... | collective-permute-start | bytes 786440 | tf_op jit(solution)/shard_map/ppermute | solution.py:87
  193.9 22.2 %collective-permute-start.42 = (bf16[1024,128]{1,0:T(8,128)(2,1)S(1)}, bf16[1024,128]{1,0:T(8,128)(2,1)S(1)}, u32[]{:S(2)}, u32[]{:S(2)}) collective-permute-start(bf16[1024,128]{1,0:T(8,128)(2,1)S(1)} %copy-done.38), channel_id=1, source_target_pairs={{0,3},{1,0},{2,1},{3,2},{4,7},{5,4},{6,5},{7,6},{8,11},{9,8},{10,9... | collective-permute-start | bytes 786440 | tf_op jit(solution)/shard_map/ppermute | solution.py:87
  196.8 19.2 %collective-permute-start.40 = (bf16[64,1024]{1,0:T(8,128)(2,1)S(1)}, bf16[64,1024]{1,0:T(8,128)(2,1)S(1)}, u32[]{:S(2)}, u32[]{:S(2)}) collective-permute-start(bf16[64,1024]{1,0:T(8,128)(2,1)S(1)} %get-tuple-element.417), channel_id=1, source_target_pairs={{0,8},{4,12},{8,24},{12,28},{24,16},{28,20},{16,0},{20,4},{1,9},{5... | collective-permute-start | bytes 393224 | tf_op jit(solution)/shard_map/ppermute | solution.py:38
  198.0 18.1 %collective-permute-start.41 = (bf16[64,1024]{1,0:T(8,128)(2,1)S(1)}, bf16[64,1024]{1,0:T(8,128)(2,1)S(1)}, u32[]{:S(2)}, u32[]{:S(2)}) collective-permute-start(bf16[64,1024]{1,0:T(8,128)(2,1)S(1)} %get-tuple-element.416), channel_id=1, source_target_pairs={{0,16},{4,20},{8,0},{12,4},{24,8},{28,12},{16,24},{20,28},{1,17},{... | collective-permute-start | bytes 393224 | tf_op jit(solution)/shard_map/ppermute | solution.py:38
  220.1 11.7 %collective-permute-start.47 = (bf16[128,1024]{1,0:T(8,128)(2,1)S(1)}, bf16[128,1024]{1,0:T(8,128)(2,1)S(1)}, u32[]{:S(2)}, u32[]{:S(2)}) collective-permute-start(bf16[128,1024]{1,0:T(8,128)(2,1)S(1)} %get-tuple-element.415), channel_id=1, source_target_pairs={{0,8},{4,12},{8,24},{12,28},{24,16},{28,20},{16,0},{20,4},{1,9},{5... | collective-permute-start | bytes 786440 | tf_op jit(solution)/shard_map/ppermute | solution.py:38
  232.6 27.6 %collective-permute-start.49 = (bf16[4096,128]{1,0:T(8,128)(2,1)}, bf16[4096,128]{1,0:T(8,128)(2,1)S(1)}, u32[]{:S(2)}, u32[]{:S(2)}) collective-permute-start(bf16[4096,128]{1,0:T(8,128)(2,1)} %get-tuple-element.349), channel_id=1, source_target_pairs={{0,8},{4,12},{8,24},{12,28},{24,16},{28,20},{16,0},{20,4},{1,9},{5... | collective-permute-start | bytes 3145736 | tf_op jit(solution)/shard_map/ppermute | solution.py:38
  233.7 26.5 %collective-permute-start.50 = (bf16[4096,128]{1,0:T(8,128)(2,1)}, bf16[4096,128]{1,0:T(8,128)(2,1)S(1)}, u32[]{:S(2)}, u32[]{:S(2)}) collective-permute-start(bf16[4096,128]{1,0:T(8,128)(2,1)} %get-tuple-element.350), channel_id=1, source_target_pairs={{0,16},{4,20},{8,0},{12,4},{24,8},{28,12},{16,24},{20,28},{1,17},{... | collective-permute-start | bytes 3145736 | tf_op jit(solution)/shard_map/ppermute | solution.py:38
  234.6 25.5 %collective-permute-start.51 = (bf16[1024,256]{1,0:T(8,128)(2,1)S(1)}, bf16[1024,256]{1,0:T(8,128)(2,1)S(1)}, u32[]{:S(2)}, u32[]{:S(2)}) collective-permute-start(bf16[1024,256]{1,0:T(8,128)(2,1)S(1)} %copy-done.27), channel_id=1, source_target_pairs={{0,2},{1,3},{2,0},{3,1},{4,6},{5,7},{6,4},{7,5},{8,10},{9,11},{10,... | collective-permute-start | bytes 1572872 | tf_op jit(solution)/shard_map/ppermute | solution.py:87
  265.9 15.1 %collective-permute-start.52 = (bf16[2048,128]{1,0:T(8,128)(2,1)}, bf16[2048,128]{1,0:T(8,128)(2,1)}, u32[]{:S(2)}, u32[]{:S(2)}) collective-permute-start(bf16[2048,128]{1,0:T(8,128)(2,1)} %get-tuple-element.395), channel_id=1, source_target_pairs={{0,8},{4,12},{8,24},{12,28},{24,16},{28,20},{16,0},{20,4},{1,9},{5... | collective-permute-start | bytes 1572872 | tf_op jit(solution)/shard_map/ppermute | solution.py:38
  267.0 15.1 %collective-permute-start.53 = (bf16[2048,128]{1,0:T(8,128)(2,1)}, bf16[2048,128]{1,0:T(8,128)(2,1)}, u32[]{:S(2)}, u32[]{:S(2)}) collective-permute-start(bf16[2048,128]{1,0:T(8,128)(2,1)} %get-tuple-element.394), channel_id=1, source_target_pairs={{0,16},{4,20},{8,0},{12,4},{24,8},{28,12},{16,24},{20,28},{1,17},{... | collective-permute-start | bytes 1572872 | tf_op jit(solution)/shard_map/ppermute | solution.py:38
  269.2 22.4 %collective-permute-start.59 = (bf16[2048,128]{1,0:T(8,128)(2,1)}, bf16[2048,128]{1,0:T(8,128)(2,1)}, u32[]{:S(2)}, u32[]{:S(2)}) collective-permute-start(bf16[2048,128]{1,0:T(8,128)(2,1)} %get-tuple-element.397), channel_id=1, source_target_pairs={{0,8},{4,12},{8,24},{12,28},{24,16},{28,20},{16,0},{20,4},{1,9},{5... | collective-permute-start | bytes 1572872 | tf_op jit(solution)/shard_map/ppermute | solution.py:38
  270.3 22.2 %collective-permute-start.60 = (bf16[2048,128]{1,0:T(8,128)(2,1)}, bf16[2048,128]{1,0:T(8,128)(2,1)}, u32[]{:S(2)}, u32[]{:S(2)}) collective-permute-start(bf16[2048,128]{1,0:T(8,128)(2,1)} %get-tuple-element.396), channel_id=1, source_target_pairs={{0,16},{4,20},{8,0},{12,4},{24,8},{28,12},{16,24},{20,28},{1,17},{... | collective-permute-start | bytes 1572872 | tf_op jit(solution)/shard_map/ppermute | solution.py:38
  272.5 19.9 %collective-permute-start.56 = (bf16[128,256]{1,0:T(8,128)(2,1)S(1)}, bf16[128,256]{1,0:T(8,128)(2,1)S(1)}, u32[]{:S(2)}, u32[]{:S(2)}) collective-permute-start(bf16[128,256]{1,0:T(8,128)(2,1)S(1)} %get-tuple-element.366), channel_id=1, source_target_pairs={{0,3},{1,0},{2,1},{3,2},{4,7},{5,4},{6,5},{7,6},{8,11},{9,8},{10,9... | collective-permute-start | bytes 196616 | tf_op jit(solution)/shard_map/ppermute | solution.py:87
  280.9 11.5 %collective-permute-start.57 = (bf16[128,256]{1,0:T(8,128)(2,1)S(1)}, bf16[128,256]{1,0:T(8,128)(2,1)S(1)}, u32[]{:S(2)}, u32[]{:S(2)}) collective-permute-start(bf16[128,256]{1,0:T(8,128)(2,1)S(1)} %get-tuple-element.367), channel_id=1, source_target_pairs={{0,2},{1,3},{2,0},{3,1},{4,6},{5,7},{6,4},{7,5},{8,10},{9,11},{10,... | collective-permute-start | bytes 196616 | tf_op jit(solution)/shard_map/ppermute | solution.py:87
  297.3 26.0 %collective-permute-start.63 = (bf16[4096,128]{1,0:T(8,128)(2,1)}, bf16[4096,128]{1,0:T(8,128)(2,1)S(1)}, u32[]{:S(2)}, u32[]{:S(2)}) collective-permute-start(bf16[4096,128]{1,0:T(8,128)(2,1)} %get-tuple-element.385), channel_id=1, source_target_pairs={{0,8},{4,12},{8,24},{12,28},{24,16},{28,20},{16,0},{20,4},{1,9},{5... | collective-permute-start | bytes 3145736 | tf_op jit(solution)/shard_map/ppermute | solution.py:38
  298.1 25.3 %collective-permute-start.64 = (bf16[4096,128]{1,0:T(8,128)(2,1)}, bf16[4096,128]{1,0:T(8,128)(2,1)S(1)}, u32[]{:S(2)}, u32[]{:S(2)}) collective-permute-start(bf16[4096,128]{1,0:T(8,128)(2,1)} %get-tuple-element.386), channel_id=1, source_target_pairs={{0,16},{4,20},{8,0},{12,4},{24,8},{28,12},{16,24},{20,28},{1,17},{... | collective-permute-start | bytes 3145736 | tf_op jit(solution)/shard_map/ppermute | solution.py:38
  299.3 14.9 %collective-permute-start.61 = (bf16[1024,256]{1,0:T(8,128)(2,1)}, bf16[1024,256]{1,0:T(8,128)(2,1)}, u32[]{:S(2)}, u32[]{:S(2)}) collective-permute-start(bf16[1024,256]{1,0:T(8,128)(2,1)} %get-tuple-element.378), channel_id=1, source_target_pairs={{0,3},{1,0},{2,1},{3,2},{4,7},{5,4},{6,5},{7,6},{8,11},{9,8},{10,9... | collective-permute-start | bytes 1572872 | tf_op jit(solution)/shard_map/ppermute | solution.py:87
  301.0 22.3 %collective-permute-start.62 = (bf16[1024,256]{1,0:T(8,128)(2,1)}, bf16[1024,256]{1,0:T(8,128)(2,1)S(1)}, u32[]{:S(2)}, u32[]{:S(2)}) collective-permute-start(bf16[1024,256]{1,0:T(8,128)(2,1)} %get-tuple-element.380), channel_id=1, source_target_pairs={{0,1},{1,2},{2,3},{3,0},{4,5},{5,6},{6,7},{7,4},{8,9},{9,10},{10,1... | collective-permute-start | bytes 1572872 | tf_op jit(solution)/shard_map/ppermute | solution.py:87
  (81 other events, 726.8 us)
Sparse Core Ops, SparseCore 0:
  113.4 26.7 all-gather.1
